TPU v7x, 32 devices: a whole 2x2x4 slice. The times are simulated.
32 devices in a mesh: dp: 4 (over y, core), expert: 8 (over z, x).
Axes of the slice: x: 2, y: 2, z: 4, core: 2. Of those that a mesh axis runs over, the one named last changes fastest.
Arguments:
- grad_out: bfloat16 [4096, 2048], P(('dp', 'expert')), may hold values from -6 to 6
- route_ids: int32 [4096, 2], P(('dp', 'expert')), may hold values from 0 to 15, all different within a row; in each aligned block of 128 rows (0 to 127, 128 to 255, ...) at most 32 rows name the same one
- route_probs: float32 [4096, 2], P(('dp', 'expert')), may hold values from 0.01 to 0.3
- hidden: bfloat16 [4, 8, 16, 32, 768], P('dp', None, 'expert'), may hold values from -2 to 2
- w_down: bfloat16 [16, 768, 2048], P('expert'), may hold values from -0.21875 to 0.21875
Outputs:
- hidden_grad: bfloat16 [4, 8, 16, 32, 768], P('dp', None, 'expert')
- prob_grad: float32 [4096, 2], P(('dp', 'expert'))
- weight_grad: float32 [768, 16, 2048], P('dp', 'expert')
Inputs may be any that keep to these rules, and one draw needn't show every extreme that they name: `route_ids`: each row names 2 different experts; among the 128 rows of one device no expert is named more than 32 times, a bound that some block reaches.
All inputs are finite; a program needn't handle non-finite values.
Results may differ from a plain program's by a relative error of at most 0.022.
Values may be sent and summed in bfloat16 or wider, within the bound.
No kernel may reach another device: no remote copies, remote signals or barrier semaphores. Data moves between devices by JAX's collectives and lax.ppermute only.
A program may use at most 128 MiB of HBM per device.

v0:
```python
import jax
import jax.numpy as jnp
from jax import lax
from jax.sharding import PartitionSpec as P


def slots_of(route_blocks, experts):
    hits = (
        (route_blocks[..., None] == jnp.arange(experts, dtype=jnp.int32)).astype(jnp.int32).sum(2)
    )
    before = jnp.cumsum(hits, axis=1) - hits
    return jnp.take_along_axis(before, route_blocks, axis=2)


def body(grad_out, route_ids, route_probs, hidden, w_down):
    groups = lax.axis_size("expert")
    held = w_down.shape[0]
    experts = groups * held
    capacity = hidden.shape[3]
    chosen = route_ids.shape[1]
    tokens_here = grad_out.shape[0]
    features = grad_out.shape[1]
    total = jnp.sum(route_probs, axis=1, keepdims=True)
    gates = route_probs / total
    gate_word = gates.astype(jnp.bfloat16)
    slot = slots_of(route_ids[None], experts)[0]
    flat = (route_ids * capacity + slot).reshape(-1)
    send_rows = (
        jnp.zeros((experts * capacity, features), jnp.bfloat16)
        .at[flat]
        .set(jnp.repeat(grad_out, chosen, axis=0))
    )
    send_gates = jnp.zeros((experts * capacity,), jnp.bfloat16).at[flat].set(gate_word.reshape(-1))
    recv_rows, recv_gates = (
        lax.all_to_all(
            send_rows.reshape(groups, held, capacity, features),
            "expert",
            split_axis=0,
            concat_axis=0,
            tiled=True,
        ),
        lax.all_to_all(
            send_gates.reshape(groups, held, capacity),
            "expert",
            split_axis=0,
            concat_axis=0,
            tiled=True,
        ),
    )
    saved = hidden[0]
    factor = recv_gates.astype(jnp.float32)[..., None]
    raw = jnp.einsum("secd,ehd->sech", recv_rows, w_down, preferred_element_type=jnp.float32)
    hidden_grad = (factor * raw).astype(jnp.bfloat16)[None]
    gate_grad = jnp.sum(raw * saved.astype(jnp.float32), axis=-1)
    returned = lax.all_to_all(gate_grad, "expert", split_axis=0, concat_axis=0, tiled=True).reshape(
        -1
    )
    picked_grad = returned[flat].reshape(tokens_here, chosen)
    prob_grad = (picked_grad - jnp.sum(gates * picked_grad, axis=1, keepdims=True)) / total
    scaled = (factor * recv_rows.astype(jnp.float32)).astype(jnp.bfloat16)
    weight_term = jnp.einsum("sech,secd->hed", saved, scaled, preferred_element_type=jnp.float32)
    weight_grad = lax.psum_scatter(
        weight_term.astype(jnp.bfloat16), "dp", scatter_dimension=0, tiled=True
    ).astype(jnp.float32)
    return (hidden_grad, prob_grad, weight_grad)


def solution(mesh):
    in_specs = (
        P(("dp", "expert"), None),
        P(("dp", "expert"), None),
        P(("dp", "expert"), None),
        P("dp", None, "expert", None, None),
        P("expert", None, None),
    )
    out_specs = (
        P("dp", None, "expert", None, None),
        P(("dp", "expert"), None),
        P("dp", "expert", None),
    )
    return jax.shard_map(body, mesh=mesh, in_specs=in_specs, out_specs=out_specs, check_vma=False)
```

profile of v0, /device:TPU:0, one launch (start us, length us, event | category | flops | bytes accessed | tf_op | source)
XLA Modules:
  0.0 232.3 jit_solution(1725086945706106446)
XLA Ops:
  7.2 0.7 convert_reduce_fusion
  7.9 0.7 bitcast_or_fusion
  9.1 1.9 gather_fusion.1
  12.0 2.2 scatter_custom_fusion
  14.1 0.7 reshape.112
  14.8 7.3 %all-to-all-start = ((bf16[8,2,32]{2,1,0:T(2,128)(2,1)}), bf16[8,2,32]{2,1,0:T(2,128)(2,1)S(1)}, u32[]{:S(2)}, u32[]{:S(2)}) async-start(bf16[8,2,32]{2,1,0:T(2,128)(2,1)} %reshape.112), calls=%async_computation | async-start | bytes 8192 | tf_op jit(solution)/shard_map/all_to_all | solution.py:42
  22.1 0.6 broadcast_in_dim.29
  22.7 0.4 reshape.145
  23.1 3.7 %scatter_custom_fusion.1 = bf16[512,2048]{1,0:T(8,128)(2,1)} fusion(s32[256]{0:T(256)S(1)} %bitcast.42, bf16[256,2048]{1,0:T(8,128)(2,1)S(1)} %reshape.145, bf16[]{:T(256)} %constant.9.clone.1), kind=kCustom, calls=%fused_computation.16 | custom fusion | bytes 2097154 | tf_op jit(solution)/shard_map/scatter | solution.py:31
  26.9 1.6 all-to-all-done
  28.5 4.5 %all-to-all-start.1 = ((bf16[8,2,32,2048]{3,2,1,0:T(8,128)(2,1)}), bf16[8,2,32,2048]{3,2,1,0:T(8,128)(2,1)S(1)}, u32[]{:S(2)}, u32[]{:S(2)}) async-start(bf16[8,2,32,2048]{3,2,1,0:T(8,128)(2,1)} %bitcast.4), calls=%async_computation.1 | async-start | bytes 4194304 | tf_op jit(solution)/shard_map/all_to_all | solution.py:35
  33.1 47.6 %all-to-all-done.1 = bf16[8,2,32,2048]{3,2,1,0:T(8,128)(2,1)S(1)} async-done(((bf16[8,2,32,2048]{3,2,1,0:T(8,128)(2,1)}), bf16[8,2,32,2048]{3,2,1,0:T(8,128)(2,1)S(1)}, u32[]{:S(2)}, u32[]{:S(2)}) %all-to-all-start.1) | async-done | bytes 2097184 | tf_op jit(solution)/shard_map/all_to_all | solution.py:35
  80.7 4.7 %fusion = bf16[768,2,2048]{0,2,1:T(8,128)(2,1)} fusion(bf16[8,2,32,2048]{3,2,1,0:T(8,128)(2,1)S(1)} %all-to-all-done.1, f32[8,2,32]{2,1,0:T(2,128)S(1)} %convert_element_type.40, bf16[1,8,2,32,768]{4,3,2,1,0:T(8,128)(2,1)S(1)} %copy-done.3), kind=kOutput, calls=%fused_computation.5 | convolution fusion | flops 1616904192 | bytes 9177088 | tf_op jit(solution)/shard_map/sech,secd->hed/dot_general | solution.py:61
  85.3 16.4 %copy.105 = bf16[768,2,2048]{2,1,0:T(2,128)(2,1)} copy(bf16[768,2,2048]{0,2,1:T(8,128)(2,1)} %fusion) | data formatting | bytes 12582912 | tf_op jit(solution)/shard_map/convert_element_type | solution.py:63
  101.8 4.9 %fusion.6 = (f32[8,2,32]{2,0,1:T(8,128)S(1)}, bf16[1,8,2,32,768]{4,3,1,2,0:T(8,128)(2,1)S(1)}) fusion(bf16[1,8,2,32,768]{4,3,2,1,0:T(8,128)(2,1)} %param.8, f32[8,2,32]{2,0,1:T(8,128)S(1)} %copy.100, bf16[2,768,2048]{2,1,0:T(8,128)(2,1)} %param.9, bf16[8,2,32,2048]{3,2,1,0:T(8,128)(2,1)S(1)} %all-to-all-done.1), kind=kOutput, calls=%fused_computation.15 | convolution fusion | flops 1612578304 | bytes 9965568 | tf_op jit(solution)/shard_map/secd,ehd->sech/dot_general | solution.py:52
  106.7 0.6 copy.103
  107.3 3.6 %all-to-all-start.2 = ((f32[8,2,32]{2,1,0:T(2,128)}), f32[8,2,32]{2,1,0:T(2,128)S(1)}, u32[]{:S(2)}, u32[]{:S(2)}) async-start(f32[8,2,32]{2,1,0:T(2,128)} %copy.103), calls=%async_computation.2 | async-start | bytes 16384 | tf_op jit(solution)/shard_map/all_to_all | solution.py:55
  111.0 0.6 dynamic-slice
  112.2 0.9 copy.106
  113.1 4.3 %all-to-all-done.2 = f32[8,2,32]{2,1,0:T(2,128)S(1)} async-done(((f32[8,2,32]{2,1,0:T(2,128)}), f32[8,2,32]{2,1,0:T(2,128)S(1)}, u32[]{:S(2)}, u32[]{:S(2)}) %all-to-all-start.2) | async-done | bytes 2080 | tf_op jit(solution)/shard_map/all_to_all | solution.py:55
  117.6 1.9 gather_fusion
  120.0 0.6 copy.107
  120.6 100.0 %all-reduce.3.cloned.1.call-done = bf16[768,2,2048]{2,1,0:T(2,128)(2,1)} async-done(((bf16[768,2,2048]{2,1,0:T(2,128)(2,1)}), bf16[768,2,2048]{2,1,0:T(2,128)(2,1)}) %all-reduce.3.cloned.1.call-update) | async-done | bytes 6291472
  220.6 4.9 %dynamic-slice_convert_fusion = f32[192,2,2048]{2,1,0:T(2,128)} fusion(bf16[768,2,2048]{2,1,0:T(2,128)(2,1)} %all-reduce.3.cloned.1.call-done, u32[]{:T(128)S(6)} %multiply.1), kind=kLoop, calls=%fused_computation.11 | loop fusion | flops 786432 | bytes 4718596 | tf_op jit(solution)/shard_map/convert_element_type | solution.py:64
  (34 shorter events, 2.0 us)
Async XLA Ops:
  9.1 2.2 copy-start.1
  9.1 2.5 %copy-start.2 = (f32[128,2]{0,1:T(2,128)S(1)}, f32[128,2]{0,1:T(2,128)}, u32[]{:S(2)}) copy-start(f32[128,2]{0,1:T(2,128)} %param.7) | copy-start | bytes 3076
  9.1 13.0 %copy-start = (bf16[128,2048]{1,0:T(8,128)(2,1)S(1)}, bf16[128,2048]{1,0:T(8,128)(2,1)}, u32[]{:S(2)}) copy-start(bf16[128,2048]{1,0:T(8,128)(2,1)} %param.5) | copy-start | bytes 1572868
  14.8 13.6 %all-to-all-start = ((bf16[8,2,32]{2,1,0:T(2,128)(2,1)}), bf16[8,2,32]{2,1,0:T(2,128)(2,1)S(1)}, u32[]{:S(2)}, u32[]{:S(2)}) async-start(bf16[8,2,32]{2,1,0:T(2,128)(2,1)} %reshape.112), calls=%async_computation | async-start | bytes 8192 | tf_op jit(solution)/shard_map/all_to_all | solution.py:42
  28.5 52.2 %copy-start.3 = (bf16[1,8,2,32,768]{4,3,2,1,0:T(8,128)(2,1)S(1)}, bf16[1,8,2,32,768]{4,3,2,1,0:T(8,128)(2,1)}, u32[]{:S(2)}) copy-start(bf16[1,8,2,32,768]{4,3,2,1,0:T(8,128)(2,1)} %param.8) | copy-start | bytes 2359300
  28.5 52.2 %all-to-all-start.1 = ((bf16[8,2,32,2048]{3,2,1,0:T(8,128)(2,1)}), bf16[8,2,32,2048]{3,2,1,0:T(8,128)(2,1)S(1)}, u32[]{:S(2)}, u32[]{:S(2)}) async-start(bf16[8,2,32,2048]{3,2,1,0:T(8,128)(2,1)} %bitcast.4), calls=%async_computation.1 | async-start | bytes 4194304 | tf_op jit(solution)/shard_map/all_to_all | solution.py:35
  33.0 187.6 %all-reduce.3.cloned.1.call-start = ((), (), s32[]{:S(2)}) async-start(), calls=%async_computation.3 | async-start | bytes 12582912
  101.8 9.2 %copy-start.4 = (u32[32]{0:T(128)S(1)}, u32[32]{0:T(128)}, u32[]{:S(2)}) copy-start(u32[32]{0:T(128)} %constant.47) | copy-start | bytes 388
  107.3 10.2 %all-to-all-start.2 = ((f32[8,2,32]{2,1,0:T(2,128)}), f32[8,2,32]{2,1,0:T(2,128)S(1)}, u32[]{:S(2)}, u32[]{:S(2)}) async-start(f32[8,2,32]{2,1,0:T(2,128)} %copy.103), calls=%async_computation.2 | async-start | bytes 16384 | tf_op jit(solution)/shard_map/all_to_all | solution.py:55
Sparse Core Ops, SparseCore 0:
  101.9 118.6 all-reduce.2
where the time goes:
time: 233 us; the launch traced here: 232 us
  waiting for transfers between devices  154 us (66%)
  local copies, waits for them, and re-layouts  32 us (14%)
  starting transfers between devices  15.5 us (7%)
  between operations  14.9 us (6%)
  matrix products  9.59 us (4%)
  other arithmetic  6.89 us (3%)
    unnamed x2, waiting for transfers between devices  100 us
    all_to_all x1, waiting for transfers between devices, body(): lax.all_to_all(send_rows.reshape(groups, held, capacity, features), 'expe...  47.6 us
    convert_element_type x1, local copies, waits for them, and re-layouts, body(): weight_term.astype(jnp.bfloat16)  16.4 us
    all_to_all x1, starting transfers between devices, body(): lax.all_to_all(send_gates.reshape(groups, held, capacity), 'expert', spli...  7.25 us
    dot_general x1, matrix products, body(): jnp.einsum('secd,ehd->sech', recv_rows, w_down, preferred_element_type=jn...  4.93 us
    convert_element_type x1, other arithmetic, body(): weight_grad = lax.psum_scatter(weight_term.astype(jnp.bfloat16), 'dp', sc...  4.91 us
  transfers between devices with their start and end apart: 4, of which 4 were waited for; matrix products, arithmetic and copies ran while one was open for 6% of the time, Pallas kernels for 0%

commit v1 on v0

v1 whole, which is shorter than its diff:
```python
import jax
import jax.numpy as jnp
from jax import lax
from jax.sharding import PartitionSpec as P


def body(grad_out, route_ids, route_probs, hidden, w_down):
    groups = lax.axis_size("expert")
    dp = lax.axis_size("dp")
    held = w_down.shape[0]
    units = w_down.shape[1]
    experts = groups * held
    capacity = hidden.shape[3]
    chosen = route_ids.shape[1]
    tokens_here = grad_out.shape[0]
    features = grad_out.shape[1]
    slots = experts * capacity
    f32, bf16 = jnp.float32, jnp.bfloat16

    total = jnp.sum(route_probs, axis=1, keepdims=True)
    gates = route_probs / total
    gate_word = gates.astype(bf16)
    named = route_ids[..., None] == jnp.arange(experts, dtype=jnp.int32)
    hits = named.any(1).astype(bf16)
    earlier = jnp.tril(jnp.ones((tokens_here, tokens_here), bf16), -1)
    before = jnp.dot(earlier, hits, preferred_element_type=f32).astype(jnp.int32)
    slot = jnp.sum(jnp.where(named, before[:, None, :], 0), axis=2)
    flat = route_ids * capacity + slot
    fills = flat[None] == jnp.arange(slots, dtype=jnp.int32)[:, None, None]
    place = fills.any(2).astype(bf16)
    send_rows = jnp.dot(place, grad_out, preferred_element_type=f32).astype(bf16)
    send_gates = jnp.sum(
        jnp.where(fills, gate_word.astype(f32)[None], 0.0), axis=(1, 2)
    ).astype(bf16)
    recv_gates = lax.all_to_all(
        send_gates.reshape(groups, held, capacity), "expert", split_axis=0, concat_axis=0, tiled=True
    )
    recv_rows = lax.all_to_all(
        send_rows.reshape(groups, held, capacity, features),
        "expert",
        split_axis=0,
        concat_axis=0,
        tiled=True,
    )
    saved = hidden[0]
    factor = recv_gates.astype(f32)[..., None]
    scaled = (factor * recv_rows.astype(f32)).astype(bf16)

    share = units // dp
    across = dp // 2
    me = lax.axis_index("dp")
    core, row = me % 2, me // 2
    term = jnp.einsum("sech,secd->ehd", saved, scaled, preferred_element_type=f32)
    term = term.astype(bf16).reshape(held, across, 2, share, features)
    keep = lax.dynamic_index_in_dim(term, core, 2, keepdims=False)
    give = lax.dynamic_index_in_dim(term, 1 - core, 2, keepdims=False)
    got = lax.ppermute(give, "dp", [(i, i ^ 1) for i in range(dp)])
    pair = keep.astype(f32) + got.astype(f32)
    sum_here = lax.dynamic_index_in_dim(pair, row, 1, keepdims=False)
    for step in range(1, across):
        there = lax.dynamic_index_in_dim(pair, (row + step) % across, 1, keepdims=False)
        shift = [(2 * r + c, 2 * ((r + step) % across) + c) for r in range(across) for c in range(2)]
        sum_here = sum_here + lax.ppermute(there.astype(bf16), "dp", shift).astype(f32)
    weight_grad = sum_here.transpose(1, 0, 2)

    raw = jnp.einsum("secd,ehd->sech", recv_rows, w_down, preferred_element_type=f32)
    hidden_grad = (factor * raw).astype(bf16)[None]
    gate_grad = jnp.sum(raw * saved.astype(f32), axis=-1)
    returned = lax.all_to_all(gate_grad, "expert", split_axis=0, concat_axis=0, tiled=True)
    picked = jnp.sum(jnp.where(fills, returned.reshape(slots, 1, 1), 0.0), axis=0)
    prob_grad = (picked - jnp.sum(gates * picked, axis=1, keepdims=True)) / total
    return (hidden_grad, prob_grad, weight_grad)


def solution(mesh):
    in_specs = (
        P(("dp", "expert"), None),
        P(("dp", "expert"), None),
        P(("dp", "expert"), None),
        P("dp", None, "expert", None, None),
        P("expert", None, None),
    )
    out_specs = (
        P("dp", None, "expert", None, None),
        P(("dp", "expert"), None),
        P("dp", "expert", None),
    )
    return jax.shard_map(body, mesh=mesh, in_specs=in_specs, out_specs=out_specs, check_vma=False)
```

time: 233 us -> 161 us (0.69)
  waiting for transfers between devices: 154 us -> 100 us
  local copies, waits for them, and re-layouts: 32 us -> 14.1 us
  between operations: 14.9 us -> 0.74 us
  other arithmetic: 6.89 us -> 19.5 us
    unnamed x2 -> x0, waiting for transfers between devices: 100 us -> none
    ppermute x0 -> x2, waiting for transfers between devices: none -> 39.5 us  [the longest x1 33.5 us: body(): lax.ppermute(there.astype(bf16), 'dp', shift).astype(f32)]
    convert_element_type x2 -> x3, local copies, waits for them, and re-layouts: 16.4 us -> 5.31 us  [the longest x1 4.63 us: body(): there.astype(bf16)]
    add x1 -> x3, other arithmetic: 0.02 us -> 10.8 us  [the longest x1 10.1 us: body(): pair = keep.astype(f32) + got.astype(f32)]
    dynamic_slice x0 -> x2, local copies, waits for them, and re-layouts: none -> 7.15 us  [the longest x1 4.9 us: body(): give = lax.dynamic_index_in_dim(term, 1 - core, 2, keepdims=False)]
    transpose x0 -> x1, other arithmetic: none -> 6.19 us  [body(): weight_grad = sum_here.transpose(1, 0, 2)]
    scatter x2 -> x0, local copies, waits for them, and re-layouts: 5.88 us -> none  [the longest x1 3.72 us: body(): send_rows = jnp.zeros((experts * capacity, features), jnp.bfloat16).at[fl...]
    convert_element_type x3 -> x2, other arithmetic: 5 us -> 0.01 us  [the longest x1 0.01 us: body(): factor = recv_gates.astype(f32)[..., None]]
  transfers between devices with their start and end apart: 4 -> 5, of which waited for: 4 -> 5; matrix products, arithmetic and copies ran while one was open for 6% -> 1% of each run, Pallas kernels for 0% -> 0%
where the time goes in v1:
time: 161 us
  waiting for transfers between devices  100 us (62%)
  other arithmetic  19.5 us (12%)
  starting transfers between devices  15.9 us (10%)
  local copies, waits for them, and re-layouts  14.1 us (9%)
  matrix products  9.91 us (6%)
    all_to_all x1, waiting for transfers between devices, body(): lax.all_to_all(send_rows.reshape(groups, held, capacity, features), 'expe...  48.2 us
    ppermute x1, waiting for transfers between devices, body(): lax.ppermute(there.astype(bf16), 'dp', shift).astype(f32)  33.5 us
    add x1, other arithmetic, body(): pair = keep.astype(f32) + got.astype(f32)  10.1 us
    all_to_all x1, starting transfers between devices, body(): lax.all_to_all(send_rows.reshape(groups, held, capacity, features), 'expe...  7.25 us
    all_to_all x1, waiting for transfers between devices, body(): lax.all_to_all(gate_grad, 'expert', split_axis=0, concat_axis=0, tiled=True)  6.51 us
    transpose x1, other arithmetic, body(): weight_grad = sum_here.transpose(1, 0, 2)  6.19 us
    all_to_all x1, waiting for transfers between devices, body(): lax.all_to_all(send_gates.reshape(groups, held, capacity), 'expert', spli...  6.12 us
    ppermute x1, waiting for transfers between devices, body(): got = lax.ppermute(give, 'dp', [(i, i ^ 1) for i in range(dp)])  6 us
  transfers between devices with their start and end apart: 5, of which 5 were waited for; matrix products, arithmetic and copies ran while one was open for 1% of the time, Pallas kernels for 0%

profile of v1, /device:TPU:0, one launch (start us, length us, event | category | flops | bytes accessed | tf_op | source)
XLA Modules:
  0.0 160.6 jit_solution(620544350445839259)
XLA Ops:
  0.7 0.7 fusion.16
  1.6 0.7 select_reduce_fusion.2
  2.3 0.7 multiply_add_fusion
  3.1 2.0 %convolution_convert_fusion = bf16[512,2048]{1,0:T(8,128)(2,1)} fusion(pred[512,128]{1,0:T(8,128)(4,1)S(1)} %fusion.10, bf16[128,2048]{1,0:T(8,128)(2,1)S(1)} %copy-done), kind=kOutput, calls=%fused_computation.10 | convolution fusion | flops 269484032 | bytes 2686976 | tf_op jit(solution)/shard_map/dot_general | solution.py:31
  5.1 7.3 %all-to-all-start.1 = ((bf16[8,2,32,2048]{3,2,1,0:T(8,128)(2,1)}), bf16[8,2,32,2048]{3,2,1,0:T(8,128)(2,1)S(1)}, u32[]{:S(2)}, u32[]{:S(2)}) async-start(bf16[8,2,32,2048]{3,2,1,0:T(8,128)(2,1)} %bitcast), calls=%async_computation.1 | async-start | bytes 4194304 | tf_op jit(solution)/shard_map/all_to_all | solution.py:38
  12.4 48.2 %all-to-all-done.1 = bf16[8,2,32,2048]{3,2,1,0:T(8,128)(2,1)S(1)} async-done(((bf16[8,2,32,2048]{3,2,1,0:T(8,128)(2,1)}), bf16[8,2,32,2048]{3,2,1,0:T(8,128)(2,1)S(1)}, u32[]{:S(2)}, u32[]{:S(2)}) %all-to-all-start.1) | async-done | bytes 2097184 | tf_op jit(solution)/shard_map/all_to_all | solution.py:38
  60.6 5.8 %fusion.7 = (f32[8,2,32]{2,0,1:T(8,128)S(1)}, f32[2,8,32,768]{3,2,1,0:T(8,128)}) fusion(bf16[1,8,2,32,768]{4,3,2,1,0:T(8,128)(2,1)S(1)} %copy-done.2, bf16[2,768,2048]{2,1,0:T(8,128)(2,1)} %param.9, bf16[8,2,32,2048]{3,2,1,0:T(8,128)(2,1)S(1)} %all-to-all-done.1), kind=kOutput, calls=%fused_computation.17 | convolution fusion | flops 1611791872 | bytes 10749952 | tf_op jit(solution)/shard_map/secd,ehd->sech/dot_general | solution.py:66
  66.4 0.6 copy.66
  67.0 3.6 %all-to-all-start.2 = ((f32[8,2,32]{2,1,0:T(2,128)}), f32[8,2,32]{2,1,0:T(2,128)S(1)}, u32[]{:S(2)}, u32[]{:S(2)}) async-start(f32[8,2,32]{2,1,0:T(2,128)} %copy.66), calls=%async_computation.2 | async-start | bytes 16384 | tf_op jit(solution)/shard_map/all_to_all | solution.py:69
  70.6 6.5 %all-to-all-done.2 = f32[8,2,32]{2,1,0:T(2,128)S(1)} async-done(((f32[8,2,32]{2,1,0:T(2,128)}), f32[8,2,32]{2,1,0:T(2,128)S(1)}, u32[]{:S(2)}, u32[]{:S(2)}) %all-to-all-start.2) | async-done | bytes 2080 | tf_op jit(solution)/shard_map/all_to_all | solution.py:69
  77.5 0.7 convert_element_type.64
  78.2 3.5 %all-to-all-start = ((bf16[8,2,32]{2,1,0:T(2,128)(2,1)}), bf16[8,2,32]{2,1,0:T(2,128)(2,1)S(1)}, u32[]{:S(2)}, u32[]{:S(2)}) async-start(bf16[8,2,32]{2,1,0:T(2,128)(2,1)} %convert_element_type.64), calls=%async_computation | async-start | bytes 8192 | tf_op jit(solution)/shard_map/all_to_all | solution.py:35
  81.7 6.1 %all-to-all-done = bf16[8,2,32]{2,1,0:T(2,128)(2,1)S(1)} async-done(((bf16[8,2,32]{2,1,0:T(2,128)(2,1)}), bf16[8,2,32]{2,1,0:T(2,128)(2,1)S(1)}, u32[]{:S(2)}, u32[]{:S(2)}) %all-to-all-start) | async-done | bytes 1056 | tf_op jit(solution)/shard_map/all_to_all | solution.py:35
  87.8 1.9 %bitcast_convert_fusion = bf16[2,2048,768]{1,2,0:T(8,128)(2,1)S(1)} fusion(bf16[8,2,32,2048]{3,2,1,0:T(8,128)(2,1)S(1)} %all-to-all-done.1, f32[8,2,32]{2,1,0:T(2,128)S(1)} %convert_element_type.65, bf16[1,8,2,32,768]{4,3,2,1,0:T(8,128)(2,1)S(1)} %copy-done.2), kind=kOutput, calls=%fused_computation | convolution fusion | flops 1616904192 | bytes 9177088 | tf_op jit(solution)/shard_map/sech,secd->ehd/dot_general | solution.py:53
  89.8 2.3 %constant_dynamic-slice_fusion.1 = (bf16[2,2,1,192,2048]{4,3,2,1,0:T(8,128)(2,1)}, bf16[2,2,1,192,2048]{4,3,2,1,0:T(8,128)(2,1)S(1)}) fusion(bf16[2,2,2,192,2048]{4,3,2,1,0:T(8,128)(2,1)S(1)} %bitcast.48, s32[]{:T(128)S(6)} %select_n.50, s32[]{:T(128)S(6)} %select_n.51), kind=kLoop, calls=%fused_computation.36 | loop fusion | bytes 12582920 | tf_op jit(solution)/shard_map/jit(dynamic_index_in_dim)/dynamic_slice | solution.py:55
  92.0 4.9 %copy.83 = bf16[2,2,1,192,2048]{4,0,3,1,2:T(2,128)(2,1)} copy(bf16[2,2,1,192,2048]{4,3,2,1,0:T(8,128)(2,1)S(1)} %get-tuple-element.26) | data formatting | bytes 6291456 | tf_op jit(solution)/shard_map/jit(dynamic_index_in_dim)/dynamic_slice | solution.py:56
  96.9 6.0 %collective-permute-done = bf16[2,2,192,2048]{3,0,2,1:T(2,128)(2,1)} collective-permute-done((bf16[2,2,192,2048]{3,0,2,1:T(2,128)(2,1)}, bf16[2,2,192,2048]{3,0,2,1:T(2,128)(2,1)}, u32[]{:S(2)}, u32[]{:S(2)}) %collective-permute-start) | collective-permute-done | bytes 3145760 | tf_op jit(solution)/shard_map/ppermute | solution.py:57
  102.9 10.1 %convert_add_fusion = f32[2,2,192,2048]{3,0,2,1:T(2,128)} fusion(bf16[2,2,192,2048]{3,0,2,1:T(2,128)(2,1)} %collective-permute-done, bf16[2,2,1,192,2048]{4,3,2,1,0:T(8,128)(2,1)} %get-tuple-element.25), kind=kLoop, calls=%fused_computation.1 | loop fusion | flops 4718592 | bytes 12582912 | tf_op jit(solution)/shard_map/add | solution.py:58
  113.0 4.6 %fusion.5 = bf16[2,192,2048]{2,0,1:T(2,128)(2,1)} fusion(f32[2,2,192,2048]{3,0,2,1:T(2,128)} %convert_add_fusion, s32[]{:T(128)S(6)} %select_n.55), kind=kLoop, calls=%fused_computation.13 | loop fusion | bytes 3145732 | tf_op jit(solution)/shard_map/convert_element_type | solution.py:63
  117.7 1.5 collective-permute-start.1
  119.2 0.6 subtract_divide_fusion
  119.9 0.9 copy.70
  120.9 33.5 %collective-permute-done.1 = bf16[2,192,2048]{2,0,1:T(2,128)(2,1)} collective-permute-done((bf16[2,192,2048]{2,0,1:T(2,128)(2,1)}, bf16[2,192,2048]{2,0,1:T(2,128)(2,1)}, u32[]{:S(2)}, u32[]{:S(2)}) %collective-permute-start.1) | collective-permute-done | bytes 1572896 | tf_op jit(solution)/shard_map/ppermute | solution.py:63
  154.4 6.2 %fusion.2 = f32[192,2,2048]{2,1,0:T(2,128)} fusion(bf16[2,192,2048]{2,0,1:T(2,128)(2,1)} %collective-permute-done.1, f32[2,2,192,2048]{3,0,2,1:T(2,128)} %convert_add_fusion, s32[]{:T(128)S(6)} %select_n.53), kind=kLoop, calls=%fused_computation.7 | loop fusion | flops 1572864 | bytes 7864324 | tf_op jit(solution)/shard_map/transpose | solution.py:64
  (20 shorter events, 0.8 us)
Async XLA Ops:
  0.6 2.4 %copy-start = (bf16[128,2048]{1,0:T(8,128)(2,1)S(1)}, bf16[128,2048]{1,0:T(8,128)(2,1)}, u32[]{:S(2)}) copy-start(bf16[128,2048]{1,0:T(8,128)(2,1)} %param.5) | copy-start | bytes 1572868
  3.1 9.3 %copy-start.3 = (f32[128,2]{0,1:T(2,128)S(1)}, f32[128,2]{0,1:T(2,128)}, u32[]{:S(2)}) copy-start(f32[128,2]{0,1:T(2,128)} %param.7) | copy-start | bytes 3076
  3.1 57.5 %copy-start.2 = (bf16[1,8,2,32,768]{4,3,2,1,0:T(8,128)(2,1)S(1)}, bf16[1,8,2,32,768]{4,3,2,1,0:T(8,128)(2,1)}, u32[]{:S(2)}) copy-start(bf16[1,8,2,32,768]{4,3,2,1,0:T(8,128)(2,1)} %param.8) | copy-start | bytes 2359300
  5.1 55.5 %all-to-all-start.1 = ((bf16[8,2,32,2048]{3,2,1,0:T(8,128)(2,1)}), bf16[8,2,32,2048]{3,2,1,0:T(8,128)(2,1)S(1)}, u32[]{:S(2)}, u32[]{:S(2)}) async-start(bf16[8,2,32,2048]{3,2,1,0:T(8,128)(2,1)} %bitcast), calls=%async_computation.1 | async-start | bytes 4194304 | tf_op jit(solution)/shard_map/all_to_all | solution.py:38
  67.0 10.2 %all-to-all-start.2 = ((f32[8,2,32]{2,1,0:T(2,128)}), f32[8,2,32]{2,1,0:T(2,128)S(1)}, u32[]{:S(2)}, u32[]{:S(2)}) async-start(f32[8,2,32]{2,1,0:T(2,128)} %copy.66), calls=%async_computation.2 | async-start | bytes 16384 | tf_op jit(solution)/shard_map/all_to_all | solution.py:69
  78.2 9.6 %all-to-all-start = ((bf16[8,2,32]{2,1,0:T(2,128)(2,1)}), bf16[8,2,32]{2,1,0:T(2,128)(2,1)S(1)}, u32[]{:S(2)}, u32[]{:S(2)}) async-start(bf16[8,2,32]{2,1,0:T(2,128)(2,1)} %convert_element_type.64), calls=%async_computation | async-start | bytes 8192 | tf_op jit(solution)/shard_map/all_to_all | solution.py:35
  96.9 6.0 %collective-permute-start = (bf16[2,2,192,2048]{3,0,2,1:T(2,128)(2,1)}, bf16[2,2,192,2048]{3,0,2,1:T(2,128)(2,1)}, u32[]{:S(2)}, u32[]{:S(2)}) collective-permute-start(bf16[2,2,192,2048]{3,0,2,1:T(2,128)(2,1)} %bitcast.47), channel_id=1, source_target_pairs={{0,8},{8,0},{16,24},{24,16},{1,9},{9,1},{17,25},{25,17},{2,10},{10... | collective-permute-start | bytes 9437192 | tf_op jit(solution)/shard_map/ppermute | solution.py:57
  113.0 6.7 %copy-start.1 = (f32[2,8,32,768]{3,2,1,0:T(8,128)S(1)}, f32[2,8,32,768]{3,2,1,0:T(8,128)}, u32[]{:S(2)}) copy-start(f32[2,8,32,768]{3,2,1,0:T(8,128)} %get-tuple-element.28) | copy-start | bytes 4718596
  117.7 36.8 %collective-permute-start.1 = (bf16[2,192,2048]{2,0,1:T(2,128)(2,1)}, bf16[2,192,2048]{2,0,1:T(2,128)(2,1)}, u32[]{:S(2)}, u32[]{:S(2)}) collective-permute-start(bf16[2,192,2048]{2,0,1:T(2,128)(2,1)} %fusion.5), channel_id=1, source_target_pairs={{0,16},{8,24},{16,0},{24,8},{1,17},{9,25},{17,1},{25,9},{2,18},{10... | collective-permute-start | bytes 4718600 | tf_op jit(solution)/shard_map/ppermute | solution.py:63

commit v2 on v0

v2 whole, which is shorter than its diff:
```python
import functools

import jax
import jax.numpy as jnp
from jax import lax
from jax.experimental import pallas as pl
from jax.experimental.pallas import tpu as pltpu
from jax.sharding import PartitionSpec as P

F32, BF16, I32 = jnp.float32, jnp.bfloat16, jnp.int32
PARAMS = pltpu.CompilerParams(vmem_limit_bytes=24 * 1024 * 1024)


def cost(flops, nbytes):
    return pl.CostEstimate(flops=flops, bytes_accessed=nbytes, transcendentals=0)


def nbytes(shapes):
    return sum(x.size * x.dtype.itemsize for x in jax.tree.leaves(shapes))


def call(kernel, outs, *args, flops=0, **kw):
    return pl.pallas_call(
        kernel,
        out_shape=outs,
        compiler_params=PARAMS,
        cost_estimate=cost(flops, nbytes(args) + nbytes(outs)),
        **kw,
    )(*args)


def gates_of(probs_ref):
    probs = probs_ref[...]
    total = jnp.sum(probs, axis=0, keepdims=True)
    gates = probs / total
    return total, gates, gates.astype(BF16).astype(F32)


def route_kernel(experts, capacity, parts, ids_ref, probs_ref, rows_ref, flat_ref, *out_refs):
    chosen, tokens = ids_ref.shape
    rows = experts * capacity // parts
    _, _, word = gates_of(probs_ref)
    ids = ids_ref[...]
    expert = lax.broadcasted_iota(I32, (experts, tokens), 0)
    named = [ids[k : k + 1] == expert for k in range(chosen)]
    hits = functools.reduce(jnp.add, [n.astype(F32) for n in named]).astype(BF16)
    earlier = lax.broadcasted_iota(I32, (tokens, tokens), 0) < lax.broadcasted_iota(
        I32, (tokens, tokens), 1
    )
    before = jnp.dot(hits, earlier.astype(F32).astype(BF16), preferred_element_type=F32)
    flat = [
        ids[k : k + 1] * capacity
        + jnp.sum(jnp.where(named[k], before, 0.0), axis=0, keepdims=True).astype(I32)
        for k in range(chosen)
    ]
    for k in range(chosen):
        flat_ref[k : k + 1, :] = flat[k]
    me = lax.axis_index("expert") if parts > 1 else 0
    blocks = []
    for part in range(parts):
        slot = lax.broadcasted_iota(I32, (rows, tokens), 0) + (me ^ part) * rows
        blocks.append(
            functools.reduce(
                jnp.add,
                [jnp.where(flat[k] == slot, word[k : k + 1], 0.0) for k in range(chosen)],
            ).astype(BF16)
        )
    place = jnp.concatenate(blocks, axis=0)
    start = 0
    for chunk in range(len(out_refs) // parts):
        outs = out_refs[chunk * parts : (chunk + 1) * parts]
        width = outs[0].shape[1]
        scaled = jnp.dot(
            place, rows_ref[:, start : start + width], preferred_element_type=F32
        ).astype(BF16)
        for part in range(parts):
            outs[part][...] = scaled[part * rows : (part + 1) * rows]
        start += width


def turn_kernel(dp, hidden_ref, out_ref):
    parts, held, _, units = hidden_ref.shape
    share, across = units // dp, dp // 2
    me = lax.axis_index("expert") if parts > 1 else 0
    mine = lax.axis_index("dp")
    core, row = mine % 2, mine // 2
    for e in range(held):
        stacked = jnp.concatenate([hidden_ref[me ^ part, e] for part in range(parts)], axis=0)
        turned = stacked.T
        for piece in range(dp):
            other = (piece % 2) ^ core
            step = (piece // 2 - row + across) % across
            out_ref[e, other, step] = turned[piece * share : (piece + 1) * share]


def stacked_rows(part_refs, held, e):
    own = part_refs[0].shape[0] // held
    return jnp.concatenate([ref[e * own : (e + 1) * own, :] for ref in part_refs], axis=0)


def term_kernel(turned_ref, *refs):
    part_refs, keep_ref, give_ref = refs[:-2], refs[-2], refs[-1]
    held, _, across, share, slots = turned_ref.shape
    for e in range(held):
        scaled = stacked_rows(part_refs, held, e)
        for other, ref in ((1, give_ref), (0, keep_ref)):
            left = turned_ref[e, other].reshape(across * share, slots)
            term = jnp.dot(left, scaled, preferred_element_type=F32).astype(BF16)
            for step in range(across):
                ref[step, e] = term[step * share : (step + 1) * share]


def pair_kernel(keep_ref, got_ref, *out_refs):
    for step, ref in enumerate(out_refs, 1):
        ref[...] = (keep_ref[step].astype(F32) + got_ref[step].astype(F32)).astype(BF16)


def last_kernel(others, keep_ref, got_ref, *refs):
    out_ref = refs[-1]
    for e in range(keep_ref.shape[1]):
        total = keep_ref[0, e].astype(F32) + got_ref[0, e].astype(F32)
        for ref in refs[:others]:
            total = total + ref[e].astype(F32)
        out_ref[:, e, :] = total


def raw_kernel(parts, first, final, weight_ref, *refs):
    part_refs, refs = refs[:parts], refs[parts:]
    if not first:
        acc_ref, refs = refs[0], refs[1:]
    held = weight_ref.shape[0]
    for e in range(held):
        raw = lax.dot_general(
            stacked_rows(part_refs, held, e),
            weight_ref[e],
            (((1,), (1,)), ((), ())),
            preferred_element_type=F32,
        )
        if not first:
            raw = raw + acc_ref[e]
        if not final:
            refs[0][e] = raw
            continue
        hidden_ref, grad_ref, sums_ref = refs
        me = lax.axis_index("expert") if parts > 1 else 0
        own = hidden_ref.shape[2]
        units = raw.shape[1]
        for part in range(parts):
            block = raw[part * own : (part + 1) * own]
            grad_ref[me ^ part, e] = block.astype(BF16)
            product = block * hidden_ref[me ^ part, e].astype(F32)
            folded = functools.reduce(
                jnp.add, [product[:, i : i + 128] for i in range(0, units, 128)]
            )
            sums_ref[me ^ part, e] = jnp.sum(folded, axis=1, keepdims=True)


def prob_kernel(flat_ref, probs_ref, returned_ref, out_ref):
    total, gates, word = gates_of(probs_ref)
    chosen, tokens = flat_ref.shape
    slots = returned_ref.shape[0]
    slot = lax.broadcasted_iota(I32, (slots, tokens), 0)
    returned = returned_ref[...]
    picked = [
        jnp.sum(jnp.where(flat_ref[k : k + 1, :] == slot, returned, 0.0), axis=0, keepdims=True)
        / word[k : k + 1]
        for k in range(chosen)
    ]
    mixed = functools.reduce(jnp.add, [gates[k : k + 1] * picked[k] for k in range(chosen)])
    for k in range(chosen):
        out_ref[k : k + 1, :] = (picked[k] - mixed) / total


def chunks_of(features):
    quarter = features // 4
    return [quarter] * 4


def body(grad_out, route_ids, route_probs, hidden, w_down):
    groups = lax.axis_size("expert")
    dp = lax.axis_size("dp")
    held, units, features = w_down.shape
    capacity = hidden.shape[3]
    experts = groups * held
    slots = experts * capacity
    tokens, chosen = route_ids.shape
    share, across = units // dp, dp // 2
    sds = jax.ShapeDtypeStruct
    direct = groups <= 8
    parts = groups if direct else 1
    rows = slots // parts
    widths = chunks_of(features)
    count = len(widths)

    ids, probs = route_ids.T, route_probs.T
    flat, *sent = call(
        functools.partial(route_kernel, experts, capacity, parts),
        [sds((chosen, tokens), I32)] + [sds((rows, w), BF16) for w in widths for _ in range(parts)],
        ids,
        probs,
        grad_out,
        flops=2 * slots * tokens * features,
    )

    def exchanged(blocks):
        if direct:
            return [blocks[0]] + [
                lax.ppermute(blocks[k], "expert", [(i, i ^ k) for i in range(groups)])
                for k in range(1, parts)
            ]
        width = blocks[0].shape[1]
        got = lax.all_to_all(
            blocks[0].reshape(groups, held, capacity, width),
            "expert",
            split_axis=0,
            concat_axis=0,
            tiled=True,
        )
        return [got.transpose(1, 0, 2, 3).reshape(slots, width)]

    if direct:
        saved = hidden[0]
    else:
        saved = hidden[0].transpose(1, 0, 2, 3).reshape(1, held, groups * capacity, units)
    per_expert = slots // held
    turned = call(
        functools.partial(turn_kernel, dp),
        sds((held, 2, across, share, per_expert), BF16),
        saved,
    )

    arrived = [exchanged(sent[c * parts : (c + 1) * parts]) for c in range(count)]
    flops = [2 * slots * units * w for w in widths]
    weight_grad, raw, start = None, None, 0
    for c, width in enumerate(widths):
        piece = sds((across, held, share, width), BF16)
        keep, give = call(term_kernel, [piece, piece], turned, *arrived[c], flops=flops[c])
        got = lax.ppermute(give, "dp", [(i, i ^ 1) for i in range(dp)])

        final = c == count - 1
        if final:
            outs = [sds(saved.shape, BF16), sds((parts, held, rows // held, 1), F32)]
            extra = [saved]
        else:
            outs, extra = [sds((held, per_expert, units), F32)], []
        extra = extra if c == 0 else [raw] + extra
        whole = pl.BlockSpec(memory_space=pltpu.VMEM)
        made = call(
            functools.partial(raw_kernel, parts, c == 0, final),
            outs,
            w_down,
            *arrived[c],
            *extra,
            flops=flops[c],
            grid=(1,),
            in_specs=[pl.BlockSpec((held, units, width), lambda i, at=start // width: (0, 0, at))]
            + [whole] * (parts + len(extra)),
            out_specs=[whole] * len(outs),
        )
        if final:
            hidden_grad, sums = made
        else:
            raw = made[0]

        piece = sds((held, share, width), BF16)
        pairs = call(pair_kernel, [piece] * (across - 1), keep, got)
        others = []
        for step in range(1, across):
            shift = [(2 * r + i, 2 * ((r + step) % across) + i) for r in range(across) for i in range(2)]
            others.append(lax.ppermute(pairs[step - 1], "dp", shift))
        first = pl.BlockSpec((1, held, share, width), lambda i: (0, 0, 0, 0))
        before = [] if c == 0 else [weight_grad]
        weight_grad = call(
            functools.partial(last_kernel, len(others)),
            sds((share, held, features), F32),
            keep,
            got,
            *others,
            *before,
            grid=(1,),
            in_specs=[first, first]
            + [whole] * len(others)
            + [pl.BlockSpec(memory_space=pl.ANY)] * len(before),
            out_specs=pl.BlockSpec((share, held, width), lambda i, at=start // width: (0, 0, at)),
            input_output_aliases={2 + len(others): 0} if before else {},
        )
        start += width

    if direct:
        sums = sums.reshape(groups, rows)
    else:
        sums = sums.reshape(held, groups, capacity).transpose(1, 0, 2).reshape(groups, -1)
        hidden_grad = hidden_grad.reshape(held, groups, capacity, units).transpose(1, 0, 2, 3)
    returned = lax.all_to_all(sums, "expert", split_axis=0, concat_axis=0, tiled=True)
    prob_grad = call(
        prob_kernel, sds((chosen, tokens), F32), flat, probs, returned.reshape(slots, 1)
    ).T
    return (hidden_grad[None], prob_grad, weight_grad)


def solution(mesh):
    in_specs = (
        P(("dp", "expert"), None),
        P(("dp", "expert"), None),
        P(("dp", "expert"), None),
        P("dp", None, "expert", None, None),
        P("expert", None, None),
    )
    out_specs = (
        P("dp", None, "expert", None, None),
        P(("dp", "expert"), None),
        P("dp", "expert", None),
    )
    return jax.shard_map(body, mesh=mesh, in_specs=in_specs, out_specs=out_specs, check_vma=False)
```

time: 233 us -> 107 us (0.46)
  waiting for transfers between devices: 154 us -> 21.3 us
  starting transfers between devices: 15.5 us -> 48.2 us
  local copies, waits for them, and re-layouts: 32 us -> 4.96 us
  Pallas kernels: 0 us -> 19.7 us
  between operations: 14.9 us -> 0.88 us
  blocking collectives: 0 us -> 10.4 us
  matrix products: 9.59 us -> 0 us
  other arithmetic: 6.89 us -> 0.81 us
    unnamed x2 -> x0, waiting for transfers between devices: 100 us -> none
    all_to_all x3 -> x0, waiting for transfers between devices: 53.5 us -> none  [the longest x1 47.6 us: body(): lax.all_to_all(send_rows.reshape(groups, held, capacity, features), 'expe...]
    ppermute x0 -> x36, starting transfers between devices: none -> 48.2 us  [the longest x28 44 us: exchanged(): lax.ppermute(blocks[k], 'expert', [(i, i ^ k) for i in range(groups)])]
    ppermute x0 -> x36, waiting for transfers between devices: none -> 21.3 us  [the longest x28 14.1 us: exchanged(): lax.ppermute(blocks[k], 'expert', [(i, i ^ k) for i in range(groups)])]
    pallas_call x0 -> x19, Pallas kernels: none -> 19.7 us  [call(): pl.pallas_call(kernel, out_shape=outs, compiler_params=PARAMS, cost_estim...]
    convert_element_type x2 -> x0, local copies, waits for them, and re-layouts: 16.4 us -> none  [the longest x1 16.4 us: body(): weight_term.astype(jnp.bfloat16)]
    all_to_all x3 -> x0, starting transfers between devices: 15.4 us -> none  [the longest x1 7.25 us: body(): lax.all_to_all(send_gates.reshape(groups, held, capacity), 'expert', spli...]
    all_to_all x0 -> x1, blocking collectives: none -> 10.4 us  [body(): lax.all_to_all(sums, 'expert', split_axis=0, concat_axis=0, tiled=True)]
  transfers between devices with their start and end apart: 4 -> 36, of which waited for: 4 -> 8; matrix products, arithmetic and copies ran while one was open for 6% -> 1% of each run, Pallas kernels for 0% -> 16%
where the time goes in v2:
time: 107 us; the launch traced here: 106 us
  starting transfers between devices  48.2 us (45%)
  waiting for transfers between devices  21.3 us (20%)
  Pallas kernels  19.7 us (18%)
  blocking collectives  10.4 us (10%)
  local copies, waits for them, and re-layouts  4.96 us (5%)
    ppermute x28, starting transfers between devices, exchanged(): lax.ppermute(blocks[k], 'expert', [(i, i ^ k) for i in range(groups)])  44 us
    pallas_call x19, Pallas kernels, call(): pl.pallas_call(kernel, out_shape=outs, compiler_params=PARAMS, cost_estim...  19.7 us
    ppermute x28, waiting for transfers between devices, exchanged(): lax.ppermute(blocks[k], 'expert', [(i, i ^ k) for i in range(groups)])  14.1 us
    all_to_all x1, blocking collectives, body(): lax.all_to_all(sums, 'expert', split_axis=0, concat_axis=0, tiled=True)  10.4 us
    ppermute x4, waiting for transfers between devices, body(): others.append(lax.ppermute(pairs[step - 1], 'dp', shift))  7.22 us
    unnamed x32, local copies, waits for them, and re-layouts  4.17 us
    ppermute x4, starting transfers between devices, body(): others.append(lax.ppermute(pairs[step - 1], 'dp', shift))  4.09 us
  transfers between devices with their start and end apart: 36, of which 8 were waited for; matrix products, arithmetic and copies ran while one was open for 1% of the time, Pallas kernels for 16%

profile of v2, /device:TPU:0, one launch (start us, length us, event | category | flops | bytes accessed | tf_op | source)
XLA Modules:
  0.0 106.3 jit_solution(15142843583083554384)
XLA Ops:
  3.9 3.0 %collective-permute-start.21 = (bf16[64,512]{1,0:T(8,128)(2,1)S(1)}, bf16[64,512]{1,0:T(8,128)(2,1)S(1)}, u32[]{:S(2)}, u32[]{:S(2)}) collective-permute-start(bf16[64,512]{1,0:T(8,128)(2,1)S(1)} %get-tuple-element.71), channel_id=1, source_target_pairs={{0,1},{1,0},{2,3},{3,2},{4,5},{5,4},{6,7},{7,6},{8,9},{9,8},{10,11... | collective-permute-start | bytes 196616 | tf_op jit(solution)/shard_map/ppermute | solution.py:208
  6.9 1.6 %collective-permute-start.22 = (bf16[64,512]{1,0:T(8,128)(2,1)S(1)}, bf16[64,512]{1,0:T(8,128)(2,1)S(1)}, u32[]{:S(2)}, u32[]{:S(2)}) collective-permute-start(bf16[64,512]{1,0:T(8,128)(2,1)S(1)} %get-tuple-element.72), channel_id=1, source_target_pairs={{0,2},{1,3},{2,0},{3,1},{4,6},{5,7},{6,4},{7,5},{8,10},{9,11},{10,... | collective-permute-start | bytes 196616 | tf_op jit(solution)/shard_map/ppermute | solution.py:208
  8.5 3.0 %collective-permute-start.24 = (bf16[64,512]{1,0:T(8,128)(2,1)S(1)}, bf16[64,512]{1,0:T(8,128)(2,1)S(1)}, u32[]{:S(2)}, u32[]{:S(2)}) collective-permute-start(bf16[64,512]{1,0:T(8,128)(2,1)S(1)} %get-tuple-element.74), channel_id=1, source_target_pairs={{0,4},{1,5},{2,6},{3,7},{4,0},{5,1},{6,2},{7,3},{8,12},{9,13},{10,... | collective-permute-start | bytes 196616 | tf_op jit(solution)/shard_map/ppermute | solution.py:208
  12.7 3.6 %collective-permute-start.26 = (bf16[64,512]{1,0:T(8,128)(2,1)S(1)}, bf16[64,512]{1,0:T(8,128)(2,1)S(1)}, u32[]{:S(2)}, u32[]{:S(2)}) collective-permute-start(bf16[64,512]{1,0:T(8,128)(2,1)S(1)} %get-tuple-element.76), channel_id=1, source_target_pairs={{0,6},{1,7},{2,4},{3,5},{4,2},{5,3},{6,0},{7,1},{8,14},{9,15},{10,... | collective-permute-start | bytes 196616 | tf_op jit(solution)/shard_map/ppermute | solution.py:208
  16.4 1.6 %collective-permute-start.14 = (bf16[64,512]{1,0:T(8,128)(2,1)S(1)}, bf16[64,512]{1,0:T(8,128)(2,1)S(1)}, u32[]{:S(2)}, u32[]{:S(2)}) collective-permute-start(bf16[64,512]{1,0:T(8,128)(2,1)S(1)} %get-tuple-element.63), channel_id=1, source_target_pairs={{0,1},{1,0},{2,3},{3,2},{4,5},{5,4},{6,7},{7,6},{8,9},{9,8},{10,11... | collective-permute-start | bytes 196616 | tf_op jit(solution)/shard_map/ppermute | solution.py:208
  18.1 3.5 %collective-permute-done.25.refs_5_ = bf16[64,512]{1,0:T(8,128)(2,1)S(1)} collective-permute-done((bf16[64,512]{1,0:T(8,128)(2,1)S(1)}, bf16[64,512]{1,0:T(8,128)(2,1)S(1)}, u32[]{:S(2)}, u32[]{:S(2)}) %collective-permute-start.25) | collective-permute-done | bytes 65568 | tf_op jit(solution)/shard_map/ppermute | solution.py:208
  22.0 3.4 %collective-permute-start.17 = (bf16[64,512]{1,0:T(8,128)(2,1)S(1)}, bf16[64,512]{1,0:T(8,128)(2,1)S(1)}, u32[]{:S(2)}, u32[]{:S(2)}) collective-permute-start(bf16[64,512]{1,0:T(8,128)(2,1)S(1)} %get-tuple-element.66), channel_id=1, source_target_pairs={{0,4},{1,5},{2,6},{3,7},{4,0},{5,1},{6,2},{7,3},{8,12},{9,13},{10,... | collective-permute-start | bytes 196616 | tf_op jit(solution)/shard_map/ppermute | solution.py:208
  27.8 3.7 %collective-permute-start.20 = (bf16[64,512]{1,0:T(8,128)(2,1)S(1)}, bf16[64,512]{1,0:T(8,128)(2,1)S(1)}, u32[]{:S(2)}, u32[]{:S(2)}) collective-permute-start(bf16[64,512]{1,0:T(8,128)(2,1)S(1)} %get-tuple-element.69), channel_id=1, source_target_pairs={{0,7},{1,6},{2,5},{3,4},{4,3},{5,2},{6,1},{7,0},{8,15},{9,14},{10,... | collective-permute-start | bytes 196616 | tf_op jit(solution)/shard_map/ppermute | solution.py:208
  31.5 2.6 %collective-permute-start.11 = (bf16[64,512]{1,0:T(8,128)(2,1)S(1)}, bf16[64,512]{1,0:T(8,128)(2,1)S(1)}, u32[]{:S(2)}, u32[]{:S(2)}) collective-permute-start(bf16[64,512]{1,0:T(8,128)(2,1)S(1)} %get-tuple-element.59), channel_id=1, source_target_pairs={{0,5},{1,4},{2,7},{3,6},{4,1},{5,0},{6,3},{7,2},{8,13},{9,12},{10,... | collective-permute-start | bytes 196616 | tf_op jit(solution)/shard_map/ppermute | solution.py:208
  34.0 3.5 %collective-permute-done.18.refs_5_ = bf16[64,512]{1,0:T(8,128)(2,1)S(1)} collective-permute-done((bf16[64,512]{1,0:T(8,128)(2,1)S(1)}, bf16[64,512]{1,0:T(8,128)(2,1)S(1)}, u32[]{:S(2)}, u32[]{:S(2)}) %collective-permute-start.18) | collective-permute-done | bytes 65568 | tf_op jit(solution)/shard_map/ppermute | solution.py:208
  37.6 2.1 %collective-permute-start.12 = (bf16[64,512]{1,0:T(8,128)(2,1)S(1)}, bf16[64,512]{1,0:T(8,128)(2,1)S(1)}, u32[]{:S(2)}, u32[]{:S(2)}) collective-permute-start(bf16[64,512]{1,0:T(8,128)(2,1)S(1)} %get-tuple-element.60), channel_id=1, source_target_pairs={{0,6},{1,7},{2,4},{3,5},{4,2},{5,3},{6,0},{7,1},{8,14},{9,15},{10,... | collective-permute-start | bytes 196616 | tf_op jit(solution)/shard_map/ppermute | solution.py:208
  39.7 2.8 %collective-permute-start.13 = (bf16[64,512]{1,0:T(8,128)(2,1)S(1)}, bf16[64,512]{1,0:T(8,128)(2,1)S(1)}, u32[]{:S(2)}, u32[]{:S(2)}) collective-permute-start(bf16[64,512]{1,0:T(8,128)(2,1)S(1)} %get-tuple-element.61), channel_id=1, source_target_pairs={{0,7},{1,6},{2,5},{3,4},{4,3},{5,2},{6,1},{7,0},{8,15},{9,14},{10,... | collective-permute-start | bytes 196616 | tf_op jit(solution)/shard_map/ppermute | solution.py:208
  43.3 2.7 %collective-permute-done.11.refs_5_ = bf16[64,512]{1,0:T(8,128)(2,1)S(1)} collective-permute-done((bf16[64,512]{1,0:T(8,128)(2,1)S(1)}, bf16[64,512]{1,0:T(8,128)(2,1)S(1)}, u32[]{:S(2)}, u32[]{:S(2)}) %collective-permute-start.11) | collective-permute-done | bytes 65568 | tf_op jit(solution)/shard_map/ppermute | solution.py:208
  47.0 2.5 %collective-permute-start.1 = (bf16[64,512]{1,0:T(8,128)(2,1)S(1)}, bf16[64,512]{1,0:T(8,128)(2,1)S(1)}, u32[]{:S(2)}, u32[]{:S(2)}) collective-permute-start(bf16[64,512]{1,0:T(8,128)(2,1)S(1)} %get-tuple-element.48), channel_id=1, source_target_pairs={{0,2},{1,3},{2,0},{3,1},{4,6},{5,7},{6,4},{7,5},{8,10},{9,11},{10,... | collective-permute-start | bytes 196616 | tf_op jit(solution)/shard_map/ppermute | solution.py:208
  52.0 2.4 %collective-permute-start.3 = (bf16[64,512]{1,0:T(8,128)(2,1)S(1)}, bf16[64,512]{1,0:T(8,128)(2,1)S(1)}, u32[]{:S(2)}, u32[]{:S(2)}) collective-permute-start(bf16[64,512]{1,0:T(8,128)(2,1)S(1)} %get-tuple-element.50), channel_id=1, source_target_pairs={{0,4},{1,5},{2,6},{3,7},{4,0},{5,1},{6,2},{7,3},{8,12},{9,13},{10,... | collective-permute-start | bytes 196616 | tf_op jit(solution)/shard_map/ppermute | solution.py:208
  55.9 2.3 %collective-permute-start.5 = (bf16[64,512]{1,0:T(8,128)(2,1)S(1)}, bf16[64,512]{1,0:T(8,128)(2,1)S(1)}, u32[]{:S(2)}, u32[]{:S(2)}) collective-permute-start(bf16[64,512]{1,0:T(8,128)(2,1)S(1)} %get-tuple-element.52), channel_id=1, source_target_pairs={{0,6},{1,7},{2,4},{3,5},{4,2},{5,3},{6,0},{7,1},{8,14},{9,15},{10,... | collective-permute-start | bytes 196616 | tf_op jit(solution)/shard_map/ppermute | solution.py:208
  66.8 2.1 %collective-permute-start.35 = (bf16[2,192,512]{2,1,0:T(8,128)(2,1)}, bf16[2,192,512]{2,1,0:T(8,128)(2,1)}, u32[]{:S(2)}, u32[]{:S(2)}) collective-permute-start(bf16[2,192,512]{2,1,0:T(8,128)(2,1)} %shard_map.90), channel_id=1, source_target_pairs={{0,16},{8,24},{16,0},{24,8},{1,17},{9,25},{17,1},{25,9},{2,18},{10... | collective-permute-start | bytes 1179656 | tf_op jit(solution)/shard_map/ppermute | solution.py:270
  70.7 2.0 %collective-permute-start.31 = (bf16[2,192,512]{2,1,0:T(8,128)(2,1)}, bf16[2,192,512]{2,1,0:T(8,128)(2,1)}, u32[]{:S(2)}, u32[]{:S(2)}) collective-permute-start(bf16[2,192,512]{2,1,0:T(8,128)(2,1)} %shard_map.86), channel_id=1, source_target_pairs={{0,16},{8,24},{16,0},{24,8},{1,17},{9,25},{17,1},{25,9},{2,18},{10... | collective-permute-start | bytes 1179656 | tf_op jit(solution)/shard_map/ppermute | solution.py:270
  78.0 10.4 %all_to_all.9 = f32[8,1,64]{2,1,0:T(1,128)S(1)} all-to-all(f32[8,1,64]{2,1,0:T(1,128)S(1)} %bitcast.13), channel_id=1, replica_groups=mesh['dp'=4,'expert'=8] {'expert'}, dimensions={0} | all-to-all | bytes 4096 | tf_op jit(solution)/shard_map/all_to_all | solution.py:294
  90.5 2.1 %shard_map.91.refs_1_ = f32[192,2,2048]{2,1,0:T(2,128)} custom-call(bf16[2,2,192,512]{3,2,1,0:T(8,128)(2,1)S(1)} %get-tuple-element.87.keep_ref, bf16[2,2,192,512]{3,2,1,0:T(8,128)(2,1)S(1)} %collective-permute-done.34.got_ref, bf16[2,192,512]{2,1,0:T(8,128)(2,1)} %collective-permute-done.35.refs_0_), custom_call_target="tpu_custom_call" | custom-call | bytes 5111808 | tf_op jit(solution)/shard_map/pallas_call | solution.py:23
  92.6 2.2 %shard_map.92.refs_1_ = f32[192,2,2048]{2,1,0:T(2,128)} custom-call(bf16[2,2,192,512]{3,2,1,0:T(8,128)(2,1)S(1)} %get-tuple-element.85.keep_ref, bf16[2,2,192,512]{3,2,1,0:T(8,128)(2,1)S(1)} %copy-done.5, bf16[2,192,512]{2,1,0:T(8,128)(2,1)} %collective-permute-done.33.refs_0_, f32[192,2,2048]{2,1,0:T(2,128)} %shard_map.91.refs_1_), custom_call_target="tpu_custom_call", output_to_operand_aliasing={{}: (3, {})} | custom-call | bytes 8257536 | tf_op jit(solution)/shard_map/pallas_call | solution.py:23
  96.0 2.1 %shard_map.93.refs_1_ = f32[192,2,2048]{2,1,0:T(2,128)} custom-call(bf16[2,2,192,512]{3,2,1,0:T(8,128)(2,1)S(1)} %get-tuple-element.83.keep_ref, bf16[2,2,192,512]{3,2,1,0:T(8,128)(2,1)S(1)} %copy-done.3, bf16[2,192,512]{2,1,0:T(8,128)(2,1)} %collective-permute-done.31.refs_0_, f32[192,2,2048]{2,1,0:T(2,128)} %shard_map.92.refs_1_), custom_call_target="tpu_custom_call", output_to_operand_aliasing={{}: (3, {})} | custom-call | bytes 8257536 | tf_op jit(solution)/shard_map/pallas_call | solution.py:23
  98.1 6.1 %collective-permute-done.29.refs_0_ = bf16[2,192,512]{2,1,0:T(8,128)(2,1)} collective-permute-done((bf16[2,192,512]{2,1,0:T(8,128)(2,1)}, bf16[2,192,512]{2,1,0:T(8,128)(2,1)}, u32[]{:S(2)}, u32[]{:S(2)}) %collective-permute-start.29) | collective-permute-done | bytes 393248 | tf_op jit(solution)/shard_map/ppermute | solution.py:270
  104.2 2.1 %shard_map.94 = f32[192,2,2048]{2,1,0:T(2,128)} custom-call(bf16[2,2,192,512]{3,2,1,0:T(8,128)(2,1)S(1)} %copy-done.7, bf16[2,2,192,512]{3,2,1,0:T(8,128)(2,1)S(1)} %copy-done.9, bf16[2,192,512]{2,1,0:T(8,128)(2,1)} %collective-permute-done.29.refs_0_, f32[192,2,2048]{2,1,0:T(2,128)} %shard_map.93.refs_1_), custom_call_target="tpu_custom_call", output_to_operand_aliasing={{}: (3, {})} | custom-call | bytes 8257536 | tf_op jit(solution)/shard_map/pallas_call | solution.py:23
  (106 shorter events, 31.9 us)
Async XLA Ops:
  6.9 9.5 %collective-permute-start.22 = (bf16[64,512]{1,0:T(8,128)(2,1)S(1)}, bf16[64,512]{1,0:T(8,128)(2,1)S(1)}, u32[]{:S(2)}, u32[]{:S(2)}) collective-permute-start(bf16[64,512]{1,0:T(8,128)(2,1)S(1)} %get-tuple-element.72), channel_id=1, source_target_pairs={{0,2},{1,3},{2,0},{3,1},{4,6},{5,7},{6,4},{7,5},{8,10},{9,11},{10,... | collective-permute-start | bytes 196616 | tf_op jit(solution)/shard_map/ppermute | solution.py:208
  8.5 9.6 %collective-permute-start.24 = (bf16[64,512]{1,0:T(8,128)(2,1)S(1)}, bf16[64,512]{1,0:T(8,128)(2,1)S(1)}, u32[]{:S(2)}, u32[]{:S(2)}) collective-permute-start(bf16[64,512]{1,0:T(8,128)(2,1)S(1)} %get-tuple-element.74), channel_id=1, source_target_pairs={{0,4},{1,5},{2,6},{3,7},{4,0},{5,1},{6,2},{7,3},{8,12},{9,13},{10,... | collective-permute-start | bytes 196616 | tf_op jit(solution)/shard_map/ppermute | solution.py:208
  11.5 10.2 %collective-permute-start.25 = (bf16[64,512]{1,0:T(8,128)(2,1)S(1)}, bf16[64,512]{1,0:T(8,128)(2,1)S(1)}, u32[]{:S(2)}, u32[]{:S(2)}) collective-permute-start(bf16[64,512]{1,0:T(8,128)(2,1)S(1)} %get-tuple-element.75), channel_id=1, source_target_pairs={{0,5},{1,4},{2,7},{3,6},{4,1},{5,0},{6,3},{7,2},{8,13},{9,12},{10,... | collective-permute-start | bytes 196616 | tf_op jit(solution)/shard_map/ppermute | solution.py:208
  12.7 9.3 %collective-permute-start.26 = (bf16[64,512]{1,0:T(8,128)(2,1)S(1)}, bf16[64,512]{1,0:T(8,128)(2,1)S(1)}, u32[]{:S(2)}, u32[]{:S(2)}) collective-permute-start(bf16[64,512]{1,0:T(8,128)(2,1)S(1)} %get-tuple-element.76), channel_id=1, source_target_pairs={{0,6},{1,7},{2,4},{3,5},{4,2},{5,3},{6,0},{7,1},{8,14},{9,15},{10,... | collective-permute-start | bytes 196616 | tf_op jit(solution)/shard_map/ppermute | solution.py:208
  16.3 9.0 %collective-permute-start.27 = (bf16[64,512]{1,0:T(8,128)(2,1)S(1)}, bf16[64,512]{1,0:T(8,128)(2,1)S(1)}, u32[]{:S(2)}, u32[]{:S(2)}) collective-permute-start(bf16[64,512]{1,0:T(8,128)(2,1)S(1)} %get-tuple-element.77), channel_id=1, source_target_pairs={{0,7},{1,6},{2,5},{3,4},{4,3},{5,2},{6,1},{7,0},{8,15},{9,14},{10,... | collective-permute-start | bytes 196616 | tf_op jit(solution)/shard_map/ppermute | solution.py:208
  16.4 10.0 %collective-permute-start.14 = (bf16[64,512]{1,0:T(8,128)(2,1)S(1)}, bf16[64,512]{1,0:T(8,128)(2,1)S(1)}, u32[]{:S(2)}, u32[]{:S(2)}) collective-permute-start(bf16[64,512]{1,0:T(8,128)(2,1)S(1)} %get-tuple-element.63), channel_id=1, source_target_pairs={{0,1},{1,0},{2,3},{3,2},{4,5},{5,4},{6,7},{7,6},{8,9},{9,8},{10,11... | collective-permute-start | bytes 196616 | tf_op jit(solution)/shard_map/ppermute | solution.py:208
  18.0 9.7 %collective-permute-start.15 = (bf16[64,512]{1,0:T(8,128)(2,1)S(1)}, bf16[64,512]{1,0:T(8,128)(2,1)S(1)}, u32[]{:S(2)}, u32[]{:S(2)}) collective-permute-start(bf16[64,512]{1,0:T(8,128)(2,1)S(1)} %get-tuple-element.64), channel_id=1, source_target_pairs={{0,2},{1,3},{2,0},{3,1},{4,6},{5,7},{6,4},{7,5},{8,10},{9,11},{10,... | collective-permute-start | bytes 196616 | tf_op jit(solution)/shard_map/ppermute | solution.py:208
  21.7 9.8 %collective-permute-start.16 = (bf16[64,512]{1,0:T(8,128)(2,1)S(1)}, bf16[64,512]{1,0:T(8,128)(2,1)S(1)}, u32[]{:S(2)}, u32[]{:S(2)}) collective-permute-start(bf16[64,512]{1,0:T(8,128)(2,1)S(1)} %get-tuple-element.65), channel_id=1, source_target_pairs={{0,3},{1,2},{2,1},{3,0},{4,7},{5,6},{6,5},{7,4},{8,11},{9,10},{10,... | collective-permute-start | bytes 196616 | tf_op jit(solution)/shard_map/ppermute | solution.py:208
  22.0 9.5 %collective-permute-start.17 = (bf16[64,512]{1,0:T(8,128)(2,1)S(1)}, bf16[64,512]{1,0:T(8,128)(2,1)S(1)}, u32[]{:S(2)}, u32[]{:S(2)}) collective-permute-start(bf16[64,512]{1,0:T(8,128)(2,1)S(1)} %get-tuple-element.66), channel_id=1, source_target_pairs={{0,4},{1,5},{2,6},{3,7},{4,0},{5,1},{6,2},{7,3},{8,12},{9,13},{10,... | collective-permute-start | bytes 196616 | tf_op jit(solution)/shard_map/ppermute | solution.py:208
  25.4 12.2 %collective-permute-start.18 = (bf16[64,512]{1,0:T(8,128)(2,1)S(1)}, bf16[64,512]{1,0:T(8,128)(2,1)S(1)}, u32[]{:S(2)}, u32[]{:S(2)}) collective-permute-start(bf16[64,512]{1,0:T(8,128)(2,1)S(1)} %get-tuple-element.67), channel_id=1, source_target_pairs={{0,5},{1,4},{2,7},{3,6},{4,1},{5,0},{6,3},{7,2},{8,13},{9,12},{10,... | collective-permute-start | bytes 196616 | tf_op jit(solution)/shard_map/ppermute | solution.py:208
  26.4 13.3 %collective-permute-start.19 = (bf16[64,512]{1,0:T(8,128)(2,1)S(1)}, bf16[64,512]{1,0:T(8,128)(2,1)S(1)}, u32[]{:S(2)}, u32[]{:S(2)}) collective-permute-start(bf16[64,512]{1,0:T(8,128)(2,1)S(1)} %get-tuple-element.68), channel_id=1, source_target_pairs={{0,6},{1,7},{2,4},{3,5},{4,2},{5,3},{6,0},{7,1},{8,14},{9,15},{10,... | collective-permute-start | bytes 196616 | tf_op jit(solution)/shard_map/ppermute | solution.py:208
  27.8 14.8 %collective-permute-start.20 = (bf16[64,512]{1,0:T(8,128)(2,1)S(1)}, bf16[64,512]{1,0:T(8,128)(2,1)S(1)}, u32[]{:S(2)}, u32[]{:S(2)}) collective-permute-start(bf16[64,512]{1,0:T(8,128)(2,1)S(1)} %get-tuple-element.69), channel_id=1, source_target_pairs={{0,7},{1,6},{2,5},{3,4},{4,3},{5,2},{6,1},{7,0},{8,15},{9,14},{10,... | collective-permute-start | bytes 196616 | tf_op jit(solution)/shard_map/ppermute | solution.py:208
  31.5 11.4 %collective-permute-start.10 = (bf16[64,512]{1,0:T(8,128)(2,1)S(1)}, bf16[64,512]{1,0:T(8,128)(2,1)S(1)}, u32[]{:S(2)}, u32[]{:S(2)}) collective-permute-start(bf16[64,512]{1,0:T(8,128)(2,1)S(1)} %get-tuple-element.58), channel_id=1, source_target_pairs={{0,4},{1,5},{2,6},{3,7},{4,0},{5,1},{6,2},{7,3},{8,12},{9,13},{10,... | collective-permute-start | bytes 196616 | tf_op jit(solution)/shard_map/ppermute | solution.py:208
  31.5 14.5 %collective-permute-start.11 = (bf16[64,512]{1,0:T(8,128)(2,1)S(1)}, bf16[64,512]{1,0:T(8,128)(2,1)S(1)}, u32[]{:S(2)}, u32[]{:S(2)}) collective-permute-start(bf16[64,512]{1,0:T(8,128)(2,1)S(1)} %get-tuple-element.59), channel_id=1, source_target_pairs={{0,5},{1,4},{2,7},{3,6},{4,1},{5,0},{6,3},{7,2},{8,13},{9,12},{10,... | collective-permute-start | bytes 196616 | tf_op jit(solution)/shard_map/ppermute | solution.py:208
  42.9 9.1 %collective-permute-start.8 = (bf16[64,512]{1,0:T(8,128)(2,1)S(1)}, bf16[64,512]{1,0:T(8,128)(2,1)S(1)}, u32[]{:S(2)}, u32[]{:S(2)}) collective-permute-start(bf16[64,512]{1,0:T(8,128)(2,1)S(1)} %get-tuple-element.56), channel_id=1, source_target_pairs={{0,2},{1,3},{2,0},{3,1},{4,6},{5,7},{6,4},{7,5},{8,10},{9,11},{10,... | collective-permute-start | bytes 196616 | tf_op jit(solution)/shard_map/ppermute | solution.py:208
  46.0 9.9 %collective-permute-start = (bf16[64,512]{1,0:T(8,128)(2,1)S(1)}, bf16[64,512]{1,0:T(8,128)(2,1)S(1)}, u32[]{:S(2)}, u32[]{:S(2)}) collective-permute-start(bf16[64,512]{1,0:T(8,128)(2,1)S(1)} %get-tuple-element.47), channel_id=1, source_target_pairs={{0,1},{1,0},{2,3},{3,2},{4,5},{5,4},{6,7},{7,6},{8,9},{9,8},{10,11... | collective-permute-start | bytes 196616 | tf_op jit(solution)/shard_map/ppermute | solution.py:208
  47.0 11.2 %collective-permute-start.1 = (bf16[64,512]{1,0:T(8,128)(2,1)S(1)}, bf16[64,512]{1,0:T(8,128)(2,1)S(1)}, u32[]{:S(2)}, u32[]{:S(2)}) collective-permute-start(bf16[64,512]{1,0:T(8,128)(2,1)S(1)} %get-tuple-element.48), channel_id=1, source_target_pairs={{0,2},{1,3},{2,0},{3,1},{4,6},{5,7},{6,4},{7,5},{8,10},{9,11},{10,... | collective-permute-start | bytes 196616 | tf_op jit(solution)/shard_map/ppermute | solution.py:208
  51.5 9.4 %collective-permute-start.2 = (bf16[64,512]{1,0:T(8,128)(2,1)S(1)}, bf16[64,512]{1,0:T(8,128)(2,1)S(1)}, u32[]{:S(2)}, u32[]{:S(2)}) collective-permute-start(bf16[64,512]{1,0:T(8,128)(2,1)S(1)} %get-tuple-element.49), channel_id=1, source_target_pairs={{0,3},{1,2},{2,1},{3,0},{4,7},{5,6},{6,5},{7,4},{8,11},{9,10},{10,... | collective-permute-start | bytes 196616 | tf_op jit(solution)/shard_map/ppermute | solution.py:208
  52.0 10.5 %collective-permute-start.3 = (bf16[64,512]{1,0:T(8,128)(2,1)S(1)}, bf16[64,512]{1,0:T(8,128)(2,1)S(1)}, u32[]{:S(2)}, u32[]{:S(2)}) collective-permute-start(bf16[64,512]{1,0:T(8,128)(2,1)S(1)} %get-tuple-element.50), channel_id=1, source_target_pairs={{0,4},{1,5},{2,6},{3,7},{4,0},{5,1},{6,2},{7,3},{8,12},{9,13},{10,... | collective-permute-start | bytes 196616 | tf_op jit(solution)/shard_map/ppermute | solution.py:208
  54.4 9.3 %collective-permute-start.4 = (bf16[64,512]{1,0:T(8,128)(2,1)S(1)}, bf16[64,512]{1,0:T(8,128)(2,1)S(1)}, u32[]{:S(2)}, u32[]{:S(2)}) collective-permute-start(bf16[64,512]{1,0:T(8,128)(2,1)S(1)} %get-tuple-element.51), channel_id=1, source_target_pairs={{0,5},{1,4},{2,7},{3,6},{4,1},{5,0},{6,3},{7,2},{8,13},{9,12},{10,... | collective-permute-start | bytes 196616 | tf_op jit(solution)/shard_map/ppermute | solution.py:208
  66.8 23.7 %collective-permute-start.35 = (bf16[2,192,512]{2,1,0:T(8,128)(2,1)}, bf16[2,192,512]{2,1,0:T(8,128)(2,1)}, u32[]{:S(2)}, u32[]{:S(2)}) collective-permute-start(bf16[2,192,512]{2,1,0:T(8,128)(2,1)} %shard_map.90), channel_id=1, source_target_pairs={{0,16},{8,24},{16,0},{24,8},{1,17},{9,25},{17,1},{25,9},{2,18},{10... | collective-permute-start | bytes 1179656 | tf_op jit(solution)/shard_map/ppermute | solution.py:270
  69.8 22.8 %collective-permute-start.33 = (bf16[2,192,512]{2,1,0:T(8,128)(2,1)}, bf16[2,192,512]{2,1,0:T(8,128)(2,1)}, u32[]{:S(2)}, u32[]{:S(2)}) collective-permute-start(bf16[2,192,512]{2,1,0:T(8,128)(2,1)} %shard_map.88), channel_id=1, source_target_pairs={{0,16},{8,24},{16,0},{24,8},{1,17},{9,25},{17,1},{25,9},{2,18},{10... | collective-permute-start | bytes 1179656 | tf_op jit(solution)/shard_map/ppermute | solution.py:270
  70.7 25.3 %collective-permute-start.31 = (bf16[2,192,512]{2,1,0:T(8,128)(2,1)}, bf16[2,192,512]{2,1,0:T(8,128)(2,1)}, u32[]{:S(2)}, u32[]{:S(2)}) collective-permute-start(bf16[2,192,512]{2,1,0:T(8,128)(2,1)} %shard_map.86), channel_id=1, source_target_pairs={{0,16},{8,24},{16,0},{24,8},{1,17},{9,25},{17,1},{25,9},{2,18},{10... | collective-permute-start | bytes 1179656 | tf_op jit(solution)/shard_map/ppermute | solution.py:270
  73.8 30.4 %collective-permute-start.29 = (bf16[2,192,512]{2,1,0:T(8,128)(2,1)}, bf16[2,192,512]{2,1,0:T(8,128)(2,1)}, u32[]{:S(2)}, u32[]{:S(2)}) collective-permute-start(bf16[2,192,512]{2,1,0:T(8,128)(2,1)} %shard_map.84), channel_id=1, source_target_pairs={{0,16},{8,24},{16,0},{24,8},{1,17},{9,25},{17,1},{25,9},{2,18},{10... | collective-permute-start | bytes 1179656 | tf_op jit(solution)/shard_map/ppermute | solution.py:270
  (28 other events, 173.4 us)

commit v3 on v2

v3 whole, which is shorter than its diff:
```python
import functools

import jax
import jax.numpy as jnp
from jax import lax
from jax.experimental import pallas as pl
from jax.experimental.pallas import tpu as pltpu
from jax.sharding import PartitionSpec as P

F32, BF16, I32 = jnp.float32, jnp.bfloat16, jnp.int32
PARAMS = pltpu.CompilerParams(vmem_limit_bytes=24 * 1024 * 1024)
VMEM = pl.BlockSpec(memory_space=pltpu.VMEM)
HBM = pl.BlockSpec(memory_space=pltpu.HBM)

LINE, SIDES = 4, 2
FAR, NEAR, PASSED = (3, 2, 1, 0), (1, 0, 3, 2), (2, 0, 3, 1)
FROM = (0, 1, 3, 2)
MASKS = tuple(d * SIDES for d in FROM) + tuple(d * SIDES + 1 for d in FROM)
INFO = 16


def nbytes(shapes):
    return sum(x.size * x.dtype.itemsize for x in jax.tree.leaves(shapes))


def call(kernel, outs, *args, flops=0, **kw):
    return pl.pallas_call(
        kernel,
        out_shape=outs,
        compiler_params=PARAMS,
        cost_estimate=pl.CostEstimate(
            flops=flops, bytes_accessed=nbytes(args) + nbytes(outs), transcendentals=0
        ),
        **kw,
    )(*args)


def gates_of(probs):
    total = jnp.sum(probs, axis=0, keepdims=True)
    gates = probs / total
    return total, gates, gates.astype(BF16).astype(F32)


def slots_of(ids, experts):
    chosen, tokens = ids.shape
    expert = lax.broadcasted_iota(I32, (experts, tokens), 0)
    named = [ids[k : k + 1] == expert for k in range(chosen)]
    hits = functools.reduce(jnp.add, [n.astype(F32) for n in named]).astype(BF16)
    row = lax.broadcasted_iota(I32, (tokens, tokens), 0)
    earlier = (row < lax.broadcasted_iota(I32, (tokens, tokens), 1)).astype(F32).astype(BF16)
    before = jnp.dot(hits, earlier, preferred_element_type=F32)
    return [jnp.sum(jnp.where(n, before, 0.0), axis=0, keepdims=True) for n in named]


def begin_kernel(experts, capacity, ids_ref, probs_ref, rows_ref, flat_ref, out_ref, sem):
    chosen, tokens = ids_ref.shape
    width = out_ref.shape[1]
    copy = pltpu.make_async_copy(rows_ref.at[:, :width], out_ref.at[:tokens], sem)
    copy.start()
    ids = ids_ref[...]
    _, _, word = gates_of(probs_ref[...])
    slots = slots_of(ids, experts)
    for k in range(chosen):
        flat_ref[k : k + 1, :] = ids[k : k + 1] * capacity + slots[k].astype(I32)
    rest = jnp.zeros((INFO - 3 * chosen, tokens), F32)
    info = jnp.concatenate([ids.astype(F32), *slots, word, rest], axis=0).astype(BF16)
    out_ref[tokens:, :tokens] = info
    if width > tokens:
        out_ref[tokens:, tokens:] = jnp.zeros((INFO, width - tokens), BF16)
    copy.wait()


def next_kernel(start, own_ref, far_ref, *refs):
    if start is not None:
        rows_ref, pass_ref, out_ref, sem = refs
        copy = pltpu.make_async_copy(rows_ref.at[:, pl.ds(start, out_ref.shape[1])], out_ref, sem)
        copy.start()
    else:
        (pass_ref,) = refs
    place = lax.axis_index("expert") // SIDES
    inner = jnp.logical_and(place > 0, place < LINE - 1)

    @pl.when(inner)
    def _():
        pass_ref[...] = far_ref[...]

    @pl.when(jnp.logical_not(inner))
    def _():
        pass_ref[...] = own_ref[...]

    if start is not None:
        copy.wait()


def pick_kernel(held, capacity, chosen, first, *refs):
    block_refs, refs = refs[:LINE], refs[LINE:]
    place_ref, own_ref, other_ref = refs
    tokens = place_ref.shape[2]
    if first:
        me = lax.axis_index("expert")
        local = lax.broadcasted_iota(I32, (held * capacity, tokens), 0)
        for j, ref in enumerate(block_refs):
            info = ref[tokens:, :tokens].astype(F32)
            flat = (info[:chosen] * capacity + info[chosen : 2 * chosen]).astype(I32)
            word = info[2 * chosen : 3 * chosen]
            for side in range(SIDES):
                slot = local + (me ^ side) * (held * capacity)
                hits = [
                    jnp.where(flat[k : k + 1] == slot, word[k : k + 1], 0.0) for k in range(chosen)
                ]
                at = pl.ds(side * held * capacity, held * capacity)
                place_ref[j, at, :] = functools.reduce(jnp.add, hits).astype(BF16)
    for j, ref in enumerate(block_refs):
        scaled = jnp.dot(place_ref[j], ref[:tokens, :], preferred_element_type=F32).astype(BF16)
        for side, out_ref in enumerate((own_ref, other_ref)):
            for e in range(held):
                at = (side * held + e) * capacity
                out_ref[e, j * capacity : (j + 1) * capacity, :] = scaled[at : at + capacity]


def turn_kernel(dp, hidden_ref, out_ref):
    parts, held, _, units = hidden_ref.shape
    share, across = units // dp, dp // 2
    me = lax.axis_index("expert") if parts > 1 else 0
    mine = lax.axis_index("dp")
    core, row = mine % 2, mine // 2
    masks = MASKS if parts > 1 else (0,)
    for e in range(held):
        stacked = jnp.concatenate([hidden_ref[me ^ mask, e] for mask in masks], axis=0)
        turned = stacked.T
        for piece in range(dp):
            other = (piece % 2) ^ core
            step = (piece // 2 - row + across) % across
            out_ref[e, other, step] = turned[piece * share : (piece + 1) * share]


def stacked_rows(refs, e):
    return refs[0][e] if len(refs) == 1 else jnp.concatenate([ref[e] for ref in refs], axis=0)


def term_kernel(turned_ref, *refs):
    part_refs, keep_ref, give_ref = refs[:-2], refs[-2], refs[-1]
    held, _, across, share, slots = turned_ref.shape
    for e in range(held):
        scaled = stacked_rows(part_refs, e)
        for other, ref in ((1, give_ref), (0, keep_ref)):
            left = turned_ref[e, other].reshape(across * share, slots)
            term = jnp.dot(left, scaled, preferred_element_type=F32).astype(BF16)
            for step in range(across):
                ref[step, e] = term[step * share : (step + 1) * share]


def pair_kernel(keep_ref, got_ref, *out_refs):
    for step, ref in enumerate(out_refs, 1):
        ref[...] = (keep_ref[step].astype(F32) + got_ref[step].astype(F32)).astype(BF16)


def last_kernel(others, keep_ref, got_ref, *refs):
    out_ref = refs[-1]
    for e in range(keep_ref.shape[1]):
        total = keep_ref[0, e].astype(F32) + got_ref[0, e].astype(F32)
        for ref in refs[:others]:
            total = total + ref[e].astype(F32)
        out_ref[:, e, :] = total


def raw_kernel(parts, first, final, weight_ref, *refs):
    part_refs, refs = refs[:parts], refs[parts:]
    if not first:
        acc_ref, refs = refs[0], refs[1:]
    held = weight_ref.shape[0]
    for e in range(held):
        raw = lax.dot_general(
            stacked_rows(part_refs, e),
            weight_ref[e],
            (((1,), (1,)), ((), ())),
            preferred_element_type=F32,
        )
        if not first:
            raw = raw + acc_ref[e]
        if not final:
            refs[0][e] = raw
            continue
        hidden_ref, grad_ref, sums_ref = refs
        sources, _, own, units = hidden_ref.shape
        me = lax.axis_index("expert") if sources > 1 else 0
        folds = []
        for part, mask in enumerate(MASKS if sources > 1 else (0,)):
            block = raw[part * own : (part + 1) * own]
            grad_ref[me ^ mask, e] = block.astype(BF16)
            product = block * hidden_ref[me ^ mask, e].astype(F32)
            folds.append(
                functools.reduce(jnp.add, [product[:, i : i + 128] for i in range(0, units, 128)])
            )
        folded = jnp.concatenate(folds, axis=0) if len(folds) > 1 else folds[0]
        sums_ref[e : e + 1, :] = jnp.sum(folded.T, axis=0, keepdims=True)


def prob_kernel(direct, capacity, flat_ref, probs_ref, *refs):
    out_ref = refs[-1]
    chosen, tokens = flat_ref.shape
    if direct:
        values = []
        for mask in range(LINE * SIDES):
            at = MASKS.index(mask) * capacity
            ref = refs[mask // SIDES]
            values += [ref[mask % SIDES, e : e + 1, at : at + capacity] for e in range(ref.shape[1])]
        lanes = 128 // capacity
        values = jnp.concatenate(
            [
                jnp.concatenate([v.reshape(1, capacity) for v in values[i : i + lanes]], axis=1)
                for i in range(0, len(values), lanes)
            ],
            axis=0,
        )
        me = lax.axis_index("expert")
    else:
        values = refs[0][...]
        me = 0
    lines = values.shape[0]
    spare = jnp.zeros((-lines % 8, 128), F32)
    columns = jnp.concatenate([values, spare], axis=0).T if spare.size else values.T
    total, gates, word = gates_of(probs_ref[...])
    group = lines * 128 // (LINE * SIDES)
    picked = [jnp.zeros((1, tokens), F32) for _ in range(chosen)]
    for line in range(lines):
        at = lax.broadcasted_iota(I32, (128, tokens), 0) + line * 128
        slot = (at // group ^ me) * group + at % group
        for k in range(chosen):
            hit = jnp.where(flat_ref[k : k + 1, :] == slot, columns[:, line : line + 1], 0.0)
            picked[k] += jnp.sum(hit, axis=0, keepdims=True)
    picked = [picked[k] / word[k : k + 1] for k in range(chosen)]
    mixed = functools.reduce(jnp.add, [gates[k : k + 1] * picked[k] for k in range(chosen)])
    for k in range(chosen):
        out_ref[k : k + 1, :] = (picked[k] - mixed) / total


def chunks_of(features):
    return [features // 4] * 4


sds = jax.ShapeDtypeStruct


def relayed(grad_out, ids, probs, held, capacity, widths):
    tokens, features = grad_out.shape
    chosen = ids.shape[0]
    experts = LINE * SIDES * held

    def along(block, targets):
        pairs = [
            (p * SIDES + s, targets[p] * SIDES + s) for p in range(LINE) for s in range(SIDES)
        ]
        return lax.ppermute(block, "expert", pairs)

    scratch = [pltpu.SemaphoreType.DMA]
    flat, own = call(
        functools.partial(begin_kernel, experts, capacity),
        [sds((chosen, tokens), I32), sds((tokens + INFO, widths[0]), BF16)],
        ids,
        probs,
        grad_out,
        in_specs=[VMEM, VMEM, HBM],
        out_specs=[VMEM, VMEM],
        scratch_shapes=scratch,
    )
    arrived, place, start = [], None, 0
    for c, width in enumerate(widths):
        far = along(own, FAR)
        near = along(own, NEAR)
        start += width
        shape = sds(own.shape, BF16)
        if c + 1 < len(widths):
            hand, following = call(
                functools.partial(next_kernel, start),
                [shape, sds((tokens, widths[c + 1]), BF16)],
                own,
                far,
                grad_out,
                in_specs=[VMEM, VMEM, HBM],
                out_specs=[VMEM, VMEM],
                scratch_shapes=scratch,
            )
        else:
            hand, following = call(functools.partial(next_kernel, None), shape, own, far), None
        passed = along(hand, PASSED)
        blocks = [own, near, far, passed]
        rows = [sds((held, LINE * capacity, width), BF16)] * SIDES
        places = sds((LINE, SIDES * held * capacity, tokens), BF16)
        kernel = functools.partial(pick_kernel, held, capacity, chosen, c == 0)
        flops = 2 * LINE * SIDES * held * capacity * tokens * width
        if c == 0:
            place, mine, other = call(kernel, [places, *rows], *blocks, flops=flops)
        else:
            mine, other = call(kernel, rows, *blocks, place, flops=flops)
        swap = [(i, i ^ 1) for i in range(LINE * SIDES)]
        arrived.append([mine, lax.ppermute(other, "expert", swap)])
        own = following
    return flat, arrived


def exchanged(grad_out, ids, probs, groups, held, capacity, widths):
    tokens = grad_out.shape[0]
    experts = groups * held
    slots = experts * capacity
    _, _, word = gates_of(probs)
    flat = ids * capacity + jnp.concatenate(slots_of(ids, experts), axis=0).astype(I32)
    slot = lax.broadcasted_iota(I32, (slots, tokens), 0)
    place = sum(jnp.where(f == slot, w, 0.0) for f, w in zip(flat, word)).astype(BF16)
    arrived, start = [], 0
    for width in widths:
        rows = grad_out[:, start : start + width]
        sent = jnp.dot(place, rows, preferred_element_type=F32).astype(BF16)
        got = lax.all_to_all(
            sent.reshape(groups, held, capacity, width),
            "expert",
            split_axis=0,
            concat_axis=0,
            tiled=True,
        )
        arrived.append([got.transpose(1, 0, 2, 3).reshape(held, groups * capacity, width)])
        start += width
    return flat, arrived


def body(grad_out, route_ids, route_probs, hidden, w_down):
    groups = lax.axis_size("expert")
    dp = lax.axis_size("dp")
    held, units, features = w_down.shape
    capacity = hidden.shape[3]
    slots = groups * held * capacity
    per_expert = slots // held
    tokens, chosen = route_ids.shape
    share, across = units // dp, dp // 2
    direct = groups == LINE * SIDES
    widths = chunks_of(features)
    count = len(widths)

    ids, probs = route_ids.T, route_probs.T
    if direct:
        flat, arrived = relayed(grad_out, ids, probs, held, capacity, widths)
        saved = hidden[0]
    else:
        flat, arrived = exchanged(grad_out, ids, probs, groups, held, capacity, widths)
        saved = hidden[0].transpose(1, 0, 2, 3).reshape(1, held, per_expert, units)
    parts = len(arrived[0])
    turned = call(
        functools.partial(turn_kernel, dp),
        sds((held, 2, across, share, per_expert), BF16),
        saved,
    )

    flops = [2 * slots * units * w for w in widths]
    weight_grad, raw, start = None, None, 0
    for c, width in enumerate(widths):
        piece = sds((across, held, share, width), BF16)
        keep, give = call(term_kernel, [piece, piece], turned, *arrived[c], flops=flops[c])
        got = lax.ppermute(give, "dp", [(i, i ^ 1) for i in range(dp)])

        final = c == count - 1
        if final:
            outs = [sds(saved.shape, BF16), sds((held, per_expert), F32)]
            extra = [saved]
        else:
            outs, extra = [sds((held, per_expert, units), F32)], []
        extra = extra if c == 0 else [raw] + extra
        made = call(
            functools.partial(raw_kernel, parts, c == 0, final),
            outs,
            w_down,
            *arrived[c],
            *extra,
            flops=flops[c],
            grid=(1,),
            in_specs=[pl.BlockSpec((held, units, width), lambda i, at=start // width: (0, 0, at))]
            + [VMEM] * (parts + len(extra)),
            out_specs=[VMEM] * len(outs),
        )
        if final:
            hidden_grad, sums = made
        else:
            raw = made[0]

        piece = sds((held, share, width), BF16)
        pairs = call(pair_kernel, [piece] * (across - 1), keep, got)
        others = []
        for step in range(1, across):
            shift = [(2 * r + i, 2 * ((r + step) % across) + i) for r in range(across) for i in range(2)]
            others.append(lax.ppermute(pairs[step - 1], "dp", shift))
        first = pl.BlockSpec((1, held, share, width), lambda i: (0, 0, 0, 0))
        before = [] if c == 0 else [weight_grad]
        weight_grad = call(
            functools.partial(last_kernel, len(others)),
            sds((share, held, features), F32),
            keep,
            got,
            *others,
            *before,
            grid=(1,),
            in_specs=[first, first]
            + [VMEM] * len(others)
            + [pl.BlockSpec(memory_space=pl.ANY)] * len(before),
            out_specs=pl.BlockSpec((share, held, width), lambda i, at=start // width: (0, 0, at)),
            input_output_aliases={2 + len(others): 0} if before else {},
        )
        start += width

    if direct:
        swap = [(i, i ^ 1) for i in range(groups)]
        both = jnp.stack([sums, lax.ppermute(sums, "expert", swap)])
        returned = [both] + [
            lax.ppermute(both, "expert", [(i, i ^ (SIDES * d)) for i in range(groups)])
            for d in range(1, LINE)
        ]
    else:
        sums = sums.reshape(held, groups, capacity).transpose(1, 0, 2).reshape(groups, -1)
        hidden_grad = hidden_grad.reshape(held, groups, capacity, units).transpose(1, 0, 2, 3)
        returned = lax.all_to_all(sums, "expert", split_axis=0, concat_axis=0, tiled=True)
        returned = [returned.reshape(-1, 128)]
    prob_grad = call(
        functools.partial(prob_kernel, direct, capacity),
        sds((chosen, tokens), F32),
        flat,
        probs,
        *returned,
    ).T
    return (hidden_grad.reshape(hidden.shape), prob_grad, weight_grad)


def solution(mesh):
    in_specs = (
        P(("dp", "expert"), None),
        P(("dp", "expert"), None),
        P(("dp", "expert"), None),
        P("dp", None, "expert", None, None),
        P("expert", None, None),
    )
    out_specs = (
        P("dp", None, "expert", None, None),
        P(("dp", "expert"), None),
        P("dp", "expert", None),
    )
    return jax.shard_map(body, mesh=mesh, in_specs=in_specs, out_specs=out_specs, check_vma=False)
```

time: 107 us -> 104 us (0.972)
  waiting for transfers between devices: 21.3 us -> 42.8 us
  blocking collectives: 10.4 us -> 0 us
  Pallas kernels: 19.7 us -> 13.2 us
  starting transfers between devices: 48.2 us -> 43.4 us
  local copies, waits for them, and re-layouts: 4.96 us -> 3.46 us
    ppermute x28 -> x20, waiting for transfers between devices: 14.1 us -> 35.8 us  [the longest x12 16.6 us: along(): return lax.ppermute(block, 'expert', pairs)]
    all_to_all x1 -> x0, blocking collectives: 10.4 us -> none  [body(): lax.all_to_all(sums, 'expert', split_axis=0, concat_axis=0, tiled=True)]
    pallas_call x19 -> x27, Pallas kernels: 19.7 us -> 13.2 us  [call(): pl.pallas_call(kernel, out_shape=outs, compiler_params=PARAMS, cost_estim...]
    ppermute x28 -> x20, starting transfers between devices: 44 us -> 38.9 us  [the longest x12 26.6 us: along(): return lax.ppermute(block, 'expert', pairs)]
    unnamed x32 -> x16, local copies, waits for them, and re-layouts: 4.17 us -> 3.46 us
  transfers between devices with their start and end apart: 36 -> 28, of which waited for: 8 -> 18; matrix products, arithmetic and copies ran while one was open for 1% -> 0% of each run, Pallas kernels for 16% -> 11%
where the time goes in v3:
time: 104 us
  starting transfers between devices  43.4 us (42%)
  waiting for transfers between devices  42.8 us (41%)
  Pallas kernels  13.2 us (13%)
  local copies, waits for them, and re-layouts  3.46 us (3%)
    ppermute x12, starting transfers between devices, along(): return lax.ppermute(block, 'expert', pairs)  26.6 us
    ppermute x12, waiting for transfers between devices, along(): return lax.ppermute(block, 'expert', pairs)  16.6 us
    pallas_call x27, Pallas kernels, call(): pl.pallas_call(kernel, out_shape=outs, compiler_params=PARAMS, cost_estim...  13.2 us
    ppermute x4, waiting for transfers between devices, relayed(): arrived.append([mine, lax.ppermute(other, 'expert', swap)])  8.49 us
    ppermute x3, waiting for transfers between devices, body(): lax.ppermute(both, 'expert', [(i, i ^ SIDES * d) for i in range(groups)])  7.43 us
    ppermute x4, waiting for transfers between devices, body(): others.append(lax.ppermute(pairs[step - 1], 'dp', shift))  6.97 us
    ppermute x3, starting transfers between devices, body(): lax.ppermute(both, 'expert', [(i, i ^ SIDES * d) for i in range(groups)])  6.48 us
    ppermute x4, starting transfers between devices, relayed(): arrived.append([mine, lax.ppermute(other, 'expert', swap)])  5.49 us
  transfers between devices with their start and end apart: 28, of which 18 were waited for; matrix products, arithmetic and copies ran while one was open for 0% of the time, Pallas kernels for 11%

profile of v3, /device:TPU:0, one launch (start us, length us, event | category | flops | bytes accessed | tf_op | source)
XLA Modules:
  0.0 103.8 jit_solution(8472369527804702631)
XLA Ops:
  3.2 5.1 %collective-permute-start = (bf16[144,512]{1,0:T(8,128)(2,1)S(1)}, bf16[144,512]{1,0:T(8,128)(2,1)S(1)}, u32[]{:S(2)}, u32[]{:S(2)}) collective-permute-start(bf16[144,512]{1,0:T(8,128)(2,1)S(1)} %get-tuple-element.30.own_ref.refs_0_), channel_id=1, source_target_pairs={{0,6},{1,7},{2,4},{3,5},{4,2},{5,3},{6,0},{7,1},{8,14},{9,15},{10,... | collective-permute-start | bytes 442376 | tf_op jit(solution)/shard_map/ppermute | solution.py:254
  8.3 4.0 %collective-permute-done.far_ref.refs_2_ = bf16[144,512]{1,0:T(8,128)(2,1)S(1)} collective-permute-done((bf16[144,512]{1,0:T(8,128)(2,1)S(1)}, bf16[144,512]{1,0:T(8,128)(2,1)S(1)}, u32[]{:S(2)}, u32[]{:S(2)}) %collective-permute-start) | collective-permute-done | bytes 147488 | tf_op jit(solution)/shard_map/ppermute | solution.py:254
  13.4 3.6 %collective-permute-start.1 = (bf16[128,512]{1,0:T(8,128)(2,1)S(1)}, bf16[128,512]{1,0:T(8,128)(2,1)S(1)}, u32[]{:S(2)}, u32[]{:S(2)}) collective-permute-start(bf16[128,512]{1,0:T(8,128)(2,1)S(1)} %get-tuple-element.31.own_ref.refs_0_), channel_id=1, source_target_pairs={{0,6},{1,7},{2,4},{3,5},{4,2},{5,3},{6,0},{7,1},{8,14},{9,15},{10,... | collective-permute-start | bytes 393224 | tf_op jit(solution)/shard_map/ppermute | solution.py:254
  17.0 3.3 %collective-permute-done.1.far_ref.refs_2_ = bf16[128,512]{1,0:T(8,128)(2,1)S(1)} collective-permute-done((bf16[128,512]{1,0:T(8,128)(2,1)S(1)}, bf16[128,512]{1,0:T(8,128)(2,1)S(1)}, u32[]{:S(2)}, u32[]{:S(2)}) %collective-permute-start.1) | collective-permute-done | bytes 131104 | tf_op jit(solution)/shard_map/ppermute | solution.py:254
  20.3 3.7 %collective-permute-start.2 = (bf16[128,512]{1,0:T(8,128)(2,1)S(1)}, bf16[128,512]{1,0:T(8,128)(2,1)S(1)}, u32[]{:S(2)}, u32[]{:S(2)}) collective-permute-start(bf16[128,512]{1,0:T(8,128)(2,1)S(1)} %get-tuple-element.32.own_ref.refs_0_), channel_id=1, source_target_pairs={{0,6},{1,7},{2,4},{3,5},{4,2},{5,3},{6,0},{7,1},{8,14},{9,15},{10,... | collective-permute-start | bytes 393224 | tf_op jit(solution)/shard_map/ppermute | solution.py:254
  24.3 3.8 %collective-permute-done.2.far_ref.refs_2_ = bf16[128,512]{1,0:T(8,128)(2,1)S(1)} collective-permute-done((bf16[128,512]{1,0:T(8,128)(2,1)S(1)}, bf16[128,512]{1,0:T(8,128)(2,1)S(1)}, u32[]{:S(2)}, u32[]{:S(2)}) %collective-permute-start.2) | collective-permute-done | bytes 131104 | tf_op jit(solution)/shard_map/ppermute | solution.py:254
  28.2 2.8 %collective-permute-start.4 = (bf16[128,512]{1,0:T(8,128)(2,1)S(1)}, bf16[128,512]{1,0:T(8,128)(2,1)S(1)}, u32[]{:S(2)}, u32[]{:S(2)}) collective-permute-start(bf16[128,512]{1,0:T(8,128)(2,1)S(1)} %get-tuple-element.33.own_ref.refs_0_), channel_id=1, source_target_pairs={{0,6},{1,7},{2,4},{3,5},{4,2},{5,3},{6,0},{7,1},{8,14},{9,15},{10,... | collective-permute-start | bytes 393224 | tf_op jit(solution)/shard_map/ppermute | solution.py:254
  31.4 1.6 %collective-permute-start.12 = (bf16[128,512]{1,0:T(8,128)(2,1)S(1)}, bf16[128,512]{1,0:T(8,128)(2,1)S(1)}, u32[]{:S(2)}, u32[]{:S(2)}) collective-permute-start(bf16[128,512]{1,0:T(8,128)(2,1)S(1)} %get-tuple-element.31.own_ref.refs_0_), channel_id=1, source_target_pairs={{0,2},{1,3},{2,0},{3,1},{4,6},{5,7},{6,4},{7,5},{8,10},{9,11},{10,... | collective-permute-start | bytes 393224 | tf_op jit(solution)/shard_map/ppermute | solution.py:254
  36.6 5.0 %collective-permute-start.10 = (bf16[128,512]{1,0:T(8,128)(2,1)S(1)}, bf16[128,512]{1,0:T(8,128)(2,1)S(1)}, u32[]{:S(2)}, u32[]{:S(2)}) collective-permute-start(bf16[128,512]{1,0:T(8,128)(2,1)S(1)} %get-tuple-element.38), channel_id=1, source_target_pairs={{0,4},{1,5},{2,0},{3,1},{4,6},{5,7},{6,2},{7,3},{8,12},{9,13},{10,... | collective-permute-start | bytes 393224 | tf_op jit(solution)/shard_map/ppermute | solution.py:254
  41.7 1.8 %collective-permute-start.3 = (bf16[128,512]{1,0:T(8,128)(2,1)S(1)}, bf16[128,512]{1,0:T(8,128)(2,1)S(1)}, u32[]{:S(2)}, u32[]{:S(2)}) collective-permute-start(bf16[128,512]{1,0:T(8,128)(2,1)S(1)} %get-tuple-element.33.own_ref.refs_0_), channel_id=1, source_target_pairs={{0,2},{1,3},{2,0},{3,1},{4,6},{5,7},{6,4},{7,5},{8,10},{9,11},{10,... | collective-permute-start | bytes 393224 | tf_op jit(solution)/shard_map/ppermute | solution.py:254
  44.4 1.7 %collective-permute-start.15 = (bf16[2,128,512]{2,1,0:T(8,128)(2,1)S(1)}, bf16[2,128,512]{2,1,0:T(8,128)(2,1)S(1)}, u32[]{:S(2)}, u32[]{:S(2)}) collective-permute-start(bf16[2,128,512]{2,1,0:T(8,128)(2,1)S(1)} %get-tuple-element.45), channel_id=1, source_target_pairs={{0,1},{1,0},{2,3},{3,2},{4,5},{5,4},{6,7},{7,6},{8,9},{9,8},{10,11... | collective-permute-start | bytes 786440 | tf_op jit(solution)/shard_map/ppermute | solution.py:297
  47.2 1.7 %collective-permute-start.14 = (bf16[2,128,512]{2,1,0:T(8,128)(2,1)S(1)}, bf16[2,128,512]{2,1,0:T(8,128)(2,1)S(1)}, u32[]{:S(2)}, u32[]{:S(2)}) collective-permute-start(bf16[2,128,512]{2,1,0:T(8,128)(2,1)S(1)} %get-tuple-element.43), channel_id=1, source_target_pairs={{0,1},{1,0},{2,3},{3,2},{4,5},{5,4},{6,7},{7,6},{8,9},{9,8},{10,11... | collective-permute-start | bytes 786440 | tf_op jit(solution)/shard_map/ppermute | solution.py:297
  55.3 4.0 %collective-permute-done.14.refs_1_ = bf16[2,128,512]{2,1,0:T(8,128)(2,1)S(1)} collective-permute-done((bf16[2,128,512]{2,1,0:T(8,128)(2,1)S(1)}, bf16[2,128,512]{2,1,0:T(8,128)(2,1)S(1)}, u32[]{:S(2)}, u32[]{:S(2)}) %collective-permute-start.14) | collective-permute-done | bytes 262176 | tf_op jit(solution)/shard_map/ppermute | solution.py:297
  59.9 2.3 %collective-permute-done.11.refs_1_ = bf16[2,128,512]{2,1,0:T(8,128)(2,1)S(1)} collective-permute-done((bf16[2,128,512]{2,1,0:T(8,128)(2,1)S(1)}, bf16[2,128,512]{2,1,0:T(8,128)(2,1)S(1)}, u32[]{:S(2)}, u32[]{:S(2)}) %collective-permute-start.11) | collective-permute-done | bytes 262176 | tf_op jit(solution)/shard_map/ppermute | solution.py:297
  62.9 2.2 %collective-permute-done.8.refs_1_ = bf16[2,128,512]{2,1,0:T(8,128)(2,1)S(1)} collective-permute-done((bf16[2,128,512]{2,1,0:T(8,128)(2,1)S(1)}, bf16[2,128,512]{2,1,0:T(8,128)(2,1)S(1)}, u32[]{:S(2)}, u32[]{:S(2)}) %collective-permute-start.8) | collective-permute-done | bytes 262176 | tf_op jit(solution)/shard_map/ppermute | solution.py:297
  66.0 2.1 %collective-permute-start.25 = (bf16[2,192,512]{2,1,0:T(8,128)(2,1)S(1)}, bf16[2,192,512]{2,1,0:T(8,128)(2,1)S(1)}, u32[]{:S(2)}, u32[]{:S(2)}) collective-permute-start(bf16[2,192,512]{2,1,0:T(8,128)(2,1)S(1)} %shard_map.96), channel_id=1, source_target_pairs={{0,16},{8,24},{16,0},{24,8},{1,17},{9,25},{17,1},{25,9},{2,18},{10... | collective-permute-start | bytes 1179656 | tf_op jit(solution)/shard_map/ppermute | solution.py:389
  68.4 2.1 %collective-permute-start.21 = (bf16[2,192,512]{2,1,0:T(8,128)(2,1)S(1)}, bf16[2,192,512]{2,1,0:T(8,128)(2,1)S(1)}, u32[]{:S(2)}, u32[]{:S(2)}) collective-permute-start(bf16[2,192,512]{2,1,0:T(8,128)(2,1)S(1)} %shard_map.92), channel_id=1, source_target_pairs={{0,16},{8,24},{16,0},{24,8},{1,17},{9,25},{17,1},{25,9},{2,18},{10... | collective-permute-start | bytes 1179656 | tf_op jit(solution)/shard_map/ppermute | solution.py:389
  74.1 3.3 %collective-permute-done.16 = f32[2,256]{1,0:T(2,128)S(1)} collective-permute-done((f32[2,256]{1,0:T(2,128)S(1)}, f32[2,256]{1,0:T(2,128)S(1)}, u32[]{:S(2)}, u32[]{:S(2)}) %collective-permute-start.16) | collective-permute-done | bytes 2080 | tf_op jit(solution)/shard_map/ppermute | solution.py:410
  77.5 2.4 %collective-permute-start.17 = (f32[2,2,256]{2,1,0:T(2,128)S(1)}, f32[2,2,256]{2,1,0:T(2,128)S(1)}, u32[]{:S(2)}, u32[]{:S(2)}) collective-permute-start(f32[2,2,256]{2,1,0:T(2,128)S(1)} %pad_maximum_fusion.refs_0_), channel_id=1, source_target_pairs={{0,2},{1,3},{2,0},{3,1},{4,6},{5,7},{6,4},{7,5},{8,10},{9,11},{10,... | collective-permute-start | bytes 12296 | tf_op jit(solution)/shard_map/ppermute | solution.py:412
  81.5 2.3 %collective-permute-start.18 = (f32[2,2,256]{2,1,0:T(2,128)S(1)}, f32[2,2,256]{2,1,0:T(2,128)S(1)}, u32[]{:S(2)}, u32[]{:S(2)}) collective-permute-start(f32[2,2,256]{2,1,0:T(2,128)S(1)} %pad_maximum_fusion.refs_0_), channel_id=1, source_target_pairs={{0,4},{1,5},{2,6},{3,7},{4,0},{5,1},{6,2},{7,3},{8,12},{9,13},{10,... | collective-permute-start | bytes 12296 | tf_op jit(solution)/shard_map/ppermute | solution.py:412
  83.8 2.2 %collective-permute-done.18.refs_2_ = f32[2,2,256]{2,1,0:T(2,128)S(1)} collective-permute-done((f32[2,2,256]{2,1,0:T(2,128)S(1)}, f32[2,2,256]{2,1,0:T(2,128)S(1)}, u32[]{:S(2)}, u32[]{:S(2)}) %collective-permute-start.18) | collective-permute-done | bytes 4128 | tf_op jit(solution)/shard_map/ppermute | solution.py:412
  86.0 1.8 %collective-permute-start.19 = (f32[2,2,256]{2,1,0:T(2,128)S(1)}, f32[2,2,256]{2,1,0:T(2,128)S(1)}, u32[]{:S(2)}, u32[]{:S(2)}) collective-permute-start(f32[2,2,256]{2,1,0:T(2,128)S(1)} %pad_maximum_fusion.refs_0_), channel_id=1, source_target_pairs={{0,6},{1,7},{2,4},{3,5},{4,2},{5,3},{6,0},{7,1},{8,14},{9,15},{10,... | collective-permute-start | bytes 12296 | tf_op jit(solution)/shard_map/ppermute | solution.py:412
  87.7 3.7 %collective-permute-done.19.refs_3_ = f32[2,2,256]{2,1,0:T(2,128)S(1)} collective-permute-done((f32[2,2,256]{2,1,0:T(2,128)S(1)}, f32[2,2,256]{2,1,0:T(2,128)S(1)}, u32[]{:S(2)}, u32[]{:S(2)}) %collective-permute-start.19) | collective-permute-done | bytes 4128 | tf_op jit(solution)/shard_map/ppermute | solution.py:412
  95.8 6.9 %collective-permute-done.21.refs_0_ = bf16[2,192,512]{2,1,0:T(8,128)(2,1)S(1)} collective-permute-done((bf16[2,192,512]{2,1,0:T(8,128)(2,1)S(1)}, bf16[2,192,512]{2,1,0:T(8,128)(2,1)S(1)}, u32[]{:S(2)}, u32[]{:S(2)}) %collective-permute-start.21) | collective-permute-done | bytes 393248 | tf_op jit(solution)/shard_map/ppermute | solution.py:389
  (77 shorter events, 29.7 us)
Async XLA Ops:
  3.2 9.1 %collective-permute-start = (bf16[144,512]{1,0:T(8,128)(2,1)S(1)}, bf16[144,512]{1,0:T(8,128)(2,1)S(1)}, u32[]{:S(2)}, u32[]{:S(2)}) collective-permute-start(bf16[144,512]{1,0:T(8,128)(2,1)S(1)} %get-tuple-element.30.own_ref.refs_0_), channel_id=1, source_target_pairs={{0,6},{1,7},{2,4},{3,5},{4,2},{5,3},{6,0},{7,1},{8,14},{9,15},{10,... | collective-permute-start | bytes 442376 | tf_op jit(solution)/shard_map/ppermute | solution.py:254
  13.4 6.9 %collective-permute-start.1 = (bf16[128,512]{1,0:T(8,128)(2,1)S(1)}, bf16[128,512]{1,0:T(8,128)(2,1)S(1)}, u32[]{:S(2)}, u32[]{:S(2)}) collective-permute-start(bf16[128,512]{1,0:T(8,128)(2,1)S(1)} %get-tuple-element.31.own_ref.refs_0_), channel_id=1, source_target_pairs={{0,6},{1,7},{2,4},{3,5},{4,2},{5,3},{6,0},{7,1},{8,14},{9,15},{10,... | collective-permute-start | bytes 393224 | tf_op jit(solution)/shard_map/ppermute | solution.py:254
  20.3 7.8 %collective-permute-start.2 = (bf16[128,512]{1,0:T(8,128)(2,1)S(1)}, bf16[128,512]{1,0:T(8,128)(2,1)S(1)}, u32[]{:S(2)}, u32[]{:S(2)}) collective-permute-start(bf16[128,512]{1,0:T(8,128)(2,1)S(1)} %get-tuple-element.32.own_ref.refs_0_), channel_id=1, source_target_pairs={{0,6},{1,7},{2,4},{3,5},{4,2},{5,3},{6,0},{7,1},{8,14},{9,15},{10,... | collective-permute-start | bytes 393224 | tf_op jit(solution)/shard_map/ppermute | solution.py:254
  24.0 10.4 %collective-permute-start.6 = (bf16[144,512]{1,0:T(8,128)(2,1)S(1)}, bf16[144,512]{1,0:T(8,128)(2,1)S(1)}, u32[]{:S(2)}, u32[]{:S(2)}) collective-permute-start(bf16[144,512]{1,0:T(8,128)(2,1)S(1)} %get-tuple-element.30.own_ref.refs_0_), channel_id=1, source_target_pairs={{0,2},{1,3},{2,0},{3,1},{4,6},{5,7},{6,4},{7,5},{8,10},{9,11},{10,... | collective-permute-start | bytes 442376 | tf_op jit(solution)/shard_map/ppermute | solution.py:254
  28.2 8.4 %collective-permute-start.4 = (bf16[128,512]{1,0:T(8,128)(2,1)S(1)}, bf16[128,512]{1,0:T(8,128)(2,1)S(1)}, u32[]{:S(2)}, u32[]{:S(2)}) collective-permute-start(bf16[128,512]{1,0:T(8,128)(2,1)S(1)} %get-tuple-element.33.own_ref.refs_0_), channel_id=1, source_target_pairs={{0,6},{1,7},{2,4},{3,5},{4,2},{5,3},{6,0},{7,1},{8,14},{9,15},{10,... | collective-permute-start | bytes 393224 | tf_op jit(solution)/shard_map/ppermute | solution.py:254
  31.0 12.4 %collective-permute-start.7 = (bf16[144,512]{1,0:T(8,128)(2,1)S(1)}, bf16[144,512]{1,0:T(8,128)(2,1)S(1)}, u32[]{:S(2)}, u32[]{:S(2)}) collective-permute-start(bf16[144,512]{1,0:T(8,128)(2,1)S(1)} %get-tuple-element.34), channel_id=1, source_target_pairs={{0,4},{1,5},{2,0},{3,1},{4,6},{5,7},{6,2},{7,3},{8,12},{9,13},{10,... | collective-permute-start | bytes 442376 | tf_op jit(solution)/shard_map/ppermute | solution.py:254
  31.4 10.2 %collective-permute-start.12 = (bf16[128,512]{1,0:T(8,128)(2,1)S(1)}, bf16[128,512]{1,0:T(8,128)(2,1)S(1)}, u32[]{:S(2)}, u32[]{:S(2)}) collective-permute-start(bf16[128,512]{1,0:T(8,128)(2,1)S(1)} %get-tuple-element.31.own_ref.refs_0_), channel_id=1, source_target_pairs={{0,2},{1,3},{2,0},{3,1},{4,6},{5,7},{6,4},{7,5},{8,10},{9,11},{10,... | collective-permute-start | bytes 393224 | tf_op jit(solution)/shard_map/ppermute | solution.py:254
  33.1 11.4 %collective-permute-start.13 = (bf16[128,512]{1,0:T(8,128)(2,1)S(1)}, bf16[128,512]{1,0:T(8,128)(2,1)S(1)}, u32[]{:S(2)}, u32[]{:S(2)}) collective-permute-start(bf16[128,512]{1,0:T(8,128)(2,1)S(1)} %get-tuple-element.41), channel_id=1, source_target_pairs={{0,4},{1,5},{2,0},{3,1},{4,6},{5,7},{6,2},{7,3},{8,12},{9,13},{10,... | collective-permute-start | bytes 393224 | tf_op jit(solution)/shard_map/ppermute | solution.py:254
  34.4 12.8 %collective-permute-start.9 = (bf16[128,512]{1,0:T(8,128)(2,1)S(1)}, bf16[128,512]{1,0:T(8,128)(2,1)S(1)}, u32[]{:S(2)}, u32[]{:S(2)}) collective-permute-start(bf16[128,512]{1,0:T(8,128)(2,1)S(1)} %get-tuple-element.32.own_ref.refs_0_), channel_id=1, source_target_pairs={{0,2},{1,3},{2,0},{3,1},{4,6},{5,7},{6,4},{7,5},{8,10},{9,11},{10,... | collective-permute-start | bytes 393224 | tf_op jit(solution)/shard_map/ppermute | solution.py:254
  36.6 13.4 %collective-permute-start.10 = (bf16[128,512]{1,0:T(8,128)(2,1)S(1)}, bf16[128,512]{1,0:T(8,128)(2,1)S(1)}, u32[]{:S(2)}, u32[]{:S(2)}) collective-permute-start(bf16[128,512]{1,0:T(8,128)(2,1)S(1)} %get-tuple-element.38), channel_id=1, source_target_pairs={{0,4},{1,5},{2,0},{3,1},{4,6},{5,7},{6,2},{7,3},{8,12},{9,13},{10,... | collective-permute-start | bytes 393224 | tf_op jit(solution)/shard_map/ppermute | solution.py:254
  41.7 10.1 %collective-permute-start.3 = (bf16[128,512]{1,0:T(8,128)(2,1)S(1)}, bf16[128,512]{1,0:T(8,128)(2,1)S(1)}, u32[]{:S(2)}, u32[]{:S(2)}) collective-permute-start(bf16[128,512]{1,0:T(8,128)(2,1)S(1)} %get-tuple-element.33.own_ref.refs_0_), channel_id=1, source_target_pairs={{0,2},{1,3},{2,0},{3,1},{4,6},{5,7},{6,4},{7,5},{8,10},{9,11},{10,... | collective-permute-start | bytes 393224 | tf_op jit(solution)/shard_map/ppermute | solution.py:254
  43.5 9.7 %collective-permute-start.5 = (bf16[128,512]{1,0:T(8,128)(2,1)S(1)}, bf16[128,512]{1,0:T(8,128)(2,1)S(1)}, u32[]{:S(2)}, u32[]{:S(2)}) collective-permute-start(bf16[128,512]{1,0:T(8,128)(2,1)S(1)} %shard_map.80), channel_id=1, source_target_pairs={{0,4},{1,5},{2,0},{3,1},{4,6},{5,7},{6,2},{7,3},{8,12},{9,13},{10,... | collective-permute-start | bytes 393224 | tf_op jit(solution)/shard_map/ppermute | solution.py:254
  44.4 10.2 %collective-permute-start.15 = (bf16[2,128,512]{2,1,0:T(8,128)(2,1)S(1)}, bf16[2,128,512]{2,1,0:T(8,128)(2,1)S(1)}, u32[]{:S(2)}, u32[]{:S(2)}) collective-permute-start(bf16[2,128,512]{2,1,0:T(8,128)(2,1)S(1)} %get-tuple-element.45), channel_id=1, source_target_pairs={{0,1},{1,0},{2,3},{3,2},{4,5},{5,4},{6,7},{7,6},{8,9},{9,8},{10,11... | collective-permute-start | bytes 786440 | tf_op jit(solution)/shard_map/ppermute | solution.py:297
  47.2 12.1 %collective-permute-start.14 = (bf16[2,128,512]{2,1,0:T(8,128)(2,1)S(1)}, bf16[2,128,512]{2,1,0:T(8,128)(2,1)S(1)}, u32[]{:S(2)}, u32[]{:S(2)}) collective-permute-start(bf16[2,128,512]{2,1,0:T(8,128)(2,1)S(1)} %get-tuple-element.43), channel_id=1, source_target_pairs={{0,1},{1,0},{2,3},{3,2},{4,5},{5,4},{6,7},{7,6},{8,9},{9,8},{10,11... | collective-permute-start | bytes 786440 | tf_op jit(solution)/shard_map/ppermute | solution.py:297
  50.3 11.9 %collective-permute-start.11 = (bf16[2,128,512]{2,1,0:T(8,128)(2,1)S(1)}, bf16[2,128,512]{2,1,0:T(8,128)(2,1)S(1)}, u32[]{:S(2)}, u32[]{:S(2)}) collective-permute-start(bf16[2,128,512]{2,1,0:T(8,128)(2,1)S(1)} %get-tuple-element.40), channel_id=1, source_target_pairs={{0,1},{1,0},{2,3},{3,2},{4,5},{5,4},{6,7},{7,6},{8,9},{9,8},{10,11... | collective-permute-start | bytes 786440 | tf_op jit(solution)/shard_map/ppermute | solution.py:297
  53.5 11.6 %collective-permute-start.8 = (bf16[2,128,512]{2,1,0:T(8,128)(2,1)S(1)}, bf16[2,128,512]{2,1,0:T(8,128)(2,1)S(1)}, u32[]{:S(2)}, u32[]{:S(2)}) collective-permute-start(bf16[2,128,512]{2,1,0:T(8,128)(2,1)S(1)} %get-tuple-element.37), channel_id=1, source_target_pairs={{0,1},{1,0},{2,3},{3,2},{4,5},{5,4},{6,7},{7,6},{8,9},{9,8},{10,11... | collective-permute-start | bytes 786440 | tf_op jit(solution)/shard_map/ppermute | solution.py:297
  55.2 10.5 %collective-permute-start.26 = (bf16[2,2,192,512]{3,2,1,0:T(8,128)(2,1)S(1)}, bf16[2,2,192,512]{3,2,1,0:T(8,128)(2,1)S(1)}, u32[]{:S(2)}, u32[]{:S(2)}) collective-permute-start(bf16[2,2,192,512]{3,2,1,0:T(8,128)(2,1)S(1)} %get-tuple-element.56), channel_id=1, source_target_pairs={{0,8},{8,0},{16,24},{24,16},{1,9},{9,1},{17,25},{25,17},{2,10},{10... | collective-permute-start | bytes 2359304 | tf_op jit(solution)/shard_map/ppermute | solution.py:358
  59.9 6.1 %collective-permute-start.24 = (bf16[2,2,192,512]{3,2,1,0:T(8,128)(2,1)S(1)}, bf16[2,2,192,512]{3,2,1,0:T(8,128)(2,1)S(1)}, u32[]{:S(2)}, u32[]{:S(2)}) collective-permute-start(bf16[2,2,192,512]{3,2,1,0:T(8,128)(2,1)S(1)} %get-tuple-element.54), channel_id=1, source_target_pairs={{0,8},{8,0},{16,24},{24,16},{1,9},{9,1},{17,25},{25,17},{2,10},{10... | collective-permute-start | bytes 2359304 | tf_op jit(solution)/shard_map/ppermute | solution.py:358
  62.8 5.3 %collective-permute-start.22 = (bf16[2,2,192,512]{3,2,1,0:T(8,128)(2,1)S(1)}, bf16[2,2,192,512]{3,2,1,0:T(8,128)(2,1)S(1)}, u32[]{:S(2)}, u32[]{:S(2)}) collective-permute-start(bf16[2,2,192,512]{3,2,1,0:T(8,128)(2,1)S(1)} %get-tuple-element.52), channel_id=1, source_target_pairs={{0,8},{8,0},{16,24},{24,16},{1,9},{9,1},{17,25},{25,17},{2,10},{10... | collective-permute-start | bytes 2359304 | tf_op jit(solution)/shard_map/ppermute | solution.py:358
  65.8 26.5 %collective-permute-start.27 = (bf16[2,192,512]{2,1,0:T(8,128)(2,1)S(1)}, bf16[2,192,512]{2,1,0:T(8,128)(2,1)S(1)}, u32[]{:S(2)}, u32[]{:S(2)}) collective-permute-start(bf16[2,192,512]{2,1,0:T(8,128)(2,1)S(1)} %shard_map.98), channel_id=1, source_target_pairs={{0,16},{8,24},{16,0},{24,8},{1,17},{9,25},{17,1},{25,9},{2,18},{10... | collective-permute-start | bytes 1179656 | tf_op jit(solution)/shard_map/ppermute | solution.py:389
  66.0 27.4 %collective-permute-start.25 = (bf16[2,192,512]{2,1,0:T(8,128)(2,1)S(1)}, bf16[2,192,512]{2,1,0:T(8,128)(2,1)S(1)}, u32[]{:S(2)}, u32[]{:S(2)}) collective-permute-start(bf16[2,192,512]{2,1,0:T(8,128)(2,1)S(1)} %shard_map.96), channel_id=1, source_target_pairs={{0,16},{8,24},{16,0},{24,8},{1,17},{9,25},{17,1},{25,9},{2,18},{10... | collective-permute-start | bytes 1179656 | tf_op jit(solution)/shard_map/ppermute | solution.py:389
  68.2 26.5 %collective-permute-start.23 = (bf16[2,192,512]{2,1,0:T(8,128)(2,1)S(1)}, bf16[2,192,512]{2,1,0:T(8,128)(2,1)S(1)}, u32[]{:S(2)}, u32[]{:S(2)}) collective-permute-start(bf16[2,192,512]{2,1,0:T(8,128)(2,1)S(1)} %shard_map.94), channel_id=1, source_target_pairs={{0,16},{8,24},{16,0},{24,8},{1,17},{9,25},{17,1},{25,9},{2,18},{10... | collective-permute-start | bytes 1179656 | tf_op jit(solution)/shard_map/ppermute | solution.py:389
  68.4 34.3 %collective-permute-start.21 = (bf16[2,192,512]{2,1,0:T(8,128)(2,1)S(1)}, bf16[2,192,512]{2,1,0:T(8,128)(2,1)S(1)}, u32[]{:S(2)}, u32[]{:S(2)}) collective-permute-start(bf16[2,192,512]{2,1,0:T(8,128)(2,1)S(1)} %shard_map.92), channel_id=1, source_target_pairs={{0,16},{8,24},{16,0},{24,8},{1,17},{9,25},{17,1},{25,9},{2,18},{10... | collective-permute-start | bytes 1179656 | tf_op jit(solution)/shard_map/ppermute | solution.py:389
  86.0 5.4 %collective-permute-start.19 = (f32[2,2,256]{2,1,0:T(2,128)S(1)}, f32[2,2,256]{2,1,0:T(2,128)S(1)}, u32[]{:S(2)}, u32[]{:S(2)}) collective-permute-start(f32[2,2,256]{2,1,0:T(2,128)S(1)} %pad_maximum_fusion.refs_0_), channel_id=1, source_target_pairs={{0,6},{1,7},{2,4},{3,5},{4,2},{5,3},{6,0},{7,1},{8,14},{9,15},{10,... | collective-permute-start | bytes 12296 | tf_op jit(solution)/shard_map/ppermute | solution.py:412
  (12 other events, 94.2 us)

commit v4 on v3

v4 whole, which is shorter than its diff:
```python
import functools

import jax
import jax.numpy as jnp
from jax import lax
from jax.experimental import pallas as pl
from jax.experimental.pallas import tpu as pltpu
from jax.sharding import PartitionSpec as P

F32, BF16, I32 = jnp.float32, jnp.bfloat16, jnp.int32
PARAMS = pltpu.CompilerParams(vmem_limit_bytes=24 * 1024 * 1024)
VMEM = pl.BlockSpec(memory_space=pltpu.VMEM)
ANY = pl.BlockSpec(memory_space=pl.ANY)
HBM = pl.BlockSpec(memory_space=pltpu.HBM)

LINE, SIDES = 4, 2
INFO = 16


def nbytes(shapes):
    return sum(x.size * x.dtype.itemsize for x in jax.tree.leaves(shapes))


class Chain:
    def __init__(self):
        self.last = None

    def __call__(self, kernel, outs, *args, flops=0, in_specs=None, keep=True, **kw):
        in_specs = list(in_specs or [VMEM] * len(args))
        count = len(args)
        body = kernel
        if self.last is not None:
            args, in_specs = (*args, self.last), in_specs + [ANY]

            def body(*refs):
                kernel(*refs[:count], *refs[count + 1 :])

        made = pl.pallas_call(
            body,
            out_shape=outs,
            in_specs=in_specs,
            compiler_params=PARAMS,
            cost_estimate=pl.CostEstimate(flops=1, bytes_accessed=1, transcendentals=0),
            **kw,
        )(*args)
        if keep:
            self.last = jax.tree.leaves(made)[-1]
        return made


def gates_of(probs):
    total = jnp.sum(probs, axis=0, keepdims=True)
    gates = probs / total
    return total, gates, gates.astype(BF16).astype(F32)


def slots_of(ids, experts):
    chosen, tokens = ids.shape
    expert = lax.broadcasted_iota(I32, (experts, tokens), 0)
    named = [ids[k : k + 1] == expert for k in range(chosen)]
    hits = functools.reduce(jnp.add, [n.astype(F32) for n in named]).astype(BF16)
    row = lax.broadcasted_iota(I32, (tokens, tokens), 0)
    earlier = (row < lax.broadcasted_iota(I32, (tokens, tokens), 1)).astype(F32).astype(BF16)
    before = jnp.dot(hits, earlier, preferred_element_type=F32)
    return [jnp.sum(jnp.where(n, before, 0.0), axis=0, keepdims=True) for n in named]


def begin_kernel(experts, capacity, ids_ref, probs_ref, rows_ref, flat_ref, rest_ref, out_ref, sems):
    chosen, tokens = ids_ref.shape
    width = out_ref.shape[1]
    copies = [
        pltpu.make_async_copy(rows_ref.at[:, :width], out_ref.at[:tokens], sems.at[0]),
        pltpu.make_async_copy(rows_ref.at[:, width:], rest_ref, sems.at[1]),
    ]
    for copy in copies:
        copy.start()
    ids = ids_ref[...]
    _, _, word = gates_of(probs_ref[...])
    slots = slots_of(ids, experts)
    for k in range(chosen):
        flat_ref[k : k + 1, :] = ids[k : k + 1] * capacity + slots[k].astype(I32)
    rest = jnp.zeros((INFO - 3 * chosen, tokens), F32)
    info = jnp.concatenate([ids.astype(F32), *slots, word, rest], axis=0).astype(BF16)
    out_ref[tokens:, :tokens] = info
    if width > tokens:
        out_ref[tokens:, tokens:] = jnp.zeros((INFO, width - tokens), BF16)
    for copy in copies:
        copy.wait()


def pick_kernel(held, capacity, chosen, start, own_ref, other_ref, *refs):
    tokens = own_ref.shape[0] - (INFO if start is None else 0)
    rows = held * capacity
    if start is None:
        place_ref, out_refs = refs[-1], refs[:-1]
        me = lax.axis_index("expert")
        local = lax.broadcasted_iota(I32, (rows, tokens), 0)
        for side, ref in enumerate((own_ref, other_ref)):
            info = ref[tokens:, :tokens].astype(F32)
            flat = (info[:chosen] * capacity + info[chosen : 2 * chosen]).astype(I32)
            word = info[2 * chosen : 3 * chosen]
            for d in range(LINE):
                slot = local + (me ^ (SIDES * d)) * rows
                hits = [
                    jnp.where(flat[k : k + 1] == slot, word[k : k + 1], 0.0) for k in range(chosen)
                ]
                place_ref[side, d * rows : (d + 1) * rows, :] = functools.reduce(
                    jnp.add, hits
                ).astype(BF16)
        blocks = own_ref[:tokens, :], other_ref[:tokens, :]
    else:
        place_ref, out_refs = refs[0], refs[1:]
        width, first = out_refs[0].shape[2], own_ref.shape[1] - other_ref.shape[1]
        blocks = (
            own_ref[:, start : start + width],
            other_ref[:, start - first : start - first + width],
        )
    for side, block in enumerate(blocks):
        scaled = jnp.dot(place_ref[side], block, preferred_element_type=F32).astype(BF16)
        for d, out_ref in enumerate(out_refs):
            for e in range(held):
                at = d * rows + e * capacity
                out_ref[e, side * capacity : (side + 1) * capacity, :] = scaled[at : at + capacity]


def turn_kernel(dp, hidden_ref, out_ref):
    parts, held, _, units = hidden_ref.shape
    share, across = units // dp, dp // 2
    me = lax.axis_index("expert") if parts > 1 else 0
    mine = lax.axis_index("dp")
    core, row = mine % 2, mine // 2
    for e in range(held):
        stacked = jnp.concatenate([hidden_ref[me ^ mask, e] for mask in range(parts)], axis=0)
        turned = stacked.T
        for piece in range(dp):
            other = (piece % 2) ^ core
            step = (piece // 2 - row + across) % across
            out_ref[e, other, step] = turned[piece * share : (piece + 1) * share]


def stacked_rows(refs, e):
    return refs[0][e] if len(refs) == 1 else jnp.concatenate([ref[e] for ref in refs], axis=0)


def term_kernel(turned_ref, *refs):
    part_refs, keep_ref, give_ref = refs[:-2], refs[-2], refs[-1]
    held, _, across, share, slots = turned_ref.shape
    for e in range(held):
        scaled = stacked_rows(part_refs, e)
        for other, ref in ((1, give_ref), (0, keep_ref)):
            left = turned_ref[e, other].reshape(across * share, slots)
            term = jnp.dot(left, scaled, preferred_element_type=F32).astype(BF16)
            for step in range(across):
                ref[step, e] = term[step * share : (step + 1) * share]


def pair_kernel(keep_ref, got_ref, *out_refs):
    for step, ref in enumerate(out_refs, 1):
        ref[...] = (keep_ref[step].astype(F32) + got_ref[step].astype(F32)).astype(BF16)


def last_kernel(others, start, keep_ref, got_ref, *refs):
    out_ref, mark_ref, total_ref, sem = refs[-4:]
    mark_ref[...] = jnp.zeros(mark_ref.shape, F32)
    for e in range(keep_ref.shape[1]):
        total = keep_ref[0, e].astype(F32) + got_ref[0, e].astype(F32)
        for ref in refs[:others]:
            total = total + ref[e].astype(F32)
        total_ref[:, e, :] = total
    copy = pltpu.make_async_copy(
        total_ref, out_ref.at[:, :, start : start + total_ref.shape[2]], sem
    )
    copy.start()
    copy.wait()


def raw_kernel(parts, start, final, weight_ref, *refs):
    part_refs, refs = refs[:parts], refs[parts:]
    if start:
        acc_ref, refs = refs[0], refs[1:]
    width = part_refs[0].shape[2]
    for e in range(weight_ref.shape[0]):
        raw = lax.dot_general(
            stacked_rows(part_refs, e),
            weight_ref[e, :, start : start + width],
            (((1,), (1,)), ((), ())),
            preferred_element_type=F32,
        )
        if start:
            raw = raw + acc_ref[e]
        if not final:
            refs[0][e] = raw
            continue
        hidden_ref, grad_ref, sums_ref = refs
        sources, _, own, units = hidden_ref.shape
        me = lax.axis_index("expert") if sources > 1 else 0
        folds = []
        for mask in range(sources):
            block = raw[mask * own : (mask + 1) * own]
            grad_ref[me ^ mask, e] = block.astype(BF16)
            product = block * hidden_ref[me ^ mask, e].astype(F32)
            folds.append(
                functools.reduce(jnp.add, [product[:, i : i + 128] for i in range(0, units, 128)])
            )
        folded = jnp.concatenate(folds, axis=0) if len(folds) > 1 else folds[0]
        sums_ref[e : e + 1, :] = jnp.sum(folded.T, axis=0, keepdims=True)


def prob_kernel(direct, capacity, flat_ref, probs_ref, *refs):
    out_ref = refs[-1]
    chosen, tokens = flat_ref.shape
    if direct:
        values = []
        for mask in range(LINE * SIDES):
            at = mask * capacity
            ref = refs[mask // SIDES]
            values += [ref[mask % SIDES, e : e + 1, at : at + capacity] for e in range(ref.shape[1])]
        lanes = 128 // capacity
        values = jnp.concatenate(
            [
                jnp.concatenate([v.reshape(1, capacity) for v in values[i : i + lanes]], axis=1)
                for i in range(0, len(values), lanes)
            ],
            axis=0,
        )
        me = lax.axis_index("expert")
    else:
        values = refs[0][...]
        me = 0
    lines = values.shape[0]
    spare = jnp.zeros((-lines % 8, 128), F32)
    columns = jnp.concatenate([values, spare], axis=0).T if spare.size else values.T
    total, gates, word = gates_of(probs_ref[...])
    group = lines * 128 // (LINE * SIDES)
    picked = [jnp.zeros((1, tokens), F32) for _ in range(chosen)]
    for line in range(lines):
        at = lax.broadcasted_iota(I32, (128, tokens), 0) + line * 128
        slot = (at // group ^ me) * group + at % group
        for k in range(chosen):
            hit = jnp.where(flat_ref[k : k + 1, :] == slot, columns[:, line : line + 1], 0.0)
            picked[k] += jnp.sum(hit, axis=0, keepdims=True)
    picked = [picked[k] / word[k : k + 1] for k in range(chosen)]
    mixed = functools.reduce(jnp.add, [gates[k : k + 1] * picked[k] for k in range(chosen)])
    for k in range(chosen):
        out_ref[k : k + 1, :] = (picked[k] - mixed) / total


def chunks_of(features):
    return [features // 4] * 4


sds = jax.ShapeDtypeStruct


class Relay:
    def __init__(self, call, grad_out, ids, probs, held, capacity, widths):
        tokens, features = grad_out.shape
        self.call, self.rows, self.held, self.capacity = call, grad_out, held, capacity
        self.chosen, self.widths, self.place = ids.shape[0], widths, None
        self.flat, rest, self.first = call(
            functools.partial(begin_kernel, LINE * SIDES * held, capacity),
            [
                sds(ids.shape, I32),
                sds((tokens, features - widths[0]), BF16),
                sds((tokens + INFO, widths[0]), BF16),
            ],
            ids,
            probs,
            grad_out,
            in_specs=[VMEM, VMEM, HBM],
            scratch_shapes=[pltpu.SemaphoreType.DMA((2,))],
        )
        self.first_other = self.send(self.first, 1)
        self.rest_other = self.send(rest, 1)

    def send(self, block, mask):
        return lax.ppermute(block, "expert", [(i, i ^ mask) for i in range(LINE * SIDES)])

    def chunk(self, c):
        held, capacity, tokens = self.held, self.capacity, self.rows.shape[0]
        rows = [sds((held, SIDES * capacity, self.widths[c]), BF16)] * LINE
        place = sds((SIDES, LINE * held * capacity, tokens), BF16)
        flops = 2 * SIDES * LINE * held * capacity * tokens * self.widths[c]
        start = sum(self.widths[:c]) if c else None
        kernel = functools.partial(pick_kernel, held, capacity, self.chosen, start)
        if c == 0:
            *sent, self.place = self.call(
                kernel, [*rows, place], self.first, self.first_other, flops=flops
            )
        else:
            sent = self.call(kernel, rows, self.rows, self.rest_other, self.place, flops=flops)
        return [sent[0]] + [self.send(sent[d], SIDES * d) for d in range(1, LINE)]


def exchanged(grad_out, ids, probs, groups, held, capacity, widths):
    tokens = grad_out.shape[0]
    experts = groups * held
    slots = experts * capacity
    _, _, word = gates_of(probs)
    flat = ids * capacity + jnp.concatenate(slots_of(ids, experts), axis=0).astype(I32)
    slot = lax.broadcasted_iota(I32, (slots, tokens), 0)
    place = sum(jnp.where(f == slot, w, 0.0) for f, w in zip(flat, word)).astype(BF16)
    arrived, start = [], 0
    for width in widths:
        rows = grad_out[:, start : start + width]
        sent = jnp.dot(place, rows, preferred_element_type=F32).astype(BF16)
        got = lax.all_to_all(
            sent.reshape(groups, held, capacity, width),
            "expert",
            split_axis=0,
            concat_axis=0,
            tiled=True,
        )
        arrived.append([got.transpose(1, 0, 2, 3).reshape(held, groups * capacity, width)])
        start += width
    return flat, arrived


def body(grad_out, route_ids, route_probs, hidden, w_down):
    groups = lax.axis_size("expert")
    dp = lax.axis_size("dp")
    held, units, features = w_down.shape
    capacity = hidden.shape[3]
    slots = groups * held * capacity
    per_expert = slots // held
    tokens, chosen = route_ids.shape
    share, across = units // dp, dp // 2
    direct = groups == LINE * SIDES
    widths = chunks_of(features)
    count = len(widths)

    ids, probs = route_ids.T, route_probs.T
    call = Chain()
    if direct:
        relay = Relay(call, grad_out, ids, probs, held, capacity, widths)
        flat, saved = relay.flat, hidden[0]
    else:
        flat, arrived = exchanged(grad_out, ids, probs, groups, held, capacity, widths)
        saved = hidden[0].transpose(1, 0, 2, 3).reshape(1, held, per_expert, units)
    turned = call(
        functools.partial(turn_kernel, dp),
        sds((held, 2, across, share, per_expert), BF16),
        saved,
    )
    if direct:
        arrived = [relay.chunk(c) for c in range(min(2, count))]

    starts = [sum(widths[:c]) for c in range(count)]
    flops = [2 * slots * units * w for w in widths]
    state = {"raw": None, "grad": None}
    summed = []

    def reduced(c):
        parts, width = arrived[c], widths[c]
        piece = sds((across, held, share, width), BF16)
        keep, give = call(term_kernel, [piece, piece], turned, *parts, flops=flops[c])
        got = lax.ppermute(give, "dp", [(i, i ^ 1) for i in range(dp)])
        final = c == count - 1
        if final:
            outs = [sds(saved.shape, BF16), sds((held, per_expert), F32)]
        else:
            outs = [sds((held, per_expert, units), F32)]
        extra = ([state["raw"]] if c else []) + ([saved] if final else [])
        kernel = functools.partial(raw_kernel, len(parts), starts[c], final)
        made = call(kernel, outs, w_down, *parts, *extra, flops=flops[c])
        state["raw"] = made if final else made[0]
        pairs = call(pair_kernel, [sds((held, share, width), BF16)] * (across - 1), keep, got)
        others = []
        for step in range(1, across):
            shift = [(2 * r + i, 2 * ((r + step) % across) + i) for r in range(across) for i in range(2)]
            others.append(lax.ppermute(pairs[step - 1], "dp", shift))
        summed.append((keep, got, others))

    def finished(c):
        keep, got, others = summed[c]
        before = [] if state["grad"] is None else [state["grad"]]
        count = 2 + len(others)
        state["grad"], _ = call(
            functools.partial(last_kernel, len(others), starts[c]),
            [sds((share, held, features), F32), sds((8, 128), F32)],
            keep,
            got,
            *others,
            *before,
            in_specs=[VMEM] * count + [ANY] * len(before),
            out_specs=[ANY, VMEM],
            input_output_aliases={count: 0} if before else {},
            scratch_shapes=[
                pltpu.VMEM((share, held, widths[c]), F32),
                pltpu.SemaphoreType.DMA,
            ],
        )

    for c in range(count):
        reduced(c)
        if direct and c + 2 < count:
            arrived.append(relay.chunk(c + 2))
        if c >= 1:
            finished(c - 1)
    hidden_grad, sums = state["raw"]

    if direct:
        swap = [(i, i ^ 1) for i in range(groups)]
        both = jnp.stack([sums, lax.ppermute(sums, "expert", swap)])
        returned = [both] + [
            lax.ppermute(both, "expert", [(i, i ^ (SIDES * d)) for i in range(groups)])
            for d in range(1, LINE)
        ]
    else:
        sums = sums.reshape(held, groups, capacity).transpose(1, 0, 2).reshape(groups, -1)
        hidden_grad = hidden_grad.reshape(held, groups, capacity, units).transpose(1, 0, 2, 3)
        returned = lax.all_to_all(sums, "expert", split_axis=0, concat_axis=0, tiled=True)
        returned = [returned.reshape(-1, 128)]
    prob_grad = call(
        functools.partial(prob_kernel, direct, capacity),
        sds((chosen, tokens), F32),
        flat,
        probs,
        *returned,
        keep=False,
    ).T
    finished(count - 1)
    weight_grad = state["grad"]
    return (hidden_grad.reshape(hidden.shape), prob_grad, weight_grad)


def solution(mesh):
    in_specs = (
        P(("dp", "expert"), None),
        P(("dp", "expert"), None),
        P(("dp", "expert"), None),
        P("dp", None, "expert", None, None),
        P("expert", None, None),
    )
    out_specs = (
        P("dp", None, "expert", None, None),
        P(("dp", "expert"), None),
        P("dp", "expert", None),
    )
    return jax.shard_map(body, mesh=mesh, in_specs=in_specs, out_specs=out_specs, check_vma=False)
```

time: 104 us -> 105 us (level)
  starting transfers between devices: 43.4 us -> 32.5 us
  waiting for transfers between devices: 42.8 us -> 51.4 us
  local copies, waits for them, and re-layouts: 3.46 us -> 6.33 us
    ppermute x24 -> x22, waiting for transfers between devices: 32.1 us -> 47.5 us  [the longest x14 34.1 us: send(): lax.ppermute(block, 'expert', [(i, i ^ mask) for i in range(LINE * SIDES)])]
    ppermute x24 -> x22, starting transfers between devices: 36.7 us -> 26.6 us  [the longest x14 21.9 us: send(): lax.ppermute(block, 'expert', [(i, i ^ mask) for i in range(LINE * SIDES)])]
    ppermute x3, waiting for transfers between devices: 7.43 us -> 1.81 us  [body(): lax.ppermute(both, 'expert', [(i, i ^ SIDES * d) for i in range(groups)])]
    unnamed x16 -> x18, local copies, waits for them, and re-layouts: 3.46 us -> 6.33 us
    ppermute x3, starting transfers between devices: 6.48 us -> 4.39 us  [body(): lax.ppermute(both, 'expert', [(i, i ^ SIDES * d) for i in range(groups)])]
    ppermute x1, starting transfers between devices: 0.27 us -> 1.49 us  [body(): both = jnp.stack([sums, lax.ppermute(sums, 'expert', swap)])]
    ppermute x1, waiting for transfers between devices: 3.32 us -> 2.09 us  [body(): both = jnp.stack([sums, lax.ppermute(sums, 'expert', swap)])]
    pallas_call x27 -> x23, Pallas kernels: 13.2 us -> 13.7 us  [__call__(): pl.pallas_call(body, out_shape=outs, in_specs=in_specs, compiler_params=P...]
  transfers between devices with their start and end apart: 28 -> 26, of which waited for: 18 -> 12; matrix products, arithmetic and copies ran while one was open for 0% -> 0% of each run, Pallas kernels for 11% -> 9%
where the time goes in v4:
time: 105 us
  waiting for transfers between devices  51.4 us (49%)
  starting transfers between devices  32.5 us (31%)
  Pallas kernels  13.7 us (13%)
  local copies, waits for them, and re-layouts  6.33 us (6%)
    ppermute x14, waiting for transfers between devices, send(): lax.ppermute(block, 'expert', [(i, i ^ mask) for i in range(LINE * SIDES)])  34.1 us
    ppermute x14, starting transfers between devices, send(): lax.ppermute(block, 'expert', [(i, i ^ mask) for i in range(LINE * SIDES)])  21.9 us
    pallas_call x23, Pallas kernels, __call__(): pl.pallas_call(body, out_shape=outs, in_specs=in_specs, compiler_params=P...  13.7 us
    ppermute x4, waiting for transfers between devices, reduced(): others.append(lax.ppermute(pairs[step - 1], 'dp', shift))  13.4 us
    unnamed x18, local copies, waits for them, and re-layouts  6.33 us
    ppermute x4, starting transfers between devices, reduced(): others.append(lax.ppermute(pairs[step - 1], 'dp', shift))  4.46 us
    ppermute x3, starting transfers between devices, body(): lax.ppermute(both, 'expert', [(i, i ^ SIDES * d) for i in range(groups)])  4.39 us
  transfers between devices with their start and end apart: 26, of which 12 were waited for; matrix products, arithmetic and copies ran while one was open for 0% of the time, Pallas kernels for 9%

profile of v4, /device:TPU:0, one launch (start us, length us, event | category | flops | bytes accessed | tf_op | source)
XLA Modules:
  0.0 104.9 jit_solution(8665748718300258315)
XLA Ops:
  3.3 3.0 %collective-permute-start = (bf16[128,1536]{1,0:T(8,128)(2,1)S(1)}, bf16[128,1536]{1,0:T(8,128)(2,1)S(1)}, u32[]{:S(2)}, u32[]{:S(2)}) collective-permute-start(bf16[128,1536]{1,0:T(8,128)(2,1)S(1)} %get-tuple-element.40), channel_id=1, source_target_pairs={{0,1},{1,0},{2,3},{3,2},{4,5},{5,4},{6,7},{7,6},{8,9},{9,8},{10,11... | collective-permute-start | bytes 1179656 | tf_op jit(solution)/shard_map/ppermute | solution.py:277
  7.7 10.8 %collective-permute-done.1.refs_1_ = bf16[144,512]{1,0:T(8,128)(2,1)S(1)} collective-permute-done((bf16[144,512]{1,0:T(8,128)(2,1)S(1)}, bf16[144,512]{1,0:T(8,128)(2,1)S(1)}, u32[]{:S(2)}, u32[]{:S(2)}) %collective-permute-start.1) | collective-permute-done | bytes 147488 | tf_op jit(solution)/shard_map/ppermute | solution.py:277
  18.8 1.9 %collective-permute-start.5 = (bf16[2,64,512]{2,1,0:T(8,128)(2,1)S(1)}, bf16[2,64,512]{2,1,0:T(8,128)(2,1)S(1)}, u32[]{:S(2)}, u32[]{:S(2)}) collective-permute-start(bf16[2,64,512]{2,1,0:T(8,128)(2,1)S(1)} %get-tuple-element.48), channel_id=1, source_target_pairs={{0,2},{1,3},{2,0},{3,1},{4,6},{5,7},{6,4},{7,5},{8,10},{9,11},{10,... | collective-permute-start | bytes 393224 | tf_op jit(solution)/shard_map/ppermute | solution.py:277
  20.7 2.6 %collective-permute-start.6 = (bf16[2,64,512]{2,1,0:T(8,128)(2,1)S(1)}, bf16[2,64,512]{2,1,0:T(8,128)(2,1)S(1)}, u32[]{:S(2)}, u32[]{:S(2)}) collective-permute-start(bf16[2,64,512]{2,1,0:T(8,128)(2,1)S(1)} %get-tuple-element.49), channel_id=1, source_target_pairs={{0,4},{1,5},{2,6},{3,7},{4,0},{5,1},{6,2},{7,3},{8,12},{9,13},{10,... | collective-permute-start | bytes 393224 | tf_op jit(solution)/shard_map/ppermute | solution.py:277
  23.6 1.7 %collective-permute-done.5.refs_2_ = bf16[2,64,512]{2,1,0:T(8,128)(2,1)S(1)} collective-permute-done((bf16[2,64,512]{2,1,0:T(8,128)(2,1)S(1)}, bf16[2,64,512]{2,1,0:T(8,128)(2,1)S(1)}, u32[]{:S(2)}, u32[]{:S(2)}) %collective-permute-start.5) | collective-permute-done | bytes 131104 | tf_op jit(solution)/shard_map/ppermute | solution.py:277
  25.3 7.5 %collective-permute-done.6.refs_3_ = bf16[2,64,512]{2,1,0:T(8,128)(2,1)S(1)} collective-permute-done((bf16[2,64,512]{2,1,0:T(8,128)(2,1)S(1)}, bf16[2,64,512]{2,1,0:T(8,128)(2,1)S(1)}, u32[]{:S(2)}, u32[]{:S(2)}) %collective-permute-start.6) | collective-permute-done | bytes 131104 | tf_op jit(solution)/shard_map/ppermute | solution.py:277
  33.4 2.0 %collective-permute-start.2 = (bf16[2,64,512]{2,1,0:T(8,128)(2,1)S(1)}, bf16[2,64,512]{2,1,0:T(8,128)(2,1)S(1)}, u32[]{:S(2)}, u32[]{:S(2)}) collective-permute-start(bf16[2,64,512]{2,1,0:T(8,128)(2,1)S(1)} %get-tuple-element.44), channel_id=1, source_target_pairs={{0,2},{1,3},{2,0},{3,1},{4,6},{5,7},{6,4},{7,5},{8,10},{9,11},{10,... | collective-permute-start | bytes 393224 | tf_op jit(solution)/shard_map/ppermute | solution.py:277
  37.9 2.8 %copy-done = bf16[2,768,2048]{2,1,0:T(8,128)(2,1)S(1)} copy-done((bf16[2,768,2048]{2,1,0:T(8,128)(2,1)S(1)}, bf16[2,768,2048]{2,1,0:T(8,128)(2,1)}, u32[]{:S(2)}) %copy-start) | copy-done | bytes 6291480
  41.8 6.6 %collective-permute-done.3.refs_3_ = bf16[2,64,512]{2,1,0:T(8,128)(2,1)S(1)} collective-permute-done((bf16[2,64,512]{2,1,0:T(8,128)(2,1)S(1)}, bf16[2,64,512]{2,1,0:T(8,128)(2,1)S(1)}, u32[]{:S(2)}, u32[]{:S(2)}) %collective-permute-start.3) | collective-permute-done | bytes 131104 | tf_op jit(solution)/shard_map/ppermute | solution.py:277
  49.0 1.6 %collective-permute-start.16 = (bf16[2,192,512]{2,1,0:T(8,128)(2,1)S(1)}, bf16[2,192,512]{2,1,0:T(8,128)(2,1)S(1)}, u32[]{:S(2)}, u32[]{:S(2)}) collective-permute-start(bf16[2,192,512]{2,1,0:T(8,128)(2,1)S(1)} %shard_map.82.refs_3_), channel_id=1, source_target_pairs={{0,16},{8,24},{16,0},{24,8},{1,17},{9,25},{17,1},{25,9},{2,18},{10... | collective-permute-start | bytes 1179656 | tf_op jit(solution)/shard_map/ppermute | solution.py:371
  50.6 2.6 %collective-permute-start.13 = (bf16[2,64,512]{2,1,0:T(8,128)(2,1)S(1)}, bf16[2,64,512]{2,1,0:T(8,128)(2,1)S(1)}, u32[]{:S(2)}, u32[]{:S(2)}) collective-permute-start(bf16[2,64,512]{2,1,0:T(8,128)(2,1)S(1)} %get-tuple-element.61), channel_id=1, source_target_pairs={{0,2},{1,3},{2,0},{3,1},{4,6},{5,7},{6,4},{7,5},{8,10},{9,11},{10,... | collective-permute-start | bytes 393224 | tf_op jit(solution)/shard_map/ppermute | solution.py:277
  56.7 3.9 %collective-permute-done.16.refs_2_ = bf16[2,192,512]{2,1,0:T(8,128)(2,1)S(1)} collective-permute-done((bf16[2,192,512]{2,1,0:T(8,128)(2,1)S(1)}, bf16[2,192,512]{2,1,0:T(8,128)(2,1)S(1)}, u32[]{:S(2)}, u32[]{:S(2)}) %collective-permute-start.16) | collective-permute-done | bytes 393248 | tf_op jit(solution)/shard_map/ppermute | solution.py:371
  61.7 4.4 %collective-permute-done.14.refs_3_ = bf16[2,64,512]{2,1,0:T(8,128)(2,1)S(1)} collective-permute-done((bf16[2,64,512]{2,1,0:T(8,128)(2,1)S(1)}, bf16[2,64,512]{2,1,0:T(8,128)(2,1)S(1)}, u32[]{:S(2)}, u32[]{:S(2)}) %collective-permute-start.14) | collective-permute-done | bytes 131104 | tf_op jit(solution)/shard_map/ppermute | solution.py:277
  67.3 2.3 %collective-permute-start.10 = (bf16[2,64,512]{2,1,0:T(8,128)(2,1)S(1)}, bf16[2,64,512]{2,1,0:T(8,128)(2,1)S(1)}, u32[]{:S(2)}, u32[]{:S(2)}) collective-permute-start(bf16[2,64,512]{2,1,0:T(8,128)(2,1)S(1)} %get-tuple-element.57), channel_id=1, source_target_pairs={{0,2},{1,3},{2,0},{3,1},{4,6},{5,7},{6,4},{7,5},{8,10},{9,11},{10,... | collective-permute-start | bytes 393224 | tf_op jit(solution)/shard_map/ppermute | solution.py:277
  72.8 5.5 %collective-permute-done.17.refs_2_ = bf16[2,192,512]{2,1,0:T(8,128)(2,1)S(1)} collective-permute-done((bf16[2,192,512]{2,1,0:T(8,128)(2,1)S(1)}, bf16[2,192,512]{2,1,0:T(8,128)(2,1)S(1)}, u32[]{:S(2)}, u32[]{:S(2)}) %collective-permute-start.17) | collective-permute-done | bytes 393248 | tf_op jit(solution)/shard_map/ppermute | solution.py:371
  79.5 3.1 %collective-permute-done.11.refs_3_ = bf16[2,64,512]{2,1,0:T(8,128)(2,1)S(1)} collective-permute-done((bf16[2,64,512]{2,1,0:T(8,128)(2,1)S(1)}, bf16[2,64,512]{2,1,0:T(8,128)(2,1)S(1)}, u32[]{:S(2)}, u32[]{:S(2)}) %collective-permute-start.11) | collective-permute-done | bytes 131104 | tf_op jit(solution)/shard_map/ppermute | solution.py:277
  83.2 1.6 %collective-permute-start.23 = (bf16[2,192,512]{2,1,0:T(8,128)(2,1)S(1)}, bf16[2,192,512]{2,1,0:T(8,128)(2,1)S(1)}, u32[]{:S(2)}, u32[]{:S(2)}) collective-permute-start(bf16[2,192,512]{2,1,0:T(8,128)(2,1)S(1)} %shard_map.91.refs_4_), channel_id=1, source_target_pairs={{0,16},{8,24},{16,0},{24,8},{1,17},{9,25},{17,1},{25,9},{2,18},{10... | collective-permute-start | bytes 1179656 | tf_op jit(solution)/shard_map/ppermute | solution.py:371
  84.8 1.5 %shard_map.94 = (bf16[8,2,32,768]{3,2,1,0:T(8,128)(2,1)}, f32[2,256]{1,0:T(2,128)S(1)}) custom-call(bf16[2,768,2048]{2,1,0:T(8,128)(2,1)S(1)} %copy-done.1, bf16[2,64,512]{2,1,0:T(8,128)(2,1)S(1)} %get-tuple-element.56.refs_1_, bf16[2,64,512]{2,1,0:T(8,128)(2,1)S(1)} %collective-permute-done.10.refs_2_, ...), custom_call_target="tpu_custom_call" | custom-call | flops 1 | bytes 1 | tf_op jit(solution)/shard_map/pallas_call | solution.py:38
  87.2 1.5 %collective-permute-start.19 = (f32[2,256]{1,0:T(2,128)S(1)}, f32[2,256]{1,0:T(2,128)S(1)}, u32[]{:S(2)}, u32[]{:S(2)}) collective-permute-start(f32[2,256]{1,0:T(2,128)S(1)} %get-tuple-element.71.refs_2_), channel_id=1, source_target_pairs={{0,1},{1,0},{2,3},{3,2},{4,5},{5,4},{6,7},{7,6},{8,9},{9,8},{10,11... | collective-permute-start | bytes 6152 | tf_op jit(solution)/shard_map/ppermute | solution.py:404
  88.7 2.1 %collective-permute-done.19 = f32[2,256]{1,0:T(2,128)S(1)} collective-permute-done((f32[2,256]{1,0:T(2,128)S(1)}, f32[2,256]{1,0:T(2,128)S(1)}, u32[]{:S(2)}, u32[]{:S(2)}) %collective-permute-start.19) | collective-permute-done | bytes 2080 | tf_op jit(solution)/shard_map/ppermute | solution.py:404
  90.8 2.3 %collective-permute-start.22 = (f32[2,2,256]{2,1,0:T(2,128)S(1)}, f32[2,2,256]{2,1,0:T(2,128)S(1)}, u32[]{:S(2)}, u32[]{:S(2)}) collective-permute-start(f32[2,2,256]{2,1,0:T(2,128)S(1)} %pad_maximum_fusion.refs_2_), channel_id=1, source_target_pairs={{0,6},{1,7},{2,4},{3,5},{4,2},{5,3},{6,0},{7,1},{8,14},{9,15},{10,... | collective-permute-start | bytes 12296 | tf_op jit(solution)/shard_map/ppermute | solution.py:406
  93.1 1.5 %collective-permute-start.21 = (f32[2,2,256]{2,1,0:T(2,128)S(1)}, f32[2,2,256]{2,1,0:T(2,128)S(1)}, u32[]{:S(2)}, u32[]{:S(2)}) collective-permute-start(f32[2,2,256]{2,1,0:T(2,128)S(1)} %pad_maximum_fusion.refs_2_), channel_id=1, source_target_pairs={{0,4},{1,5},{2,6},{3,7},{4,0},{5,1},{6,2},{7,3},{8,12},{9,13},{10,... | collective-permute-start | bytes 12296 | tf_op jit(solution)/shard_map/ppermute | solution.py:406
  99.1 4.1 %collective-permute-done.25.refs_2_ = bf16[2,192,512]{2,1,0:T(8,128)(2,1)S(1)} collective-permute-done((bf16[2,192,512]{2,1,0:T(8,128)(2,1)S(1)}, bf16[2,192,512]{2,1,0:T(8,128)(2,1)S(1)}, u32[]{:S(2)}, u32[]{:S(2)}) %collective-permute-start.25) | collective-permute-done | bytes 393248 | tf_op jit(solution)/shard_map/ppermute | solution.py:371
  103.2 1.7 %shard_map.98 = (f32[192,2,2048]{2,1,0:T(2,128)}, f32[8,128]{1,0:T(8,128)}) custom-call(bf16[2,2,192,512]{3,2,1,0:T(8,128)(2,1)S(1)} %get-tuple-element.73.refs_0_, bf16[2,2,192,512]{3,2,1,0:T(8,128)(2,1)S(1)} %collective-permute-done.24.refs_1_, bf16[2,192,512]{2,1,0:T(8,128)(2,1)S(1)} %collective-permute-done.25.refs_2_, ...), custom_call_target="tpu_custom_call", output_to_operand_aliasing={{0}: (3, {})} | custom-call | flops 1 | bytes 1 | tf_op jit(solution)/shard_map/pallas_call | solution.py:38
  (70 shorter events, 25.5 us)
Async XLA Ops:
  3.3 20.1 %collective-permute-start = (bf16[128,1536]{1,0:T(8,128)(2,1)S(1)}, bf16[128,1536]{1,0:T(8,128)(2,1)S(1)}, u32[]{:S(2)}, u32[]{:S(2)}) collective-permute-start(bf16[128,1536]{1,0:T(8,128)(2,1)S(1)} %get-tuple-element.40), channel_id=1, source_target_pairs={{0,1},{1,0},{2,3},{3,2},{4,5},{5,4},{6,7},{7,6},{8,9},{9,8},{10,11... | collective-permute-start | bytes 1179656 | tf_op jit(solution)/shard_map/ppermute | solution.py:277
  6.3 12.3 %collective-permute-start.1 = (bf16[144,512]{1,0:T(8,128)(2,1)S(1)}, bf16[144,512]{1,0:T(8,128)(2,1)S(1)}, u32[]{:S(2)}, u32[]{:S(2)}) collective-permute-start(bf16[144,512]{1,0:T(8,128)(2,1)S(1)} %get-tuple-element.41.refs_1_.refs_0_), channel_id=1, source_target_pairs={{0,1},{1,0},{2,3},{3,2},{4,5},{5,4},{6,7},{7,6},{8,9},{9,8},{10,11... | collective-permute-start | bytes 442376 | tf_op jit(solution)/shard_map/ppermute | solution.py:277
  18.8 6.4 %collective-permute-start.5 = (bf16[2,64,512]{2,1,0:T(8,128)(2,1)S(1)}, bf16[2,64,512]{2,1,0:T(8,128)(2,1)S(1)}, u32[]{:S(2)}, u32[]{:S(2)}) collective-permute-start(bf16[2,64,512]{2,1,0:T(8,128)(2,1)S(1)} %get-tuple-element.48), channel_id=1, source_target_pairs={{0,2},{1,3},{2,0},{3,1},{4,6},{5,7},{6,4},{7,5},{8,10},{9,11},{10,... | collective-permute-start | bytes 393224 | tf_op jit(solution)/shard_map/ppermute | solution.py:277
  20.7 12.1 %collective-permute-start.6 = (bf16[2,64,512]{2,1,0:T(8,128)(2,1)S(1)}, bf16[2,64,512]{2,1,0:T(8,128)(2,1)S(1)}, u32[]{:S(2)}, u32[]{:S(2)}) collective-permute-start(bf16[2,64,512]{2,1,0:T(8,128)(2,1)S(1)} %get-tuple-element.49), channel_id=1, source_target_pairs={{0,4},{1,5},{2,6},{3,7},{4,0},{5,1},{6,2},{7,3},{8,12},{9,13},{10,... | collective-permute-start | bytes 393224 | tf_op jit(solution)/shard_map/ppermute | solution.py:277
  23.3 9.5 %collective-permute-start.7 = (bf16[2,64,512]{2,1,0:T(8,128)(2,1)S(1)}, bf16[2,64,512]{2,1,0:T(8,128)(2,1)S(1)}, u32[]{:S(2)}, u32[]{:S(2)}) collective-permute-start(bf16[2,64,512]{2,1,0:T(8,128)(2,1)S(1)} %get-tuple-element.50), channel_id=1, source_target_pairs={{0,6},{1,7},{2,4},{3,5},{4,2},{5,3},{6,0},{7,1},{8,14},{9,15},{10,... | collective-permute-start | bytes 393224 | tf_op jit(solution)/shard_map/ppermute | solution.py:277
  33.4 8.0 %collective-permute-start.8 = (bf16[2,2,192,512]{3,2,1,0:T(8,128)(2,1)S(1)}, bf16[2,2,192,512]{3,2,1,0:T(8,128)(2,1)S(1)}, u32[]{:S(2)}, u32[]{:S(2)}) collective-permute-start(bf16[2,2,192,512]{3,2,1,0:T(8,128)(2,1)S(1)} %get-tuple-element.52.refs_5_), channel_id=1, source_target_pairs={{0,8},{8,0},{16,24},{24,16},{1,9},{9,1},{17,25},{25,17},{2,10},{10... | collective-permute-start | bytes 2359304 | tf_op jit(solution)/shard_map/ppermute | solution.py:357
  33.4 8.3 %collective-permute-start.2 = (bf16[2,64,512]{2,1,0:T(8,128)(2,1)S(1)}, bf16[2,64,512]{2,1,0:T(8,128)(2,1)S(1)}, u32[]{:S(2)}, u32[]{:S(2)}) collective-permute-start(bf16[2,64,512]{2,1,0:T(8,128)(2,1)S(1)} %get-tuple-element.44), channel_id=1, source_target_pairs={{0,2},{1,3},{2,0},{3,1},{4,6},{5,7},{6,4},{7,5},{8,10},{9,11},{10,... | collective-permute-start | bytes 393224 | tf_op jit(solution)/shard_map/ppermute | solution.py:277
  35.5 12.9 %collective-permute-start.3 = (bf16[2,64,512]{2,1,0:T(8,128)(2,1)S(1)}, bf16[2,64,512]{2,1,0:T(8,128)(2,1)S(1)}, u32[]{:S(2)}, u32[]{:S(2)}) collective-permute-start(bf16[2,64,512]{2,1,0:T(8,128)(2,1)S(1)} %get-tuple-element.45), channel_id=1, source_target_pairs={{0,4},{1,5},{2,6},{3,7},{4,0},{5,1},{6,2},{7,3},{8,12},{9,13},{10,... | collective-permute-start | bytes 393224 | tf_op jit(solution)/shard_map/ppermute | solution.py:277
  36.6 11.8 %collective-permute-start.4 = (bf16[2,64,512]{2,1,0:T(8,128)(2,1)S(1)}, bf16[2,64,512]{2,1,0:T(8,128)(2,1)S(1)}, u32[]{:S(2)}, u32[]{:S(2)}) collective-permute-start(bf16[2,64,512]{2,1,0:T(8,128)(2,1)S(1)} %get-tuple-element.46.refs_5_), channel_id=1, source_target_pairs={{0,6},{1,7},{2,4},{3,5},{4,2},{5,3},{6,0},{7,1},{8,14},{9,15},{10,... | collective-permute-start | bytes 393224 | tf_op jit(solution)/shard_map/ppermute | solution.py:277
  49.0 7.4 %collective-permute-start.9 = (bf16[2,2,192,512]{3,2,1,0:T(8,128)(2,1)S(1)}, bf16[2,2,192,512]{3,2,1,0:T(8,128)(2,1)S(1)}, u32[]{:S(2)}, u32[]{:S(2)}) collective-permute-start(bf16[2,2,192,512]{3,2,1,0:T(8,128)(2,1)S(1)} %get-tuple-element.55.refs_6_), channel_id=1, source_target_pairs={{0,8},{8,0},{16,24},{24,16},{1,9},{9,1},{17,25},{25,17},{2,10},{10... | collective-permute-start | bytes 2359304 | tf_op jit(solution)/shard_map/ppermute | solution.py:357
  49.0 11.5 %collective-permute-start.16 = (bf16[2,192,512]{2,1,0:T(8,128)(2,1)S(1)}, bf16[2,192,512]{2,1,0:T(8,128)(2,1)S(1)}, u32[]{:S(2)}, u32[]{:S(2)}) collective-permute-start(bf16[2,192,512]{2,1,0:T(8,128)(2,1)S(1)} %shard_map.82.refs_3_), channel_id=1, source_target_pairs={{0,16},{8,24},{16,0},{24,8},{1,17},{9,25},{17,1},{25,9},{2,18},{10... | collective-permute-start | bytes 1179656 | tf_op jit(solution)/shard_map/ppermute | solution.py:371
  50.6 11.1 %collective-permute-start.13 = (bf16[2,64,512]{2,1,0:T(8,128)(2,1)S(1)}, bf16[2,64,512]{2,1,0:T(8,128)(2,1)S(1)}, u32[]{:S(2)}, u32[]{:S(2)}) collective-permute-start(bf16[2,64,512]{2,1,0:T(8,128)(2,1)S(1)} %get-tuple-element.61), channel_id=1, source_target_pairs={{0,2},{1,3},{2,0},{3,1},{4,6},{5,7},{6,4},{7,5},{8,10},{9,11},{10,... | collective-permute-start | bytes 393224 | tf_op jit(solution)/shard_map/ppermute | solution.py:277
  53.2 12.9 %collective-permute-start.14 = (bf16[2,64,512]{2,1,0:T(8,128)(2,1)S(1)}, bf16[2,64,512]{2,1,0:T(8,128)(2,1)S(1)}, u32[]{:S(2)}, u32[]{:S(2)}) collective-permute-start(bf16[2,64,512]{2,1,0:T(8,128)(2,1)S(1)} %get-tuple-element.62), channel_id=1, source_target_pairs={{0,4},{1,5},{2,6},{3,7},{4,0},{5,1},{6,2},{7,3},{8,12},{9,13},{10,... | collective-permute-start | bytes 393224 | tf_op jit(solution)/shard_map/ppermute | solution.py:277
  54.2 11.9 %collective-permute-start.15 = (bf16[2,64,512]{2,1,0:T(8,128)(2,1)S(1)}, bf16[2,64,512]{2,1,0:T(8,128)(2,1)S(1)}, u32[]{:S(2)}, u32[]{:S(2)}) collective-permute-start(bf16[2,64,512]{2,1,0:T(8,128)(2,1)S(1)} %get-tuple-element.53.refs_5_), channel_id=1, source_target_pairs={{0,6},{1,7},{2,4},{3,5},{4,2},{5,3},{6,0},{7,1},{8,14},{9,15},{10,... | collective-permute-start | bytes 393224 | tf_op jit(solution)/shard_map/ppermute | solution.py:277
  66.7 6.0 %collective-permute-start.18 = (bf16[2,2,192,512]{3,2,1,0:T(8,128)(2,1)S(1)}, bf16[2,2,192,512]{3,2,1,0:T(8,128)(2,1)S(1)}, u32[]{:S(2)}, u32[]{:S(2)}) collective-permute-start(bf16[2,2,192,512]{3,2,1,0:T(8,128)(2,1)S(1)} %get-tuple-element.64.refs_6_), channel_id=1, source_target_pairs={{0,8},{8,0},{16,24},{24,16},{1,9},{9,1},{17,25},{25,17},{2,10},{10... | collective-permute-start | bytes 2359304 | tf_op jit(solution)/shard_map/ppermute | solution.py:357
  66.8 11.5 %collective-permute-start.17 = (bf16[2,192,512]{2,1,0:T(8,128)(2,1)S(1)}, bf16[2,192,512]{2,1,0:T(8,128)(2,1)S(1)}, u32[]{:S(2)}, u32[]{:S(2)}) collective-permute-start(bf16[2,192,512]{2,1,0:T(8,128)(2,1)S(1)} %shard_map.86.refs_3_), channel_id=1, source_target_pairs={{0,16},{8,24},{16,0},{24,8},{1,17},{9,25},{17,1},{25,9},{2,18},{10... | collective-permute-start | bytes 1179656 | tf_op jit(solution)/shard_map/ppermute | solution.py:371
  67.3 12.1 %collective-permute-start.10 = (bf16[2,64,512]{2,1,0:T(8,128)(2,1)S(1)}, bf16[2,64,512]{2,1,0:T(8,128)(2,1)S(1)}, u32[]{:S(2)}, u32[]{:S(2)}) collective-permute-start(bf16[2,64,512]{2,1,0:T(8,128)(2,1)S(1)} %get-tuple-element.57), channel_id=1, source_target_pairs={{0,2},{1,3},{2,0},{3,1},{4,6},{5,7},{6,4},{7,5},{8,10},{9,11},{10,... | collective-permute-start | bytes 393224 | tf_op jit(solution)/shard_map/ppermute | solution.py:277
  69.7 12.9 %collective-permute-start.11 = (bf16[2,64,512]{2,1,0:T(8,128)(2,1)S(1)}, bf16[2,64,512]{2,1,0:T(8,128)(2,1)S(1)}, u32[]{:S(2)}, u32[]{:S(2)}) collective-permute-start(bf16[2,64,512]{2,1,0:T(8,128)(2,1)S(1)} %get-tuple-element.58), channel_id=1, source_target_pairs={{0,4},{1,5},{2,6},{3,7},{4,0},{5,1},{6,2},{7,3},{8,12},{9,13},{10,... | collective-permute-start | bytes 393224 | tf_op jit(solution)/shard_map/ppermute | solution.py:277
  70.6 11.9 %collective-permute-start.12 = (bf16[2,64,512]{2,1,0:T(8,128)(2,1)S(1)}, bf16[2,64,512]{2,1,0:T(8,128)(2,1)S(1)}, u32[]{:S(2)}, u32[]{:S(2)}) collective-permute-start(bf16[2,64,512]{2,1,0:T(8,128)(2,1)S(1)} %get-tuple-element.59.refs_3_), channel_id=1, source_target_pairs={{0,6},{1,7},{2,4},{3,5},{4,2},{5,3},{6,0},{7,1},{8,14},{9,15},{10,... | collective-permute-start | bytes 393224 | tf_op jit(solution)/shard_map/ppermute | solution.py:277
  83.2 12.0 %collective-permute-start.23 = (bf16[2,192,512]{2,1,0:T(8,128)(2,1)S(1)}, bf16[2,192,512]{2,1,0:T(8,128)(2,1)S(1)}, u32[]{:S(2)}, u32[]{:S(2)}) collective-permute-start(bf16[2,192,512]{2,1,0:T(8,128)(2,1)S(1)} %shard_map.91.refs_4_), channel_id=1, source_target_pairs={{0,16},{8,24},{16,0},{24,8},{1,17},{9,25},{17,1},{25,9},{2,18},{10... | collective-permute-start | bytes 1179656 | tf_op jit(solution)/shard_map/ppermute | solution.py:371
  86.5 16.7 %collective-permute-start.25 = (bf16[2,192,512]{2,1,0:T(8,128)(2,1)S(1)}, bf16[2,192,512]{2,1,0:T(8,128)(2,1)S(1)}, u32[]{:S(2)}, u32[]{:S(2)}) collective-permute-start(bf16[2,192,512]{2,1,0:T(8,128)(2,1)S(1)} %shard_map.95.refs_4_), channel_id=1, source_target_pairs={{0,16},{8,24},{16,0},{24,8},{1,17},{9,25},{17,1},{25,9},{2,18},{10... | collective-permute-start | bytes 1179656 | tf_op jit(solution)/shard_map/ppermute | solution.py:371
  90.8 5.6 %collective-permute-start.22 = (f32[2,2,256]{2,1,0:T(2,128)S(1)}, f32[2,2,256]{2,1,0:T(2,128)S(1)}, u32[]{:S(2)}, u32[]{:S(2)}) collective-permute-start(f32[2,2,256]{2,1,0:T(2,128)S(1)} %pad_maximum_fusion.refs_2_), channel_id=1, source_target_pairs={{0,6},{1,7},{2,4},{3,5},{4,2},{5,3},{6,0},{7,1},{8,14},{9,15},{10,... | collective-permute-start | bytes 12296 | tf_op jit(solution)/shard_map/ppermute | solution.py:406
  93.1 4.5 %collective-permute-start.21 = (f32[2,2,256]{2,1,0:T(2,128)S(1)}, f32[2,2,256]{2,1,0:T(2,128)S(1)}, u32[]{:S(2)}, u32[]{:S(2)}) collective-permute-start(f32[2,2,256]{2,1,0:T(2,128)S(1)} %pad_maximum_fusion.refs_2_), channel_id=1, source_target_pairs={{0,4},{1,5},{2,6},{3,7},{4,0},{5,1},{6,2},{7,3},{8,12},{9,13},{10,... | collective-permute-start | bytes 12296 | tf_op jit(solution)/shard_map/ppermute | solution.py:406
  94.6 3.6 %collective-permute-start.20 = (f32[2,2,256]{2,1,0:T(2,128)S(1)}, f32[2,2,256]{2,1,0:T(2,128)S(1)}, u32[]{:S(2)}, u32[]{:S(2)}) collective-permute-start(f32[2,2,256]{2,1,0:T(2,128)S(1)} %pad_maximum_fusion.refs_2_), channel_id=1, source_target_pairs={{0,2},{1,3},{2,0},{3,1},{4,6},{5,7},{6,4},{7,5},{8,10},{9,11},{10,... | collective-permute-start | bytes 12296 | tf_op jit(solution)/shard_map/ppermute | solution.py:406
  (11 other events, 66.0 us)

commit v5 on v4

--- a/solution.py
+++ b/solution.py
@@ -8,7 +8,6 @@
 from jax.sharding import PartitionSpec as P
 
 F32, BF16, I32 = jnp.float32, jnp.bfloat16, jnp.int32
-PARAMS = pltpu.CompilerParams(vmem_limit_bytes=24 * 1024 * 1024)
 VMEM = pl.BlockSpec(memory_space=pltpu.VMEM)
 ANY = pl.BlockSpec(memory_space=pl.ANY)
 HBM = pl.BlockSpec(memory_space=pltpu.HBM)
@@ -17,34 +16,31 @@
 INFO = 16
 
 
-def nbytes(shapes):
-    return sum(x.size * x.dtype.itemsize for x in jax.tree.leaves(shapes))
-
-
 class Chain:
     def __init__(self):
         self.last = None
 
-    def __call__(self, kernel, outs, *args, flops=0, in_specs=None, keep=True, **kw):
+    def __call__(self, kernel, outs, *args, in_specs=None, keep=True, after=(), room=24, **kw):
         in_specs = list(in_specs or [VMEM] * len(args))
         count = len(args)
         body = kernel
-        if self.last is not None:
-            args, in_specs = (*args, self.last), in_specs + [ANY]
+        unread = [*after] if self.last is None else [self.last, *after]
+        if unread:
+            args, in_specs = (*args, *unread), in_specs + [ANY] * len(unread)
 
             def body(*refs):
-                kernel(*refs[:count], *refs[count + 1 :])
+                kernel(*refs[:count], *refs[count + len(unread) :])
 
         made = pl.pallas_call(
             body,
             out_shape=outs,
             in_specs=in_specs,
-            compiler_params=PARAMS,
+            compiler_params=pltpu.CompilerParams(vmem_limit_bytes=room * 1024 * 1024),
             cost_estimate=pl.CostEstimate(flops=1, bytes_accessed=1, transcendentals=0),
             **kw,
         )(*args)
         if keep:
-            self.last = jax.tree.leaves(made)[-1]
+            self.last = min(jax.tree.leaves(made), key=lambda x: x.size)
         return made
 
 
@@ -65,17 +61,21 @@
     return [jnp.sum(jnp.where(n, before, 0.0), axis=0, keepdims=True) for n in named]
 
 
-def begin_kernel(experts, capacity, ids_ref, probs_ref, rows_ref, flat_ref, rest_ref, out_ref, sems):
-    chosen, tokens = ids_ref.shape
+def begin_kernel(experts, capacity, ids_ref, probs_ref, rows_ref, flat_ref, out_ref, *scratch):
+    ids_got, probs_got, sems = scratch
+    chosen, tokens = ids_got.shape
     width = out_ref.shape[1]
     copies = [
-        pltpu.make_async_copy(rows_ref.at[:, :width], out_ref.at[:tokens], sems.at[0]),
-        pltpu.make_async_copy(rows_ref.at[:, width:], rest_ref, sems.at[1]),
+        pltpu.make_async_copy(ids_ref, ids_got, sems.at[0]),
+        pltpu.make_async_copy(probs_ref, probs_got, sems.at[1]),
+        pltpu.make_async_copy(rows_ref.at[:, :width], out_ref.at[:tokens], sems.at[2]),
     ]
     for copy in copies:
         copy.start()
-    ids = ids_ref[...]
-    _, _, word = gates_of(probs_ref[...])
+    for copy in copies:
+        copy.wait()
+    ids = ids_got[...]
+    _, _, word = gates_of(probs_got[...])
     slots = slots_of(ids, experts)
     for k in range(chosen):
         flat_ref[k : k + 1, :] = ids[k : k + 1] * capacity + slots[k].astype(I32)
@@ -84,15 +84,15 @@
     out_ref[tokens:, :tokens] = info
     if width > tokens:
         out_ref[tokens:, tokens:] = jnp.zeros((INFO, width - tokens), BF16)
-    for copy in copies:
-        copy.wait()
 
 
 def pick_kernel(held, capacity, chosen, start, own_ref, other_ref, *refs):
     tokens = own_ref.shape[0] - (INFO if start is None else 0)
     rows = held * capacity
     if start is None:
-        place_ref, out_refs = refs[-1], refs[:-1]
+        rows_ref, *out_refs, place_ref, rest_ref, sem = refs
+        copy = pltpu.make_async_copy(rows_ref.at[:, own_ref.shape[1] :], rest_ref, sem)
+        copy.start()
         me = lax.axis_index("expert")
         local = lax.broadcasted_iota(I32, (rows, tokens), 0)
         for side, ref in enumerate((own_ref, other_ref)):
@@ -121,9 +121,12 @@
             for e in range(held):
                 at = d * rows + e * capacity
                 out_ref[e, side * capacity : (side + 1) * capacity, :] = scaled[at : at + capacity]
-
-
-def turn_kernel(dp, hidden_ref, out_ref):
+    if start is None:
+        copy.wait()
+
+
+def turn_kernel(dp, hidden_ref, *refs):
+    out_ref = refs[-1]
     parts, held, _, units = hidden_ref.shape
     share, across = units // dp, dp // 2
     me = lax.axis_index("expert") if parts > 1 else 0
@@ -155,18 +158,25 @@
 
 
 def pair_kernel(keep_ref, got_ref, *out_refs):
-    for step, ref in enumerate(out_refs, 1):
-        ref[...] = (keep_ref[step].astype(F32) + got_ref[step].astype(F32)).astype(BF16)
+    for step in range(1, keep_ref.shape[0]):
+        start = 0
+        for ref in out_refs[2 * step - 2 : 2 * step]:
+            at = slice(start, start + ref.shape[1])
+            pair = keep_ref[step, :, at].astype(F32) + got_ref[step, :, at].astype(F32)
+            ref[...] = pair.astype(BF16)
+            start += ref.shape[1]
 
 
 def last_kernel(others, start, keep_ref, got_ref, *refs):
     out_ref, mark_ref, total_ref, sem = refs[-4:]
     mark_ref[...] = jnp.zeros(mark_ref.shape, F32)
+    cut = refs[0].shape[1]
     for e in range(keep_ref.shape[1]):
-        total = keep_ref[0, e].astype(F32) + got_ref[0, e].astype(F32)
-        for ref in refs[:others]:
-            total = total + ref[e].astype(F32)
-        total_ref[:, e, :] = total
+        for part, at in enumerate((slice(0, cut), slice(cut, keep_ref.shape[2]))):
+            total = keep_ref[0, e, at].astype(F32) + got_ref[0, e, at].astype(F32)
+            for ref in refs[part:others:2]:
+                total = total + ref[e].astype(F32)
+            total_ref[at, e, :] = total
     copy = pltpu.make_async_copy(
         total_ref, out_ref.at[:, :, start : start + total_ref.shape[2]], sem
     )
@@ -246,7 +256,8 @@
 
 
 def chunks_of(features):
-    return [features // 4] * 4
+    unit = features // 16
+    return [5 * unit, 5 * unit, 4 * unit, 2 * unit]
 
 
 sds = jax.ShapeDtypeStruct
@@ -257,21 +268,21 @@
         tokens, features = grad_out.shape
         self.call, self.rows, self.held, self.capacity = call, grad_out, held, capacity
         self.chosen, self.widths, self.place = ids.shape[0], widths, None
-        self.flat, rest, self.first = call(
+        self.flat, self.first = call(
             functools.partial(begin_kernel, LINE * SIDES * held, capacity),
-            [
-                sds(ids.shape, I32),
-                sds((tokens, features - widths[0]), BF16),
-                sds((tokens + INFO, widths[0]), BF16),
-            ],
+            [sds(ids.shape, I32), sds((tokens + INFO, widths[0]), BF16)],
             ids,
             probs,
             grad_out,
-            in_specs=[VMEM, VMEM, HBM],
-            scratch_shapes=[pltpu.SemaphoreType.DMA((2,))],
+            in_specs=[HBM] * 3,
+            scratch_shapes=[
+                pltpu.VMEM(ids.shape, I32),
+                pltpu.VMEM(probs.shape, F32),
+                pltpu.SemaphoreType.DMA((3,)),
+            ],
+            room=60,
         )
         self.first_other = self.send(self.first, 1)
-        self.rest_other = self.send(rest, 1)
 
     def send(self, block, mask):
         return lax.ppermute(block, "expert", [(i, i ^ mask) for i in range(LINE * SIDES)])
@@ -280,16 +291,27 @@
         held, capacity, tokens = self.held, self.capacity, self.rows.shape[0]
         rows = [sds((held, SIDES * capacity, self.widths[c]), BF16)] * LINE
         place = sds((SIDES, LINE * held * capacity, tokens), BF16)
-        flops = 2 * SIDES * LINE * held * capacity * tokens * self.widths[c]
         start = sum(self.widths[:c]) if c else None
         kernel = functools.partial(pick_kernel, held, capacity, self.chosen, start)
         if c == 0:
-            *sent, self.place = self.call(
-                kernel, [*rows, place], self.first, self.first_other, flops=flops
+            rest = sds((tokens, self.rows.shape[1] - self.widths[0]), BF16)
+            *sent, self.place, rest = self.call(
+                kernel,
+                [*rows, place, rest],
+                self.first,
+                self.first_other,
+                self.rows,
+                in_specs=[VMEM, VMEM, HBM],
+                scratch_shapes=[pltpu.SemaphoreType.DMA],
             )
         else:
-            sent = self.call(kernel, rows, self.rows, self.rest_other, self.place, flops=flops)
-        return [sent[0]] + [self.send(sent[d], SIDES * d) for d in range(1, LINE)]
+            sent = self.call(kernel, rows, self.rows, self.rest_other, self.place)
+        got = [sent[0]] + [None] * (LINE - 1)
+        for d in range(LINE - 1, 0, -1):
+            got[d] = self.send(sent[d], SIDES * d)
+        if c == 0:
+            self.rest_other = self.send(rest, 1)
+        return got
 
 
 def exchanged(grad_out, ids, probs, groups, held, capacity, widths):
@@ -341,19 +363,20 @@
         functools.partial(turn_kernel, dp),
         sds((held, 2, across, share, per_expert), BF16),
         saved,
+        *([grad_out, w_down] if direct else []),
     )
     if direct:
         arrived = [relay.chunk(c) for c in range(min(2, count))]
 
     starts = [sum(widths[:c]) for c in range(count)]
-    flops = [2 * slots * units * w for w in widths]
     state = {"raw": None, "grad": None}
     summed = []
 
     def reduced(c):
         parts, width = arrived[c], widths[c]
         piece = sds((across, held, share, width), BF16)
-        keep, give = call(term_kernel, [piece, piece], turned, *parts, flops=flops[c])
+        after = summed[-1][2][:1] if c else ()
+        keep, give = call(term_kernel, [piece, piece], turned, *parts, after=after)
         got = lax.ppermute(give, "dp", [(i, i ^ 1) for i in range(dp)])
         final = c == count - 1
         if final:
@@ -362,13 +385,22 @@
             outs = [sds((held, per_expert, units), F32)]
         extra = ([state["raw"]] if c else []) + ([saved] if final else [])
         kernel = functools.partial(raw_kernel, len(parts), starts[c], final)
-        made = call(kernel, outs, w_down, *parts, *extra, flops=flops[c])
+        made = call(
+            kernel,
+            outs,
+            w_down,
+            *parts,
+            *extra,
+        )
         state["raw"] = made if final else made[0]
-        pairs = call(pair_kernel, [sds((held, share, width), BF16)] * (across - 1), keep, got)
+        cut = 16 * max(1, share // 64)
+        pieces = [sds((held, rows, width), BF16) for rows in (cut, share - cut)]
+        pairs = call(pair_kernel, pieces * (across - 1), keep, got)
         others = []
-        for step in range(1, across):
-            shift = [(2 * r + i, 2 * ((r + step) % across) + i) for r in range(across) for i in range(2)]
-            others.append(lax.ppermute(pairs[step - 1], "dp", shift))
+        for i, pair in enumerate(pairs):
+            step = 1 + i // 2
+            shift = [(2 * r + k, 2 * ((r + step) % across) + k) for r in range(across) for k in range(2)]
+            others.append(lax.ppermute(pair, "dp", shift))
         summed.append((keep, got, others))
 
     def finished(c):

time: 105 us -> 97.8 us (0.931)
  waiting for transfers between devices: 51.4 us -> 36 us
  starting transfers between devices: 32.5 us -> 38.3 us
  Pallas kernels: 13.7 us -> 16 us
    ppermute x4 -> x8, waiting for transfers between devices: 13.4 us -> 6.01 us  [reduced(): others.append(lax.ppermute(pair, 'dp', shift))]
    ppermute x14, waiting for transfers between devices: 34.1 us -> 27.1 us  [send(): lax.ppermute(block, 'expert', [(i, i ^ mask) for i in range(LINE * SIDES)])]
    ppermute x4 -> x8, starting transfers between devices: 4.46 us -> 8.55 us  [reduced(): others.append(lax.ppermute(pair, 'dp', shift))]
    pallas_call x23, Pallas kernels: 13.7 us -> 16 us  [__call__(): pl.pallas_call(body, out_shape=outs, in_specs=in_specs, compiler_params=p...]
    ppermute x1, waiting for transfers between devices: 2.09 us -> 0.57 us  [body(): both = jnp.stack([sums, lax.ppermute(sums, 'expert', swap)])]
    ppermute x14, starting transfers between devices: 21.9 us -> 23.1 us  [send(): lax.ppermute(block, 'expert', [(i, i ^ mask) for i in range(LINE * SIDES)])]
    ppermute x4, waiting for transfers between devices: 0.01 us -> 1.08 us  [reduced(): got = lax.ppermute(give, 'dp', [(i, i ^ 1) for i in range(dp)])]
    unnamed x18 -> x20, local copies, waits for them, and re-layouts: 6.33 us -> 6.31 us
  transfers between devices with their start and end apart: 26 -> 30, of which waited for: 12 -> 12; matrix products, arithmetic and copies ran while one was open for 0% -> 0% of each run, Pallas kernels for 9% -> 10%
where the time goes in v5:
time: 97.8 us; the launch traced here: 97.5 us
  starting transfers between devices  38.3 us (39%)
  waiting for transfers between devices  36 us (37%)
  Pallas kernels  16 us (16%)
  local copies, waits for them, and re-layouts  6.31 us (6%)
    ppermute x14, waiting for transfers between devices, send(): lax.ppermute(block, 'expert', [(i, i ^ mask) for i in range(LINE * SIDES)])  27.1 us
    ppermute x14, starting transfers between devices, send(): lax.ppermute(block, 'expert', [(i, i ^ mask) for i in range(LINE * SIDES)])  23.1 us
    pallas_call x23, Pallas kernels, __call__(): pl.pallas_call(body, out_shape=outs, in_specs=in_specs, compiler_params=p...  16 us
    ppermute x8, starting transfers between devices, reduced(): others.append(lax.ppermute(pair, 'dp', shift))  8.55 us
    unnamed x20, local copies, waits for them, and re-layouts  6.31 us
    ppermute x8, waiting for transfers between devices, reduced(): others.append(lax.ppermute(pair, 'dp', shift))  6.01 us
    ppermute x3, starting transfers between devices, body(): lax.ppermute(both, 'expert', [(i, i ^ SIDES * d) for i in range(groups)])  4.86 us
  transfers between devices with their start and end apart: 30, of which 12 were waited for; matrix products, arithmetic and copies ran while one was open for 0% of the time, Pallas kernels for 10%

profile of v5, /device:TPU:0, one launch (start us, length us, event | category | flops | bytes accessed | tf_op | source)
XLA Modules:
  0.0 97.5 jit_solution(6223452569620567139)
XLA Ops:
  0.6 1.8 %shard_map.76 = (s32[2,128]{1,0:T(2,128)}, bf16[144,640]{1,0:T(8,128)(2,1)}) custom-call(s32[2,128]{1,0:T(2,128)} %bitcast.13, f32[2,128]{1,0:T(2,128)} %bitcast.10, bf16[128,2048]{1,0:T(8,128)(2,1)} %refs_0_.11), custom_call_target="tpu_custom_call" | custom-call | flops 1 | bytes 1 | tf_op jit(solution)/shard_map/pallas_call | solution.py:34
  2.4 3.0 %collective-permute-start = (bf16[144,640]{1,0:T(8,128)(2,1)}, bf16[144,640]{1,0:T(8,128)(2,1)S(1)}, u32[]{:S(2)}, u32[]{:S(2)}) collective-permute-start(bf16[144,640]{1,0:T(8,128)(2,1)} %get-tuple-element.48.refs_0_), channel_id=1, source_target_pairs={{0,1},{1,0},{2,3},{3,2},{4,5},{5,4},{6,7},{7,6},{8,9},{9,8},{10,11... | collective-permute-start | bytes 552968 | tf_op jit(solution)/shard_map/ppermute | solution.py:288
  5.4 2.8 %copy-done = bf16[2,768,2048]{2,1,0:T(8,128)(2,1)S(1)} copy-done((bf16[2,768,2048]{2,1,0:T(8,128)(2,1)S(1)}, bf16[2,768,2048]{2,1,0:T(8,128)(2,1)}, u32[]{:S(2)}) %copy-start) | copy-done | bytes 6291480
  12.5 2.1 %collective-permute-start.5 = (bf16[2,64,640]{2,1,0:T(8,128)(2,1)S(1)}, bf16[2,64,640]{2,1,0:T(8,128)(2,1)S(1)}, u32[]{:S(2)}, u32[]{:S(2)}) collective-permute-start(bf16[2,64,640]{2,1,0:T(8,128)(2,1)S(1)} %get-tuple-element.57), channel_id=1, source_target_pairs={{0,2},{1,3},{2,0},{3,1},{4,6},{5,7},{6,4},{7,5},{8,10},{9,11},{10,... | collective-permute-start | bytes 491528 | tf_op jit(solution)/shard_map/ppermute | solution.py:288
  14.6 2.6 %collective-permute-start.6 = (bf16[2,64,640]{2,1,0:T(8,128)(2,1)S(1)}, bf16[2,64,640]{2,1,0:T(8,128)(2,1)S(1)}, u32[]{:S(2)}, u32[]{:S(2)}) collective-permute-start(bf16[2,64,640]{2,1,0:T(8,128)(2,1)S(1)} %get-tuple-element.58), channel_id=1, source_target_pairs={{0,4},{1,5},{2,6},{3,7},{4,0},{5,1},{6,2},{7,3},{8,12},{9,13},{10,... | collective-permute-start | bytes 491528 | tf_op jit(solution)/shard_map/ppermute | solution.py:288
  17.1 5.2 %collective-permute-done.1.refs_1_ = bf16[128,1408]{1,0:T(8,128)(2,1)S(1)} collective-permute-done((bf16[128,1408]{1,0:T(8,128)(2,1)S(1)}, bf16[128,1408]{1,0:T(8,128)(2,1)S(1)}, u32[]{:S(2)}, u32[]{:S(2)}) %collective-permute-start.1) | collective-permute-done | bytes 360480 | tf_op jit(solution)/shard_map/ppermute | solution.py:288
  22.7 6.7 %collective-permute-done.6.refs_3_ = bf16[2,64,640]{2,1,0:T(8,128)(2,1)S(1)} collective-permute-done((bf16[2,64,640]{2,1,0:T(8,128)(2,1)S(1)}, bf16[2,64,640]{2,1,0:T(8,128)(2,1)S(1)}, u32[]{:S(2)}, u32[]{:S(2)}) %collective-permute-start.6) | collective-permute-done | bytes 163872 | tf_op jit(solution)/shard_map/ppermute | solution.py:288
  30.2 2.4 %collective-permute-start.2 = (bf16[2,64,640]{2,1,0:T(8,128)(2,1)S(1)}, bf16[2,64,640]{2,1,0:T(8,128)(2,1)S(1)}, u32[]{:S(2)}, u32[]{:S(2)}) collective-permute-start(bf16[2,64,640]{2,1,0:T(8,128)(2,1)S(1)} %get-tuple-element.53), channel_id=1, source_target_pairs={{0,2},{1,3},{2,0},{3,1},{4,6},{5,7},{6,4},{7,5},{8,10},{9,11},{10,... | collective-permute-start | bytes 491528 | tf_op jit(solution)/shard_map/ppermute | solution.py:288
  36.1 1.6 %collective-permute-start.9 = (bf16[2,48,640]{2,1,0:T(8,128)(2,1)S(1)}, bf16[2,48,640]{2,1,0:T(8,128)(2,1)S(1)}, u32[]{:S(2)}, u32[]{:S(2)}) collective-permute-start(bf16[2,48,640]{2,1,0:T(8,128)(2,1)S(1)} %get-tuple-element.62.refs_3_), channel_id=1, source_target_pairs={{0,16},{8,24},{16,0},{24,8},{1,17},{9,25},{17,1},{25,9},{2,18},{10... | collective-permute-start | bytes 368648 | tf_op jit(solution)/shard_map/ppermute | solution.py:403
  38.0 2.5 %collective-permute-done.2.refs_2_ = bf16[2,64,640]{2,1,0:T(8,128)(2,1)S(1)} collective-permute-done((bf16[2,64,640]{2,1,0:T(8,128)(2,1)S(1)}, bf16[2,64,640]{2,1,0:T(8,128)(2,1)S(1)}, u32[]{:S(2)}, u32[]{:S(2)}) %collective-permute-start.2) | collective-permute-done | bytes 163872 | tf_op jit(solution)/shard_map/ppermute | solution.py:288
  40.5 7.2 %collective-permute-done.3.refs_3_ = bf16[2,64,640]{2,1,0:T(8,128)(2,1)S(1)} collective-permute-done((bf16[2,64,640]{2,1,0:T(8,128)(2,1)S(1)}, bf16[2,64,640]{2,1,0:T(8,128)(2,1)S(1)}, u32[]{:S(2)}, u32[]{:S(2)}) %collective-permute-start.3) | collective-permute-done | bytes 163872 | tf_op jit(solution)/shard_map/ppermute | solution.py:288
  48.5 1.6 %collective-permute-start.17 = (bf16[2,144,640]{2,1,0:T(8,128)(2,1)S(1)}, bf16[2,144,640]{2,1,0:T(8,128)(2,1)S(1)}, u32[]{:S(2)}, u32[]{:S(2)}) collective-permute-start(bf16[2,144,640]{2,1,0:T(8,128)(2,1)S(1)} %get-tuple-element.74), channel_id=1, source_target_pairs={{0,16},{8,24},{16,0},{24,8},{1,17},{9,25},{17,1},{25,9},{2,18},{10... | collective-permute-start | bytes 1105928 | tf_op jit(solution)/shard_map/ppermute | solution.py:403
  50.1 3.3 %collective-permute-start.14 = (bf16[2,64,512]{2,1,0:T(8,128)(2,1)S(1)}, bf16[2,64,512]{2,1,0:T(8,128)(2,1)S(1)}, u32[]{:S(2)}, u32[]{:S(2)}) collective-permute-start(bf16[2,64,512]{2,1,0:T(8,128)(2,1)S(1)} %get-tuple-element.71), channel_id=1, source_target_pairs={{0,2},{1,3},{2,0},{3,1},{4,6},{5,7},{6,4},{7,5},{8,10},{9,11},{10,... | collective-permute-start | bytes 393224 | tf_op jit(solution)/shard_map/ppermute | solution.py:288
  54.4 1.5 %collective-permute-start.16 = (bf16[2,64,512]{2,1,0:T(8,128)(2,1)S(1)}, bf16[2,64,512]{2,1,0:T(8,128)(2,1)S(1)}, u32[]{:S(2)}, u32[]{:S(2)}) collective-permute-start(bf16[2,64,512]{2,1,0:T(8,128)(2,1)S(1)} %get-tuple-element.73), channel_id=1, source_target_pairs={{0,6},{1,7},{2,4},{3,5},{4,2},{5,3},{6,0},{7,1},{8,14},{9,15},{10,... | collective-permute-start | bytes 393224 | tf_op jit(solution)/shard_map/ppermute | solution.py:288
  57.6 2.2 %collective-permute-done.17.refs_3_ = bf16[2,144,640]{2,1,0:T(8,128)(2,1)S(1)} collective-permute-done((bf16[2,144,640]{2,1,0:T(8,128)(2,1)S(1)}, bf16[2,144,640]{2,1,0:T(8,128)(2,1)S(1)}, u32[]{:S(2)}, u32[]{:S(2)}) %collective-permute-start.17) | collective-permute-done | bytes 368672 | tf_op jit(solution)/shard_map/ppermute | solution.py:403
  61.2 5.1 %collective-permute-done.15.refs_3_ = bf16[2,64,512]{2,1,0:T(8,128)(2,1)S(1)} collective-permute-done((bf16[2,64,512]{2,1,0:T(8,128)(2,1)S(1)}, bf16[2,64,512]{2,1,0:T(8,128)(2,1)S(1)}, u32[]{:S(2)}, u32[]{:S(2)}) %collective-permute-start.15) | collective-permute-done | bytes 131104 | tf_op jit(solution)/shard_map/ppermute | solution.py:288
  69.9 2.3 %collective-permute-start.11 = (bf16[2,64,256]{2,1,0:T(8,128)(2,1)S(1)}, bf16[2,64,256]{2,1,0:T(8,128)(2,1)S(1)}, u32[]{:S(2)}, u32[]{:S(2)}) collective-permute-start(bf16[2,64,256]{2,1,0:T(8,128)(2,1)S(1)} %get-tuple-element.68), channel_id=1, source_target_pairs={{0,2},{1,3},{2,0},{3,1},{4,6},{5,7},{6,4},{7,5},{8,10},{9,11},{10,... | collective-permute-start | bytes 196616 | tf_op jit(solution)/shard_map/ppermute | solution.py:288
  73.2 1.5 %collective-permute-start.13 = (bf16[2,64,256]{2,1,0:T(8,128)(2,1)S(1)}, bf16[2,64,256]{2,1,0:T(8,128)(2,1)S(1)}, u32[]{:S(2)}, u32[]{:S(2)}) collective-permute-start(bf16[2,64,256]{2,1,0:T(8,128)(2,1)S(1)} %get-tuple-element.70), channel_id=1, source_target_pairs={{0,6},{1,7},{2,4},{3,5},{4,2},{5,3},{6,0},{7,1},{8,14},{9,15},{10,... | collective-permute-start | bytes 196616 | tf_op jit(solution)/shard_map/ppermute | solution.py:288
  74.6 3.8 %collective-permute-done.19.refs_3_ = bf16[2,144,640]{2,1,0:T(8,128)(2,1)S(1)} collective-permute-done((bf16[2,144,640]{2,1,0:T(8,128)(2,1)S(1)}, bf16[2,144,640]{2,1,0:T(8,128)(2,1)S(1)}, u32[]{:S(2)}, u32[]{:S(2)}) %collective-permute-start.19) | collective-permute-done | bytes 368672 | tf_op jit(solution)/shard_map/ppermute | solution.py:403
  80.7 1.6 %collective-permute-start.26 = (bf16[2,144,512]{2,1,0:T(8,128)(2,1)S(1)}, bf16[2,144,512]{2,1,0:T(8,128)(2,1)S(1)}, u32[]{:S(2)}, u32[]{:S(2)}) collective-permute-start(bf16[2,144,512]{2,1,0:T(8,128)(2,1)S(1)} %get-tuple-element.85), channel_id=1, source_target_pairs={{0,16},{8,24},{16,0},{24,8},{1,17},{9,25},{17,1},{25,9},{2,18},{10... | collective-permute-start | bytes 884744 | tf_op jit(solution)/shard_map/ppermute | solution.py:403
  84.3 1.5 %collective-permute-start.22 = (f32[2,256]{1,0:T(2,128)S(1)}, f32[2,256]{1,0:T(2,128)S(1)}, u32[]{:S(2)}, u32[]{:S(2)}) collective-permute-start(f32[2,256]{1,0:T(2,128)S(1)} %get-tuple-element.84.refs_2_), channel_id=1, source_target_pairs={{0,1},{1,0},{2,3},{3,2},{4,5},{5,4},{6,7},{7,6},{8,9},{9,8},{10,11... | collective-permute-start | bytes 6152 | tf_op jit(solution)/shard_map/ppermute | solution.py:436
  85.8 1.5 %collective-permute-start.28 = (bf16[2,48,256]{2,1,0:T(8,128)(2,1)S(1)}, bf16[2,48,256]{2,1,0:T(8,128)(2,1)S(1)}, u32[]{:S(2)}, u32[]{:S(2)}) collective-permute-start(bf16[2,48,256]{2,1,0:T(8,128)(2,1)S(1)} %get-tuple-element.88.refs_5_), channel_id=1, source_target_pairs={{0,16},{8,24},{16,0},{24,8},{1,17},{9,25},{17,1},{25,9},{2,18},{10... | collective-permute-start | bytes 147464 | tf_op jit(solution)/shard_map/ppermute | solution.py:403
  87.8 2.2 %collective-permute-start.25 = (f32[2,2,256]{2,1,0:T(2,128)S(1)}, f32[2,2,256]{2,1,0:T(2,128)S(1)}, u32[]{:S(2)}, u32[]{:S(2)}) collective-permute-start(f32[2,2,256]{2,1,0:T(2,128)S(1)} %pad_maximum_fusion.refs_2_), channel_id=1, source_target_pairs={{0,6},{1,7},{2,4},{3,5},{4,2},{5,3},{6,0},{7,1},{8,14},{9,15},{10,... | collective-permute-start | bytes 12296 | tf_op jit(solution)/shard_map/ppermute | solution.py:438
  96.0 1.5 %shard_map.98 = (f32[192,2,2048]{2,1,0:T(2,128)}, f32[8,128]{1,0:T(8,128)}) custom-call(bf16[2,2,192,256]{3,2,1,0:T(8,128)(2,1)S(1)} %get-tuple-element.82.refs_7_.refs_0_, bf16[2,2,192,256]{3,2,1,0:T(8,128)(2,1)S(1)} %collective-permute-done.27.refs_1_, bf16[2,48,256]{2,1,0:T(8,128)(2,1)S(1)} %collective-permute-done.28.refs_2_, ...), custom_call_target="tpu_custom_call", output_to_operand_aliasing={{0}: (4, {})} | custom-call | flops 1 | bytes 1 | tf_op jit(solution)/shard_map/pallas_call | solution.py:34
  (80 shorter events, 29.3 us)
Async XLA Ops:
  2.4 8.9 %collective-permute-start = (bf16[144,640]{1,0:T(8,128)(2,1)}, bf16[144,640]{1,0:T(8,128)(2,1)S(1)}, u32[]{:S(2)}, u32[]{:S(2)}) collective-permute-start(bf16[144,640]{1,0:T(8,128)(2,1)} %get-tuple-element.48.refs_0_), channel_id=1, source_target_pairs={{0,1},{1,0},{2,3},{3,2},{4,5},{5,4},{6,7},{7,6},{8,9},{9,8},{10,11... | collective-permute-start | bytes 552968 | tf_op jit(solution)/shard_map/ppermute | solution.py:288
  12.4 9.9 %collective-permute-start.1 = (bf16[128,1408]{1,0:T(8,128)(2,1)S(1)}, bf16[128,1408]{1,0:T(8,128)(2,1)S(1)}, u32[]{:S(2)}, u32[]{:S(2)}) collective-permute-start(bf16[128,1408]{1,0:T(8,128)(2,1)S(1)} %get-tuple-element.50), channel_id=1, source_target_pairs={{0,1},{1,0},{2,3},{3,2},{4,5},{5,4},{6,7},{7,6},{8,9},{9,8},{10,11... | collective-permute-start | bytes 1081352 | tf_op jit(solution)/shard_map/ppermute | solution.py:288
  12.5 10.2 %collective-permute-start.5 = (bf16[2,64,640]{2,1,0:T(8,128)(2,1)S(1)}, bf16[2,64,640]{2,1,0:T(8,128)(2,1)S(1)}, u32[]{:S(2)}, u32[]{:S(2)}) collective-permute-start(bf16[2,64,640]{2,1,0:T(8,128)(2,1)S(1)} %get-tuple-element.57), channel_id=1, source_target_pairs={{0,2},{1,3},{2,0},{3,1},{4,6},{5,7},{6,4},{7,5},{8,10},{9,11},{10,... | collective-permute-start | bytes 491528 | tf_op jit(solution)/shard_map/ppermute | solution.py:288
  14.6 14.8 %collective-permute-start.6 = (bf16[2,64,640]{2,1,0:T(8,128)(2,1)S(1)}, bf16[2,64,640]{2,1,0:T(8,128)(2,1)S(1)}, u32[]{:S(2)}, u32[]{:S(2)}) collective-permute-start(bf16[2,64,640]{2,1,0:T(8,128)(2,1)S(1)} %get-tuple-element.58), channel_id=1, source_target_pairs={{0,4},{1,5},{2,6},{3,7},{4,0},{5,1},{6,2},{7,3},{8,12},{9,13},{10,... | collective-permute-start | bytes 491528 | tf_op jit(solution)/shard_map/ppermute | solution.py:288
  17.1 12.2 %collective-permute-start.7 = (bf16[2,64,640]{2,1,0:T(8,128)(2,1)S(1)}, bf16[2,64,640]{2,1,0:T(8,128)(2,1)S(1)}, u32[]{:S(2)}, u32[]{:S(2)}) collective-permute-start(bf16[2,64,640]{2,1,0:T(8,128)(2,1)S(1)} %get-tuple-element.59), channel_id=1, source_target_pairs={{0,6},{1,7},{2,4},{3,5},{4,2},{5,3},{6,0},{7,1},{8,14},{9,15},{10,... | collective-permute-start | bytes 491528 | tf_op jit(solution)/shard_map/ppermute | solution.py:288
  30.2 10.2 %collective-permute-start.2 = (bf16[2,64,640]{2,1,0:T(8,128)(2,1)S(1)}, bf16[2,64,640]{2,1,0:T(8,128)(2,1)S(1)}, u32[]{:S(2)}, u32[]{:S(2)}) collective-permute-start(bf16[2,64,640]{2,1,0:T(8,128)(2,1)S(1)} %get-tuple-element.53), channel_id=1, source_target_pairs={{0,2},{1,3},{2,0},{3,1},{4,6},{5,7},{6,4},{7,5},{8,10},{9,11},{10,... | collective-permute-start | bytes 491528 | tf_op jit(solution)/shard_map/ppermute | solution.py:288
  32.6 15.0 %collective-permute-start.3 = (bf16[2,64,640]{2,1,0:T(8,128)(2,1)S(1)}, bf16[2,64,640]{2,1,0:T(8,128)(2,1)S(1)}, u32[]{:S(2)}, u32[]{:S(2)}) collective-permute-start(bf16[2,64,640]{2,1,0:T(8,128)(2,1)S(1)} %get-tuple-element.54), channel_id=1, source_target_pairs={{0,4},{1,5},{2,6},{3,7},{4,0},{5,1},{6,2},{7,3},{8,12},{9,13},{10,... | collective-permute-start | bytes 491528 | tf_op jit(solution)/shard_map/ppermute | solution.py:288
  33.7 13.9 %collective-permute-start.4 = (bf16[2,64,640]{2,1,0:T(8,128)(2,1)S(1)}, bf16[2,64,640]{2,1,0:T(8,128)(2,1)S(1)}, u32[]{:S(2)}, u32[]{:S(2)}) collective-permute-start(bf16[2,64,640]{2,1,0:T(8,128)(2,1)S(1)} %get-tuple-element.55), channel_id=1, source_target_pairs={{0,6},{1,7},{2,4},{3,5},{4,2},{5,3},{6,0},{7,1},{8,14},{9,15},{10,... | collective-permute-start | bytes 491528 | tf_op jit(solution)/shard_map/ppermute | solution.py:288
  36.1 11.6 %collective-permute-start.9 = (bf16[2,48,640]{2,1,0:T(8,128)(2,1)S(1)}, bf16[2,48,640]{2,1,0:T(8,128)(2,1)S(1)}, u32[]{:S(2)}, u32[]{:S(2)}) collective-permute-start(bf16[2,48,640]{2,1,0:T(8,128)(2,1)S(1)} %get-tuple-element.62.refs_3_), channel_id=1, source_target_pairs={{0,16},{8,24},{16,0},{24,8},{1,17},{9,25},{17,1},{25,9},{2,18},{10... | collective-permute-start | bytes 368648 | tf_op jit(solution)/shard_map/ppermute | solution.py:403
  48.4 8.3 %collective-permute-start.10 = (bf16[2,2,192,640]{3,2,1,0:T(8,128)(2,1)S(1)}, bf16[2,2,192,640]{3,2,1,0:T(8,128)(2,1)S(1)}, u32[]{:S(2)}, u32[]{:S(2)}) collective-permute-start(bf16[2,2,192,640]{3,2,1,0:T(8,128)(2,1)S(1)} %get-tuple-element.65), channel_id=1, source_target_pairs={{0,8},{8,0},{16,24},{24,16},{1,9},{9,1},{17,25},{25,17},{2,10},{10... | collective-permute-start | bytes 2949128 | tf_op jit(solution)/shard_map/ppermute | solution.py:380
  48.5 11.3 %collective-permute-start.17 = (bf16[2,144,640]{2,1,0:T(8,128)(2,1)S(1)}, bf16[2,144,640]{2,1,0:T(8,128)(2,1)S(1)}, u32[]{:S(2)}, u32[]{:S(2)}) collective-permute-start(bf16[2,144,640]{2,1,0:T(8,128)(2,1)S(1)} %get-tuple-element.74), channel_id=1, source_target_pairs={{0,16},{8,24},{16,0},{24,8},{1,17},{9,25},{17,1},{25,9},{2,18},{10... | collective-permute-start | bytes 1105928 | tf_op jit(solution)/shard_map/ppermute | solution.py:403
  50.1 11.1 %collective-permute-start.14 = (bf16[2,64,512]{2,1,0:T(8,128)(2,1)S(1)}, bf16[2,64,512]{2,1,0:T(8,128)(2,1)S(1)}, u32[]{:S(2)}, u32[]{:S(2)}) collective-permute-start(bf16[2,64,512]{2,1,0:T(8,128)(2,1)S(1)} %get-tuple-element.71), channel_id=1, source_target_pairs={{0,2},{1,3},{2,0},{3,1},{4,6},{5,7},{6,4},{7,5},{8,10},{9,11},{10,... | collective-permute-start | bytes 393224 | tf_op jit(solution)/shard_map/ppermute | solution.py:288
  53.4 12.9 %collective-permute-start.15 = (bf16[2,64,512]{2,1,0:T(8,128)(2,1)S(1)}, bf16[2,64,512]{2,1,0:T(8,128)(2,1)S(1)}, u32[]{:S(2)}, u32[]{:S(2)}) collective-permute-start(bf16[2,64,512]{2,1,0:T(8,128)(2,1)S(1)} %get-tuple-element.72), channel_id=1, source_target_pairs={{0,4},{1,5},{2,6},{3,7},{4,0},{5,1},{6,2},{7,3},{8,12},{9,13},{10,... | collective-permute-start | bytes 393224 | tf_op jit(solution)/shard_map/ppermute | solution.py:288
  54.4 11.9 %collective-permute-start.16 = (bf16[2,64,512]{2,1,0:T(8,128)(2,1)S(1)}, bf16[2,64,512]{2,1,0:T(8,128)(2,1)S(1)}, u32[]{:S(2)}, u32[]{:S(2)}) collective-permute-start(bf16[2,64,512]{2,1,0:T(8,128)(2,1)S(1)} %get-tuple-element.73), channel_id=1, source_target_pairs={{0,6},{1,7},{2,4},{3,5},{4,2},{5,3},{6,0},{7,1},{8,14},{9,15},{10,... | collective-permute-start | bytes 393224 | tf_op jit(solution)/shard_map/ppermute | solution.py:288
  56.8 9.5 %collective-permute-start.18 = (bf16[2,48,640]{2,1,0:T(8,128)(2,1)S(1)}, bf16[2,48,640]{2,1,0:T(8,128)(2,1)S(1)}, u32[]{:S(2)}, u32[]{:S(2)}) collective-permute-start(bf16[2,48,640]{2,1,0:T(8,128)(2,1)S(1)} %get-tuple-element.66.refs_3_), channel_id=1, source_target_pairs={{0,16},{8,24},{16,0},{24,8},{1,17},{9,25},{17,1},{25,9},{2,18},{10... | collective-permute-start | bytes 368648 | tf_op jit(solution)/shard_map/ppermute | solution.py:403
  67.0 11.5 %collective-permute-start.19 = (bf16[2,144,640]{2,1,0:T(8,128)(2,1)S(1)}, bf16[2,144,640]{2,1,0:T(8,128)(2,1)S(1)}, u32[]{:S(2)}, u32[]{:S(2)}) collective-permute-start(bf16[2,144,640]{2,1,0:T(8,128)(2,1)S(1)} %get-tuple-element.77), channel_id=1, source_target_pairs={{0,16},{8,24},{16,0},{24,8},{1,17},{9,25},{17,1},{25,9},{2,18},{10... | collective-permute-start | bytes 1105928 | tf_op jit(solution)/shard_map/ppermute | solution.py:403
  69.3 10.9 %collective-permute-start.21 = (bf16[2,48,512]{2,1,0:T(8,128)(2,1)S(1)}, bf16[2,48,512]{2,1,0:T(8,128)(2,1)S(1)}, u32[]{:S(2)}, u32[]{:S(2)}) collective-permute-start(bf16[2,48,512]{2,1,0:T(8,128)(2,1)S(1)} %get-tuple-element.80.refs_5_), channel_id=1, source_target_pairs={{0,16},{8,24},{16,0},{24,8},{1,17},{9,25},{17,1},{25,9},{2,18},{10... | collective-permute-start | bytes 294920 | tf_op jit(solution)/shard_map/ppermute | solution.py:403
  69.9 9.9 %collective-permute-start.11 = (bf16[2,64,256]{2,1,0:T(8,128)(2,1)S(1)}, bf16[2,64,256]{2,1,0:T(8,128)(2,1)S(1)}, u32[]{:S(2)}, u32[]{:S(2)}) collective-permute-start(bf16[2,64,256]{2,1,0:T(8,128)(2,1)S(1)} %get-tuple-element.68), channel_id=1, source_target_pairs={{0,2},{1,3},{2,0},{3,1},{4,6},{5,7},{6,4},{7,5},{8,10},{9,11},{10,... | collective-permute-start | bytes 196616 | tf_op jit(solution)/shard_map/ppermute | solution.py:288
  72.2 8.0 %collective-permute-start.12 = (bf16[2,64,256]{2,1,0:T(8,128)(2,1)S(1)}, bf16[2,64,256]{2,1,0:T(8,128)(2,1)S(1)}, u32[]{:S(2)}, u32[]{:S(2)}) collective-permute-start(bf16[2,64,256]{2,1,0:T(8,128)(2,1)S(1)} %get-tuple-element.69), channel_id=1, source_target_pairs={{0,4},{1,5},{2,6},{3,7},{4,0},{5,1},{6,2},{7,3},{8,12},{9,13},{10,... | collective-permute-start | bytes 196616 | tf_op jit(solution)/shard_map/ppermute | solution.py:288
  73.2 7.0 %collective-permute-start.13 = (bf16[2,64,256]{2,1,0:T(8,128)(2,1)S(1)}, bf16[2,64,256]{2,1,0:T(8,128)(2,1)S(1)}, u32[]{:S(2)}, u32[]{:S(2)}) collective-permute-start(bf16[2,64,256]{2,1,0:T(8,128)(2,1)S(1)} %get-tuple-element.70), channel_id=1, source_target_pairs={{0,6},{1,7},{2,4},{3,5},{4,2},{5,3},{6,0},{7,1},{8,14},{9,15},{10,... | collective-permute-start | bytes 196616 | tf_op jit(solution)/shard_map/ppermute | solution.py:288
  80.7 10.8 %collective-permute-start.26 = (bf16[2,144,512]{2,1,0:T(8,128)(2,1)S(1)}, bf16[2,144,512]{2,1,0:T(8,128)(2,1)S(1)}, u32[]{:S(2)}, u32[]{:S(2)}) collective-permute-start(bf16[2,144,512]{2,1,0:T(8,128)(2,1)S(1)} %get-tuple-element.85), channel_id=1, source_target_pairs={{0,16},{8,24},{16,0},{24,8},{1,17},{9,25},{17,1},{25,9},{2,18},{10... | collective-permute-start | bytes 884744 | tf_op jit(solution)/shard_map/ppermute | solution.py:403
  83.7 12.4 %collective-permute-start.29 = (bf16[2,144,256]{2,1,0:T(8,128)(2,1)S(1)}, bf16[2,144,256]{2,1,0:T(8,128)(2,1)S(1)}, u32[]{:S(2)}, u32[]{:S(2)}) collective-permute-start(bf16[2,144,256]{2,1,0:T(8,128)(2,1)S(1)} %get-tuple-element.90), channel_id=1, source_target_pairs={{0,16},{8,24},{16,0},{24,8},{1,17},{9,25},{17,1},{25,9},{2,18},{10... | collective-permute-start | bytes 442376 | tf_op jit(solution)/shard_map/ppermute | solution.py:403
  85.8 10.3 %collective-permute-start.28 = (bf16[2,48,256]{2,1,0:T(8,128)(2,1)S(1)}, bf16[2,48,256]{2,1,0:T(8,128)(2,1)S(1)}, u32[]{:S(2)}, u32[]{:S(2)}) collective-permute-start(bf16[2,48,256]{2,1,0:T(8,128)(2,1)S(1)} %get-tuple-element.88.refs_5_), channel_id=1, source_target_pairs={{0,16},{8,24},{16,0},{24,8},{1,17},{9,25},{17,1},{25,9},{2,18},{10... | collective-permute-start | bytes 147464 | tf_op jit(solution)/shard_map/ppermute | solution.py:403
  87.8 6.0 %collective-permute-start.25 = (f32[2,2,256]{2,1,0:T(2,128)S(1)}, f32[2,2,256]{2,1,0:T(2,128)S(1)}, u32[]{:S(2)}, u32[]{:S(2)}) collective-permute-start(f32[2,2,256]{2,1,0:T(2,128)S(1)} %pad_maximum_fusion.refs_2_), channel_id=1, source_target_pairs={{0,6},{1,7},{2,4},{3,5},{4,2},{5,3},{6,0},{7,1},{8,14},{9,15},{10,... | collective-permute-start | bytes 12296 | tf_op jit(solution)/shard_map/ppermute | solution.py:438
  (16 other events, 82.0 us)

commit v6 on v5

--- a/solution.py
+++ b/solution.py
@@ -13,6 +13,9 @@
 HBM = pl.BlockSpec(memory_space=pltpu.HBM)
 
 LINE, SIDES = 4, 2
+FAR, NEAR, PASSED = (3, 2, 1, 0), (1, 0, 3, 2), (2, 0, 3, 1)
+FROM = (0, 1, 3, 2)
+MASKS = tuple(SIDES * d + s for s in range(SIDES) for d in FROM)
 INFO = 16
 
 
@@ -86,43 +89,70 @@
         out_ref[tokens:, tokens:] = jnp.zeros((INFO, width - tokens), BF16)
 
 
-def pick_kernel(held, capacity, chosen, start, own_ref, other_ref, *refs):
-    tokens = own_ref.shape[0] - (INFO if start is None else 0)
+def places(held, capacity, chosen, ref, place_ref):
+    tokens = place_ref.shape[1]
     rows = held * capacity
-    if start is None:
-        rows_ref, *out_refs, place_ref, rest_ref, sem = refs
-        copy = pltpu.make_async_copy(rows_ref.at[:, own_ref.shape[1] :], rest_ref, sem)
+    me = lax.axis_index("expert")
+    local = lax.broadcasted_iota(I32, (rows, tokens), 0)
+    info = ref[tokens:, :tokens].astype(F32)
+    flat = (info[:chosen] * capacity + info[chosen : 2 * chosen]).astype(I32)
+    word = info[2 * chosen : 3 * chosen]
+    for side in range(SIDES):
+        slot = local + (me ^ side) * rows
+        hits = [jnp.where(flat[k : k + 1] == slot, word[k : k + 1], 0.0) for k in range(chosen)]
+        place_ref[side * rows : (side + 1) * rows, :] = functools.reduce(jnp.add, hits).astype(BF16)
+
+
+def pick(held, capacity, block_refs, place_ref, out_refs):
+    tokens = place_ref.shape[2]
+    for j, ref in enumerate(block_refs):
+        scaled = jnp.dot(place_ref[j], ref[:tokens, :], preferred_element_type=F32).astype(BF16)
+        for side, out_ref in enumerate(out_refs):
+            for e in range(held):
+                at = (side * held + e) * capacity
+                out_ref[e, j * capacity : (j + 1) * capacity, :] = scaled[at : at + capacity]
+
+
+def hand_kernel(held, capacity, chosen, first, start, own_ref, near_ref, far_ref, *refs):
+    blocks = (own_ref, near_ref, far_ref)
+    if start:
+        rows_ref, refs = refs[0], refs[1:]
+        *refs, sem = refs
+        next_ref, refs = refs[-1], refs[:-1]
+        copy = pltpu.make_async_copy(
+            rows_ref.at[:, start : start + next_ref.shape[1]], next_ref, sem
+        )
         copy.start()
-        me = lax.axis_index("expert")
-        local = lax.broadcasted_iota(I32, (rows, tokens), 0)
-        for side, ref in enumerate((own_ref, other_ref)):
-            info = ref[tokens:, :tokens].astype(F32)
-            flat = (info[:chosen] * capacity + info[chosen : 2 * chosen]).astype(I32)
-            word = info[2 * chosen : 3 * chosen]
-            for d in range(LINE):
-                slot = local + (me ^ (SIDES * d)) * rows
-                hits = [
-                    jnp.where(flat[k : k + 1] == slot, word[k : k + 1], 0.0) for k in range(chosen)
-                ]
-                place_ref[side, d * rows : (d + 1) * rows, :] = functools.reduce(
-                    jnp.add, hits
-                ).astype(BF16)
-        blocks = own_ref[:tokens, :], other_ref[:tokens, :]
+    if first:
+        mine_ref, other_ref, pass_ref, place_ref = refs
     else:
-        place_ref, out_refs = refs[0], refs[1:]
-        width, first = out_refs[0].shape[2], own_ref.shape[1] - other_ref.shape[1]
-        blocks = (
-            own_ref[:, start : start + width],
-            other_ref[:, start - first : start - first + width],
-        )
-    for side, block in enumerate(blocks):
-        scaled = jnp.dot(place_ref[side], block, preferred_element_type=F32).astype(BF16)
-        for d, out_ref in enumerate(out_refs):
-            for e in range(held):
-                at = d * rows + e * capacity
-                out_ref[e, side * capacity : (side + 1) * capacity, :] = scaled[at : at + capacity]
-    if start is None:
+        place_ref, mine_ref, other_ref, pass_ref = refs
+    place = lax.axis_index("expert") // SIDES
+    inner = jnp.logical_and(place > 0, place < LINE - 1)
+
+    @pl.when(inner)
+    def _():
+        pass_ref[...] = far_ref[...]
+
+    @pl.when(jnp.logical_not(inner))
+    def _():
+        pass_ref[...] = own_ref[...]
+
+    if first:
+        for j, ref in enumerate(blocks):
+            places(held, capacity, chosen, ref, place_ref.at[j])
+    pick(held, capacity, blocks, place_ref, (mine_ref, other_ref))
+    if start:
         copy.wait()
+
+
+def passed_kernel(held, capacity, chosen, first, block_ref, *refs):
+    if first:
+        mine_ref, other_ref, place_ref = refs
+        places(held, capacity, chosen, block_ref, place_ref.at[0])
+    else:
+        place_ref, mine_ref, other_ref = refs
+    pick(held, capacity, (block_ref,), place_ref, (mine_ref, other_ref))
 
 
 def turn_kernel(dp, hidden_ref, *refs):
@@ -130,10 +160,11 @@
     parts, held, _, units = hidden_ref.shape
     share, across = units // dp, dp // 2
     me = lax.axis_index("expert") if parts > 1 else 0
+    masks = MASKS if parts > 1 else (0,)
     mine = lax.axis_index("dp")
     core, row = mine % 2, mine // 2
     for e in range(held):
-        stacked = jnp.concatenate([hidden_ref[me ^ mask, e] for mask in range(parts)], axis=0)
+        stacked = jnp.concatenate([hidden_ref[me ^ mask, e] for mask in masks], axis=0)
         turned = stacked.T
         for piece in range(dp):
             other = (piece % 2) ^ core
@@ -141,15 +172,17 @@
             out_ref[e, other, step] = turned[piece * share : (piece + 1) * share]
 
 
-def stacked_rows(refs, e):
-    return refs[0][e] if len(refs) == 1 else jnp.concatenate([ref[e] for ref in refs], axis=0)
-
-
-def term_kernel(turned_ref, *refs):
+def stacked_rows(refs, e, at):
+    rows = [ref[e, :, at] for ref in refs]
+    return rows[0] if len(rows) == 1 else jnp.concatenate(rows, axis=0)
+
+
+def term_kernel(start, turned_ref, *refs):
     part_refs, keep_ref, give_ref = refs[:-2], refs[-2], refs[-1]
     held, _, across, share, slots = turned_ref.shape
+    at = slice(start, start + keep_ref.shape[3])
     for e in range(held):
-        scaled = stacked_rows(part_refs, e)
+        scaled = stacked_rows(part_refs, e, at)
         for other, ref in ((1, give_ref), (0, keep_ref)):
             left = turned_ref[e, other].reshape(across * share, slots)
             term = jnp.dot(left, scaled, preferred_element_type=F32).astype(BF16)
@@ -158,25 +191,18 @@
 
 
 def pair_kernel(keep_ref, got_ref, *out_refs):
-    for step in range(1, keep_ref.shape[0]):
-        start = 0
-        for ref in out_refs[2 * step - 2 : 2 * step]:
-            at = slice(start, start + ref.shape[1])
-            pair = keep_ref[step, :, at].astype(F32) + got_ref[step, :, at].astype(F32)
-            ref[...] = pair.astype(BF16)
-            start += ref.shape[1]
+    for step, ref in enumerate(out_refs, 1):
+        ref[...] = (keep_ref[step].astype(F32) + got_ref[step].astype(F32)).astype(BF16)
 
 
 def last_kernel(others, start, keep_ref, got_ref, *refs):
     out_ref, mark_ref, total_ref, sem = refs[-4:]
     mark_ref[...] = jnp.zeros(mark_ref.shape, F32)
-    cut = refs[0].shape[1]
     for e in range(keep_ref.shape[1]):
-        for part, at in enumerate((slice(0, cut), slice(cut, keep_ref.shape[2]))):
-            total = keep_ref[0, e, at].astype(F32) + got_ref[0, e, at].astype(F32)
-            for ref in refs[part:others:2]:
-                total = total + ref[e].astype(F32)
-            total_ref[at, e, :] = total
+        total = keep_ref[0, e].astype(F32) + got_ref[0, e].astype(F32)
+        for ref in refs[:others]:
+            total = total + ref[e].astype(F32)
+        total_ref[:, e, :] = total
     copy = pltpu.make_async_copy(
         total_ref, out_ref.at[:, :, start : start + total_ref.shape[2]], sem
     )
@@ -184,14 +210,13 @@
     copy.wait()
 
 
-def raw_kernel(parts, start, final, weight_ref, *refs):
+def raw_kernel(parts, start, width, at, final, weight_ref, *refs):
     part_refs, refs = refs[:parts], refs[parts:]
     if start:
         acc_ref, refs = refs[0], refs[1:]
-    width = part_refs[0].shape[2]
     for e in range(weight_ref.shape[0]):
         raw = lax.dot_general(
-            stacked_rows(part_refs, e),
+            stacked_rows(part_refs, e, slice(at, at + width)),
             weight_ref[e, :, start : start + width],
             (((1,), (1,)), ((), ())),
             preferred_element_type=F32,
@@ -205,8 +230,8 @@
         sources, _, own, units = hidden_ref.shape
         me = lax.axis_index("expert") if sources > 1 else 0
         folds = []
-        for mask in range(sources):
-            block = raw[mask * own : (mask + 1) * own]
+        for part, mask in enumerate(MASKS if sources > 1 else (0,)):
+            block = raw[part * own : (part + 1) * own]
             grad_ref[me ^ mask, e] = block.astype(BF16)
             product = block * hidden_ref[me ^ mask, e].astype(F32)
             folds.append(
@@ -222,7 +247,7 @@
     if direct:
         values = []
         for mask in range(LINE * SIDES):
-            at = mask * capacity
+            at = MASKS.index(mask) * capacity
             ref = refs[mask // SIDES]
             values += [ref[mask % SIDES, e : e + 1, at : at + capacity] for e in range(ref.shape[1])]
         lanes = 128 // capacity
@@ -257,7 +282,7 @@
 
 def chunks_of(features):
     unit = features // 16
-    return [5 * unit, 5 * unit, 4 * unit, 2 * unit]
+    return [[6 * unit], [2 * unit, 4 * unit, 4 * unit]]
 
 
 sds = jax.ShapeDtypeStruct
@@ -265,10 +290,11 @@
 
 class Relay:
     def __init__(self, call, grad_out, ids, probs, held, capacity, widths):
-        tokens, features = grad_out.shape
+        tokens = grad_out.shape[0]
         self.call, self.rows, self.held, self.capacity = call, grad_out, held, capacity
-        self.chosen, self.widths, self.place = ids.shape[0], widths, None
-        self.flat, self.first = call(
+        self.chosen, self.widths = ids.shape[0], widths
+        self.place, self.passed_place, self.blocks = None, None, None
+        self.flat, first = call(
             functools.partial(begin_kernel, LINE * SIDES * held, capacity),
             [sds(ids.shape, I32), sds((tokens + INFO, widths[0]), BF16)],
             ids,
@@ -281,37 +307,62 @@
                 pltpu.SemaphoreType.DMA((3,)),
             ],
             room=60,
+            keep=False,
         )
-        self.first_other = self.send(self.first, 1)
-
-    def send(self, block, mask):
-        return lax.ppermute(block, "expert", [(i, i ^ mask) for i in range(LINE * SIDES)])
-
-    def chunk(self, c):
+        self.leave(first)
+
+    def leave(self, own):
+        self.blocks = [own, self.along(own, NEAR), self.along(own, FAR)]
+
+    def along(self, block, targets):
+        pairs = [(p * SIDES + s, targets[p] * SIDES + s) for p in range(LINE) for s in range(SIDES)]
+        return lax.ppermute(block, "expert", pairs)
+
+    def swap(self, block):
+        return lax.ppermute(block, "expert", [(i, i ^ 1) for i in range(LINE * SIDES)])
+
+    def selected(self, blocks, width):
+        return [sds((self.held, blocks * self.capacity, width), BF16)] * SIDES
+
+    def hand(self, c):
         held, capacity, tokens = self.held, self.capacity, self.rows.shape[0]
-        rows = [sds((held, SIDES * capacity, self.widths[c]), BF16)] * LINE
-        place = sds((SIDES, LINE * held * capacity, tokens), BF16)
-        start = sum(self.widths[:c]) if c else None
-        kernel = functools.partial(pick_kernel, held, capacity, self.chosen, start)
+        start = sum(self.widths[: c + 1]) if c + 1 < len(self.widths) else 0
+        kernel = functools.partial(hand_kernel, held, capacity, self.chosen, c == 0, start)
+        blocks = self.blocks
+        args, outs = list(blocks), self.selected(LINE - 1, self.widths[c])
+        outs.append(sds(blocks[0].shape, BF16))
+        specs = [VMEM] * 3
+        scratch = []
+        if start:
+            args.append(self.rows)
+            specs.append(HBM)
+            scratch.append(pltpu.SemaphoreType.DMA)
         if c == 0:
-            rest = sds((tokens, self.rows.shape[1] - self.widths[0]), BF16)
-            *sent, self.place, rest = self.call(
-                kernel,
-                [*rows, place, rest],
-                self.first,
-                self.first_other,
-                self.rows,
-                in_specs=[VMEM, VMEM, HBM],
-                scratch_shapes=[pltpu.SemaphoreType.DMA],
-            )
+            outs.append(sds((LINE - 1, SIDES * held * capacity, tokens), BF16))
         else:
-            sent = self.call(kernel, rows, self.rows, self.rest_other, self.place)
-        got = [sent[0]] + [None] * (LINE - 1)
-        for d in range(LINE - 1, 0, -1):
-            got[d] = self.send(sent[d], SIDES * d)
+            args.append(self.place)
+            specs.append(VMEM)
+        if start:
+            outs.append(sds((tokens, self.widths[c + 1]), BF16))
+        made = self.call(kernel, outs, *args, in_specs=specs, scratch_shapes=scratch)
+        mine, other, handed = made[:3]
         if c == 0:
-            self.rest_other = self.send(rest, 1)
-        return got
+            self.place = made[3]
+        passed = self.along(handed, PASSED)
+        if start:
+            self.leave(made[-1])
+        return passed, [mine, self.swap(other)]
+
+    def arrive(self, c, passed, parts):
+        held, capacity, tokens = self.held, self.capacity, self.rows.shape[0]
+        kernel = functools.partial(passed_kernel, held, capacity, self.chosen, c == 0)
+        rows = self.selected(1, self.widths[c])
+        if c == 0:
+            place = sds((1, SIDES * held * capacity, tokens), BF16)
+            mine, other, self.passed_place = self.call(kernel, [*rows, place], passed)
+        else:
+            mine, other = self.call(kernel, rows, passed, self.passed_place)
+        return [parts[0], mine, parts[1], self.swap(other)]
 
 
 def exchanged(grad_out, ids, probs, groups, held, capacity, widths):
@@ -348,8 +399,8 @@
     tokens, chosen = route_ids.shape
     share, across = units // dp, dp // 2
     direct = groups == LINE * SIDES
-    widths = chunks_of(features)
-    count = len(widths)
+    chunks = chunks_of(features)
+    widths = [sum(chunk) for chunk in chunks]
 
     ids, probs = route_ids.T, route_probs.T
     call = Chain()
@@ -363,52 +414,41 @@
         functools.partial(turn_kernel, dp),
         sds((held, 2, across, share, per_expert), BF16),
         saved,
-        *([grad_out, w_down] if direct else []),
+        *([grad_out] if direct else []),
     )
-    if direct:
-        arrived = [relay.chunk(c) for c in range(min(2, count))]
-
-    starts = [sum(widths[:c]) for c in range(count)]
-    state = {"raw": None, "grad": None}
-    summed = []
-
-    def reduced(c):
-        parts, width = arrived[c], widths[c]
+
+    state = {"raw": None, "grad": None, "start": 0}
+    summed, starts = [], []
+
+    def reduced(parts, at, width):
+        start = state["start"]
+        starts.append(start)
+        state["start"] = start + width
         piece = sds((across, held, share, width), BF16)
-        after = summed[-1][2][:1] if c else ()
-        keep, give = call(term_kernel, [piece, piece], turned, *parts, after=after)
+        keep, give = call(functools.partial(term_kernel, at), [piece, piece], turned, *parts)
         got = lax.ppermute(give, "dp", [(i, i ^ 1) for i in range(dp)])
-        final = c == count - 1
+        final = start + width == features
         if final:
             outs = [sds(saved.shape, BF16), sds((held, per_expert), F32)]
         else:
             outs = [sds((held, per_expert, units), F32)]
-        extra = ([state["raw"]] if c else []) + ([saved] if final else [])
-        kernel = functools.partial(raw_kernel, len(parts), starts[c], final)
-        made = call(
-            kernel,
-            outs,
-            w_down,
-            *parts,
-            *extra,
-        )
+        extra = ([state["raw"]] if start else []) + ([saved] if final else [])
+        kernel = functools.partial(raw_kernel, len(parts), start, width, at, final)
+        made = call(kernel, outs, w_down, *parts, *extra)
         state["raw"] = made if final else made[0]
-        cut = 16 * max(1, share // 64)
-        pieces = [sds((held, rows, width), BF16) for rows in (cut, share - cut)]
-        pairs = call(pair_kernel, pieces * (across - 1), keep, got)
+        pairs = call(pair_kernel, [sds((held, share, width), BF16)] * (across - 1), keep, got)
         others = []
-        for i, pair in enumerate(pairs):
-            step = 1 + i // 2
+        for step, pair in enumerate(pairs, 1):
             shift = [(2 * r + k, 2 * ((r + step) % across) + k) for r in range(across) for k in range(2)]
             others.append(lax.ppermute(pair, "dp", shift))
         summed.append((keep, got, others))
 
-    def finished(c):
-        keep, got, others = summed[c]
+    def finished(j):
+        keep, got, others = summed[j]
         before = [] if state["grad"] is None else [state["grad"]]
         count = 2 + len(others)
         state["grad"], _ = call(
-            functools.partial(last_kernel, len(others), starts[c]),
+            functools.partial(last_kernel, len(others), starts[j]),
             [sds((share, held, features), F32), sds((8, 128), F32)],
             keep,
             got,
@@ -418,18 +458,31 @@
             out_specs=[ANY, VMEM],
             input_output_aliases={count: 0} if before else {},
             scratch_shapes=[
-                pltpu.VMEM((share, held, widths[c]), F32),
+                pltpu.VMEM((share, held, keep.shape[3]), F32),
                 pltpu.SemaphoreType.DMA,
             ],
         )
 
-    for c in range(count):
-        reduced(c)
-        if direct and c + 2 < count:
-            arrived.append(relay.chunk(c + 2))
-        if c >= 1:
-            finished(c - 1)
+    def rest(parts, chunk):
+        at = 0
+        for width in chunk:
+            reduced(parts, at, width)
+            at += width
+            if 2 <= len(summed) < sum(map(len, chunks)):
+                finished(len(summed) - 2)
+
+    if direct:
+        passed, parts = relay.hand(0)
+        for c, chunk in enumerate(chunks):
+            whole = relay.arrive(c, passed, parts)
+            if c + 1 < len(chunks):
+                passed, parts = relay.hand(c + 1)
+            rest(whole, chunk)
+    else:
+        for c, chunk in enumerate(chunks):
+            rest(arrived[c], chunk)
     hidden_grad, sums = state["raw"]
+    finished(len(summed) - 2)
 
     if direct:
         swap = [(i, i ^ 1) for i in range(groups)]
@@ -451,7 +504,7 @@
         *returned,
         keep=False,
     ).T
-    finished(count - 1)
+    finished(len(summed) - 1)
     weight_grad = state["grad"]
     return (hidden_grad.reshape(hidden.shape), prob_grad, weight_grad)
 

time: 97.8 us -> 100 us (1.022)
  waiting for transfers between devices: 36 us -> 52.5 us
  starting transfers between devices: 38.3 us -> 28 us
  local copies, waits for them, and re-layouts: 6.31 us -> 3.13 us
    ppermute x14 -> x10, waiting for transfers between devices: 27.1 us -> 37.9 us  [the longest x6 29.1 us: along(): return lax.ppermute(block, 'expert', pairs)]
    ppermute x14 -> x10, starting transfers between devices: 23.1 us -> 16.6 us  [the longest x6 10.9 us: along(): return lax.ppermute(block, 'expert', pairs)]
    ppermute x8 -> x4, starting transfers between devices: 8.55 us -> 5.11 us  [reduced(): others.append(lax.ppermute(pair, 'dp', shift))]
    unnamed x20 -> x14, local copies, waits for them, and re-layouts: 6.31 us -> 3.13 us
    ppermute x8 -> x4, waiting for transfers between devices: 6.01 us -> 8.95 us  [reduced(): others.append(lax.ppermute(pair, 'dp', shift))]
    ppermute x1, waiting for transfers between devices: 0.57 us -> 2.13 us  [body(): both = jnp.stack([sums, lax.ppermute(sums, 'expert', swap)])]
  transfers between devices with their start and end apart: 30 -> 22, of which waited for: 12 -> 14; matrix products, arithmetic and copies ran while one was open for 0% -> 0% of each run, Pallas kernels for 10% -> 7%
where the time goes in v6:
time: 100 us
  waiting for transfers between devices  52.5 us (52%)
  starting transfers between devices  28 us (28%)
  Pallas kernels  15.5 us (16%)
  local copies, waits for them, and re-layouts  3.13 us (3%)
    ppermute x6, waiting for transfers between devices, along(): return lax.ppermute(block, 'expert', pairs)  29.1 us
    pallas_call x23, Pallas kernels, __call__(): pl.pallas_call(body, out_shape=outs, in_specs=in_specs, compiler_params=p...  15.5 us
    ppermute x6, starting transfers between devices, along(): return lax.ppermute(block, 'expert', pairs)  10.9 us
    ppermute x4, waiting for transfers between devices, reduced(): others.append(lax.ppermute(pair, 'dp', shift))  8.95 us
    ppermute x4, waiting for transfers between devices, swap(): lax.ppermute(block, 'expert', [(i, i ^ 1) for i in range(LINE * SIDES)])  8.78 us
    ppermute x4, starting transfers between devices, swap(): lax.ppermute(block, 'expert', [(i, i ^ 1) for i in range(LINE * SIDES)])  5.76 us
    ppermute x4, starting transfers between devices, reduced(): others.append(lax.ppermute(pair, 'dp', shift))  5.11 us
    ppermute x3, starting transfers between devices, body(): lax.ppermute(both, 'expert', [(i, i ^ SIDES * d) for i in range(groups)])  4.39 us
  transfers between devices with their start and end apart: 22, of which 14 were waited for; matrix products, arithmetic and copies ran while one was open for 0% of the time, Pallas kernels for 7%

profile of v6, /device:TPU:0, one launch (start us, length us, event | category | flops | bytes accessed | tf_op | source)
XLA Modules:
  0.0 100.0 jit_solution(7768934884869374019)
XLA Ops:
  0.6 1.8 %shard_map.76 = (s32[2,128]{1,0:T(2,128)}, bf16[144,768]{1,0:T(8,128)(2,1)}) custom-call(s32[2,128]{1,0:T(2,128)} %bitcast.13, f32[2,128]{1,0:T(2,128)} %bitcast.10, bf16[128,2048]{1,0:T(8,128)(2,1)} %refs_3_.1), custom_call_target="tpu_custom_call" | custom-call | flops 1 | bytes 1 | tf_op jit(solution)/shard_map/pallas_call | solution.py:37
  2.5 5.1 %collective-permute-start.1 = (bf16[144,768]{1,0:T(8,128)(2,1)}, bf16[144,768]{1,0:T(8,128)(2,1)S(1)}, u32[]{:S(2)}, u32[]{:S(2)}) collective-permute-start(bf16[144,768]{1,0:T(8,128)(2,1)} %get-tuple-element.35.refs_0_), channel_id=1, source_target_pairs={{0,6},{1,7},{2,4},{3,5},{4,2},{5,3},{6,0},{7,1},{8,14},{9,15},{10,... | collective-permute-start | bytes 663560 | tf_op jit(solution)/shard_map/ppermute | solution.py:319
  10.0 4.1 %collective-permute-done.1.refs_2_ = bf16[144,768]{1,0:T(8,128)(2,1)S(1)} collective-permute-done((bf16[144,768]{1,0:T(8,128)(2,1)}, bf16[144,768]{1,0:T(8,128)(2,1)S(1)}, u32[]{:S(2)}, u32[]{:S(2)}) %collective-permute-start.1) | collective-permute-done | bytes 221216 | tf_op jit(solution)/shard_map/ppermute | solution.py:319
  14.1 4.0 %collective-permute-done.refs_1_ = bf16[144,768]{1,0:T(8,128)(2,1)S(1)} collective-permute-done((bf16[144,768]{1,0:T(8,128)(2,1)}, bf16[144,768]{1,0:T(8,128)(2,1)S(1)}, u32[]{:S(2)}, u32[]{:S(2)}) %collective-permute-start) | collective-permute-done | bytes 221216 | tf_op jit(solution)/shard_map/ppermute | solution.py:319
  19.4 1.8 %collective-permute-start.3 = (bf16[128,1280]{1,0:T(8,128)(2,1)S(1)}, bf16[128,1280]{1,0:T(8,128)(2,1)S(1)}, u32[]{:S(2)}, u32[]{:S(2)}) collective-permute-start(bf16[128,1280]{1,0:T(8,128)(2,1)S(1)} %get-tuple-element.36.refs_0_), channel_id=1, source_target_pairs={{0,6},{1,7},{2,4},{3,5},{4,2},{5,3},{6,0},{7,1},{8,14},{9,15},{10,... | collective-permute-start | bytes 983048 | tf_op jit(solution)/shard_map/ppermute | solution.py:319
  21.2 2.6 %collective-permute-start.4 = (bf16[144,768]{1,0:T(8,128)(2,1)S(1)}, bf16[144,768]{1,0:T(8,128)(2,1)S(1)}, u32[]{:S(2)}, u32[]{:S(2)}) collective-permute-start(bf16[144,768]{1,0:T(8,128)(2,1)S(1)} %get-tuple-element.38), channel_id=1, source_target_pairs={{0,4},{1,5},{2,0},{3,1},{4,6},{5,7},{6,2},{7,3},{8,12},{9,13},{10,... | collective-permute-start | bytes 663560 | tf_op jit(solution)/shard_map/ppermute | solution.py:319
  23.8 1.5 %collective-permute-start.6 = (bf16[2,96,768]{2,1,0:T(8,128)(2,1)S(1)}, bf16[2,96,768]{2,1,0:T(8,128)(2,1)S(1)}, u32[]{:S(2)}, u32[]{:S(2)}) collective-permute-start(bf16[2,96,768]{2,1,0:T(8,128)(2,1)S(1)} %get-tuple-element.44), channel_id=1, source_target_pairs={{0,1},{1,0},{2,3},{3,2},{4,5},{5,4},{6,7},{7,6},{8,9},{9,8},{10,11... | collective-permute-start | bytes 884744 | tf_op jit(solution)/shard_map/ppermute | solution.py:322
  25.3 15.9 %collective-permute-done.4.refs_0_ = bf16[144,768]{1,0:T(8,128)(2,1)S(1)} collective-permute-done((bf16[144,768]{1,0:T(8,128)(2,1)S(1)}, bf16[144,768]{1,0:T(8,128)(2,1)S(1)}, u32[]{:S(2)}, u32[]{:S(2)}) %collective-permute-start.4) | collective-permute-done | bytes 221216 | tf_op jit(solution)/shard_map/ppermute | solution.py:319
  43.3 2.8 %collective-permute-done.7.refs_4_ = bf16[2,32,768]{2,1,0:T(8,128)(2,1)S(1)} collective-permute-done((bf16[2,32,768]{2,1,0:T(8,128)(2,1)S(1)}, bf16[2,32,768]{2,1,0:T(8,128)(2,1)S(1)}, u32[]{:S(2)}, u32[]{:S(2)}) %collective-permute-start.7) | collective-permute-done | bytes 98336 | tf_op jit(solution)/shard_map/ppermute | solution.py:322
  50.6 1.6 %collective-permute-start.11 = (bf16[2,192,768]{2,1,0:T(8,128)(2,1)S(1)}, bf16[2,192,768]{2,1,0:T(8,128)(2,1)S(1)}, u32[]{:S(2)}, u32[]{:S(2)}) collective-permute-start(bf16[2,192,768]{2,1,0:T(8,128)(2,1)S(1)} %shard_map.83.refs_2_), channel_id=1, source_target_pairs={{0,16},{8,24},{16,0},{24,8},{1,17},{9,25},{17,1},{25,9},{2,18},{10... | collective-permute-start | bytes 1769480 | tf_op jit(solution)/shard_map/ppermute | solution.py:443
  52.2 5.2 %collective-permute-done.5.refs_0_ = bf16[128,1280]{1,0:T(8,128)(2,1)S(1)} collective-permute-done((bf16[128,1280]{1,0:T(8,128)(2,1)S(1)}, bf16[128,1280]{1,0:T(8,128)(2,1)S(1)}, u32[]{:S(2)}, u32[]{:S(2)}) %collective-permute-start.5) | collective-permute-done | bytes 327712 | tf_op jit(solution)/shard_map/ppermute | solution.py:319
  57.6 1.6 %collective-permute-start.10 = (bf16[2,32,1280]{2,1,0:T(8,128)(2,1)S(1)}, bf16[2,32,1280]{2,1,0:T(8,128)(2,1)S(1)}, u32[]{:S(2)}, u32[]{:S(2)}) collective-permute-start(bf16[2,32,1280]{2,1,0:T(8,128)(2,1)S(1)} %get-tuple-element.50), channel_id=1, source_target_pairs={{0,1},{1,0},{2,3},{3,2},{4,5},{5,4},{6,7},{7,6},{8,9},{9,8},{10,11... | collective-permute-start | bytes 491528 | tf_op jit(solution)/shard_map/ppermute | solution.py:322
  59.2 3.2 %collective-permute-done.9.refs_3_ = bf16[2,96,1280]{2,1,0:T(8,128)(2,1)S(1)} collective-permute-done((bf16[2,96,1280]{2,1,0:T(8,128)(2,1)S(1)}, bf16[2,96,1280]{2,1,0:T(8,128)(2,1)S(1)}, u32[]{:S(2)}, u32[]{:S(2)}) %collective-permute-start.9) | collective-permute-done | bytes 491552 | tf_op jit(solution)/shard_map/ppermute | solution.py:322
  62.4 2.7 %collective-permute-done.10.refs_4_ = bf16[2,32,1280]{2,1,0:T(8,128)(2,1)S(1)} collective-permute-done((bf16[2,32,1280]{2,1,0:T(8,128)(2,1)S(1)}, bf16[2,32,1280]{2,1,0:T(8,128)(2,1)S(1)}, u32[]{:S(2)}, u32[]{:S(2)}) %collective-permute-start.10) | collective-permute-done | bytes 163872 | tf_op jit(solution)/shard_map/ppermute | solution.py:322
  67.3 1.4 %shard_map.88 = (f32[192,2,2048]{2,1,0:T(2,128)}, f32[8,128]{1,0:T(8,128)S(1)}) custom-call(bf16[2,2,192,768]{3,2,1,0:T(8,128)(2,1)S(1)} %get-tuple-element.46.refs_5_.refs_0_, bf16[2,2,192,768]{3,2,1,0:T(8,128)(2,1)S(1)} %collective-permute-done.8.refs_1_, bf16[2,192,768]{2,1,0:T(8,128)(2,1)S(1)} %collective-permute-done.11.refs_2_, ...), custom_call_target="tpu_custom_call" | custom-call | flops 1 | bytes 1 | tf_op jit(solution)/shard_map/pallas_call | solution.py:37
  71.8 4.9 %collective-permute-done.13.refs_2_ = bf16[2,192,256]{2,1,0:T(8,128)(2,1)S(1)} collective-permute-done((bf16[2,192,256]{2,1,0:T(8,128)(2,1)S(1)}, bf16[2,192,256]{2,1,0:T(8,128)(2,1)S(1)}, u32[]{:S(2)}, u32[]{:S(2)}) %collective-permute-start.13) | collective-permute-done | bytes 196640 | tf_op jit(solution)/shard_map/ppermute | solution.py:443
  78.3 1.4 %collective-permute-start.19 = (bf16[2,192,512]{2,1,0:T(8,128)(2,1)S(1)}, bf16[2,192,512]{2,1,0:T(8,128)(2,1)S(1)}, u32[]{:S(2)}, u32[]{:S(2)}) collective-permute-start(bf16[2,192,512]{2,1,0:T(8,128)(2,1)S(1)} %shard_map.91.refs_4_), channel_id=1, source_target_pairs={{0,16},{8,24},{16,0},{24,8},{1,17},{9,25},{17,1},{25,9},{2,18},{10... | collective-permute-start | bytes 1179656 | tf_op jit(solution)/shard_map/ppermute | solution.py:443
  79.7 1.6 %shard_map.94 = (bf16[8,2,32,768]{3,2,1,0:T(8,128)(2,1)}, f32[2,256]{1,0:T(2,128)S(1)}) custom-call(bf16[2,768,2048]{2,1,0:T(8,128)(2,1)S(1)} %copy-done, bf16[2,96,1280]{2,1,0:T(8,128)(2,1)S(1)} %get-tuple-element.40.refs_1_, bf16[2,32,1280]{2,1,0:T(8,128)(2,1)S(1)} %get-tuple-element.48.refs_2_.refs_5_, ...), custom_call_target="tpu_custom_call" | custom-call | flops 1 | bytes 1 | tf_op jit(solution)/shard_map/pallas_call | solution.py:37
  82.1 1.5 %collective-permute-start.15 = (f32[2,256]{1,0:T(2,128)S(1)}, f32[2,256]{1,0:T(2,128)S(1)}, u32[]{:S(2)}, u32[]{:S(2)}) collective-permute-start(f32[2,256]{1,0:T(2,128)S(1)} %get-tuple-element.61.refs_2_), channel_id=1, source_target_pairs={{0,1},{1,0},{2,3},{3,2},{4,5},{5,4},{6,7},{7,6},{8,9},{9,8},{10,11... | collective-permute-start | bytes 6152 | tf_op jit(solution)/shard_map/ppermute | solution.py:489
  83.6 2.1 %collective-permute-done.15 = f32[2,256]{1,0:T(2,128)S(1)} collective-permute-done((f32[2,256]{1,0:T(2,128)S(1)}, f32[2,256]{1,0:T(2,128)S(1)}, u32[]{:S(2)}, u32[]{:S(2)}) %collective-permute-start.15) | collective-permute-done | bytes 2080 | tf_op jit(solution)/shard_map/ppermute | solution.py:489
  85.7 3.3 %collective-permute-start.18 = (f32[2,2,256]{2,1,0:T(2,128)S(1)}, f32[2,2,256]{2,1,0:T(2,128)S(1)}, u32[]{:S(2)}, u32[]{:S(2)}) collective-permute-start(f32[2,2,256]{2,1,0:T(2,128)S(1)} %pad_maximum_fusion.refs_2_), channel_id=1, source_target_pairs={{0,6},{1,7},{2,4},{3,5},{4,2},{5,3},{6,0},{7,1},{8,14},{9,15},{10,... | collective-permute-start | bytes 12296 | tf_op jit(solution)/shard_map/ppermute | solution.py:491
  91.5 2.0 %collective-permute-done.17.refs_4_ = f32[2,2,256]{2,1,0:T(2,128)S(1)} collective-permute-done((f32[2,2,256]{2,1,0:T(2,128)S(1)}, f32[2,2,256]{2,1,0:T(2,128)S(1)}, u32[]{:S(2)}, u32[]{:S(2)}) %collective-permute-start.17) | collective-permute-done | bytes 4128 | tf_op jit(solution)/shard_map/ppermute | solution.py:491
  94.4 3.8 %collective-permute-done.21.refs_2_ = bf16[2,192,512]{2,1,0:T(8,128)(2,1)S(1)} collective-permute-done((bf16[2,192,512]{2,1,0:T(8,128)(2,1)S(1)}, bf16[2,192,512]{2,1,0:T(8,128)(2,1)S(1)}, u32[]{:S(2)}, u32[]{:S(2)}) %collective-permute-start.21) | collective-permute-done | bytes 393248 | tf_op jit(solution)/shard_map/ppermute | solution.py:443
  98.3 1.7 %shard_map.98 = (f32[192,2,2048]{2,1,0:T(2,128)}, f32[8,128]{1,0:T(8,128)}) custom-call(bf16[2,2,192,512]{3,2,1,0:T(8,128)(2,1)S(1)} %get-tuple-element.58.refs_7_.refs_0_, bf16[2,2,192,512]{3,2,1,0:T(8,128)(2,1)S(1)} %collective-permute-done.20.refs_1_, bf16[2,192,512]{2,1,0:T(8,128)(2,1)S(1)} %collective-permute-done.21.refs_2_, ...), custom_call_target="tpu_custom_call", output_to_operand_aliasing={{0}: (3, {})} | custom-call | flops 1 | bytes 1 | tf_op jit(solution)/shard_map/pallas_call | solution.py:37
  (58 shorter events, 21.5 us)
Async XLA Ops:
  2.5 11.6 %collective-permute-start.1 = (bf16[144,768]{1,0:T(8,128)(2,1)}, bf16[144,768]{1,0:T(8,128)(2,1)S(1)}, u32[]{:S(2)}, u32[]{:S(2)}) collective-permute-start(bf16[144,768]{1,0:T(8,128)(2,1)} %get-tuple-element.35.refs_0_), channel_id=1, source_target_pairs={{0,6},{1,7},{2,4},{3,5},{4,2},{5,3},{6,0},{7,1},{8,14},{9,15},{10,... | collective-permute-start | bytes 663560 | tf_op jit(solution)/shard_map/ppermute | solution.py:319
  7.6 10.5 %collective-permute-start = (bf16[144,768]{1,0:T(8,128)(2,1)}, bf16[144,768]{1,0:T(8,128)(2,1)S(1)}, u32[]{:S(2)}, u32[]{:S(2)}) collective-permute-start(bf16[144,768]{1,0:T(8,128)(2,1)} %get-tuple-element.35.refs_0_), channel_id=1, source_target_pairs={{0,2},{1,3},{2,0},{3,1},{4,6},{5,7},{6,4},{7,5},{8,10},{9,11},{10,... | collective-permute-start | bytes 663560 | tf_op jit(solution)/shard_map/ppermute | solution.py:319
  9.7 39.9 %copy-start = (bf16[2,768,2048]{2,1,0:T(8,128)(2,1)S(1)}, bf16[2,768,2048]{2,1,0:T(8,128)(2,1)}, u32[]{:S(2)}) copy-start(bf16[2,768,2048]{2,1,0:T(8,128)(2,1)} %refs_0_.9) | copy-start | bytes 18874372
  19.4 23.4 %collective-permute-start.3 = (bf16[128,1280]{1,0:T(8,128)(2,1)S(1)}, bf16[128,1280]{1,0:T(8,128)(2,1)S(1)}, u32[]{:S(2)}, u32[]{:S(2)}) collective-permute-start(bf16[128,1280]{1,0:T(8,128)(2,1)S(1)} %get-tuple-element.36.refs_0_), channel_id=1, source_target_pairs={{0,6},{1,7},{2,4},{3,5},{4,2},{5,3},{6,0},{7,1},{8,14},{9,15},{10,... | collective-permute-start | bytes 983048 | tf_op jit(solution)/shard_map/ppermute | solution.py:319
  21.2 21.7 %collective-permute-start.2 = (bf16[128,1280]{1,0:T(8,128)(2,1)S(1)}, bf16[128,1280]{1,0:T(8,128)(2,1)S(1)}, u32[]{:S(2)}, u32[]{:S(2)}) collective-permute-start(bf16[128,1280]{1,0:T(8,128)(2,1)S(1)} %get-tuple-element.36.refs_0_), channel_id=1, source_target_pairs={{0,2},{1,3},{2,0},{3,1},{4,6},{5,7},{6,4},{7,5},{8,10},{9,11},{10,... | collective-permute-start | bytes 983048 | tf_op jit(solution)/shard_map/ppermute | solution.py:319
  21.2 20.0 %collective-permute-start.4 = (bf16[144,768]{1,0:T(8,128)(2,1)S(1)}, bf16[144,768]{1,0:T(8,128)(2,1)S(1)}, u32[]{:S(2)}, u32[]{:S(2)}) collective-permute-start(bf16[144,768]{1,0:T(8,128)(2,1)S(1)} %get-tuple-element.38), channel_id=1, source_target_pairs={{0,4},{1,5},{2,0},{3,1},{4,6},{5,7},{6,2},{7,3},{8,12},{9,13},{10,... | collective-permute-start | bytes 663560 | tf_op jit(solution)/shard_map/ppermute | solution.py:319
  23.8 19.4 %collective-permute-start.6 = (bf16[2,96,768]{2,1,0:T(8,128)(2,1)S(1)}, bf16[2,96,768]{2,1,0:T(8,128)(2,1)S(1)}, u32[]{:S(2)}, u32[]{:S(2)}) collective-permute-start(bf16[2,96,768]{2,1,0:T(8,128)(2,1)S(1)} %get-tuple-element.44), channel_id=1, source_target_pairs={{0,1},{1,0},{2,3},{3,2},{4,5},{5,4},{6,7},{7,6},{8,9},{9,8},{10,11... | collective-permute-start | bytes 884744 | tf_op jit(solution)/shard_map/ppermute | solution.py:322
  41.4 4.7 %collective-permute-start.7 = (bf16[2,32,768]{2,1,0:T(8,128)(2,1)S(1)}, bf16[2,32,768]{2,1,0:T(8,128)(2,1)S(1)}, u32[]{:S(2)}, u32[]{:S(2)}) collective-permute-start(bf16[2,32,768]{2,1,0:T(8,128)(2,1)S(1)} %get-tuple-element.45), channel_id=1, source_target_pairs={{0,1},{1,0},{2,3},{3,2},{4,5},{5,4},{6,7},{7,6},{8,9},{9,8},{10,11... | collective-permute-start | bytes 294920 | tf_op jit(solution)/shard_map/ppermute | solution.py:322
  46.9 3.5 %collective-permute-start.8 = (bf16[2,2,192,768]{3,2,1,0:T(8,128)(2,1)S(1)}, bf16[2,2,192,768]{3,2,1,0:T(8,128)(2,1)S(1)}, u32[]{:S(2)}, u32[]{:S(2)}) collective-permute-start(bf16[2,2,192,768]{3,2,1,0:T(8,128)(2,1)S(1)} %get-tuple-element.47), channel_id=1, source_target_pairs={{0,8},{8,0},{16,24},{24,16},{1,9},{9,1},{17,25},{25,17},{2,10},{10... | collective-permute-start | bytes 3538952 | tf_op jit(solution)/shard_map/ppermute | solution.py:429
  47.0 10.4 %collective-permute-start.5 = (bf16[128,1280]{1,0:T(8,128)(2,1)S(1)}, bf16[128,1280]{1,0:T(8,128)(2,1)S(1)}, u32[]{:S(2)}, u32[]{:S(2)}) collective-permute-start(bf16[128,1280]{1,0:T(8,128)(2,1)S(1)} %get-tuple-element.41.refs_5_), channel_id=1, source_target_pairs={{0,4},{1,5},{2,0},{3,1},{4,6},{5,7},{6,2},{7,3},{8,12},{9,13},{10,... | collective-permute-start | bytes 983048 | tf_op jit(solution)/shard_map/ppermute | solution.py:319
  48.3 14.1 %collective-permute-start.9 = (bf16[2,96,1280]{2,1,0:T(8,128)(2,1)S(1)}, bf16[2,96,1280]{2,1,0:T(8,128)(2,1)S(1)}, u32[]{:S(2)}, u32[]{:S(2)}) collective-permute-start(bf16[2,96,1280]{2,1,0:T(8,128)(2,1)S(1)} %get-tuple-element.49), channel_id=1, source_target_pairs={{0,1},{1,0},{2,3},{3,2},{4,5},{5,4},{6,7},{7,6},{8,9},{9,8},{10,11... | collective-permute-start | bytes 1474568 | tf_op jit(solution)/shard_map/ppermute | solution.py:322
  50.6 16.7 %collective-permute-start.11 = (bf16[2,192,768]{2,1,0:T(8,128)(2,1)S(1)}, bf16[2,192,768]{2,1,0:T(8,128)(2,1)S(1)}, u32[]{:S(2)}, u32[]{:S(2)}) collective-permute-start(bf16[2,192,768]{2,1,0:T(8,128)(2,1)S(1)} %shard_map.83.refs_2_), channel_id=1, source_target_pairs={{0,16},{8,24},{16,0},{24,8},{1,17},{9,25},{17,1},{25,9},{2,18},{10... | collective-permute-start | bytes 1769480 | tf_op jit(solution)/shard_map/ppermute | solution.py:443
  57.6 7.5 %collective-permute-start.10 = (bf16[2,32,1280]{2,1,0:T(8,128)(2,1)S(1)}, bf16[2,32,1280]{2,1,0:T(8,128)(2,1)S(1)}, u32[]{:S(2)}, u32[]{:S(2)}) collective-permute-start(bf16[2,32,1280]{2,1,0:T(8,128)(2,1)S(1)} %get-tuple-element.50), channel_id=1, source_target_pairs={{0,1},{1,0},{2,3},{3,2},{4,5},{5,4},{6,7},{7,6},{8,9},{9,8},{10,11... | collective-permute-start | bytes 491528 | tf_op jit(solution)/shard_map/ppermute | solution.py:322
  65.5 1.8 %collective-permute-start.12 = (bf16[2,2,192,256]{3,2,1,0:T(8,128)(2,1)S(1)}, bf16[2,2,192,256]{3,2,1,0:T(8,128)(2,1)S(1)}, u32[]{:S(2)}, u32[]{:S(2)}) collective-permute-start(bf16[2,2,192,256]{3,2,1,0:T(8,128)(2,1)S(1)} %get-tuple-element.52), channel_id=1, source_target_pairs={{0,8},{8,0},{16,24},{24,16},{1,9},{9,1},{17,25},{25,17},{2,10},{10... | collective-permute-start | bytes 1179656 | tf_op jit(solution)/shard_map/ppermute | solution.py:429
  69.3 2.4 %collective-permute-start.14 = (bf16[2,2,192,512]{3,2,1,0:T(8,128)(2,1)S(1)}, bf16[2,2,192,512]{3,2,1,0:T(8,128)(2,1)S(1)}, u32[]{:S(2)}, u32[]{:S(2)}) collective-permute-start(bf16[2,2,192,512]{3,2,1,0:T(8,128)(2,1)S(1)} %get-tuple-element.56), channel_id=1, source_target_pairs={{0,8},{8,0},{16,24},{24,16},{1,9},{9,1},{17,25},{25,17},{2,10},{10... | collective-permute-start | bytes 2359304 | tf_op jit(solution)/shard_map/ppermute | solution.py:429
  69.5 7.2 %collective-permute-start.13 = (bf16[2,192,256]{2,1,0:T(8,128)(2,1)S(1)}, bf16[2,192,256]{2,1,0:T(8,128)(2,1)S(1)}, u32[]{:S(2)}, u32[]{:S(2)}) collective-permute-start(bf16[2,192,256]{2,1,0:T(8,128)(2,1)S(1)} %shard_map.87.refs_3_), channel_id=1, source_target_pairs={{0,16},{8,24},{16,0},{24,8},{1,17},{9,25},{17,1},{25,9},{2,18},{10... | collective-permute-start | bytes 589832 | tf_op jit(solution)/shard_map/ppermute | solution.py:443
  78.2 3.1 %collective-permute-start.20 = (bf16[2,2,192,512]{3,2,1,0:T(8,128)(2,1)S(1)}, bf16[2,2,192,512]{3,2,1,0:T(8,128)(2,1)S(1)}, u32[]{:S(2)}, u32[]{:S(2)}) collective-permute-start(bf16[2,2,192,512]{3,2,1,0:T(8,128)(2,1)S(1)} %get-tuple-element.63), channel_id=1, source_target_pairs={{0,8},{8,0},{16,24},{24,16},{1,9},{9,1},{17,25},{25,17},{2,10},{10... | collective-permute-start | bytes 2359304 | tf_op jit(solution)/shard_map/ppermute | solution.py:429
  78.3 12.0 %collective-permute-start.19 = (bf16[2,192,512]{2,1,0:T(8,128)(2,1)S(1)}, bf16[2,192,512]{2,1,0:T(8,128)(2,1)S(1)}, u32[]{:S(2)}, u32[]{:S(2)}) collective-permute-start(bf16[2,192,512]{2,1,0:T(8,128)(2,1)S(1)} %shard_map.91.refs_4_), channel_id=1, source_target_pairs={{0,16},{8,24},{16,0},{24,8},{1,17},{9,25},{17,1},{25,9},{2,18},{10... | collective-permute-start | bytes 1179656 | tf_op jit(solution)/shard_map/ppermute | solution.py:443
  81.4 16.9 %collective-permute-start.21 = (bf16[2,192,512]{2,1,0:T(8,128)(2,1)S(1)}, bf16[2,192,512]{2,1,0:T(8,128)(2,1)S(1)}, u32[]{:S(2)}, u32[]{:S(2)}) collective-permute-start(bf16[2,192,512]{2,1,0:T(8,128)(2,1)S(1)} %shard_map.95.refs_4_), channel_id=1, source_target_pairs={{0,16},{8,24},{16,0},{24,8},{1,17},{9,25},{17,1},{25,9},{2,18},{10... | collective-permute-start | bytes 1179656 | tf_op jit(solution)/shard_map/ppermute | solution.py:443
  82.1 3.6 %collective-permute-start.15 = (f32[2,256]{1,0:T(2,128)S(1)}, f32[2,256]{1,0:T(2,128)S(1)}, u32[]{:S(2)}, u32[]{:S(2)}) collective-permute-start(f32[2,256]{1,0:T(2,128)S(1)} %get-tuple-element.61.refs_2_), channel_id=1, source_target_pairs={{0,1},{1,0},{2,3},{3,2},{4,5},{5,4},{6,7},{7,6},{8,9},{9,8},{10,11... | collective-permute-start | bytes 6152 | tf_op jit(solution)/shard_map/ppermute | solution.py:489
  85.7 5.7 %collective-permute-start.18 = (f32[2,2,256]{2,1,0:T(2,128)S(1)}, f32[2,2,256]{2,1,0:T(2,128)S(1)}, u32[]{:S(2)}, u32[]{:S(2)}) collective-permute-start(f32[2,2,256]{2,1,0:T(2,128)S(1)} %pad_maximum_fusion.refs_2_), channel_id=1, source_target_pairs={{0,6},{1,7},{2,4},{3,5},{4,2},{5,3},{6,0},{7,1},{8,14},{9,15},{10,... | collective-permute-start | bytes 12296 | tf_op jit(solution)/shard_map/ppermute | solution.py:491
  89.0 4.5 %collective-permute-start.17 = (f32[2,2,256]{2,1,0:T(2,128)S(1)}, f32[2,2,256]{2,1,0:T(2,128)S(1)}, u32[]{:S(2)}, u32[]{:S(2)}) collective-permute-start(f32[2,2,256]{2,1,0:T(2,128)S(1)} %pad_maximum_fusion.refs_2_), channel_id=1, source_target_pairs={{0,4},{1,5},{2,6},{3,7},{4,0},{5,1},{6,2},{7,3},{8,12},{9,13},{10,... | collective-permute-start | bytes 12296 | tf_op jit(solution)/shard_map/ppermute | solution.py:491
  89.0 4.5 %collective-permute-start.16 = (f32[2,2,256]{2,1,0:T(2,128)S(1)}, f32[2,2,256]{2,1,0:T(2,128)S(1)}, u32[]{:S(2)}, u32[]{:S(2)}) collective-permute-start(f32[2,2,256]{2,1,0:T(2,128)S(1)} %pad_maximum_fusion.refs_2_), channel_id=1, source_target_pairs={{0,2},{1,3},{2,0},{3,1},{4,6},{5,7},{6,4},{7,5},{8,10},{9,11},{10,... | collective-permute-start | bytes 12296 | tf_op jit(solution)/shard_map/ppermute | solution.py:491
  90.3 3.2 %copy-start.6 = (s32[2,128]{1,0:T(2,128)S(1)}, s32[2,128]{1,0:T(2,128)}, u32[]{:S(2)}) copy-start(s32[2,128]{1,0:T(2,128)} %get-tuple-element.60.refs_0_) | copy-start | bytes 3076
  (5 other events, 8.4 us)

commit v7 on v6

--- a/solution.py
+++ b/solution.py
@@ -12,11 +12,7 @@
 ANY = pl.BlockSpec(memory_space=pl.ANY)
 HBM = pl.BlockSpec(memory_space=pltpu.HBM)
 
-LINE, SIDES = 4, 2
-FAR, NEAR, PASSED = (3, 2, 1, 0), (1, 0, 3, 2), (2, 0, 3, 1)
-FROM = (0, 1, 3, 2)
-MASKS = tuple(SIDES * d + s for s in range(SIDES) for d in FROM)
-INFO = 16
+GROUPS, INFO = 8, 16
 
 
 class Chain:
@@ -64,19 +60,24 @@
     return [jnp.sum(jnp.where(n, before, 0.0), axis=0, keepdims=True) for n in named]
 
 
-def begin_kernel(experts, capacity, ids_ref, probs_ref, rows_ref, flat_ref, out_ref, *scratch):
-    ids_got, probs_got, sems = scratch
+def begin_kernel(experts, capacity, ids_ref, probs_ref, rows_ref, flat_ref, *refs):
+    out_refs, (ids_got, probs_got, sems) = refs[:-3], refs[-3:]
     chosen, tokens = ids_got.shape
-    width = out_ref.shape[1]
     copies = [
         pltpu.make_async_copy(ids_ref, ids_got, sems.at[0]),
         pltpu.make_async_copy(probs_ref, probs_got, sems.at[1]),
-        pltpu.make_async_copy(rows_ref.at[:, :width], out_ref.at[:tokens], sems.at[2]),
     ]
+    start = 0
+    for i, ref in enumerate(out_refs):
+        width = ref.shape[1]
+        rows = rows_ref.at[:, start : start + width]
+        copies.append(pltpu.make_async_copy(rows, ref.at[:tokens], sems.at[2 + i]))
+        start += width
     for copy in copies:
         copy.start()
     for copy in copies:
         copy.wait()
+    out_ref, width = out_refs[0], out_refs[0].shape[1]
     ids = ids_got[...]
     _, _, word = gates_of(probs_got[...])
     slots = slots_of(ids, experts)
@@ -89,70 +90,27 @@
         out_ref[tokens:, tokens:] = jnp.zeros((INFO, width - tokens), BF16)
 
 
-def places(held, capacity, chosen, ref, place_ref):
-    tokens = place_ref.shape[1]
-    rows = held * capacity
+def pick_kernel(held, capacity, chosen, first, blocks_ref, *refs):
+    if first:
+        out_ref, place_ref = refs
+    else:
+        place_ref, out_ref = refs
+    sources, rows, tokens = place_ref.shape
     me = lax.axis_index("expert")
-    local = lax.broadcasted_iota(I32, (rows, tokens), 0)
-    info = ref[tokens:, :tokens].astype(F32)
-    flat = (info[:chosen] * capacity + info[chosen : 2 * chosen]).astype(I32)
-    word = info[2 * chosen : 3 * chosen]
-    for side in range(SIDES):
-        slot = local + (me ^ side) * rows
-        hits = [jnp.where(flat[k : k + 1] == slot, word[k : k + 1], 0.0) for k in range(chosen)]
-        place_ref[side * rows : (side + 1) * rows, :] = functools.reduce(jnp.add, hits).astype(BF16)
-
-
-def pick(held, capacity, block_refs, place_ref, out_refs):
-    tokens = place_ref.shape[2]
-    for j, ref in enumerate(block_refs):
-        scaled = jnp.dot(place_ref[j], ref[:tokens, :], preferred_element_type=F32).astype(BF16)
-        for side, out_ref in enumerate(out_refs):
-            for e in range(held):
-                at = (side * held + e) * capacity
-                out_ref[e, j * capacity : (j + 1) * capacity, :] = scaled[at : at + capacity]
-
-
-def hand_kernel(held, capacity, chosen, first, start, own_ref, near_ref, far_ref, *refs):
-    blocks = (own_ref, near_ref, far_ref)
-    if start:
-        rows_ref, refs = refs[0], refs[1:]
-        *refs, sem = refs
-        next_ref, refs = refs[-1], refs[:-1]
-        copy = pltpu.make_async_copy(
-            rows_ref.at[:, start : start + next_ref.shape[1]], next_ref, sem
-        )
-        copy.start()
-    if first:
-        mine_ref, other_ref, pass_ref, place_ref = refs
-    else:
-        place_ref, mine_ref, other_ref, pass_ref = refs
-    place = lax.axis_index("expert") // SIDES
-    inner = jnp.logical_and(place > 0, place < LINE - 1)
-
-    @pl.when(inner)
-    def _():
-        pass_ref[...] = far_ref[...]
-
-    @pl.when(jnp.logical_not(inner))
-    def _():
-        pass_ref[...] = own_ref[...]
-
-    if first:
-        for j, ref in enumerate(blocks):
-            places(held, capacity, chosen, ref, place_ref.at[j])
-    pick(held, capacity, blocks, place_ref, (mine_ref, other_ref))
-    if start:
-        copy.wait()
-
-
-def passed_kernel(held, capacity, chosen, first, block_ref, *refs):
-    if first:
-        mine_ref, other_ref, place_ref = refs
-        places(held, capacity, chosen, block_ref, place_ref.at[0])
-    else:
-        place_ref, mine_ref, other_ref = refs
-    pick(held, capacity, (block_ref,), place_ref, (mine_ref, other_ref))
+    for part in range(sources):
+        if first:
+            info = blocks_ref[me ^ part, tokens:, :tokens].astype(F32)
+            flat = (info[:chosen] * capacity + info[chosen : 2 * chosen]).astype(I32)
+            word = info[2 * chosen : 3 * chosen]
+            slot = lax.broadcasted_iota(I32, (rows, tokens), 0) + me * rows
+            hits = [jnp.where(flat[k : k + 1] == slot, word[k : k + 1], 0.0) for k in range(chosen)]
+            place_ref[part] = functools.reduce(jnp.add, hits).astype(BF16)
+        scaled = jnp.dot(
+            place_ref[part], blocks_ref[me ^ part, :tokens], preferred_element_type=F32
+        ).astype(BF16)
+        for e in range(held):
+            at = slice(part * capacity, (part + 1) * capacity)
+            out_ref[e, at, :] = scaled[e * capacity : (e + 1) * capacity]
 
 
 def turn_kernel(dp, hidden_ref, *refs):
@@ -160,7 +118,7 @@
     parts, held, _, units = hidden_ref.shape
     share, across = units // dp, dp // 2
     me = lax.axis_index("expert") if parts > 1 else 0
-    masks = MASKS if parts > 1 else (0,)
+    masks = range(parts)
     mine = lax.axis_index("dp")
     core, row = mine % 2, mine // 2
     for e in range(held):
@@ -230,7 +188,7 @@
         sources, _, own, units = hidden_ref.shape
         me = lax.axis_index("expert") if sources > 1 else 0
         folds = []
-        for part, mask in enumerate(MASKS if sources > 1 else (0,)):
+        for part, mask in enumerate(range(sources)):
             block = raw[part * own : (part + 1) * own]
             grad_ref[me ^ mask, e] = block.astype(BF16)
             product = block * hidden_ref[me ^ mask, e].astype(F32)
@@ -246,10 +204,10 @@
     chosen, tokens = flat_ref.shape
     if direct:
         values = []
-        for mask in range(LINE * SIDES):
-            at = MASKS.index(mask) * capacity
-            ref = refs[mask // SIDES]
-            values += [ref[mask % SIDES, e : e + 1, at : at + capacity] for e in range(ref.shape[1])]
+        for mask in range(GROUPS):
+            at = mask * capacity
+            ref = refs[mask // 2]
+            values += [ref[mask % 2, e : e + 1, at : at + capacity] for e in range(ref.shape[1])]
         lanes = 128 // capacity
         values = jnp.concatenate(
             [
@@ -266,7 +224,7 @@
     spare = jnp.zeros((-lines % 8, 128), F32)
     columns = jnp.concatenate([values, spare], axis=0).T if spare.size else values.T
     total, gates, word = gates_of(probs_ref[...])
-    group = lines * 128 // (LINE * SIDES)
+    group = lines * 128 // GROUPS
     picked = [jnp.zeros((1, tokens), F32) for _ in range(chosen)]
     for line in range(lines):
         at = lax.broadcasted_iota(I32, (128, tokens), 0) + line * 128
@@ -281,88 +239,10 @@
 
 
 def chunks_of(features):
-    unit = features // 16
-    return [[6 * unit], [2 * unit, 4 * unit, 4 * unit]]
+    return [features // 4] * 4
 
 
 sds = jax.ShapeDtypeStruct
-
-
-class Relay:
-    def __init__(self, call, grad_out, ids, probs, held, capacity, widths):
-        tokens = grad_out.shape[0]
-        self.call, self.rows, self.held, self.capacity = call, grad_out, held, capacity
-        self.chosen, self.widths = ids.shape[0], widths
-        self.place, self.passed_place, self.blocks = None, None, None
-        self.flat, first = call(
-            functools.partial(begin_kernel, LINE * SIDES * held, capacity),
-            [sds(ids.shape, I32), sds((tokens + INFO, widths[0]), BF16)],
-            ids,
-            probs,
-            grad_out,
-            in_specs=[HBM] * 3,
-            scratch_shapes=[
-                pltpu.VMEM(ids.shape, I32),
-                pltpu.VMEM(probs.shape, F32),
-                pltpu.SemaphoreType.DMA((3,)),
-            ],
-            room=60,
-            keep=False,
-        )
-        self.leave(first)
-
-    def leave(self, own):
-        self.blocks = [own, self.along(own, NEAR), self.along(own, FAR)]
-
-    def along(self, block, targets):
-        pairs = [(p * SIDES + s, targets[p] * SIDES + s) for p in range(LINE) for s in range(SIDES)]
-        return lax.ppermute(block, "expert", pairs)
-
-    def swap(self, block):
-        return lax.ppermute(block, "expert", [(i, i ^ 1) for i in range(LINE * SIDES)])
-
-    def selected(self, blocks, width):
-        return [sds((self.held, blocks * self.capacity, width), BF16)] * SIDES
-
-    def hand(self, c):
-        held, capacity, tokens = self.held, self.capacity, self.rows.shape[0]
-        start = sum(self.widths[: c + 1]) if c + 1 < len(self.widths) else 0
-        kernel = functools.partial(hand_kernel, held, capacity, self.chosen, c == 0, start)
-        blocks = self.blocks
-        args, outs = list(blocks), self.selected(LINE - 1, self.widths[c])
-        outs.append(sds(blocks[0].shape, BF16))
-        specs = [VMEM] * 3
-        scratch = []
-        if start:
-            args.append(self.rows)
-            specs.append(HBM)
-            scratch.append(pltpu.SemaphoreType.DMA)
-        if c == 0:
-            outs.append(sds((LINE - 1, SIDES * held * capacity, tokens), BF16))
-        else:
-            args.append(self.place)
-            specs.append(VMEM)
-        if start:
-            outs.append(sds((tokens, self.widths[c + 1]), BF16))
-        made = self.call(kernel, outs, *args, in_specs=specs, scratch_shapes=scratch)
-        mine, other, handed = made[:3]
-        if c == 0:
-            self.place = made[3]
-        passed = self.along(handed, PASSED)
-        if start:
-            self.leave(made[-1])
-        return passed, [mine, self.swap(other)]
-
-    def arrive(self, c, passed, parts):
-        held, capacity, tokens = self.held, self.capacity, self.rows.shape[0]
-        kernel = functools.partial(passed_kernel, held, capacity, self.chosen, c == 0)
-        rows = self.selected(1, self.widths[c])
-        if c == 0:
-            place = sds((1, SIDES * held * capacity, tokens), BF16)
-            mine, other, self.passed_place = self.call(kernel, [*rows, place], passed)
-        else:
-            mine, other = self.call(kernel, rows, passed, self.passed_place)
-        return [parts[0], mine, parts[1], self.swap(other)]
 
 
 def exchanged(grad_out, ids, probs, groups, held, capacity, widths):
@@ -398,15 +278,30 @@
     per_expert = slots // held
     tokens, chosen = route_ids.shape
     share, across = units // dp, dp // 2
-    direct = groups == LINE * SIDES
-    chunks = chunks_of(features)
-    widths = [sum(chunk) for chunk in chunks]
+    direct = groups == GROUPS
+    widths = chunks_of(features)
 
     ids, probs = route_ids.T, route_probs.T
     call = Chain()
     if direct:
-        relay = Relay(call, grad_out, ids, probs, held, capacity, widths)
-        flat, saved = relay.flat, hidden[0]
+        flat, *blocks = call(
+            functools.partial(begin_kernel, groups * held, capacity),
+            [sds(ids.shape, I32)]
+            + [sds((tokens + (0 if c else INFO), w), BF16) for c, w in enumerate(widths)],
+            ids,
+            probs,
+            grad_out,
+            in_specs=[HBM] * 3,
+            scratch_shapes=[
+                pltpu.VMEM(ids.shape, I32),
+                pltpu.VMEM(probs.shape, F32),
+                pltpu.SemaphoreType.DMA((2 + len(widths),)),
+            ],
+            room=60,
+            keep=False,
+        )
+        gathered = [lax.all_gather(block, "expert") for block in blocks]
+        saved = hidden[0]
     else:
         flat, arrived = exchanged(grad_out, ids, probs, groups, held, capacity, widths)
         saved = hidden[0].transpose(1, 0, 2, 3).reshape(1, held, per_expert, units)
@@ -414,7 +309,6 @@
         functools.partial(turn_kernel, dp),
         sds((held, 2, across, share, per_expert), BF16),
         saved,
-        *([grad_out] if direct else []),
     )
 
     state = {"raw": None, "grad": None, "start": 0}
@@ -463,24 +357,22 @@
             ],
         )
 
-    def rest(parts, chunk):
-        at = 0
-        for width in chunk:
-            reduced(parts, at, width)
-            at += width
-            if 2 <= len(summed) < sum(map(len, chunks)):
-                finished(len(summed) - 2)
-
-    if direct:
-        passed, parts = relay.hand(0)
-        for c, chunk in enumerate(chunks):
-            whole = relay.arrive(c, passed, parts)
-            if c + 1 < len(chunks):
-                passed, parts = relay.hand(c + 1)
-            rest(whole, chunk)
-    else:
-        for c, chunk in enumerate(chunks):
-            rest(arrived[c], chunk)
+    place = None
+    for c, width in enumerate(widths):
+        if direct:
+            kernel = functools.partial(pick_kernel, held, capacity, chosen, c == 0)
+            rows = sds((held, per_expert, width), BF16)
+            if c == 0:
+                rows, place = call(
+                    kernel, [rows, sds((groups, held * capacity, tokens), BF16)], gathered[c]
+                )
+            else:
+                rows = call(kernel, rows, gathered[c], place)
+            reduced([rows], 0, width)
+        else:
+            reduced(arrived[c], 0, width)
+        if c >= 2:
+            finished(c - 2)
     hidden_grad, sums = state["raw"]
     finished(len(summed) - 2)
 
@@ -488,8 +380,8 @@
         swap = [(i, i ^ 1) for i in range(groups)]
         both = jnp.stack([sums, lax.ppermute(sums, "expert", swap)])
         returned = [both] + [
-            lax.ppermute(both, "expert", [(i, i ^ (SIDES * d)) for i in range(groups)])
-            for d in range(1, LINE)
+            lax.ppermute(both, "expert", [(i, i ^ d) for i in range(groups)])
+            for d in range(2, groups, 2)
         ]
     else:
         sums = sums.reshape(held, groups, capacity).transpose(1, 0, 2).reshape(groups, -1)

time: 100 us -> 217 us (2.17)
  waiting for transfers between devices: 52.5 us -> 149 us
  local copies, waits for them, and re-layouts: 3.13 us -> 24.2 us
  starting transfers between devices: 28 us -> 10.5 us
  between operations: 0.86 us -> 14.1 us
  Pallas kernels: 15.5 us -> 19.4 us
    all_gather x0 -> x4, waiting for transfers between devices: none -> 130 us  [body(): gathered = [lax.all_gather(block, 'expert') for block in blocks]]
    ppermute x13 -> x3, waiting for transfers between devices: 40 us -> 0.01 us  [body(): lax.ppermute(both, 'expert', [(i, i ^ d) for i in range(groups)])]
    unnamed x14 -> x54, local copies, waits for them, and re-layouts: 3.13 us -> 24.2 us
    ppermute x13 -> x3, starting transfers between devices: 21 us -> 4.39 us  [body(): lax.ppermute(both, 'expert', [(i, i ^ d) for i in range(groups)])]
    ppermute x4, waiting for transfers between devices: 8.95 us -> 14 us  [reduced(): others.append(lax.ppermute(pair, 'dp', shift))]
    pallas_call x23, Pallas kernels: 15.5 us -> 19.4 us  [__call__(): pl.pallas_call(body, out_shape=outs, in_specs=in_specs, compiler_params=p...]
  transfers between devices with their start and end apart: 22 -> 16, of which waited for: 14 -> 8; matrix products, arithmetic and copies ran while one was open for 0% -> 0% of each run, Pallas kernels for 7% -> 7%
where the time goes in v7:
time: 217 us
  waiting for transfers between devices  149 us (69%)
  local copies, waits for them, and re-layouts  24.2 us (11%)
  Pallas kernels  19.4 us (9%)
  between operations  14.1 us (6%)
  starting transfers between devices  10.5 us (5%)
    all_gather x4, waiting for transfers between devices, body(): gathered = [lax.all_gather(block, 'expert') for block in blocks]  130 us
    unnamed x54, local copies, waits for them, and re-layouts  24.2 us
    pallas_call x23, Pallas kernels, __call__(): pl.pallas_call(body, out_shape=outs, in_specs=in_specs, compiler_params=p...  19.4 us
    ppermute x4, waiting for transfers between devices, reduced(): others.append(lax.ppermute(pair, 'dp', shift))  14 us
    ppermute x4, starting transfers between devices, reduced(): others.append(lax.ppermute(pair, 'dp', shift))  5.15 us
    ppermute x3, starting transfers between devices, body(): lax.ppermute(both, 'expert', [(i, i ^ d) for i in range(groups)])  4.39 us
  transfers between devices with their start and end apart: 16, of which 8 were waited for; matrix products, arithmetic and copies ran while one was open for 0% of the time, Pallas kernels for 7%

profile of v7, /device:TPU:0, one launch (start us, length us, event | category | flops | bytes accessed | tf_op | source)
XLA Modules:
  0.0 216.8 jit_solution(609152764068283822)
XLA Ops:
  7.2 2.0 shard_map.76
  12.2 42.3 %all-gather.11.cloned.1.call-done = bf16[1152,512]{1,0:T(8,128)(2,1)} async-done(((bf16[144,512]{1,0:T(8,128)(2,1)}), bf16[1152,512]{1,0:T(8,128)(2,1)}) %all-gather.11.cloned.1.call-update) | async-done | bytes 1179664 | tf_op jit(solution)/shard_map/all_gather | solution.py:303
  56.1 1.4 shard_map.79
  58.3 2.8 %copy-done = bf16[2,768,2048]{2,1,0:T(8,128)(2,1)S(1)} copy-done((bf16[2,768,2048]{2,1,0:T(8,128)(2,1)S(1)}, bf16[2,768,2048]{2,1,0:T(8,128)(2,1)}, u32[]{:S(2)}) %copy-start) | copy-done | bytes 6291480
  62.7 2.0 shard_map.81.refs_2_
  64.7 31.0 %all-gather.15.cloned.1.call-done = bf16[1024,512]{1,0:T(8,128)(2,1)} async-done(((bf16[128,512]{1,0:T(8,128)(2,1)}), bf16[1024,512]{1,0:T(8,128)(2,1)}) %all-gather.15.cloned.1.call-update) | async-done | bytes 1048592 | tf_op jit(solution)/shard_map/all_gather | solution.py:303
  97.9 3.0 %copy-done.1 = bf16[2,768,2048]{2,1,0:T(8,128)(2,1)S(1)} copy-done((bf16[2,768,2048]{2,1,0:T(8,128)(2,1)S(1)}, bf16[2,768,2048]{2,1,0:T(8,128)(2,1)}, u32[]{:S(2)}) %copy-start.1) | copy-done | bytes 6291480
  103.6 33.1 %all-gather.13.cloned.1.call-done = bf16[1024,512]{1,0:T(8,128)(2,1)} async-done(((bf16[128,512]{1,0:T(8,128)(2,1)}), bf16[1024,512]{1,0:T(8,128)(2,1)}) %all-gather.13.cloned.1.call-update) | async-done | bytes 1048592 | tf_op jit(solution)/shard_map/all_gather | solution.py:303
  136.8 1.3 copy-done.22
  139.1 1.5 collective-permute-start.1
  140.6 2.8 %copy-done.2 = bf16[2,768,2048]{2,1,0:T(8,128)(2,1)S(1)} copy-done((bf16[2,768,2048]{2,1,0:T(8,128)(2,1)S(1)}, bf16[2,768,2048]{2,1,0:T(8,128)(2,1)}, u32[]{:S(2)}) %copy-start.2) | copy-done | bytes 6291480
  145.0 5.9 %collective-permute-done.1.refs_2_ = bf16[2,192,512]{2,1,0:T(8,128)(2,1)S(1)} collective-permute-done((bf16[2,192,512]{2,1,0:T(8,128)(2,1)}, bf16[2,192,512]{2,1,0:T(8,128)(2,1)S(1)}, u32[]{:S(2)}, u32[]{:S(2)}) %collective-permute-start.1) | collective-permute-done | bytes 393248 | tf_op jit(solution)/shard_map/ppermute | solution.py:337
  150.8 2.3 %shard_map.90 = (f32[192,2,2048]{2,1,0:T(2,128)}, f32[8,128]{1,0:T(8,128)S(1)}) custom-call(bf16[2,2,192,512]{3,2,1,0:T(8,128)(2,1)S(1)} %get-tuple-element.31.refs_2_.refs_0_, bf16[2,2,192,512]{3,2,1,0:T(8,128)(2,1)} %collective-permute-done.refs_1_, bf16[2,192,512]{2,1,0:T(8,128)(2,1)S(1)} %collective-permute-done.1.refs_2_, ...), custom_call_target="tpu_custom_call" | custom-call | flops 1 | bytes 1 | tf_op jit(solution)/shard_map/pallas_call | solution.py:33
  153.8 23.8 %all-gather.9.cloned.1.call-done = bf16[1024,512]{1,0:T(8,128)(2,1)} async-done(((bf16[128,512]{1,0:T(8,128)(2,1)}), bf16[1024,512]{1,0:T(8,128)(2,1)}) %all-gather.9.cloned.1.call-update) | async-done | bytes 1048592 | tf_op jit(solution)/shard_map/all_gather | solution.py:303
  179.9 1.5 collective-permute-start.9
  182.0 2.8 %copy-done.3 = bf16[2,768,2048]{2,1,0:T(8,128)(2,1)S(1)} copy-done((bf16[2,768,2048]{2,1,0:T(8,128)(2,1)S(1)}, bf16[2,768,2048]{2,1,0:T(8,128)(2,1)}, u32[]{:S(2)}) %copy-start.3) | copy-done | bytes 6291480
  185.9 1.5 shard_map.93
  187.6 1.5 collective-permute-start.11
  189.7 3.0 %collective-permute-done.4 = f32[2,256]{1,0:T(2,128)S(1)} collective-permute-done((f32[2,256]{1,0:T(2,128)S(1)}, f32[2,256]{1,0:T(2,128)S(1)}, u32[]{:S(2)}, u32[]{:S(2)}) %collective-permute-start.4) | collective-permute-done | bytes 2080 | tf_op jit(solution)/shard_map/ppermute | solution.py:381
  193.2 2.1 collective-permute-start.6
  195.4 1.7 collective-permute-start.7
  198.3 2.2 %collective-permute-done.8.refs_2_ = bf16[2,192,512]{2,1,0:T(8,128)(2,1)S(1)} collective-permute-done((bf16[2,192,512]{2,1,0:T(8,128)(2,1)S(1)}, bf16[2,192,512]{2,1,0:T(8,128)(2,1)S(1)}, u32[]{:S(2)}, u32[]{:S(2)}) %collective-permute-start.8) | collective-permute-done | bytes 393248 | tf_op jit(solution)/shard_map/ppermute | solution.py:337
  202.7 5.8 %collective-permute-done.11.refs_2_ = bf16[2,192,512]{2,1,0:T(8,128)(2,1)S(1)} collective-permute-done((bf16[2,192,512]{2,1,0:T(8,128)(2,1)S(1)}, bf16[2,192,512]{2,1,0:T(8,128)(2,1)S(1)}, u32[]{:S(2)}, u32[]{:S(2)}) %collective-permute-start.11) | collective-permute-done | bytes 393248 | tf_op jit(solution)/shard_map/ppermute | solution.py:337
  208.5 1.7 shard_map.98
  (90 shorter events, 23.4 us)
Async XLA Ops:
  7.2 47.4 %all-gather.11.cloned.1.call-start = ((), (), s32[]{:S(2)}) async-start(), calls=%async_computation.1 | async-start | bytes 1327104 | tf_op jit(solution)/shard_map/all_gather | solution.py:303
  9.3 86.4 %all-gather.15.cloned.1.call-start = ((), (), s32[]{:S(2)}) async-start(), calls=%async_computation.3 | async-start | bytes 1179648 | tf_op jit(solution)/shard_map/all_gather | solution.py:303
  10.0 126.7 %all-gather.13.cloned.1.call-start = ((), (), s32[]{:S(2)}) async-start(), calls=%async_computation.2 | async-start | bytes 1179648 | tf_op jit(solution)/shard_map/all_gather | solution.py:303
  10.8 166.9 %all-gather.9.cloned.1.call-start = ((), (), s32[]{:S(2)}) async-start(), calls=%async_computation | async-start | bytes 1179648 | tf_op jit(solution)/shard_map/all_gather | solution.py:303
  58.3 4.5 %collective-permute-start = (bf16[2,2,192,512]{3,2,1,0:T(8,128)(2,1)}, bf16[2,2,192,512]{3,2,1,0:T(8,128)(2,1)}, u32[]{:S(2)}, u32[]{:S(2)}) collective-permute-start(bf16[2,2,192,512]{3,2,1,0:T(8,128)(2,1)} %get-tuple-element.32), channel_id=1, source_target_pairs={{0,8},{8,0},{16,24},{24,16},{1,9},{9,1},{17,25},{25,17},{2,10},{10... | collective-permute-start | bytes 2359304 | tf_op jit(solution)/shard_map/ppermute | solution.py:323
  97.8 3.7 %collective-permute-start.2 = (bf16[2,2,192,512]{3,2,1,0:T(8,128)(2,1)S(1)}, bf16[2,2,192,512]{3,2,1,0:T(8,128)(2,1)S(1)}, u32[]{:S(2)}, u32[]{:S(2)}) collective-permute-start(bf16[2,2,192,512]{3,2,1,0:T(8,128)(2,1)S(1)} %get-tuple-element.36), channel_id=1, source_target_pairs={{0,8},{8,0},{16,24},{24,16},{1,9},{9,1},{17,25},{25,17},{2,10},{10... | collective-permute-start | bytes 2359304 | tf_op jit(solution)/shard_map/ppermute | solution.py:323
  103.6 37.0 %copy-start.18 = (bf16[2,192,512]{2,1,0:T(8,128)(2,1)}, bf16[2,192,512]{2,1,0:T(8,128)(2,1)S(1)}, u32[]{:S(2)}) copy-start(bf16[2,192,512]{2,1,0:T(8,128)(2,1)S(1)} %shard_map.85.refs_2_) | copy-start | bytes 1179652
  136.8 3.9 %copy-start.5 = (f32[2,256,768]{2,1,0:T(8,128)S(1)}, f32[2,256,768]{2,1,0:T(8,128)}, u32[]{:S(2)}) copy-start(f32[2,256,768]{2,1,0:T(8,128)} %copy-done.4) | copy-start | bytes 4718596
  139.0 5.0 %copy-start.8 = (bf16[2,2,192,512]{3,2,1,0:T(8,128)(2,1)}, bf16[2,2,192,512]{3,2,1,0:T(8,128)(2,1)S(1)}, u32[]{:S(2)}) copy-start(bf16[2,2,192,512]{3,2,1,0:T(8,128)(2,1)S(1)} %get-tuple-element.37.refs_3_.refs_0_) | copy-start | bytes 2359300
  139.0 5.0 %collective-permute-start.3 = (bf16[2,2,192,512]{3,2,1,0:T(8,128)(2,1)S(1)}, bf16[2,2,192,512]{3,2,1,0:T(8,128)(2,1)S(1)}, u32[]{:S(2)}, u32[]{:S(2)}) collective-permute-start(bf16[2,2,192,512]{3,2,1,0:T(8,128)(2,1)S(1)} %get-tuple-element.38), channel_id=1, source_target_pairs={{0,8},{8,0},{16,24},{24,16},{1,9},{9,1},{17,25},{25,17},{2,10},{10... | collective-permute-start | bytes 2359304 | tf_op jit(solution)/shard_map/ppermute | solution.py:323
  139.1 11.7 %collective-permute-start.1 = (bf16[2,192,512]{2,1,0:T(8,128)(2,1)}, bf16[2,192,512]{2,1,0:T(8,128)(2,1)S(1)}, u32[]{:S(2)}, u32[]{:S(2)}) collective-permute-start(bf16[2,192,512]{2,1,0:T(8,128)(2,1)} %shard_map.81.refs_2_), channel_id=1, source_target_pairs={{0,16},{8,24},{16,0},{24,8},{1,17},{9,25},{17,1},{25,9},{2,18},{10... | collective-permute-start | bytes 1179656 | tf_op jit(solution)/shard_map/ppermute | solution.py:337
  177.7 3.8 %copy-start.20 = (bf16[2,192,512]{2,1,0:T(8,128)(2,1)S(1)}, bf16[2,192,512]{2,1,0:T(8,128)(2,1)}, u32[]{:S(2)}) copy-start(bf16[2,192,512]{2,1,0:T(8,128)(2,1)} %copy-done.19) | copy-start | bytes 1179652
  179.8 7.6 %collective-permute-start.10 = (bf16[2,2,192,512]{3,2,1,0:T(8,128)(2,1)S(1)}, bf16[2,2,192,512]{3,2,1,0:T(8,128)(2,1)S(1)}, u32[]{:S(2)}, u32[]{:S(2)}) collective-permute-start(bf16[2,2,192,512]{3,2,1,0:T(8,128)(2,1)S(1)} %get-tuple-element.45), channel_id=1, source_target_pairs={{0,8},{8,0},{16,24},{24,16},{1,9},{9,1},{17,25},{25,17},{2,10},{10... | collective-permute-start | bytes 2359304 | tf_op jit(solution)/shard_map/ppermute | solution.py:323
  179.9 15.5 %collective-permute-start.9 = (bf16[2,192,512]{2,1,0:T(8,128)(2,1)}, bf16[2,192,512]{2,1,0:T(8,128)(2,1)S(1)}, u32[]{:S(2)}, u32[]{:S(2)}) collective-permute-start(bf16[2,192,512]{2,1,0:T(8,128)(2,1)} %copy-done.18), channel_id=1, source_target_pairs={{0,16},{8,24},{16,0},{24,8},{1,17},{9,25},{17,1},{25,9},{2,18},{10... | collective-permute-start | bytes 1179656 | tf_op jit(solution)/shard_map/ppermute | solution.py:337
  181.5 19.1 %collective-permute-start.8 = (bf16[2,192,512]{2,1,0:T(8,128)(2,1)S(1)}, bf16[2,192,512]{2,1,0:T(8,128)(2,1)S(1)}, u32[]{:S(2)}, u32[]{:S(2)}) collective-permute-start(bf16[2,192,512]{2,1,0:T(8,128)(2,1)S(1)} %copy-done.20), channel_id=1, source_target_pairs={{0,16},{8,24},{16,0},{24,8},{1,17},{9,25},{17,1},{25,9},{2,18},{10... | collective-permute-start | bytes 1179656 | tf_op jit(solution)/shard_map/ppermute | solution.py:337
  185.9 11.2 %copy-start.7 = (bf16[2,2,192,512]{3,2,1,0:T(8,128)(2,1)S(1)}, bf16[2,2,192,512]{3,2,1,0:T(8,128)(2,1)}, u32[]{:S(2)}) copy-start(bf16[2,2,192,512]{3,2,1,0:T(8,128)(2,1)} %copy-done.6) | copy-start | bytes 2359300
  185.9 11.2 %copy-start.13 = (bf16[2,2,192,512]{3,2,1,0:T(8,128)(2,1)S(1)}, bf16[2,2,192,512]{3,2,1,0:T(8,128)(2,1)}, u32[]{:S(2)}) copy-start(bf16[2,2,192,512]{3,2,1,0:T(8,128)(2,1)} %copy-done.12) | copy-start | bytes 2359300
  187.6 13.0 %copy-start.9 = (bf16[2,2,192,512]{3,2,1,0:T(8,128)(2,1)S(1)}, bf16[2,2,192,512]{3,2,1,0:T(8,128)(2,1)}, u32[]{:S(2)}) copy-start(bf16[2,2,192,512]{3,2,1,0:T(8,128)(2,1)} %copy-done.8) | copy-start | bytes 2359300
  187.6 13.0 %copy-start.15 = (bf16[2,2,192,512]{3,2,1,0:T(8,128)(2,1)S(1)}, bf16[2,2,192,512]{3,2,1,0:T(8,128)(2,1)}, u32[]{:S(2)}) copy-start(bf16[2,2,192,512]{3,2,1,0:T(8,128)(2,1)} %copy-done.14) | copy-start | bytes 2359300
  187.6 20.9 %collective-permute-start.11 = (bf16[2,192,512]{2,1,0:T(8,128)(2,1)S(1)}, bf16[2,192,512]{2,1,0:T(8,128)(2,1)S(1)}, u32[]{:S(2)}, u32[]{:S(2)}) collective-permute-start(bf16[2,192,512]{2,1,0:T(8,128)(2,1)S(1)} %shard_map.94.refs_4_), channel_id=1, source_target_pairs={{0,16},{8,24},{16,0},{24,8},{1,17},{9,25},{17,1},{25,9},{2,18},{10... | collective-permute-start | bytes 1179656 | tf_op jit(solution)/shard_map/ppermute | solution.py:337
  189.1 3.6 %collective-permute-start.4 = (f32[2,256]{1,0:T(2,128)S(1)}, f32[2,256]{1,0:T(2,128)S(1)}, u32[]{:S(2)}, u32[]{:S(2)}) collective-permute-start(f32[2,256]{1,0:T(2,128)S(1)} %get-tuple-element.43.refs_2_), channel_id=1, source_target_pairs={{0,1},{1,0},{2,3},{3,2},{4,5},{5,4},{6,7},{7,6},{8,9},{9,8},{10,11... | collective-permute-start | bytes 6152 | tf_op jit(solution)/shard_map/ppermute | solution.py:381
  192.7 9.0 %collective-permute-start.5 = (f32[2,2,256]{2,1,0:T(2,128)S(1)}, f32[2,2,256]{2,1,0:T(2,128)S(1)}, u32[]{:S(2)}, u32[]{:S(2)}) collective-permute-start(f32[2,2,256]{2,1,0:T(2,128)S(1)} %pad_maximum_fusion.refs_2_), channel_id=1, source_target_pairs={{0,2},{1,3},{2,0},{3,1},{4,6},{5,7},{6,4},{7,5},{8,10},{9,11},{10,... | collective-permute-start | bytes 12296 | tf_op jit(solution)/shard_map/ppermute | solution.py:383
  193.2 8.5 %collective-permute-start.6 = (f32[2,2,256]{2,1,0:T(2,128)S(1)}, f32[2,2,256]{2,1,0:T(2,128)S(1)}, u32[]{:S(2)}, u32[]{:S(2)}) collective-permute-start(f32[2,2,256]{2,1,0:T(2,128)S(1)} %pad_maximum_fusion.refs_2_), channel_id=1, source_target_pairs={{0,4},{1,5},{2,6},{3,7},{4,0},{5,1},{6,2},{7,3},{8,12},{9,13},{10,... | collective-permute-start | bytes 12296 | tf_op jit(solution)/shard_map/ppermute | solution.py:383
  195.4 6.3 %collective-permute-start.7 = (f32[2,2,256]{2,1,0:T(2,128)S(1)}, f32[2,2,256]{2,1,0:T(2,128)S(1)}, u32[]{:S(2)}, u32[]{:S(2)}) collective-permute-start(f32[2,2,256]{2,1,0:T(2,128)S(1)} %pad_maximum_fusion.refs_2_), channel_id=1, source_target_pairs={{0,6},{1,7},{2,4},{3,5},{4,2},{5,3},{6,0},{7,1},{8,14},{9,15},{10,... | collective-permute-start | bytes 12296 | tf_op jit(solution)/shard_map/ppermute | solution.py:383
  (19 other events, 34.9 us)
Sparse Core Ops, SparseCore 0:
  10.8 43.7 all-gather.10
  56.7 38.9 all-gather.14
  97.8 38.8 all-gather.12
  138.7 38.8 all-gather.8

commit v8 on v5

--- a/solution.py
+++ b/solution.py
@@ -157,26 +157,30 @@
                 ref[step, e] = term[step * share : (step + 1) * share]
 
 
-def pair_kernel(keep_ref, got_ref, *out_refs):
+def pair_kernel(cuts, keep_ref, got_ref, *out_refs):
+    out_refs = iter(out_refs)
     for step in range(1, keep_ref.shape[0]):
         start = 0
-        for ref in out_refs[2 * step - 2 : 2 * step]:
-            at = slice(start, start + ref.shape[1])
+        for rows in cuts:
+            at = slice(start, start + rows)
             pair = keep_ref[step, :, at].astype(F32) + got_ref[step, :, at].astype(F32)
-            ref[...] = pair.astype(BF16)
-            start += ref.shape[1]
-
-
-def last_kernel(others, start, keep_ref, got_ref, *refs):
+            next(out_refs)[...] = pair.astype(BF16)
+            start += rows
+
+
+def last_kernel(cuts, start, keep_ref, got_ref, *refs):
     out_ref, mark_ref, total_ref, sem = refs[-4:]
     mark_ref[...] = jnp.zeros(mark_ref.shape, F32)
-    cut = refs[0].shape[1]
+    others = len(cuts) * (keep_ref.shape[0] - 1)
     for e in range(keep_ref.shape[1]):
-        for part, at in enumerate((slice(0, cut), slice(cut, keep_ref.shape[2]))):
+        row = 0
+        for part, rows in enumerate(cuts):
+            at = slice(row, row + rows)
             total = keep_ref[0, e, at].astype(F32) + got_ref[0, e, at].astype(F32)
-            for ref in refs[part:others:2]:
+            for ref in refs[part : others : len(cuts)]:
                 total = total + ref[e].astype(F32)
             total_ref[at, e, :] = total
+            row += rows
     copy = pltpu.make_async_copy(
         total_ref, out_ref.at[:, :, start : start + total_ref.shape[2]], sem
     )
@@ -257,7 +261,11 @@
 
 def chunks_of(features):
     unit = features // 16
-    return [5 * unit, 5 * unit, 4 * unit, 2 * unit]
+    return [6 * unit, 8 * unit, 2 * unit]
+
+
+def cuts_of(share, c):
+    return [share // 3] * 3 if c == 0 else [share]
 
 
 sds = jax.ShapeDtypeStruct
@@ -281,6 +289,7 @@
                 pltpu.SemaphoreType.DMA((3,)),
             ],
             room=60,
+            keep=False,
         )
         self.first_other = self.send(self.first, 1)
 
@@ -363,7 +372,7 @@
         functools.partial(turn_kernel, dp),
         sds((held, 2, across, share, per_expert), BF16),
         saved,
-        *([grad_out, w_down] if direct else []),
+        *([grad_out] if direct else []),
     )
     if direct:
         arrived = [relay.chunk(c) for c in range(min(2, count))]
@@ -375,7 +384,7 @@
     def reduced(c):
         parts, width = arrived[c], widths[c]
         piece = sds((across, held, share, width), BF16)
-        after = summed[-1][2][:1] if c else ()
+        after = summed[0][2][:2] if c == 1 else ()
         keep, give = call(term_kernel, [piece, piece], turned, *parts, after=after)
         got = lax.ppermute(give, "dp", [(i, i ^ 1) for i in range(dp)])
         final = c == count - 1
@@ -393,12 +402,12 @@
             *extra,
         )
         state["raw"] = made if final else made[0]
-        cut = 16 * max(1, share // 64)
-        pieces = [sds((held, rows, width), BF16) for rows in (cut, share - cut)]
-        pairs = call(pair_kernel, pieces * (across - 1), keep, got)
+        cuts = cuts_of(share, c)
+        pieces = [sds((held, rows, width), BF16) for rows in cuts]
+        pairs = call(functools.partial(pair_kernel, cuts), pieces * (across - 1), keep, got)
         others = []
         for i, pair in enumerate(pairs):
-            step = 1 + i // 2
+            step = 1 + i // len(cuts)
             shift = [(2 * r + k, 2 * ((r + step) % across) + k) for r in range(across) for k in range(2)]
             others.append(lax.ppermute(pair, "dp", shift))
         summed.append((keep, got, others))
@@ -408,7 +417,7 @@
         before = [] if state["grad"] is None else [state["grad"]]
         count = 2 + len(others)
         state["grad"], _ = call(
-            functools.partial(last_kernel, len(others), starts[c]),
+            functools.partial(last_kernel, cuts_of(share, c), starts[c]),
             [sds((share, held, features), F32), sds((8, 128), F32)],
             keep,
             got,

time: 97.8 us -> 92.3 us (0.944)
  starting transfers between devices: 38.3 us -> 33.3 us
  waiting for transfers between devices: 36 us -> 40.5 us
  local copies, waits for them, and re-layouts: 6.31 us -> 3.14 us
  Pallas kernels: 16 us -> 14.3 us
    ppermute x14 -> x11, waiting for transfers between devices: 27.1 us -> 36.3 us  [send(): lax.ppermute(block, 'expert', [(i, i ^ mask) for i in range(LINE * SIDES)])]
    ppermute x8 -> x5, waiting for transfers between devices: 6.01 us -> 0.01 us  [reduced(): others.append(lax.ppermute(pair, 'dp', shift))]
    unnamed x20 -> x16, local copies, waits for them, and re-layouts: 6.31 us -> 3.14 us
    ppermute x8 -> x5, starting transfers between devices: 8.55 us -> 5.83 us  [reduced(): others.append(lax.ppermute(pair, 'dp', shift))]
    ppermute x1, waiting for transfers between devices: 0.57 us -> 3.05 us  [body(): both = jnp.stack([sums, lax.ppermute(sums, 'expert', swap)])]
    pallas_call x23 -> x18, Pallas kernels: 16 us -> 14.3 us  [__call__(): pl.pallas_call(body, out_shape=outs, in_specs=in_specs, compiler_params=p...]
    ppermute x3, waiting for transfers between devices: 1.22 us -> 0.01 us  [body(): lax.ppermute(both, 'expert', [(i, i ^ SIDES * d) for i in range(groups)])]
    ppermute x14 -> x11, starting transfers between devices: 23.1 us -> 22.3 us  [send(): lax.ppermute(block, 'expert', [(i, i ^ mask) for i in range(LINE * SIDES)])]
  transfers between devices with their start and end apart: 30 -> 23, of which waited for: 12 -> 10; matrix products, arithmetic and copies ran while one was open for 0% -> 0% of each run, Pallas kernels for 10% -> 10%
where the time goes in v8:
time: 92.3 us; the launch traced here: 92 us
  waiting for transfers between devices  40.5 us (44%)
  starting transfers between devices  33.3 us (36%)
  Pallas kernels  14.3 us (15%)
  local copies, waits for them, and re-layouts  3.14 us (3%)
    ppermute x11, waiting for transfers between devices, send(): lax.ppermute(block, 'expert', [(i, i ^ mask) for i in range(LINE * SIDES)])  36.3 us
    ppermute x11, starting transfers between devices, send(): lax.ppermute(block, 'expert', [(i, i ^ mask) for i in range(LINE * SIDES)])  22.3 us
    pallas_call x18, Pallas kernels, __call__(): pl.pallas_call(body, out_shape=outs, in_specs=in_specs, compiler_params=p...  14.3 us
    ppermute x5, starting transfers between devices, reduced(): others.append(lax.ppermute(pair, 'dp', shift))  5.83 us
    ppermute x3, starting transfers between devices, body(): lax.ppermute(both, 'expert', [(i, i ^ SIDES * d) for i in range(groups)])  4.39 us
    unnamed x16, local copies, waits for them, and re-layouts  3.14 us
    ppermute x1, waiting for transfers between devices, body(): both = jnp.stack([sums, lax.ppermute(sums, 'expert', swap)])  3.05 us
  transfers between devices with their start and end apart: 23, of which 10 were waited for; matrix products, arithmetic and copies ran while one was open for 0% of the time, Pallas kernels for 10%

profile of v8, /device:TPU:0, one launch (start us, length us, event | category | flops | bytes accessed | tf_op | source)
XLA Modules:
  0.0 92.0 jit_solution(17612418785336000393)
XLA Ops:
  0.6 1.8 %shard_map.76 = (s32[2,128]{1,0:T(2,128)}, bf16[144,768]{1,0:T(8,128)(2,1)}) custom-call(s32[2,128]{1,0:T(2,128)} %bitcast.13, f32[2,128]{1,0:T(2,128)} %bitcast.10, bf16[128,2048]{1,0:T(8,128)(2,1)} %refs_0_.9), custom_call_target="tpu_custom_call" | custom-call | flops 1 | bytes 1 | tf_op jit(solution)/shard_map/pallas_call | solution.py:34
  2.5 3.0 %collective-permute-start = (bf16[144,768]{1,0:T(8,128)(2,1)}, bf16[144,768]{1,0:T(8,128)(2,1)S(1)}, u32[]{:S(2)}, u32[]{:S(2)}) collective-permute-start(bf16[144,768]{1,0:T(8,128)(2,1)} %get-tuple-element.35.refs_0_), channel_id=1, source_target_pairs={{0,1},{1,0},{2,3},{3,2},{4,5},{5,4},{6,7},{7,6},{8,9},{9,8},{10,11... | collective-permute-start | bytes 663560 | tf_op jit(solution)/shard_map/ppermute | solution.py:297
  7.9 3.2 %collective-permute-done.refs_1_ = bf16[144,768]{1,0:T(8,128)(2,1)S(1)} collective-permute-done((bf16[144,768]{1,0:T(8,128)(2,1)}, bf16[144,768]{1,0:T(8,128)(2,1)S(1)}, u32[]{:S(2)}, u32[]{:S(2)}) %collective-permute-start) | collective-permute-done | bytes 221216 | tf_op jit(solution)/shard_map/ppermute | solution.py:297
  12.4 1.8 %collective-permute-start.1 = (bf16[128,1280]{1,0:T(8,128)(2,1)S(1)}, bf16[128,1280]{1,0:T(8,128)(2,1)S(1)}, u32[]{:S(2)}, u32[]{:S(2)}) collective-permute-start(bf16[128,1280]{1,0:T(8,128)(2,1)S(1)} %get-tuple-element.36), channel_id=1, source_target_pairs={{0,1},{1,0},{2,3},{3,2},{4,5},{5,4},{6,7},{7,6},{8,9},{9,8},{10,11... | collective-permute-start | bytes 983048 | tf_op jit(solution)/shard_map/ppermute | solution.py:297
  14.2 1.6 %collective-permute-start.2 = (bf16[2,64,768]{2,1,0:T(8,128)(2,1)S(1)}, bf16[2,64,768]{2,1,0:T(8,128)(2,1)S(1)}, u32[]{:S(2)}, u32[]{:S(2)}) collective-permute-start(bf16[2,64,768]{2,1,0:T(8,128)(2,1)S(1)} %get-tuple-element.39), channel_id=1, source_target_pairs={{0,2},{1,3},{2,0},{3,1},{4,6},{5,7},{6,4},{7,5},{8,10},{9,11},{10,... | collective-permute-start | bytes 589832 | tf_op jit(solution)/shard_map/ppermute | solution.py:297
  15.8 2.6 %collective-permute-start.3 = (bf16[2,64,768]{2,1,0:T(8,128)(2,1)S(1)}, bf16[2,64,768]{2,1,0:T(8,128)(2,1)S(1)}, u32[]{:S(2)}, u32[]{:S(2)}) collective-permute-start(bf16[2,64,768]{2,1,0:T(8,128)(2,1)S(1)} %get-tuple-element.40), channel_id=1, source_target_pairs={{0,4},{1,5},{2,6},{3,7},{4,0},{5,1},{6,2},{7,3},{8,12},{9,13},{10,... | collective-permute-start | bytes 589832 | tf_op jit(solution)/shard_map/ppermute | solution.py:297
  18.6 2.8 %collective-permute-done.1.refs_1_ = bf16[128,1280]{1,0:T(8,128)(2,1)S(1)} collective-permute-done((bf16[128,1280]{1,0:T(8,128)(2,1)S(1)}, bf16[128,1280]{1,0:T(8,128)(2,1)S(1)}, u32[]{:S(2)}, u32[]{:S(2)}) %collective-permute-start.1) | collective-permute-done | bytes 327712 | tf_op jit(solution)/shard_map/ppermute | solution.py:297
  22.4 10.1 %collective-permute-done.3.refs_3_ = bf16[2,64,768]{2,1,0:T(8,128)(2,1)S(1)} collective-permute-done((bf16[2,64,768]{2,1,0:T(8,128)(2,1)S(1)}, bf16[2,64,768]{2,1,0:T(8,128)(2,1)S(1)}, u32[]{:S(2)}, u32[]{:S(2)}) %collective-permute-start.3) | collective-permute-done | bytes 196640 | tf_op jit(solution)/shard_map/ppermute | solution.py:297
  33.4 2.7 %collective-permute-start.9 = (bf16[2,64,1024]{2,1,0:T(8,128)(2,1)S(1)}, bf16[2,64,1024]{2,1,0:T(8,128)(2,1)S(1)}, u32[]{:S(2)}, u32[]{:S(2)}) collective-permute-start(bf16[2,64,1024]{2,1,0:T(8,128)(2,1)S(1)} %get-tuple-element.50), channel_id=1, source_target_pairs={{0,2},{1,3},{2,0},{3,1},{4,6},{5,7},{6,4},{7,5},{8,10},{9,11},{10,... | collective-permute-start | bytes 786440 | tf_op jit(solution)/shard_map/ppermute | solution.py:297
  37.2 1.4 %collective-permute-start.11 = (bf16[2,64,1024]{2,1,0:T(8,128)(2,1)S(1)}, bf16[2,64,1024]{2,1,0:T(8,128)(2,1)S(1)}, u32[]{:S(2)}, u32[]{:S(2)}) collective-permute-start(bf16[2,64,1024]{2,1,0:T(8,128)(2,1)S(1)} %get-tuple-element.52), channel_id=1, source_target_pairs={{0,6},{1,7},{2,4},{3,5},{4,2},{5,3},{6,0},{7,1},{8,14},{9,15},{10,... | collective-permute-start | bytes 786440 | tf_op jit(solution)/shard_map/ppermute | solution.py:297
  39.6 1.6 %collective-permute-start.13 = (bf16[2,64,768]{2,1,0:T(8,128)(2,1)S(1)}, bf16[2,64,768]{2,1,0:T(8,128)(2,1)S(1)}, u32[]{:S(2)}, u32[]{:S(2)}) collective-permute-start(bf16[2,64,768]{2,1,0:T(8,128)(2,1)S(1)} %get-tuple-element.53), channel_id=1, source_target_pairs={{0,16},{8,24},{16,0},{24,8},{1,17},{9,25},{17,1},{25,9},{2,18},{10... | collective-permute-start | bytes 589832 | tf_op jit(solution)/shard_map/ppermute | solution.py:412
  41.9 6.3 %collective-permute-done.9.refs_2_ = bf16[2,64,1024]{2,1,0:T(8,128)(2,1)S(1)} collective-permute-done((bf16[2,64,1024]{2,1,0:T(8,128)(2,1)S(1)}, bf16[2,64,1024]{2,1,0:T(8,128)(2,1)S(1)}, u32[]{:S(2)}, u32[]{:S(2)}) %collective-permute-start.9) | collective-permute-done | bytes 262176 | tf_op jit(solution)/shard_map/ppermute | solution.py:297
  48.2 9.3 %collective-permute-done.10.refs_3_ = bf16[2,64,1024]{2,1,0:T(8,128)(2,1)S(1)} collective-permute-done((bf16[2,64,1024]{2,1,0:T(8,128)(2,1)S(1)}, bf16[2,64,1024]{2,1,0:T(8,128)(2,1)S(1)}, u32[]{:S(2)}, u32[]{:S(2)}) %collective-permute-start.10) | collective-permute-done | bytes 262176 | tf_op jit(solution)/shard_map/ppermute | solution.py:297
  58.5 1.6 %collective-permute-start.14 = (bf16[2,64,768]{2,1,0:T(8,128)(2,1)S(1)}, bf16[2,64,768]{2,1,0:T(8,128)(2,1)S(1)}, u32[]{:S(2)}, u32[]{:S(2)}) collective-permute-start(bf16[2,64,768]{2,1,0:T(8,128)(2,1)S(1)} %get-tuple-element.55), channel_id=1, source_target_pairs={{0,16},{8,24},{16,0},{24,8},{1,17},{9,25},{17,1},{25,9},{2,18},{10... | collective-permute-start | bytes 589832 | tf_op jit(solution)/shard_map/ppermute | solution.py:412
  62.1 1.6 %collective-permute-start.20 = (bf16[2,192,1024]{2,1,0:T(8,128)(2,1)S(1)}, bf16[2,192,1024]{2,1,0:T(8,128)(2,1)S(1)}, u32[]{:S(2)}, u32[]{:S(2)}) collective-permute-start(bf16[2,192,1024]{2,1,0:T(8,128)(2,1)S(1)} %shard_map.86.refs_5_), channel_id=1, source_target_pairs={{0,16},{8,24},{16,0},{24,8},{1,17},{9,25},{17,1},{25,9},{2,18},{10... | collective-permute-start | bytes 2359304 | tf_op jit(solution)/shard_map/ppermute | solution.py:412
  63.7 5.4 %collective-permute-start.6 = (bf16[2,64,256]{2,1,0:T(8,128)(2,1)S(1)}, bf16[2,64,256]{2,1,0:T(8,128)(2,1)S(1)}, u32[]{:S(2)}, u32[]{:S(2)}) collective-permute-start(bf16[2,64,256]{2,1,0:T(8,128)(2,1)S(1)} %get-tuple-element.47), channel_id=1, source_target_pairs={{0,2},{1,3},{2,0},{3,1},{4,6},{5,7},{6,4},{7,5},{8,10},{9,11},{10,... | collective-permute-start | bytes 196616 | tf_op jit(solution)/shard_map/ppermute | solution.py:297
  70.1 1.5 %collective-permute-start.8 = (bf16[2,64,256]{2,1,0:T(8,128)(2,1)S(1)}, bf16[2,64,256]{2,1,0:T(8,128)(2,1)S(1)}, u32[]{:S(2)}, u32[]{:S(2)}) collective-permute-start(bf16[2,64,256]{2,1,0:T(8,128)(2,1)S(1)} %get-tuple-element.49), channel_id=1, source_target_pairs={{0,6},{1,7},{2,4},{3,5},{4,2},{5,3},{6,0},{7,1},{8,14},{9,15},{10,... | collective-permute-start | bytes 196616 | tf_op jit(solution)/shard_map/ppermute | solution.py:297
  71.6 1.4 %shard_map.87 = (f32[192,2,2048]{2,1,0:T(2,128)}, f32[8,128]{1,0:T(8,128)S(1)}) custom-call(bf16[2,2,192,768]{3,2,1,0:T(8,128)(2,1)S(1)} %get-tuple-element.43.refs_5_.refs_0_, bf16[2,2,192,768]{3,2,1,0:T(8,128)(2,1)S(1)} %collective-permute-done.5.refs_1_, bf16[2,64,768]{2,1,0:T(8,128)(2,1)S(1)} %collective-permute-done.12.refs_6_.refs_2_, ...), custom_call_target="tpu_custom_call" | custom-call | flops 1 | bytes 1 | tf_op jit(solution)/shard_map/pallas_call | solution.py:34
  73.0 4.1 %collective-permute-done.7.refs_3_ = bf16[2,64,256]{2,1,0:T(8,128)(2,1)S(1)} collective-permute-done((bf16[2,64,256]{2,1,0:T(8,128)(2,1)S(1)}, bf16[2,64,256]{2,1,0:T(8,128)(2,1)S(1)}, u32[]{:S(2)}, u32[]{:S(2)}) %collective-permute-start.7) | collective-permute-done | bytes 65568 | tf_op jit(solution)/shard_map/ppermute | solution.py:297
  80.4 3.0 %collective-permute-done.16 = f32[2,256]{1,0:T(2,128)S(1)} collective-permute-done((f32[2,256]{1,0:T(2,128)S(1)}, f32[2,256]{1,0:T(2,128)S(1)}, u32[]{:S(2)}, u32[]{:S(2)}) %collective-permute-start.16) | collective-permute-done | bytes 2080 | tf_op jit(solution)/shard_map/ppermute | solution.py:445
  83.5 2.3 %collective-permute-start.19 = (f32[2,2,256]{2,1,0:T(2,128)S(1)}, f32[2,2,256]{2,1,0:T(2,128)S(1)}, u32[]{:S(2)}, u32[]{:S(2)}) collective-permute-start(f32[2,2,256]{2,1,0:T(2,128)S(1)} %pad_maximum_fusion.refs_2_), channel_id=1, source_target_pairs={{0,6},{1,7},{2,4},{3,5},{4,2},{5,3},{6,0},{7,1},{8,14},{9,15},{10,... | collective-permute-start | bytes 12296 | tf_op jit(solution)/shard_map/ppermute | solution.py:447
  86.2 1.7 %collective-permute-start.17 = (f32[2,2,256]{2,1,0:T(2,128)S(1)}, f32[2,2,256]{2,1,0:T(2,128)S(1)}, u32[]{:S(2)}, u32[]{:S(2)}) collective-permute-start(f32[2,2,256]{2,1,0:T(2,128)S(1)} %pad_maximum_fusion.refs_2_), channel_id=1, source_target_pairs={{0,2},{1,3},{2,0},{3,1},{4,6},{5,7},{6,4},{7,5},{8,10},{9,11},{10,... | collective-permute-start | bytes 12296 | tf_op jit(solution)/shard_map/ppermute | solution.py:447
  87.9 1.7 %shard_map.91 = (f32[192,2,2048]{2,1,0:T(2,128)}, f32[8,128]{1,0:T(8,128)S(1)}) custom-call(bf16[2,2,192,1024]{3,2,1,0:T(8,128)(2,1)S(1)} %get-tuple-element.54.refs_6_.refs_0_, bf16[2,2,192,1024]{3,2,1,0:T(8,128)(2,1)S(1)} %collective-permute-done.15.refs_1_, ...), custom_call_target="tpu_custom_call", output_to_operand_aliasing={{0}: (3, {})} | custom-call | flops 1 | bytes 1 | tf_op jit(solution)/shard_map/pallas_call | solution.py:34
  89.6 1.5 %shard_map.93 = (f32[192,2,2048]{2,1,0:T(2,128)}, f32[8,128]{1,0:T(8,128)}) custom-call(bf16[2,2,192,256]{3,2,1,0:T(8,128)(2,1)S(1)} %get-tuple-element.58.refs_7_.refs_0_, bf16[2,2,192,256]{3,2,1,0:T(8,128)(2,1)S(1)} %collective-permute-done.21.refs_1_, bf16[2,192,256]{2,1,0:T(8,128)(2,1)S(1)} %collective-permute-done.22.refs_2_, ...), custom_call_target="tpu_custom_call", output_to_operand_aliasing={{0}: (3, {})} | custom-call | flops 1 | bytes 1 | tf_op jit(solution)/shard_map/pallas_call | solution.py:34
  (57 shorter events, 17.4 us)
Async XLA Ops:
  2.5 8.6 %collective-permute-start = (bf16[144,768]{1,0:T(8,128)(2,1)}, bf16[144,768]{1,0:T(8,128)(2,1)S(1)}, u32[]{:S(2)}, u32[]{:S(2)}) collective-permute-start(bf16[144,768]{1,0:T(8,128)(2,1)} %get-tuple-element.35.refs_0_), channel_id=1, source_target_pairs={{0,1},{1,0},{2,3},{3,2},{4,5},{5,4},{6,7},{7,6},{8,9},{9,8},{10,11... | collective-permute-start | bytes 663560 | tf_op jit(solution)/shard_map/ppermute | solution.py:297
  7.6 31.0 %copy-start = (bf16[2,768,2048]{2,1,0:T(8,128)(2,1)S(1)}, bf16[2,768,2048]{2,1,0:T(8,128)(2,1)}, u32[]{:S(2)}) copy-start(bf16[2,768,2048]{2,1,0:T(8,128)(2,1)} %refs_0_.11) | copy-start | bytes 18874372
  12.4 9.0 %collective-permute-start.1 = (bf16[128,1280]{1,0:T(8,128)(2,1)S(1)}, bf16[128,1280]{1,0:T(8,128)(2,1)S(1)}, u32[]{:S(2)}, u32[]{:S(2)}) collective-permute-start(bf16[128,1280]{1,0:T(8,128)(2,1)S(1)} %get-tuple-element.36), channel_id=1, source_target_pairs={{0,1},{1,0},{2,3},{3,2},{4,5},{5,4},{6,7},{7,6},{8,9},{9,8},{10,11... | collective-permute-start | bytes 983048 | tf_op jit(solution)/shard_map/ppermute | solution.py:297
  14.2 8.2 %collective-permute-start.2 = (bf16[2,64,768]{2,1,0:T(8,128)(2,1)S(1)}, bf16[2,64,768]{2,1,0:T(8,128)(2,1)S(1)}, u32[]{:S(2)}, u32[]{:S(2)}) collective-permute-start(bf16[2,64,768]{2,1,0:T(8,128)(2,1)S(1)} %get-tuple-element.39), channel_id=1, source_target_pairs={{0,2},{1,3},{2,0},{3,1},{4,6},{5,7},{6,4},{7,5},{8,10},{9,11},{10,... | collective-permute-start | bytes 589832 | tf_op jit(solution)/shard_map/ppermute | solution.py:297
  15.8 16.7 %collective-permute-start.3 = (bf16[2,64,768]{2,1,0:T(8,128)(2,1)S(1)}, bf16[2,64,768]{2,1,0:T(8,128)(2,1)S(1)}, u32[]{:S(2)}, u32[]{:S(2)}) collective-permute-start(bf16[2,64,768]{2,1,0:T(8,128)(2,1)S(1)} %get-tuple-element.40), channel_id=1, source_target_pairs={{0,4},{1,5},{2,6},{3,7},{4,0},{5,1},{6,2},{7,3},{8,12},{9,13},{10,... | collective-permute-start | bytes 589832 | tf_op jit(solution)/shard_map/ppermute | solution.py:297
  18.4 14.1 %collective-permute-start.4 = (bf16[2,64,768]{2,1,0:T(8,128)(2,1)S(1)}, bf16[2,64,768]{2,1,0:T(8,128)(2,1)S(1)}, u32[]{:S(2)}, u32[]{:S(2)}) collective-permute-start(bf16[2,64,768]{2,1,0:T(8,128)(2,1)S(1)} %get-tuple-element.41), channel_id=1, source_target_pairs={{0,6},{1,7},{2,4},{3,5},{4,2},{5,3},{6,0},{7,1},{8,14},{9,15},{10,... | collective-permute-start | bytes 589832 | tf_op jit(solution)/shard_map/ppermute | solution.py:297
  33.3 6.1 %collective-permute-start.5 = (bf16[2,2,192,768]{3,2,1,0:T(8,128)(2,1)S(1)}, bf16[2,2,192,768]{3,2,1,0:T(8,128)(2,1)S(1)}, u32[]{:S(2)}, u32[]{:S(2)}) collective-permute-start(bf16[2,2,192,768]{3,2,1,0:T(8,128)(2,1)S(1)} %get-tuple-element.44), channel_id=1, source_target_pairs={{0,8},{8,0},{16,24},{24,16},{1,9},{9,1},{17,25},{25,17},{2,10},{10... | collective-permute-start | bytes 3538952 | tf_op jit(solution)/shard_map/ppermute | solution.py:389
  33.4 14.8 %collective-permute-start.9 = (bf16[2,64,1024]{2,1,0:T(8,128)(2,1)S(1)}, bf16[2,64,1024]{2,1,0:T(8,128)(2,1)S(1)}, u32[]{:S(2)}, u32[]{:S(2)}) collective-permute-start(bf16[2,64,1024]{2,1,0:T(8,128)(2,1)S(1)} %get-tuple-element.50), channel_id=1, source_target_pairs={{0,2},{1,3},{2,0},{3,1},{4,6},{5,7},{6,4},{7,5},{8,10},{9,11},{10,... | collective-permute-start | bytes 786440 | tf_op jit(solution)/shard_map/ppermute | solution.py:297
  36.1 21.3 %collective-permute-start.10 = (bf16[2,64,1024]{2,1,0:T(8,128)(2,1)S(1)}, bf16[2,64,1024]{2,1,0:T(8,128)(2,1)S(1)}, u32[]{:S(2)}, u32[]{:S(2)}) collective-permute-start(bf16[2,64,1024]{2,1,0:T(8,128)(2,1)S(1)} %get-tuple-element.51), channel_id=1, source_target_pairs={{0,4},{1,5},{2,6},{3,7},{4,0},{5,1},{6,2},{7,3},{8,12},{9,13},{10,... | collective-permute-start | bytes 786440 | tf_op jit(solution)/shard_map/ppermute | solution.py:297
  37.2 20.2 %collective-permute-start.11 = (bf16[2,64,1024]{2,1,0:T(8,128)(2,1)S(1)}, bf16[2,64,1024]{2,1,0:T(8,128)(2,1)S(1)}, u32[]{:S(2)}, u32[]{:S(2)}) collective-permute-start(bf16[2,64,1024]{2,1,0:T(8,128)(2,1)S(1)} %get-tuple-element.52), channel_id=1, source_target_pairs={{0,6},{1,7},{2,4},{3,5},{4,2},{5,3},{6,0},{7,1},{8,14},{9,15},{10,... | collective-permute-start | bytes 786440 | tf_op jit(solution)/shard_map/ppermute | solution.py:297
  39.6 17.9 %collective-permute-start.13 = (bf16[2,64,768]{2,1,0:T(8,128)(2,1)S(1)}, bf16[2,64,768]{2,1,0:T(8,128)(2,1)S(1)}, u32[]{:S(2)}, u32[]{:S(2)}) collective-permute-start(bf16[2,64,768]{2,1,0:T(8,128)(2,1)S(1)} %get-tuple-element.53), channel_id=1, source_target_pairs={{0,16},{8,24},{16,0},{24,8},{1,17},{9,25},{17,1},{25,9},{2,18},{10... | collective-permute-start | bytes 589832 | tf_op jit(solution)/shard_map/ppermute | solution.py:412
  41.2 16.3 %collective-permute-start.12 = (bf16[2,64,768]{2,1,0:T(8,128)(2,1)S(1)}, bf16[2,64,768]{2,1,0:T(8,128)(2,1)S(1)}, u32[]{:S(2)}, u32[]{:S(2)}) collective-permute-start(bf16[2,64,768]{2,1,0:T(8,128)(2,1)S(1)} %get-tuple-element.45.refs_3_), channel_id=1, source_target_pairs={{0,16},{8,24},{16,0},{24,8},{1,17},{9,25},{17,1},{25,9},{2,18},{10... | collective-permute-start | bytes 589832 | tf_op jit(solution)/shard_map/ppermute | solution.py:412
  58.4 3.5 %collective-permute-start.15 = (bf16[2,2,192,1024]{3,2,1,0:T(8,128)(2,1)S(1)}, bf16[2,2,192,1024]{3,2,1,0:T(8,128)(2,1)S(1)}, u32[]{:S(2)}, u32[]{:S(2)}) collective-permute-start(bf16[2,2,192,1024]{3,2,1,0:T(8,128)(2,1)S(1)} %get-tuple-element.56), channel_id=1, source_target_pairs={{0,8},{8,0},{16,24},{24,16},{1,9},{9,1},{17,25},{25,17},{2,10},{10... | collective-permute-start | bytes 4718600 | tf_op jit(solution)/shard_map/ppermute | solution.py:389
  58.5 13.1 %collective-permute-start.14 = (bf16[2,64,768]{2,1,0:T(8,128)(2,1)S(1)}, bf16[2,64,768]{2,1,0:T(8,128)(2,1)S(1)}, u32[]{:S(2)}, u32[]{:S(2)}) collective-permute-start(bf16[2,64,768]{2,1,0:T(8,128)(2,1)S(1)} %get-tuple-element.55), channel_id=1, source_target_pairs={{0,16},{8,24},{16,0},{24,8},{1,17},{9,25},{17,1},{25,9},{2,18},{10... | collective-permute-start | bytes 589832 | tf_op jit(solution)/shard_map/ppermute | solution.py:412
  62.1 25.8 %collective-permute-start.20 = (bf16[2,192,1024]{2,1,0:T(8,128)(2,1)S(1)}, bf16[2,192,1024]{2,1,0:T(8,128)(2,1)S(1)}, u32[]{:S(2)}, u32[]{:S(2)}) collective-permute-start(bf16[2,192,1024]{2,1,0:T(8,128)(2,1)S(1)} %shard_map.86.refs_5_), channel_id=1, source_target_pairs={{0,16},{8,24},{16,0},{24,8},{1,17},{9,25},{17,1},{25,9},{2,18},{10... | collective-permute-start | bytes 2359304 | tf_op jit(solution)/shard_map/ppermute | solution.py:412
  63.7 9.3 %collective-permute-start.6 = (bf16[2,64,256]{2,1,0:T(8,128)(2,1)S(1)}, bf16[2,64,256]{2,1,0:T(8,128)(2,1)S(1)}, u32[]{:S(2)}, u32[]{:S(2)}) collective-permute-start(bf16[2,64,256]{2,1,0:T(8,128)(2,1)S(1)} %get-tuple-element.47), channel_id=1, source_target_pairs={{0,2},{1,3},{2,0},{3,1},{4,6},{5,7},{6,4},{7,5},{8,10},{9,11},{10,... | collective-permute-start | bytes 196616 | tf_op jit(solution)/shard_map/ppermute | solution.py:297
  69.1 8.0 %collective-permute-start.7 = (bf16[2,64,256]{2,1,0:T(8,128)(2,1)S(1)}, bf16[2,64,256]{2,1,0:T(8,128)(2,1)S(1)}, u32[]{:S(2)}, u32[]{:S(2)}) collective-permute-start(bf16[2,64,256]{2,1,0:T(8,128)(2,1)S(1)} %get-tuple-element.48), channel_id=1, source_target_pairs={{0,4},{1,5},{2,6},{3,7},{4,0},{5,1},{6,2},{7,3},{8,12},{9,13},{10,... | collective-permute-start | bytes 196616 | tf_op jit(solution)/shard_map/ppermute | solution.py:297
  70.1 7.0 %collective-permute-start.8 = (bf16[2,64,256]{2,1,0:T(8,128)(2,1)S(1)}, bf16[2,64,256]{2,1,0:T(8,128)(2,1)S(1)}, u32[]{:S(2)}, u32[]{:S(2)}) collective-permute-start(bf16[2,64,256]{2,1,0:T(8,128)(2,1)S(1)} %get-tuple-element.49), channel_id=1, source_target_pairs={{0,6},{1,7},{2,4},{3,5},{4,2},{5,3},{6,0},{7,1},{8,14},{9,15},{10,... | collective-permute-start | bytes 196616 | tf_op jit(solution)/shard_map/ppermute | solution.py:297
  77.5 1.8 %collective-permute-start.21 = (bf16[2,2,192,256]{3,2,1,0:T(8,128)(2,1)S(1)}, bf16[2,2,192,256]{3,2,1,0:T(8,128)(2,1)S(1)}, u32[]{:S(2)}, u32[]{:S(2)}) collective-permute-start(bf16[2,2,192,256]{3,2,1,0:T(8,128)(2,1)S(1)} %get-tuple-element.63), channel_id=1, source_target_pairs={{0,8},{8,0},{16,24},{24,16},{1,9},{9,1},{17,25},{25,17},{2,10},{10... | collective-permute-start | bytes 1179656 | tf_op jit(solution)/shard_map/ppermute | solution.py:389
  79.3 10.2 %collective-permute-start.22 = (bf16[2,192,256]{2,1,0:T(8,128)(2,1)S(1)}, bf16[2,192,256]{2,1,0:T(8,128)(2,1)S(1)}, u32[]{:S(2)}, u32[]{:S(2)}) collective-permute-start(bf16[2,192,256]{2,1,0:T(8,128)(2,1)S(1)} %shard_map.90.refs_4_), channel_id=1, source_target_pairs={{0,16},{8,24},{16,0},{24,8},{1,17},{9,25},{17,1},{25,9},{2,18},{10... | collective-permute-start | bytes 589832 | tf_op jit(solution)/shard_map/ppermute | solution.py:412
  79.9 3.6 %collective-permute-start.16 = (f32[2,256]{1,0:T(2,128)S(1)}, f32[2,256]{1,0:T(2,128)S(1)}, u32[]{:S(2)}, u32[]{:S(2)}) collective-permute-start(f32[2,256]{1,0:T(2,128)S(1)} %get-tuple-element.61.refs_2_), channel_id=1, source_target_pairs={{0,1},{1,0},{2,3},{3,2},{4,5},{5,4},{6,7},{7,6},{8,9},{9,8},{10,11... | collective-permute-start | bytes 6152 | tf_op jit(solution)/shard_map/ppermute | solution.py:445
  83.5 7.6 %collective-permute-start.19 = (f32[2,2,256]{2,1,0:T(2,128)S(1)}, f32[2,2,256]{2,1,0:T(2,128)S(1)}, u32[]{:S(2)}, u32[]{:S(2)}) collective-permute-start(f32[2,2,256]{2,1,0:T(2,128)S(1)} %pad_maximum_fusion.refs_2_), channel_id=1, source_target_pairs={{0,6},{1,7},{2,4},{3,5},{4,2},{5,3},{6,0},{7,1},{8,14},{9,15},{10,... | collective-permute-start | bytes 12296 | tf_op jit(solution)/shard_map/ppermute | solution.py:447
  85.7 5.3 %collective-permute-start.18 = (f32[2,2,256]{2,1,0:T(2,128)S(1)}, f32[2,2,256]{2,1,0:T(2,128)S(1)}, u32[]{:S(2)}, u32[]{:S(2)}) collective-permute-start(f32[2,2,256]{2,1,0:T(2,128)S(1)} %pad_maximum_fusion.refs_2_), channel_id=1, source_target_pairs={{0,4},{1,5},{2,6},{3,7},{4,0},{5,1},{6,2},{7,3},{8,12},{9,13},{10,... | collective-permute-start | bytes 12296 | tf_op jit(solution)/shard_map/ppermute | solution.py:447
  86.2 4.9 %collective-permute-start.17 = (f32[2,2,256]{2,1,0:T(2,128)S(1)}, f32[2,2,256]{2,1,0:T(2,128)S(1)}, u32[]{:S(2)}, u32[]{:S(2)}) collective-permute-start(f32[2,2,256]{2,1,0:T(2,128)S(1)} %pad_maximum_fusion.refs_2_), channel_id=1, source_target_pairs={{0,2},{1,3},{2,0},{3,1},{4,6},{5,7},{6,4},{7,5},{8,10},{9,11},{10,... | collective-permute-start | bytes 12296 | tf_op jit(solution)/shard_map/ppermute | solution.py:447
  (7 other events, 16.0 us)

commit v9 on v8

--- a/solution.py
+++ b/solution.py
@@ -14,6 +14,14 @@
 
 LINE, SIDES = 4, 2
 INFO = 16
+
+
+def target_of(me, part):
+    return (me // SIDES + part // SIDES) % LINE * SIDES + (me % SIDES ^ part % SIDES)
+
+
+def source_of(me, part):
+    return (me // SIDES + LINE - part // SIDES) % LINE * SIDES + (me % SIDES ^ part % SIDES)
 
 
 class Chain:
@@ -100,7 +108,7 @@
             flat = (info[:chosen] * capacity + info[chosen : 2 * chosen]).astype(I32)
             word = info[2 * chosen : 3 * chosen]
             for d in range(LINE):
-                slot = local + (me ^ (SIDES * d)) * rows
+                slot = local + target_of(me, SIDES * d) * rows
                 hits = [
                     jnp.where(flat[k : k + 1] == slot, word[k : k + 1], 0.0) for k in range(chosen)
                 ]
@@ -133,7 +141,8 @@
     mine = lax.axis_index("dp")
     core, row = mine % 2, mine // 2
     for e in range(held):
-        stacked = jnp.concatenate([hidden_ref[me ^ mask, e] for mask in range(parts)], axis=0)
+        sources = [source_of(me, p) if parts > 1 else 0 for p in range(parts)]
+        stacked = jnp.concatenate([hidden_ref[source, e] for source in sources], axis=0)
         turned = stacked.T
         for piece in range(dp):
             other = (piece % 2) ^ core
@@ -209,10 +218,11 @@
         sources, _, own, units = hidden_ref.shape
         me = lax.axis_index("expert") if sources > 1 else 0
         folds = []
-        for mask in range(sources):
-            block = raw[mask * own : (mask + 1) * own]
-            grad_ref[me ^ mask, e] = block.astype(BF16)
-            product = block * hidden_ref[me ^ mask, e].astype(F32)
+        for part in range(sources):
+            source = source_of(me, part) if sources > 1 else 0
+            block = raw[part * own : (part + 1) * own]
+            grad_ref[source, e] = block.astype(BF16)
+            product = block * hidden_ref[source, e].astype(F32)
             folds.append(
                 functools.reduce(jnp.add, [product[:, i : i + 128] for i in range(0, units, 128)])
             )
@@ -225,10 +235,10 @@
     chosen, tokens = flat_ref.shape
     if direct:
         values = []
-        for mask in range(LINE * SIDES):
-            at = mask * capacity
-            ref = refs[mask // SIDES]
-            values += [ref[mask % SIDES, e : e + 1, at : at + capacity] for e in range(ref.shape[1])]
+        for part in range(LINE * SIDES):
+            at = part * capacity
+            ref = refs[part // SIDES]
+            values += [ref[part % SIDES, e : e + 1, at : at + capacity] for e in range(ref.shape[1])]
         lanes = 128 // capacity
         values = jnp.concatenate(
             [
@@ -249,7 +259,7 @@
     picked = [jnp.zeros((1, tokens), F32) for _ in range(chosen)]
     for line in range(lines):
         at = lax.broadcasted_iota(I32, (128, tokens), 0) + line * 128
-        slot = (at // group ^ me) * group + at % group
+        slot = (target_of(me, at // group) if direct else at // group) * group + at % group
         for k in range(chosen):
             hit = jnp.where(flat_ref[k : k + 1, :] == slot, columns[:, line : line + 1], 0.0)
             picked[k] += jnp.sum(hit, axis=0, keepdims=True)
@@ -291,10 +301,14 @@
             room=60,
             keep=False,
         )
-        self.first_other = self.send(self.first, 1)
-
-    def send(self, block, mask):
-        return lax.ppermute(block, "expert", [(i, i ^ mask) for i in range(LINE * SIDES)])
+        self.first_other = self.swap(self.first)
+
+    def swap(self, block):
+        return lax.ppermute(block, "expert", [(i, i ^ 1) for i in range(LINE * SIDES)])
+
+    def send(self, block, d):
+        pairs = [(i, target_of(i, SIDES * d)) for i in range(LINE * SIDES)]
+        return lax.ppermute(block, "expert", pairs)
 
     def chunk(self, c):
         held, capacity, tokens = self.held, self.capacity, self.rows.shape[0]
@@ -317,9 +331,9 @@
             sent = self.call(kernel, rows, self.rows, self.rest_other, self.place)
         got = [sent[0]] + [None] * (LINE - 1)
         for d in range(LINE - 1, 0, -1):
-            got[d] = self.send(sent[d], SIDES * d)
+            got[d] = self.send(sent[d], d)
         if c == 0:
-            self.rest_other = self.send(rest, 1)
+            self.rest_other = self.swap(rest)
         return got
 
 
@@ -444,7 +458,7 @@
         swap = [(i, i ^ 1) for i in range(groups)]
         both = jnp.stack([sums, lax.ppermute(sums, "expert", swap)])
         returned = [both] + [
-            lax.ppermute(both, "expert", [(i, i ^ (SIDES * d)) for i in range(groups)])
+            lax.ppermute(both, "expert", [(target_of(i, SIDES * d), i) for i in range(groups)])
             for d in range(1, LINE)
         ]
     else:

time: 92.3 us -> 90.4 us (0.979)
  the two profiles are of different devices: /device:TPU:0 before, /device:TPU:12 now
where the time goes in v9:
time: 90.4 us; the launch traced here: 90.2 us
  waiting for transfers between devices  47.8 us (53%)
  starting transfers between devices  24 us (27%)
  Pallas kernels  14.4 us (16%)
  local copies, waits for them, and re-layouts  3.13 us (3%)
    ppermute x9, waiting for transfers between devices, send(): return lax.ppermute(block, 'expert', pairs)  32.6 us
    pallas_call x18, Pallas kernels, __call__(): pl.pallas_call(body, out_shape=outs, in_specs=in_specs, compiler_params=p...  14.4 us
    ppermute x9, starting transfers between devices, send(): return lax.ppermute(block, 'expert', pairs)  11.6 us
    ppermute x2, waiting for transfers between devices, swap(): lax.ppermute(block, 'expert', [(i, i ^ 1) for i in range(LINE * SIDES)])  5.92 us
    ppermute x5, starting transfers between devices, reduced(): others.append(lax.ppermute(pair, 'dp', shift))  4.79 us
    ppermute x5, waiting for transfers between devices, reduced(): others.append(lax.ppermute(pair, 'dp', shift))  4.09 us
    ppermute x3, starting transfers between devices, body(): lax.ppermute(both, 'expert', [(target_of(i, SIDES * d), i) for i in range...  3.7 us
    unnamed x16, local copies, waits for them, and re-layouts  3.13 us
  transfers between devices with their start and end apart: 23, of which 16 were waited for; matrix products, arithmetic and copies ran while one was open for 0% of the time, Pallas kernels for 10%

profile of v9, /device:TPU:12, one launch (start us, length us, event | category | flops | bytes accessed | tf_op | source)
XLA Modules:
  0.0 90.2 jit_solution(16536198176567908416)
XLA Ops:
  0.6 1.8 %shard_map.76 = (s32[2,128]{1,0:T(2,128)}, bf16[144,768]{1,0:T(8,128)(2,1)}) custom-call(s32[2,128]{1,0:T(2,128)} %bitcast.13, f32[2,128]{1,0:T(2,128)} %bitcast.10, bf16[128,2048]{1,0:T(8,128)(2,1)} %refs_0_.9), custom_call_target="tpu_custom_call" | custom-call | flops 1 | bytes 1 | tf_op jit(solution)/shard_map/pallas_call | solution.py:42
  2.5 1.6 %collective-permute-start = (bf16[144,768]{1,0:T(8,128)(2,1)}, bf16[144,768]{1,0:T(8,128)(2,1)S(1)}, u32[]{:S(2)}, u32[]{:S(2)}) collective-permute-start(bf16[144,768]{1,0:T(8,128)(2,1)} %get-tuple-element.35.refs_0_), channel_id=1, source_target_pairs={{0,1},{1,0},{2,3},{3,2},{4,5},{5,4},{6,7},{7,6},{8,9},{9,8},{10,11... | collective-permute-start | bytes 663560 | tf_op jit(solution)/shard_map/ppermute | solution.py:307
  6.4 3.4 %collective-permute-done.refs_1_ = bf16[144,768]{1,0:T(8,128)(2,1)S(1)} collective-permute-done((bf16[144,768]{1,0:T(8,128)(2,1)}, bf16[144,768]{1,0:T(8,128)(2,1)S(1)}, u32[]{:S(2)}, u32[]{:S(2)}) %collective-permute-start) | collective-permute-done | bytes 221216 | tf_op jit(solution)/shard_map/ppermute | solution.py:307
  11.2 1.6 %collective-permute-start.1 = (bf16[128,1280]{1,0:T(8,128)(2,1)S(1)}, bf16[128,1280]{1,0:T(8,128)(2,1)S(1)}, u32[]{:S(2)}, u32[]{:S(2)}) collective-permute-start(bf16[128,1280]{1,0:T(8,128)(2,1)S(1)} %get-tuple-element.36), channel_id=1, source_target_pairs={{0,1},{1,0},{2,3},{3,2},{4,5},{5,4},{6,7},{7,6},{8,9},{9,8},{10,11... | collective-permute-start | bytes 983048 | tf_op jit(solution)/shard_map/ppermute | solution.py:307
  12.8 1.6 %collective-permute-start.2 = (bf16[2,64,768]{2,1,0:T(8,128)(2,1)S(1)}, bf16[2,64,768]{2,1,0:T(8,128)(2,1)S(1)}, u32[]{:S(2)}, u32[]{:S(2)}) collective-permute-start(bf16[2,64,768]{2,1,0:T(8,128)(2,1)S(1)} %get-tuple-element.39), channel_id=1, source_target_pairs={{0,2},{1,3},{2,4},{3,5},{4,6},{5,7},{6,0},{7,1},{8,10},{9,11},{10,... | collective-permute-start | bytes 589832 | tf_op jit(solution)/shard_map/ppermute | solution.py:311
  15.6 1.8 %collective-permute-start.4 = (bf16[2,64,768]{2,1,0:T(8,128)(2,1)S(1)}, bf16[2,64,768]{2,1,0:T(8,128)(2,1)S(1)}, u32[]{:S(2)}, u32[]{:S(2)}) collective-permute-start(bf16[2,64,768]{2,1,0:T(8,128)(2,1)S(1)} %get-tuple-element.41), channel_id=1, source_target_pairs={{0,6},{1,7},{2,0},{3,1},{4,2},{5,3},{6,4},{7,5},{8,14},{9,15},{10,... | collective-permute-start | bytes 589832 | tf_op jit(solution)/shard_map/ppermute | solution.py:311
  17.4 2.5 %collective-permute-done.1.refs_1_ = bf16[128,1280]{1,0:T(8,128)(2,1)S(1)} collective-permute-done((bf16[128,1280]{1,0:T(8,128)(2,1)S(1)}, bf16[128,1280]{1,0:T(8,128)(2,1)S(1)}, u32[]{:S(2)}, u32[]{:S(2)}) %collective-permute-start.1) | collective-permute-done | bytes 327712 | tf_op jit(solution)/shard_map/ppermute | solution.py:307
  20.3 7.6 %collective-permute-done.2.refs_2_ = bf16[2,64,768]{2,1,0:T(8,128)(2,1)S(1)} collective-permute-done((bf16[2,64,768]{2,1,0:T(8,128)(2,1)S(1)}, bf16[2,64,768]{2,1,0:T(8,128)(2,1)S(1)}, u32[]{:S(2)}, u32[]{:S(2)}) %collective-permute-start.2) | collective-permute-done | bytes 196640 | tf_op jit(solution)/shard_map/ppermute | solution.py:311
  27.9 2.1 %collective-permute-done.3.refs_3_ = bf16[2,64,768]{2,1,0:T(8,128)(2,1)S(1)} collective-permute-done((bf16[2,64,768]{2,1,0:T(8,128)(2,1)S(1)}, bf16[2,64,768]{2,1,0:T(8,128)(2,1)S(1)}, u32[]{:S(2)}, u32[]{:S(2)}) %collective-permute-start.3) | collective-permute-done | bytes 196640 | tf_op jit(solution)/shard_map/ppermute | solution.py:311
  30.0 1.8 %collective-permute-done.4.refs_4_ = bf16[2,64,768]{2,1,0:T(8,128)(2,1)S(1)} collective-permute-done((bf16[2,64,768]{2,1,0:T(8,128)(2,1)S(1)}, bf16[2,64,768]{2,1,0:T(8,128)(2,1)S(1)}, u32[]{:S(2)}, u32[]{:S(2)}) %collective-permute-start.4) | collective-permute-done | bytes 196640 | tf_op jit(solution)/shard_map/ppermute | solution.py:311
  32.7 1.7 %collective-permute-start.10 = (bf16[2,64,1024]{2,1,0:T(8,128)(2,1)S(1)}, bf16[2,64,1024]{2,1,0:T(8,128)(2,1)S(1)}, u32[]{:S(2)}, u32[]{:S(2)}) collective-permute-start(bf16[2,64,1024]{2,1,0:T(8,128)(2,1)S(1)} %get-tuple-element.51), channel_id=1, source_target_pairs={{0,4},{1,5},{2,6},{3,7},{4,0},{5,1},{6,2},{7,3},{8,12},{9,13},{10,... | collective-permute-start | bytes 786440 | tf_op jit(solution)/shard_map/ppermute | solution.py:311
  34.4 1.9 %collective-permute-start.11 = (bf16[2,64,1024]{2,1,0:T(8,128)(2,1)S(1)}, bf16[2,64,1024]{2,1,0:T(8,128)(2,1)S(1)}, u32[]{:S(2)}, u32[]{:S(2)}) collective-permute-start(bf16[2,64,1024]{2,1,0:T(8,128)(2,1)S(1)} %get-tuple-element.52), channel_id=1, source_target_pairs={{0,6},{1,7},{2,0},{3,1},{4,2},{5,3},{6,4},{7,5},{8,14},{9,15},{10,... | collective-permute-start | bytes 786440 | tf_op jit(solution)/shard_map/ppermute | solution.py:311
  39.7 2.1 %collective-permute-done.9.refs_2_ = bf16[2,64,1024]{2,1,0:T(8,128)(2,1)S(1)} collective-permute-done((bf16[2,64,1024]{2,1,0:T(8,128)(2,1)S(1)}, bf16[2,64,1024]{2,1,0:T(8,128)(2,1)S(1)}, u32[]{:S(2)}, u32[]{:S(2)}) %collective-permute-start.9) | collective-permute-done | bytes 262176 | tf_op jit(solution)/shard_map/ppermute | solution.py:311
  41.8 14.2 %collective-permute-done.10.refs_3_ = bf16[2,64,1024]{2,1,0:T(8,128)(2,1)S(1)} collective-permute-done((bf16[2,64,1024]{2,1,0:T(8,128)(2,1)S(1)}, bf16[2,64,1024]{2,1,0:T(8,128)(2,1)S(1)}, u32[]{:S(2)}, u32[]{:S(2)}) %collective-permute-start.10) | collective-permute-done | bytes 262176 | tf_op jit(solution)/shard_map/ppermute | solution.py:311
  56.0 2.1 %collective-permute-done.11.refs_4_ = bf16[2,64,1024]{2,1,0:T(8,128)(2,1)S(1)} collective-permute-done((bf16[2,64,1024]{2,1,0:T(8,128)(2,1)S(1)}, bf16[2,64,1024]{2,1,0:T(8,128)(2,1)S(1)}, u32[]{:S(2)}, u32[]{:S(2)}) %collective-permute-start.11) | collective-permute-done | bytes 262176 | tf_op jit(solution)/shard_map/ppermute | solution.py:311
  60.8 1.8 %collective-permute-done.15.refs_1_ = bf16[2,2,192,1024]{3,2,1,0:T(8,128)(2,1)S(1)} collective-permute-done((bf16[2,2,192,1024]{3,2,1,0:T(8,128)(2,1)S(1)}, bf16[2,2,192,1024]{3,2,1,0:T(8,128)(2,1)S(1)}, u32[]{:S(2)}, u32[]{:S(2)}) %collective-permute-start.15) | collective-permute-done | bytes 1572896 | tf_op jit(solution)/shard_map/ppermute | solution.py:403
  64.6 2.0 %collective-permute-start.8 = (bf16[2,64,256]{2,1,0:T(8,128)(2,1)S(1)}, bf16[2,64,256]{2,1,0:T(8,128)(2,1)S(1)}, u32[]{:S(2)}, u32[]{:S(2)}) collective-permute-start(bf16[2,64,256]{2,1,0:T(8,128)(2,1)S(1)} %get-tuple-element.49), channel_id=1, source_target_pairs={{0,6},{1,7},{2,0},{3,1},{4,2},{5,3},{6,4},{7,5},{8,14},{9,15},{10,... | collective-permute-start | bytes 196616 | tf_op jit(solution)/shard_map/ppermute | solution.py:311
  69.0 2.1 %collective-permute-done.8.refs_4_ = bf16[2,64,256]{2,1,0:T(8,128)(2,1)S(1)} collective-permute-done((bf16[2,64,256]{2,1,0:T(8,128)(2,1)S(1)}, bf16[2,64,256]{2,1,0:T(8,128)(2,1)S(1)}, u32[]{:S(2)}, u32[]{:S(2)}) %collective-permute-start.8) | collective-permute-done | bytes 65568 | tf_op jit(solution)/shard_map/ppermute | solution.py:311
  73.3 1.6 %collective-permute-start.22 = (bf16[2,192,256]{2,1,0:T(8,128)(2,1)S(1)}, bf16[2,192,256]{2,1,0:T(8,128)(2,1)S(1)}, u32[]{:S(2)}, u32[]{:S(2)}) collective-permute-start(bf16[2,192,256]{2,1,0:T(8,128)(2,1)S(1)} %shard_map.90.refs_4_), channel_id=1, source_target_pairs={{0,16},{8,24},{16,0},{24,8},{1,17},{9,25},{17,1},{25,9},{2,18},{10... | collective-permute-start | bytes 589832 | tf_op jit(solution)/shard_map/ppermute | solution.py:426
  75.4 3.0 %collective-permute-done.16 = f32[2,256]{1,0:T(2,128)S(1)} collective-permute-done((f32[2,256]{1,0:T(2,128)S(1)}, f32[2,256]{1,0:T(2,128)S(1)}, u32[]{:S(2)}, u32[]{:S(2)}) %collective-permute-start.16) | collective-permute-done | bytes 2080 | tf_op jit(solution)/shard_map/ppermute | solution.py:459
  78.5 3.0 %collective-permute-start.18 = (f32[2,2,256]{2,1,0:T(2,128)S(1)}, f32[2,2,256]{2,1,0:T(2,128)S(1)}, u32[]{:S(2)}, u32[]{:S(2)}) collective-permute-start(f32[2,2,256]{2,1,0:T(2,128)S(1)} %pad_maximum_fusion.refs_2_), channel_id=1, source_target_pairs={{4,0},{5,1},{6,2},{7,3},{0,4},{1,5},{2,6},{3,7},{12,8},{13,9},{14,... | collective-permute-start | bytes 12296 | tf_op jit(solution)/shard_map/ppermute | solution.py:461
  82.2 1.7 %collective-permute-done.20.refs_2_ = bf16[2,192,1024]{2,1,0:T(8,128)(2,1)S(1)} collective-permute-done((bf16[2,192,1024]{2,1,0:T(8,128)(2,1)S(1)}, bf16[2,192,1024]{2,1,0:T(8,128)(2,1)S(1)}, u32[]{:S(2)}, u32[]{:S(2)}) %collective-permute-start.20) | collective-permute-done | bytes 786464 | tf_op jit(solution)/shard_map/ppermute | solution.py:426
  83.8 1.7 %shard_map.91 = (f32[192,2,2048]{2,1,0:T(2,128)}, f32[8,128]{1,0:T(8,128)S(1)}) custom-call(bf16[2,2,192,1024]{3,2,1,0:T(8,128)(2,1)S(1)} %get-tuple-element.54.refs_6_.refs_0_, bf16[2,2,192,1024]{3,2,1,0:T(8,128)(2,1)S(1)} %collective-permute-done.15.refs_1_, ...), custom_call_target="tpu_custom_call", output_to_operand_aliasing={{0}: (3, {})} | custom-call | flops 1 | bytes 1 | tf_op jit(solution)/shard_map/pallas_call | solution.py:42
  85.5 2.1 %collective-permute-done.22.refs_2_ = bf16[2,192,256]{2,1,0:T(8,128)(2,1)S(1)} collective-permute-done((bf16[2,192,256]{2,1,0:T(8,128)(2,1)S(1)}, bf16[2,192,256]{2,1,0:T(8,128)(2,1)S(1)}, u32[]{:S(2)}, u32[]{:S(2)}) %collective-permute-start.22) | collective-permute-done | bytes 196640 | tf_op jit(solution)/shard_map/ppermute | solution.py:426
  (57 shorter events, 22.6 us)
Async XLA Ops:
  2.5 7.4 %collective-permute-start = (bf16[144,768]{1,0:T(8,128)(2,1)}, bf16[144,768]{1,0:T(8,128)(2,1)S(1)}, u32[]{:S(2)}, u32[]{:S(2)}) collective-permute-start(bf16[144,768]{1,0:T(8,128)(2,1)} %get-tuple-element.35.refs_0_), channel_id=1, source_target_pairs={{0,1},{1,0},{2,3},{3,2},{4,5},{5,4},{6,7},{7,6},{8,9},{9,8},{10,11... | collective-permute-start | bytes 663560 | tf_op jit(solution)/shard_map/ppermute | solution.py:307
  6.2 30.2 %copy-start = (bf16[2,768,2048]{2,1,0:T(8,128)(2,1)S(1)}, bf16[2,768,2048]{2,1,0:T(8,128)(2,1)}, u32[]{:S(2)}) copy-start(bf16[2,768,2048]{2,1,0:T(8,128)(2,1)} %refs_0_.11) | copy-start | bytes 18874372
  11.2 8.6 %collective-permute-start.1 = (bf16[128,1280]{1,0:T(8,128)(2,1)S(1)}, bf16[128,1280]{1,0:T(8,128)(2,1)S(1)}, u32[]{:S(2)}, u32[]{:S(2)}) collective-permute-start(bf16[128,1280]{1,0:T(8,128)(2,1)S(1)} %get-tuple-element.36), channel_id=1, source_target_pairs={{0,1},{1,0},{2,3},{3,2},{4,5},{5,4},{6,7},{7,6},{8,9},{9,8},{10,11... | collective-permute-start | bytes 983048 | tf_op jit(solution)/shard_map/ppermute | solution.py:307
  12.8 15.1 %collective-permute-start.2 = (bf16[2,64,768]{2,1,0:T(8,128)(2,1)S(1)}, bf16[2,64,768]{2,1,0:T(8,128)(2,1)S(1)}, u32[]{:S(2)}, u32[]{:S(2)}) collective-permute-start(bf16[2,64,768]{2,1,0:T(8,128)(2,1)S(1)} %get-tuple-element.39), channel_id=1, source_target_pairs={{0,2},{1,3},{2,4},{3,5},{4,6},{5,7},{6,0},{7,1},{8,10},{9,11},{10,... | collective-permute-start | bytes 589832 | tf_op jit(solution)/shard_map/ppermute | solution.py:311
  14.4 15.6 %collective-permute-start.3 = (bf16[2,64,768]{2,1,0:T(8,128)(2,1)S(1)}, bf16[2,64,768]{2,1,0:T(8,128)(2,1)S(1)}, u32[]{:S(2)}, u32[]{:S(2)}) collective-permute-start(bf16[2,64,768]{2,1,0:T(8,128)(2,1)S(1)} %get-tuple-element.40), channel_id=1, source_target_pairs={{0,4},{1,5},{2,6},{3,7},{4,0},{5,1},{6,2},{7,3},{8,12},{9,13},{10,... | collective-permute-start | bytes 589832 | tf_op jit(solution)/shard_map/ppermute | solution.py:311
  15.6 16.2 %collective-permute-start.4 = (bf16[2,64,768]{2,1,0:T(8,128)(2,1)S(1)}, bf16[2,64,768]{2,1,0:T(8,128)(2,1)S(1)}, u32[]{:S(2)}, u32[]{:S(2)}) collective-permute-start(bf16[2,64,768]{2,1,0:T(8,128)(2,1)S(1)} %get-tuple-element.41), channel_id=1, source_target_pairs={{0,6},{1,7},{2,0},{3,1},{4,2},{5,3},{6,4},{7,5},{8,14},{9,15},{10,... | collective-permute-start | bytes 589832 | tf_op jit(solution)/shard_map/ppermute | solution.py:311
  32.6 4.6 %collective-permute-start.5 = (bf16[2,2,192,768]{3,2,1,0:T(8,128)(2,1)S(1)}, bf16[2,2,192,768]{3,2,1,0:T(8,128)(2,1)S(1)}, u32[]{:S(2)}, u32[]{:S(2)}) collective-permute-start(bf16[2,2,192,768]{3,2,1,0:T(8,128)(2,1)S(1)} %get-tuple-element.44), channel_id=1, source_target_pairs={{0,8},{8,0},{16,24},{24,16},{1,9},{9,1},{17,25},{25,17},{2,10},{10... | collective-permute-start | bytes 3538952 | tf_op jit(solution)/shard_map/ppermute | solution.py:403
  32.6 9.2 %collective-permute-start.9 = (bf16[2,64,1024]{2,1,0:T(8,128)(2,1)S(1)}, bf16[2,64,1024]{2,1,0:T(8,128)(2,1)S(1)}, u32[]{:S(2)}, u32[]{:S(2)}) collective-permute-start(bf16[2,64,1024]{2,1,0:T(8,128)(2,1)S(1)} %get-tuple-element.50), channel_id=1, source_target_pairs={{0,2},{1,3},{2,4},{3,5},{4,6},{5,7},{6,0},{7,1},{8,10},{9,11},{10,... | collective-permute-start | bytes 786440 | tf_op jit(solution)/shard_map/ppermute | solution.py:311
  32.7 23.3 %collective-permute-start.10 = (bf16[2,64,1024]{2,1,0:T(8,128)(2,1)S(1)}, bf16[2,64,1024]{2,1,0:T(8,128)(2,1)S(1)}, u32[]{:S(2)}, u32[]{:S(2)}) collective-permute-start(bf16[2,64,1024]{2,1,0:T(8,128)(2,1)S(1)} %get-tuple-element.51), channel_id=1, source_target_pairs={{0,4},{1,5},{2,6},{3,7},{4,0},{5,1},{6,2},{7,3},{8,12},{9,13},{10,... | collective-permute-start | bytes 786440 | tf_op jit(solution)/shard_map/ppermute | solution.py:311
  34.4 23.7 %collective-permute-start.11 = (bf16[2,64,1024]{2,1,0:T(8,128)(2,1)S(1)}, bf16[2,64,1024]{2,1,0:T(8,128)(2,1)S(1)}, u32[]{:S(2)}, u32[]{:S(2)}) collective-permute-start(bf16[2,64,1024]{2,1,0:T(8,128)(2,1)S(1)} %get-tuple-element.52), channel_id=1, source_target_pairs={{0,6},{1,7},{2,0},{3,1},{4,2},{5,3},{6,4},{7,5},{8,14},{9,15},{10,... | collective-permute-start | bytes 786440 | tf_op jit(solution)/shard_map/ppermute | solution.py:311
  37.3 20.8 %collective-permute-start.13 = (bf16[2,64,768]{2,1,0:T(8,128)(2,1)S(1)}, bf16[2,64,768]{2,1,0:T(8,128)(2,1)S(1)}, u32[]{:S(2)}, u32[]{:S(2)}) collective-permute-start(bf16[2,64,768]{2,1,0:T(8,128)(2,1)S(1)} %get-tuple-element.53), channel_id=1, source_target_pairs={{0,16},{8,24},{16,0},{24,8},{1,17},{9,25},{17,1},{25,9},{2,18},{10... | collective-permute-start | bytes 589832 | tf_op jit(solution)/shard_map/ppermute | solution.py:426
  37.9 20.2 %collective-permute-start.12 = (bf16[2,64,768]{2,1,0:T(8,128)(2,1)S(1)}, bf16[2,64,768]{2,1,0:T(8,128)(2,1)S(1)}, u32[]{:S(2)}, u32[]{:S(2)}) collective-permute-start(bf16[2,64,768]{2,1,0:T(8,128)(2,1)S(1)} %get-tuple-element.45.refs_3_), channel_id=1, source_target_pairs={{0,16},{8,24},{16,0},{24,8},{1,17},{9,25},{17,1},{25,9},{2,18},{10... | collective-permute-start | bytes 589832 | tf_op jit(solution)/shard_map/ppermute | solution.py:426
  59.1 3.5 %collective-permute-start.15 = (bf16[2,2,192,1024]{3,2,1,0:T(8,128)(2,1)S(1)}, bf16[2,2,192,1024]{3,2,1,0:T(8,128)(2,1)S(1)}, u32[]{:S(2)}, u32[]{:S(2)}) collective-permute-start(bf16[2,2,192,1024]{3,2,1,0:T(8,128)(2,1)S(1)} %get-tuple-element.56), channel_id=1, source_target_pairs={{0,8},{8,0},{16,24},{24,16},{1,9},{9,1},{17,25},{25,17},{2,10},{10... | collective-permute-start | bytes 4718600 | tf_op jit(solution)/shard_map/ppermute | solution.py:403
  59.2 7.7 %collective-permute-start.14 = (bf16[2,64,768]{2,1,0:T(8,128)(2,1)S(1)}, bf16[2,64,768]{2,1,0:T(8,128)(2,1)S(1)}, u32[]{:S(2)}, u32[]{:S(2)}) collective-permute-start(bf16[2,64,768]{2,1,0:T(8,128)(2,1)S(1)} %get-tuple-element.55), channel_id=1, source_target_pairs={{0,16},{8,24},{16,0},{24,8},{1,17},{9,25},{17,1},{25,9},{2,18},{10... | collective-permute-start | bytes 589832 | tf_op jit(solution)/shard_map/ppermute | solution.py:426
  62.8 21.0 %collective-permute-start.20 = (bf16[2,192,1024]{2,1,0:T(8,128)(2,1)S(1)}, bf16[2,192,1024]{2,1,0:T(8,128)(2,1)S(1)}, u32[]{:S(2)}, u32[]{:S(2)}) collective-permute-start(bf16[2,192,1024]{2,1,0:T(8,128)(2,1)S(1)} %shard_map.86.refs_5_), channel_id=1, source_target_pairs={{0,16},{8,24},{16,0},{24,8},{1,17},{9,25},{17,1},{25,9},{2,18},{10... | collective-permute-start | bytes 2359304 | tf_op jit(solution)/shard_map/ppermute | solution.py:426
  63.4 5.1 %collective-permute-start.6 = (bf16[2,64,256]{2,1,0:T(8,128)(2,1)S(1)}, bf16[2,64,256]{2,1,0:T(8,128)(2,1)S(1)}, u32[]{:S(2)}, u32[]{:S(2)}) collective-permute-start(bf16[2,64,256]{2,1,0:T(8,128)(2,1)S(1)} %get-tuple-element.47), channel_id=1, source_target_pairs={{0,2},{1,3},{2,4},{3,5},{4,6},{5,7},{6,0},{7,1},{8,10},{9,11},{10,... | collective-permute-start | bytes 196616 | tf_op jit(solution)/shard_map/ppermute | solution.py:311
  63.4 5.6 %collective-permute-start.7 = (bf16[2,64,256]{2,1,0:T(8,128)(2,1)S(1)}, bf16[2,64,256]{2,1,0:T(8,128)(2,1)S(1)}, u32[]{:S(2)}, u32[]{:S(2)}) collective-permute-start(bf16[2,64,256]{2,1,0:T(8,128)(2,1)S(1)} %get-tuple-element.48), channel_id=1, source_target_pairs={{0,4},{1,5},{2,6},{3,7},{4,0},{5,1},{6,2},{7,3},{8,12},{9,13},{10,... | collective-permute-start | bytes 196616 | tf_op jit(solution)/shard_map/ppermute | solution.py:311
  64.6 6.5 %collective-permute-start.8 = (bf16[2,64,256]{2,1,0:T(8,128)(2,1)S(1)}, bf16[2,64,256]{2,1,0:T(8,128)(2,1)S(1)}, u32[]{:S(2)}, u32[]{:S(2)}) collective-permute-start(bf16[2,64,256]{2,1,0:T(8,128)(2,1)S(1)} %get-tuple-element.49), channel_id=1, source_target_pairs={{0,6},{1,7},{2,0},{3,1},{4,2},{5,3},{6,4},{7,5},{8,14},{9,15},{10,... | collective-permute-start | bytes 196616 | tf_op jit(solution)/shard_map/ppermute | solution.py:311
  71.5 1.8 %collective-permute-start.21 = (bf16[2,2,192,256]{3,2,1,0:T(8,128)(2,1)S(1)}, bf16[2,2,192,256]{3,2,1,0:T(8,128)(2,1)S(1)}, u32[]{:S(2)}, u32[]{:S(2)}) collective-permute-start(bf16[2,2,192,256]{3,2,1,0:T(8,128)(2,1)S(1)} %get-tuple-element.63), channel_id=1, source_target_pairs={{0,8},{8,0},{16,24},{24,16},{1,9},{9,1},{17,25},{25,17},{2,10},{10... | collective-permute-start | bytes 1179656 | tf_op jit(solution)/shard_map/ppermute | solution.py:403
  73.3 14.3 %collective-permute-start.22 = (bf16[2,192,256]{2,1,0:T(8,128)(2,1)S(1)}, bf16[2,192,256]{2,1,0:T(8,128)(2,1)S(1)}, u32[]{:S(2)}, u32[]{:S(2)}) collective-permute-start(bf16[2,192,256]{2,1,0:T(8,128)(2,1)S(1)} %shard_map.90.refs_4_), channel_id=1, source_target_pairs={{0,16},{8,24},{16,0},{24,8},{1,17},{9,25},{17,1},{25,9},{2,18},{10... | collective-permute-start | bytes 589832 | tf_op jit(solution)/shard_map/ppermute | solution.py:426
  74.9 3.6 %collective-permute-start.16 = (f32[2,256]{1,0:T(2,128)S(1)}, f32[2,256]{1,0:T(2,128)S(1)}, u32[]{:S(2)}, u32[]{:S(2)}) collective-permute-start(f32[2,256]{1,0:T(2,128)S(1)} %get-tuple-element.61.refs_2_), channel_id=1, source_target_pairs={{0,1},{1,0},{2,3},{3,2},{4,5},{5,4},{6,7},{7,6},{8,9},{9,8},{10,11... | collective-permute-start | bytes 6152 | tf_op jit(solution)/shard_map/ppermute | solution.py:459
  78.5 10.6 %collective-permute-start.19 = (f32[2,2,256]{2,1,0:T(2,128)S(1)}, f32[2,2,256]{2,1,0:T(2,128)S(1)}, u32[]{:S(2)}, u32[]{:S(2)}) collective-permute-start(f32[2,2,256]{2,1,0:T(2,128)S(1)} %pad_maximum_fusion.refs_2_), channel_id=1, source_target_pairs={{6,0},{7,1},{0,2},{1,3},{2,4},{3,5},{4,6},{5,7},{14,8},{15,9},{8,1... | collective-permute-start | bytes 12296 | tf_op jit(solution)/shard_map/ppermute | solution.py:461
  78.5 10.6 %collective-permute-start.18 = (f32[2,2,256]{2,1,0:T(2,128)S(1)}, f32[2,2,256]{2,1,0:T(2,128)S(1)}, u32[]{:S(2)}, u32[]{:S(2)}) collective-permute-start(f32[2,2,256]{2,1,0:T(2,128)S(1)} %pad_maximum_fusion.refs_2_), channel_id=1, source_target_pairs={{4,0},{5,1},{6,2},{7,3},{0,4},{1,5},{2,6},{3,7},{12,8},{13,9},{14,... | collective-permute-start | bytes 12296 | tf_op jit(solution)/shard_map/ppermute | solution.py:461
  81.5 7.7 %collective-permute-start.17 = (f32[2,2,256]{2,1,0:T(2,128)S(1)}, f32[2,2,256]{2,1,0:T(2,128)S(1)}, u32[]{:S(2)}, u32[]{:S(2)}) collective-permute-start(f32[2,2,256]{2,1,0:T(2,128)S(1)} %pad_maximum_fusion.refs_2_), channel_id=1, source_target_pairs={{2,0},{3,1},{4,2},{5,3},{6,4},{7,5},{0,6},{1,7},{10,8},{11,9},{12,... | collective-permute-start | bytes 12296 | tf_op jit(solution)/shard_map/ppermute | solution.py:461
  (7 other events, 15.4 us)

commit v10 on v9

--- a/solution.py
+++ b/solution.py
@@ -13,15 +13,16 @@
 HBM = pl.BlockSpec(memory_space=pltpu.HBM)
 
 LINE, SIDES = 4, 2
+BACK = (0, 1, 3, 2)
 INFO = 16
 
 
-def target_of(me, part):
-    return (me // SIDES + part // SIDES) % LINE * SIDES + (me % SIDES ^ part % SIDES)
+def moved(me, places, side):
+    return (me // SIDES + places) % LINE * SIDES + (me % SIDES ^ side)
 
 
 def source_of(me, part):
-    return (me // SIDES + LINE - part // SIDES) % LINE * SIDES + (me % SIDES ^ part % SIDES)
+    return moved(me, LINE - BACK[part % LINE], part // LINE)
 
 
 class Chain:
@@ -94,47 +95,43 @@
         out_ref[tokens:, tokens:] = jnp.zeros((INFO, width - tokens), BF16)
 
 
-def pick_kernel(held, capacity, chosen, start, own_ref, other_ref, *refs):
-    tokens = own_ref.shape[0] - (INFO if start is None else 0)
+def places(held, capacity, chosen, ref, place_ref):
+    tokens = place_ref.shape[1]
     rows = held * capacity
-    if start is None:
-        rows_ref, *out_refs, place_ref, rest_ref, sem = refs
-        copy = pltpu.make_async_copy(rows_ref.at[:, own_ref.shape[1] :], rest_ref, sem)
-        copy.start()
-        me = lax.axis_index("expert")
-        local = lax.broadcasted_iota(I32, (rows, tokens), 0)
-        for side, ref in enumerate((own_ref, other_ref)):
-            info = ref[tokens:, :tokens].astype(F32)
-            flat = (info[:chosen] * capacity + info[chosen : 2 * chosen]).astype(I32)
-            word = info[2 * chosen : 3 * chosen]
-            for d in range(LINE):
-                slot = local + target_of(me, SIDES * d) * rows
-                hits = [
-                    jnp.where(flat[k : k + 1] == slot, word[k : k + 1], 0.0) for k in range(chosen)
-                ]
-                place_ref[side, d * rows : (d + 1) * rows, :] = functools.reduce(
-                    jnp.add, hits
-                ).astype(BF16)
-        blocks = own_ref[:tokens, :], other_ref[:tokens, :]
+    me = lax.axis_index("expert")
+    local = lax.broadcasted_iota(I32, (rows, tokens), 0)
+    info = ref[tokens:, :tokens].astype(F32)
+    flat = (info[:chosen] * capacity + info[chosen : 2 * chosen]).astype(I32)
+    word = info[2 * chosen : 3 * chosen]
+    for side in range(SIDES):
+        slot = local + (me ^ side) * rows
+        hits = [jnp.where(flat[k : k + 1] == slot, word[k : k + 1], 0.0) for k in range(chosen)]
+        place_ref[side * rows : (side + 1) * rows, :] = functools.reduce(jnp.add, hits).astype(BF16)
+
+
+def pick(held, capacity, block_refs, place_ref, out_refs):
+    tokens = place_ref.shape[2]
+    for j, ref in enumerate(block_refs):
+        scaled = jnp.dot(place_ref[j], ref[:tokens, :], preferred_element_type=F32).astype(BF16)
+        for side, out_ref in enumerate(out_refs):
+            for e in range(held):
+                at = (side * held + e) * capacity
+                out_ref[e, j * capacity : (j + 1) * capacity, :] = scaled[at : at + capacity]
+
+
+def pick_kernel(held, capacity, chosen, first, count, *refs):
+    block_refs, refs = refs[:count], refs[count:]
+    if first:
+        mine_ref, other_ref, place_ref = refs
+        for j, ref in enumerate(block_refs):
+            places(held, capacity, chosen, ref, place_ref.at[j])
     else:
-        place_ref, out_refs = refs[0], refs[1:]
-        width, first = out_refs[0].shape[2], own_ref.shape[1] - other_ref.shape[1]
-        blocks = (
-            own_ref[:, start : start + width],
-            other_ref[:, start - first : start - first + width],
-        )
-    for side, block in enumerate(blocks):
-        scaled = jnp.dot(place_ref[side], block, preferred_element_type=F32).astype(BF16)
-        for d, out_ref in enumerate(out_refs):
-            for e in range(held):
-                at = d * rows + e * capacity
-                out_ref[e, side * capacity : (side + 1) * capacity, :] = scaled[at : at + capacity]
-    if start is None:
-        copy.wait()
+        place_ref, mine_ref, other_ref = refs
+    pick(held, capacity, block_refs, place_ref, (mine_ref, other_ref))
 
 
 def turn_kernel(dp, hidden_ref, *refs):
-    out_ref = refs[-1]
+    out_ref, refs = refs[-1], refs[:-1]
     parts, held, _, units = hidden_ref.shape
     share, across = units // dp, dp // 2
     me = lax.axis_index("expert") if parts > 1 else 0
@@ -148,6 +145,19 @@
             other = (piece % 2) ^ core
             step = (piece // 2 - row + across) % across
             out_ref[e, other, step] = turned[piece * share : (piece + 1) * share]
+
+
+def cut_kernel(start, rows_ref, *refs):
+    out_refs, sems = refs[:-1], refs[-1]
+    copies = []
+    for i, ref in enumerate(out_refs):
+        at = slice(start, start + ref.shape[1])
+        copies.append(pltpu.make_async_copy(rows_ref.at[:, at], ref, sems.at[i]))
+        start += ref.shape[1]
+    for copy in copies:
+        copy.start()
+    for copy in copies:
+        copy.wait()
 
 
 def stacked_rows(refs, e):
@@ -235,10 +245,10 @@
     chosen, tokens = flat_ref.shape
     if direct:
         values = []
-        for part in range(LINE * SIDES):
-            at = part * capacity
-            ref = refs[part // SIDES]
-            values += [ref[part % SIDES, e : e + 1, at : at + capacity] for e in range(ref.shape[1])]
+        for q in range(LINE * SIDES):
+            at = (BACK.index(q // SIDES) + LINE * (q % SIDES)) * capacity
+            ref = refs[q // SIDES]
+            values += [ref[q % SIDES, e : e + 1, at : at + capacity] for e in range(ref.shape[1])]
         lanes = 128 // capacity
         values = jnp.concatenate(
             [
@@ -259,7 +269,8 @@
     picked = [jnp.zeros((1, tokens), F32) for _ in range(chosen)]
     for line in range(lines):
         at = lax.broadcasted_iota(I32, (128, tokens), 0) + line * 128
-        slot = (target_of(me, at // group) if direct else at // group) * group + at % group
+        q = at // group
+        slot = (moved(me, q // SIDES, q % SIDES) if direct else q) * group + at % group
         for k in range(chosen):
             hit = jnp.where(flat_ref[k : k + 1, :] == slot, columns[:, line : line + 1], 0.0)
             picked[k] += jnp.sum(hit, axis=0, keepdims=True)
@@ -271,11 +282,12 @@
 
 def chunks_of(features):
     unit = features // 16
-    return [6 * unit, 8 * unit, 2 * unit]
+    return [4 * unit, 6 * unit, 6 * unit]
 
 
 def cuts_of(share, c):
-    return [share // 3] * 3 if c == 0 else [share]
+    first = 16 * (share // 32)
+    return [first, share - first] if c == 1 else [share]
 
 
 sds = jax.ShapeDtypeStruct
@@ -284,9 +296,9 @@
 class Relay:
     def __init__(self, call, grad_out, ids, probs, held, capacity, widths):
         tokens, features = grad_out.shape
-        self.call, self.rows, self.held, self.capacity = call, grad_out, held, capacity
-        self.chosen, self.widths, self.place = ids.shape[0], widths, None
-        self.flat, self.first = call(
+        self.call, self.held, self.capacity, self.widths = call, held, capacity, widths
+        self.tokens, self.chosen, self.place = tokens, ids.shape[0], {}
+        self.flat, first = call(
             functools.partial(begin_kernel, LINE * SIDES * held, capacity),
             [sds(ids.shape, I32), sds((tokens + INFO, widths[0]), BF16)],
             ids,
@@ -301,40 +313,41 @@
             room=60,
             keep=False,
         )
-        self.first_other = self.swap(self.first)
-
-    def swap(self, block):
-        return lax.ppermute(block, "expert", [(i, i ^ 1) for i in range(LINE * SIDES)])
-
-    def send(self, block, d):
-        pairs = [(i, target_of(i, SIDES * d)) for i in range(LINE * SIDES)]
+        rest = call(
+            functools.partial(cut_kernel, widths[0]),
+            [sds((tokens, w), BF16) for w in widths[1:]],
+            grad_out,
+            in_specs=[HBM],
+            scratch_shapes=[pltpu.SemaphoreType.DMA((len(widths) - 1,))],
+            keep=False,
+        )
+        self.blocks, self.passed = [], []
+        for own in [first, *rest]:
+            on, back = self.along(own, 1), self.along(own, LINE - 1)
+            self.blocks.append([own, on, back])
+            self.passed.append(self.along(on, 1))
+
+    def along(self, block, places):
+        pairs = [(i, moved(i, places, 0)) for i in range(LINE * SIDES)]
         return lax.ppermute(block, "expert", pairs)
 
-    def chunk(self, c):
-        held, capacity, tokens = self.held, self.capacity, self.rows.shape[0]
-        rows = [sds((held, SIDES * capacity, self.widths[c]), BF16)] * LINE
-        place = sds((SIDES, LINE * held * capacity, tokens), BF16)
-        start = sum(self.widths[:c]) if c else None
-        kernel = functools.partial(pick_kernel, held, capacity, self.chosen, start)
+    def pick(self, c, name, blocks):
+        held, capacity, count = self.held, self.capacity, len(blocks)
+        rows = [sds((held, count * capacity, self.widths[c]), BF16)] * SIDES
+        kernel = functools.partial(pick_kernel, held, capacity, self.chosen, c == 0, count)
         if c == 0:
-            rest = sds((tokens, self.rows.shape[1] - self.widths[0]), BF16)
-            *sent, self.place, rest = self.call(
-                kernel,
-                [*rows, place, rest],
-                self.first,
-                self.first_other,
-                self.rows,
-                in_specs=[VMEM, VMEM, HBM],
-                scratch_shapes=[pltpu.SemaphoreType.DMA],
-            )
+            place = sds((count, SIDES * held * capacity, self.tokens), BF16)
+            mine, other, self.place[name] = self.call(kernel, [*rows, place], *blocks)
         else:
-            sent = self.call(kernel, rows, self.rows, self.rest_other, self.place)
-        got = [sent[0]] + [None] * (LINE - 1)
-        for d in range(LINE - 1, 0, -1):
-            got[d] = self.send(sent[d], d)
-        if c == 0:
-            self.rest_other = self.swap(rest)
-        return got
+            mine, other = self.call(kernel, rows, *blocks, self.place[name])
+        return mine, lax.ppermute(other, "expert", [(i, i ^ 1) for i in range(LINE * SIDES)])
+
+    def early(self, c):
+        return self.pick(c, "early", self.blocks[c])
+
+    def late(self, c, early):
+        late = self.pick(c, "late", [self.passed[c]])
+        return [early[0], late[0], early[1], late[1]]
 
 
 def exchanged(grad_out, ids, probs, groups, held, capacity, widths):
@@ -386,22 +399,13 @@
         functools.partial(turn_kernel, dp),
         sds((held, 2, across, share, per_expert), BF16),
         saved,
-        *([grad_out] if direct else []),
     )
-    if direct:
-        arrived = [relay.chunk(c) for c in range(min(2, count))]
-
     starts = [sum(widths[:c]) for c in range(count)]
     state = {"raw": None, "grad": None}
     summed = []
 
-    def reduced(c):
-        parts, width = arrived[c], widths[c]
-        piece = sds((across, held, share, width), BF16)
-        after = summed[0][2][:2] if c == 1 else ()
-        keep, give = call(term_kernel, [piece, piece], turned, *parts, after=after)
-        got = lax.ppermute(give, "dp", [(i, i ^ 1) for i in range(dp)])
-        final = c == count - 1
+    def accumulated(c):
+        parts, width, final = arrived[c], widths[c], c == count - 1
         if final:
             outs = [sds(saved.shape, BF16), sds((held, per_expert), F32)]
         else:
@@ -416,6 +420,15 @@
             *extra,
         )
         state["raw"] = made if final else made[0]
+
+    def reduced(c):
+        parts, width = arrived[c], widths[c]
+        piece = sds((across, held, share, width), BF16)
+        after = summed[-1][2][:1] if c else ()
+        keep, give = call(term_kernel, [piece, piece], turned, *parts, after=after)
+        got = lax.ppermute(give, "dp", [(i, i ^ 1) for i in range(dp)])
+        if c == count - 1:
+            accumulated(c)
         cuts = cuts_of(share, c)
         pieces = [sds((held, rows, width), BF16) for rows in cuts]
         pairs = call(functools.partial(pair_kernel, cuts), pieces * (across - 1), keep, got)
@@ -446,10 +459,16 @@
             ],
         )
 
+    if direct:
+        arrived, early = [], relay.early(0)
     for c in range(count):
+        if direct:
+            arrived.append(relay.late(c, early))
+            if c + 1 < count:
+                early = relay.early(c + 1)
+        if c >= 1:
+            accumulated(c - 1)
         reduced(c)
-        if direct and c + 2 < count:
-            arrived.append(relay.chunk(c + 2))
         if c >= 1:
             finished(c - 1)
     hidden_grad, sums = state["raw"]
@@ -458,7 +477,7 @@
         swap = [(i, i ^ 1) for i in range(groups)]
         both = jnp.stack([sums, lax.ppermute(sums, "expert", swap)])
         returned = [both] + [
-            lax.ppermute(both, "expert", [(target_of(i, SIDES * d), i) for i in range(groups)])
+            lax.ppermute(both, "expert", [(moved(i, d, 0), i) for i in range(groups)])
             for d in range(1, LINE)
         ]
     else:

time: 90.4 us -> 94.7 us (1.048)
  the two profiles are of different devices: /device:TPU:12 before, /device:TPU:0 now
where the time goes in v10:
time: 94.7 us; the launch traced here: 94.5 us
  waiting for transfers between devices  47.7 us (50%)
  starting transfers between devices  29.8 us (31%)
  Pallas kernels  15 us (16%)
  local copies, waits for them, and re-layouts  1.06 us (1%)
    ppermute x9, waiting for transfers between devices, along(): return lax.ppermute(block, 'expert', pairs)  23.4 us
    pallas_call x22, Pallas kernels, __call__(): pl.pallas_call(body, out_shape=outs, in_specs=in_specs, compiler_params=p...  15 us
    ppermute x9, starting transfers between devices, along(): return lax.ppermute(block, 'expert', pairs)  14.1 us
    ppermute x4, waiting for transfers between devices, reduced(): others.append(lax.ppermute(pair, 'dp', shift))  14 us
    ppermute x6, starting transfers between devices, pick(): lax.ppermute(other, 'expert', [(i, i ^ 1) for i in range(LINE * SIDES)])  8.66 us
    ppermute x4, starting transfers between devices, reduced(): others.append(lax.ppermute(pair, 'dp', shift))  4.26 us
    ppermute x3, waiting for transfers between devices, reduced(): got = lax.ppermute(give, 'dp', [(i, i ^ 1) for i in range(dp)])  4.03 us
    ppermute x6, waiting for transfers between devices, pick(): lax.ppermute(other, 'expert', [(i, i ^ 1) for i in range(LINE * SIDES)])  3.22 us
  transfers between devices with their start and end apart: 26, of which 14 were waited for; matrix products, arithmetic and copies ran while one was open for 0% of the time, Pallas kernels for 9%

profile of v10, /device:TPU:0, one launch (start us, length us, event | category | flops | bytes accessed | tf_op | source)
XLA Modules:
  0.0 94.5 jit_solution(18018144052351157554)
XLA Ops:
  0.6 1.8 %shard_map.77 = (s32[2,128]{1,0:T(2,128)}, bf16[144,512]{1,0:T(8,128)(2,1)}) custom-call(s32[2,128]{1,0:T(2,128)} %bitcast.13, f32[2,128]{1,0:T(2,128)} %bitcast.10, bf16[128,2048]{1,0:T(8,128)(2,1)} %rows_ref.3), custom_call_target="tpu_custom_call" | custom-call | flops 1 | bytes 1 | tf_op jit(solution)/shard_map/pallas_call | solution.py:43
  2.5 3.1 %collective-permute-start.2 = (bf16[144,512]{1,0:T(8,128)(2,1)}, bf16[144,512]{1,0:T(8,128)(2,1)S(1)}, u32[]{:S(2)}, u32[]{:S(2)}) collective-permute-start(bf16[144,512]{1,0:T(8,128)(2,1)} %get-tuple-element.37.refs_0_), channel_id=1, source_target_pairs={{0,2},{1,3},{2,4},{3,5},{4,6},{5,7},{6,0},{7,1},{8,10},{9,11},{10,... | collective-permute-start | bytes 442376 | tf_op jit(solution)/shard_map/ppermute | solution.py:332
  5.6 2.1 %collective-permute-start.3 = (bf16[144,512]{1,0:T(8,128)(2,1)}, bf16[144,512]{1,0:T(8,128)(2,1)S(1)}, u32[]{:S(2)}, u32[]{:S(2)}) collective-permute-start(bf16[144,512]{1,0:T(8,128)(2,1)} %get-tuple-element.37.refs_0_), channel_id=1, source_target_pairs={{0,6},{1,7},{2,0},{3,1},{4,2},{5,3},{6,4},{7,5},{8,14},{9,15},{10,... | collective-permute-start | bytes 442376 | tf_op jit(solution)/shard_map/ppermute | solution.py:332
  7.7 4.9 %collective-permute-done.2.refs_1_ = bf16[144,512]{1,0:T(8,128)(2,1)S(1)} collective-permute-done((bf16[144,512]{1,0:T(8,128)(2,1)}, bf16[144,512]{1,0:T(8,128)(2,1)S(1)}, u32[]{:S(2)}, u32[]{:S(2)}) %collective-permute-start.2) | collective-permute-done | bytes 147488 | tf_op jit(solution)/shard_map/ppermute | solution.py:332
  13.7 3.1 %collective-permute-start.4 = (bf16[128,768]{1,0:T(8,128)(2,1)S(1)}, bf16[128,768]{1,0:T(8,128)(2,1)S(1)}, u32[]{:S(2)}, u32[]{:S(2)}) collective-permute-start(bf16[128,768]{1,0:T(8,128)(2,1)S(1)} %get-tuple-element.39.refs_0_), channel_id=1, source_target_pairs={{0,2},{1,3},{2,4},{3,5},{4,6},{5,7},{6,0},{7,1},{8,10},{9,11},{10,... | collective-permute-start | bytes 589832 | tf_op jit(solution)/shard_map/ppermute | solution.py:332
  18.1 1.8 %collective-permute-start.7 = (bf16[2,96,512]{2,1,0:T(8,128)(2,1)S(1)}, bf16[2,96,512]{2,1,0:T(8,128)(2,1)S(1)}, u32[]{:S(2)}, u32[]{:S(2)}) collective-permute-start(bf16[2,96,512]{2,1,0:T(8,128)(2,1)S(1)} %get-tuple-element.43), channel_id=1, source_target_pairs={{0,1},{1,0},{2,3},{3,2},{4,5},{5,4},{6,7},{7,6},{8,9},{9,8},{10,11... | collective-permute-start | bytes 589832 | tf_op jit(solution)/shard_map/ppermute | solution.py:343
  21.4 1.7 %collective-permute-start.8 = (bf16[2,32,512]{2,1,0:T(8,128)(2,1)S(1)}, bf16[2,32,512]{2,1,0:T(8,128)(2,1)S(1)}, u32[]{:S(2)}, u32[]{:S(2)}) collective-permute-start(bf16[2,32,512]{2,1,0:T(8,128)(2,1)S(1)} %get-tuple-element.44), channel_id=1, source_target_pairs={{0,1},{1,0},{2,3},{3,2},{4,5},{5,4},{6,7},{7,6},{8,9},{9,8},{10,11... | collective-permute-start | bytes 196616 | tf_op jit(solution)/shard_map/ppermute | solution.py:343
  23.1 1.9 %collective-permute-done.4.refs_1_ = bf16[128,768]{1,0:T(8,128)(2,1)S(1)} collective-permute-done((bf16[128,768]{1,0:T(8,128)(2,1)S(1)}, bf16[128,768]{1,0:T(8,128)(2,1)S(1)}, u32[]{:S(2)}, u32[]{:S(2)}) %collective-permute-start.4) | collective-permute-done | bytes 196640 | tf_op jit(solution)/shard_map/ppermute | solution.py:332
  25.0 1.7 %collective-permute-done.9.refs_2_ = bf16[128,768]{1,0:T(8,128)(2,1)S(1)} collective-permute-done((bf16[128,768]{1,0:T(8,128)(2,1)S(1)}, bf16[128,768]{1,0:T(8,128)(2,1)S(1)}, u32[]{:S(2)}, u32[]{:S(2)}) %collective-permute-start.9) | collective-permute-done | bytes 196640 | tf_op jit(solution)/shard_map/ppermute | solution.py:332
  27.7 2.3 %collective-permute-done.10.refs_1_ = bf16[2,2,192,512]{3,2,1,0:T(8,128)(2,1)S(1)} collective-permute-done((bf16[2,2,192,512]{3,2,1,0:T(8,128)(2,1)S(1)}, bf16[2,2,192,512]{3,2,1,0:T(8,128)(2,1)S(1)}, u32[]{:S(2)}, u32[]{:S(2)}) %collective-permute-start.10) | collective-permute-done | bytes 786464 | tf_op jit(solution)/shard_map/ppermute | solution.py:429
  30.1 1.5 %collective-permute-start.12 = (bf16[2,192,512]{2,1,0:T(8,128)(2,1)S(1)}, bf16[2,192,512]{2,1,0:T(8,128)(2,1)S(1)}, u32[]{:S(2)}, u32[]{:S(2)}) collective-permute-start(bf16[2,192,512]{2,1,0:T(8,128)(2,1)S(1)} %shard_map.83.refs_2_), channel_id=1, source_target_pairs={{0,16},{8,24},{16,0},{24,8},{1,17},{9,25},{17,1},{25,9},{2,18},{10... | collective-permute-start | bytes 1179656 | tf_op jit(solution)/shard_map/ppermute | solution.py:439
  34.3 3.2 %collective-permute-start.1 = (bf16[128,768]{1,0:T(8,128)(2,1)S(1)}, bf16[128,768]{1,0:T(8,128)(2,1)S(1)}, u32[]{:S(2)}, u32[]{:S(2)}) collective-permute-start(bf16[128,768]{1,0:T(8,128)(2,1)S(1)} %get-tuple-element.36.refs_0_), channel_id=1, source_target_pairs={{0,6},{1,7},{2,0},{3,1},{4,2},{5,3},{6,4},{7,5},{8,14},{9,15},{10,... | collective-permute-start | bytes 589832 | tf_op jit(solution)/shard_map/ppermute | solution.py:332
  37.5 3.9 %collective-permute-done.5.refs_0_ = bf16[128,768]{1,0:T(8,128)(2,1)S(1)} collective-permute-done((bf16[128,768]{1,0:T(8,128)(2,1)S(1)}, bf16[128,768]{1,0:T(8,128)(2,1)S(1)}, u32[]{:S(2)}, u32[]{:S(2)}) %collective-permute-start.5) | collective-permute-done | bytes 196640 | tf_op jit(solution)/shard_map/ppermute | solution.py:332
  41.6 1.6 %collective-permute-start.14 = (bf16[2,32,768]{2,1,0:T(8,128)(2,1)S(1)}, bf16[2,32,768]{2,1,0:T(8,128)(2,1)S(1)}, u32[]{:S(2)}, u32[]{:S(2)}) collective-permute-start(bf16[2,32,768]{2,1,0:T(8,128)(2,1)S(1)} %get-tuple-element.51), channel_id=1, source_target_pairs={{0,1},{1,0},{2,3},{3,2},{4,5},{5,4},{6,7},{7,6},{8,9},{9,8},{10,11... | collective-permute-start | bytes 294920 | tf_op jit(solution)/shard_map/ppermute | solution.py:343
  43.1 2.4 %collective-permute-done.refs_1_ = bf16[128,768]{1,0:T(8,128)(2,1)S(1)} collective-permute-done((bf16[128,768]{1,0:T(8,128)(2,1)S(1)}, bf16[128,768]{1,0:T(8,128)(2,1)S(1)}, u32[]{:S(2)}, u32[]{:S(2)}) %collective-permute-start) | collective-permute-done | bytes 196640 | tf_op jit(solution)/shard_map/ppermute | solution.py:332
  45.5 3.0 %collective-permute-done.1.refs_2_ = bf16[128,768]{1,0:T(8,128)(2,1)S(1)} collective-permute-done((bf16[128,768]{1,0:T(8,128)(2,1)S(1)}, bf16[128,768]{1,0:T(8,128)(2,1)S(1)}, u32[]{:S(2)}, u32[]{:S(2)}) %collective-permute-start.1) | collective-permute-done | bytes 196640 | tf_op jit(solution)/shard_map/ppermute | solution.py:332
  51.0 1.5 %collective-permute-start.16 = (bf16[2,96,768]{2,1,0:T(8,128)(2,1)S(1)}, bf16[2,96,768]{2,1,0:T(8,128)(2,1)S(1)}, u32[]{:S(2)}, u32[]{:S(2)}) collective-permute-start(bf16[2,96,768]{2,1,0:T(8,128)(2,1)S(1)} %get-tuple-element.57), channel_id=1, source_target_pairs={{0,1},{1,0},{2,3},{3,2},{4,5},{5,4},{6,7},{7,6},{8,9},{9,8},{10,11... | collective-permute-start | bytes 884744 | tf_op jit(solution)/shard_map/ppermute | solution.py:343
  55.1 4.4 %collective-permute-done.11.refs_0_ = bf16[128,768]{1,0:T(8,128)(2,1)S(1)} collective-permute-done((bf16[128,768]{1,0:T(8,128)(2,1)S(1)}, bf16[128,768]{1,0:T(8,128)(2,1)S(1)}, u32[]{:S(2)}, u32[]{:S(2)}) %collective-permute-start.11) | collective-permute-done | bytes 196640 | tf_op jit(solution)/shard_map/ppermute | solution.py:332
  61.1 3.2 %collective-permute-done.17.refs_4_ = bf16[2,32,768]{2,1,0:T(8,128)(2,1)S(1)} collective-permute-done((bf16[2,32,768]{2,1,0:T(8,128)(2,1)S(1)}, bf16[2,32,768]{2,1,0:T(8,128)(2,1)S(1)}, u32[]{:S(2)}, u32[]{:S(2)}) %collective-permute-start.17) | collective-permute-done | bytes 98336 | tf_op jit(solution)/shard_map/ppermute | solution.py:343
  65.2 1.8 %shard_map.93 = (bf16[8,2,32,768]{3,2,1,0:T(8,128)(2,1)}, f32[2,256]{1,0:T(2,128)S(1)}) custom-call(bf16[2,768,2048]{2,1,0:T(8,128)(2,1)S(1)} %copy-done, bf16[2,96,768]{2,1,0:T(8,128)(2,1)S(1)} %get-tuple-element.49.refs_5_.refs_1_, bf16[2,32,768]{2,1,0:T(8,128)(2,1)S(1)} %get-tuple-element.56.refs_6_.refs_2_, ...), custom_call_target="tpu_custom_call" | custom-call | flops 1 | bytes 1 | tf_op jit(solution)/shard_map/pallas_call | solution.py:43
  68.8 1.5 %collective-permute-start.23 = (bf16[2,96,768]{2,1,0:T(8,128)(2,1)S(1)}, bf16[2,96,768]{2,1,0:T(8,128)(2,1)S(1)}, u32[]{:S(2)}, u32[]{:S(2)}) collective-permute-start(bf16[2,96,768]{2,1,0:T(8,128)(2,1)S(1)} %get-tuple-element.63), channel_id=1, source_target_pairs={{0,16},{8,24},{16,0},{24,8},{1,17},{9,25},{17,1},{25,9},{2,18},{10... | collective-permute-start | bytes 884744 | tf_op jit(solution)/shard_map/ppermute | solution.py:439
  70.8 3.1 %collective-permute-done.19 = f32[2,256]{1,0:T(2,128)S(1)} collective-permute-done((f32[2,256]{1,0:T(2,128)S(1)}, f32[2,256]{1,0:T(2,128)S(1)}, u32[]{:S(2)}, u32[]{:S(2)}) %collective-permute-start.19) | collective-permute-done | bytes 2080 | tf_op jit(solution)/shard_map/ppermute | solution.py:478
  75.9 14.0 %collective-permute-done.23.refs_3_ = bf16[2,96,768]{2,1,0:T(8,128)(2,1)S(1)} collective-permute-done((bf16[2,96,768]{2,1,0:T(8,128)(2,1)S(1)}, bf16[2,96,768]{2,1,0:T(8,128)(2,1)S(1)}, u32[]{:S(2)}, u32[]{:S(2)}) %collective-permute-start.23) | collective-permute-done | bytes 294944 | tf_op jit(solution)/shard_map/ppermute | solution.py:439
  92.5 2.1 %shard_map.97 = (f32[192,2,2048]{2,1,0:T(2,128)}, f32[8,128]{1,0:T(8,128)}) custom-call(bf16[2,2,192,768]{3,2,1,0:T(8,128)(2,1)S(1)} %get-tuple-element.59.refs_7_.refs_0_, bf16[2,2,192,768]{3,2,1,0:T(8,128)(2,1)S(1)} %collective-permute-done.24.refs_1_, bf16[2,192,768]{2,1,0:T(8,128)(2,1)S(1)} %collective-permute-done.25.refs_2_, ...), custom_call_target="tpu_custom_call", output_to_operand_aliasing={{0}: (3, {})} | custom-call | flops 1 | bytes 1 | tf_op jit(solution)/shard_map/pallas_call | solution.py:43
  (63 shorter events, 22.1 us)
Async XLA Ops:
  2.5 10.0 %collective-permute-start.2 = (bf16[144,512]{1,0:T(8,128)(2,1)}, bf16[144,512]{1,0:T(8,128)(2,1)S(1)}, u32[]{:S(2)}, u32[]{:S(2)}) collective-permute-start(bf16[144,512]{1,0:T(8,128)(2,1)} %get-tuple-element.37.refs_0_), channel_id=1, source_target_pairs={{0,2},{1,3},{2,4},{3,5},{4,6},{5,7},{6,0},{7,1},{8,10},{9,11},{10,... | collective-permute-start | bytes 442376 | tf_op jit(solution)/shard_map/ppermute | solution.py:332
  5.6 12.3 %collective-permute-start.3 = (bf16[144,512]{1,0:T(8,128)(2,1)}, bf16[144,512]{1,0:T(8,128)(2,1)S(1)}, u32[]{:S(2)}, u32[]{:S(2)}) collective-permute-start(bf16[144,512]{1,0:T(8,128)(2,1)} %get-tuple-element.37.refs_0_), channel_id=1, source_target_pairs={{0,6},{1,7},{2,0},{3,1},{4,2},{5,3},{6,4},{7,5},{8,14},{9,15},{10,... | collective-permute-start | bytes 442376 | tf_op jit(solution)/shard_map/ppermute | solution.py:332
  12.5 8.7 %collective-permute-start.6 = (bf16[144,512]{1,0:T(8,128)(2,1)S(1)}, bf16[144,512]{1,0:T(8,128)(2,1)S(1)}, u32[]{:S(2)}, u32[]{:S(2)}) collective-permute-start(bf16[144,512]{1,0:T(8,128)(2,1)S(1)} %collective-permute-done.2.refs_1_), channel_id=1, source_target_pairs={{0,2},{1,3},{2,4},{3,5},{4,6},{5,7},{6,0},{7,1},{8,10},{9,11},{10,... | collective-permute-start | bytes 442376 | tf_op jit(solution)/shard_map/ppermute | solution.py:332
  13.7 11.3 %collective-permute-start.4 = (bf16[128,768]{1,0:T(8,128)(2,1)S(1)}, bf16[128,768]{1,0:T(8,128)(2,1)S(1)}, u32[]{:S(2)}, u32[]{:S(2)}) collective-permute-start(bf16[128,768]{1,0:T(8,128)(2,1)S(1)} %get-tuple-element.39.refs_0_), channel_id=1, source_target_pairs={{0,2},{1,3},{2,4},{3,5},{4,6},{5,7},{6,0},{7,1},{8,10},{9,11},{10,... | collective-permute-start | bytes 589832 | tf_op jit(solution)/shard_map/ppermute | solution.py:332
  16.8 9.9 %collective-permute-start.9 = (bf16[128,768]{1,0:T(8,128)(2,1)S(1)}, bf16[128,768]{1,0:T(8,128)(2,1)S(1)}, u32[]{:S(2)}, u32[]{:S(2)}) collective-permute-start(bf16[128,768]{1,0:T(8,128)(2,1)S(1)} %get-tuple-element.39.refs_0_), channel_id=1, source_target_pairs={{0,6},{1,7},{2,0},{3,1},{4,2},{5,3},{6,4},{7,5},{8,14},{9,15},{10,... | collective-permute-start | bytes 589832 | tf_op jit(solution)/shard_map/ppermute | solution.py:332
  18.1 8.9 %collective-permute-start.7 = (bf16[2,96,512]{2,1,0:T(8,128)(2,1)S(1)}, bf16[2,96,512]{2,1,0:T(8,128)(2,1)S(1)}, u32[]{:S(2)}, u32[]{:S(2)}) collective-permute-start(bf16[2,96,512]{2,1,0:T(8,128)(2,1)S(1)} %get-tuple-element.43), channel_id=1, source_target_pairs={{0,1},{1,0},{2,3},{3,2},{4,5},{5,4},{6,7},{7,6},{8,9},{9,8},{10,11... | collective-permute-start | bytes 589832 | tf_op jit(solution)/shard_map/ppermute | solution.py:343
  21.4 5.7 %collective-permute-start.8 = (bf16[2,32,512]{2,1,0:T(8,128)(2,1)S(1)}, bf16[2,32,512]{2,1,0:T(8,128)(2,1)S(1)}, u32[]{:S(2)}, u32[]{:S(2)}) collective-permute-start(bf16[2,32,512]{2,1,0:T(8,128)(2,1)S(1)} %get-tuple-element.44), channel_id=1, source_target_pairs={{0,1},{1,0},{2,3},{3,2},{4,5},{5,4},{6,7},{7,6},{8,9},{9,8},{10,11... | collective-permute-start | bytes 196616 | tf_op jit(solution)/shard_map/ppermute | solution.py:343
  30.1 19.4 %collective-permute-start.12 = (bf16[2,192,512]{2,1,0:T(8,128)(2,1)S(1)}, bf16[2,192,512]{2,1,0:T(8,128)(2,1)S(1)}, u32[]{:S(2)}, u32[]{:S(2)}) collective-permute-start(bf16[2,192,512]{2,1,0:T(8,128)(2,1)S(1)} %shard_map.83.refs_2_), channel_id=1, source_target_pairs={{0,16},{8,24},{16,0},{24,8},{1,17},{9,25},{17,1},{25,9},{2,18},{10... | collective-permute-start | bytes 1179656 | tf_op jit(solution)/shard_map/ppermute | solution.py:439
  31.6 9.7 %collective-permute-start.5 = (bf16[128,768]{1,0:T(8,128)(2,1)S(1)}, bf16[128,768]{1,0:T(8,128)(2,1)S(1)}, u32[]{:S(2)}, u32[]{:S(2)}) collective-permute-start(bf16[128,768]{1,0:T(8,128)(2,1)S(1)} %collective-permute-done.4.refs_1_), channel_id=1, source_target_pairs={{0,2},{1,3},{2,4},{3,5},{4,6},{5,7},{6,0},{7,1},{8,10},{9,11},{10,... | collective-permute-start | bytes 589832 | tf_op jit(solution)/shard_map/ppermute | solution.py:332
  32.2 17.3 %collective-permute-start.13 = (bf16[2,96,768]{2,1,0:T(8,128)(2,1)S(1)}, bf16[2,96,768]{2,1,0:T(8,128)(2,1)S(1)}, u32[]{:S(2)}, u32[]{:S(2)}) collective-permute-start(bf16[2,96,768]{2,1,0:T(8,128)(2,1)S(1)} %get-tuple-element.50), channel_id=1, source_target_pairs={{0,1},{1,0},{2,3},{3,2},{4,5},{5,4},{6,7},{7,6},{8,9},{9,8},{10,11... | collective-permute-start | bytes 884744 | tf_op jit(solution)/shard_map/ppermute | solution.py:343
  33.7 11.8 %collective-permute-start = (bf16[128,768]{1,0:T(8,128)(2,1)S(1)}, bf16[128,768]{1,0:T(8,128)(2,1)S(1)}, u32[]{:S(2)}, u32[]{:S(2)}) collective-permute-start(bf16[128,768]{1,0:T(8,128)(2,1)S(1)} %get-tuple-element.36.refs_0_), channel_id=1, source_target_pairs={{0,2},{1,3},{2,4},{3,5},{4,6},{5,7},{6,0},{7,1},{8,10},{9,11},{10,... | collective-permute-start | bytes 589832 | tf_op jit(solution)/shard_map/ppermute | solution.py:332
  34.3 14.2 %collective-permute-start.1 = (bf16[128,768]{1,0:T(8,128)(2,1)S(1)}, bf16[128,768]{1,0:T(8,128)(2,1)S(1)}, u32[]{:S(2)}, u32[]{:S(2)}) collective-permute-start(bf16[128,768]{1,0:T(8,128)(2,1)S(1)} %get-tuple-element.36.refs_0_), channel_id=1, source_target_pairs={{0,6},{1,7},{2,0},{3,1},{4,2},{5,3},{6,4},{7,5},{8,14},{9,15},{10,... | collective-permute-start | bytes 589832 | tf_op jit(solution)/shard_map/ppermute | solution.py:332
  41.6 7.9 %collective-permute-start.14 = (bf16[2,32,768]{2,1,0:T(8,128)(2,1)S(1)}, bf16[2,32,768]{2,1,0:T(8,128)(2,1)S(1)}, u32[]{:S(2)}, u32[]{:S(2)}) collective-permute-start(bf16[2,32,768]{2,1,0:T(8,128)(2,1)S(1)} %get-tuple-element.51), channel_id=1, source_target_pairs={{0,1},{1,0},{2,3},{3,2},{4,5},{5,4},{6,7},{7,6},{8,9},{9,8},{10,11... | collective-permute-start | bytes 294920 | tf_op jit(solution)/shard_map/ppermute | solution.py:343
  50.3 2.9 %collective-permute-start.15 = (bf16[2,2,192,768]{3,2,1,0:T(8,128)(2,1)S(1)}, bf16[2,2,192,768]{3,2,1,0:T(8,128)(2,1)S(1)}, u32[]{:S(2)}, u32[]{:S(2)}) collective-permute-start(bf16[2,2,192,768]{3,2,1,0:T(8,128)(2,1)S(1)} %get-tuple-element.53), channel_id=1, source_target_pairs={{0,8},{8,0},{16,24},{24,16},{1,9},{9,1},{17,25},{25,17},{2,10},{10... | collective-permute-start | bytes 3538952 | tf_op jit(solution)/shard_map/ppermute | solution.py:429
  50.4 9.1 %collective-permute-start.11 = (bf16[128,768]{1,0:T(8,128)(2,1)S(1)}, bf16[128,768]{1,0:T(8,128)(2,1)S(1)}, u32[]{:S(2)}, u32[]{:S(2)}) collective-permute-start(bf16[128,768]{1,0:T(8,128)(2,1)S(1)} %collective-permute-done.refs_1_), channel_id=1, source_target_pairs={{0,2},{1,3},{2,4},{3,5},{4,6},{5,7},{6,0},{7,1},{8,10},{9,11},{10,... | collective-permute-start | bytes 589832 | tf_op jit(solution)/shard_map/ppermute | solution.py:332
  51.0 10.2 %collective-permute-start.16 = (bf16[2,96,768]{2,1,0:T(8,128)(2,1)S(1)}, bf16[2,96,768]{2,1,0:T(8,128)(2,1)S(1)}, u32[]{:S(2)}, u32[]{:S(2)}) collective-permute-start(bf16[2,96,768]{2,1,0:T(8,128)(2,1)S(1)} %get-tuple-element.57), channel_id=1, source_target_pairs={{0,1},{1,0},{2,3},{3,2},{4,5},{5,4},{6,7},{7,6},{8,9},{9,8},{10,11... | collective-permute-start | bytes 884744 | tf_op jit(solution)/shard_map/ppermute | solution.py:343
  53.3 11.0 %collective-permute-start.18 = (bf16[2,96,768]{2,1,0:T(8,128)(2,1)S(1)}, bf16[2,96,768]{2,1,0:T(8,128)(2,1)S(1)}, u32[]{:S(2)}, u32[]{:S(2)}) collective-permute-start(bf16[2,96,768]{2,1,0:T(8,128)(2,1)S(1)} %get-tuple-element.54.refs_3_), channel_id=1, source_target_pairs={{0,16},{8,24},{16,0},{24,8},{1,17},{9,25},{17,1},{25,9},{2,18},{10... | collective-permute-start | bytes 884744 | tf_op jit(solution)/shard_map/ppermute | solution.py:439
  59.7 4.7 %collective-permute-start.17 = (bf16[2,32,768]{2,1,0:T(8,128)(2,1)S(1)}, bf16[2,32,768]{2,1,0:T(8,128)(2,1)S(1)}, u32[]{:S(2)}, u32[]{:S(2)}) collective-permute-start(bf16[2,32,768]{2,1,0:T(8,128)(2,1)S(1)} %get-tuple-element.58), channel_id=1, source_target_pairs={{0,1},{1,0},{2,3},{3,2},{4,5},{5,4},{6,7},{7,6},{8,9},{9,8},{10,11... | collective-permute-start | bytes 294920 | tf_op jit(solution)/shard_map/ppermute | solution.py:343
  68.2 24.3 %collective-permute-start.25 = (bf16[2,192,768]{2,1,0:T(8,128)(2,1)S(1)}, bf16[2,192,768]{2,1,0:T(8,128)(2,1)S(1)}, u32[]{:S(2)}, u32[]{:S(2)}) collective-permute-start(bf16[2,192,768]{2,1,0:T(8,128)(2,1)S(1)} %shard_map.94.refs_5_), channel_id=1, source_target_pairs={{0,16},{8,24},{16,0},{24,8},{1,17},{9,25},{17,1},{25,9},{2,18},{10... | collective-permute-start | bytes 1769480 | tf_op jit(solution)/shard_map/ppermute | solution.py:439
  68.8 21.2 %collective-permute-start.23 = (bf16[2,96,768]{2,1,0:T(8,128)(2,1)S(1)}, bf16[2,96,768]{2,1,0:T(8,128)(2,1)S(1)}, u32[]{:S(2)}, u32[]{:S(2)}) collective-permute-start(bf16[2,96,768]{2,1,0:T(8,128)(2,1)S(1)} %get-tuple-element.63), channel_id=1, source_target_pairs={{0,16},{8,24},{16,0},{24,8},{1,17},{9,25},{17,1},{25,9},{2,18},{10... | collective-permute-start | bytes 884744 | tf_op jit(solution)/shard_map/ppermute | solution.py:439
  70.3 3.6 %collective-permute-start.19 = (f32[2,256]{1,0:T(2,128)S(1)}, f32[2,256]{1,0:T(2,128)S(1)}, u32[]{:S(2)}, u32[]{:S(2)}) collective-permute-start(f32[2,256]{1,0:T(2,128)S(1)} %get-tuple-element.62.refs_2_), channel_id=1, source_target_pairs={{0,1},{1,0},{2,3},{3,2},{4,5},{5,4},{6,7},{7,6},{8,9},{9,8},{10,11... | collective-permute-start | bytes 6152 | tf_op jit(solution)/shard_map/ppermute | solution.py:478
  73.9 17.5 %collective-permute-start.20 = (f32[2,2,256]{2,1,0:T(2,128)S(1)}, f32[2,2,256]{2,1,0:T(2,128)S(1)}, u32[]{:S(2)}, u32[]{:S(2)}) collective-permute-start(f32[2,2,256]{2,1,0:T(2,128)S(1)} %pad_maximum_fusion.refs_2_), channel_id=1, source_target_pairs={{2,0},{3,1},{4,2},{5,3},{6,4},{7,5},{0,6},{1,7},{10,8},{11,9},{12,... | collective-permute-start | bytes 12296 | tf_op jit(solution)/shard_map/ppermute | solution.py:480
  75.0 16.4 %collective-permute-start.21 = (f32[2,2,256]{2,1,0:T(2,128)S(1)}, f32[2,2,256]{2,1,0:T(2,128)S(1)}, u32[]{:S(2)}, u32[]{:S(2)}) collective-permute-start(f32[2,2,256]{2,1,0:T(2,128)S(1)} %pad_maximum_fusion.refs_2_), channel_id=1, source_target_pairs={{4,0},{5,1},{6,2},{7,3},{0,4},{1,5},{2,6},{3,7},{12,8},{13,9},{14,... | collective-permute-start | bytes 12296 | tf_op jit(solution)/shard_map/ppermute | solution.py:480
  75.0 16.5 %collective-permute-start.22 = (f32[2,2,256]{2,1,0:T(2,128)S(1)}, f32[2,2,256]{2,1,0:T(2,128)S(1)}, u32[]{:S(2)}, u32[]{:S(2)}) collective-permute-start(f32[2,2,256]{2,1,0:T(2,128)S(1)} %pad_maximum_fusion.refs_2_), channel_id=1, source_target_pairs={{6,0},{7,1},{0,2},{1,3},{2,4},{3,5},{4,6},{5,7},{14,8},{15,9},{8,1... | collective-permute-start | bytes 12296 | tf_op jit(solution)/shard_map/ppermute | solution.py:480
  (8 other events, 52.7 us)

commit v11 on v10

--- a/solution.py
+++ b/solution.py
@@ -136,13 +136,13 @@
     share, across = units // dp, dp // 2
     me = lax.axis_index("expert") if parts > 1 else 0
     mine = lax.axis_index("dp")
-    core, row = mine % 2, mine // 2
+    row = mine // 2
     for e in range(held):
         sources = [source_of(me, p) if parts > 1 else 0 for p in range(parts)]
         stacked = jnp.concatenate([hidden_ref[source, e] for source in sources], axis=0)
         turned = stacked.T
         for piece in range(dp):
-            other = (piece % 2) ^ core
+            other = piece % 2
             step = (piece // 2 - row + across) % across
             out_ref[e, other, step] = turned[piece * share : (piece + 1) * share]
 
@@ -165,37 +165,37 @@
 
 
 def term_kernel(turned_ref, *refs):
-    part_refs, keep_ref, give_ref = refs[:-2], refs[-2], refs[-1]
-    held, _, across, share, slots = turned_ref.shape
+    part_refs, out_ref = refs[:-1], refs[-1]
+    held, cores, across, share, slots = turned_ref.shape
     for e in range(held):
         scaled = stacked_rows(part_refs, e)
-        for other, ref in ((1, give_ref), (0, keep_ref)):
-            left = turned_ref[e, other].reshape(across * share, slots)
+        for core in range(cores):
+            left = turned_ref[e, core].reshape(across * share, slots)
             term = jnp.dot(left, scaled, preferred_element_type=F32).astype(BF16)
             for step in range(across):
-                ref[step, e] = term[step * share : (step + 1) * share]
-
-
-def pair_kernel(cuts, keep_ref, got_ref, *out_refs):
+                out_ref[core, step, e] = term[step * share : (step + 1) * share]
+
+
+def pair_kernel(cuts, both_ref, *out_refs):
     out_refs = iter(out_refs)
-    for step in range(1, keep_ref.shape[0]):
+    for step in range(1, both_ref.shape[1]):
         start = 0
         for rows in cuts:
             at = slice(start, start + rows)
-            pair = keep_ref[step, :, at].astype(F32) + got_ref[step, :, at].astype(F32)
+            pair = both_ref[0, step, :, at].astype(F32) + both_ref[1, step, :, at].astype(F32)
             next(out_refs)[...] = pair.astype(BF16)
             start += rows
 
 
-def last_kernel(cuts, start, keep_ref, got_ref, *refs):
+def last_kernel(cuts, start, both_ref, *refs):
     out_ref, mark_ref, total_ref, sem = refs[-4:]
     mark_ref[...] = jnp.zeros(mark_ref.shape, F32)
-    others = len(cuts) * (keep_ref.shape[0] - 1)
-    for e in range(keep_ref.shape[1]):
+    others = len(cuts) * (both_ref.shape[1] - 1)
+    for e in range(both_ref.shape[2]):
         row = 0
         for part, rows in enumerate(cuts):
             at = slice(row, row + rows)
-            total = keep_ref[0, e, at].astype(F32) + got_ref[0, e, at].astype(F32)
+            total = both_ref[0, 0, e, at].astype(F32) + both_ref[1, 0, e, at].astype(F32)
             for ref in refs[part : others : len(cuts)]:
                 total = total + ref[e].astype(F32)
             total_ref[at, e, :] = total
@@ -287,7 +287,7 @@
 
 def cuts_of(share, c):
     first = 16 * (share // 32)
-    return [first, share - first] if c == 1 else [share]
+    return [share]
 
 
 sds = jax.ShapeDtypeStruct
@@ -423,31 +423,35 @@
 
     def reduced(c):
         parts, width = arrived[c], widths[c]
-        piece = sds((across, held, share, width), BF16)
-        after = summed[-1][2][:1] if c else ()
-        keep, give = call(term_kernel, [piece, piece], turned, *parts, after=after)
-        got = lax.ppermute(give, "dp", [(i, i ^ 1) for i in range(dp)])
+        piece = sds((2, across, held, share, width), BF16)
+        both = lax.all_to_all(
+            call(term_kernel, piece, turned, *parts),
+            "dp",
+            0,
+            0,
+            axis_index_groups=[[i, i + 1] for i in range(0, dp, 2)],
+            tiled=True,
+        )
         if c == count - 1:
             accumulated(c)
         cuts = cuts_of(share, c)
         pieces = [sds((held, rows, width), BF16) for rows in cuts]
-        pairs = call(functools.partial(pair_kernel, cuts), pieces * (across - 1), keep, got)
+        pairs = call(functools.partial(pair_kernel, cuts), pieces * (across - 1), both)
         others = []
         for i, pair in enumerate(pairs):
             step = 1 + i // len(cuts)
             shift = [(2 * r + k, 2 * ((r + step) % across) + k) for r in range(across) for k in range(2)]
             others.append(lax.ppermute(pair, "dp", shift))
-        summed.append((keep, got, others))
+        summed.append((both, others))
 
     def finished(c):
-        keep, got, others = summed[c]
+        both, others = summed[c]
         before = [] if state["grad"] is None else [state["grad"]]
-        count = 2 + len(others)
+        count = 1 + len(others)
         state["grad"], _ = call(
             functools.partial(last_kernel, cuts_of(share, c), starts[c]),
             [sds((share, held, features), F32), sds((8, 128), F32)],
-            keep,
-            got,
+            both,
             *others,
             *before,
             in_specs=[VMEM] * count + [ANY] * len(before),
@@ -469,7 +473,7 @@
         if c >= 1:
             accumulated(c - 1)
         reduced(c)
-        if c >= 1:
+        if 1 <= c < count - 1:
             finished(c - 1)
     hidden_grad, sums = state["raw"]
 
@@ -493,7 +497,8 @@
         *returned,
         keep=False,
     ).T
-    finished(count - 1)
+    for c in range(max(0, count - 2), count):
+        finished(c)
     weight_grad = state["grad"]
     return (hidden_grad.reshape(hidden.shape), prob_grad, weight_grad)
 

time: 94.7 us -> 110 us (1.16)
  waiting for transfers between devices: 47.7 us -> 30.3 us
  local copies, waits for them, and re-layouts: 1.06 us -> 14.8 us
  blocking collectives: 0 us -> 10.9 us
  Pallas kernels: 15 us -> 20 us
  starting transfers between devices: 29.8 us -> 32.5 us
    unnamed x12 -> x34, local copies, waits for them, and re-layouts: 1.06 us -> 14.8 us
    ppermute x4 -> x3, waiting for transfers between devices: 14 us -> 0.41 us  [reduced(): others.append(lax.ppermute(pair, 'dp', shift))]
    all_to_all x0 -> x2, blocking collectives: none -> 10.9 us  [reduced(): lax.all_to_all(call(term_kernel, piece, turned, *parts), 'dp', 0, 0, axis...]
    ppermute x9, waiting for transfers between devices: 23.4 us -> 13.4 us  [along(): return lax.ppermute(block, 'expert', pairs)]
    ppermute x6, waiting for transfers between devices: 3.22 us -> 9.71 us  [pick(): lax.ppermute(other, 'expert', [(i, i ^ 1) for i in range(LINE * SIDES)])]
    all_to_all x0 -> x1, starting transfers between devices: none -> 5.1 us  [reduced(): lax.all_to_all(call(term_kernel, piece, turned, *parts), 'dp', 0, 0, axis...]
    pallas_call x22, Pallas kernels: 15 us -> 20 us  [__call__(): pl.pallas_call(body, out_shape=outs, in_specs=in_specs, compiler_params=p...]
    ppermute x3, waiting for transfers between devices: 0.01 us -> 4.47 us  [body(): lax.ppermute(both, 'expert', [(moved(i, d, 0), i) for i in range(groups)])]
  transfers between devices with their start and end apart: 26 -> 23, of which waited for: 14 -> 11; matrix products, arithmetic and copies ran while one was open for 0% -> 0% of each run, Pallas kernels for 9% -> 13%
where the time goes in v11:
time: 110 us; the launch traced here: 109 us
  starting transfers between devices  32.5 us (30%)
  waiting for transfers between devices  30.3 us (28%)
  Pallas kernels  20 us (18%)
  local copies, waits for them, and re-layouts  14.8 us (13%)
  blocking collectives  10.9 us (10%)
    pallas_call x22, Pallas kernels, __call__(): pl.pallas_call(body, out_shape=outs, in_specs=in_specs, compiler_params=p...  20 us
    unnamed x34, local copies, waits for them, and re-layouts  14.8 us
    ppermute x9, waiting for transfers between devices, along(): return lax.ppermute(block, 'expert', pairs)  13.4 us
    ppermute x9, starting transfers between devices, along(): return lax.ppermute(block, 'expert', pairs)  11.8 us
    all_to_all x2, blocking collectives, reduced(): lax.all_to_all(call(term_kernel, piece, turned, *parts), 'dp', 0, 0, axis...  10.9 us
    ppermute x6, waiting for transfers between devices, pick(): lax.ppermute(other, 'expert', [(i, i ^ 1) for i in range(LINE * SIDES)])  9.71 us
    ppermute x6, starting transfers between devices, pick(): lax.ppermute(other, 'expert', [(i, i ^ 1) for i in range(LINE * SIDES)])  8.1 us
    all_to_all x1, starting transfers between devices, reduced(): lax.all_to_all(call(term_kernel, piece, turned, *parts), 'dp', 0, 0, axis...  5.1 us
  transfers between devices with their start and end apart: 23, of which 11 were waited for; matrix products, arithmetic and copies ran while one was open for 0% of the time, Pallas kernels for 13%

profile of v11, /device:TPU:0, one launch (start us, length us, event | category | flops | bytes accessed | tf_op | source)
XLA Modules:
  0.0 109.4 jit_solution(2778784384266495824)
XLA Ops:
  0.6 1.8 %shard_map.77 = (s32[2,128]{1,0:T(2,128)}, bf16[144,512]{1,0:T(8,128)(2,1)}) custom-call(s32[2,128]{1,0:T(2,128)} %bitcast.15, f32[2,128]{1,0:T(2,128)} %bitcast.12, bf16[128,2048]{1,0:T(8,128)(2,1)} %rows_ref.3), custom_call_target="tpu_custom_call" | custom-call | flops 1 | bytes 1 | tf_op jit(solution)/shard_map/pallas_call | solution.py:43
  2.4 3.1 %collective-permute-start.2 = (bf16[144,512]{1,0:T(8,128)(2,1)}, bf16[144,512]{1,0:T(8,128)(2,1)S(1)}, u32[]{:S(2)}, u32[]{:S(2)}) collective-permute-start(bf16[144,512]{1,0:T(8,128)(2,1)} %get-tuple-element.29.refs_0_), channel_id=1, source_target_pairs={{0,2},{1,3},{2,4},{3,5},{4,6},{5,7},{6,0},{7,1},{8,10},{9,11},{10,... | collective-permute-start | bytes 442376 | tf_op jit(solution)/shard_map/ppermute | solution.py:332
  5.5 2.1 %collective-permute-start.3 = (bf16[144,512]{1,0:T(8,128)(2,1)}, bf16[144,512]{1,0:T(8,128)(2,1)S(1)}, u32[]{:S(2)}, u32[]{:S(2)}) collective-permute-start(bf16[144,512]{1,0:T(8,128)(2,1)} %get-tuple-element.29.refs_0_), channel_id=1, source_target_pairs={{0,6},{1,7},{2,0},{3,1},{4,2},{5,3},{6,4},{7,5},{8,14},{9,15},{10,... | collective-permute-start | bytes 442376 | tf_op jit(solution)/shard_map/ppermute | solution.py:332
  7.6 4.9 %collective-permute-done.2.refs_1_ = bf16[144,512]{1,0:T(8,128)(2,1)S(1)} collective-permute-done((bf16[144,512]{1,0:T(8,128)(2,1)}, bf16[144,512]{1,0:T(8,128)(2,1)S(1)}, u32[]{:S(2)}, u32[]{:S(2)}) %collective-permute-start.2) | collective-permute-done | bytes 147488 | tf_op jit(solution)/shard_map/ppermute | solution.py:332
  13.6 3.1 %collective-permute-start.4 = (bf16[128,768]{1,0:T(8,128)(2,1)S(1)}, bf16[128,768]{1,0:T(8,128)(2,1)S(1)}, u32[]{:S(2)}, u32[]{:S(2)}) collective-permute-start(bf16[128,768]{1,0:T(8,128)(2,1)S(1)} %get-tuple-element.31.refs_0_), channel_id=1, source_target_pairs={{0,2},{1,3},{2,4},{3,5},{4,6},{5,7},{6,0},{7,1},{8,10},{9,11},{10,... | collective-permute-start | bytes 589832 | tf_op jit(solution)/shard_map/ppermute | solution.py:332
  20.1 1.8 %collective-permute-start.7 = (bf16[2,96,512]{2,1,0:T(8,128)(2,1)S(1)}, bf16[2,96,512]{2,1,0:T(8,128)(2,1)S(1)}, u32[]{:S(2)}, u32[]{:S(2)}) collective-permute-start(bf16[2,96,512]{2,1,0:T(8,128)(2,1)S(1)} %get-tuple-element.35), channel_id=1, source_target_pairs={{0,1},{1,0},{2,3},{3,2},{4,5},{5,4},{6,7},{7,6},{8,9},{9,8},{10,11... | collective-permute-start | bytes 589832 | tf_op jit(solution)/shard_map/ppermute | solution.py:343
  23.6 1.8 %collective-permute-done.4.refs_1_ = bf16[128,768]{1,0:T(8,128)(2,1)S(1)} collective-permute-done((bf16[128,768]{1,0:T(8,128)(2,1)S(1)}, bf16[128,768]{1,0:T(8,128)(2,1)S(1)}, u32[]{:S(2)}, u32[]{:S(2)}) %collective-permute-start.4) | collective-permute-done | bytes 196640 | tf_op jit(solution)/shard_map/ppermute | solution.py:332
  25.5 3.4 %collective-permute-done.9.refs_2_ = bf16[128,768]{1,0:T(8,128)(2,1)S(1)} collective-permute-done((bf16[128,768]{1,0:T(8,128)(2,1)S(1)}, bf16[128,768]{1,0:T(8,128)(2,1)S(1)}, u32[]{:S(2)}, u32[]{:S(2)}) %collective-permute-start.9) | collective-permute-done | bytes 196640 | tf_op jit(solution)/shard_map/ppermute | solution.py:332
  29.8 5.3 %all_to_all.15.refs_0_ = bf16[2,2,2,192,512]{4,3,2,1,0:T(8,128)(2,1)S(1)} all-to-all(bf16[2,2,2,192,512]{4,3,2,1,0:T(8,128)(2,1)S(1)} %shard_map.82.refs_1_), channel_id=1, replica_groups={{0,8},{16,24},{1,9},{17,25},{2,10},{18,26},{3,11},{19,27},{4,12},{20,28..., dimensions={0} | all-to-all | bytes 3145728 | tf_op jit(solution)/shard_map/all_to_all | solution.py:427
  35.2 1.9 %collective-permute-start.11 = (bf16[2,192,512]{2,1,0:T(8,128)(2,1)S(1)}, bf16[2,192,512]{2,1,0:T(8,128)(2,1)S(1)}, u32[]{:S(2)}, u32[]{:S(2)}) collective-permute-start(bf16[2,192,512]{2,1,0:T(8,128)(2,1)S(1)} %shard_map.83.refs_2_), channel_id=1, source_target_pairs={{0,16},{8,24},{16,0},{24,8},{1,17},{9,25},{17,1},{25,9},{2,18},{10... | collective-permute-start | bytes 1179656 | tf_op jit(solution)/shard_map/ppermute | solution.py:444
  40.8 3.3 %collective-permute-done.1.refs_2_ = bf16[128,768]{1,0:T(8,128)(2,1)S(1)} collective-permute-done((bf16[128,768]{1,0:T(8,128)(2,1)S(1)}, bf16[128,768]{1,0:T(8,128)(2,1)S(1)}, u32[]{:S(2)}, u32[]{:S(2)}) %collective-permute-start.1) | collective-permute-done | bytes 196640 | tf_op jit(solution)/shard_map/ppermute | solution.py:332
  44.5 2.2 %collective-permute-start.14 = (bf16[2,96,768]{2,1,0:T(8,128)(2,1)S(1)}, bf16[2,96,768]{2,1,0:T(8,128)(2,1)S(1)}, u32[]{:S(2)}, u32[]{:S(2)}) collective-permute-start(bf16[2,96,768]{2,1,0:T(8,128)(2,1)S(1)} %get-tuple-element.44), channel_id=1, source_target_pairs={{0,1},{1,0},{2,3},{3,2},{4,5},{5,4},{6,7},{7,6},{8,9},{9,8},{10,11... | collective-permute-start | bytes 884744 | tf_op jit(solution)/shard_map/ppermute | solution.py:343
  47.4 7.7 %collective-permute-done.13.refs_4_ = bf16[2,32,768]{2,1,0:T(8,128)(2,1)S(1)} collective-permute-done((bf16[2,32,768]{2,1,0:T(8,128)(2,1)S(1)}, bf16[2,32,768]{2,1,0:T(8,128)(2,1)S(1)}, u32[]{:S(2)}, u32[]{:S(2)}) %collective-permute-start.13) | collective-permute-done | bytes 98336 | tf_op jit(solution)/shard_map/ppermute | solution.py:343
  55.9 5.6 %all_to_all.16.refs_0_ = bf16[2,2,2,192,768]{4,3,2,1,0:T(8,128)(2,1)S(1)} all-to-all(bf16[2,2,2,192,768]{4,3,2,1,0:T(8,128)(2,1)S(1)} %shard_map.87.refs_1_), channel_id=1, replica_groups={{0,8},{16,24},{1,9},{17,25},{2,10},{18,26},{3,11},{19,27},{4,12},{20,28..., dimensions={0} | all-to-all | bytes 4718592 | tf_op jit(solution)/shard_map/all_to_all | solution.py:427
  66.7 2.0 %collective-permute-done.15.refs_4_ = bf16[2,32,768]{2,1,0:T(8,128)(2,1)S(1)} collective-permute-done((bf16[2,32,768]{2,1,0:T(8,128)(2,1)S(1)}, bf16[2,32,768]{2,1,0:T(8,128)(2,1)S(1)}, u32[]{:S(2)}, u32[]{:S(2)}) %collective-permute-start.15) | collective-permute-done | bytes 98336 | tf_op jit(solution)/shard_map/ppermute | solution.py:343
  73.5 5.1 %all-to-all-start.2 = ((bf16[2,2,2,192,768]{4,3,2,1,0:T(8,128)(2,1)}), bf16[2,2,2,192,768]{4,3,2,1,0:T(8,128)(2,1)}, u32[]{:S(2)}, u32[]{:S(2)}) async-start(bf16[2,2,2,192,768]{4,3,2,1,0:T(8,128)(2,1)} %copy-done.1), calls=%async_computation.2 | async-start | bytes 4718592 | tf_op jit(solution)/shard_map/all_to_all | solution.py:427
  78.6 2.8 %copy-done = bf16[2,768,2048]{2,1,0:T(8,128)(2,1)S(1)} copy-done((bf16[2,768,2048]{2,1,0:T(8,128)(2,1)S(1)}, bf16[2,768,2048]{2,1,0:T(8,128)(2,1)}, u32[]{:S(2)}) %copy-start) | copy-done | bytes 6291480
  86.3 1.8 %shard_map.93 = (bf16[8,2,32,768]{3,2,1,0:T(8,128)(2,1)}, f32[2,256]{1,0:T(2,128)S(1)}) custom-call(bf16[2,768,2048]{2,1,0:T(8,128)(2,1)S(1)} %copy-done, bf16[2,96,768]{2,1,0:T(8,128)(2,1)S(1)} %get-tuple-element.39.refs_5_.refs_1_, bf16[2,32,768]{2,1,0:T(8,128)(2,1)S(1)} %get-tuple-element.43.refs_6_.refs_2_, bf16[2,96,768]{2,1,0:T(8,128)(2,1)S(1)} %copy-done.9, ...), custom_call_target="tpu_custom_call" | custom-call | flops 1 | bytes 1 | tf_op jit(solution)/shard_map/pallas_call | solution.py:43
  88.1 1.8 %shard_map.94.refs_6_.refs_3_ = bf16[2,192,768]{2,1,0:T(8,128)(2,1)S(1)} custom-call(bf16[2,2,2,192,768]{4,3,2,1,0:T(8,128)(2,1)} %all-to-all-done.2.refs_0_, f32[2,256]{1,0:T(2,128)S(1)} %get-tuple-element.48.refs_1_), custom_call_target="tpu_custom_call" | custom-call | flops 1 | bytes 1 | tf_op jit(solution)/shard_map/pallas_call | solution.py:43
  92.0 2.4 %collective-permute-done.16 = f32[2,256]{1,0:T(2,128)S(1)} collective-permute-done((f32[2,256]{1,0:T(2,128)S(1)}, f32[2,256]{1,0:T(2,128)S(1)}, u32[]{:S(2)}, u32[]{:S(2)}) %collective-permute-start.16) | collective-permute-done | bytes 2080 | tf_op jit(solution)/shard_map/ppermute | solution.py:482
  94.3 2.0 %collective-permute-start.17 = (f32[2,2,256]{2,1,0:T(2,128)S(1)}, f32[2,2,256]{2,1,0:T(2,128)S(1)}, u32[]{:S(2)}, u32[]{:S(2)}) collective-permute-start(f32[2,2,256]{2,1,0:T(2,128)S(1)} %pad_maximum_fusion.refs_2_), channel_id=1, source_target_pairs={{2,0},{3,1},{4,2},{5,3},{6,4},{7,5},{0,6},{1,7},{10,8},{11,9},{12,... | collective-permute-start | bytes 12296 | tf_op jit(solution)/shard_map/ppermute | solution.py:484
  98.0 2.9 %collective-permute-done.18.refs_4_ = f32[2,2,256]{2,1,0:T(2,128)S(1)} collective-permute-done((f32[2,2,256]{2,1,0:T(2,128)S(1)}, f32[2,2,256]{2,1,0:T(2,128)S(1)}, u32[]{:S(2)}, u32[]{:S(2)}) %collective-permute-start.18) | collective-permute-done | bytes 4128 | tf_op jit(solution)/shard_map/ppermute | solution.py:484
  102.8 2.5 %shard_map.96 = (f32[192,2,2048]{2,1,0:T(2,128)}, f32[8,128]{1,0:T(8,128)S(1)}) custom-call(bf16[2,2,2,192,768]{4,3,2,1,0:T(8,128)(2,1)S(1)} %all_to_all.16.refs_0_, bf16[2,192,768]{2,1,0:T(8,128)(2,1)} %collective-permute-done.21.refs_1_, f32[192,2,2048]{2,1,0:T(2,128)} %get-tuple-element.49.refs_2_, ...), custom_call_target="tpu_custom_call", output_to_operand_aliasing={{0}: (2, {})} | custom-call | flops 1 | bytes 1 | tf_op jit(solution)/shard_map/pallas_call | solution.py:43
  105.7 3.7 %shard_map.97 = (f32[192,2,2048]{2,1,0:T(2,128)}, f32[8,128]{1,0:T(8,128)}) custom-call(bf16[2,2,2,192,768]{4,3,2,1,0:T(8,128)(2,1)} %all-to-all-done.2.refs_0_, bf16[2,192,768]{2,1,0:T(8,128)(2,1)S(1)} %collective-permute-done.20.refs_1_, f32[192,2,2048]{2,1,0:T(2,128)} %get-tuple-element.50.refs_2_, ...), custom_call_target="tpu_custom_call", output_to_operand_aliasing={{0}: (2, {})} | custom-call | flops 1 | bytes 1 | tf_op jit(solution)/shard_map/pallas_call | solution.py:43
  (82 shorter events, 33.7 us)
Async XLA Ops:
  2.4 10.0 %collective-permute-start.2 = (bf16[144,512]{1,0:T(8,128)(2,1)}, bf16[144,512]{1,0:T(8,128)(2,1)S(1)}, u32[]{:S(2)}, u32[]{:S(2)}) collective-permute-start(bf16[144,512]{1,0:T(8,128)(2,1)} %get-tuple-element.29.refs_0_), channel_id=1, source_target_pairs={{0,2},{1,3},{2,4},{3,5},{4,6},{5,7},{6,0},{7,1},{8,10},{9,11},{10,... | collective-permute-start | bytes 442376 | tf_op jit(solution)/shard_map/ppermute | solution.py:332
  5.5 13.4 %collective-permute-start.3 = (bf16[144,512]{1,0:T(8,128)(2,1)}, bf16[144,512]{1,0:T(8,128)(2,1)S(1)}, u32[]{:S(2)}, u32[]{:S(2)}) collective-permute-start(bf16[144,512]{1,0:T(8,128)(2,1)} %get-tuple-element.29.refs_0_), channel_id=1, source_target_pairs={{0,6},{1,7},{2,0},{3,1},{4,2},{5,3},{6,4},{7,5},{8,14},{9,15},{10,... | collective-permute-start | bytes 442376 | tf_op jit(solution)/shard_map/ppermute | solution.py:332
  12.4 9.4 %collective-permute-start.6 = (bf16[144,512]{1,0:T(8,128)(2,1)S(1)}, bf16[144,512]{1,0:T(8,128)(2,1)S(1)}, u32[]{:S(2)}, u32[]{:S(2)}) collective-permute-start(bf16[144,512]{1,0:T(8,128)(2,1)S(1)} %collective-permute-done.2.refs_1_), channel_id=1, source_target_pairs={{0,2},{1,3},{2,4},{3,5},{4,6},{5,7},{6,0},{7,1},{8,10},{9,11},{10,... | collective-permute-start | bytes 442376 | tf_op jit(solution)/shard_map/ppermute | solution.py:332
  13.6 11.9 %collective-permute-start.4 = (bf16[128,768]{1,0:T(8,128)(2,1)S(1)}, bf16[128,768]{1,0:T(8,128)(2,1)S(1)}, u32[]{:S(2)}, u32[]{:S(2)}) collective-permute-start(bf16[128,768]{1,0:T(8,128)(2,1)S(1)} %get-tuple-element.31.refs_0_), channel_id=1, source_target_pairs={{0,2},{1,3},{2,4},{3,5},{4,6},{5,7},{6,0},{7,1},{8,10},{9,11},{10,... | collective-permute-start | bytes 589832 | tf_op jit(solution)/shard_map/ppermute | solution.py:332
  16.7 12.2 %collective-permute-start.9 = (bf16[128,768]{1,0:T(8,128)(2,1)S(1)}, bf16[128,768]{1,0:T(8,128)(2,1)S(1)}, u32[]{:S(2)}, u32[]{:S(2)}) collective-permute-start(bf16[128,768]{1,0:T(8,128)(2,1)S(1)} %get-tuple-element.31.refs_0_), channel_id=1, source_target_pairs={{0,6},{1,7},{2,0},{3,1},{4,2},{5,3},{6,4},{7,5},{8,14},{9,15},{10,... | collective-permute-start | bytes 589832 | tf_op jit(solution)/shard_map/ppermute | solution.py:332
  20.1 9.1 %collective-permute-start.7 = (bf16[2,96,512]{2,1,0:T(8,128)(2,1)S(1)}, bf16[2,96,512]{2,1,0:T(8,128)(2,1)S(1)}, u32[]{:S(2)}, u32[]{:S(2)}) collective-permute-start(bf16[2,96,512]{2,1,0:T(8,128)(2,1)S(1)} %get-tuple-element.35), channel_id=1, source_target_pairs={{0,1},{1,0},{2,3},{3,2},{4,5},{5,4},{6,7},{7,6},{8,9},{9,8},{10,11... | collective-permute-start | bytes 589832 | tf_op jit(solution)/shard_map/ppermute | solution.py:343
  22.0 7.2 %collective-permute-start.8 = (bf16[2,32,512]{2,1,0:T(8,128)(2,1)S(1)}, bf16[2,32,512]{2,1,0:T(8,128)(2,1)S(1)}, u32[]{:S(2)}, u32[]{:S(2)}) collective-permute-start(bf16[2,32,512]{2,1,0:T(8,128)(2,1)S(1)} %get-tuple-element.36), channel_id=1, source_target_pairs={{0,1},{1,0},{2,3},{3,2},{4,5},{5,4},{6,7},{7,6},{8,9},{9,8},{10,11... | collective-permute-start | bytes 196616 | tf_op jit(solution)/shard_map/ppermute | solution.py:343
  23.0 16.6 %collective-permute-start = (bf16[128,768]{1,0:T(8,128)(2,1)S(1)}, bf16[128,768]{1,0:T(8,128)(2,1)S(1)}, u32[]{:S(2)}, u32[]{:S(2)}) collective-permute-start(bf16[128,768]{1,0:T(8,128)(2,1)S(1)} %get-tuple-element.28.refs_0_), channel_id=1, source_target_pairs={{0,2},{1,3},{2,4},{3,5},{4,6},{5,7},{6,0},{7,1},{8,10},{9,11},{10,... | collective-permute-start | bytes 589832 | tf_op jit(solution)/shard_map/ppermute | solution.py:332
  25.4 15.2 %collective-permute-start.5 = (bf16[128,768]{1,0:T(8,128)(2,1)S(1)}, bf16[128,768]{1,0:T(8,128)(2,1)S(1)}, u32[]{:S(2)}, u32[]{:S(2)}) collective-permute-start(bf16[128,768]{1,0:T(8,128)(2,1)S(1)} %collective-permute-done.4.refs_1_), channel_id=1, source_target_pairs={{0,2},{1,3},{2,4},{3,5},{4,6},{5,7},{6,0},{7,1},{8,10},{9,11},{10,... | collective-permute-start | bytes 589832 | tf_op jit(solution)/shard_map/ppermute | solution.py:332
  28.9 17.9 %slice-start = ((s8[6291456]{0:T(1024)(128)(4,1)}), s8[4194304]{0:T(1024)(128)(4,1)S(1)}, s32[]{:S(2)}) async-start(s8[6291456]{0:T(1024)(128)(4,1)} %bitcast.7), calls=%async_computation.3 | async-start | bytes 8388608
  35.2 27.3 %collective-permute-start.11 = (bf16[2,192,512]{2,1,0:T(8,128)(2,1)S(1)}, bf16[2,192,512]{2,1,0:T(8,128)(2,1)S(1)}, u32[]{:S(2)}, u32[]{:S(2)}) collective-permute-start(bf16[2,192,512]{2,1,0:T(8,128)(2,1)S(1)} %shard_map.83.refs_2_), channel_id=1, source_target_pairs={{0,16},{8,24},{16,0},{24,8},{1,17},{9,25},{17,1},{25,9},{2,18},{10... | collective-permute-start | bytes 1179656 | tf_op jit(solution)/shard_map/ppermute | solution.py:444
  37.1 7.0 %collective-permute-start.1 = (bf16[128,768]{1,0:T(8,128)(2,1)S(1)}, bf16[128,768]{1,0:T(8,128)(2,1)S(1)}, u32[]{:S(2)}, u32[]{:S(2)}) collective-permute-start(bf16[128,768]{1,0:T(8,128)(2,1)S(1)} %get-tuple-element.28.refs_0_), channel_id=1, source_target_pairs={{0,6},{1,7},{2,0},{3,1},{4,2},{5,3},{6,4},{7,5},{8,14},{9,15},{10,... | collective-permute-start | bytes 589832 | tf_op jit(solution)/shard_map/ppermute | solution.py:332
  38.2 16.9 %collective-permute-start.12 = (bf16[2,96,768]{2,1,0:T(8,128)(2,1)S(1)}, bf16[2,96,768]{2,1,0:T(8,128)(2,1)S(1)}, u32[]{:S(2)}, u32[]{:S(2)}) collective-permute-start(bf16[2,96,768]{2,1,0:T(8,128)(2,1)S(1)} %get-tuple-element.40), channel_id=1, source_target_pairs={{0,1},{1,0},{2,3},{3,2},{4,5},{5,4},{6,7},{7,6},{8,9},{9,8},{10,11... | collective-permute-start | bytes 884744 | tf_op jit(solution)/shard_map/ppermute | solution.py:343
  39.6 23.9 %collective-permute-start.10 = (bf16[128,768]{1,0:T(8,128)(2,1)S(1)}, bf16[128,768]{1,0:T(8,128)(2,1)S(1)}, u32[]{:S(2)}, u32[]{:S(2)}) collective-permute-start(bf16[128,768]{1,0:T(8,128)(2,1)S(1)} %collective-permute-done.refs_1_), channel_id=1, source_target_pairs={{0,2},{1,3},{2,4},{3,5},{4,6},{5,7},{6,0},{7,1},{8,10},{9,11},{10,... | collective-permute-start | bytes 589832 | tf_op jit(solution)/shard_map/ppermute | solution.py:332
  44.5 22.2 %collective-permute-start.14 = (bf16[2,96,768]{2,1,0:T(8,128)(2,1)S(1)}, bf16[2,96,768]{2,1,0:T(8,128)(2,1)S(1)}, u32[]{:S(2)}, u32[]{:S(2)}) collective-permute-start(bf16[2,96,768]{2,1,0:T(8,128)(2,1)S(1)} %get-tuple-element.44), channel_id=1, source_target_pairs={{0,1},{1,0},{2,3},{3,2},{4,5},{5,4},{6,7},{7,6},{8,9},{9,8},{10,11... | collective-permute-start | bytes 884744 | tf_op jit(solution)/shard_map/ppermute | solution.py:343
  46.7 8.4 %collective-permute-start.13 = (bf16[2,32,768]{2,1,0:T(8,128)(2,1)S(1)}, bf16[2,32,768]{2,1,0:T(8,128)(2,1)S(1)}, u32[]{:S(2)}, u32[]{:S(2)}) collective-permute-start(bf16[2,32,768]{2,1,0:T(8,128)(2,1)S(1)} %get-tuple-element.41), channel_id=1, source_target_pairs={{0,1},{1,0},{2,3},{3,2},{4,5},{5,4},{6,7},{7,6},{8,9},{9,8},{10,11... | collective-permute-start | bytes 294920 | tf_op jit(solution)/shard_map/ppermute | solution.py:343
  63.8 4.9 %collective-permute-start.15 = (bf16[2,32,768]{2,1,0:T(8,128)(2,1)S(1)}, bf16[2,32,768]{2,1,0:T(8,128)(2,1)S(1)}, u32[]{:S(2)}, u32[]{:S(2)}) collective-permute-start(bf16[2,32,768]{2,1,0:T(8,128)(2,1)S(1)} %get-tuple-element.45), channel_id=1, source_target_pairs={{0,1},{1,0},{2,3},{3,2},{4,5},{5,4},{6,7},{7,6},{8,9},{9,8},{10,11... | collective-permute-start | bytes 294920 | tf_op jit(solution)/shard_map/ppermute | solution.py:343
  65.4 37.4 %collective-permute-start.21 = (bf16[2,192,768]{2,1,0:T(8,128)(2,1)}, bf16[2,192,768]{2,1,0:T(8,128)(2,1)}, u32[]{:S(2)}, u32[]{:S(2)}) collective-permute-start(bf16[2,192,768]{2,1,0:T(8,128)(2,1)} %shard_map.88.refs_2_), channel_id=1, source_target_pairs={{0,16},{8,24},{16,0},{24,8},{1,17},{9,25},{17,1},{25,9},{2,18},{10... | collective-permute-start | bytes 1769480 | tf_op jit(solution)/shard_map/ppermute | solution.py:444
  73.5 14.6 %all-to-all-start.2 = ((bf16[2,2,2,192,768]{4,3,2,1,0:T(8,128)(2,1)}), bf16[2,2,2,192,768]{4,3,2,1,0:T(8,128)(2,1)}, u32[]{:S(2)}, u32[]{:S(2)}) async-start(bf16[2,2,2,192,768]{4,3,2,1,0:T(8,128)(2,1)} %copy-done.1), calls=%async_computation.2 | async-start | bytes 4718592 | tf_op jit(solution)/shard_map/all_to_all | solution.py:427
  89.9 15.8 %collective-permute-start.20 = (bf16[2,192,768]{2,1,0:T(8,128)(2,1)S(1)}, bf16[2,192,768]{2,1,0:T(8,128)(2,1)S(1)}, u32[]{:S(2)}, u32[]{:S(2)}) collective-permute-start(bf16[2,192,768]{2,1,0:T(8,128)(2,1)S(1)} %shard_map.94.refs_6_.refs_3_), channel_id=1, source_target_pairs={{0,16},{8,24},{16,0},{24,8},{1,17},{9,25},{17,1},{25,9},{2,18},{10... | collective-permute-start | bytes 1769480 | tf_op jit(solution)/shard_map/ppermute | solution.py:444
  90.8 3.6 %collective-permute-start.16 = (f32[2,256]{1,0:T(2,128)S(1)}, f32[2,256]{1,0:T(2,128)S(1)}, u32[]{:S(2)}, u32[]{:S(2)}) collective-permute-start(f32[2,256]{1,0:T(2,128)S(1)} %get-tuple-element.48.refs_1_), channel_id=1, source_target_pairs={{0,1},{1,0},{2,3},{3,2},{4,5},{5,4},{6,7},{7,6},{8,9},{9,8},{10,11... | collective-permute-start | bytes 6152 | tf_op jit(solution)/shard_map/ppermute | solution.py:482
  94.3 3.6 %collective-permute-start.17 = (f32[2,2,256]{2,1,0:T(2,128)S(1)}, f32[2,2,256]{2,1,0:T(2,128)S(1)}, u32[]{:S(2)}, u32[]{:S(2)}) collective-permute-start(f32[2,2,256]{2,1,0:T(2,128)S(1)} %pad_maximum_fusion.refs_2_), channel_id=1, source_target_pairs={{2,0},{3,1},{4,2},{5,3},{6,4},{7,5},{0,6},{1,7},{10,8},{11,9},{12,... | collective-permute-start | bytes 12296 | tf_op jit(solution)/shard_map/ppermute | solution.py:484
  96.3 4.5 %collective-permute-start.18 = (f32[2,2,256]{2,1,0:T(2,128)S(1)}, f32[2,2,256]{2,1,0:T(2,128)S(1)}, u32[]{:S(2)}, u32[]{:S(2)}) collective-permute-start(f32[2,2,256]{2,1,0:T(2,128)S(1)} %pad_maximum_fusion.refs_2_), channel_id=1, source_target_pairs={{4,0},{5,1},{6,2},{7,3},{0,4},{1,5},{2,6},{3,7},{12,8},{13,9},{14,... | collective-permute-start | bytes 12296 | tf_op jit(solution)/shard_map/ppermute | solution.py:484
  96.4 5.4 %collective-permute-start.19 = (f32[2,2,256]{2,1,0:T(2,128)S(1)}, f32[2,2,256]{2,1,0:T(2,128)S(1)}, u32[]{:S(2)}, u32[]{:S(2)}) collective-permute-start(f32[2,2,256]{2,1,0:T(2,128)S(1)} %pad_maximum_fusion.refs_2_), channel_id=1, source_target_pairs={{6,0},{7,1},{0,2},{1,3},{2,4},{3,5},{4,6},{5,7},{14,8},{15,9},{8,1... | collective-permute-start | bytes 12296 | tf_op jit(solution)/shard_map/ppermute | solution.py:484
  (16 other events, 64.3 us)

commit v12 on v10

--- a/solution.py
+++ b/solution.py
@@ -282,12 +282,12 @@
 
 def chunks_of(features):
     unit = features // 16
-    return [4 * unit, 6 * unit, 6 * unit]
+    return [6 * unit, 8 * unit, 2 * unit]
 
 
 def cuts_of(share, c):
     first = 16 * (share // 32)
-    return [first, share - first] if c == 1 else [share]
+    return [first, share - first] if c == 0 else [share]
 
 
 sds = jax.ShapeDtypeStruct
@@ -424,7 +424,7 @@
     def reduced(c):
         parts, width = arrived[c], widths[c]
         piece = sds((across, held, share, width), BF16)
-        after = summed[-1][2][:1] if c else ()
+        after = summed[0][2][:1] if c == 1 else ()
         keep, give = call(term_kernel, [piece, piece], turned, *parts, after=after)
         got = lax.ppermute(give, "dp", [(i, i ^ 1) for i in range(dp)])
         if c == count - 1:
@@ -460,17 +460,17 @@
         )
 
     if direct:
-        arrived, early = [], relay.early(0)
+        arrived = [relay.late(c, relay.early(c)) for c in range(2)]
     for c in range(count):
-        if direct:
-            arrived.append(relay.late(c, early))
-            if c + 1 < count:
-                early = relay.early(c + 1)
-        if c >= 1:
+        if c >= 2:
+            if direct:
+                arrived.append(relay.late(c, relay.early(c)))
             accumulated(c - 1)
+            finished(c - 2)
         reduced(c)
-        if c >= 1:
-            finished(c - 1)
+        if c == 1:
+            accumulated(0)
+    finished(count - 2)
     hidden_grad, sums = state["raw"]
 
     if direct:

time: 94.7 us -> 93.5 us (0.987)
  waiting for transfers between devices: 47.7 us -> 45.5 us
  starting transfers between devices: 29.8 us -> 30.9 us
    ppermute x4, waiting for transfers between devices: 14 us -> 0.01 us  [reduced(): others.append(lax.ppermute(pair, 'dp', shift))]
    ppermute x9, waiting for transfers between devices: 23.4 us -> 29.6 us  [along(): return lax.ppermute(block, 'expert', pairs)]
    ppermute x6, waiting for transfers between devices: 3.22 us -> 9.05 us  [pick(): lax.ppermute(other, 'expert', [(i, i ^ 1) for i in range(LINE * SIDES)])]
    ppermute x3, starting transfers between devices: 2.03 us -> 3.82 us  [body(): lax.ppermute(both, 'expert', [(moved(i, d, 0), i) for i in range(groups)])]
    ppermute x9, starting transfers between devices: 14.1 us -> 12.8 us  [along(): return lax.ppermute(block, 'expert', pairs)]
    ppermute x4, starting transfers between devices: 4.26 us -> 5.46 us  [reduced(): others.append(lax.ppermute(pair, 'dp', shift))]
    ppermute x6, starting transfers between devices: 8.66 us -> 7.65 us  [pick(): lax.ppermute(other, 'expert', [(i, i ^ 1) for i in range(LINE * SIDES)])]
  transfers between devices with their start and end apart: 26 -> 26, of which waited for: 14 -> 12; matrix products, arithmetic and copies ran while one was open for 0% -> 0% of each run, Pallas kernels for 9% -> 11%
where the time goes in v12:
time: 93.5 us; the launch traced here: 93.3 us
  waiting for transfers between devices  45.5 us (49%)
  starting transfers between devices  30.9 us (33%)
  Pallas kernels  14.9 us (16%)
  local copies, waits for them, and re-layouts  1.07 us (1%)
  between operations  0.94 us (1%)
    ppermute x9, waiting for transfers between devices, along(): return lax.ppermute(block, 'expert', pairs)  29.6 us
    pallas_call x22, Pallas kernels, __call__(): pl.pallas_call(body, out_shape=outs, in_specs=in_specs, compiler_params=p...  14.9 us
    ppermute x9, starting transfers between devices, along(): return lax.ppermute(block, 'expert', pairs)  12.8 us
    ppermute x6, waiting for transfers between devices, pick(): lax.ppermute(other, 'expert', [(i, i ^ 1) for i in range(LINE * SIDES)])  9.05 us
    ppermute x6, starting transfers between devices, pick(): lax.ppermute(other, 'expert', [(i, i ^ 1) for i in range(LINE * SIDES)])  7.65 us
    ppermute x4, starting transfers between devices, reduced(): others.append(lax.ppermute(pair, 'dp', shift))  5.46 us
    ppermute x3, waiting for transfers between devices, reduced(): got = lax.ppermute(give, 'dp', [(i, i ^ 1) for i in range(dp)])  4.22 us
    ppermute x3, starting transfers between devices, body(): lax.ppermute(both, 'expert', [(moved(i, d, 0), i) for i in range(groups)])  3.82 us
  transfers between devices with their start and end apart: 26, of which 12 were waited for; matrix products, arithmetic and copies ran while one was open for 0% of the time, Pallas kernels for 11%

profile of v12, /device:TPU:0, one launch (start us, length us, event | category | flops | bytes accessed | tf_op | source)
XLA Modules:
  0.0 93.3 jit_solution(807266273628277997)
XLA Ops:
  0.6 1.9 %shard_map.77 = (s32[2,128]{1,0:T(2,128)}, bf16[144,768]{1,0:T(8,128)(2,1)}) custom-call(s32[2,128]{1,0:T(2,128)} %bitcast.15, f32[2,128]{1,0:T(2,128)} %bitcast.12, bf16[128,2048]{1,0:T(8,128)(2,1)} %rows_ref.3), custom_call_target="tpu_custom_call" | custom-call | flops 1 | bytes 1 | tf_op jit(solution)/shard_map/pallas_call | solution.py:43
  2.5 3.1 %collective-permute-start.2 = (bf16[144,768]{1,0:T(8,128)(2,1)}, bf16[144,768]{1,0:T(8,128)(2,1)S(1)}, u32[]{:S(2)}, u32[]{:S(2)}) collective-permute-start(bf16[144,768]{1,0:T(8,128)(2,1)} %get-tuple-element.37.refs_0_), channel_id=1, source_target_pairs={{0,2},{1,3},{2,4},{3,5},{4,6},{5,7},{6,0},{7,1},{8,10},{9,11},{10,... | collective-permute-start | bytes 663560 | tf_op jit(solution)/shard_map/ppermute | solution.py:332
  6.7 1.6 %collective-permute-start.7 = (bf16[128,1024]{1,0:T(8,128)(2,1)S(1)}, bf16[128,1024]{1,0:T(8,128)(2,1)S(1)}, u32[]{:S(2)}, u32[]{:S(2)}) collective-permute-start(bf16[128,1024]{1,0:T(8,128)(2,1)S(1)} %get-tuple-element.43.refs_0_), channel_id=1, source_target_pairs={{0,2},{1,3},{2,4},{3,5},{4,6},{5,7},{6,0},{7,1},{8,10},{9,11},{10,... | collective-permute-start | bytes 786440 | tf_op jit(solution)/shard_map/ppermute | solution.py:332
  8.3 2.2 %collective-permute-start.3 = (bf16[144,768]{1,0:T(8,128)(2,1)}, bf16[144,768]{1,0:T(8,128)(2,1)S(1)}, u32[]{:S(2)}, u32[]{:S(2)}) collective-permute-start(bf16[144,768]{1,0:T(8,128)(2,1)} %get-tuple-element.37.refs_0_), channel_id=1, source_target_pairs={{0,6},{1,7},{2,0},{3,1},{4,2},{5,3},{6,4},{7,5},{8,14},{9,15},{10,... | collective-permute-start | bytes 663560 | tf_op jit(solution)/shard_map/ppermute | solution.py:332
  10.6 3.7 %collective-permute-done.2.refs_1_ = bf16[144,768]{1,0:T(8,128)(2,1)S(1)} collective-permute-done((bf16[144,768]{1,0:T(8,128)(2,1)}, bf16[144,768]{1,0:T(8,128)(2,1)S(1)}, u32[]{:S(2)}, u32[]{:S(2)}) %collective-permute-start.2) | collective-permute-done | bytes 221216 | tf_op jit(solution)/shard_map/ppermute | solution.py:332
  14.5 9.9 %collective-permute-done.3.refs_2_ = bf16[144,768]{1,0:T(8,128)(2,1)S(1)} collective-permute-done((bf16[144,768]{1,0:T(8,128)(2,1)}, bf16[144,768]{1,0:T(8,128)(2,1)S(1)}, u32[]{:S(2)}, u32[]{:S(2)}) %collective-permute-start.3) | collective-permute-done | bytes 221216 | tf_op jit(solution)/shard_map/ppermute | solution.py:332
  24.7 1.8 %collective-permute-start.5 = (bf16[2,96,768]{2,1,0:T(8,128)(2,1)S(1)}, bf16[2,96,768]{2,1,0:T(8,128)(2,1)S(1)}, u32[]{:S(2)}, u32[]{:S(2)}) collective-permute-start(bf16[2,96,768]{2,1,0:T(8,128)(2,1)S(1)} %get-tuple-element.41), channel_id=1, source_target_pairs={{0,1},{1,0},{2,3},{3,2},{4,5},{5,4},{6,7},{7,6},{8,9},{9,8},{10,11... | collective-permute-start | bytes 884744 | tf_op jit(solution)/shard_map/ppermute | solution.py:343
  26.5 1.7 %collective-permute-start.8 = (bf16[128,1024]{1,0:T(8,128)(2,1)S(1)}, bf16[128,1024]{1,0:T(8,128)(2,1)S(1)}, u32[]{:S(2)}, u32[]{:S(2)}) collective-permute-start(bf16[128,1024]{1,0:T(8,128)(2,1)S(1)} %get-tuple-element.43.refs_0_), channel_id=1, source_target_pairs={{0,6},{1,7},{2,0},{3,1},{4,2},{5,3},{6,4},{7,5},{8,14},{9,15},{10,... | collective-permute-start | bytes 786440 | tf_op jit(solution)/shard_map/ppermute | solution.py:332
  29.5 1.8 %collective-permute-start.6 = (bf16[2,32,768]{2,1,0:T(8,128)(2,1)S(1)}, bf16[2,32,768]{2,1,0:T(8,128)(2,1)S(1)}, u32[]{:S(2)}, u32[]{:S(2)}) collective-permute-start(bf16[2,32,768]{2,1,0:T(8,128)(2,1)S(1)} %get-tuple-element.42), channel_id=1, source_target_pairs={{0,1},{1,0},{2,3},{3,2},{4,5},{5,4},{6,7},{7,6},{8,9},{9,8},{10,11... | collective-permute-start | bytes 294920 | tf_op jit(solution)/shard_map/ppermute | solution.py:343
  31.3 9.0 %collective-permute-done.8.refs_2_ = bf16[128,1024]{1,0:T(8,128)(2,1)S(1)} collective-permute-done((bf16[128,1024]{1,0:T(8,128)(2,1)S(1)}, bf16[128,1024]{1,0:T(8,128)(2,1)S(1)}, u32[]{:S(2)}, u32[]{:S(2)}) %collective-permute-start.8) | collective-permute-done | bytes 262176 | tf_op jit(solution)/shard_map/ppermute | solution.py:332
  42.4 2.1 %collective-permute-done.12.refs_1_ = bf16[2,2,192,768]{3,2,1,0:T(8,128)(2,1)S(1)} collective-permute-done((bf16[2,2,192,768]{3,2,1,0:T(8,128)(2,1)S(1)}, bf16[2,2,192,768]{3,2,1,0:T(8,128)(2,1)S(1)}, u32[]{:S(2)}, u32[]{:S(2)}) %collective-permute-start.12) | collective-permute-done | bytes 1179680 | tf_op jit(solution)/shard_map/ppermute | solution.py:429
  44.7 1.7 %collective-permute-start.13 = (bf16[2,96,768]{2,1,0:T(8,128)(2,1)S(1)}, bf16[2,96,768]{2,1,0:T(8,128)(2,1)S(1)}, u32[]{:S(2)}, u32[]{:S(2)}) collective-permute-start(bf16[2,96,768]{2,1,0:T(8,128)(2,1)S(1)} %get-tuple-element.51.refs_5_), channel_id=1, source_target_pairs={{0,16},{8,24},{16,0},{24,8},{1,17},{9,25},{17,1},{25,9},{2,18},{10... | collective-permute-start | bytes 884744 | tf_op jit(solution)/shard_map/ppermute | solution.py:439
  47.4 8.7 %collective-permute-done.11.refs_4_ = bf16[2,32,1024]{2,1,0:T(8,128)(2,1)S(1)} collective-permute-done((bf16[2,32,1024]{2,1,0:T(8,128)(2,1)S(1)}, bf16[2,32,1024]{2,1,0:T(8,128)(2,1)S(1)}, u32[]{:S(2)}, u32[]{:S(2)}) %collective-permute-start.11) | collective-permute-done | bytes 131104 | tf_op jit(solution)/shard_map/ppermute | solution.py:343
  57.1 1.7 %collective-permute-start.18 = (bf16[2,96,768]{2,1,0:T(8,128)(2,1)S(1)}, bf16[2,96,768]{2,1,0:T(8,128)(2,1)S(1)}, u32[]{:S(2)}, u32[]{:S(2)}) collective-permute-start(bf16[2,96,768]{2,1,0:T(8,128)(2,1)S(1)} %get-tuple-element.58), channel_id=1, source_target_pairs={{0,16},{8,24},{16,0},{24,8},{1,17},{9,25},{17,1},{25,9},{2,18},{10... | collective-permute-start | bytes 884744 | tf_op jit(solution)/shard_map/ppermute | solution.py:439
  58.8 1.7 %collective-permute-done.14.refs_1_ = bf16[2,2,192,1024]{3,2,1,0:T(8,128)(2,1)S(1)} collective-permute-done((bf16[2,2,192,1024]{3,2,1,0:T(8,128)(2,1)S(1)}, bf16[2,2,192,1024]{3,2,1,0:T(8,128)(2,1)S(1)}, u32[]{:S(2)}, u32[]{:S(2)}) %collective-permute-start.14) | collective-permute-done | bytes 1572896 | tf_op jit(solution)/shard_map/ppermute | solution.py:429
  60.7 1.7 %collective-permute-start.23 = (bf16[2,192,1024]{2,1,0:T(8,128)(2,1)S(1)}, bf16[2,192,1024]{2,1,0:T(8,128)(2,1)S(1)}, u32[]{:S(2)}, u32[]{:S(2)}) collective-permute-start(bf16[2,192,1024]{2,1,0:T(8,128)(2,1)S(1)} %shard_map.86.refs_5_), channel_id=1, source_target_pairs={{0,16},{8,24},{16,0},{24,8},{1,17},{9,25},{17,1},{25,9},{2,18},{10... | collective-permute-start | bytes 2359304 | tf_op jit(solution)/shard_map/ppermute | solution.py:439
  62.9 3.2 %collective-permute-start.1 = (bf16[128,256]{1,0:T(8,128)(2,1)S(1)}, bf16[128,256]{1,0:T(8,128)(2,1)S(1)}, u32[]{:S(2)}, u32[]{:S(2)}) collective-permute-start(bf16[128,256]{1,0:T(8,128)(2,1)S(1)} %get-tuple-element.36.refs_0_), channel_id=1, source_target_pairs={{0,6},{1,7},{2,0},{3,1},{4,2},{5,3},{6,4},{7,5},{8,14},{9,15},{10,... | collective-permute-start | bytes 196616 | tf_op jit(solution)/shard_map/ppermute | solution.py:332
  66.2 2.5 %collective-permute-done.refs_1_ = bf16[128,256]{1,0:T(8,128)(2,1)S(1)} collective-permute-done((bf16[128,256]{1,0:T(8,128)(2,1)S(1)}, bf16[128,256]{1,0:T(8,128)(2,1)S(1)}, u32[]{:S(2)}, u32[]{:S(2)}) %collective-permute-start) | collective-permute-done | bytes 65568 | tf_op jit(solution)/shard_map/ppermute | solution.py:332
  70.9 3.9 %collective-permute-done.15.refs_0_ = bf16[128,256]{1,0:T(8,128)(2,1)S(1)} collective-permute-done((bf16[128,256]{1,0:T(8,128)(2,1)S(1)}, bf16[128,256]{1,0:T(8,128)(2,1)S(1)}, u32[]{:S(2)}, u32[]{:S(2)}) %collective-permute-start.15) | collective-permute-done | bytes 65568 | tf_op jit(solution)/shard_map/ppermute | solution.py:332
  77.1 1.4 %shard_map.91 = (f32[192,2,2048]{2,1,0:T(2,128)}, f32[8,128]{1,0:T(8,128)S(1)}) custom-call(bf16[2,2,192,768]{3,2,1,0:T(8,128)(2,1)S(1)} %get-tuple-element.49.refs_0_.refs_2_, bf16[2,2,192,768]{3,2,1,0:T(8,128)(2,1)S(1)} %collective-permute-done.12.refs_1_, bf16[2,96,768]{2,1,0:T(8,128)(2,1)S(1)} %collective-permute-done.13.refs_6_.refs_2_, ...), custom_call_target="tpu_custom_call" | custom-call | flops 1 | bytes 1 | tf_op jit(solution)/shard_map/pallas_call | solution.py:43
  82.6 2.6 %collective-permute-done.19 = f32[2,256]{1,0:T(2,128)S(1)} collective-permute-done((f32[2,256]{1,0:T(2,128)S(1)}, f32[2,256]{1,0:T(2,128)S(1)}, u32[]{:S(2)}, u32[]{:S(2)}) %collective-permute-start.19) | collective-permute-done | bytes 2080 | tf_op jit(solution)/shard_map/ppermute | solution.py:478
  85.6 3.4 %collective-permute-start.20 = (f32[2,2,256]{2,1,0:T(2,128)S(1)}, f32[2,2,256]{2,1,0:T(2,128)S(1)}, u32[]{:S(2)}, u32[]{:S(2)}) collective-permute-start(f32[2,2,256]{2,1,0:T(2,128)S(1)} %pad_maximum_fusion.refs_2_), channel_id=1, source_target_pairs={{2,0},{3,1},{4,2},{5,3},{6,4},{7,5},{0,6},{1,7},{10,8},{11,9},{12,... | collective-permute-start | bytes 12296 | tf_op jit(solution)/shard_map/ppermute | solution.py:480
  89.1 1.7 %shard_map.95 = (f32[192,2,2048]{2,1,0:T(2,128)}, f32[8,128]{1,0:T(8,128)S(1)}) custom-call(bf16[2,2,192,1024]{3,2,1,0:T(8,128)(2,1)S(1)} %get-tuple-element.52.refs_0_.refs_2_, bf16[2,2,192,1024]{3,2,1,0:T(8,128)(2,1)S(1)} %collective-permute-done.14.refs_1_, ...), custom_call_target="tpu_custom_call", output_to_operand_aliasing={{0}: (3, {})} | custom-call | flops 1 | bytes 1 | tf_op jit(solution)/shard_map/pallas_call | solution.py:43
  90.8 1.5 %shard_map.97 = (f32[192,2,2048]{2,1,0:T(2,128)}, f32[8,128]{1,0:T(8,128)}) custom-call(bf16[2,2,192,256]{3,2,1,0:T(8,128)(2,1)S(1)} %get-tuple-element.60.refs_7_.refs_0_, bf16[2,2,192,256]{3,2,1,0:T(8,128)(2,1)S(1)} %collective-permute-done.24.refs_1_, bf16[2,192,256]{2,1,0:T(8,128)(2,1)S(1)} %collective-permute-done.25.refs_2_, ...), custom_call_target="tpu_custom_call", output_to_operand_aliasing={{0}: (3, {})} | custom-call | flops 1 | bytes 1 | tf_op jit(solution)/shard_map/pallas_call | solution.py:43
  (66 shorter events, 18.0 us)
Async XLA Ops:
  2.5 11.7 %collective-permute-start.2 = (bf16[144,768]{1,0:T(8,128)(2,1)}, bf16[144,768]{1,0:T(8,128)(2,1)S(1)}, u32[]{:S(2)}, u32[]{:S(2)}) collective-permute-start(bf16[144,768]{1,0:T(8,128)(2,1)} %get-tuple-element.37.refs_0_), channel_id=1, source_target_pairs={{0,2},{1,3},{2,4},{3,5},{4,6},{5,7},{6,0},{7,1},{8,10},{9,11},{10,... | collective-permute-start | bytes 663560 | tf_op jit(solution)/shard_map/ppermute | solution.py:332
  6.7 21.5 %collective-permute-start.7 = (bf16[128,1024]{1,0:T(8,128)(2,1)S(1)}, bf16[128,1024]{1,0:T(8,128)(2,1)S(1)}, u32[]{:S(2)}, u32[]{:S(2)}) collective-permute-start(bf16[128,1024]{1,0:T(8,128)(2,1)S(1)} %get-tuple-element.43.refs_0_), channel_id=1, source_target_pairs={{0,2},{1,3},{2,4},{3,5},{4,6},{5,7},{6,0},{7,1},{8,10},{9,11},{10,... | collective-permute-start | bytes 786440 | tf_op jit(solution)/shard_map/ppermute | solution.py:332
  8.3 16.1 %collective-permute-start.3 = (bf16[144,768]{1,0:T(8,128)(2,1)}, bf16[144,768]{1,0:T(8,128)(2,1)S(1)}, u32[]{:S(2)}, u32[]{:S(2)}) collective-permute-start(bf16[144,768]{1,0:T(8,128)(2,1)} %get-tuple-element.37.refs_0_), channel_id=1, source_target_pairs={{0,6},{1,7},{2,0},{3,1},{4,2},{5,3},{6,4},{7,5},{8,14},{9,15},{10,... | collective-permute-start | bytes 663560 | tf_op jit(solution)/shard_map/ppermute | solution.py:332
  14.3 15.0 %collective-permute-start.4 = (bf16[144,768]{1,0:T(8,128)(2,1)S(1)}, bf16[144,768]{1,0:T(8,128)(2,1)S(1)}, u32[]{:S(2)}, u32[]{:S(2)}) collective-permute-start(bf16[144,768]{1,0:T(8,128)(2,1)S(1)} %collective-permute-done.2.refs_1_), channel_id=1, source_target_pairs={{0,2},{1,3},{2,4},{3,5},{4,6},{5,7},{6,0},{7,1},{8,10},{9,11},{10,... | collective-permute-start | bytes 663560 | tf_op jit(solution)/shard_map/ppermute | solution.py:332
  24.7 16.1 %collective-permute-start.5 = (bf16[2,96,768]{2,1,0:T(8,128)(2,1)S(1)}, bf16[2,96,768]{2,1,0:T(8,128)(2,1)S(1)}, u32[]{:S(2)}, u32[]{:S(2)}) collective-permute-start(bf16[2,96,768]{2,1,0:T(8,128)(2,1)S(1)} %get-tuple-element.41), channel_id=1, source_target_pairs={{0,1},{1,0},{2,3},{3,2},{4,5},{5,4},{6,7},{7,6},{8,9},{9,8},{10,11... | collective-permute-start | bytes 884744 | tf_op jit(solution)/shard_map/ppermute | solution.py:343
  26.5 13.7 %collective-permute-start.8 = (bf16[128,1024]{1,0:T(8,128)(2,1)S(1)}, bf16[128,1024]{1,0:T(8,128)(2,1)S(1)}, u32[]{:S(2)}, u32[]{:S(2)}) collective-permute-start(bf16[128,1024]{1,0:T(8,128)(2,1)S(1)} %get-tuple-element.43.refs_0_), channel_id=1, source_target_pairs={{0,6},{1,7},{2,0},{3,1},{4,2},{5,3},{6,4},{7,5},{8,14},{9,15},{10,... | collective-permute-start | bytes 786440 | tf_op jit(solution)/shard_map/ppermute | solution.py:332
  28.2 12.4 %collective-permute-start.9 = (bf16[128,1024]{1,0:T(8,128)(2,1)S(1)}, bf16[128,1024]{1,0:T(8,128)(2,1)S(1)}, u32[]{:S(2)}, u32[]{:S(2)}) collective-permute-start(bf16[128,1024]{1,0:T(8,128)(2,1)S(1)} %collective-permute-done.7.refs_1_), channel_id=1, source_target_pairs={{0,2},{1,3},{2,4},{3,5},{4,6},{5,7},{6,0},{7,1},{8,10},{9,11},{10,... | collective-permute-start | bytes 786440 | tf_op jit(solution)/shard_map/ppermute | solution.py:332
  29.5 11.4 %collective-permute-start.6 = (bf16[2,32,768]{2,1,0:T(8,128)(2,1)S(1)}, bf16[2,32,768]{2,1,0:T(8,128)(2,1)S(1)}, u32[]{:S(2)}, u32[]{:S(2)}) collective-permute-start(bf16[2,32,768]{2,1,0:T(8,128)(2,1)S(1)} %get-tuple-element.42), channel_id=1, source_target_pairs={{0,1},{1,0},{2,3},{3,2},{4,5},{5,4},{6,7},{7,6},{8,9},{9,8},{10,11... | collective-permute-start | bytes 294920 | tf_op jit(solution)/shard_map/ppermute | solution.py:343
  41.7 14.3 %collective-permute-start.10 = (bf16[2,96,1024]{2,1,0:T(8,128)(2,1)S(1)}, bf16[2,96,1024]{2,1,0:T(8,128)(2,1)S(1)}, u32[]{:S(2)}, u32[]{:S(2)}) collective-permute-start(bf16[2,96,1024]{2,1,0:T(8,128)(2,1)S(1)} %get-tuple-element.47), channel_id=1, source_target_pairs={{0,1},{1,0},{2,3},{3,2},{4,5},{5,4},{6,7},{7,6},{8,9},{9,8},{10,11... | collective-permute-start | bytes 1179656 | tf_op jit(solution)/shard_map/ppermute | solution.py:343
  44.7 11.4 %collective-permute-start.13 = (bf16[2,96,768]{2,1,0:T(8,128)(2,1)S(1)}, bf16[2,96,768]{2,1,0:T(8,128)(2,1)S(1)}, u32[]{:S(2)}, u32[]{:S(2)}) collective-permute-start(bf16[2,96,768]{2,1,0:T(8,128)(2,1)S(1)} %get-tuple-element.51.refs_5_), channel_id=1, source_target_pairs={{0,16},{8,24},{16,0},{24,8},{1,17},{9,25},{17,1},{25,9},{2,18},{10... | collective-permute-start | bytes 884744 | tf_op jit(solution)/shard_map/ppermute | solution.py:439
  46.3 9.7 %collective-permute-start.11 = (bf16[2,32,1024]{2,1,0:T(8,128)(2,1)S(1)}, bf16[2,32,1024]{2,1,0:T(8,128)(2,1)S(1)}, u32[]{:S(2)}, u32[]{:S(2)}) collective-permute-start(bf16[2,32,1024]{2,1,0:T(8,128)(2,1)S(1)} %get-tuple-element.48), channel_id=1, source_target_pairs={{0,1},{1,0},{2,3},{3,2},{4,5},{5,4},{6,7},{7,6},{8,9},{9,8},{10,11... | collective-permute-start | bytes 393224 | tf_op jit(solution)/shard_map/ppermute | solution.py:343
  57.0 3.5 %collective-permute-start.14 = (bf16[2,2,192,1024]{3,2,1,0:T(8,128)(2,1)S(1)}, bf16[2,2,192,1024]{3,2,1,0:T(8,128)(2,1)S(1)}, u32[]{:S(2)}, u32[]{:S(2)}) collective-permute-start(bf16[2,2,192,1024]{3,2,1,0:T(8,128)(2,1)S(1)} %get-tuple-element.53), channel_id=1, source_target_pairs={{0,8},{8,0},{16,24},{24,16},{1,9},{9,1},{17,25},{25,17},{2,10},{10... | collective-permute-start | bytes 4718600 | tf_op jit(solution)/shard_map/ppermute | solution.py:429
  57.1 19.9 %collective-permute-start.18 = (bf16[2,96,768]{2,1,0:T(8,128)(2,1)S(1)}, bf16[2,96,768]{2,1,0:T(8,128)(2,1)S(1)}, u32[]{:S(2)}, u32[]{:S(2)}) collective-permute-start(bf16[2,96,768]{2,1,0:T(8,128)(2,1)S(1)} %get-tuple-element.58), channel_id=1, source_target_pairs={{0,16},{8,24},{16,0},{24,8},{1,17},{9,25},{17,1},{25,9},{2,18},{10... | collective-permute-start | bytes 884744 | tf_op jit(solution)/shard_map/ppermute | solution.py:439
  60.7 28.3 %collective-permute-start.23 = (bf16[2,192,1024]{2,1,0:T(8,128)(2,1)S(1)}, bf16[2,192,1024]{2,1,0:T(8,128)(2,1)S(1)}, u32[]{:S(2)}, u32[]{:S(2)}) collective-permute-start(bf16[2,192,1024]{2,1,0:T(8,128)(2,1)S(1)} %shard_map.86.refs_5_), channel_id=1, source_target_pairs={{0,16},{8,24},{16,0},{24,8},{1,17},{9,25},{17,1},{25,9},{2,18},{10... | collective-permute-start | bytes 2359304 | tf_op jit(solution)/shard_map/ppermute | solution.py:439
  62.4 6.4 %collective-permute-start = (bf16[128,256]{1,0:T(8,128)(2,1)S(1)}, bf16[128,256]{1,0:T(8,128)(2,1)S(1)}, u32[]{:S(2)}, u32[]{:S(2)}) collective-permute-start(bf16[128,256]{1,0:T(8,128)(2,1)S(1)} %get-tuple-element.36.refs_0_), channel_id=1, source_target_pairs={{0,2},{1,3},{2,4},{3,5},{4,6},{5,7},{6,0},{7,1},{8,10},{9,11},{10,... | collective-permute-start | bytes 196616 | tf_op jit(solution)/shard_map/ppermute | solution.py:332
  62.9 6.6 %collective-permute-start.1 = (bf16[128,256]{1,0:T(8,128)(2,1)S(1)}, bf16[128,256]{1,0:T(8,128)(2,1)S(1)}, u32[]{:S(2)}, u32[]{:S(2)}) collective-permute-start(bf16[128,256]{1,0:T(8,128)(2,1)S(1)} %get-tuple-element.36.refs_0_), channel_id=1, source_target_pairs={{0,6},{1,7},{2,0},{3,1},{4,2},{5,3},{6,4},{7,5},{8,14},{9,15},{10,... | collective-permute-start | bytes 196616 | tf_op jit(solution)/shard_map/ppermute | solution.py:332
  68.7 6.1 %collective-permute-start.15 = (bf16[128,256]{1,0:T(8,128)(2,1)S(1)}, bf16[128,256]{1,0:T(8,128)(2,1)S(1)}, u32[]{:S(2)}, u32[]{:S(2)}) collective-permute-start(bf16[128,256]{1,0:T(8,128)(2,1)S(1)} %collective-permute-done.refs_1_), channel_id=1, source_target_pairs={{0,2},{1,3},{2,4},{3,5},{4,6},{5,7},{6,0},{7,1},{8,10},{9,11},{10,... | collective-permute-start | bytes 196616 | tf_op jit(solution)/shard_map/ppermute | solution.py:332
  69.8 9.1 %collective-permute-start.16 = (bf16[2,96,256]{2,1,0:T(8,128)(2,1)S(1)}, bf16[2,96,256]{2,1,0:T(8,128)(2,1)S(1)}, u32[]{:S(2)}, u32[]{:S(2)}) collective-permute-start(bf16[2,96,256]{2,1,0:T(8,128)(2,1)S(1)} %get-tuple-element.56), channel_id=1, source_target_pairs={{0,1},{1,0},{2,3},{3,2},{4,5},{5,4},{6,7},{7,6},{8,9},{9,8},{10,11... | collective-permute-start | bytes 294920 | tf_op jit(solution)/shard_map/ppermute | solution.py:343
  74.9 4.0 %collective-permute-start.17 = (bf16[2,32,256]{2,1,0:T(8,128)(2,1)S(1)}, bf16[2,32,256]{2,1,0:T(8,128)(2,1)S(1)}, u32[]{:S(2)}, u32[]{:S(2)}) collective-permute-start(bf16[2,32,256]{2,1,0:T(8,128)(2,1)S(1)} %get-tuple-element.57), channel_id=1, source_target_pairs={{0,1},{1,0},{2,3},{3,2},{4,5},{5,4},{6,7},{7,6},{8,9},{9,8},{10,11... | collective-permute-start | bytes 98312 | tf_op jit(solution)/shard_map/ppermute | solution.py:343
  81.1 9.6 %collective-permute-start.25 = (bf16[2,192,256]{2,1,0:T(8,128)(2,1)S(1)}, bf16[2,192,256]{2,1,0:T(8,128)(2,1)S(1)}, u32[]{:S(2)}, u32[]{:S(2)}) collective-permute-start(bf16[2,192,256]{2,1,0:T(8,128)(2,1)S(1)} %shard_map.94.refs_4_), channel_id=1, source_target_pairs={{0,16},{8,24},{16,0},{24,8},{1,17},{9,25},{17,1},{25,9},{2,18},{10... | collective-permute-start | bytes 589832 | tf_op jit(solution)/shard_map/ppermute | solution.py:439
  81.6 3.6 %collective-permute-start.19 = (f32[2,256]{1,0:T(2,128)S(1)}, f32[2,256]{1,0:T(2,128)S(1)}, u32[]{:S(2)}, u32[]{:S(2)}) collective-permute-start(f32[2,256]{1,0:T(2,128)S(1)} %get-tuple-element.63.refs_2_), channel_id=1, source_target_pairs={{0,1},{1,0},{2,3},{3,2},{4,5},{5,4},{6,7},{7,6},{8,9},{9,8},{10,11... | collective-permute-start | bytes 6152 | tf_op jit(solution)/shard_map/ppermute | solution.py:478
  85.2 7.0 %collective-permute-start.22 = (f32[2,2,256]{2,1,0:T(2,128)S(1)}, f32[2,2,256]{2,1,0:T(2,128)S(1)}, u32[]{:S(2)}, u32[]{:S(2)}) collective-permute-start(f32[2,2,256]{2,1,0:T(2,128)S(1)} %pad_maximum_fusion.refs_2_), channel_id=1, source_target_pairs={{6,0},{7,1},{0,2},{1,3},{2,4},{3,5},{4,6},{5,7},{14,8},{15,9},{8,1... | collective-permute-start | bytes 12296 | tf_op jit(solution)/shard_map/ppermute | solution.py:480
  85.2 7.0 %collective-permute-start.21 = (f32[2,2,256]{2,1,0:T(2,128)S(1)}, f32[2,2,256]{2,1,0:T(2,128)S(1)}, u32[]{:S(2)}, u32[]{:S(2)}) collective-permute-start(f32[2,2,256]{2,1,0:T(2,128)S(1)} %pad_maximum_fusion.refs_2_), channel_id=1, source_target_pairs={{4,0},{5,1},{6,2},{7,3},{0,4},{1,5},{2,6},{3,7},{12,8},{13,9},{14,... | collective-permute-start | bytes 12296 | tf_op jit(solution)/shard_map/ppermute | solution.py:480
  85.6 6.7 %collective-permute-start.20 = (f32[2,2,256]{2,1,0:T(2,128)S(1)}, f32[2,2,256]{2,1,0:T(2,128)S(1)}, u32[]{:S(2)}, u32[]{:S(2)}) collective-permute-start(f32[2,2,256]{2,1,0:T(2,128)S(1)} %pad_maximum_fusion.refs_2_), channel_id=1, source_target_pairs={{2,0},{3,1},{4,2},{5,3},{6,4},{7,5},{0,6},{1,7},{10,8},{11,9},{12,... | collective-permute-start | bytes 12296 | tf_op jit(solution)/shard_map/ppermute | solution.py:480
  (9 other events, 86.8 us)

commit v13 on v10

--- a/solution.py
+++ b/solution.py
@@ -176,30 +176,25 @@
                 ref[step, e] = term[step * share : (step + 1) * share]
 
 
-def pair_kernel(cuts, keep_ref, got_ref, *out_refs):
-    out_refs = iter(out_refs)
-    for step in range(1, keep_ref.shape[0]):
-        start = 0
-        for rows in cuts:
-            at = slice(start, start + rows)
-            pair = keep_ref[step, :, at].astype(F32) + got_ref[step, :, at].astype(F32)
-            next(out_refs)[...] = pair.astype(BF16)
-            start += rows
-
-
-def last_kernel(cuts, start, keep_ref, got_ref, *refs):
+def pair_kernel(keep_ref, got_ref, *out_refs):
+    for step, ref in enumerate(out_refs, 1):
+        ref[...] = (keep_ref[step].astype(F32) + got_ref[step].astype(F32)).astype(BF16)
+
+
+def last_kernel(chunks, start, *refs):
     out_ref, mark_ref, total_ref, sem = refs[-4:]
     mark_ref[...] = jnp.zeros(mark_ref.shape, F32)
-    others = len(cuts) * (keep_ref.shape[0] - 1)
-    for e in range(keep_ref.shape[1]):
-        row = 0
-        for part, rows in enumerate(cuts):
-            at = slice(row, row + rows)
-            total = keep_ref[0, e, at].astype(F32) + got_ref[0, e, at].astype(F32)
-            for ref in refs[part : others : len(cuts)]:
+    across, held = refs[0].shape[:2]
+    column = 0
+    for chunk in range(chunks):
+        keep_ref, got_ref, *other_refs = refs[chunk * (across + 1) : (chunk + 1) * (across + 1)]
+        at = slice(column, column + keep_ref.shape[3])
+        column = at.stop
+        for e in range(held):
+            total = keep_ref[0, e].astype(F32) + got_ref[0, e].astype(F32)
+            for ref in other_refs:
                 total = total + ref[e].astype(F32)
-            total_ref[at, e, :] = total
-            row += rows
+            total_ref[:, e, at] = total
     copy = pltpu.make_async_copy(
         total_ref, out_ref.at[:, :, start : start + total_ref.shape[2]], sem
     )
@@ -282,12 +277,7 @@
 
 def chunks_of(features):
     unit = features // 16
-    return [4 * unit, 6 * unit, 6 * unit]
-
-
-def cuts_of(share, c):
-    first = 16 * (share // 32)
-    return [first, share - first] if c == 1 else [share]
+    return [5 * unit, 8 * unit, 3 * unit]
 
 
 sds = jax.ShapeDtypeStruct
@@ -429,32 +419,26 @@
         got = lax.ppermute(give, "dp", [(i, i ^ 1) for i in range(dp)])
         if c == count - 1:
             accumulated(c)
-        cuts = cuts_of(share, c)
-        pieces = [sds((held, rows, width), BF16) for rows in cuts]
-        pairs = call(functools.partial(pair_kernel, cuts), pieces * (across - 1), keep, got)
+        pairs = call(pair_kernel, [sds((held, share, width), BF16)] * (across - 1), keep, got)
         others = []
-        for i, pair in enumerate(pairs):
-            step = 1 + i // len(cuts)
+        for step, pair in enumerate(pairs, 1):
             shift = [(2 * r + k, 2 * ((r + step) % across) + k) for r in range(across) for k in range(2)]
             others.append(lax.ppermute(pair, "dp", shift))
         summed.append((keep, got, others))
 
-    def finished(c):
-        keep, got, others = summed[c]
+    def finished(chunks):
         before = [] if state["grad"] is None else [state["grad"]]
-        count = 2 + len(others)
+        args = [x for c in chunks for x in (*summed[c][:2], *summed[c][2])]
         state["grad"], _ = call(
-            functools.partial(last_kernel, cuts_of(share, c), starts[c]),
+            functools.partial(last_kernel, len(chunks), starts[chunks[0]]),
             [sds((share, held, features), F32), sds((8, 128), F32)],
-            keep,
-            got,
-            *others,
+            *args,
             *before,
-            in_specs=[VMEM] * count + [ANY] * len(before),
+            in_specs=[VMEM] * len(args) + [ANY] * len(before),
             out_specs=[ANY, VMEM],
-            input_output_aliases={count: 0} if before else {},
+            input_output_aliases={len(args): 0} if before else {},
             scratch_shapes=[
-                pltpu.VMEM((share, held, widths[c]), F32),
+                pltpu.VMEM((share, held, sum(widths[c] for c in chunks)), F32),
                 pltpu.SemaphoreType.DMA,
             ],
         )
@@ -464,13 +448,15 @@
     for c in range(count):
         if direct:
             arrived.append(relay.late(c, early))
-            if c + 1 < count:
-                early = relay.early(c + 1)
+            if c == 0:
+                early = relay.early(1)
         if c >= 1:
             accumulated(c - 1)
         reduced(c)
-        if c >= 1:
-            finished(c - 1)
+        if direct and 1 <= c < count - 1:
+            early = relay.early(c + 1)
+        if 1 <= c < count - 1:
+            finished([c - 1])
     hidden_grad, sums = state["raw"]
 
     if direct:
@@ -493,7 +479,7 @@
         *returned,
         keep=False,
     ).T
-    finished(count - 1)
+    finished([count - 2, count - 1])
     weight_grad = state["grad"]
     return (hidden_grad.reshape(hidden.shape), prob_grad, weight_grad)
 

time: 94.7 us -> 93.7 us (0.989)
  waiting for transfers between devices: 47.7 us -> 45 us
  starting transfers between devices: 29.8 us -> 31.8 us
    ppermute x4 -> x3, waiting for transfers between devices: 14 us -> 0.88 us  [reduced(): others.append(lax.ppermute(pair, 'dp', shift))]
    ppermute x9, waiting for transfers between devices: 23.4 us -> 30 us  [along(): return lax.ppermute(block, 'expert', pairs)]
    ppermute x3, starting transfers between devices: 2.03 us -> 4.64 us  [body(): lax.ppermute(both, 'expert', [(moved(i, d, 0), i) for i in range(groups)])]
    ppermute x3, waiting for transfers between devices: 4.03 us -> 6.37 us  [reduced(): got = lax.ppermute(give, 'dp', [(i, i ^ 1) for i in range(dp)])]
    ppermute x3, waiting for transfers between devices: 0.01 us -> 1.49 us  [body(): lax.ppermute(both, 'expert', [(moved(i, d, 0), i) for i in range(groups)])]
    ppermute x4 -> x3, starting transfers between devices: 4.26 us -> 2.87 us  [reduced(): others.append(lax.ppermute(pair, 'dp', shift))]
    ppermute x9, starting transfers between devices: 14.1 us -> 12.9 us  [along(): return lax.ppermute(block, 'expert', pairs)]
    ppermute x6, starting transfers between devices: 8.66 us -> 9.7 us  [pick(): lax.ppermute(other, 'expert', [(i, i ^ 1) for i in range(LINE * SIDES)])]
  transfers between devices with their start and end apart: 26 -> 25, of which waited for: 14 -> 16; matrix products, arithmetic and copies ran while one was open for 0% -> 0% of each run, Pallas kernels for 9% -> 8%
where the time goes in v13:
time: 93.7 us; the launch traced here: 93.5 us
  waiting for transfers between devices  45 us (48%)
  starting transfers between devices  31.8 us (34%)
  Pallas kernels  14.7 us (16%)
  local copies, waits for them, and re-layouts  1.07 us (1%)
    ppermute x9, waiting for transfers between devices, along(): return lax.ppermute(block, 'expert', pairs)  30 us
    pallas_call x21, Pallas kernels, __call__(): pl.pallas_call(body, out_shape=outs, in_specs=in_specs, compiler_params=p...  14.7 us
    ppermute x9, starting transfers between devices, along(): return lax.ppermute(block, 'expert', pairs)  12.9 us
    ppermute x6, starting transfers between devices, pick(): lax.ppermute(other, 'expert', [(i, i ^ 1) for i in range(LINE * SIDES)])  9.7 us
    ppermute x3, waiting for transfers between devices, reduced(): got = lax.ppermute(give, 'dp', [(i, i ^ 1) for i in range(dp)])  6.37 us
    ppermute x3, starting transfers between devices, body(): lax.ppermute(both, 'expert', [(moved(i, d, 0), i) for i in range(groups)])  4.64 us
    ppermute x6, waiting for transfers between devices, pick(): lax.ppermute(other, 'expert', [(i, i ^ 1) for i in range(LINE * SIDES)])  4.24 us
    ppermute x3, starting transfers between devices, reduced(): others.append(lax.ppermute(pair, 'dp', shift))  2.87 us
  transfers between devices with their start and end apart: 25, of which 16 were waited for; matrix products, arithmetic and copies ran while one was open for 0% of the time, Pallas kernels for 8%

profile of v13, /device:TPU:0, one launch (start us, length us, event | category | flops | bytes accessed | tf_op | source)
XLA Modules:
  0.0 93.5 jit_solution(3335706587612873449)
XLA Ops:
  0.6 1.9 %shard_map.77 = (s32[2,128]{1,0:T(2,128)}, bf16[144,640]{1,0:T(8,128)(2,1)}) custom-call(s32[2,128]{1,0:T(2,128)} %bitcast.13, f32[2,128]{1,0:T(2,128)} %bitcast.10, bf16[128,2048]{1,0:T(8,128)(2,1)} %rows_ref.3), custom_call_target="tpu_custom_call" | custom-call | flops 1 | bytes 1 | tf_op jit(solution)/shard_map/pallas_call | solution.py:43
  2.5 3.1 %collective-permute-start.2 = (bf16[144,640]{1,0:T(8,128)(2,1)}, bf16[144,640]{1,0:T(8,128)(2,1)S(1)}, u32[]{:S(2)}, u32[]{:S(2)}) collective-permute-start(bf16[144,640]{1,0:T(8,128)(2,1)} %get-tuple-element.33.refs_0_), channel_id=1, source_target_pairs={{0,2},{1,3},{2,4},{3,5},{4,6},{5,7},{6,0},{7,1},{8,10},{9,11},{10,... | collective-permute-start | bytes 552968 | tf_op jit(solution)/shard_map/ppermute | solution.py:322
  5.6 2.1 %collective-permute-start.3 = (bf16[144,640]{1,0:T(8,128)(2,1)}, bf16[144,640]{1,0:T(8,128)(2,1)S(1)}, u32[]{:S(2)}, u32[]{:S(2)}) collective-permute-start(bf16[144,640]{1,0:T(8,128)(2,1)} %get-tuple-element.33.refs_0_), channel_id=1, source_target_pairs={{0,6},{1,7},{2,0},{3,1},{4,2},{5,3},{6,4},{7,5},{8,14},{9,15},{10,... | collective-permute-start | bytes 552968 | tf_op jit(solution)/shard_map/ppermute | solution.py:322
  7.7 5.7 %collective-permute-done.2.refs_1_ = bf16[144,640]{1,0:T(8,128)(2,1)S(1)} collective-permute-done((bf16[144,640]{1,0:T(8,128)(2,1)}, bf16[144,640]{1,0:T(8,128)(2,1)S(1)}, u32[]{:S(2)}, u32[]{:S(2)}) %collective-permute-start.2) | collective-permute-done | bytes 184352 | tf_op jit(solution)/shard_map/ppermute | solution.py:322
  14.4 3.9 %collective-permute-start.5 = (bf16[128,1024]{1,0:T(8,128)(2,1)S(1)}, bf16[128,1024]{1,0:T(8,128)(2,1)S(1)}, u32[]{:S(2)}, u32[]{:S(2)}) collective-permute-start(bf16[128,1024]{1,0:T(8,128)(2,1)S(1)} %get-tuple-element.35.refs_0_), channel_id=1, source_target_pairs={{0,6},{1,7},{2,0},{3,1},{4,2},{5,3},{6,4},{7,5},{8,14},{9,15},{10,... | collective-permute-start | bytes 786440 | tf_op jit(solution)/shard_map/ppermute | solution.py:322
  18.9 1.8 %collective-permute-start.8 = (bf16[2,96,640]{2,1,0:T(8,128)(2,1)S(1)}, bf16[2,96,640]{2,1,0:T(8,128)(2,1)S(1)}, u32[]{:S(2)}, u32[]{:S(2)}) collective-permute-start(bf16[2,96,640]{2,1,0:T(8,128)(2,1)S(1)} %get-tuple-element.40), channel_id=1, source_target_pairs={{0,1},{1,0},{2,3},{3,2},{4,5},{5,4},{6,7},{7,6},{8,9},{9,8},{10,11... | collective-permute-start | bytes 737288 | tf_op jit(solution)/shard_map/ppermute | solution.py:333
  20.7 2.0 %collective-permute-done.6.refs_0_ = bf16[144,640]{1,0:T(8,128)(2,1)S(1)} collective-permute-done((bf16[144,640]{1,0:T(8,128)(2,1)S(1)}, bf16[144,640]{1,0:T(8,128)(2,1)S(1)}, u32[]{:S(2)}, u32[]{:S(2)}) %collective-permute-start.6) | collective-permute-done | bytes 184352 | tf_op jit(solution)/shard_map/ppermute | solution.py:322
  22.9 1.8 %collective-permute-start.9 = (bf16[2,32,640]{2,1,0:T(8,128)(2,1)S(1)}, bf16[2,32,640]{2,1,0:T(8,128)(2,1)S(1)}, u32[]{:S(2)}, u32[]{:S(2)}) collective-permute-start(bf16[2,32,640]{2,1,0:T(8,128)(2,1)S(1)} %get-tuple-element.41), channel_id=1, source_target_pairs={{0,1},{1,0},{2,3},{3,2},{4,5},{5,4},{6,7},{7,6},{8,9},{9,8},{10,11... | collective-permute-start | bytes 245768 | tf_op jit(solution)/shard_map/ppermute | solution.py:333
  24.7 2.4 %collective-permute-done.5.refs_2_ = bf16[128,1024]{1,0:T(8,128)(2,1)S(1)} collective-permute-done((bf16[128,1024]{1,0:T(8,128)(2,1)S(1)}, bf16[128,1024]{1,0:T(8,128)(2,1)S(1)}, u32[]{:S(2)}, u32[]{:S(2)}) %collective-permute-start.5) | collective-permute-done | bytes 262176 | tf_op jit(solution)/shard_map/ppermute | solution.py:322
  27.1 4.6 %collective-permute-done.4.refs_1_ = bf16[128,1024]{1,0:T(8,128)(2,1)S(1)} collective-permute-done((bf16[128,1024]{1,0:T(8,128)(2,1)S(1)}, bf16[128,1024]{1,0:T(8,128)(2,1)S(1)}, u32[]{:S(2)}, u32[]{:S(2)}) %collective-permute-start.4) | collective-permute-done | bytes 262176 | tf_op jit(solution)/shard_map/ppermute | solution.py:322
  32.9 2.6 %collective-permute-done.10.refs_1_ = bf16[2,2,192,640]{3,2,1,0:T(8,128)(2,1)S(1)} collective-permute-done((bf16[2,2,192,640]{3,2,1,0:T(8,128)(2,1)S(1)}, bf16[2,2,192,640]{3,2,1,0:T(8,128)(2,1)S(1)}, u32[]{:S(2)}, u32[]{:S(2)}) %collective-permute-start.10) | collective-permute-done | bytes 983072 | tf_op jit(solution)/shard_map/ppermute | solution.py:419
  35.6 1.6 %collective-permute-start.13 = (bf16[2,192,640]{2,1,0:T(8,128)(2,1)S(1)}, bf16[2,192,640]{2,1,0:T(8,128)(2,1)S(1)}, u32[]{:S(2)}, u32[]{:S(2)}) collective-permute-start(bf16[2,192,640]{2,1,0:T(8,128)(2,1)S(1)} %shard_map.83.refs_2_), channel_id=1, source_target_pairs={{0,16},{8,24},{16,0},{24,8},{1,17},{9,25},{17,1},{25,9},{2,18},{10... | collective-permute-start | bytes 1474568 | tf_op jit(solution)/shard_map/ppermute | solution.py:426
  38.7 8.4 %collective-permute-done.7.refs_0_ = bf16[128,1024]{1,0:T(8,128)(2,1)S(1)} collective-permute-done((bf16[128,1024]{1,0:T(8,128)(2,1)S(1)}, bf16[128,1024]{1,0:T(8,128)(2,1)S(1)}, u32[]{:S(2)}, u32[]{:S(2)}) %collective-permute-start.7) | collective-permute-done | bytes 262176 | tf_op jit(solution)/shard_map/ppermute | solution.py:322
  49.7 2.6 %collective-permute-done.12.refs_4_ = bf16[2,32,1024]{2,1,0:T(8,128)(2,1)S(1)} collective-permute-done((bf16[2,32,1024]{2,1,0:T(8,128)(2,1)S(1)}, bf16[2,32,1024]{2,1,0:T(8,128)(2,1)S(1)}, u32[]{:S(2)}, u32[]{:S(2)}) %collective-permute-start.12) | collective-permute-done | bytes 131104 | tf_op jit(solution)/shard_map/ppermute | solution.py:333
  53.4 3.4 %collective-permute-done.14.refs_1_ = bf16[2,2,192,1024]{3,2,1,0:T(8,128)(2,1)S(1)} collective-permute-done((bf16[2,2,192,1024]{3,2,1,0:T(8,128)(2,1)S(1)}, bf16[2,2,192,1024]{3,2,1,0:T(8,128)(2,1)S(1)}, u32[]{:S(2)}, u32[]{:S(2)}) %collective-permute-start.14) | collective-permute-done | bytes 1572896 | tf_op jit(solution)/shard_map/ppermute | solution.py:419
  58.3 3.1 %collective-permute-start.1 = (bf16[128,384]{1,0:T(8,128)(2,1)S(1)}, bf16[128,384]{1,0:T(8,128)(2,1)S(1)}, u32[]{:S(2)}, u32[]{:S(2)}) collective-permute-start(bf16[128,384]{1,0:T(8,128)(2,1)S(1)} %get-tuple-element.32.refs_0_), channel_id=1, source_target_pairs={{0,6},{1,7},{2,0},{3,1},{4,2},{5,3},{6,4},{7,5},{8,14},{9,15},{10,... | collective-permute-start | bytes 294920 | tf_op jit(solution)/shard_map/ppermute | solution.py:322
  61.4 3.6 %collective-permute-done.refs_1_ = bf16[128,384]{1,0:T(8,128)(2,1)S(1)} collective-permute-done((bf16[128,384]{1,0:T(8,128)(2,1)S(1)}, bf16[128,384]{1,0:T(8,128)(2,1)S(1)}, u32[]{:S(2)}, u32[]{:S(2)}) %collective-permute-start) | collective-permute-done | bytes 98336 | tf_op jit(solution)/shard_map/ppermute | solution.py:322
  65.2 1.6 %collective-permute-start.16 = (bf16[2,96,384]{2,1,0:T(8,128)(2,1)S(1)}, bf16[2,96,384]{2,1,0:T(8,128)(2,1)S(1)}, u32[]{:S(2)}, u32[]{:S(2)}) collective-permute-start(bf16[2,96,384]{2,1,0:T(8,128)(2,1)S(1)} %get-tuple-element.52), channel_id=1, source_target_pairs={{0,1},{1,0},{2,3},{3,2},{4,5},{5,4},{6,7},{7,6},{8,9},{9,8},{10,11... | collective-permute-start | bytes 442376 | tf_op jit(solution)/shard_map/ppermute | solution.py:333
  68.1 3.3 %collective-permute-done.15.refs_0_ = bf16[128,384]{1,0:T(8,128)(2,1)S(1)} collective-permute-done((bf16[128,384]{1,0:T(8,128)(2,1)S(1)}, bf16[128,384]{1,0:T(8,128)(2,1)S(1)}, u32[]{:S(2)}, u32[]{:S(2)}) %collective-permute-start.15) | collective-permute-done | bytes 98336 | tf_op jit(solution)/shard_map/ppermute | solution.py:322
  74.2 1.6 %collective-permute-done.17.refs_4_ = bf16[2,32,384]{2,1,0:T(8,128)(2,1)S(1)} collective-permute-done((bf16[2,32,384]{2,1,0:T(8,128)(2,1)S(1)}, bf16[2,32,384]{2,1,0:T(8,128)(2,1)S(1)}, u32[]{:S(2)}, u32[]{:S(2)}) %collective-permute-start.17) | collective-permute-done | bytes 49184 | tf_op jit(solution)/shard_map/ppermute | solution.py:333
  81.6 2.1 %collective-permute-done.19 = f32[2,256]{1,0:T(2,128)S(1)} collective-permute-done((f32[2,256]{1,0:T(2,128)S(1)}, f32[2,256]{1,0:T(2,128)S(1)}, u32[]{:S(2)}, u32[]{:S(2)}) %collective-permute-start.19) | collective-permute-done | bytes 2080 | tf_op jit(solution)/shard_map/ppermute | solution.py:464
  84.2 2.0 %collective-permute-start.21 = (f32[2,2,256]{2,1,0:T(2,128)S(1)}, f32[2,2,256]{2,1,0:T(2,128)S(1)}, u32[]{:S(2)}, u32[]{:S(2)}) collective-permute-start(f32[2,2,256]{2,1,0:T(2,128)S(1)} %pad_maximum_fusion.refs_2_), channel_id=1, source_target_pairs={{4,0},{5,1},{6,2},{7,3},{0,4},{1,5},{2,6},{3,7},{12,8},{13,9},{14,... | collective-permute-start | bytes 12296 | tf_op jit(solution)/shard_map/ppermute | solution.py:466
  86.2 2.1 %collective-permute-start.20 = (f32[2,2,256]{2,1,0:T(2,128)S(1)}, f32[2,2,256]{2,1,0:T(2,128)S(1)}, u32[]{:S(2)}, u32[]{:S(2)}) collective-permute-start(f32[2,2,256]{2,1,0:T(2,128)S(1)} %pad_maximum_fusion.refs_2_), channel_id=1, source_target_pairs={{2,0},{3,1},{4,2},{5,3},{6,4},{7,5},{0,6},{1,7},{10,8},{11,9},{12,... | collective-permute-start | bytes 12296 | tf_op jit(solution)/shard_map/ppermute | solution.py:466
  90.8 2.7 %shard_map.96 = (f32[192,2,2048]{2,1,0:T(2,128)}, f32[8,128]{1,0:T(8,128)}) custom-call(bf16[2,2,192,1024]{3,2,1,0:T(8,128)(2,1)S(1)} %get-tuple-element.47.refs_0_.refs_2_, bf16[2,2,192,1024]{3,2,1,0:T(8,128)(2,1)S(1)} %collective-permute-done.14.refs_1_, ...), custom_call_target="tpu_custom_call", output_to_operand_aliasing={{0}: (6, {})} | custom-call | flops 1 | bytes 1 | tf_op jit(solution)/shard_map/pallas_call | solution.py:43
  (60 shorter events, 22.9 us)
Async XLA Ops:
  2.5 10.8 %collective-permute-start.2 = (bf16[144,640]{1,0:T(8,128)(2,1)}, bf16[144,640]{1,0:T(8,128)(2,1)S(1)}, u32[]{:S(2)}, u32[]{:S(2)}) collective-permute-start(bf16[144,640]{1,0:T(8,128)(2,1)} %get-tuple-element.33.refs_0_), channel_id=1, source_target_pairs={{0,2},{1,3},{2,4},{3,5},{4,6},{5,7},{6,0},{7,1},{8,10},{9,11},{10,... | collective-permute-start | bytes 552968 | tf_op jit(solution)/shard_map/ppermute | solution.py:322
  5.6 13.0 %collective-permute-start.3 = (bf16[144,640]{1,0:T(8,128)(2,1)}, bf16[144,640]{1,0:T(8,128)(2,1)S(1)}, u32[]{:S(2)}, u32[]{:S(2)}) collective-permute-start(bf16[144,640]{1,0:T(8,128)(2,1)} %get-tuple-element.33.refs_0_), channel_id=1, source_target_pairs={{0,6},{1,7},{2,0},{3,1},{4,2},{5,3},{6,4},{7,5},{8,14},{9,15},{10,... | collective-permute-start | bytes 552968 | tf_op jit(solution)/shard_map/ppermute | solution.py:322
  13.3 9.4 %collective-permute-start.6 = (bf16[144,640]{1,0:T(8,128)(2,1)S(1)}, bf16[144,640]{1,0:T(8,128)(2,1)S(1)}, u32[]{:S(2)}, u32[]{:S(2)}) collective-permute-start(bf16[144,640]{1,0:T(8,128)(2,1)S(1)} %collective-permute-done.2.refs_1_), channel_id=1, source_target_pairs={{0,2},{1,3},{2,4},{3,5},{4,6},{5,7},{6,0},{7,1},{8,10},{9,11},{10,... | collective-permute-start | bytes 552968 | tf_op jit(solution)/shard_map/ppermute | solution.py:322
  14.4 12.6 %collective-permute-start.5 = (bf16[128,1024]{1,0:T(8,128)(2,1)S(1)}, bf16[128,1024]{1,0:T(8,128)(2,1)S(1)}, u32[]{:S(2)}, u32[]{:S(2)}) collective-permute-start(bf16[128,1024]{1,0:T(8,128)(2,1)S(1)} %get-tuple-element.35.refs_0_), channel_id=1, source_target_pairs={{0,6},{1,7},{2,0},{3,1},{4,2},{5,3},{6,4},{7,5},{8,14},{9,15},{10,... | collective-permute-start | bytes 786440 | tf_op jit(solution)/shard_map/ppermute | solution.py:322
  18.4 13.3 %collective-permute-start.4 = (bf16[128,1024]{1,0:T(8,128)(2,1)S(1)}, bf16[128,1024]{1,0:T(8,128)(2,1)S(1)}, u32[]{:S(2)}, u32[]{:S(2)}) collective-permute-start(bf16[128,1024]{1,0:T(8,128)(2,1)S(1)} %get-tuple-element.35.refs_0_), channel_id=1, source_target_pairs={{0,2},{1,3},{2,4},{3,5},{4,6},{5,7},{6,0},{7,1},{8,10},{9,11},{10,... | collective-permute-start | bytes 786440 | tf_op jit(solution)/shard_map/ppermute | solution.py:322
  18.9 13.1 %collective-permute-start.8 = (bf16[2,96,640]{2,1,0:T(8,128)(2,1)S(1)}, bf16[2,96,640]{2,1,0:T(8,128)(2,1)S(1)}, u32[]{:S(2)}, u32[]{:S(2)}) collective-permute-start(bf16[2,96,640]{2,1,0:T(8,128)(2,1)S(1)} %get-tuple-element.40), channel_id=1, source_target_pairs={{0,1},{1,0},{2,3},{3,2},{4,5},{5,4},{6,7},{7,6},{8,9},{9,8},{10,11... | collective-permute-start | bytes 737288 | tf_op jit(solution)/shard_map/ppermute | solution.py:333
  22.9 9.1 %collective-permute-start.9 = (bf16[2,32,640]{2,1,0:T(8,128)(2,1)S(1)}, bf16[2,32,640]{2,1,0:T(8,128)(2,1)S(1)}, u32[]{:S(2)}, u32[]{:S(2)}) collective-permute-start(bf16[2,32,640]{2,1,0:T(8,128)(2,1)S(1)} %get-tuple-element.41), channel_id=1, source_target_pairs={{0,1},{1,0},{2,3},{3,2},{4,5},{5,4},{6,7},{7,6},{8,9},{9,8},{10,11... | collective-permute-start | bytes 245768 | tf_op jit(solution)/shard_map/ppermute | solution.py:333
  32.9 2.6 %collective-permute-start.10 = (bf16[2,2,192,640]{3,2,1,0:T(8,128)(2,1)S(1)}, bf16[2,2,192,640]{3,2,1,0:T(8,128)(2,1)S(1)}, u32[]{:S(2)}, u32[]{:S(2)}) collective-permute-start(bf16[2,2,192,640]{3,2,1,0:T(8,128)(2,1)S(1)} %get-tuple-element.43), channel_id=1, source_target_pairs={{0,8},{8,0},{16,24},{24,16},{1,9},{9,1},{17,25},{25,17},{2,10},{10... | collective-permute-start | bytes 2949128 | tf_op jit(solution)/shard_map/ppermute | solution.py:419
  35.6 16.7 %collective-permute-start.13 = (bf16[2,192,640]{2,1,0:T(8,128)(2,1)S(1)}, bf16[2,192,640]{2,1,0:T(8,128)(2,1)S(1)}, u32[]{:S(2)}, u32[]{:S(2)}) collective-permute-start(bf16[2,192,640]{2,1,0:T(8,128)(2,1)S(1)} %shard_map.83.refs_2_), channel_id=1, source_target_pairs={{0,16},{8,24},{16,0},{24,8},{1,17},{9,25},{17,1},{25,9},{2,18},{10... | collective-permute-start | bytes 1474568 | tf_op jit(solution)/shard_map/ppermute | solution.py:426
  37.2 9.9 %collective-permute-start.7 = (bf16[128,1024]{1,0:T(8,128)(2,1)S(1)}, bf16[128,1024]{1,0:T(8,128)(2,1)S(1)}, u32[]{:S(2)}, u32[]{:S(2)}) collective-permute-start(bf16[128,1024]{1,0:T(8,128)(2,1)S(1)} %collective-permute-done.4.refs_1_), channel_id=1, source_target_pairs={{0,2},{1,3},{2,4},{3,5},{4,6},{5,7},{6,0},{7,1},{8,10},{9,11},{10,... | collective-permute-start | bytes 786440 | tf_op jit(solution)/shard_map/ppermute | solution.py:322
  37.2 12.5 %collective-permute-start.11 = (bf16[2,96,1024]{2,1,0:T(8,128)(2,1)S(1)}, bf16[2,96,1024]{2,1,0:T(8,128)(2,1)S(1)}, u32[]{:S(2)}, u32[]{:S(2)}) collective-permute-start(bf16[2,96,1024]{2,1,0:T(8,128)(2,1)S(1)} %get-tuple-element.45), channel_id=1, source_target_pairs={{0,1},{1,0},{2,3},{3,2},{4,5},{5,4},{6,7},{7,6},{8,9},{9,8},{10,11... | collective-permute-start | bytes 1179656 | tf_op jit(solution)/shard_map/ppermute | solution.py:333
  47.3 5.0 %collective-permute-start.12 = (bf16[2,32,1024]{2,1,0:T(8,128)(2,1)S(1)}, bf16[2,32,1024]{2,1,0:T(8,128)(2,1)S(1)}, u32[]{:S(2)}, u32[]{:S(2)}) collective-permute-start(bf16[2,32,1024]{2,1,0:T(8,128)(2,1)S(1)} %get-tuple-element.46), channel_id=1, source_target_pairs={{0,1},{1,0},{2,3},{3,2},{4,5},{5,4},{6,7},{7,6},{8,9},{9,8},{10,11... | collective-permute-start | bytes 393224 | tf_op jit(solution)/shard_map/ppermute | solution.py:333
  53.3 3.5 %collective-permute-start.14 = (bf16[2,2,192,1024]{3,2,1,0:T(8,128)(2,1)S(1)}, bf16[2,2,192,1024]{3,2,1,0:T(8,128)(2,1)S(1)}, u32[]{:S(2)}, u32[]{:S(2)}) collective-permute-start(bf16[2,2,192,1024]{3,2,1,0:T(8,128)(2,1)S(1)} %get-tuple-element.48), channel_id=1, source_target_pairs={{0,8},{8,0},{16,24},{24,16},{1,9},{9,1},{17,25},{25,17},{2,10},{10... | collective-permute-start | bytes 4718600 | tf_op jit(solution)/shard_map/ppermute | solution.py:419
  57.0 19.6 %collective-permute-start.18 = (bf16[2,192,1024]{2,1,0:T(8,128)(2,1)S(1)}, bf16[2,192,1024]{2,1,0:T(8,128)(2,1)S(1)}, u32[]{:S(2)}, u32[]{:S(2)}) collective-permute-start(bf16[2,192,1024]{2,1,0:T(8,128)(2,1)S(1)} %shard_map.87.refs_4_), channel_id=1, source_target_pairs={{0,16},{8,24},{16,0},{24,8},{1,17},{9,25},{17,1},{25,9},{2,18},{10... | collective-permute-start | bytes 2359304 | tf_op jit(solution)/shard_map/ppermute | solution.py:426
  57.5 7.5 %collective-permute-start = (bf16[128,384]{1,0:T(8,128)(2,1)S(1)}, bf16[128,384]{1,0:T(8,128)(2,1)S(1)}, u32[]{:S(2)}, u32[]{:S(2)}) collective-permute-start(bf16[128,384]{1,0:T(8,128)(2,1)S(1)} %get-tuple-element.32.refs_0_), channel_id=1, source_target_pairs={{0,2},{1,3},{2,4},{3,5},{4,6},{5,7},{6,0},{7,1},{8,10},{9,11},{10,... | collective-permute-start | bytes 294920 | tf_op jit(solution)/shard_map/ppermute | solution.py:322
  58.3 6.7 %collective-permute-start.1 = (bf16[128,384]{1,0:T(8,128)(2,1)S(1)}, bf16[128,384]{1,0:T(8,128)(2,1)S(1)}, u32[]{:S(2)}, u32[]{:S(2)}) collective-permute-start(bf16[128,384]{1,0:T(8,128)(2,1)S(1)} %get-tuple-element.32.refs_0_), channel_id=1, source_target_pairs={{0,6},{1,7},{2,0},{3,1},{4,2},{5,3},{6,4},{7,5},{8,14},{9,15},{10,... | collective-permute-start | bytes 294920 | tf_op jit(solution)/shard_map/ppermute | solution.py:322
  65.0 6.4 %collective-permute-start.15 = (bf16[128,384]{1,0:T(8,128)(2,1)S(1)}, bf16[128,384]{1,0:T(8,128)(2,1)S(1)}, u32[]{:S(2)}, u32[]{:S(2)}) collective-permute-start(bf16[128,384]{1,0:T(8,128)(2,1)S(1)} %collective-permute-done.refs_1_), channel_id=1, source_target_pairs={{0,2},{1,3},{2,4},{3,5},{4,6},{5,7},{6,0},{7,1},{8,10},{9,11},{10,... | collective-permute-start | bytes 294920 | tf_op jit(solution)/shard_map/ppermute | solution.py:322
  65.2 10.5 %collective-permute-start.16 = (bf16[2,96,384]{2,1,0:T(8,128)(2,1)S(1)}, bf16[2,96,384]{2,1,0:T(8,128)(2,1)S(1)}, u32[]{:S(2)}, u32[]{:S(2)}) collective-permute-start(bf16[2,96,384]{2,1,0:T(8,128)(2,1)S(1)} %get-tuple-element.52), channel_id=1, source_target_pairs={{0,1},{1,0},{2,3},{3,2},{4,5},{5,4},{6,7},{7,6},{8,9},{9,8},{10,11... | collective-permute-start | bytes 442376 | tf_op jit(solution)/shard_map/ppermute | solution.py:333
  71.6 4.2 %collective-permute-start.17 = (bf16[2,32,384]{2,1,0:T(8,128)(2,1)S(1)}, bf16[2,32,384]{2,1,0:T(8,128)(2,1)S(1)}, u32[]{:S(2)}, u32[]{:S(2)}) collective-permute-start(bf16[2,32,384]{2,1,0:T(8,128)(2,1)S(1)} %get-tuple-element.53), channel_id=1, source_target_pairs={{0,1},{1,0},{2,3},{3,2},{4,5},{5,4},{6,7},{7,6},{8,9},{9,8},{10,11... | collective-permute-start | bytes 147464 | tf_op jit(solution)/shard_map/ppermute | solution.py:333
  79.3 11.5 %collective-permute-start.24 = (bf16[2,192,384]{2,1,0:T(8,128)(2,1)S(1)}, bf16[2,192,384]{2,1,0:T(8,128)(2,1)S(1)}, u32[]{:S(2)}, u32[]{:S(2)}) collective-permute-start(bf16[2,192,384]{2,1,0:T(8,128)(2,1)S(1)} %shard_map.94.refs_6_.refs_7_), channel_id=1, source_target_pairs={{0,16},{8,24},{16,0},{24,8},{1,17},{9,25},{17,1},{25,9},{2,18},{10... | collective-permute-start | bytes 884744 | tf_op jit(solution)/shard_map/ppermute | solution.py:426
  80.1 3.6 %collective-permute-start.19 = (f32[2,256]{1,0:T(2,128)S(1)}, f32[2,256]{1,0:T(2,128)S(1)}, u32[]{:S(2)}, u32[]{:S(2)}) collective-permute-start(f32[2,256]{1,0:T(2,128)S(1)} %get-tuple-element.57.refs_2_), channel_id=1, source_target_pairs={{0,1},{1,0},{2,3},{3,2},{4,5},{5,4},{6,7},{7,6},{8,9},{9,8},{10,11... | collective-permute-start | bytes 6152 | tf_op jit(solution)/shard_map/ppermute | solution.py:464
  83.7 5.4 %collective-permute-start.22 = (f32[2,2,256]{2,1,0:T(2,128)S(1)}, f32[2,2,256]{2,1,0:T(2,128)S(1)}, u32[]{:S(2)}, u32[]{:S(2)}) collective-permute-start(f32[2,2,256]{2,1,0:T(2,128)S(1)} %pad_maximum_fusion.refs_2_), channel_id=1, source_target_pairs={{6,0},{7,1},{0,2},{1,3},{2,4},{3,5},{4,6},{5,7},{14,8},{15,9},{8,1... | collective-permute-start | bytes 12296 | tf_op jit(solution)/shard_map/ppermute | solution.py:466
  84.2 4.8 %collective-permute-start.21 = (f32[2,2,256]{2,1,0:T(2,128)S(1)}, f32[2,2,256]{2,1,0:T(2,128)S(1)}, u32[]{:S(2)}, u32[]{:S(2)}) collective-permute-start(f32[2,2,256]{2,1,0:T(2,128)S(1)} %pad_maximum_fusion.refs_2_), channel_id=1, source_target_pairs={{4,0},{5,1},{6,2},{7,3},{0,4},{1,5},{2,6},{3,7},{12,8},{13,9},{14,... | collective-permute-start | bytes 12296 | tf_op jit(solution)/shard_map/ppermute | solution.py:466
  86.2 3.6 %collective-permute-start.20 = (f32[2,2,256]{2,1,0:T(2,128)S(1)}, f32[2,2,256]{2,1,0:T(2,128)S(1)}, u32[]{:S(2)}, u32[]{:S(2)}) collective-permute-start(f32[2,2,256]{2,1,0:T(2,128)S(1)} %pad_maximum_fusion.refs_2_), channel_id=1, source_target_pairs={{2,0},{3,1},{4,2},{5,3},{6,4},{7,5},{0,6},{1,7},{10,8},{11,9},{12,... | collective-permute-start | bytes 12296 | tf_op jit(solution)/shard_map/ppermute | solution.py:466
  (7 other events, 67.3 us)

commit v14 on v10

--- a/solution.py
+++ b/solution.py
@@ -160,15 +160,17 @@
         copy.wait()
 
 
-def stacked_rows(refs, e):
-    return refs[0][e] if len(refs) == 1 else jnp.concatenate([ref[e] for ref in refs], axis=0)
-
-
-def term_kernel(turned_ref, *refs):
+def stacked_rows(refs, e, at):
+    rows = [ref[e, :, at] for ref in refs]
+    return rows[0] if len(rows) == 1 else jnp.concatenate(rows, axis=0)
+
+
+def term_kernel(start, turned_ref, *refs):
     part_refs, keep_ref, give_ref = refs[:-2], refs[-2], refs[-1]
     held, _, across, share, slots = turned_ref.shape
+    at = slice(start, start + keep_ref.shape[3])
     for e in range(held):
-        scaled = stacked_rows(part_refs, e)
+        scaled = stacked_rows(part_refs, e, at)
         for other, ref in ((1, give_ref), (0, keep_ref)):
             left = turned_ref[e, other].reshape(across * share, slots)
             term = jnp.dot(left, scaled, preferred_element_type=F32).astype(BF16)
@@ -187,19 +189,25 @@
             start += rows
 
 
-def last_kernel(cuts, start, keep_ref, got_ref, *refs):
+def last_kernel(cuts, start, *refs):
     out_ref, mark_ref, total_ref, sem = refs[-4:]
     mark_ref[...] = jnp.zeros(mark_ref.shape, F32)
-    others = len(cuts) * (keep_ref.shape[0] - 1)
-    for e in range(keep_ref.shape[1]):
-        row = 0
-        for part, rows in enumerate(cuts):
-            at = slice(row, row + rows)
-            total = keep_ref[0, e, at].astype(F32) + got_ref[0, e, at].astype(F32)
-            for ref in refs[part : others : len(cuts)]:
-                total = total + ref[e].astype(F32)
-            total_ref[at, e, :] = total
-            row += rows
+    column = 0
+    for rows_of in cuts:
+        keep_ref, got_ref, *refs = refs
+        across, held, _, width = keep_ref.shape
+        others, refs = refs[: len(rows_of) * (across - 1)], refs[len(rows_of) * (across - 1) :]
+        columns = slice(column, column + width)
+        column += width
+        for e in range(held):
+            row = 0
+            for cut, rows in enumerate(rows_of):
+                at = slice(row, row + rows)
+                total = keep_ref[0, e, at].astype(F32) + got_ref[0, e, at].astype(F32)
+                for ref in others[cut :: len(rows_of)]:
+                    total = total + ref[e].astype(F32)
+                total_ref[at, e, columns] = total
+                row += rows
     copy = pltpu.make_async_copy(
         total_ref, out_ref.at[:, :, start : start + total_ref.shape[2]], sem
     )
@@ -214,7 +222,7 @@
     width = part_refs[0].shape[2]
     for e in range(weight_ref.shape[0]):
         raw = lax.dot_general(
-            stacked_rows(part_refs, e),
+            stacked_rows(part_refs, e, slice(None)),
             weight_ref[e, :, start : start + width],
             (((1,), (1,)), ((), ())),
             preferred_element_type=F32,
@@ -282,12 +290,11 @@
 
 def chunks_of(features):
     unit = features // 16
-    return [4 * unit, 6 * unit, 6 * unit]
-
-
-def cuts_of(share, c):
-    first = 16 * (share // 32)
-    return [first, share - first] if c == 1 else [share]
+    return [[7 * unit], [5 * unit, 4 * unit]]
+
+
+def cuts_of(share, first):
+    return [share // 3] * 3 if first else [share]
 
 
 sds = jax.ShapeDtypeStruct
@@ -384,7 +391,8 @@
     tokens, chosen = route_ids.shape
     share, across = units // dp, dp // 2
     direct = groups == LINE * SIDES
-    widths = chunks_of(features)
+    chunks = chunks_of(features)
+    widths = [sum(chunk) for chunk in chunks]
     count = len(widths)
 
     ids, probs = route_ids.T, route_probs.T
@@ -421,15 +429,15 @@
         )
         state["raw"] = made if final else made[0]
 
-    def reduced(c):
-        parts, width = arrived[c], widths[c]
+    def reduced(c, at, width):
         piece = sds((across, held, share, width), BF16)
-        after = summed[-1][2][:1] if c else ()
-        keep, give = call(term_kernel, [piece, piece], turned, *parts, after=after)
+        after = summed[0][2][:2] if len(summed) == 1 else ()
+        kernel = functools.partial(term_kernel, at)
+        keep, give = call(kernel, [piece, piece], turned, *arrived[c], after=after)
         got = lax.ppermute(give, "dp", [(i, i ^ 1) for i in range(dp)])
-        if c == count - 1:
+        if c == count - 1 and at == 0:
             accumulated(c)
-        cuts = cuts_of(share, c)
+        cuts = cuts_of(share, not summed)
         pieces = [sds((held, rows, width), BF16) for rows in cuts]
         pairs = call(functools.partial(pair_kernel, cuts), pieces * (across - 1), keep, got)
         others = []
@@ -437,40 +445,42 @@
             step = 1 + i // len(cuts)
             shift = [(2 * r + k, 2 * ((r + step) % across) + k) for r in range(across) for k in range(2)]
             others.append(lax.ppermute(pair, "dp", shift))
-        summed.append((keep, got, others))
-
-    def finished(c):
-        keep, got, others = summed[c]
+        summed.append((keep, got, others, starts[c] + at))
+
+    def finished(first, last):
         before = [] if state["grad"] is None else [state["grad"]]
-        count = 2 + len(others)
+        done = summed[first:last]
+        args = [x for keep, got, others, _ in done for x in (keep, got, *others)]
+        cuts = [cuts_of(share, j == 0) for j in range(first, last)]
         state["grad"], _ = call(
-            functools.partial(last_kernel, cuts_of(share, c), starts[c]),
+            functools.partial(last_kernel, cuts, done[0][3]),
             [sds((share, held, features), F32), sds((8, 128), F32)],
-            keep,
-            got,
-            *others,
+            *args,
             *before,
-            in_specs=[VMEM] * count + [ANY] * len(before),
+            in_specs=[VMEM] * len(args) + [ANY] * len(before),
             out_specs=[ANY, VMEM],
-            input_output_aliases={count: 0} if before else {},
+            input_output_aliases={len(args): 0} if before else {},
             scratch_shapes=[
-                pltpu.VMEM((share, held, widths[c]), F32),
+                pltpu.VMEM((share, held, sum(keep.shape[3] for keep, *_ in done)), F32),
                 pltpu.SemaphoreType.DMA,
             ],
         )
 
     if direct:
         arrived, early = [], relay.early(0)
-    for c in range(count):
+    for c, chunk in enumerate(chunks):
         if direct:
             arrived.append(relay.late(c, early))
             if c + 1 < count:
                 early = relay.early(c + 1)
         if c >= 1:
             accumulated(c - 1)
-        reduced(c)
-        if c >= 1:
-            finished(c - 1)
+        at = 0
+        for width in chunk:
+            reduced(c, at, width)
+            at += width
+            if len(summed) > 1:
+                finished(len(summed) - 2, len(summed) - 1)
     hidden_grad, sums = state["raw"]
 
     if direct:
@@ -493,7 +503,7 @@
         *returned,
         keep=False,
     ).T
-    finished(count - 1)
+    finished(len(summed) - 1, len(summed))
     weight_grad = state["grad"]
     return (hidden_grad.reshape(hidden.shape), prob_grad, weight_grad)
 

time: 94.7 us -> 91.7 us (0.968)
  starting transfers between devices: 29.8 us -> 27 us
  waiting for transfers between devices: 47.7 us -> 46.5 us
  local copies, waits for them, and re-layouts: 1.06 us -> 2.11 us
    ppermute x9 -> x6, starting transfers between devices: 14.1 us -> 9.65 us  [along(): return lax.ppermute(block, 'expert', pairs)]
    ppermute x6 -> x4, starting transfers between devices: 8.66 us -> 5.37 us  [pick(): lax.ppermute(other, 'expert', [(i, i ^ 1) for i in range(LINE * SIDES)])]
    ppermute x9 -> x6, waiting for transfers between devices: 23.4 us -> 26.4 us  [along(): return lax.ppermute(block, 'expert', pairs)]
    ppermute x4 -> x5, starting transfers between devices: 4.26 us -> 6.84 us  [reduced(): others.append(lax.ppermute(pair, 'dp', shift))]
    ppermute x3, waiting for transfers between devices: 4.03 us -> 2.03 us  [reduced(): got = lax.ppermute(give, 'dp', [(i, i ^ 1) for i in range(dp)])]
    ppermute x3, starting transfers between devices: 2.03 us -> 3.79 us  [body(): lax.ppermute(both, 'expert', [(moved(i, d, 0), i) for i in range(groups)])]
    ppermute x4 -> x5, waiting for transfers between devices: 14 us -> 12.4 us  [reduced(): others.append(lax.ppermute(pair, 'dp', shift))]
    unnamed x12 -> x14, local copies, waits for them, and re-layouts: 1.06 us -> 2.11 us
  transfers between devices with their start and end apart: 26 -> 22, of which waited for: 14 -> 12; matrix products, arithmetic and copies ran while one was open for 0% -> 0% of each run, Pallas kernels for 9% -> 8%
where the time goes in v14:
time: 91.7 us; the launch traced here: 91.5 us
  waiting for transfers between devices  46.5 us (51%)
  starting transfers between devices  27 us (29%)
  Pallas kernels  15 us (16%)
  local copies, waits for them, and re-layouts  2.11 us (2%)
    ppermute x6, waiting for transfers between devices, along(): return lax.ppermute(block, 'expert', pairs)  26.4 us
    pallas_call x19, Pallas kernels, __call__(): pl.pallas_call(body, out_shape=outs, in_specs=in_specs, compiler_params=p...  15 us
    ppermute x5, waiting for transfers between devices, reduced(): others.append(lax.ppermute(pair, 'dp', shift))  12.4 us
    ppermute x6, starting transfers between devices, along(): return lax.ppermute(block, 'expert', pairs)  9.65 us
    ppermute x5, starting transfers between devices, reduced(): others.append(lax.ppermute(pair, 'dp', shift))  6.84 us
    ppermute x4, starting transfers between devices, pick(): lax.ppermute(other, 'expert', [(i, i ^ 1) for i in range(LINE * SIDES)])  5.37 us
    ppermute x3, starting transfers between devices, body(): lax.ppermute(both, 'expert', [(moved(i, d, 0), i) for i in range(groups)])  3.79 us
    ppermute x4, waiting for transfers between devices, pick(): lax.ppermute(other, 'expert', [(i, i ^ 1) for i in range(LINE * SIDES)])  3.19 us
  transfers between devices with their start and end apart: 22, of which 12 were waited for; matrix products, arithmetic and copies ran while one was open for 0% of the time, Pallas kernels for 8%

profile of v14, /device:TPU:0, one launch (start us, length us, event | category | flops | bytes accessed | tf_op | source)
XLA Modules:
  0.0 91.5 jit_solution(16527350317444112971)
XLA Ops:
  0.6 1.9 %shard_map.77 = (s32[2,128]{1,0:T(2,128)}, bf16[144,896]{1,0:T(8,128)(2,1)}) custom-call(s32[2,128]{1,0:T(2,128)} %bitcast.13, f32[2,128]{1,0:T(2,128)} %bitcast.10, bf16[128,2048]{1,0:T(8,128)(2,1)} %rows_ref.3), custom_call_target="tpu_custom_call" | custom-call | flops 1 | bytes 1 | tf_op jit(solution)/shard_map/pallas_call | solution.py:43
  2.5 3.1 %collective-permute-start.2 = (bf16[144,896]{1,0:T(8,128)(2,1)}, bf16[144,896]{1,0:T(8,128)(2,1)S(1)}, u32[]{:S(2)}, u32[]{:S(2)}) collective-permute-start(bf16[144,896]{1,0:T(8,128)(2,1)} %get-tuple-element.31.refs_0_), channel_id=1, source_target_pairs={{0,2},{1,3},{2,4},{3,5},{4,6},{5,7},{6,0},{7,1},{8,10},{9,11},{10,... | collective-permute-start | bytes 774152 | tf_op jit(solution)/shard_map/ppermute | solution.py:339
  5.6 2.1 %collective-permute-start.3 = (bf16[144,896]{1,0:T(8,128)(2,1)}, bf16[144,896]{1,0:T(8,128)(2,1)S(1)}, u32[]{:S(2)}, u32[]{:S(2)}) collective-permute-start(bf16[144,896]{1,0:T(8,128)(2,1)} %get-tuple-element.31.refs_0_), channel_id=1, source_target_pairs={{0,6},{1,7},{2,0},{3,1},{4,2},{5,3},{6,4},{7,5},{8,14},{9,15},{10,... | collective-permute-start | bytes 774152 | tf_op jit(solution)/shard_map/ppermute | solution.py:339
  7.7 7.2 %collective-permute-done.2.refs_1_ = bf16[144,896]{1,0:T(8,128)(2,1)S(1)} collective-permute-done((bf16[144,896]{1,0:T(8,128)(2,1)}, bf16[144,896]{1,0:T(8,128)(2,1)S(1)}, u32[]{:S(2)}, u32[]{:S(2)}) %collective-permute-start.2) | collective-permute-done | bytes 258080 | tf_op jit(solution)/shard_map/ppermute | solution.py:339
  16.3 2.9 %collective-permute-done.3.refs_2_ = bf16[144,896]{1,0:T(8,128)(2,1)S(1)} collective-permute-done((bf16[144,896]{1,0:T(8,128)(2,1)}, bf16[144,896]{1,0:T(8,128)(2,1)S(1)}, u32[]{:S(2)}, u32[]{:S(2)}) %collective-permute-start.3) | collective-permute-done | bytes 258080 | tf_op jit(solution)/shard_map/ppermute | solution.py:339
  20.6 1.8 %collective-permute-start.6 = (bf16[2,96,896]{2,1,0:T(8,128)(2,1)S(1)}, bf16[2,96,896]{2,1,0:T(8,128)(2,1)S(1)}, u32[]{:S(2)}, u32[]{:S(2)}) collective-permute-start(bf16[2,96,896]{2,1,0:T(8,128)(2,1)S(1)} %get-tuple-element.37), channel_id=1, source_target_pairs={{0,1},{1,0},{2,3},{3,2},{4,5},{5,4},{6,7},{7,6},{8,9},{9,8},{10,11... | collective-permute-start | bytes 1032200 | tf_op jit(solution)/shard_map/ppermute | solution.py:350
  22.4 1.8 %collective-permute-start = (bf16[128,1152]{1,0:T(8,128)(2,1)S(1)}, bf16[128,1152]{1,0:T(8,128)(2,1)S(1)}, u32[]{:S(2)}, u32[]{:S(2)}) collective-permute-start(bf16[128,1152]{1,0:T(8,128)(2,1)S(1)} %shard_map.76.refs_0_), channel_id=1, source_target_pairs={{0,2},{1,3},{2,4},{3,5},{4,6},{5,7},{6,0},{7,1},{8,10},{9,11},{10,... | collective-permute-start | bytes 884744 | tf_op jit(solution)/shard_map/ppermute | solution.py:339
  24.2 2.1 %collective-permute-start.1 = (bf16[128,1152]{1,0:T(8,128)(2,1)S(1)}, bf16[128,1152]{1,0:T(8,128)(2,1)S(1)}, u32[]{:S(2)}, u32[]{:S(2)}) collective-permute-start(bf16[128,1152]{1,0:T(8,128)(2,1)S(1)} %shard_map.76.refs_0_), channel_id=1, source_target_pairs={{0,6},{1,7},{2,0},{3,1},{4,2},{5,3},{6,4},{7,5},{8,14},{9,15},{10,... | collective-permute-start | bytes 884744 | tf_op jit(solution)/shard_map/ppermute | solution.py:339
  27.7 6.5 %collective-permute-done.refs_1_ = bf16[128,1152]{1,0:T(8,128)(2,1)S(1)} collective-permute-done((bf16[128,1152]{1,0:T(8,128)(2,1)S(1)}, bf16[128,1152]{1,0:T(8,128)(2,1)S(1)}, u32[]{:S(2)}, u32[]{:S(2)}) %collective-permute-start) | collective-permute-done | bytes 294944 | tf_op jit(solution)/shard_map/ppermute | solution.py:339
  34.2 3.9 %collective-permute-done.1.refs_2_ = bf16[128,1152]{1,0:T(8,128)(2,1)S(1)} collective-permute-done((bf16[128,1152]{1,0:T(8,128)(2,1)S(1)}, bf16[128,1152]{1,0:T(8,128)(2,1)S(1)}, u32[]{:S(2)}, u32[]{:S(2)}) %collective-permute-start.1) | collective-permute-done | bytes 294944 | tf_op jit(solution)/shard_map/ppermute | solution.py:339
  42.9 1.6 %collective-permute-start.11 = (bf16[2,64,896]{2,1,0:T(8,128)(2,1)S(1)}, bf16[2,64,896]{2,1,0:T(8,128)(2,1)S(1)}, u32[]{:S(2)}, u32[]{:S(2)}) collective-permute-start(bf16[2,64,896]{2,1,0:T(8,128)(2,1)S(1)} %get-tuple-element.41.refs_2_), channel_id=1, source_target_pairs={{0,16},{8,24},{16,0},{24,8},{1,17},{9,25},{17,1},{25,9},{2,18},{10... | collective-permute-start | bytes 688136 | tf_op jit(solution)/shard_map/ppermute | solution.py:447
  45.0 5.8 %collective-permute-done.5.refs_0_ = bf16[128,1152]{1,0:T(8,128)(2,1)S(1)} collective-permute-done((bf16[128,1152]{1,0:T(8,128)(2,1)S(1)}, bf16[128,1152]{1,0:T(8,128)(2,1)S(1)}, u32[]{:S(2)}, u32[]{:S(2)}) %collective-permute-start.5) | collective-permute-done | bytes 294944 | tf_op jit(solution)/shard_map/ppermute | solution.py:339
  53.4 3.2 %collective-permute-done.10.refs_4_ = bf16[2,32,1152]{2,1,0:T(8,128)(2,1)S(1)} collective-permute-done((bf16[2,32,1152]{2,1,0:T(8,128)(2,1)S(1)}, bf16[2,32,1152]{2,1,0:T(8,128)(2,1)S(1)}, u32[]{:S(2)}, u32[]{:S(2)}) %collective-permute-start.10) | collective-permute-done | bytes 147488 | tf_op jit(solution)/shard_map/ppermute | solution.py:350
  57.4 1.6 %collective-permute-start.19 = (bf16[2,64,896]{2,1,0:T(8,128)(2,1)S(1)}, bf16[2,64,896]{2,1,0:T(8,128)(2,1)S(1)}, u32[]{:S(2)}, u32[]{:S(2)}) collective-permute-start(bf16[2,64,896]{2,1,0:T(8,128)(2,1)S(1)} %get-tuple-element.51), channel_id=1, source_target_pairs={{0,16},{8,24},{16,0},{24,8},{1,17},{9,25},{17,1},{25,9},{2,18},{10... | collective-permute-start | bytes 688136 | tf_op jit(solution)/shard_map/ppermute | solution.py:447
  59.0 2.2 %shard_map.87 = (bf16[8,2,32,768]{3,2,1,0:T(8,128)(2,1)}, f32[2,256]{1,0:T(2,128)S(1)}) custom-call(bf16[2,768,2048]{2,1,0:T(8,128)(2,1)S(1)} %copy-done, bf16[2,96,1152]{2,1,0:T(8,128)(2,1)S(1)} %get-tuple-element.34.refs_5_.refs_1_, bf16[2,32,1152]{2,1,0:T(8,128)(2,1)S(1)} %get-tuple-element.42.refs_5_.refs_2_, ...), custom_call_target="tpu_custom_call" | custom-call | flops 1 | bytes 1 | tf_op jit(solution)/shard_map/pallas_call | solution.py:43
  61.3 4.1 %collective-permute-done.19.refs_4_ = bf16[2,64,896]{2,1,0:T(8,128)(2,1)S(1)} collective-permute-done((bf16[2,64,896]{2,1,0:T(8,128)(2,1)S(1)}, bf16[2,64,896]{2,1,0:T(8,128)(2,1)S(1)}, u32[]{:S(2)}, u32[]{:S(2)}) %collective-permute-start.19) | collective-permute-done | bytes 229408 | tf_op jit(solution)/shard_map/ppermute | solution.py:447
  65.4 1.6 %shard_map.89 = (f32[192,2,2048]{2,1,0:T(2,128)}, f32[8,128]{1,0:T(8,128)S(1)}) custom-call(bf16[2,2,192,896]{3,2,1,0:T(8,128)(2,1)S(1)} %get-tuple-element.39.refs_0_.refs_2_, bf16[2,2,192,896]{3,2,1,0:T(8,128)(2,1)S(1)} %collective-permute-done.8.refs_1_, bf16[2,64,896]{2,1,0:T(8,128)(2,1)S(1)} %collective-permute-done.11.refs_6_.refs_2_, ...), custom_call_target="tpu_custom_call" | custom-call | flops 1 | bytes 1 | tf_op jit(solution)/shard_map/pallas_call | solution.py:43
  67.7 1.6 %collective-permute-start.18 = (bf16[2,192,640]{2,1,0:T(8,128)(2,1)S(1)}, bf16[2,192,640]{2,1,0:T(8,128)(2,1)S(1)}, u32[]{:S(2)}, u32[]{:S(2)}) collective-permute-start(bf16[2,192,640]{2,1,0:T(8,128)(2,1)S(1)} %shard_map.88.refs_5_), channel_id=1, source_target_pairs={{0,16},{8,24},{16,0},{24,8},{1,17},{9,25},{17,1},{25,9},{2,18},{10... | collective-permute-start | bytes 1474568 | tf_op jit(solution)/shard_map/ppermute | solution.py:447
  70.1 1.6 %collective-permute-start.21 = (bf16[2,192,512]{2,1,0:T(8,128)(2,1)S(1)}, bf16[2,192,512]{2,1,0:T(8,128)(2,1)S(1)}, u32[]{:S(2)}, u32[]{:S(2)}) collective-permute-start(bf16[2,192,512]{2,1,0:T(8,128)(2,1)S(1)} %shard_map.91.refs_4_), channel_id=1, source_target_pairs={{0,16},{8,24},{16,0},{24,8},{1,17},{9,25},{17,1},{25,9},{2,18},{10... | collective-permute-start | bytes 1179656 | tf_op jit(solution)/shard_map/ppermute | solution.py:447
  72.8 2.4 %collective-permute-done.13 = f32[2,256]{1,0:T(2,128)S(1)} collective-permute-done((f32[2,256]{1,0:T(2,128)S(1)}, f32[2,256]{1,0:T(2,128)S(1)}, u32[]{:S(2)}, u32[]{:S(2)}) %collective-permute-start.13) | collective-permute-done | bytes 2080 | tf_op jit(solution)/shard_map/ppermute | solution.py:488
  75.3 2.4 %collective-permute-start.14 = (f32[2,2,256]{2,1,0:T(2,128)S(1)}, f32[2,2,256]{2,1,0:T(2,128)S(1)}, u32[]{:S(2)}, u32[]{:S(2)}) collective-permute-start(f32[2,2,256]{2,1,0:T(2,128)S(1)} %pad_maximum_fusion.refs_2_), channel_id=1, source_target_pairs={{2,0},{3,1},{4,2},{5,3},{6,4},{7,5},{0,6},{1,7},{10,8},{11,9},{12,... | collective-permute-start | bytes 12296 | tf_op jit(solution)/shard_map/ppermute | solution.py:490
  79.0 2.7 %collective-permute-done.18.refs_2_ = bf16[2,192,640]{2,1,0:T(8,128)(2,1)S(1)} collective-permute-done((bf16[2,192,640]{2,1,0:T(8,128)(2,1)S(1)}, bf16[2,192,640]{2,1,0:T(8,128)(2,1)S(1)}, u32[]{:S(2)}, u32[]{:S(2)}) %collective-permute-start.18) | collective-permute-done | bytes 491552 | tf_op jit(solution)/shard_map/ppermute | solution.py:447
  84.2 5.6 %collective-permute-done.21.refs_2_ = bf16[2,192,512]{2,1,0:T(8,128)(2,1)S(1)} collective-permute-done((bf16[2,192,512]{2,1,0:T(8,128)(2,1)S(1)}, bf16[2,192,512]{2,1,0:T(8,128)(2,1)S(1)}, u32[]{:S(2)}, u32[]{:S(2)}) %collective-permute-start.21) | collective-permute-done | bytes 393248 | tf_op jit(solution)/shard_map/ppermute | solution.py:447
  89.7 1.7 %shard_map.94 = (f32[192,2,2048]{2,1,0:T(2,128)}, f32[8,128]{1,0:T(8,128)}) custom-call(bf16[2,2,192,512]{3,2,1,0:T(8,128)(2,1)S(1)} %get-tuple-element.54.refs_0_.refs_2_, bf16[2,2,192,512]{3,2,1,0:T(8,128)(2,1)S(1)} %collective-permute-done.20.refs_1_, bf16[2,192,512]{2,1,0:T(8,128)(2,1)S(1)} %collective-permute-done.21.refs_2_, ...), custom_call_target="tpu_custom_call", output_to_operand_aliasing={{0}: (3, {})} | custom-call | flops 1 | bytes 1 | tf_op jit(solution)/shard_map/pallas_call | solution.py:43
  (54 shorter events, 19.2 us)
Async XLA Ops:
  0.6 21.7 %copy-start.3 = (bf16[128,2048]{1,0:T(8,128)(2,1)S(1)}, bf16[128,2048]{1,0:T(8,128)(2,1)}, u32[]{:S(2)}) copy-start(bf16[128,2048]{1,0:T(8,128)(2,1)} %rows_ref.3) | copy-start | bytes 1572868
  2.5 12.4 %collective-permute-start.2 = (bf16[144,896]{1,0:T(8,128)(2,1)}, bf16[144,896]{1,0:T(8,128)(2,1)S(1)}, u32[]{:S(2)}, u32[]{:S(2)}) collective-permute-start(bf16[144,896]{1,0:T(8,128)(2,1)} %get-tuple-element.31.refs_0_), channel_id=1, source_target_pairs={{0,2},{1,3},{2,4},{3,5},{4,6},{5,7},{6,0},{7,1},{8,10},{9,11},{10,... | collective-permute-start | bytes 774152 | tf_op jit(solution)/shard_map/ppermute | solution.py:339
  5.6 13.6 %collective-permute-start.3 = (bf16[144,896]{1,0:T(8,128)(2,1)}, bf16[144,896]{1,0:T(8,128)(2,1)S(1)}, u32[]{:S(2)}, u32[]{:S(2)}) collective-permute-start(bf16[144,896]{1,0:T(8,128)(2,1)} %get-tuple-element.31.refs_0_), channel_id=1, source_target_pairs={{0,6},{1,7},{2,0},{3,1},{4,2},{5,3},{6,4},{7,5},{8,14},{9,15},{10,... | collective-permute-start | bytes 774152 | tf_op jit(solution)/shard_map/ppermute | solution.py:339
  14.9 11.3 %collective-permute-start.4 = (bf16[144,896]{1,0:T(8,128)(2,1)S(1)}, bf16[144,896]{1,0:T(8,128)(2,1)S(1)}, u32[]{:S(2)}, u32[]{:S(2)}) collective-permute-start(bf16[144,896]{1,0:T(8,128)(2,1)S(1)} %collective-permute-done.2.refs_1_), channel_id=1, source_target_pairs={{0,2},{1,3},{2,4},{3,5},{4,6},{5,7},{6,0},{7,1},{8,10},{9,11},{10,... | collective-permute-start | bytes 774152 | tf_op jit(solution)/shard_map/ppermute | solution.py:339
  20.6 18.0 %collective-permute-start.6 = (bf16[2,96,896]{2,1,0:T(8,128)(2,1)S(1)}, bf16[2,96,896]{2,1,0:T(8,128)(2,1)S(1)}, u32[]{:S(2)}, u32[]{:S(2)}) collective-permute-start(bf16[2,96,896]{2,1,0:T(8,128)(2,1)S(1)} %get-tuple-element.37), channel_id=1, source_target_pairs={{0,1},{1,0},{2,3},{3,2},{4,5},{5,4},{6,7},{7,6},{8,9},{9,8},{10,11... | collective-permute-start | bytes 1032200 | tf_op jit(solution)/shard_map/ppermute | solution.py:350
  22.4 11.8 %collective-permute-start = (bf16[128,1152]{1,0:T(8,128)(2,1)S(1)}, bf16[128,1152]{1,0:T(8,128)(2,1)S(1)}, u32[]{:S(2)}, u32[]{:S(2)}) collective-permute-start(bf16[128,1152]{1,0:T(8,128)(2,1)S(1)} %shard_map.76.refs_0_), channel_id=1, source_target_pairs={{0,2},{1,3},{2,4},{3,5},{4,6},{5,7},{6,0},{7,1},{8,10},{9,11},{10,... | collective-permute-start | bytes 884744 | tf_op jit(solution)/shard_map/ppermute | solution.py:339
  24.2 14.0 %collective-permute-start.1 = (bf16[128,1152]{1,0:T(8,128)(2,1)S(1)}, bf16[128,1152]{1,0:T(8,128)(2,1)S(1)}, u32[]{:S(2)}, u32[]{:S(2)}) collective-permute-start(bf16[128,1152]{1,0:T(8,128)(2,1)S(1)} %shard_map.76.refs_0_), channel_id=1, source_target_pairs={{0,6},{1,7},{2,0},{3,1},{4,2},{5,3},{6,4},{7,5},{8,14},{9,15},{10,... | collective-permute-start | bytes 884744 | tf_op jit(solution)/shard_map/ppermute | solution.py:339
  26.5 12.0 %collective-permute-start.7 = (bf16[2,32,896]{2,1,0:T(8,128)(2,1)S(1)}, bf16[2,32,896]{2,1,0:T(8,128)(2,1)S(1)}, u32[]{:S(2)}, u32[]{:S(2)}) collective-permute-start(bf16[2,32,896]{2,1,0:T(8,128)(2,1)S(1)} %get-tuple-element.38), channel_id=1, source_target_pairs={{0,1},{1,0},{2,3},{3,2},{4,5},{5,4},{6,7},{7,6},{8,9},{9,8},{10,11... | collective-permute-start | bytes 344072 | tf_op jit(solution)/shard_map/ppermute | solution.py:350
  38.6 13.8 %copy-start = (bf16[2,768,2048]{2,1,0:T(8,128)(2,1)S(1)}, bf16[2,768,2048]{2,1,0:T(8,128)(2,1)}, u32[]{:S(2)}) copy-start(bf16[2,768,2048]{2,1,0:T(8,128)(2,1)} %refs_0_.3) | copy-start | bytes 18874372
  39.6 3.2 %collective-permute-start.8 = (bf16[2,2,192,896]{3,2,1,0:T(8,128)(2,1)S(1)}, bf16[2,2,192,896]{3,2,1,0:T(8,128)(2,1)S(1)}, u32[]{:S(2)}, u32[]{:S(2)}) collective-permute-start(bf16[2,2,192,896]{3,2,1,0:T(8,128)(2,1)S(1)} %get-tuple-element.40), channel_id=1, source_target_pairs={{0,8},{8,0},{16,24},{24,16},{1,9},{9,1},{17,25},{25,17},{2,10},{10... | collective-permute-start | bytes 4128776 | tf_op jit(solution)/shard_map/ppermute | solution.py:437
  39.6 11.2 %collective-permute-start.5 = (bf16[128,1152]{1,0:T(8,128)(2,1)S(1)}, bf16[128,1152]{1,0:T(8,128)(2,1)S(1)}, u32[]{:S(2)}, u32[]{:S(2)}) collective-permute-start(bf16[128,1152]{1,0:T(8,128)(2,1)S(1)} %collective-permute-done.refs_1_), channel_id=1, source_target_pairs={{0,2},{1,3},{2,4},{3,5},{4,6},{5,7},{6,0},{7,1},{8,10},{9,11},{10,... | collective-permute-start | bytes 884744 | tf_op jit(solution)/shard_map/ppermute | solution.py:339
  40.2 13.1 %collective-permute-start.9 = (bf16[2,96,1152]{2,1,0:T(8,128)(2,1)S(1)}, bf16[2,96,1152]{2,1,0:T(8,128)(2,1)S(1)}, u32[]{:S(2)}, u32[]{:S(2)}) collective-permute-start(bf16[2,96,1152]{2,1,0:T(8,128)(2,1)S(1)} %get-tuple-element.43), channel_id=1, source_target_pairs={{0,1},{1,0},{2,3},{3,2},{4,5},{5,4},{6,7},{7,6},{8,9},{9,8},{10,11... | collective-permute-start | bytes 1327112 | tf_op jit(solution)/shard_map/ppermute | solution.py:350
  42.9 13.6 %collective-permute-start.11 = (bf16[2,64,896]{2,1,0:T(8,128)(2,1)S(1)}, bf16[2,64,896]{2,1,0:T(8,128)(2,1)S(1)}, u32[]{:S(2)}, u32[]{:S(2)}) collective-permute-start(bf16[2,64,896]{2,1,0:T(8,128)(2,1)S(1)} %get-tuple-element.41.refs_2_), channel_id=1, source_target_pairs={{0,16},{8,24},{16,0},{24,8},{1,17},{9,25},{17,1},{25,9},{2,18},{10... | collective-permute-start | bytes 688136 | tf_op jit(solution)/shard_map/ppermute | solution.py:447
  44.5 12.0 %collective-permute-start.12 = (bf16[2,64,896]{2,1,0:T(8,128)(2,1)S(1)}, bf16[2,64,896]{2,1,0:T(8,128)(2,1)S(1)}, u32[]{:S(2)}, u32[]{:S(2)}) collective-permute-start(bf16[2,64,896]{2,1,0:T(8,128)(2,1)S(1)} %get-tuple-element.45), channel_id=1, source_target_pairs={{0,16},{8,24},{16,0},{24,8},{1,17},{9,25},{17,1},{25,9},{2,18},{10... | collective-permute-start | bytes 688136 | tf_op jit(solution)/shard_map/ppermute | solution.py:447
  51.1 5.5 %collective-permute-start.10 = (bf16[2,32,1152]{2,1,0:T(8,128)(2,1)S(1)}, bf16[2,32,1152]{2,1,0:T(8,128)(2,1)S(1)}, u32[]{:S(2)}, u32[]{:S(2)}) collective-permute-start(bf16[2,32,1152]{2,1,0:T(8,128)(2,1)S(1)} %get-tuple-element.44), channel_id=1, source_target_pairs={{0,1},{1,0},{2,3},{3,2},{4,5},{5,4},{6,7},{7,6},{8,9},{9,8},{10,11... | collective-permute-start | bytes 442376 | tf_op jit(solution)/shard_map/ppermute | solution.py:350
  57.3 3.9 %collective-permute-start.17 = (bf16[2,2,192,640]{3,2,1,0:T(8,128)(2,1)S(1)}, bf16[2,2,192,640]{3,2,1,0:T(8,128)(2,1)S(1)}, u32[]{:S(2)}, u32[]{:S(2)}) collective-permute-start(bf16[2,2,192,640]{3,2,1,0:T(8,128)(2,1)S(1)} %get-tuple-element.50), channel_id=1, source_target_pairs={{0,8},{8,0},{16,24},{24,16},{1,9},{9,1},{17,25},{25,17},{2,10},{10... | collective-permute-start | bytes 2949128 | tf_op jit(solution)/shard_map/ppermute | solution.py:437
  57.4 8.0 %collective-permute-start.19 = (bf16[2,64,896]{2,1,0:T(8,128)(2,1)S(1)}, bf16[2,64,896]{2,1,0:T(8,128)(2,1)S(1)}, u32[]{:S(2)}, u32[]{:S(2)}) collective-permute-start(bf16[2,64,896]{2,1,0:T(8,128)(2,1)S(1)} %get-tuple-element.51), channel_id=1, source_target_pairs={{0,16},{8,24},{16,0},{24,8},{1,17},{9,25},{17,1},{25,9},{2,18},{10... | collective-permute-start | bytes 688136 | tf_op jit(solution)/shard_map/ppermute | solution.py:447
  67.6 2.4 %collective-permute-start.20 = (bf16[2,2,192,512]{3,2,1,0:T(8,128)(2,1)S(1)}, bf16[2,2,192,512]{3,2,1,0:T(8,128)(2,1)S(1)}, u32[]{:S(2)}, u32[]{:S(2)}) collective-permute-start(bf16[2,2,192,512]{3,2,1,0:T(8,128)(2,1)S(1)} %get-tuple-element.55), channel_id=1, source_target_pairs={{0,8},{8,0},{16,24},{24,16},{1,9},{9,1},{17,25},{25,17},{2,10},{10... | collective-permute-start | bytes 2359304 | tf_op jit(solution)/shard_map/ppermute | solution.py:437
  67.7 14.1 %collective-permute-start.18 = (bf16[2,192,640]{2,1,0:T(8,128)(2,1)S(1)}, bf16[2,192,640]{2,1,0:T(8,128)(2,1)S(1)}, u32[]{:S(2)}, u32[]{:S(2)}) collective-permute-start(bf16[2,192,640]{2,1,0:T(8,128)(2,1)S(1)} %shard_map.88.refs_5_), channel_id=1, source_target_pairs={{0,16},{8,24},{16,0},{24,8},{1,17},{9,25},{17,1},{25,9},{2,18},{10... | collective-permute-start | bytes 1474568 | tf_op jit(solution)/shard_map/ppermute | solution.py:447
  70.1 19.7 %collective-permute-start.21 = (bf16[2,192,512]{2,1,0:T(8,128)(2,1)S(1)}, bf16[2,192,512]{2,1,0:T(8,128)(2,1)S(1)}, u32[]{:S(2)}, u32[]{:S(2)}) collective-permute-start(bf16[2,192,512]{2,1,0:T(8,128)(2,1)S(1)} %shard_map.91.refs_4_), channel_id=1, source_target_pairs={{0,16},{8,24},{16,0},{24,8},{1,17},{9,25},{17,1},{25,9},{2,18},{10... | collective-permute-start | bytes 1179656 | tf_op jit(solution)/shard_map/ppermute | solution.py:447
  71.7 3.6 %collective-permute-start.13 = (f32[2,256]{1,0:T(2,128)S(1)}, f32[2,256]{1,0:T(2,128)S(1)}, u32[]{:S(2)}, u32[]{:S(2)}) collective-permute-start(f32[2,256]{1,0:T(2,128)S(1)} %get-tuple-element.49.refs_2_), channel_id=1, source_target_pairs={{0,1},{1,0},{2,3},{3,2},{4,5},{5,4},{6,7},{7,6},{8,9},{9,8},{10,11... | collective-permute-start | bytes 6152 | tf_op jit(solution)/shard_map/ppermute | solution.py:488
  75.3 7.9 %collective-permute-start.14 = (f32[2,2,256]{2,1,0:T(2,128)S(1)}, f32[2,2,256]{2,1,0:T(2,128)S(1)}, u32[]{:S(2)}, u32[]{:S(2)}) collective-permute-start(f32[2,2,256]{2,1,0:T(2,128)S(1)} %pad_maximum_fusion.refs_2_), channel_id=1, source_target_pairs={{2,0},{3,1},{4,2},{5,3},{6,4},{7,5},{0,6},{1,7},{10,8},{11,9},{12,... | collective-permute-start | bytes 12296 | tf_op jit(solution)/shard_map/ppermute | solution.py:490
  77.6 5.5 %collective-permute-start.15 = (f32[2,2,256]{2,1,0:T(2,128)S(1)}, f32[2,2,256]{2,1,0:T(2,128)S(1)}, u32[]{:S(2)}, u32[]{:S(2)}) collective-permute-start(f32[2,2,256]{2,1,0:T(2,128)S(1)} %pad_maximum_fusion.refs_2_), channel_id=1, source_target_pairs={{4,0},{5,1},{6,2},{7,3},{0,4},{1,5},{2,6},{3,7},{12,8},{13,9},{14,... | collective-permute-start | bytes 12296 | tf_op jit(solution)/shard_map/ppermute | solution.py:490
  77.6 5.5 %collective-permute-start.16 = (f32[2,2,256]{2,1,0:T(2,128)S(1)}, f32[2,2,256]{2,1,0:T(2,128)S(1)}, u32[]{:S(2)}, u32[]{:S(2)}) collective-permute-start(f32[2,2,256]{2,1,0:T(2,128)S(1)} %pad_maximum_fusion.refs_2_), channel_id=1, source_target_pairs={{6,0},{7,1},{0,2},{1,3},{2,4},{3,5},{4,6},{5,7},{14,8},{15,9},{8,1... | collective-permute-start | bytes 12296 | tf_op jit(solution)/shard_map/ppermute | solution.py:490
  (5 other events, 34.0 us)

commit v15 on v14

--- a/solution.py
+++ b/solution.py
@@ -109,17 +109,17 @@
         place_ref[side * rows : (side + 1) * rows, :] = functools.reduce(jnp.add, hits).astype(BF16)
 
 
-def pick(held, capacity, block_refs, place_ref, out_refs):
+def pick(held, capacity, begin, block_refs, place_ref, out_refs):
     tokens = place_ref.shape[2]
     for j, ref in enumerate(block_refs):
-        scaled = jnp.dot(place_ref[j], ref[:tokens, :], preferred_element_type=F32).astype(BF16)
+        scaled = jnp.dot(place_ref[begin + j], ref[:tokens, :], preferred_element_type=F32).astype(BF16)
         for side, out_ref in enumerate(out_refs):
             for e in range(held):
                 at = (side * held + e) * capacity
                 out_ref[e, j * capacity : (j + 1) * capacity, :] = scaled[at : at + capacity]
 
 
-def pick_kernel(held, capacity, chosen, first, count, *refs):
+def pick_kernel(held, capacity, chosen, first, at, count, *refs):
     block_refs, refs = refs[:count], refs[count:]
     if first:
         mine_ref, other_ref, place_ref = refs
@@ -127,7 +127,7 @@
             places(held, capacity, chosen, ref, place_ref.at[j])
     else:
         place_ref, mine_ref, other_ref = refs
-    pick(held, capacity, block_refs, place_ref, (mine_ref, other_ref))
+    pick(held, capacity, at, block_refs, place_ref, (mine_ref, other_ref))
 
 
 def turn_kernel(dp, hidden_ref, *refs):
@@ -338,10 +338,10 @@
         pairs = [(i, moved(i, places, 0)) for i in range(LINE * SIDES)]
         return lax.ppermute(block, "expert", pairs)
 
-    def pick(self, c, name, blocks):
+    def pick(self, c, name, blocks, at=0):
         held, capacity, count = self.held, self.capacity, len(blocks)
         rows = [sds((held, count * capacity, self.widths[c]), BF16)] * SIDES
-        kernel = functools.partial(pick_kernel, held, capacity, self.chosen, c == 0, count)
+        kernel = functools.partial(pick_kernel, held, capacity, self.chosen, c == 0, at, count)
         if c == 0:
             place = sds((count, SIDES * held * capacity, self.tokens), BF16)
             mine, other, self.place[name] = self.call(kernel, [*rows, place], *blocks)
@@ -350,11 +350,14 @@
         return mine, lax.ppermute(other, "expert", [(i, i ^ 1) for i in range(LINE * SIDES)])
 
     def early(self, c):
-        return self.pick(c, "early", self.blocks[c])
+        if c == 0:
+            return [self.pick(c, "early", self.blocks[c])]
+        own = self.pick(c, "early", self.blocks[c][:1])
+        return [own, self.pick(c, "early", self.blocks[c][1:], 1)]
 
     def late(self, c, early):
-        late = self.pick(c, "late", [self.passed[c]])
-        return [early[0], late[0], early[1], late[1]]
+        picked = [*early, self.pick(c, "late", [self.passed[c]])]
+        return [mine for mine, _ in picked] + [other for _, other in picked]
 
 
 def exchanged(grad_out, ids, probs, groups, held, capacity, widths):
@@ -429,23 +432,26 @@
         )
         state["raw"] = made if final else made[0]
 
-    def reduced(c, at, width):
+    def termed(c, at, width):
         piece = sds((across, held, share, width), BF16)
-        after = summed[0][2][:2] if len(summed) == 1 else ()
+        after = summed[0][2][:2] if summed and at == 0 else ()
+        if direct and not c:
+            after = [early[0][1]]
         kernel = functools.partial(term_kernel, at)
         keep, give = call(kernel, [piece, piece], turned, *arrived[c], after=after)
         got = lax.ppermute(give, "dp", [(i, i ^ 1) for i in range(dp)])
-        if c == count - 1 and at == 0:
-            accumulated(c)
+        return keep, got, starts[c] + at
+
+    def paired(keep, got, start):
         cuts = cuts_of(share, not summed)
-        pieces = [sds((held, rows, width), BF16) for rows in cuts]
+        pieces = [sds((held, rows, keep.shape[3]), BF16) for rows in cuts]
         pairs = call(functools.partial(pair_kernel, cuts), pieces * (across - 1), keep, got)
         others = []
         for i, pair in enumerate(pairs):
             step = 1 + i // len(cuts)
             shift = [(2 * r + k, 2 * ((r + step) % across) + k) for r in range(across) for k in range(2)]
             others.append(lax.ppermute(pair, "dp", shift))
-        summed.append((keep, got, others, starts[c] + at))
+        summed.append((keep, got, others, start))
 
     def finished(first, last):
         before = [] if state["grad"] is None else [state["grad"]]
@@ -475,12 +481,13 @@
                 early = relay.early(c + 1)
         if c >= 1:
             accumulated(c - 1)
-        at = 0
-        for width in chunk:
-            reduced(c, at, width)
-            at += width
-            if len(summed) > 1:
-                finished(len(summed) - 2, len(summed) - 1)
+        terms = [termed(c, sum(chunk[:i]), width) for i, width in enumerate(chunk)]
+        if c == count - 1:
+            accumulated(c)
+        for term in terms:
+            paired(*term)
+    for j in range(1, len(summed)):
+        finished(j, j + 1)
     hidden_grad, sums = state["raw"]
 
     if direct:
@@ -501,9 +508,8 @@
         flat,
         probs,
         *returned,
-        keep=False,
     ).T
-    finished(len(summed) - 1, len(summed))
+    finished(0, 1)
     weight_grad = state["grad"]
     return (hidden_grad.reshape(hidden.shape), prob_grad, weight_grad)
 

time: 91.7 us -> 90.5 us (0.987)
  starting transfers between devices: 27 us -> 25.3 us
    ppermute x3, starting transfers between devices: 3.79 us -> 1.68 us  [body(): lax.ppermute(both, 'expert', [(moved(i, d, 0), i) for i in range(groups)])]
    ppermute x6, waiting for transfers between devices: 26.4 us -> 25.3 us  [along(): return lax.ppermute(block, 'expert', pairs)]
    ppermute x4 -> x5, starting transfers between devices: 5.37 us -> 6.3 us  [pick(): lax.ppermute(other, 'expert', [(i, i ^ 1) for i in range(LINE * SIDES)])]
    unnamed x14 -> x16, local copies, waits for them, and re-layouts: 2.11 us -> 2.79 us
    pallas_call x19 -> x20, Pallas kernels: 15 us -> 15.2 us  [__call__(): pl.pallas_call(body, out_shape=outs, in_specs=in_specs, compiler_params=p...]
    ppermute x4 -> x5, waiting for transfers between devices: 3.19 us -> 3.19 us  [pick(): lax.ppermute(other, 'expert', [(i, i ^ 1) for i in range(LINE * SIDES)])]
  transfers between devices with their start and end apart: 22 -> 23, of which waited for: 12 -> 11; matrix products, arithmetic and copies ran while one was open for 0% -> 0% of each run, Pallas kernels for 8% -> 10%
where the time goes in v15:
time: 90.5 us; the launch traced here: 90.3 us
  waiting for transfers between devices  46.2 us (51%)
  starting transfers between devices  25.3 us (28%)
  Pallas kernels  15.2 us (17%)
  local copies, waits for them, and re-layouts  2.79 us (3%)
    ppermute x6, waiting for transfers between devices, along(): return lax.ppermute(block, 'expert', pairs)  25.3 us
    pallas_call x20, Pallas kernels, __call__(): pl.pallas_call(body, out_shape=outs, in_specs=in_specs, compiler_params=p...  15.2 us
    ppermute x5, waiting for transfers between devices, paired(): others.append(lax.ppermute(pair, 'dp', shift))  13.9 us
    ppermute x6, starting transfers between devices, along(): return lax.ppermute(block, 'expert', pairs)  9.65 us
    ppermute x5, starting transfers between devices, pick(): lax.ppermute(other, 'expert', [(i, i ^ 1) for i in range(LINE * SIDES)])  6.3 us
    ppermute x5, starting transfers between devices, paired(): others.append(lax.ppermute(pair, 'dp', shift))  5.77 us
    ppermute x5, waiting for transfers between devices, pick(): lax.ppermute(other, 'expert', [(i, i ^ 1) for i in range(LINE * SIDES)])  3.19 us
    unnamed x16, local copies, waits for them, and re-layouts  2.79 us
  transfers between devices with their start and end apart: 23, of which 11 were waited for; matrix products, arithmetic and copies ran while one was open for 0% of the time, Pallas kernels for 10%

profile of v15, /device:TPU:0, one launch (start us, length us, event | category | flops | bytes accessed | tf_op | source)
XLA Modules:
  0.0 90.3 jit_solution(16157079374896619644)
XLA Ops:
  0.6 1.9 %shard_map.77 = (s32[2,128]{1,0:T(2,128)}, bf16[144,896]{1,0:T(8,128)(2,1)}) custom-call(s32[2,128]{1,0:T(2,128)} %bitcast.14, f32[2,128]{1,0:T(2,128)} %bitcast.10, bf16[128,2048]{1,0:T(8,128)(2,1)} %rows_ref.3), custom_call_target="tpu_custom_call" | custom-call | flops 1 | bytes 1 | tf_op jit(solution)/shard_map/pallas_call | solution.py:43
  2.5 3.1 %collective-permute-start = (bf16[144,896]{1,0:T(8,128)(2,1)}, bf16[144,896]{1,0:T(8,128)(2,1)S(1)}, u32[]{:S(2)}, u32[]{:S(2)}) collective-permute-start(bf16[144,896]{1,0:T(8,128)(2,1)} %get-tuple-element.33.refs_0_), channel_id=1, source_target_pairs={{0,2},{1,3},{2,4},{3,5},{4,6},{5,7},{6,0},{7,1},{8,10},{9,11},{10,... | collective-permute-start | bytes 774152 | tf_op jit(solution)/shard_map/ppermute | solution.py:339
  5.6 2.1 %collective-permute-start.1 = (bf16[144,896]{1,0:T(8,128)(2,1)}, bf16[144,896]{1,0:T(8,128)(2,1)S(1)}, u32[]{:S(2)}, u32[]{:S(2)}) collective-permute-start(bf16[144,896]{1,0:T(8,128)(2,1)} %get-tuple-element.33.refs_0_), channel_id=1, source_target_pairs={{0,6},{1,7},{2,0},{3,1},{4,2},{5,3},{6,4},{7,5},{8,14},{9,15},{10,... | collective-permute-start | bytes 774152 | tf_op jit(solution)/shard_map/ppermute | solution.py:339
  7.7 7.2 %collective-permute-done.refs_1_ = bf16[144,896]{1,0:T(8,128)(2,1)S(1)} collective-permute-done((bf16[144,896]{1,0:T(8,128)(2,1)}, bf16[144,896]{1,0:T(8,128)(2,1)S(1)}, u32[]{:S(2)}, u32[]{:S(2)}) %collective-permute-start) | collective-permute-done | bytes 258080 | tf_op jit(solution)/shard_map/ppermute | solution.py:339
  16.3 2.9 %collective-permute-done.1.refs_2_ = bf16[144,896]{1,0:T(8,128)(2,1)S(1)} collective-permute-done((bf16[144,896]{1,0:T(8,128)(2,1)}, bf16[144,896]{1,0:T(8,128)(2,1)S(1)}, u32[]{:S(2)}, u32[]{:S(2)}) %collective-permute-start.1) | collective-permute-done | bytes 258080 | tf_op jit(solution)/shard_map/ppermute | solution.py:339
  20.6 1.8 %collective-permute-start.6 = (bf16[2,96,896]{2,1,0:T(8,128)(2,1)S(1)}, bf16[2,96,896]{2,1,0:T(8,128)(2,1)S(1)}, u32[]{:S(2)}, u32[]{:S(2)}) collective-permute-start(bf16[2,96,896]{2,1,0:T(8,128)(2,1)S(1)} %get-tuple-element.40), channel_id=1, source_target_pairs={{0,1},{1,0},{2,3},{3,2},{4,5},{5,4},{6,7},{7,6},{8,9},{9,8},{10,11... | collective-permute-start | bytes 1032200 | tf_op jit(solution)/shard_map/ppermute | solution.py:350
  22.4 1.8 %collective-permute-start.3 = (bf16[128,1152]{1,0:T(8,128)(2,1)S(1)}, bf16[128,1152]{1,0:T(8,128)(2,1)S(1)}, u32[]{:S(2)}, u32[]{:S(2)}) collective-permute-start(bf16[128,1152]{1,0:T(8,128)(2,1)S(1)} %shard_map.76.refs_0_), channel_id=1, source_target_pairs={{0,2},{1,3},{2,4},{3,5},{4,6},{5,7},{6,0},{7,1},{8,10},{9,11},{10,... | collective-permute-start | bytes 884744 | tf_op jit(solution)/shard_map/ppermute | solution.py:339
  24.2 2.1 %collective-permute-start.4 = (bf16[128,1152]{1,0:T(8,128)(2,1)S(1)}, bf16[128,1152]{1,0:T(8,128)(2,1)S(1)}, u32[]{:S(2)}, u32[]{:S(2)}) collective-permute-start(bf16[128,1152]{1,0:T(8,128)(2,1)S(1)} %shard_map.76.refs_0_), channel_id=1, source_target_pairs={{0,6},{1,7},{2,0},{3,1},{4,2},{5,3},{6,4},{7,5},{8,14},{9,15},{10,... | collective-permute-start | bytes 884744 | tf_op jit(solution)/shard_map/ppermute | solution.py:339
  28.8 5.4 %collective-permute-done.3.refs_0_ = bf16[128,1152]{1,0:T(8,128)(2,1)S(1)} collective-permute-done((bf16[128,1152]{1,0:T(8,128)(2,1)S(1)}, bf16[128,1152]{1,0:T(8,128)(2,1)S(1)}, u32[]{:S(2)}, u32[]{:S(2)}) %collective-permute-start.3) | collective-permute-done | bytes 294944 | tf_op jit(solution)/shard_map/ppermute | solution.py:339
  34.2 4.0 %collective-permute-done.4.refs_1_ = bf16[128,1152]{1,0:T(8,128)(2,1)S(1)} collective-permute-done((bf16[128,1152]{1,0:T(8,128)(2,1)S(1)}, bf16[128,1152]{1,0:T(8,128)(2,1)S(1)}, u32[]{:S(2)}, u32[]{:S(2)}) %collective-permute-start.4) | collective-permute-done | bytes 294944 | tf_op jit(solution)/shard_map/ppermute | solution.py:339
  41.3 1.3 %collective-permute-done.9.refs_1_ = bf16[2,2,192,896]{3,2,1,0:T(8,128)(2,1)S(1)} collective-permute-done((bf16[2,2,192,896]{3,2,1,0:T(8,128)(2,1)S(1)}, bf16[2,2,192,896]{3,2,1,0:T(8,128)(2,1)S(1)}, u32[]{:S(2)}, u32[]{:S(2)}) %collective-permute-start.9) | collective-permute-done | bytes 1376288 | tf_op jit(solution)/shard_map/ppermute | solution.py:442
  42.9 1.6 %collective-permute-start.12 = (bf16[2,64,896]{2,1,0:T(8,128)(2,1)S(1)}, bf16[2,64,896]{2,1,0:T(8,128)(2,1)S(1)}, u32[]{:S(2)}, u32[]{:S(2)}) collective-permute-start(bf16[2,64,896]{2,1,0:T(8,128)(2,1)S(1)} %get-tuple-element.45.refs_2_), channel_id=1, source_target_pairs={{0,16},{8,24},{16,0},{24,8},{1,17},{9,25},{17,1},{25,9},{2,18},{10... | collective-permute-start | bytes 688136 | tf_op jit(solution)/shard_map/ppermute | solution.py:453
  45.0 5.8 %collective-permute-done.5.refs_0_ = bf16[128,1152]{1,0:T(8,128)(2,1)S(1)} collective-permute-done((bf16[128,1152]{1,0:T(8,128)(2,1)S(1)}, bf16[128,1152]{1,0:T(8,128)(2,1)S(1)}, u32[]{:S(2)}, u32[]{:S(2)}) %collective-permute-start.5) | collective-permute-done | bytes 294944 | tf_op jit(solution)/shard_map/ppermute | solution.py:339
  53.3 3.2 %collective-permute-done.11.refs_6_ = bf16[2,32,1152]{2,1,0:T(8,128)(2,1)S(1)} collective-permute-done((bf16[2,32,1152]{2,1,0:T(8,128)(2,1)S(1)}, bf16[2,32,1152]{2,1,0:T(8,128)(2,1)S(1)}, u32[]{:S(2)}, u32[]{:S(2)}) %collective-permute-start.11) | collective-permute-done | bytes 147488 | tf_op jit(solution)/shard_map/ppermute | solution.py:350
  58.5 2.2 %shard_map.89 = (bf16[8,2,32,768]{3,2,1,0:T(8,128)(2,1)}, f32[2,256]{1,0:T(2,128)S(1)}) custom-call(bf16[2,768,2048]{2,1,0:T(8,128)(2,1)S(1)} %copy-done, bf16[2,32,1152]{2,1,0:T(8,128)(2,1)S(1)} %get-tuple-element.36.refs_3_.refs_1_, bf16[2,64,1152]{2,1,0:T(8,128)(2,1)S(1)} %get-tuple-element.37.refs_5_.refs_2_, ...), custom_call_target="tpu_custom_call" | custom-call | flops 1 | bytes 1 | tf_op jit(solution)/shard_map/pallas_call | solution.py:43
  60.9 1.6 %collective-permute-start.21 = (bf16[2,192,640]{2,1,0:T(8,128)(2,1)S(1)}, bf16[2,192,640]{2,1,0:T(8,128)(2,1)S(1)}, u32[]{:S(2)}, u32[]{:S(2)}) collective-permute-start(bf16[2,192,640]{2,1,0:T(8,128)(2,1)S(1)} %shard_map.90.refs_2_), channel_id=1, source_target_pairs={{0,16},{8,24},{16,0},{24,8},{1,17},{9,25},{17,1},{25,9},{2,18},{10... | collective-permute-start | bytes 1474568 | tf_op jit(solution)/shard_map/ppermute | solution.py:453
  63.1 1.5 %collective-permute-start.22 = (bf16[2,64,896]{2,1,0:T(8,128)(2,1)S(1)}, bf16[2,64,896]{2,1,0:T(8,128)(2,1)S(1)}, u32[]{:S(2)}, u32[]{:S(2)}) collective-permute-start(bf16[2,64,896]{2,1,0:T(8,128)(2,1)S(1)} %get-tuple-element.60), channel_id=1, source_target_pairs={{0,16},{8,24},{16,0},{24,8},{1,17},{9,25},{17,1},{25,9},{2,18},{10... | collective-permute-start | bytes 688136 | tf_op jit(solution)/shard_map/ppermute | solution.py:453
  65.8 2.4 %collective-permute-done.14 = f32[2,256]{1,0:T(2,128)S(1)} collective-permute-done((f32[2,256]{1,0:T(2,128)S(1)}, f32[2,256]{1,0:T(2,128)S(1)}, u32[]{:S(2)}, u32[]{:S(2)}) %collective-permute-start.14) | collective-permute-done | bytes 2080 | tf_op jit(solution)/shard_map/ppermute | solution.py:495
  68.2 1.7 %collective-permute-start.15 = (f32[2,2,256]{2,1,0:T(2,128)S(1)}, f32[2,2,256]{2,1,0:T(2,128)S(1)}, u32[]{:S(2)}, u32[]{:S(2)}) collective-permute-start(f32[2,2,256]{2,1,0:T(2,128)S(1)} %pad_maximum_fusion.refs_2_), channel_id=1, source_target_pairs={{2,0},{3,1},{4,2},{5,3},{6,4},{7,5},{0,6},{1,7},{10,8},{11,9},{12,... | collective-permute-start | bytes 12296 | tf_op jit(solution)/shard_map/ppermute | solution.py:497
  69.9 5.1 %collective-permute-done.21.refs_2_ = bf16[2,192,640]{2,1,0:T(8,128)(2,1)S(1)} collective-permute-done((bf16[2,192,640]{2,1,0:T(8,128)(2,1)S(1)}, bf16[2,192,640]{2,1,0:T(8,128)(2,1)S(1)}, u32[]{:S(2)}, u32[]{:S(2)}) %collective-permute-start.21) | collective-permute-done | bytes 491552 | tf_op jit(solution)/shard_map/ppermute | solution.py:453
  75.0 1.4 %shard_map.92 = (f32[192,2,2048]{2,1,0:T(2,128)}, f32[8,128]{1,0:T(8,128)S(1)}) custom-call(bf16[2,2,192,640]{3,2,1,0:T(8,128)(2,1)S(1)} %get-tuple-element.50.refs_7_.refs_0_, bf16[2,2,192,640]{3,2,1,0:T(8,128)(2,1)S(1)} %collective-permute-done.19.refs_1_, bf16[2,192,640]{2,1,0:T(8,128)(2,1)S(1)} %collective-permute-done.21.refs_2_, ...), custom_call_target="tpu_custom_call" | custom-call | flops 1 | bytes 1 | tf_op jit(solution)/shard_map/pallas_call | solution.py:43
  76.4 7.0 %collective-permute-done.20.refs_2_ = bf16[2,192,512]{2,1,0:T(8,128)(2,1)S(1)} collective-permute-done((bf16[2,192,512]{2,1,0:T(8,128)(2,1)S(1)}, bf16[2,192,512]{2,1,0:T(8,128)(2,1)S(1)}, u32[]{:S(2)}, u32[]{:S(2)}) %collective-permute-start.20) | collective-permute-done | bytes 393248 | tf_op jit(solution)/shard_map/ppermute | solution.py:453
  85.6 1.8 %collective-permute-done.22.refs_4_ = bf16[2,64,896]{2,1,0:T(8,128)(2,1)S(1)} collective-permute-done((bf16[2,64,896]{2,1,0:T(8,128)(2,1)S(1)}, bf16[2,64,896]{2,1,0:T(8,128)(2,1)S(1)}, u32[]{:S(2)}, u32[]{:S(2)}) %collective-permute-start.22) | collective-permute-done | bytes 229408 | tf_op jit(solution)/shard_map/ppermute | solution.py:453
  88.1 2.2 %shard_map.95 = (f32[192,2,2048]{2,1,0:T(2,128)}, f32[8,128]{1,0:T(8,128)}) custom-call(bf16[2,2,192,896]{3,2,1,0:T(8,128)(2,1)S(1)} %get-tuple-element.43.refs_0_.refs_2_, bf16[2,2,192,896]{3,2,1,0:T(8,128)(2,1)S(1)} %collective-permute-done.9.refs_1_, ...), custom_call_target="tpu_custom_call", output_to_operand_aliasing={{0}: (5, {})} | custom-call | flops 1 | bytes 1 | tf_op jit(solution)/shard_map/pallas_call | solution.py:43
  (59 shorter events, 18.4 us)
Async XLA Ops:
  0.6 21.7 %copy-start.3 = (bf16[128,2048]{1,0:T(8,128)(2,1)S(1)}, bf16[128,2048]{1,0:T(8,128)(2,1)}, u32[]{:S(2)}) copy-start(bf16[128,2048]{1,0:T(8,128)(2,1)} %rows_ref.3) | copy-start | bytes 1572868
  2.5 12.4 %collective-permute-start = (bf16[144,896]{1,0:T(8,128)(2,1)}, bf16[144,896]{1,0:T(8,128)(2,1)S(1)}, u32[]{:S(2)}, u32[]{:S(2)}) collective-permute-start(bf16[144,896]{1,0:T(8,128)(2,1)} %get-tuple-element.33.refs_0_), channel_id=1, source_target_pairs={{0,2},{1,3},{2,4},{3,5},{4,6},{5,7},{6,0},{7,1},{8,10},{9,11},{10,... | collective-permute-start | bytes 774152 | tf_op jit(solution)/shard_map/ppermute | solution.py:339
  5.6 13.6 %collective-permute-start.1 = (bf16[144,896]{1,0:T(8,128)(2,1)}, bf16[144,896]{1,0:T(8,128)(2,1)S(1)}, u32[]{:S(2)}, u32[]{:S(2)}) collective-permute-start(bf16[144,896]{1,0:T(8,128)(2,1)} %get-tuple-element.33.refs_0_), channel_id=1, source_target_pairs={{0,6},{1,7},{2,0},{3,1},{4,2},{5,3},{6,4},{7,5},{8,14},{9,15},{10,... | collective-permute-start | bytes 774152 | tf_op jit(solution)/shard_map/ppermute | solution.py:339
  14.9 11.3 %collective-permute-start.2 = (bf16[144,896]{1,0:T(8,128)(2,1)S(1)}, bf16[144,896]{1,0:T(8,128)(2,1)S(1)}, u32[]{:S(2)}, u32[]{:S(2)}) collective-permute-start(bf16[144,896]{1,0:T(8,128)(2,1)S(1)} %collective-permute-done.refs_1_), channel_id=1, source_target_pairs={{0,2},{1,3},{2,4},{3,5},{4,6},{5,7},{6,0},{7,1},{8,10},{9,11},{10,... | collective-permute-start | bytes 774152 | tf_op jit(solution)/shard_map/ppermute | solution.py:339
  20.6 17.9 %collective-permute-start.6 = (bf16[2,96,896]{2,1,0:T(8,128)(2,1)S(1)}, bf16[2,96,896]{2,1,0:T(8,128)(2,1)S(1)}, u32[]{:S(2)}, u32[]{:S(2)}) collective-permute-start(bf16[2,96,896]{2,1,0:T(8,128)(2,1)S(1)} %get-tuple-element.40), channel_id=1, source_target_pairs={{0,1},{1,0},{2,3},{3,2},{4,5},{5,4},{6,7},{7,6},{8,9},{9,8},{10,11... | collective-permute-start | bytes 1032200 | tf_op jit(solution)/shard_map/ppermute | solution.py:350
  22.4 11.8 %collective-permute-start.3 = (bf16[128,1152]{1,0:T(8,128)(2,1)S(1)}, bf16[128,1152]{1,0:T(8,128)(2,1)S(1)}, u32[]{:S(2)}, u32[]{:S(2)}) collective-permute-start(bf16[128,1152]{1,0:T(8,128)(2,1)S(1)} %shard_map.76.refs_0_), channel_id=1, source_target_pairs={{0,2},{1,3},{2,4},{3,5},{4,6},{5,7},{6,0},{7,1},{8,10},{9,11},{10,... | collective-permute-start | bytes 884744 | tf_op jit(solution)/shard_map/ppermute | solution.py:339
  24.2 14.0 %collective-permute-start.4 = (bf16[128,1152]{1,0:T(8,128)(2,1)S(1)}, bf16[128,1152]{1,0:T(8,128)(2,1)S(1)}, u32[]{:S(2)}, u32[]{:S(2)}) collective-permute-start(bf16[128,1152]{1,0:T(8,128)(2,1)S(1)} %shard_map.76.refs_0_), channel_id=1, source_target_pairs={{0,6},{1,7},{2,0},{3,1},{4,2},{5,3},{6,4},{7,5},{8,14},{9,15},{10,... | collective-permute-start | bytes 884744 | tf_op jit(solution)/shard_map/ppermute | solution.py:339
  26.7 11.7 %collective-permute-start.8 = (bf16[2,32,1152]{2,1,0:T(8,128)(2,1)S(1)}, bf16[2,32,1152]{2,1,0:T(8,128)(2,1)S(1)}, u32[]{:S(2)}, u32[]{:S(2)}) collective-permute-start(bf16[2,32,1152]{2,1,0:T(8,128)(2,1)S(1)} %get-tuple-element.42), channel_id=1, source_target_pairs={{0,1},{1,0},{2,3},{3,2},{4,5},{5,4},{6,7},{7,6},{8,9},{9,8},{10,11... | collective-permute-start | bytes 442376 | tf_op jit(solution)/shard_map/ppermute | solution.py:350
  27.9 10.6 %collective-permute-start.7 = (bf16[2,32,896]{2,1,0:T(8,128)(2,1)S(1)}, bf16[2,32,896]{2,1,0:T(8,128)(2,1)S(1)}, u32[]{:S(2)}, u32[]{:S(2)}) collective-permute-start(bf16[2,32,896]{2,1,0:T(8,128)(2,1)S(1)} %get-tuple-element.41), channel_id=1, source_target_pairs={{0,1},{1,0},{2,3},{3,2},{4,5},{5,4},{6,7},{7,6},{8,9},{9,8},{10,11... | collective-permute-start | bytes 344072 | tf_op jit(solution)/shard_map/ppermute | solution.py:350
  39.5 3.2 %collective-permute-start.9 = (bf16[2,2,192,896]{3,2,1,0:T(8,128)(2,1)S(1)}, bf16[2,2,192,896]{3,2,1,0:T(8,128)(2,1)S(1)}, u32[]{:S(2)}, u32[]{:S(2)}) collective-permute-start(bf16[2,2,192,896]{3,2,1,0:T(8,128)(2,1)S(1)} %get-tuple-element.44), channel_id=1, source_target_pairs={{0,8},{8,0},{16,24},{24,16},{1,9},{9,1},{17,25},{25,17},{2,10},{10... | collective-permute-start | bytes 4128776 | tf_op jit(solution)/shard_map/ppermute | solution.py:442
  39.6 11.2 %collective-permute-start.5 = (bf16[128,1152]{1,0:T(8,128)(2,1)S(1)}, bf16[128,1152]{1,0:T(8,128)(2,1)S(1)}, u32[]{:S(2)}, u32[]{:S(2)}) collective-permute-start(bf16[128,1152]{1,0:T(8,128)(2,1)S(1)} %collective-permute-done.3.refs_0_), channel_id=1, source_target_pairs={{0,2},{1,3},{2,4},{3,5},{4,6},{5,7},{6,0},{7,1},{8,10},{9,11},{10,... | collective-permute-start | bytes 884744 | tf_op jit(solution)/shard_map/ppermute | solution.py:339
  40.2 13.1 %collective-permute-start.10 = (bf16[2,64,1152]{2,1,0:T(8,128)(2,1)S(1)}, bf16[2,64,1152]{2,1,0:T(8,128)(2,1)S(1)}, u32[]{:S(2)}, u32[]{:S(2)}) collective-permute-start(bf16[2,64,1152]{2,1,0:T(8,128)(2,1)S(1)} %get-tuple-element.47), channel_id=1, source_target_pairs={{0,1},{1,0},{2,3},{3,2},{4,5},{5,4},{6,7},{7,6},{8,9},{9,8},{10,11... | collective-permute-start | bytes 884744 | tf_op jit(solution)/shard_map/ppermute | solution.py:350
  42.9 13.6 %collective-permute-start.12 = (bf16[2,64,896]{2,1,0:T(8,128)(2,1)S(1)}, bf16[2,64,896]{2,1,0:T(8,128)(2,1)S(1)}, u32[]{:S(2)}, u32[]{:S(2)}) collective-permute-start(bf16[2,64,896]{2,1,0:T(8,128)(2,1)S(1)} %get-tuple-element.45.refs_2_), channel_id=1, source_target_pairs={{0,16},{8,24},{16,0},{24,8},{1,17},{9,25},{17,1},{25,9},{2,18},{10... | collective-permute-start | bytes 688136 | tf_op jit(solution)/shard_map/ppermute | solution.py:453
  44.5 12.0 %collective-permute-start.13 = (bf16[2,64,896]{2,1,0:T(8,128)(2,1)S(1)}, bf16[2,64,896]{2,1,0:T(8,128)(2,1)S(1)}, u32[]{:S(2)}, u32[]{:S(2)}) collective-permute-start(bf16[2,64,896]{2,1,0:T(8,128)(2,1)S(1)} %get-tuple-element.49), channel_id=1, source_target_pairs={{0,16},{8,24},{16,0},{24,8},{1,17},{9,25},{17,1},{25,9},{2,18},{10... | collective-permute-start | bytes 688136 | tf_op jit(solution)/shard_map/ppermute | solution.py:453
  51.0 5.5 %collective-permute-start.11 = (bf16[2,32,1152]{2,1,0:T(8,128)(2,1)S(1)}, bf16[2,32,1152]{2,1,0:T(8,128)(2,1)S(1)}, u32[]{:S(2)}, u32[]{:S(2)}) collective-permute-start(bf16[2,32,1152]{2,1,0:T(8,128)(2,1)S(1)} %get-tuple-element.48), channel_id=1, source_target_pairs={{0,1},{1,0},{2,3},{3,2},{4,5},{5,4},{6,7},{7,6},{8,9},{9,8},{10,11... | collective-permute-start | bytes 442376 | tf_op jit(solution)/shard_map/ppermute | solution.py:350
  57.3 3.5 %collective-permute-start.19 = (bf16[2,2,192,640]{3,2,1,0:T(8,128)(2,1)S(1)}, bf16[2,2,192,640]{3,2,1,0:T(8,128)(2,1)S(1)}, u32[]{:S(2)}, u32[]{:S(2)}) collective-permute-start(bf16[2,2,192,640]{3,2,1,0:T(8,128)(2,1)S(1)} %get-tuple-element.56), channel_id=1, source_target_pairs={{0,8},{8,0},{16,24},{24,16},{1,9},{9,1},{17,25},{25,17},{2,10},{10... | collective-permute-start | bytes 2949128 | tf_op jit(solution)/shard_map/ppermute | solution.py:442
  57.9 4.5 %collective-permute-start.18 = (bf16[2,2,192,512]{3,2,1,0:T(8,128)(2,1)S(1)}, bf16[2,2,192,512]{3,2,1,0:T(8,128)(2,1)S(1)}, u32[]{:S(2)}, u32[]{:S(2)}) collective-permute-start(bf16[2,2,192,512]{3,2,1,0:T(8,128)(2,1)S(1)} %get-tuple-element.55), channel_id=1, source_target_pairs={{0,8},{8,0},{16,24},{24,16},{1,9},{9,1},{17,25},{25,17},{2,10},{10... | collective-permute-start | bytes 2359304 | tf_op jit(solution)/shard_map/ppermute | solution.py:442
  60.9 14.1 %collective-permute-start.21 = (bf16[2,192,640]{2,1,0:T(8,128)(2,1)S(1)}, bf16[2,192,640]{2,1,0:T(8,128)(2,1)S(1)}, u32[]{:S(2)}, u32[]{:S(2)}) collective-permute-start(bf16[2,192,640]{2,1,0:T(8,128)(2,1)S(1)} %shard_map.90.refs_2_), channel_id=1, source_target_pairs={{0,16},{8,24},{16,0},{24,8},{1,17},{9,25},{17,1},{25,9},{2,18},{10... | collective-permute-start | bytes 1474568 | tf_op jit(solution)/shard_map/ppermute | solution.py:453
  62.5 20.9 %collective-permute-start.20 = (bf16[2,192,512]{2,1,0:T(8,128)(2,1)S(1)}, bf16[2,192,512]{2,1,0:T(8,128)(2,1)S(1)}, u32[]{:S(2)}, u32[]{:S(2)}) collective-permute-start(bf16[2,192,512]{2,1,0:T(8,128)(2,1)S(1)} %shard_map.91.refs_3_), channel_id=1, source_target_pairs={{0,16},{8,24},{16,0},{24,8},{1,17},{9,25},{17,1},{25,9},{2,18},{10... | collective-permute-start | bytes 1179656 | tf_op jit(solution)/shard_map/ppermute | solution.py:453
  63.1 24.3 %collective-permute-start.22 = (bf16[2,64,896]{2,1,0:T(8,128)(2,1)S(1)}, bf16[2,64,896]{2,1,0:T(8,128)(2,1)S(1)}, u32[]{:S(2)}, u32[]{:S(2)}) collective-permute-start(bf16[2,64,896]{2,1,0:T(8,128)(2,1)S(1)} %get-tuple-element.60), channel_id=1, source_target_pairs={{0,16},{8,24},{16,0},{24,8},{1,17},{9,25},{17,1},{25,9},{2,18},{10... | collective-permute-start | bytes 688136 | tf_op jit(solution)/shard_map/ppermute | solution.py:453
  64.6 3.6 %collective-permute-start.14 = (f32[2,256]{1,0:T(2,128)S(1)}, f32[2,256]{1,0:T(2,128)S(1)}, u32[]{:S(2)}, u32[]{:S(2)}) collective-permute-start(f32[2,256]{1,0:T(2,128)S(1)} %get-tuple-element.54.refs_2_), channel_id=1, source_target_pairs={{0,1},{1,0},{2,3},{3,2},{4,5},{5,4},{6,7},{7,6},{8,9},{9,8},{10,11... | collective-permute-start | bytes 6152 | tf_op jit(solution)/shard_map/ppermute | solution.py:495
  68.2 16.4 %collective-permute-start.15 = (f32[2,2,256]{2,1,0:T(2,128)S(1)}, f32[2,2,256]{2,1,0:T(2,128)S(1)}, u32[]{:S(2)}, u32[]{:S(2)}) collective-permute-start(f32[2,2,256]{2,1,0:T(2,128)S(1)} %pad_maximum_fusion.refs_2_), channel_id=1, source_target_pairs={{2,0},{3,1},{4,2},{5,3},{6,4},{7,5},{0,6},{1,7},{10,8},{11,9},{12,... | collective-permute-start | bytes 12296 | tf_op jit(solution)/shard_map/ppermute | solution.py:497
  69.9 14.7 %collective-permute-start.16 = (f32[2,2,256]{2,1,0:T(2,128)S(1)}, f32[2,2,256]{2,1,0:T(2,128)S(1)}, u32[]{:S(2)}, u32[]{:S(2)}) collective-permute-start(f32[2,2,256]{2,1,0:T(2,128)S(1)} %pad_maximum_fusion.refs_2_), channel_id=1, source_target_pairs={{4,0},{5,1},{6,2},{7,3},{0,4},{1,5},{2,6},{3,7},{12,8},{13,9},{14,... | collective-permute-start | bytes 12296 | tf_op jit(solution)/shard_map/ppermute | solution.py:497
  75.0 9.6 %collective-permute-start.17 = (f32[2,2,256]{2,1,0:T(2,128)S(1)}, f32[2,2,256]{2,1,0:T(2,128)S(1)}, u32[]{:S(2)}, u32[]{:S(2)}) collective-permute-start(f32[2,2,256]{2,1,0:T(2,128)S(1)} %pad_maximum_fusion.refs_2_), channel_id=1, source_target_pairs={{6,0},{7,1},{0,2},{1,3},{2,4},{3,5},{4,6},{5,7},{14,8},{15,9},{8,1... | collective-permute-start | bytes 12296 | tf_op jit(solution)/shard_map/ppermute | solution.py:497
  (7 other events, 38.2 us)

commit v16 on v15

--- a/solution.py
+++ b/solution.py
@@ -434,7 +434,7 @@
 
     def termed(c, at, width):
         piece = sds((across, held, share, width), BF16)
-        after = summed[0][2][:2] if summed and at == 0 else ()
+        after = summed[0][2] if summed and at == 0 and direct else ()
         if direct and not c:
             after = [early[0][1]]
         kernel = functools.partial(term_kernel, at)
@@ -482,11 +482,10 @@
         if c >= 1:
             accumulated(c - 1)
         terms = [termed(c, sum(chunk[:i]), width) for i, width in enumerate(chunk)]
-        if c == count - 1:
-            accumulated(c)
         for term in terms:
             paired(*term)
-    for j in range(1, len(summed)):
+    accumulated(count - 1)
+    for j in range(len(summed) - 1):
         finished(j, j + 1)
     hidden_grad, sums = state["raw"]
 
@@ -509,7 +508,7 @@
         probs,
         *returned,
     ).T
-    finished(0, 1)
+    finished(len(summed) - 1, len(summed))
     weight_grad = state["grad"]
     return (hidden_grad.reshape(hidden.shape), prob_grad, weight_grad)
 

time: 90.5 us -> 88.1 us (0.973)
  waiting for transfers between devices: 46.2 us -> 39.8 us
  starting transfers between devices: 25.3 us -> 29.3 us
    ppermute x5, waiting for transfers between devices: 13.9 us -> 9.25 us  [paired(): others.append(lax.ppermute(pair, 'dp', shift))]
    ppermute x3, starting transfers between devices: 1.68 us -> 3.96 us  [body(): lax.ppermute(both, 'expert', [(moved(i, d, 0), i) for i in range(groups)])]
    ppermute x6, waiting for transfers between devices: 25.3 us -> 23.8 us  [along(): return lax.ppermute(block, 'expert', pairs)]
    ppermute x5, starting transfers between devices: 6.3 us -> 7.72 us  [pick(): lax.ppermute(other, 'expert', [(i, i ^ 1) for i in range(LINE * SIDES)])]
  transfers between devices with their start and end apart: 23 -> 23, of which waited for: 11 -> 13; matrix products, arithmetic and copies ran while one was open for 0% -> 0% of each run, Pallas kernels for 10% -> 11%
where the time goes in v16:
time: 88.1 us; the launch traced here: 87.9 us
  waiting for transfers between devices  39.8 us (45%)
  starting transfers between devices  29.3 us (33%)
  Pallas kernels  15.1 us (17%)
  local copies, waits for them, and re-layouts  2.79 us (3%)
  between operations  0.89 us (1%)
    ppermute x6, waiting for transfers between devices, along(): return lax.ppermute(block, 'expert', pairs)  23.8 us
    pallas_call x20, Pallas kernels, __call__(): pl.pallas_call(body, out_shape=outs, in_specs=in_specs, compiler_params=p...  15.1 us
    ppermute x5, waiting for transfers between devices, paired(): others.append(lax.ppermute(pair, 'dp', shift))  9.25 us
    ppermute x6, starting transfers between devices, along(): return lax.ppermute(block, 'expert', pairs)  9.24 us
    ppermute x5, starting transfers between devices, pick(): lax.ppermute(other, 'expert', [(i, i ^ 1) for i in range(LINE * SIDES)])  7.72 us
    ppermute x5, starting transfers between devices, paired(): others.append(lax.ppermute(pair, 'dp', shift))  6.18 us
    ppermute x3, starting transfers between devices, body(): lax.ppermute(both, 'expert', [(moved(i, d, 0), i) for i in range(groups)])  3.96 us
    ppermute x5, waiting for transfers between devices, pick(): lax.ppermute(other, 'expert', [(i, i ^ 1) for i in range(LINE * SIDES)])  2.86 us
  transfers between devices with their start and end apart: 23, of which 13 were waited for; matrix products, arithmetic and copies ran while one was open for 0% of the time, Pallas kernels for 11%

profile of v16, /device:TPU:0, one launch (start us, length us, event | category | flops | bytes accessed | tf_op | source)
XLA Modules:
  0.0 87.9 jit_solution(4880759552212369592)
XLA Ops:
  0.6 1.9 %shard_map.77 = (s32[2,128]{1,0:T(2,128)}, bf16[144,896]{1,0:T(8,128)(2,1)}) custom-call(s32[2,128]{1,0:T(2,128)} %bitcast.14, f32[2,128]{1,0:T(2,128)} %bitcast.10, bf16[128,2048]{1,0:T(8,128)(2,1)} %rows_ref.3), custom_call_target="tpu_custom_call" | custom-call | flops 1 | bytes 1 | tf_op jit(solution)/shard_map/pallas_call | solution.py:43
  2.5 3.1 %collective-permute-start = (bf16[144,896]{1,0:T(8,128)(2,1)}, bf16[144,896]{1,0:T(8,128)(2,1)S(1)}, u32[]{:S(2)}, u32[]{:S(2)}) collective-permute-start(bf16[144,896]{1,0:T(8,128)(2,1)} %get-tuple-element.33.refs_0_), channel_id=1, source_target_pairs={{0,2},{1,3},{2,4},{3,5},{4,6},{5,7},{6,0},{7,1},{8,10},{9,11},{10,... | collective-permute-start | bytes 774152 | tf_op jit(solution)/shard_map/ppermute | solution.py:339
  5.6 2.1 %collective-permute-start.1 = (bf16[144,896]{1,0:T(8,128)(2,1)}, bf16[144,896]{1,0:T(8,128)(2,1)S(1)}, u32[]{:S(2)}, u32[]{:S(2)}) collective-permute-start(bf16[144,896]{1,0:T(8,128)(2,1)} %get-tuple-element.33.refs_0_), channel_id=1, source_target_pairs={{0,6},{1,7},{2,0},{3,1},{4,2},{5,3},{6,4},{7,5},{8,14},{9,15},{10,... | collective-permute-start | bytes 774152 | tf_op jit(solution)/shard_map/ppermute | solution.py:339
  7.7 7.2 %collective-permute-done.refs_1_ = bf16[144,896]{1,0:T(8,128)(2,1)S(1)} collective-permute-done((bf16[144,896]{1,0:T(8,128)(2,1)}, bf16[144,896]{1,0:T(8,128)(2,1)S(1)}, u32[]{:S(2)}, u32[]{:S(2)}) %collective-permute-start) | collective-permute-done | bytes 258080 | tf_op jit(solution)/shard_map/ppermute | solution.py:339
  16.3 2.9 %collective-permute-done.1.refs_2_ = bf16[144,896]{1,0:T(8,128)(2,1)S(1)} collective-permute-done((bf16[144,896]{1,0:T(8,128)(2,1)}, bf16[144,896]{1,0:T(8,128)(2,1)S(1)}, u32[]{:S(2)}, u32[]{:S(2)}) %collective-permute-start.1) | collective-permute-done | bytes 258080 | tf_op jit(solution)/shard_map/ppermute | solution.py:339
  20.6 1.8 %collective-permute-start.6 = (bf16[2,96,896]{2,1,0:T(8,128)(2,1)S(1)}, bf16[2,96,896]{2,1,0:T(8,128)(2,1)S(1)}, u32[]{:S(2)}, u32[]{:S(2)}) collective-permute-start(bf16[2,96,896]{2,1,0:T(8,128)(2,1)S(1)} %get-tuple-element.40), channel_id=1, source_target_pairs={{0,1},{1,0},{2,3},{3,2},{4,5},{5,4},{6,7},{7,6},{8,9},{9,8},{10,11... | collective-permute-start | bytes 1032200 | tf_op jit(solution)/shard_map/ppermute | solution.py:350
  22.4 2.9 %collective-permute-start.4 = (bf16[128,1152]{1,0:T(8,128)(2,1)S(1)}, bf16[128,1152]{1,0:T(8,128)(2,1)S(1)}, u32[]{:S(2)}, u32[]{:S(2)}) collective-permute-start(bf16[128,1152]{1,0:T(8,128)(2,1)S(1)} %shard_map.76.refs_0_), channel_id=1, source_target_pairs={{0,6},{1,7},{2,0},{3,1},{4,2},{5,3},{6,4},{7,5},{8,14},{9,15},{10,... | collective-permute-start | bytes 884744 | tf_op jit(solution)/shard_map/ppermute | solution.py:339
  26.3 2.8 %collective-permute-start.8 = (bf16[2,32,1152]{2,1,0:T(8,128)(2,1)S(1)}, bf16[2,32,1152]{2,1,0:T(8,128)(2,1)S(1)}, u32[]{:S(2)}, u32[]{:S(2)}) collective-permute-start(bf16[2,32,1152]{2,1,0:T(8,128)(2,1)S(1)} %get-tuple-element.42), channel_id=1, source_target_pairs={{0,1},{1,0},{2,3},{3,2},{4,5},{5,4},{6,7},{7,6},{8,9},{9,8},{10,11... | collective-permute-start | bytes 442376 | tf_op jit(solution)/shard_map/ppermute | solution.py:350
  29.2 6.3 %collective-permute-done.4.refs_1_ = bf16[128,1152]{1,0:T(8,128)(2,1)S(1)} collective-permute-done((bf16[128,1152]{1,0:T(8,128)(2,1)S(1)}, bf16[128,1152]{1,0:T(8,128)(2,1)S(1)}, u32[]{:S(2)}, u32[]{:S(2)}) %collective-permute-start.4) | collective-permute-done | bytes 294944 | tf_op jit(solution)/shard_map/ppermute | solution.py:339
  35.5 2.4 %collective-permute-done.3.refs_0_ = bf16[128,1152]{1,0:T(8,128)(2,1)S(1)} collective-permute-done((bf16[128,1152]{1,0:T(8,128)(2,1)S(1)}, bf16[128,1152]{1,0:T(8,128)(2,1)S(1)}, u32[]{:S(2)}, u32[]{:S(2)}) %collective-permute-start.3) | collective-permute-done | bytes 294944 | tf_op jit(solution)/shard_map/ppermute | solution.py:339
  40.5 1.5 %collective-permute-start.10 = (bf16[2,64,1152]{2,1,0:T(8,128)(2,1)S(1)}, bf16[2,64,1152]{2,1,0:T(8,128)(2,1)S(1)}, u32[]{:S(2)}, u32[]{:S(2)}) collective-permute-start(bf16[2,64,1152]{2,1,0:T(8,128)(2,1)S(1)} %get-tuple-element.47), channel_id=1, source_target_pairs={{0,1},{1,0},{2,3},{3,2},{4,5},{5,4},{6,7},{7,6},{8,9},{9,8},{10,11... | collective-permute-start | bytes 884744 | tf_op jit(solution)/shard_map/ppermute | solution.py:350
  42.6 1.6 %collective-permute-start.13 = (bf16[2,64,896]{2,1,0:T(8,128)(2,1)S(1)}, bf16[2,64,896]{2,1,0:T(8,128)(2,1)S(1)}, u32[]{:S(2)}, u32[]{:S(2)}) collective-permute-start(bf16[2,64,896]{2,1,0:T(8,128)(2,1)S(1)} %get-tuple-element.49), channel_id=1, source_target_pairs={{0,16},{8,24},{16,0},{24,8},{1,17},{9,25},{17,1},{25,9},{2,18},{10... | collective-permute-start | bytes 688136 | tf_op jit(solution)/shard_map/ppermute | solution.py:453
  44.7 1.5 %collective-permute-start.12 = (bf16[2,64,896]{2,1,0:T(8,128)(2,1)S(1)}, bf16[2,64,896]{2,1,0:T(8,128)(2,1)S(1)}, u32[]{:S(2)}, u32[]{:S(2)}) collective-permute-start(bf16[2,64,896]{2,1,0:T(8,128)(2,1)S(1)} %get-tuple-element.45.refs_2_), channel_id=1, source_target_pairs={{0,16},{8,24},{16,0},{24,8},{1,17},{9,25},{17,1},{25,9},{2,18},{10... | collective-permute-start | bytes 688136 | tf_op jit(solution)/shard_map/ppermute | solution.py:453
  46.3 4.3 %collective-permute-done.5.refs_0_ = bf16[128,1152]{1,0:T(8,128)(2,1)S(1)} collective-permute-done((bf16[128,1152]{1,0:T(8,128)(2,1)S(1)}, bf16[128,1152]{1,0:T(8,128)(2,1)S(1)}, u32[]{:S(2)}, u32[]{:S(2)}) %collective-permute-start.5) | collective-permute-done | bytes 294944 | tf_op jit(solution)/shard_map/ppermute | solution.py:339
  50.8 1.6 %collective-permute-start.11 = (bf16[2,32,1152]{2,1,0:T(8,128)(2,1)S(1)}, bf16[2,32,1152]{2,1,0:T(8,128)(2,1)S(1)}, u32[]{:S(2)}, u32[]{:S(2)}) collective-permute-start(bf16[2,32,1152]{2,1,0:T(8,128)(2,1)S(1)} %get-tuple-element.48), channel_id=1, source_target_pairs={{0,1},{1,0},{2,3},{3,2},{4,5},{5,4},{6,7},{7,6},{8,9},{9,8},{10,11... | collective-permute-start | bytes 442376 | tf_op jit(solution)/shard_map/ppermute | solution.py:350
  53.4 2.8 %collective-permute-done.11.refs_6_ = bf16[2,32,1152]{2,1,0:T(8,128)(2,1)S(1)} collective-permute-done((bf16[2,32,1152]{2,1,0:T(8,128)(2,1)S(1)}, bf16[2,32,1152]{2,1,0:T(8,128)(2,1)S(1)}, u32[]{:S(2)}, u32[]{:S(2)}) %collective-permute-start.11) | collective-permute-done | bytes 147488 | tf_op jit(solution)/shard_map/ppermute | solution.py:350
  56.2 3.9 %collective-permute-done.12.refs_8_.refs_2_ = bf16[2,64,896]{2,1,0:T(8,128)(2,1)S(1)} collective-permute-done((bf16[2,64,896]{2,1,0:T(8,128)(2,1)S(1)}, bf16[2,64,896]{2,1,0:T(8,128)(2,1)S(1)}, u32[]{:S(2)}, u32[]{:S(2)}) %collective-permute-start.12) | collective-permute-done | bytes 229408 | tf_op jit(solution)/shard_map/ppermute | solution.py:453
  63.7 1.6 %collective-permute-start.21 = (bf16[2,192,640]{2,1,0:T(8,128)(2,1)S(1)}, bf16[2,192,640]{2,1,0:T(8,128)(2,1)S(1)}, u32[]{:S(2)}, u32[]{:S(2)}) collective-permute-start(bf16[2,192,640]{2,1,0:T(8,128)(2,1)S(1)} %shard_map.89.refs_2_), channel_id=1, source_target_pairs={{0,16},{8,24},{16,0},{24,8},{1,17},{9,25},{17,1},{25,9},{2,18},{10... | collective-permute-start | bytes 1474568 | tf_op jit(solution)/shard_map/ppermute | solution.py:453
  66.4 2.2 %shard_map.91 = (bf16[8,2,32,768]{3,2,1,0:T(8,128)(2,1)}, f32[2,256]{1,0:T(2,128)S(1)}) custom-call(bf16[2,768,2048]{2,1,0:T(8,128)(2,1)S(1)} %copy-done, bf16[2,32,1152]{2,1,0:T(8,128)(2,1)S(1)} %get-tuple-element.36.refs_3_.refs_1_, bf16[2,64,1152]{2,1,0:T(8,128)(2,1)S(1)} %get-tuple-element.37.refs_5_.refs_2_, ...), custom_call_target="tpu_custom_call" | custom-call | flops 1 | bytes 1 | tf_op jit(solution)/shard_map/pallas_call | solution.py:43
  68.6 1.5 %collective-permute-start.17 = (f32[2,256]{1,0:T(2,128)S(1)}, f32[2,256]{1,0:T(2,128)S(1)}, u32[]{:S(2)}, u32[]{:S(2)}) collective-permute-start(f32[2,256]{1,0:T(2,128)S(1)} %get-tuple-element.57.refs_5_), channel_id=1, source_target_pairs={{0,1},{1,0},{2,3},{3,2},{4,5},{5,4},{6,7},{7,6},{8,9},{9,8},{10,11... | collective-permute-start | bytes 6152 | tf_op jit(solution)/shard_map/ppermute | solution.py:494
  70.1 2.1 %collective-permute-done.17 = f32[2,256]{1,0:T(2,128)S(1)} collective-permute-done((f32[2,256]{1,0:T(2,128)S(1)}, f32[2,256]{1,0:T(2,128)S(1)}, u32[]{:S(2)}, u32[]{:S(2)}) %collective-permute-start.17) | collective-permute-done | bytes 2080 | tf_op jit(solution)/shard_map/ppermute | solution.py:494
  76.2 1.6 %shard_map.92 = (f32[192,2,2048]{2,1,0:T(2,128)}, f32[8,128]{1,0:T(8,128)S(1)}) custom-call(bf16[2,2,192,896]{3,2,1,0:T(8,128)(2,1)S(1)} %get-tuple-element.43.refs_0_.refs_2_, bf16[2,2,192,896]{3,2,1,0:T(8,128)(2,1)S(1)} %collective-permute-done.9.refs_1_, bf16[2,64,896]{2,1,0:T(8,128)(2,1)S(1)} %collective-permute-done.12.refs_8_.refs_2_, ...), custom_call_target="tpu_custom_call" | custom-call | flops 1 | bytes 1 | tf_op jit(solution)/shard_map/pallas_call | solution.py:43
  80.3 5.2 %collective-permute-done.22.refs_2_ = bf16[2,192,512]{2,1,0:T(8,128)(2,1)S(1)} collective-permute-done((bf16[2,192,512]{2,1,0:T(8,128)(2,1)S(1)}, bf16[2,192,512]{2,1,0:T(8,128)(2,1)S(1)}, u32[]{:S(2)}, u32[]{:S(2)}) %collective-permute-start.22) | collective-permute-done | bytes 393248 | tf_op jit(solution)/shard_map/ppermute | solution.py:453
  86.2 1.7 %shard_map.95 = (f32[192,2,2048]{2,1,0:T(2,128)}, f32[8,128]{1,0:T(8,128)}) custom-call(bf16[2,2,192,512]{3,2,1,0:T(8,128)(2,1)S(1)} %get-tuple-element.52.refs_2_.refs_0_, bf16[2,2,192,512]{3,2,1,0:T(8,128)(2,1)S(1)} %collective-permute-done.15.refs_1_, bf16[2,192,512]{2,1,0:T(8,128)(2,1)S(1)} %collective-permute-done.22.refs_2_, ...), custom_call_target="tpu_custom_call", output_to_operand_aliasing={{0}: (3, {})} | custom-call | flops 1 | bytes 1 | tf_op jit(solution)/shard_map/pallas_call | solution.py:43
  (59 shorter events, 20.5 us)
Async XLA Ops:
  0.6 21.7 %copy-start.3 = (bf16[128,2048]{1,0:T(8,128)(2,1)S(1)}, bf16[128,2048]{1,0:T(8,128)(2,1)}, u32[]{:S(2)}) copy-start(bf16[128,2048]{1,0:T(8,128)(2,1)} %rows_ref.3) | copy-start | bytes 1572868
  2.5 12.4 %collective-permute-start = (bf16[144,896]{1,0:T(8,128)(2,1)}, bf16[144,896]{1,0:T(8,128)(2,1)S(1)}, u32[]{:S(2)}, u32[]{:S(2)}) collective-permute-start(bf16[144,896]{1,0:T(8,128)(2,1)} %get-tuple-element.33.refs_0_), channel_id=1, source_target_pairs={{0,2},{1,3},{2,4},{3,5},{4,6},{5,7},{6,0},{7,1},{8,10},{9,11},{10,... | collective-permute-start | bytes 774152 | tf_op jit(solution)/shard_map/ppermute | solution.py:339
  5.6 13.6 %collective-permute-start.1 = (bf16[144,896]{1,0:T(8,128)(2,1)}, bf16[144,896]{1,0:T(8,128)(2,1)S(1)}, u32[]{:S(2)}, u32[]{:S(2)}) collective-permute-start(bf16[144,896]{1,0:T(8,128)(2,1)} %get-tuple-element.33.refs_0_), channel_id=1, source_target_pairs={{0,6},{1,7},{2,0},{3,1},{4,2},{5,3},{6,4},{7,5},{8,14},{9,15},{10,... | collective-permute-start | bytes 774152 | tf_op jit(solution)/shard_map/ppermute | solution.py:339
  14.9 10.9 %collective-permute-start.2 = (bf16[144,896]{1,0:T(8,128)(2,1)S(1)}, bf16[144,896]{1,0:T(8,128)(2,1)S(1)}, u32[]{:S(2)}, u32[]{:S(2)}) collective-permute-start(bf16[144,896]{1,0:T(8,128)(2,1)S(1)} %collective-permute-done.refs_1_), channel_id=1, source_target_pairs={{0,2},{1,3},{2,4},{3,5},{4,6},{5,7},{6,0},{7,1},{8,10},{9,11},{10,... | collective-permute-start | bytes 774152 | tf_op jit(solution)/shard_map/ppermute | solution.py:339
  20.6 17.7 %collective-permute-start.6 = (bf16[2,96,896]{2,1,0:T(8,128)(2,1)S(1)}, bf16[2,96,896]{2,1,0:T(8,128)(2,1)S(1)}, u32[]{:S(2)}, u32[]{:S(2)}) collective-permute-start(bf16[2,96,896]{2,1,0:T(8,128)(2,1)S(1)} %get-tuple-element.40), channel_id=1, source_target_pairs={{0,1},{1,0},{2,3},{3,2},{4,5},{5,4},{6,7},{7,6},{8,9},{9,8},{10,11... | collective-permute-start | bytes 1032200 | tf_op jit(solution)/shard_map/ppermute | solution.py:350
  22.4 13.1 %collective-permute-start.4 = (bf16[128,1152]{1,0:T(8,128)(2,1)S(1)}, bf16[128,1152]{1,0:T(8,128)(2,1)S(1)}, u32[]{:S(2)}, u32[]{:S(2)}) collective-permute-start(bf16[128,1152]{1,0:T(8,128)(2,1)S(1)} %shard_map.76.refs_0_), channel_id=1, source_target_pairs={{0,6},{1,7},{2,0},{3,1},{4,2},{5,3},{6,4},{7,5},{8,14},{9,15},{10,... | collective-permute-start | bytes 884744 | tf_op jit(solution)/shard_map/ppermute | solution.py:339
  25.3 12.6 %collective-permute-start.3 = (bf16[128,1152]{1,0:T(8,128)(2,1)S(1)}, bf16[128,1152]{1,0:T(8,128)(2,1)S(1)}, u32[]{:S(2)}, u32[]{:S(2)}) collective-permute-start(bf16[128,1152]{1,0:T(8,128)(2,1)S(1)} %shard_map.76.refs_0_), channel_id=1, source_target_pairs={{0,2},{1,3},{2,4},{3,5},{4,6},{5,7},{6,0},{7,1},{8,10},{9,11},{10,... | collective-permute-start | bytes 884744 | tf_op jit(solution)/shard_map/ppermute | solution.py:339
  26.3 11.9 %collective-permute-start.8 = (bf16[2,32,1152]{2,1,0:T(8,128)(2,1)S(1)}, bf16[2,32,1152]{2,1,0:T(8,128)(2,1)S(1)}, u32[]{:S(2)}, u32[]{:S(2)}) collective-permute-start(bf16[2,32,1152]{2,1,0:T(8,128)(2,1)S(1)} %get-tuple-element.42), channel_id=1, source_target_pairs={{0,1},{1,0},{2,3},{3,2},{4,5},{5,4},{6,7},{7,6},{8,9},{9,8},{10,11... | collective-permute-start | bytes 442376 | tf_op jit(solution)/shard_map/ppermute | solution.py:350
  29.1 9.1 %collective-permute-start.7 = (bf16[2,32,896]{2,1,0:T(8,128)(2,1)S(1)}, bf16[2,32,896]{2,1,0:T(8,128)(2,1)S(1)}, u32[]{:S(2)}, u32[]{:S(2)}) collective-permute-start(bf16[2,32,896]{2,1,0:T(8,128)(2,1)S(1)} %get-tuple-element.41), channel_id=1, source_target_pairs={{0,1},{1,0},{2,3},{3,2},{4,5},{5,4},{6,7},{7,6},{8,9},{9,8},{10,11... | collective-permute-start | bytes 344072 | tf_op jit(solution)/shard_map/ppermute | solution.py:350
  39.2 3.2 %collective-permute-start.9 = (bf16[2,2,192,896]{3,2,1,0:T(8,128)(2,1)S(1)}, bf16[2,2,192,896]{3,2,1,0:T(8,128)(2,1)S(1)}, u32[]{:S(2)}, u32[]{:S(2)}) collective-permute-start(bf16[2,2,192,896]{3,2,1,0:T(8,128)(2,1)S(1)} %get-tuple-element.44), channel_id=1, source_target_pairs={{0,8},{8,0},{16,24},{24,16},{1,9},{9,1},{17,25},{25,17},{2,10},{10... | collective-permute-start | bytes 4128776 | tf_op jit(solution)/shard_map/ppermute | solution.py:442
  39.3 11.2 %collective-permute-start.5 = (bf16[128,1152]{1,0:T(8,128)(2,1)S(1)}, bf16[128,1152]{1,0:T(8,128)(2,1)S(1)}, u32[]{:S(2)}, u32[]{:S(2)}) collective-permute-start(bf16[128,1152]{1,0:T(8,128)(2,1)S(1)} %collective-permute-done.3.refs_0_), channel_id=1, source_target_pairs={{0,2},{1,3},{2,4},{3,5},{4,6},{5,7},{6,0},{7,1},{8,10},{9,11},{10,... | collective-permute-start | bytes 884744 | tf_op jit(solution)/shard_map/ppermute | solution.py:339
  40.5 12.9 %collective-permute-start.10 = (bf16[2,64,1152]{2,1,0:T(8,128)(2,1)S(1)}, bf16[2,64,1152]{2,1,0:T(8,128)(2,1)S(1)}, u32[]{:S(2)}, u32[]{:S(2)}) collective-permute-start(bf16[2,64,1152]{2,1,0:T(8,128)(2,1)S(1)} %get-tuple-element.47), channel_id=1, source_target_pairs={{0,1},{1,0},{2,3},{3,2},{4,5},{5,4},{6,7},{7,6},{8,9},{9,8},{10,11... | collective-permute-start | bytes 884744 | tf_op jit(solution)/shard_map/ppermute | solution.py:350
  42.6 13.6 %collective-permute-start.13 = (bf16[2,64,896]{2,1,0:T(8,128)(2,1)S(1)}, bf16[2,64,896]{2,1,0:T(8,128)(2,1)S(1)}, u32[]{:S(2)}, u32[]{:S(2)}) collective-permute-start(bf16[2,64,896]{2,1,0:T(8,128)(2,1)S(1)} %get-tuple-element.49), channel_id=1, source_target_pairs={{0,16},{8,24},{16,0},{24,8},{1,17},{9,25},{17,1},{25,9},{2,18},{10... | collective-permute-start | bytes 688136 | tf_op jit(solution)/shard_map/ppermute | solution.py:453
  44.2 12.0 %collective-permute-start.14 = (bf16[2,64,896]{2,1,0:T(8,128)(2,1)S(1)}, bf16[2,64,896]{2,1,0:T(8,128)(2,1)S(1)}, u32[]{:S(2)}, u32[]{:S(2)}) collective-permute-start(bf16[2,64,896]{2,1,0:T(8,128)(2,1)S(1)} %get-tuple-element.50), channel_id=1, source_target_pairs={{0,16},{8,24},{16,0},{24,8},{1,17},{9,25},{17,1},{25,9},{2,18},{10... | collective-permute-start | bytes 688136 | tf_op jit(solution)/shard_map/ppermute | solution.py:453
  44.7 15.4 %collective-permute-start.12 = (bf16[2,64,896]{2,1,0:T(8,128)(2,1)S(1)}, bf16[2,64,896]{2,1,0:T(8,128)(2,1)S(1)}, u32[]{:S(2)}, u32[]{:S(2)}) collective-permute-start(bf16[2,64,896]{2,1,0:T(8,128)(2,1)S(1)} %get-tuple-element.45.refs_2_), channel_id=1, source_target_pairs={{0,16},{8,24},{16,0},{24,8},{1,17},{9,25},{17,1},{25,9},{2,18},{10... | collective-permute-start | bytes 688136 | tf_op jit(solution)/shard_map/ppermute | solution.py:453
  50.8 5.5 %collective-permute-start.11 = (bf16[2,32,1152]{2,1,0:T(8,128)(2,1)S(1)}, bf16[2,32,1152]{2,1,0:T(8,128)(2,1)S(1)}, u32[]{:S(2)}, u32[]{:S(2)}) collective-permute-start(bf16[2,32,1152]{2,1,0:T(8,128)(2,1)S(1)} %get-tuple-element.48), channel_id=1, source_target_pairs={{0,1},{1,0},{2,3},{3,2},{4,5},{5,4},{6,7},{7,6},{8,9},{9,8},{10,11... | collective-permute-start | bytes 442376 | tf_op jit(solution)/shard_map/ppermute | solution.py:350
  61.0 2.6 %collective-permute-start.16 = (bf16[2,2,192,640]{3,2,1,0:T(8,128)(2,1)S(1)}, bf16[2,2,192,640]{3,2,1,0:T(8,128)(2,1)S(1)}, u32[]{:S(2)}, u32[]{:S(2)}) collective-permute-start(bf16[2,2,192,640]{3,2,1,0:T(8,128)(2,1)S(1)} %get-tuple-element.54), channel_id=1, source_target_pairs={{0,8},{8,0},{16,24},{24,16},{1,9},{9,1},{17,25},{25,17},{2,10},{10... | collective-permute-start | bytes 2949128 | tf_op jit(solution)/shard_map/ppermute | solution.py:442
  61.6 3.7 %collective-permute-start.15 = (bf16[2,2,192,512]{3,2,1,0:T(8,128)(2,1)S(1)}, bf16[2,2,192,512]{3,2,1,0:T(8,128)(2,1)S(1)}, u32[]{:S(2)}, u32[]{:S(2)}) collective-permute-start(bf16[2,2,192,512]{3,2,1,0:T(8,128)(2,1)S(1)} %get-tuple-element.53), channel_id=1, source_target_pairs={{0,8},{8,0},{16,24},{24,16},{1,9},{9,1},{17,25},{25,17},{2,10},{10... | collective-permute-start | bytes 2359304 | tf_op jit(solution)/shard_map/ppermute | solution.py:442
  63.7 14.1 %collective-permute-start.21 = (bf16[2,192,640]{2,1,0:T(8,128)(2,1)S(1)}, bf16[2,192,640]{2,1,0:T(8,128)(2,1)S(1)}, u32[]{:S(2)}, u32[]{:S(2)}) collective-permute-start(bf16[2,192,640]{2,1,0:T(8,128)(2,1)S(1)} %shard_map.89.refs_2_), channel_id=1, source_target_pairs={{0,16},{8,24},{16,0},{24,8},{1,17},{9,25},{17,1},{25,9},{2,18},{10... | collective-permute-start | bytes 1474568 | tf_op jit(solution)/shard_map/ppermute | solution.py:453
  65.4 20.1 %collective-permute-start.22 = (bf16[2,192,512]{2,1,0:T(8,128)(2,1)S(1)}, bf16[2,192,512]{2,1,0:T(8,128)(2,1)S(1)}, u32[]{:S(2)}, u32[]{:S(2)}) collective-permute-start(bf16[2,192,512]{2,1,0:T(8,128)(2,1)S(1)} %shard_map.90.refs_9_), channel_id=1, source_target_pairs={{0,16},{8,24},{16,0},{24,8},{1,17},{9,25},{17,1},{25,9},{2,18},{10... | collective-permute-start | bytes 1179656 | tf_op jit(solution)/shard_map/ppermute | solution.py:453
  68.6 3.6 %collective-permute-start.17 = (f32[2,256]{1,0:T(2,128)S(1)}, f32[2,256]{1,0:T(2,128)S(1)}, u32[]{:S(2)}, u32[]{:S(2)}) collective-permute-start(f32[2,256]{1,0:T(2,128)S(1)} %get-tuple-element.57.refs_5_), channel_id=1, source_target_pairs={{0,1},{1,0},{2,3},{3,2},{4,5},{5,4},{6,7},{7,6},{8,9},{9,8},{10,11... | collective-permute-start | bytes 6152 | tf_op jit(solution)/shard_map/ppermute | solution.py:494
  72.2 7.0 %collective-permute-start.20 = (f32[2,2,256]{2,1,0:T(2,128)S(1)}, f32[2,2,256]{2,1,0:T(2,128)S(1)}, u32[]{:S(2)}, u32[]{:S(2)}) collective-permute-start(f32[2,2,256]{2,1,0:T(2,128)S(1)} %pad_maximum_fusion.refs_2_), channel_id=1, source_target_pairs={{6,0},{7,1},{0,2},{1,3},{2,4},{3,5},{4,6},{5,7},{14,8},{15,9},{8,1... | collective-permute-start | bytes 12296 | tf_op jit(solution)/shard_map/ppermute | solution.py:496
  73.4 5.8 %collective-permute-start.19 = (f32[2,2,256]{2,1,0:T(2,128)S(1)}, f32[2,2,256]{2,1,0:T(2,128)S(1)}, u32[]{:S(2)}, u32[]{:S(2)}) collective-permute-start(f32[2,2,256]{2,1,0:T(2,128)S(1)} %pad_maximum_fusion.refs_2_), channel_id=1, source_target_pairs={{4,0},{5,1},{6,2},{7,3},{0,4},{1,5},{2,6},{3,7},{12,8},{13,9},{14,... | collective-permute-start | bytes 12296 | tf_op jit(solution)/shard_map/ppermute | solution.py:496
  74.8 4.4 %collective-permute-start.18 = (f32[2,2,256]{2,1,0:T(2,128)S(1)}, f32[2,2,256]{2,1,0:T(2,128)S(1)}, u32[]{:S(2)}, u32[]{:S(2)}) collective-permute-start(f32[2,2,256]{2,1,0:T(2,128)S(1)} %pad_maximum_fusion.refs_2_), channel_id=1, source_target_pairs={{2,0},{3,1},{4,2},{5,3},{6,4},{7,5},{0,6},{1,7},{10,8},{11,9},{12,... | collective-permute-start | bytes 12296 | tf_op jit(solution)/shard_map/ppermute | solution.py:496
  (7 other events, 24.6 us)

commit v17 on v16

--- a/solution.py
+++ b/solution.py
@@ -249,7 +249,8 @@
 
 
 def prob_kernel(direct, capacity, flat_ref, probs_ref, *refs):
-    out_ref = refs[-1]
+    out_ref, mark_ref = refs[-2:]
+    mark_ref[...] = jnp.zeros(mark_ref.shape, F32)
     chosen, tokens = flat_ref.shape
     if direct:
         values = []
@@ -290,7 +291,7 @@
 
 def chunks_of(features):
     unit = features // 16
-    return [[7 * unit], [5 * unit, 4 * unit]]
+    return [[6 * unit], [6 * unit, 4 * unit]]
 
 
 def cuts_of(share, first):
@@ -320,19 +321,23 @@
             room=60,
             keep=False,
         )
+        self.blocks, self.passed = [], []
+        self.leave(first)
         rest = call(
             functools.partial(cut_kernel, widths[0]),
             [sds((tokens, w), BF16) for w in widths[1:]],
             grad_out,
             in_specs=[HBM],
             scratch_shapes=[pltpu.SemaphoreType.DMA((len(widths) - 1,))],
-            keep=False,
-        )
-        self.blocks, self.passed = [], []
-        for own in [first, *rest]:
-            on, back = self.along(own, 1), self.along(own, LINE - 1)
-            self.blocks.append([own, on, back])
-            self.passed.append(self.along(on, 1))
+            after=[self.blocks[0][1]],
+        )
+        for own in rest:
+            self.leave(own)
+
+    def leave(self, own):
+        on, back = self.along(own, 1), self.along(own, LINE - 1)
+        self.blocks.append([own, on, back])
+        self.passed.append(self.along(on, 1))
 
     def along(self, block, places):
         pairs = [(i, moved(i, places, 0)) for i in range(LINE * SIDES)]
@@ -501,13 +506,14 @@
         hidden_grad = hidden_grad.reshape(held, groups, capacity, units).transpose(1, 0, 2, 3)
         returned = lax.all_to_all(sums, "expert", split_axis=0, concat_axis=0, tiled=True)
         returned = [returned.reshape(-1, 128)]
-    prob_grad = call(
+    prob_grad, call.last = call(
         functools.partial(prob_kernel, direct, capacity),
-        sds((chosen, tokens), F32),
+        [sds((chosen, tokens), F32), sds((8, 128), F32)],
         flat,
         probs,
         *returned,
-    ).T
+    )
+    prob_grad = prob_grad.T
     finished(len(summed) - 1, len(summed))
     weight_grad = state["grad"]
     return (hidden_grad.reshape(hidden.shape), prob_grad, weight_grad)

time: 88.1 us -> 85.5 us (0.970)
  local copies, waits for them, and re-layouts: 2.79 us -> 1.06 us
    ppermute x6, starting transfers between devices: 9.24 us -> 11.1 us  [along(): return lax.ppermute(block, 'expert', pairs)]
    unnamed x16 -> x12, local copies, waits for them, and re-layouts: 2.79 us -> 1.06 us
    ppermute x5, starting transfers between devices: 7.72 us -> 6.69 us  [pick(): lax.ppermute(other, 'expert', [(i, i ^ 1) for i in range(LINE * SIDES)])]
  transfers between devices with their start and end apart: 23 -> 23, of which waited for: 13 -> 12; matrix products, arithmetic and copies ran while one was open for 0% -> 0% of each run, Pallas kernels for 11% -> 11%
where the time goes in v17:
time: 85.5 us; the launch traced here: 85.3 us
  waiting for transfers between devices  39.2 us (46%)
  starting transfers between devices  29.5 us (35%)
  Pallas kernels  14.7 us (17%)
  local copies, waits for them, and re-layouts  1.06 us (1%)
  between operations  0.89 us (1%)
    ppermute x6, waiting for transfers between devices, along(): return lax.ppermute(block, 'expert', pairs)  23.3 us
    pallas_call x20, Pallas kernels, __call__(): pl.pallas_call(body, out_shape=outs, in_specs=in_specs, compiler_params=p...  14.7 us
    ppermute x6, starting transfers between devices, along(): return lax.ppermute(block, 'expert', pairs)  11.1 us
    ppermute x5, waiting for transfers between devices, paired(): others.append(lax.ppermute(pair, 'dp', shift))  8.48 us
    ppermute x5, starting transfers between devices, pick(): lax.ppermute(other, 'expert', [(i, i ^ 1) for i in range(LINE * SIDES)])  6.69 us
    ppermute x5, starting transfers between devices, paired(): others.append(lax.ppermute(pair, 'dp', shift))  6.19 us
    ppermute x5, waiting for transfers between devices, pick(): lax.ppermute(other, 'expert', [(i, i ^ 1) for i in range(LINE * SIDES)])  3.45 us
    ppermute x3, starting transfers between devices, body(): lax.ppermute(both, 'expert', [(moved(i, d, 0), i) for i in range(groups)])  3.36 us
  transfers between devices with their start and end apart: 23, of which 12 were waited for; matrix products, arithmetic and copies ran while one was open for 0% of the time, Pallas kernels for 11%

profile of v17, /device:TPU:0, one launch (start us, length us, event | category | flops | bytes accessed | tf_op | source)
XLA Modules:
  0.0 85.3 jit_solution(16199169569809225546)
XLA Ops:
  0.6 1.9 %shard_map.76 = (s32[2,128]{1,0:T(2,128)}, bf16[144,768]{1,0:T(8,128)(2,1)}) custom-call(s32[2,128]{1,0:T(2,128)} %bitcast.13, f32[2,128]{1,0:T(2,128)} %bitcast.10, bf16[128,2048]{1,0:T(8,128)(2,1)} %refs_0_.3), custom_call_target="tpu_custom_call" | custom-call | flops 1 | bytes 1 | tf_op jit(solution)/shard_map/pallas_call | solution.py:43
  2.5 3.1 %collective-permute-start = (bf16[144,768]{1,0:T(8,128)(2,1)}, bf16[144,768]{1,0:T(8,128)(2,1)S(1)}, u32[]{:S(2)}, u32[]{:S(2)}) collective-permute-start(bf16[144,768]{1,0:T(8,128)(2,1)} %get-tuple-element.35.refs_0_), channel_id=1, source_target_pairs={{0,2},{1,3},{2,4},{3,5},{4,6},{5,7},{6,0},{7,1},{8,10},{9,11},{10,... | collective-permute-start | bytes 663560 | tf_op jit(solution)/shard_map/ppermute | solution.py:344
  5.6 2.1 %collective-permute-start.1 = (bf16[144,768]{1,0:T(8,128)(2,1)}, bf16[144,768]{1,0:T(8,128)(2,1)S(1)}, u32[]{:S(2)}, u32[]{:S(2)}) collective-permute-start(bf16[144,768]{1,0:T(8,128)(2,1)} %get-tuple-element.35.refs_0_), channel_id=1, source_target_pairs={{0,6},{1,7},{2,0},{3,1},{4,2},{5,3},{6,4},{7,5},{8,14},{9,15},{10,... | collective-permute-start | bytes 663560 | tf_op jit(solution)/shard_map/ppermute | solution.py:344
  7.7 6.4 %collective-permute-done.refs_1_ = bf16[144,768]{1,0:T(8,128)(2,1)S(1)} collective-permute-done((bf16[144,768]{1,0:T(8,128)(2,1)}, bf16[144,768]{1,0:T(8,128)(2,1)S(1)}, u32[]{:S(2)}, u32[]{:S(2)}) %collective-permute-start) | collective-permute-done | bytes 221216 | tf_op jit(solution)/shard_map/ppermute | solution.py:344
  15.3 4.1 %collective-permute-start.3 = (bf16[128,1280]{1,0:T(8,128)(2,1)S(1)}, bf16[128,1280]{1,0:T(8,128)(2,1)S(1)}, u32[]{:S(2)}, u32[]{:S(2)}) collective-permute-start(bf16[128,1280]{1,0:T(8,128)(2,1)S(1)} %shard_map.77.refs_1_.refs_0_), channel_id=1, source_target_pairs={{0,2},{1,3},{2,4},{3,5},{4,6},{5,7},{6,0},{7,1},{8,10},{9,11},{10,... | collective-permute-start | bytes 983048 | tf_op jit(solution)/shard_map/ppermute | solution.py:344
  20.6 1.6 %collective-permute-start.6 = (bf16[2,96,768]{2,1,0:T(8,128)(2,1)S(1)}, bf16[2,96,768]{2,1,0:T(8,128)(2,1)S(1)}, u32[]{:S(2)}, u32[]{:S(2)}) collective-permute-start(bf16[2,96,768]{2,1,0:T(8,128)(2,1)S(1)} %get-tuple-element.42), channel_id=1, source_target_pairs={{0,1},{1,0},{2,3},{3,2},{4,5},{5,4},{6,7},{7,6},{8,9},{9,8},{10,11... | collective-permute-start | bytes 884744 | tf_op jit(solution)/shard_map/ppermute | solution.py:355
  22.2 3.1 %collective-permute-done.2.refs_0_ = bf16[144,768]{1,0:T(8,128)(2,1)S(1)} collective-permute-done((bf16[144,768]{1,0:T(8,128)(2,1)S(1)}, bf16[144,768]{1,0:T(8,128)(2,1)S(1)}, u32[]{:S(2)}, u32[]{:S(2)}) %collective-permute-start.2) | collective-permute-done | bytes 221216 | tf_op jit(solution)/shard_map/ppermute | solution.py:344
  25.7 1.6 %collective-permute-start.8 = (bf16[2,32,1280]{2,1,0:T(8,128)(2,1)S(1)}, bf16[2,32,1280]{2,1,0:T(8,128)(2,1)S(1)}, u32[]{:S(2)}, u32[]{:S(2)}) collective-permute-start(bf16[2,32,1280]{2,1,0:T(8,128)(2,1)S(1)} %get-tuple-element.44), channel_id=1, source_target_pairs={{0,1},{1,0},{2,3},{3,2},{4,5},{5,4},{6,7},{7,6},{8,9},{9,8},{10,11... | collective-permute-start | bytes 491528 | tf_op jit(solution)/shard_map/ppermute | solution.py:355
  27.8 4.4 %collective-permute-done.3.refs_0_ = bf16[128,1280]{1,0:T(8,128)(2,1)S(1)} collective-permute-done((bf16[128,1280]{1,0:T(8,128)(2,1)S(1)}, bf16[128,1280]{1,0:T(8,128)(2,1)S(1)}, u32[]{:S(2)}, u32[]{:S(2)}) %collective-permute-start.3) | collective-permute-done | bytes 327712 | tf_op jit(solution)/shard_map/ppermute | solution.py:344
  32.2 4.1 %collective-permute-done.4.refs_1_ = bf16[128,1280]{1,0:T(8,128)(2,1)S(1)} collective-permute-done((bf16[128,1280]{1,0:T(8,128)(2,1)S(1)}, bf16[128,1280]{1,0:T(8,128)(2,1)S(1)}, u32[]{:S(2)}, u32[]{:S(2)}) %collective-permute-start.4) | collective-permute-done | bytes 327712 | tf_op jit(solution)/shard_map/ppermute | solution.py:344
  38.6 1.5 %collective-permute-start.10 = (bf16[2,64,1280]{2,1,0:T(8,128)(2,1)S(1)}, bf16[2,64,1280]{2,1,0:T(8,128)(2,1)S(1)}, u32[]{:S(2)}, u32[]{:S(2)}) collective-permute-start(bf16[2,64,1280]{2,1,0:T(8,128)(2,1)S(1)} %get-tuple-element.49), channel_id=1, source_target_pairs={{0,1},{1,0},{2,3},{3,2},{4,5},{5,4},{6,7},{7,6},{8,9},{9,8},{10,11... | collective-permute-start | bytes 983048 | tf_op jit(solution)/shard_map/ppermute | solution.py:355
  40.5 1.6 %collective-permute-start.12 = (bf16[2,64,768]{2,1,0:T(8,128)(2,1)S(1)}, bf16[2,64,768]{2,1,0:T(8,128)(2,1)S(1)}, u32[]{:S(2)}, u32[]{:S(2)}) collective-permute-start(bf16[2,64,768]{2,1,0:T(8,128)(2,1)S(1)} %get-tuple-element.47.refs_2_), channel_id=1, source_target_pairs={{0,16},{8,24},{16,0},{24,8},{1,17},{9,25},{17,1},{25,9},{2,18},{10... | collective-permute-start | bytes 589832 | tf_op jit(solution)/shard_map/ppermute | solution.py:458
  42.5 1.5 %collective-permute-start.14 = (bf16[2,64,768]{2,1,0:T(8,128)(2,1)S(1)}, bf16[2,64,768]{2,1,0:T(8,128)(2,1)S(1)}, u32[]{:S(2)}, u32[]{:S(2)}) collective-permute-start(bf16[2,64,768]{2,1,0:T(8,128)(2,1)S(1)} %get-tuple-element.52), channel_id=1, source_target_pairs={{0,16},{8,24},{16,0},{24,8},{1,17},{9,25},{17,1},{25,9},{2,18},{10... | collective-permute-start | bytes 589832 | tf_op jit(solution)/shard_map/ppermute | solution.py:458
  44.1 5.3 %collective-permute-done.5.refs_0_ = bf16[128,1280]{1,0:T(8,128)(2,1)S(1)} collective-permute-done((bf16[128,1280]{1,0:T(8,128)(2,1)S(1)}, bf16[128,1280]{1,0:T(8,128)(2,1)S(1)}, u32[]{:S(2)}, u32[]{:S(2)}) %collective-permute-start.5) | collective-permute-done | bytes 327712 | tf_op jit(solution)/shard_map/ppermute | solution.py:344
  49.6 1.6 %collective-permute-start.11 = (bf16[2,32,1280]{2,1,0:T(8,128)(2,1)S(1)}, bf16[2,32,1280]{2,1,0:T(8,128)(2,1)S(1)}, u32[]{:S(2)}, u32[]{:S(2)}) collective-permute-start(bf16[2,32,1280]{2,1,0:T(8,128)(2,1)S(1)} %get-tuple-element.50), channel_id=1, source_target_pairs={{0,1},{1,0},{2,3},{3,2},{4,5},{5,4},{6,7},{7,6},{8,9},{9,8},{10,11... | collective-permute-start | bytes 491528 | tf_op jit(solution)/shard_map/ppermute | solution.py:355
  52.0 3.4 %collective-permute-done.11.refs_6_ = bf16[2,32,1280]{2,1,0:T(8,128)(2,1)S(1)} collective-permute-done((bf16[2,32,1280]{2,1,0:T(8,128)(2,1)S(1)}, bf16[2,32,1280]{2,1,0:T(8,128)(2,1)S(1)}, u32[]{:S(2)}, u32[]{:S(2)}) %collective-permute-start.11) | collective-permute-done | bytes 163872 | tf_op jit(solution)/shard_map/ppermute | solution.py:355
  57.9 1.7 %collective-permute-done.16.refs_1_ = bf16[2,2,192,768]{3,2,1,0:T(8,128)(2,1)S(1)} collective-permute-done((bf16[2,2,192,768]{3,2,1,0:T(8,128)(2,1)S(1)}, bf16[2,2,192,768]{3,2,1,0:T(8,128)(2,1)S(1)}, u32[]{:S(2)}, u32[]{:S(2)}) %collective-permute-start.16) | collective-permute-done | bytes 1179680 | tf_op jit(solution)/shard_map/ppermute | solution.py:447
  59.7 1.6 %collective-permute-start.21 = (bf16[2,192,768]{2,1,0:T(8,128)(2,1)S(1)}, bf16[2,192,768]{2,1,0:T(8,128)(2,1)S(1)}, u32[]{:S(2)}, u32[]{:S(2)}) collective-permute-start(bf16[2,192,768]{2,1,0:T(8,128)(2,1)S(1)} %shard_map.89.refs_2_), channel_id=1, source_target_pairs={{0,16},{8,24},{16,0},{24,8},{1,17},{9,25},{17,1},{25,9},{2,18},{10... | collective-permute-start | bytes 1769480 | tf_op jit(solution)/shard_map/ppermute | solution.py:458
  62.4 2.2 %shard_map.91 = (bf16[8,2,32,768]{3,2,1,0:T(8,128)(2,1)}, f32[2,256]{1,0:T(2,128)S(1)}) custom-call(bf16[2,768,2048]{2,1,0:T(8,128)(2,1)S(1)} %copy-done, bf16[2,32,1280]{2,1,0:T(8,128)(2,1)S(1)} %get-tuple-element.38.refs_3_.refs_1_, bf16[2,64,1280]{2,1,0:T(8,128)(2,1)S(1)} %get-tuple-element.39.refs_5_.refs_2_, ...), custom_call_target="tpu_custom_call" | custom-call | flops 1 | bytes 1 | tf_op jit(solution)/shard_map/pallas_call | solution.py:43
  66.1 2.1 %collective-permute-done.17 = f32[2,256]{1,0:T(2,128)S(1)} collective-permute-done((f32[2,256]{1,0:T(2,128)S(1)}, f32[2,256]{1,0:T(2,128)S(1)}, u32[]{:S(2)}, u32[]{:S(2)}) %collective-permute-start.17) | collective-permute-done | bytes 2080 | tf_op jit(solution)/shard_map/ppermute | solution.py:499
  68.2 2.3 %collective-permute-start.18 = (f32[2,2,256]{2,1,0:T(2,128)S(1)}, f32[2,2,256]{2,1,0:T(2,128)S(1)}, u32[]{:S(2)}, u32[]{:S(2)}) collective-permute-start(f32[2,2,256]{2,1,0:T(2,128)S(1)} %pad_maximum_fusion.refs_2_), channel_id=1, source_target_pairs={{2,0},{3,1},{4,2},{5,3},{6,4},{7,5},{0,6},{1,7},{10,8},{11,9},{12,... | collective-permute-start | bytes 12296 | tf_op jit(solution)/shard_map/ppermute | solution.py:501
  73.0 2.9 %collective-permute-done.21.refs_2_ = bf16[2,192,768]{2,1,0:T(8,128)(2,1)S(1)} collective-permute-done((bf16[2,192,768]{2,1,0:T(8,128)(2,1)S(1)}, bf16[2,192,768]{2,1,0:T(8,128)(2,1)S(1)}, u32[]{:S(2)}, u32[]{:S(2)}) %collective-permute-start.21) | collective-permute-done | bytes 589856 | tf_op jit(solution)/shard_map/ppermute | solution.py:458
  78.5 5.1 %collective-permute-done.22.refs_2_ = bf16[2,192,512]{2,1,0:T(8,128)(2,1)S(1)} collective-permute-done((bf16[2,192,512]{2,1,0:T(8,128)(2,1)S(1)}, bf16[2,192,512]{2,1,0:T(8,128)(2,1)S(1)}, u32[]{:S(2)}, u32[]{:S(2)}) %collective-permute-start.22) | collective-permute-done | bytes 393248 | tf_op jit(solution)/shard_map/ppermute | solution.py:458
  83.6 1.7 %shard_map.95 = (f32[192,2,2048]{2,1,0:T(2,128)}, f32[8,128]{1,0:T(8,128)}) custom-call(bf16[2,2,192,512]{3,2,1,0:T(8,128)(2,1)S(1)} %get-tuple-element.54.refs_2_.refs_0_, bf16[2,2,192,512]{3,2,1,0:T(8,128)(2,1)S(1)} %collective-permute-done.15.refs_1_, bf16[2,192,512]{2,1,0:T(8,128)(2,1)S(1)} %collective-permute-done.22.refs_2_, ...), custom_call_target="tpu_custom_call", output_to_operand_aliasing={{0}: (3, {})} | custom-call | flops 1 | bytes 1 | tf_op jit(solution)/shard_map/pallas_call | solution.py:43
  (55 shorter events, 17.6 us)
Async XLA Ops:
  0.6 19.4 %copy-start.1 = (bf16[1,8,2,32,768]{4,3,2,1,0:T(8,128)(2,1)S(1)}, bf16[1,8,2,32,768]{4,3,2,1,0:T(8,128)(2,1)}, u32[]{:S(2)}) copy-start(bf16[1,8,2,32,768]{4,3,2,1,0:T(8,128)(2,1)} %param.8) | copy-start | bytes 2359300
  2.5 11.6 %collective-permute-start = (bf16[144,768]{1,0:T(8,128)(2,1)}, bf16[144,768]{1,0:T(8,128)(2,1)S(1)}, u32[]{:S(2)}, u32[]{:S(2)}) collective-permute-start(bf16[144,768]{1,0:T(8,128)(2,1)} %get-tuple-element.35.refs_0_), channel_id=1, source_target_pairs={{0,2},{1,3},{2,4},{3,5},{4,6},{5,7},{6,0},{7,1},{8,10},{9,11},{10,... | collective-permute-start | bytes 663560 | tf_op jit(solution)/shard_map/ppermute | solution.py:344
  5.6 14.7 %collective-permute-start.1 = (bf16[144,768]{1,0:T(8,128)(2,1)}, bf16[144,768]{1,0:T(8,128)(2,1)S(1)}, u32[]{:S(2)}, u32[]{:S(2)}) collective-permute-start(bf16[144,768]{1,0:T(8,128)(2,1)} %get-tuple-element.35.refs_0_), channel_id=1, source_target_pairs={{0,6},{1,7},{2,0},{3,1},{4,2},{5,3},{6,4},{7,5},{8,14},{9,15},{10,... | collective-permute-start | bytes 663560 | tf_op jit(solution)/shard_map/ppermute | solution.py:344
  14.1 11.1 %collective-permute-start.2 = (bf16[144,768]{1,0:T(8,128)(2,1)S(1)}, bf16[144,768]{1,0:T(8,128)(2,1)S(1)}, u32[]{:S(2)}, u32[]{:S(2)}) collective-permute-start(bf16[144,768]{1,0:T(8,128)(2,1)S(1)} %collective-permute-done.refs_1_), channel_id=1, source_target_pairs={{0,2},{1,3},{2,4},{3,5},{4,6},{5,7},{6,0},{7,1},{8,10},{9,11},{10,... | collective-permute-start | bytes 663560 | tf_op jit(solution)/shard_map/ppermute | solution.py:344
  15.3 16.9 %collective-permute-start.3 = (bf16[128,1280]{1,0:T(8,128)(2,1)S(1)}, bf16[128,1280]{1,0:T(8,128)(2,1)S(1)}, u32[]{:S(2)}, u32[]{:S(2)}) collective-permute-start(bf16[128,1280]{1,0:T(8,128)(2,1)S(1)} %shard_map.77.refs_1_.refs_0_), channel_id=1, source_target_pairs={{0,2},{1,3},{2,4},{3,5},{4,6},{5,7},{6,0},{7,1},{8,10},{9,11},{10,... | collective-permute-start | bytes 983048 | tf_op jit(solution)/shard_map/ppermute | solution.py:344
  19.4 16.9 %collective-permute-start.4 = (bf16[128,1280]{1,0:T(8,128)(2,1)S(1)}, bf16[128,1280]{1,0:T(8,128)(2,1)S(1)}, u32[]{:S(2)}, u32[]{:S(2)}) collective-permute-start(bf16[128,1280]{1,0:T(8,128)(2,1)S(1)} %shard_map.77.refs_1_.refs_0_), channel_id=1, source_target_pairs={{0,6},{1,7},{2,0},{3,1},{4,2},{5,3},{6,4},{7,5},{8,14},{9,15},{10,... | collective-permute-start | bytes 983048 | tf_op jit(solution)/shard_map/ppermute | solution.py:344
  20.6 15.9 %collective-permute-start.6 = (bf16[2,96,768]{2,1,0:T(8,128)(2,1)S(1)}, bf16[2,96,768]{2,1,0:T(8,128)(2,1)S(1)}, u32[]{:S(2)}, u32[]{:S(2)}) collective-permute-start(bf16[2,96,768]{2,1,0:T(8,128)(2,1)S(1)} %get-tuple-element.42), channel_id=1, source_target_pairs={{0,1},{1,0},{2,3},{3,2},{4,5},{5,4},{6,7},{7,6},{8,9},{9,8},{10,11... | collective-permute-start | bytes 884744 | tf_op jit(solution)/shard_map/ppermute | solution.py:355
  25.7 10.9 %collective-permute-start.8 = (bf16[2,32,1280]{2,1,0:T(8,128)(2,1)S(1)}, bf16[2,32,1280]{2,1,0:T(8,128)(2,1)S(1)}, u32[]{:S(2)}, u32[]{:S(2)}) collective-permute-start(bf16[2,32,1280]{2,1,0:T(8,128)(2,1)S(1)} %get-tuple-element.44), channel_id=1, source_target_pairs={{0,1},{1,0},{2,3},{3,2},{4,5},{5,4},{6,7},{7,6},{8,9},{9,8},{10,11... | collective-permute-start | bytes 491528 | tf_op jit(solution)/shard_map/ppermute | solution.py:355
  27.2 9.3 %collective-permute-start.7 = (bf16[2,32,768]{2,1,0:T(8,128)(2,1)S(1)}, bf16[2,32,768]{2,1,0:T(8,128)(2,1)S(1)}, u32[]{:S(2)}, u32[]{:S(2)}) collective-permute-start(bf16[2,32,768]{2,1,0:T(8,128)(2,1)S(1)} %get-tuple-element.43), channel_id=1, source_target_pairs={{0,1},{1,0},{2,3},{3,2},{4,5},{5,4},{6,7},{7,6},{8,9},{9,8},{10,11... | collective-permute-start | bytes 294920 | tf_op jit(solution)/shard_map/ppermute | solution.py:355
  37.4 2.9 %collective-permute-start.9 = (bf16[2,2,192,768]{3,2,1,0:T(8,128)(2,1)S(1)}, bf16[2,2,192,768]{3,2,1,0:T(8,128)(2,1)S(1)}, u32[]{:S(2)}, u32[]{:S(2)}) collective-permute-start(bf16[2,2,192,768]{3,2,1,0:T(8,128)(2,1)S(1)} %get-tuple-element.46), channel_id=1, source_target_pairs={{0,8},{8,0},{16,24},{24,16},{1,9},{9,1},{17,25},{25,17},{2,10},{10... | collective-permute-start | bytes 3538952 | tf_op jit(solution)/shard_map/ppermute | solution.py:447
  37.5 11.9 %collective-permute-start.5 = (bf16[128,1280]{1,0:T(8,128)(2,1)S(1)}, bf16[128,1280]{1,0:T(8,128)(2,1)S(1)}, u32[]{:S(2)}, u32[]{:S(2)}) collective-permute-start(bf16[128,1280]{1,0:T(8,128)(2,1)S(1)} %collective-permute-done.3.refs_0_), channel_id=1, source_target_pairs={{0,2},{1,3},{2,4},{3,5},{4,6},{5,7},{6,0},{7,1},{8,10},{9,11},{10,... | collective-permute-start | bytes 983048 | tf_op jit(solution)/shard_map/ppermute | solution.py:344
  38.6 13.3 %collective-permute-start.10 = (bf16[2,64,1280]{2,1,0:T(8,128)(2,1)S(1)}, bf16[2,64,1280]{2,1,0:T(8,128)(2,1)S(1)}, u32[]{:S(2)}, u32[]{:S(2)}) collective-permute-start(bf16[2,64,1280]{2,1,0:T(8,128)(2,1)S(1)} %get-tuple-element.49), channel_id=1, source_target_pairs={{0,1},{1,0},{2,3},{3,2},{4,5},{5,4},{6,7},{7,6},{8,9},{9,8},{10,11... | collective-permute-start | bytes 983048 | tf_op jit(solution)/shard_map/ppermute | solution.py:355
  40.5 15.0 %collective-permute-start.12 = (bf16[2,64,768]{2,1,0:T(8,128)(2,1)S(1)}, bf16[2,64,768]{2,1,0:T(8,128)(2,1)S(1)}, u32[]{:S(2)}, u32[]{:S(2)}) collective-permute-start(bf16[2,64,768]{2,1,0:T(8,128)(2,1)S(1)} %get-tuple-element.47.refs_2_), channel_id=1, source_target_pairs={{0,16},{8,24},{16,0},{24,8},{1,17},{9,25},{17,1},{25,9},{2,18},{10... | collective-permute-start | bytes 589832 | tf_op jit(solution)/shard_map/ppermute | solution.py:458
  42.1 13.4 %collective-permute-start.13 = (bf16[2,64,768]{2,1,0:T(8,128)(2,1)S(1)}, bf16[2,64,768]{2,1,0:T(8,128)(2,1)S(1)}, u32[]{:S(2)}, u32[]{:S(2)}) collective-permute-start(bf16[2,64,768]{2,1,0:T(8,128)(2,1)S(1)} %get-tuple-element.51), channel_id=1, source_target_pairs={{0,16},{8,24},{16,0},{24,8},{1,17},{9,25},{17,1},{25,9},{2,18},{10... | collective-permute-start | bytes 589832 | tf_op jit(solution)/shard_map/ppermute | solution.py:458
  42.5 13.3 %collective-permute-start.14 = (bf16[2,64,768]{2,1,0:T(8,128)(2,1)S(1)}, bf16[2,64,768]{2,1,0:T(8,128)(2,1)S(1)}, u32[]{:S(2)}, u32[]{:S(2)}) collective-permute-start(bf16[2,64,768]{2,1,0:T(8,128)(2,1)S(1)} %get-tuple-element.52), channel_id=1, source_target_pairs={{0,16},{8,24},{16,0},{24,8},{1,17},{9,25},{17,1},{25,9},{2,18},{10... | collective-permute-start | bytes 589832 | tf_op jit(solution)/shard_map/ppermute | solution.py:458
  49.6 5.8 %collective-permute-start.11 = (bf16[2,32,1280]{2,1,0:T(8,128)(2,1)S(1)}, bf16[2,32,1280]{2,1,0:T(8,128)(2,1)S(1)}, u32[]{:S(2)}, u32[]{:S(2)}) collective-permute-start(bf16[2,32,1280]{2,1,0:T(8,128)(2,1)S(1)} %get-tuple-element.50), channel_id=1, source_target_pairs={{0,1},{1,0},{2,3},{3,2},{4,5},{5,4},{6,7},{7,6},{8,9},{9,8},{10,11... | collective-permute-start | bytes 491528 | tf_op jit(solution)/shard_map/ppermute | solution.py:355
  56.7 2.9 %collective-permute-start.16 = (bf16[2,2,192,768]{3,2,1,0:T(8,128)(2,1)S(1)}, bf16[2,2,192,768]{3,2,1,0:T(8,128)(2,1)S(1)}, u32[]{:S(2)}, u32[]{:S(2)}) collective-permute-start(bf16[2,2,192,768]{3,2,1,0:T(8,128)(2,1)S(1)} %get-tuple-element.56), channel_id=1, source_target_pairs={{0,8},{8,0},{16,24},{24,16},{1,9},{9,1},{17,25},{25,17},{2,10},{10... | collective-permute-start | bytes 3538952 | tf_op jit(solution)/shard_map/ppermute | solution.py:447
  57.3 4.0 %collective-permute-start.15 = (bf16[2,2,192,512]{3,2,1,0:T(8,128)(2,1)S(1)}, bf16[2,2,192,512]{3,2,1,0:T(8,128)(2,1)S(1)}, u32[]{:S(2)}, u32[]{:S(2)}) collective-permute-start(bf16[2,2,192,512]{3,2,1,0:T(8,128)(2,1)S(1)} %get-tuple-element.55), channel_id=1, source_target_pairs={{0,8},{8,0},{16,24},{24,16},{1,9},{9,1},{17,25},{25,17},{2,10},{10... | collective-permute-start | bytes 2359304 | tf_op jit(solution)/shard_map/ppermute | solution.py:447
  59.7 16.2 %collective-permute-start.21 = (bf16[2,192,768]{2,1,0:T(8,128)(2,1)S(1)}, bf16[2,192,768]{2,1,0:T(8,128)(2,1)S(1)}, u32[]{:S(2)}, u32[]{:S(2)}) collective-permute-start(bf16[2,192,768]{2,1,0:T(8,128)(2,1)S(1)} %shard_map.89.refs_2_), channel_id=1, source_target_pairs={{0,16},{8,24},{16,0},{24,8},{1,17},{9,25},{17,1},{25,9},{2,18},{10... | collective-permute-start | bytes 1769480 | tf_op jit(solution)/shard_map/ppermute | solution.py:458
  61.4 22.2 %collective-permute-start.22 = (bf16[2,192,512]{2,1,0:T(8,128)(2,1)S(1)}, bf16[2,192,512]{2,1,0:T(8,128)(2,1)S(1)}, u32[]{:S(2)}, u32[]{:S(2)}) collective-permute-start(bf16[2,192,512]{2,1,0:T(8,128)(2,1)S(1)} %shard_map.90.refs_9_), channel_id=1, source_target_pairs={{0,16},{8,24},{16,0},{24,8},{1,17},{9,25},{17,1},{25,9},{2,18},{10... | collective-permute-start | bytes 1179656 | tf_op jit(solution)/shard_map/ppermute | solution.py:458
  64.6 3.6 %collective-permute-start.17 = (f32[2,256]{1,0:T(2,128)S(1)}, f32[2,256]{1,0:T(2,128)S(1)}, u32[]{:S(2)}, u32[]{:S(2)}) collective-permute-start(f32[2,256]{1,0:T(2,128)S(1)} %get-tuple-element.59.refs_5_), channel_id=1, source_target_pairs={{0,1},{1,0},{2,3},{3,2},{4,5},{5,4},{6,7},{7,6},{8,9},{9,8},{10,11... | collective-permute-start | bytes 6152 | tf_op jit(solution)/shard_map/ppermute | solution.py:499
  68.2 9.2 %collective-permute-start.18 = (f32[2,2,256]{2,1,0:T(2,128)S(1)}, f32[2,2,256]{2,1,0:T(2,128)S(1)}, u32[]{:S(2)}, u32[]{:S(2)}) collective-permute-start(f32[2,2,256]{2,1,0:T(2,128)S(1)} %pad_maximum_fusion.refs_2_), channel_id=1, source_target_pairs={{2,0},{3,1},{4,2},{5,3},{6,4},{7,5},{0,6},{1,7},{10,8},{11,9},{12,... | collective-permute-start | bytes 12296 | tf_op jit(solution)/shard_map/ppermute | solution.py:501
  70.5 6.9 %collective-permute-start.19 = (f32[2,2,256]{2,1,0:T(2,128)S(1)}, f32[2,2,256]{2,1,0:T(2,128)S(1)}, u32[]{:S(2)}, u32[]{:S(2)}) collective-permute-start(f32[2,2,256]{2,1,0:T(2,128)S(1)} %pad_maximum_fusion.refs_2_), channel_id=1, source_target_pairs={{4,0},{5,1},{6,2},{7,3},{0,4},{1,5},{2,6},{3,7},{12,8},{13,9},{14,... | collective-permute-start | bytes 12296 | tf_op jit(solution)/shard_map/ppermute | solution.py:501
  70.8 6.7 %collective-permute-start.20 = (f32[2,2,256]{2,1,0:T(2,128)S(1)}, f32[2,2,256]{2,1,0:T(2,128)S(1)}, u32[]{:S(2)}, u32[]{:S(2)}) collective-permute-start(f32[2,2,256]{2,1,0:T(2,128)S(1)} %pad_maximum_fusion.refs_2_), channel_id=1, source_target_pairs={{6,0},{7,1},{0,2},{1,3},{2,4},{3,5},{4,6},{5,7},{14,8},{15,9},{8,1... | collective-permute-start | bytes 12296 | tf_op jit(solution)/shard_map/ppermute | solution.py:501
  (5 other events, 24.0 us)

commit v18 on v17

--- a/solution.py
+++ b/solution.py
@@ -291,7 +291,7 @@
 
 def chunks_of(features):
     unit = features // 16
-    return [[6 * unit], [6 * unit, 4 * unit]]
+    return [[6 * unit], [3 * unit, 7 * unit]]
 
 
 def cuts_of(share, first):

time: 85.5 us -> 90.1 us (1.054)
  waiting for transfers between devices: 39.2 us -> 44 us
    ppermute x5, waiting for transfers between devices: 8.48 us -> 11.6 us  [paired(): others.append(lax.ppermute(pair, 'dp', shift))]
    ppermute x3, waiting for transfers between devices: 1.85 us -> 3.63 us  [termed(): got = lax.ppermute(give, 'dp', [(i, i ^ 1) for i in range(dp)])]
  transfers between devices with their start and end apart: 23 -> 23, of which waited for: 12 -> 11; matrix products, arithmetic and copies ran while one was open for 0% -> 0% of each run, Pallas kernels for 11% -> 9%
where the time goes in v18:
time: 90.1 us; the launch traced here: 89.9 us
  waiting for transfers between devices  44 us (49%)
  starting transfers between devices  29 us (32%)
  Pallas kernels  14.9 us (17%)
  local copies, waits for them, and re-layouts  1.06 us (1%)
    ppermute x6, waiting for transfers between devices, along(): return lax.ppermute(block, 'expert', pairs)  23.3 us
    pallas_call x20, Pallas kernels, __call__(): pl.pallas_call(body, out_shape=outs, in_specs=in_specs, compiler_params=p...  14.9 us
    ppermute x5, waiting for transfers between devices, paired(): others.append(lax.ppermute(pair, 'dp', shift))  11.6 us
    ppermute x6, starting transfers between devices, along(): return lax.ppermute(block, 'expert', pairs)  11.1 us
    ppermute x5, starting transfers between devices, pick(): lax.ppermute(other, 'expert', [(i, i ^ 1) for i in range(LINE * SIDES)])  6.69 us
    ppermute x5, starting transfers between devices, paired(): others.append(lax.ppermute(pair, 'dp', shift))  5.72 us
    ppermute x3, waiting for transfers between devices, termed(): got = lax.ppermute(give, 'dp', [(i, i ^ 1) for i in range(dp)])  3.63 us
    ppermute x5, waiting for transfers between devices, pick(): lax.ppermute(other, 'expert', [(i, i ^ 1) for i in range(LINE * SIDES)])  3.46 us
  transfers between devices with their start and end apart: 23, of which 11 were waited for; matrix products, arithmetic and copies ran while one was open for 0% of the time, Pallas kernels for 9%

profile of v18, /device:TPU:0, one launch (start us, length us, event | category | flops | bytes accessed | tf_op | source)
XLA Modules:
  0.0 89.9 jit_solution(12543112876041344809)
XLA Ops:
  0.6 1.9 %shard_map.76 = (s32[2,128]{1,0:T(2,128)}, bf16[144,768]{1,0:T(8,128)(2,1)}) custom-call(s32[2,128]{1,0:T(2,128)} %bitcast.13, f32[2,128]{1,0:T(2,128)} %bitcast.10, bf16[128,2048]{1,0:T(8,128)(2,1)} %refs_0_.3), custom_call_target="tpu_custom_call" | custom-call | flops 1 | bytes 1 | tf_op jit(solution)/shard_map/pallas_call | solution.py:43
  2.5 3.1 %collective-permute-start = (bf16[144,768]{1,0:T(8,128)(2,1)}, bf16[144,768]{1,0:T(8,128)(2,1)S(1)}, u32[]{:S(2)}, u32[]{:S(2)}) collective-permute-start(bf16[144,768]{1,0:T(8,128)(2,1)} %get-tuple-element.35.refs_0_), channel_id=1, source_target_pairs={{0,2},{1,3},{2,4},{3,5},{4,6},{5,7},{6,0},{7,1},{8,10},{9,11},{10,... | collective-permute-start | bytes 663560 | tf_op jit(solution)/shard_map/ppermute | solution.py:344
  5.6 2.1 %collective-permute-start.1 = (bf16[144,768]{1,0:T(8,128)(2,1)}, bf16[144,768]{1,0:T(8,128)(2,1)S(1)}, u32[]{:S(2)}, u32[]{:S(2)}) collective-permute-start(bf16[144,768]{1,0:T(8,128)(2,1)} %get-tuple-element.35.refs_0_), channel_id=1, source_target_pairs={{0,6},{1,7},{2,0},{3,1},{4,2},{5,3},{6,4},{7,5},{8,14},{9,15},{10,... | collective-permute-start | bytes 663560 | tf_op jit(solution)/shard_map/ppermute | solution.py:344
  7.7 6.4 %collective-permute-done.refs_1_ = bf16[144,768]{1,0:T(8,128)(2,1)S(1)} collective-permute-done((bf16[144,768]{1,0:T(8,128)(2,1)}, bf16[144,768]{1,0:T(8,128)(2,1)S(1)}, u32[]{:S(2)}, u32[]{:S(2)}) %collective-permute-start) | collective-permute-done | bytes 221216 | tf_op jit(solution)/shard_map/ppermute | solution.py:344
  15.2 4.1 %collective-permute-start.3 = (bf16[128,1280]{1,0:T(8,128)(2,1)S(1)}, bf16[128,1280]{1,0:T(8,128)(2,1)S(1)}, u32[]{:S(2)}, u32[]{:S(2)}) collective-permute-start(bf16[128,1280]{1,0:T(8,128)(2,1)S(1)} %shard_map.77.refs_1_.refs_0_), channel_id=1, source_target_pairs={{0,2},{1,3},{2,4},{3,5},{4,6},{5,7},{6,0},{7,1},{8,10},{9,11},{10,... | collective-permute-start | bytes 983048 | tf_op jit(solution)/shard_map/ppermute | solution.py:344
  20.6 1.6 %collective-permute-start.6 = (bf16[2,96,768]{2,1,0:T(8,128)(2,1)S(1)}, bf16[2,96,768]{2,1,0:T(8,128)(2,1)S(1)}, u32[]{:S(2)}, u32[]{:S(2)}) collective-permute-start(bf16[2,96,768]{2,1,0:T(8,128)(2,1)S(1)} %get-tuple-element.42), channel_id=1, source_target_pairs={{0,1},{1,0},{2,3},{3,2},{4,5},{5,4},{6,7},{7,6},{8,9},{9,8},{10,11... | collective-permute-start | bytes 884744 | tf_op jit(solution)/shard_map/ppermute | solution.py:355
  22.2 3.1 %collective-permute-done.2.refs_0_ = bf16[144,768]{1,0:T(8,128)(2,1)S(1)} collective-permute-done((bf16[144,768]{1,0:T(8,128)(2,1)S(1)}, bf16[144,768]{1,0:T(8,128)(2,1)S(1)}, u32[]{:S(2)}, u32[]{:S(2)}) %collective-permute-start.2) | collective-permute-done | bytes 221216 | tf_op jit(solution)/shard_map/ppermute | solution.py:344
  25.7 1.6 %collective-permute-start.8 = (bf16[2,32,1280]{2,1,0:T(8,128)(2,1)S(1)}, bf16[2,32,1280]{2,1,0:T(8,128)(2,1)S(1)}, u32[]{:S(2)}, u32[]{:S(2)}) collective-permute-start(bf16[2,32,1280]{2,1,0:T(8,128)(2,1)S(1)} %get-tuple-element.44), channel_id=1, source_target_pairs={{0,1},{1,0},{2,3},{3,2},{4,5},{5,4},{6,7},{7,6},{8,9},{9,8},{10,11... | collective-permute-start | bytes 491528 | tf_op jit(solution)/shard_map/ppermute | solution.py:355
  27.8 4.4 %collective-permute-done.3.refs_0_ = bf16[128,1280]{1,0:T(8,128)(2,1)S(1)} collective-permute-done((bf16[128,1280]{1,0:T(8,128)(2,1)S(1)}, bf16[128,1280]{1,0:T(8,128)(2,1)S(1)}, u32[]{:S(2)}, u32[]{:S(2)}) %collective-permute-start.3) | collective-permute-done | bytes 327712 | tf_op jit(solution)/shard_map/ppermute | solution.py:344
  32.2 4.1 %collective-permute-done.4.refs_1_ = bf16[128,1280]{1,0:T(8,128)(2,1)S(1)} collective-permute-done((bf16[128,1280]{1,0:T(8,128)(2,1)S(1)}, bf16[128,1280]{1,0:T(8,128)(2,1)S(1)}, u32[]{:S(2)}, u32[]{:S(2)}) %collective-permute-start.4) | collective-permute-done | bytes 327712 | tf_op jit(solution)/shard_map/ppermute | solution.py:344
  38.6 1.5 %collective-permute-start.10 = (bf16[2,64,1280]{2,1,0:T(8,128)(2,1)S(1)}, bf16[2,64,1280]{2,1,0:T(8,128)(2,1)S(1)}, u32[]{:S(2)}, u32[]{:S(2)}) collective-permute-start(bf16[2,64,1280]{2,1,0:T(8,128)(2,1)S(1)} %get-tuple-element.49), channel_id=1, source_target_pairs={{0,1},{1,0},{2,3},{3,2},{4,5},{5,4},{6,7},{7,6},{8,9},{9,8},{10,11... | collective-permute-start | bytes 983048 | tf_op jit(solution)/shard_map/ppermute | solution.py:355
  40.4 1.6 %collective-permute-start.12 = (bf16[2,64,768]{2,1,0:T(8,128)(2,1)S(1)}, bf16[2,64,768]{2,1,0:T(8,128)(2,1)S(1)}, u32[]{:S(2)}, u32[]{:S(2)}) collective-permute-start(bf16[2,64,768]{2,1,0:T(8,128)(2,1)S(1)} %get-tuple-element.47.refs_2_), channel_id=1, source_target_pairs={{0,16},{8,24},{16,0},{24,8},{1,17},{9,25},{17,1},{25,9},{2,18},{10... | collective-permute-start | bytes 589832 | tf_op jit(solution)/shard_map/ppermute | solution.py:458
  42.5 1.5 %collective-permute-start.14 = (bf16[2,64,768]{2,1,0:T(8,128)(2,1)S(1)}, bf16[2,64,768]{2,1,0:T(8,128)(2,1)S(1)}, u32[]{:S(2)}, u32[]{:S(2)}) collective-permute-start(bf16[2,64,768]{2,1,0:T(8,128)(2,1)S(1)} %get-tuple-element.52), channel_id=1, source_target_pairs={{0,16},{8,24},{16,0},{24,8},{1,17},{9,25},{17,1},{25,9},{2,18},{10... | collective-permute-start | bytes 589832 | tf_op jit(solution)/shard_map/ppermute | solution.py:458
  44.1 5.3 %collective-permute-done.5.refs_0_ = bf16[128,1280]{1,0:T(8,128)(2,1)S(1)} collective-permute-done((bf16[128,1280]{1,0:T(8,128)(2,1)S(1)}, bf16[128,1280]{1,0:T(8,128)(2,1)S(1)}, u32[]{:S(2)}, u32[]{:S(2)}) %collective-permute-start.5) | collective-permute-done | bytes 327712 | tf_op jit(solution)/shard_map/ppermute | solution.py:344
  49.6 1.6 %collective-permute-start.11 = (bf16[2,32,1280]{2,1,0:T(8,128)(2,1)S(1)}, bf16[2,32,1280]{2,1,0:T(8,128)(2,1)S(1)}, u32[]{:S(2)}, u32[]{:S(2)}) collective-permute-start(bf16[2,32,1280]{2,1,0:T(8,128)(2,1)S(1)} %get-tuple-element.50), channel_id=1, source_target_pairs={{0,1},{1,0},{2,3},{3,2},{4,5},{5,4},{6,7},{7,6},{8,9},{9,8},{10,11... | collective-permute-start | bytes 491528 | tf_op jit(solution)/shard_map/ppermute | solution.py:355
  52.0 3.4 %collective-permute-done.11.refs_6_ = bf16[2,32,1280]{2,1,0:T(8,128)(2,1)S(1)} collective-permute-done((bf16[2,32,1280]{2,1,0:T(8,128)(2,1)S(1)}, bf16[2,32,1280]{2,1,0:T(8,128)(2,1)S(1)}, u32[]{:S(2)}, u32[]{:S(2)}) %collective-permute-start.11) | collective-permute-done | bytes 163872 | tf_op jit(solution)/shard_map/ppermute | solution.py:355
  58.0 3.5 %collective-permute-done.16.refs_1_ = bf16[2,2,192,384]{3,2,1,0:T(8,128)(2,1)S(1)} collective-permute-done((bf16[2,2,192,384]{3,2,1,0:T(8,128)(2,1)S(1)}, bf16[2,2,192,384]{3,2,1,0:T(8,128)(2,1)S(1)}, u32[]{:S(2)}, u32[]{:S(2)}) %collective-permute-start.16) | collective-permute-done | bytes 589856 | tf_op jit(solution)/shard_map/ppermute | solution.py:447
  61.8 1.6 %collective-permute-start.22 = (bf16[2,192,896]{2,1,0:T(8,128)(2,1)S(1)}, bf16[2,192,896]{2,1,0:T(8,128)(2,1)S(1)}, u32[]{:S(2)}, u32[]{:S(2)}) collective-permute-start(bf16[2,192,896]{2,1,0:T(8,128)(2,1)S(1)} %shard_map.90.refs_9_), channel_id=1, source_target_pairs={{0,16},{8,24},{16,0},{24,8},{1,17},{9,25},{17,1},{25,9},{2,18},{10... | collective-permute-start | bytes 2064392 | tf_op jit(solution)/shard_map/ppermute | solution.py:458
  63.8 2.2 %shard_map.91 = (bf16[8,2,32,768]{3,2,1,0:T(8,128)(2,1)}, f32[2,256]{1,0:T(2,128)S(1)}) custom-call(bf16[2,768,2048]{2,1,0:T(8,128)(2,1)S(1)} %copy-done, bf16[2,32,1280]{2,1,0:T(8,128)(2,1)S(1)} %get-tuple-element.38.refs_3_.refs_1_, bf16[2,64,1280]{2,1,0:T(8,128)(2,1)S(1)} %get-tuple-element.39.refs_5_.refs_2_, ...), custom_call_target="tpu_custom_call" | custom-call | flops 1 | bytes 1 | tf_op jit(solution)/shard_map/pallas_call | solution.py:43
  66.0 1.5 %collective-permute-start.17 = (f32[2,256]{1,0:T(2,128)S(1)}, f32[2,256]{1,0:T(2,128)S(1)}, u32[]{:S(2)}, u32[]{:S(2)}) collective-permute-start(f32[2,256]{1,0:T(2,128)S(1)} %get-tuple-element.59.refs_5_), channel_id=1, source_target_pairs={{0,1},{1,0},{2,3},{3,2},{4,5},{5,4},{6,7},{7,6},{8,9},{9,8},{10,11... | collective-permute-start | bytes 6152 | tf_op jit(solution)/shard_map/ppermute | solution.py:499
  67.5 2.1 %collective-permute-done.17 = f32[2,256]{1,0:T(2,128)S(1)} collective-permute-done((f32[2,256]{1,0:T(2,128)S(1)}, f32[2,256]{1,0:T(2,128)S(1)}, u32[]{:S(2)}, u32[]{:S(2)}) %collective-permute-start.17) | collective-permute-done | bytes 2080 | tf_op jit(solution)/shard_map/ppermute | solution.py:499
  69.6 2.3 %collective-permute-start.18 = (f32[2,2,256]{2,1,0:T(2,128)S(1)}, f32[2,2,256]{2,1,0:T(2,128)S(1)}, u32[]{:S(2)}, u32[]{:S(2)}) collective-permute-start(f32[2,2,256]{2,1,0:T(2,128)S(1)} %pad_maximum_fusion.refs_2_), channel_id=1, source_target_pairs={{2,0},{3,1},{4,2},{5,3},{6,4},{7,5},{0,6},{1,7},{10,8},{11,9},{12,... | collective-permute-start | bytes 12296 | tf_op jit(solution)/shard_map/ppermute | solution.py:501
  74.5 11.1 %collective-permute-done.21.refs_2_ = bf16[2,192,384]{2,1,0:T(8,128)(2,1)S(1)} collective-permute-done((bf16[2,192,384]{2,1,0:T(8,128)(2,1)S(1)}, bf16[2,192,384]{2,1,0:T(8,128)(2,1)S(1)}, u32[]{:S(2)}, u32[]{:S(2)}) %collective-permute-start.21) | collective-permute-done | bytes 294944 | tf_op jit(solution)/shard_map/ppermute | solution.py:458
  87.7 2.1 %shard_map.95 = (f32[192,2,2048]{2,1,0:T(2,128)}, f32[8,128]{1,0:T(8,128)}) custom-call(bf16[2,2,192,896]{3,2,1,0:T(8,128)(2,1)S(1)} %get-tuple-element.54.refs_2_.refs_0_, bf16[2,2,192,896]{3,2,1,0:T(8,128)(2,1)S(1)} %collective-permute-done.15.refs_1_, bf16[2,192,896]{2,1,0:T(8,128)(2,1)S(1)} %collective-permute-done.22.refs_2_, ...), custom_call_target="tpu_custom_call", output_to_operand_aliasing={{0}: (3, {})} | custom-call | flops 1 | bytes 1 | tf_op jit(solution)/shard_map/pallas_call | solution.py:43
  (55 shorter events, 15.4 us)
Async XLA Ops:
  0.6 19.4 %copy-start.1 = (bf16[1,8,2,32,768]{4,3,2,1,0:T(8,128)(2,1)S(1)}, bf16[1,8,2,32,768]{4,3,2,1,0:T(8,128)(2,1)}, u32[]{:S(2)}) copy-start(bf16[1,8,2,32,768]{4,3,2,1,0:T(8,128)(2,1)} %param.8) | copy-start | bytes 2359300
  2.5 11.6 %collective-permute-start = (bf16[144,768]{1,0:T(8,128)(2,1)}, bf16[144,768]{1,0:T(8,128)(2,1)S(1)}, u32[]{:S(2)}, u32[]{:S(2)}) collective-permute-start(bf16[144,768]{1,0:T(8,128)(2,1)} %get-tuple-element.35.refs_0_), channel_id=1, source_target_pairs={{0,2},{1,3},{2,4},{3,5},{4,6},{5,7},{6,0},{7,1},{8,10},{9,11},{10,... | collective-permute-start | bytes 663560 | tf_op jit(solution)/shard_map/ppermute | solution.py:344
  5.6 14.7 %collective-permute-start.1 = (bf16[144,768]{1,0:T(8,128)(2,1)}, bf16[144,768]{1,0:T(8,128)(2,1)S(1)}, u32[]{:S(2)}, u32[]{:S(2)}) collective-permute-start(bf16[144,768]{1,0:T(8,128)(2,1)} %get-tuple-element.35.refs_0_), channel_id=1, source_target_pairs={{0,6},{1,7},{2,0},{3,1},{4,2},{5,3},{6,4},{7,5},{8,14},{9,15},{10,... | collective-permute-start | bytes 663560 | tf_op jit(solution)/shard_map/ppermute | solution.py:344
  14.1 11.1 %collective-permute-start.2 = (bf16[144,768]{1,0:T(8,128)(2,1)S(1)}, bf16[144,768]{1,0:T(8,128)(2,1)S(1)}, u32[]{:S(2)}, u32[]{:S(2)}) collective-permute-start(bf16[144,768]{1,0:T(8,128)(2,1)S(1)} %collective-permute-done.refs_1_), channel_id=1, source_target_pairs={{0,2},{1,3},{2,4},{3,5},{4,6},{5,7},{6,0},{7,1},{8,10},{9,11},{10,... | collective-permute-start | bytes 663560 | tf_op jit(solution)/shard_map/ppermute | solution.py:344
  15.2 16.9 %collective-permute-start.3 = (bf16[128,1280]{1,0:T(8,128)(2,1)S(1)}, bf16[128,1280]{1,0:T(8,128)(2,1)S(1)}, u32[]{:S(2)}, u32[]{:S(2)}) collective-permute-start(bf16[128,1280]{1,0:T(8,128)(2,1)S(1)} %shard_map.77.refs_1_.refs_0_), channel_id=1, source_target_pairs={{0,2},{1,3},{2,4},{3,5},{4,6},{5,7},{6,0},{7,1},{8,10},{9,11},{10,... | collective-permute-start | bytes 983048 | tf_op jit(solution)/shard_map/ppermute | solution.py:344
  19.4 16.9 %collective-permute-start.4 = (bf16[128,1280]{1,0:T(8,128)(2,1)S(1)}, bf16[128,1280]{1,0:T(8,128)(2,1)S(1)}, u32[]{:S(2)}, u32[]{:S(2)}) collective-permute-start(bf16[128,1280]{1,0:T(8,128)(2,1)S(1)} %shard_map.77.refs_1_.refs_0_), channel_id=1, source_target_pairs={{0,6},{1,7},{2,0},{3,1},{4,2},{5,3},{6,4},{7,5},{8,14},{9,15},{10,... | collective-permute-start | bytes 983048 | tf_op jit(solution)/shard_map/ppermute | solution.py:344
  20.6 16.0 %collective-permute-start.6 = (bf16[2,96,768]{2,1,0:T(8,128)(2,1)S(1)}, bf16[2,96,768]{2,1,0:T(8,128)(2,1)S(1)}, u32[]{:S(2)}, u32[]{:S(2)}) collective-permute-start(bf16[2,96,768]{2,1,0:T(8,128)(2,1)S(1)} %get-tuple-element.42), channel_id=1, source_target_pairs={{0,1},{1,0},{2,3},{3,2},{4,5},{5,4},{6,7},{7,6},{8,9},{9,8},{10,11... | collective-permute-start | bytes 884744 | tf_op jit(solution)/shard_map/ppermute | solution.py:355
  25.7 10.9 %collective-permute-start.8 = (bf16[2,32,1280]{2,1,0:T(8,128)(2,1)S(1)}, bf16[2,32,1280]{2,1,0:T(8,128)(2,1)S(1)}, u32[]{:S(2)}, u32[]{:S(2)}) collective-permute-start(bf16[2,32,1280]{2,1,0:T(8,128)(2,1)S(1)} %get-tuple-element.44), channel_id=1, source_target_pairs={{0,1},{1,0},{2,3},{3,2},{4,5},{5,4},{6,7},{7,6},{8,9},{9,8},{10,11... | collective-permute-start | bytes 491528 | tf_op jit(solution)/shard_map/ppermute | solution.py:355
  27.2 9.3 %collective-permute-start.7 = (bf16[2,32,768]{2,1,0:T(8,128)(2,1)S(1)}, bf16[2,32,768]{2,1,0:T(8,128)(2,1)S(1)}, u32[]{:S(2)}, u32[]{:S(2)}) collective-permute-start(bf16[2,32,768]{2,1,0:T(8,128)(2,1)S(1)} %get-tuple-element.43), channel_id=1, source_target_pairs={{0,1},{1,0},{2,3},{3,2},{4,5},{5,4},{6,7},{7,6},{8,9},{9,8},{10,11... | collective-permute-start | bytes 294920 | tf_op jit(solution)/shard_map/ppermute | solution.py:355
  37.4 2.9 %collective-permute-start.9 = (bf16[2,2,192,768]{3,2,1,0:T(8,128)(2,1)S(1)}, bf16[2,2,192,768]{3,2,1,0:T(8,128)(2,1)S(1)}, u32[]{:S(2)}, u32[]{:S(2)}) collective-permute-start(bf16[2,2,192,768]{3,2,1,0:T(8,128)(2,1)S(1)} %get-tuple-element.46), channel_id=1, source_target_pairs={{0,8},{8,0},{16,24},{24,16},{1,9},{9,1},{17,25},{25,17},{2,10},{10... | collective-permute-start | bytes 3538952 | tf_op jit(solution)/shard_map/ppermute | solution.py:447
  37.5 11.9 %collective-permute-start.5 = (bf16[128,1280]{1,0:T(8,128)(2,1)S(1)}, bf16[128,1280]{1,0:T(8,128)(2,1)S(1)}, u32[]{:S(2)}, u32[]{:S(2)}) collective-permute-start(bf16[128,1280]{1,0:T(8,128)(2,1)S(1)} %collective-permute-done.3.refs_0_), channel_id=1, source_target_pairs={{0,2},{1,3},{2,4},{3,5},{4,6},{5,7},{6,0},{7,1},{8,10},{9,11},{10,... | collective-permute-start | bytes 983048 | tf_op jit(solution)/shard_map/ppermute | solution.py:344
  38.6 13.3 %collective-permute-start.10 = (bf16[2,64,1280]{2,1,0:T(8,128)(2,1)S(1)}, bf16[2,64,1280]{2,1,0:T(8,128)(2,1)S(1)}, u32[]{:S(2)}, u32[]{:S(2)}) collective-permute-start(bf16[2,64,1280]{2,1,0:T(8,128)(2,1)S(1)} %get-tuple-element.49), channel_id=1, source_target_pairs={{0,1},{1,0},{2,3},{3,2},{4,5},{5,4},{6,7},{7,6},{8,9},{9,8},{10,11... | collective-permute-start | bytes 983048 | tf_op jit(solution)/shard_map/ppermute | solution.py:355
  40.4 15.0 %collective-permute-start.12 = (bf16[2,64,768]{2,1,0:T(8,128)(2,1)S(1)}, bf16[2,64,768]{2,1,0:T(8,128)(2,1)S(1)}, u32[]{:S(2)}, u32[]{:S(2)}) collective-permute-start(bf16[2,64,768]{2,1,0:T(8,128)(2,1)S(1)} %get-tuple-element.47.refs_2_), channel_id=1, source_target_pairs={{0,16},{8,24},{16,0},{24,8},{1,17},{9,25},{17,1},{25,9},{2,18},{10... | collective-permute-start | bytes 589832 | tf_op jit(solution)/shard_map/ppermute | solution.py:458
  42.0 13.4 %collective-permute-start.13 = (bf16[2,64,768]{2,1,0:T(8,128)(2,1)S(1)}, bf16[2,64,768]{2,1,0:T(8,128)(2,1)S(1)}, u32[]{:S(2)}, u32[]{:S(2)}) collective-permute-start(bf16[2,64,768]{2,1,0:T(8,128)(2,1)S(1)} %get-tuple-element.51), channel_id=1, source_target_pairs={{0,16},{8,24},{16,0},{24,8},{1,17},{9,25},{17,1},{25,9},{2,18},{10... | collective-permute-start | bytes 589832 | tf_op jit(solution)/shard_map/ppermute | solution.py:458
  42.5 13.3 %collective-permute-start.14 = (bf16[2,64,768]{2,1,0:T(8,128)(2,1)S(1)}, bf16[2,64,768]{2,1,0:T(8,128)(2,1)S(1)}, u32[]{:S(2)}, u32[]{:S(2)}) collective-permute-start(bf16[2,64,768]{2,1,0:T(8,128)(2,1)S(1)} %get-tuple-element.52), channel_id=1, source_target_pairs={{0,16},{8,24},{16,0},{24,8},{1,17},{9,25},{17,1},{25,9},{2,18},{10... | collective-permute-start | bytes 589832 | tf_op jit(solution)/shard_map/ppermute | solution.py:458
  49.6 5.8 %collective-permute-start.11 = (bf16[2,32,1280]{2,1,0:T(8,128)(2,1)S(1)}, bf16[2,32,1280]{2,1,0:T(8,128)(2,1)S(1)}, u32[]{:S(2)}, u32[]{:S(2)}) collective-permute-start(bf16[2,32,1280]{2,1,0:T(8,128)(2,1)S(1)} %get-tuple-element.50), channel_id=1, source_target_pairs={{0,1},{1,0},{2,3},{3,2},{4,5},{5,4},{6,7},{7,6},{8,9},{9,8},{10,11... | collective-permute-start | bytes 491528 | tf_op jit(solution)/shard_map/ppermute | solution.py:355
  57.4 4.1 %collective-permute-start.15 = (bf16[2,2,192,896]{3,2,1,0:T(8,128)(2,1)S(1)}, bf16[2,2,192,896]{3,2,1,0:T(8,128)(2,1)S(1)}, u32[]{:S(2)}, u32[]{:S(2)}) collective-permute-start(bf16[2,2,192,896]{3,2,1,0:T(8,128)(2,1)S(1)} %get-tuple-element.55), channel_id=1, source_target_pairs={{0,8},{8,0},{16,24},{24,16},{1,9},{9,1},{17,25},{25,17},{2,10},{10... | collective-permute-start | bytes 4128776 | tf_op jit(solution)/shard_map/ppermute | solution.py:447
  57.5 4.0 %collective-permute-start.16 = (bf16[2,2,192,384]{3,2,1,0:T(8,128)(2,1)S(1)}, bf16[2,2,192,384]{3,2,1,0:T(8,128)(2,1)S(1)}, u32[]{:S(2)}, u32[]{:S(2)}) collective-permute-start(bf16[2,2,192,384]{3,2,1,0:T(8,128)(2,1)S(1)} %get-tuple-element.56), channel_id=1, source_target_pairs={{0,8},{8,0},{16,24},{24,16},{1,9},{9,1},{17,25},{25,17},{2,10},{10... | collective-permute-start | bytes 1769480 | tf_op jit(solution)/shard_map/ppermute | solution.py:447
  61.8 26.0 %collective-permute-start.22 = (bf16[2,192,896]{2,1,0:T(8,128)(2,1)S(1)}, bf16[2,192,896]{2,1,0:T(8,128)(2,1)S(1)}, u32[]{:S(2)}, u32[]{:S(2)}) collective-permute-start(bf16[2,192,896]{2,1,0:T(8,128)(2,1)S(1)} %shard_map.90.refs_9_), channel_id=1, source_target_pairs={{0,16},{8,24},{16,0},{24,8},{1,17},{9,25},{17,1},{25,9},{2,18},{10... | collective-permute-start | bytes 2064392 | tf_op jit(solution)/shard_map/ppermute | solution.py:458
  63.4 22.3 %collective-permute-start.21 = (bf16[2,192,384]{2,1,0:T(8,128)(2,1)S(1)}, bf16[2,192,384]{2,1,0:T(8,128)(2,1)S(1)}, u32[]{:S(2)}, u32[]{:S(2)}) collective-permute-start(bf16[2,192,384]{2,1,0:T(8,128)(2,1)S(1)} %shard_map.89.refs_2_), channel_id=1, source_target_pairs={{0,16},{8,24},{16,0},{24,8},{1,17},{9,25},{17,1},{25,9},{2,18},{10... | collective-permute-start | bytes 884744 | tf_op jit(solution)/shard_map/ppermute | solution.py:458
  66.0 3.6 %collective-permute-start.17 = (f32[2,256]{1,0:T(2,128)S(1)}, f32[2,256]{1,0:T(2,128)S(1)}, u32[]{:S(2)}, u32[]{:S(2)}) collective-permute-start(f32[2,256]{1,0:T(2,128)S(1)} %get-tuple-element.59.refs_5_), channel_id=1, source_target_pairs={{0,1},{1,0},{2,3},{3,2},{4,5},{5,4},{6,7},{7,6},{8,9},{9,8},{10,11... | collective-permute-start | bytes 6152 | tf_op jit(solution)/shard_map/ppermute | solution.py:499
  69.6 17.1 %collective-permute-start.18 = (f32[2,2,256]{2,1,0:T(2,128)S(1)}, f32[2,2,256]{2,1,0:T(2,128)S(1)}, u32[]{:S(2)}, u32[]{:S(2)}) collective-permute-start(f32[2,2,256]{2,1,0:T(2,128)S(1)} %pad_maximum_fusion.refs_2_), channel_id=1, source_target_pairs={{2,0},{3,1},{4,2},{5,3},{6,4},{7,5},{0,6},{1,7},{10,8},{11,9},{12,... | collective-permute-start | bytes 12296 | tf_op jit(solution)/shard_map/ppermute | solution.py:501
  71.9 14.8 %collective-permute-start.19 = (f32[2,2,256]{2,1,0:T(2,128)S(1)}, f32[2,2,256]{2,1,0:T(2,128)S(1)}, u32[]{:S(2)}, u32[]{:S(2)}) collective-permute-start(f32[2,2,256]{2,1,0:T(2,128)S(1)} %pad_maximum_fusion.refs_2_), channel_id=1, source_target_pairs={{4,0},{5,1},{6,2},{7,3},{0,4},{1,5},{2,6},{3,7},{12,8},{13,9},{14,... | collective-permute-start | bytes 12296 | tf_op jit(solution)/shard_map/ppermute | solution.py:501
  72.2 14.5 %collective-permute-start.20 = (f32[2,2,256]{2,1,0:T(2,128)S(1)}, f32[2,2,256]{2,1,0:T(2,128)S(1)}, u32[]{:S(2)}, u32[]{:S(2)}) collective-permute-start(f32[2,2,256]{2,1,0:T(2,128)S(1)} %pad_maximum_fusion.refs_2_), channel_id=1, source_target_pairs={{6,0},{7,1},{0,2},{1,3},{2,4},{3,5},{4,6},{5,7},{14,8},{15,9},{8,1... | collective-permute-start | bytes 12296 | tf_op jit(solution)/shard_map/ppermute | solution.py:501
  (5 other events, 23.3 us)

commit v19 on v18

--- a/solution.py
+++ b/solution.py
@@ -70,15 +70,19 @@
     return [jnp.sum(jnp.where(n, before, 0.0), axis=0, keepdims=True) for n in named]
 
 
-def begin_kernel(experts, capacity, ids_ref, probs_ref, rows_ref, flat_ref, out_ref, *scratch):
-    ids_got, probs_got, sems = scratch
+def begin_kernel(experts, capacity, ids_ref, probs_ref, rows_ref, flat_ref, *refs):
+    out_refs, (ids_got, probs_got, sems) = refs[:-3], refs[-3:]
     chosen, tokens = ids_got.shape
-    width = out_ref.shape[1]
+    out_ref, width = out_refs[0], out_refs[0].shape[1]
     copies = [
         pltpu.make_async_copy(ids_ref, ids_got, sems.at[0]),
         pltpu.make_async_copy(probs_ref, probs_got, sems.at[1]),
-        pltpu.make_async_copy(rows_ref.at[:, :width], out_ref.at[:tokens], sems.at[2]),
     ]
+    start = 0
+    for i, ref in enumerate(out_refs):
+        rows = rows_ref.at[:, start : start + ref.shape[1]]
+        copies.append(pltpu.make_async_copy(rows, ref.at[:tokens], sems.at[2 + i]))
+        start += ref.shape[1]
     for copy in copies:
         copy.start()
     for copy in copies:
@@ -145,19 +149,6 @@
             other = (piece % 2) ^ core
             step = (piece // 2 - row + across) % across
             out_ref[e, other, step] = turned[piece * share : (piece + 1) * share]
-
-
-def cut_kernel(start, rows_ref, *refs):
-    out_refs, sems = refs[:-1], refs[-1]
-    copies = []
-    for i, ref in enumerate(out_refs):
-        at = slice(start, start + ref.shape[1])
-        copies.append(pltpu.make_async_copy(rows_ref.at[:, at], ref, sems.at[i]))
-        start += ref.shape[1]
-    for copy in copies:
-        copy.start()
-    for copy in copies:
-        copy.wait()
 
 
 def stacked_rows(refs, e, at):
@@ -291,7 +282,7 @@
 
 def chunks_of(features):
     unit = features // 16
-    return [[6 * unit], [3 * unit, 7 * unit]]
+    return [[6 * unit], [7 * unit, 3 * unit]]
 
 
 def cuts_of(share, first):
@@ -306,9 +297,10 @@
         tokens, features = grad_out.shape
         self.call, self.held, self.capacity, self.widths = call, held, capacity, widths
         self.tokens, self.chosen, self.place = tokens, ids.shape[0], {}
-        self.flat, first = call(
+        self.flat, *owns = call(
             functools.partial(begin_kernel, LINE * SIDES * held, capacity),
-            [sds(ids.shape, I32), sds((tokens + INFO, widths[0]), BF16)],
+            [sds(ids.shape, I32)]
+            + [sds((tokens + (0 if c else INFO), w), BF16) for c, w in enumerate(widths)],
             ids,
             probs,
             grad_out,
@@ -316,22 +308,13 @@
             scratch_shapes=[
                 pltpu.VMEM(ids.shape, I32),
                 pltpu.VMEM(probs.shape, F32),
-                pltpu.SemaphoreType.DMA((3,)),
+                pltpu.SemaphoreType.DMA((2 + len(widths),)),
             ],
             room=60,
             keep=False,
         )
         self.blocks, self.passed = [], []
-        self.leave(first)
-        rest = call(
-            functools.partial(cut_kernel, widths[0]),
-            [sds((tokens, w), BF16) for w in widths[1:]],
-            grad_out,
-            in_specs=[HBM],
-            scratch_shapes=[pltpu.SemaphoreType.DMA((len(widths) - 1,))],
-            after=[self.blocks[0][1]],
-        )
-        for own in rest:
+        for own in owns:
             self.leave(own)
 
     def leave(self, own):

time: 90.1 us -> 86.1 us (0.956)
  waiting for transfers between devices: 44 us -> 39.1 us
    ppermute x5, waiting for transfers between devices: 11.6 us -> 8.67 us  [paired(): others.append(lax.ppermute(pair, 'dp', shift))]
    ppermute x3, waiting for transfers between devices: 3.63 us -> 2.14 us  [termed(): got = lax.ppermute(give, 'dp', [(i, i ^ 1) for i in range(dp)])]
    unnamed x12 -> x14, local copies, waits for them, and re-layouts: 1.06 us -> 1.82 us
    pallas_call x20 -> x19, Pallas kernels: 14.9 us -> 15.1 us  [__call__(): pl.pallas_call(body, out_shape=outs, in_specs=in_specs, compiler_params=p...]
  transfers between devices with their start and end apart: 23 -> 23, of which waited for: 11 -> 12; matrix products, arithmetic and copies ran while one was open for 0% -> 0% of each run, Pallas kernels for 9% -> 11%
where the time goes in v19:
time: 86.1 us; the launch traced here: 85.9 us
  waiting for transfers between devices  39.1 us (45%)
  starting transfers between devices  29.1 us (34%)
  Pallas kernels  15.1 us (18%)
  local copies, waits for them, and re-layouts  1.82 us (2%)
  between operations  0.87 us (1%)
    ppermute x6, waiting for transfers between devices, along(): return lax.ppermute(block, 'expert', pairs)  22.7 us
    pallas_call x19, Pallas kernels, __call__(): pl.pallas_call(body, out_shape=outs, in_specs=in_specs, compiler_params=p...  15.1 us
    ppermute x6, starting transfers between devices, along(): return lax.ppermute(block, 'expert', pairs)  11 us
    ppermute x5, waiting for transfers between devices, paired(): others.append(lax.ppermute(pair, 'dp', shift))  8.67 us
    ppermute x5, starting transfers between devices, pick(): lax.ppermute(other, 'expert', [(i, i ^ 1) for i in range(LINE * SIDES)])  6.69 us
    ppermute x5, starting transfers between devices, paired(): others.append(lax.ppermute(pair, 'dp', shift))  5.87 us
    ppermute x5, waiting for transfers between devices, pick(): lax.ppermute(other, 'expert', [(i, i ^ 1) for i in range(LINE * SIDES)])  3.46 us
    ppermute x3, starting transfers between devices, body(): lax.ppermute(both, 'expert', [(moved(i, d, 0), i) for i in range(groups)])  3.36 us
  transfers between devices with their start and end apart: 23, of which 12 were waited for; matrix products, arithmetic and copies ran while one was open for 0% of the time, Pallas kernels for 11%

profile of v19, /device:TPU:0, one launch (start us, length us, event | category | flops | bytes accessed | tf_op | source)
XLA Modules:
  0.0 85.9 jit_solution(11338572476441459624)
XLA Ops:
  0.6 2.1 %shard_map.76 = (s32[2,128]{1,0:T(2,128)}, bf16[144,768]{1,0:T(8,128)(2,1)}, bf16[128,1280]{1,0:T(8,128)(2,1)}) custom-call(s32[2,128]{1,0:T(2,128)} %bitcast.13, f32[2,128]{1,0:T(2,128)} %bitcast.10, bf16[128,2048]{1,0:T(8,128)(2,1)} %rows_ref.1), custom_call_target="tpu_custom_call" | custom-call | flops 1 | bytes 1 | tf_op jit(solution)/shard_map/pallas_call | solution.py:43
  2.7 3.1 %collective-permute-start = (bf16[144,768]{1,0:T(8,128)(2,1)}, bf16[144,768]{1,0:T(8,128)(2,1)S(1)}, u32[]{:S(2)}, u32[]{:S(2)}) collective-permute-start(bf16[144,768]{1,0:T(8,128)(2,1)} %get-tuple-element.37.refs_0_), channel_id=1, source_target_pairs={{0,2},{1,3},{2,4},{3,5},{4,6},{5,7},{6,0},{7,1},{8,10},{9,11},{10,... | collective-permute-start | bytes 663560 | tf_op jit(solution)/shard_map/ppermute | solution.py:327
  5.8 2.1 %collective-permute-start.1 = (bf16[144,768]{1,0:T(8,128)(2,1)}, bf16[144,768]{1,0:T(8,128)(2,1)S(1)}, u32[]{:S(2)}, u32[]{:S(2)}) collective-permute-start(bf16[144,768]{1,0:T(8,128)(2,1)} %get-tuple-element.37.refs_0_), channel_id=1, source_target_pairs={{0,6},{1,7},{2,0},{3,1},{4,2},{5,3},{6,4},{7,5},{8,14},{9,15},{10,... | collective-permute-start | bytes 663560 | tf_op jit(solution)/shard_map/ppermute | solution.py:327
  7.9 6.4 %collective-permute-done.refs_1_ = bf16[144,768]{1,0:T(8,128)(2,1)S(1)} collective-permute-done((bf16[144,768]{1,0:T(8,128)(2,1)}, bf16[144,768]{1,0:T(8,128)(2,1)S(1)}, u32[]{:S(2)}, u32[]{:S(2)}) %collective-permute-start) | collective-permute-done | bytes 221216 | tf_op jit(solution)/shard_map/ppermute | solution.py:327
  14.3 4.1 %collective-permute-start.3 = (bf16[128,1280]{1,0:T(8,128)(2,1)}, bf16[128,1280]{1,0:T(8,128)(2,1)S(1)}, u32[]{:S(2)}, u32[]{:S(2)}) collective-permute-start(bf16[128,1280]{1,0:T(8,128)(2,1)} %get-tuple-element.36.refs_0_), channel_id=1, source_target_pairs={{0,2},{1,3},{2,4},{3,5},{4,6},{5,7},{6,0},{7,1},{8,10},{9,11},{10,... | collective-permute-start | bytes 983048 | tf_op jit(solution)/shard_map/ppermute | solution.py:327
  21.4 1.6 %collective-permute-start.6 = (bf16[2,96,768]{2,1,0:T(8,128)(2,1)S(1)}, bf16[2,96,768]{2,1,0:T(8,128)(2,1)S(1)}, u32[]{:S(2)}, u32[]{:S(2)}) collective-permute-start(bf16[2,96,768]{2,1,0:T(8,128)(2,1)S(1)} %get-tuple-element.44), channel_id=1, source_target_pairs={{0,1},{1,0},{2,3},{3,2},{4,5},{5,4},{6,7},{7,6},{8,9},{9,8},{10,11... | collective-permute-start | bytes 884744 | tf_op jit(solution)/shard_map/ppermute | solution.py:338
  22.9 2.5 %collective-permute-done.2.refs_0_ = bf16[144,768]{1,0:T(8,128)(2,1)S(1)} collective-permute-done((bf16[144,768]{1,0:T(8,128)(2,1)S(1)}, bf16[144,768]{1,0:T(8,128)(2,1)S(1)}, u32[]{:S(2)}, u32[]{:S(2)}) %collective-permute-start.2) | collective-permute-done | bytes 221216 | tf_op jit(solution)/shard_map/ppermute | solution.py:327
  25.9 1.6 %collective-permute-start.8 = (bf16[2,32,1280]{2,1,0:T(8,128)(2,1)S(1)}, bf16[2,32,1280]{2,1,0:T(8,128)(2,1)S(1)}, u32[]{:S(2)}, u32[]{:S(2)}) collective-permute-start(bf16[2,32,1280]{2,1,0:T(8,128)(2,1)S(1)} %get-tuple-element.46), channel_id=1, source_target_pairs={{0,1},{1,0},{2,3},{3,2},{4,5},{5,4},{6,7},{7,6},{8,9},{9,8},{10,11... | collective-permute-start | bytes 491528 | tf_op jit(solution)/shard_map/ppermute | solution.py:338
  28.0 4.4 %collective-permute-done.3.refs_0_ = bf16[128,1280]{1,0:T(8,128)(2,1)S(1)} collective-permute-done((bf16[128,1280]{1,0:T(8,128)(2,1)}, bf16[128,1280]{1,0:T(8,128)(2,1)S(1)}, u32[]{:S(2)}, u32[]{:S(2)}) %collective-permute-start.3) | collective-permute-done | bytes 327712 | tf_op jit(solution)/shard_map/ppermute | solution.py:327
  32.3 4.1 %collective-permute-done.4.refs_1_ = bf16[128,1280]{1,0:T(8,128)(2,1)S(1)} collective-permute-done((bf16[128,1280]{1,0:T(8,128)(2,1)}, bf16[128,1280]{1,0:T(8,128)(2,1)S(1)}, u32[]{:S(2)}, u32[]{:S(2)}) %collective-permute-start.4) | collective-permute-done | bytes 327712 | tf_op jit(solution)/shard_map/ppermute | solution.py:327
  40.6 1.6 %collective-permute-start.12 = (bf16[2,64,768]{2,1,0:T(8,128)(2,1)S(1)}, bf16[2,64,768]{2,1,0:T(8,128)(2,1)S(1)}, u32[]{:S(2)}, u32[]{:S(2)}) collective-permute-start(bf16[2,64,768]{2,1,0:T(8,128)(2,1)S(1)} %get-tuple-element.49.refs_2_), channel_id=1, source_target_pairs={{0,16},{8,24},{16,0},{24,8},{1,17},{9,25},{17,1},{25,9},{2,18},{10... | collective-permute-start | bytes 589832 | tf_op jit(solution)/shard_map/ppermute | solution.py:441
  42.7 1.5 %collective-permute-start.14 = (bf16[2,64,768]{2,1,0:T(8,128)(2,1)S(1)}, bf16[2,64,768]{2,1,0:T(8,128)(2,1)S(1)}, u32[]{:S(2)}, u32[]{:S(2)}) collective-permute-start(bf16[2,64,768]{2,1,0:T(8,128)(2,1)S(1)} %get-tuple-element.54), channel_id=1, source_target_pairs={{0,16},{8,24},{16,0},{24,8},{1,17},{9,25},{17,1},{25,9},{2,18},{10... | collective-permute-start | bytes 589832 | tf_op jit(solution)/shard_map/ppermute | solution.py:441
  44.3 5.3 %collective-permute-done.5.refs_0_ = bf16[128,1280]{1,0:T(8,128)(2,1)S(1)} collective-permute-done((bf16[128,1280]{1,0:T(8,128)(2,1)S(1)}, bf16[128,1280]{1,0:T(8,128)(2,1)S(1)}, u32[]{:S(2)}, u32[]{:S(2)}) %collective-permute-start.5) | collective-permute-done | bytes 327712 | tf_op jit(solution)/shard_map/ppermute | solution.py:327
  49.8 1.6 %collective-permute-start.11 = (bf16[2,32,1280]{2,1,0:T(8,128)(2,1)S(1)}, bf16[2,32,1280]{2,1,0:T(8,128)(2,1)S(1)}, u32[]{:S(2)}, u32[]{:S(2)}) collective-permute-start(bf16[2,32,1280]{2,1,0:T(8,128)(2,1)S(1)} %get-tuple-element.52), channel_id=1, source_target_pairs={{0,1},{1,0},{2,3},{3,2},{4,5},{5,4},{6,7},{7,6},{8,9},{9,8},{10,11... | collective-permute-start | bytes 491528 | tf_op jit(solution)/shard_map/ppermute | solution.py:338
  52.2 3.4 %collective-permute-done.11.refs_6_ = bf16[2,32,1280]{2,1,0:T(8,128)(2,1)S(1)} collective-permute-done((bf16[2,32,1280]{2,1,0:T(8,128)(2,1)S(1)}, bf16[2,32,1280]{2,1,0:T(8,128)(2,1)S(1)}, u32[]{:S(2)}, u32[]{:S(2)}) %collective-permute-start.11) | collective-permute-done | bytes 163872 | tf_op jit(solution)/shard_map/ppermute | solution.py:338
  58.3 2.0 %collective-permute-done.16.refs_1_ = bf16[2,2,192,896]{3,2,1,0:T(8,128)(2,1)S(1)} collective-permute-done((bf16[2,2,192,896]{3,2,1,0:T(8,128)(2,1)S(1)}, bf16[2,2,192,896]{3,2,1,0:T(8,128)(2,1)S(1)}, u32[]{:S(2)}, u32[]{:S(2)}) %collective-permute-start.16) | collective-permute-done | bytes 1376288 | tf_op jit(solution)/shard_map/ppermute | solution.py:430
  60.4 1.6 %collective-permute-start.21 = (bf16[2,192,896]{2,1,0:T(8,128)(2,1)S(1)}, bf16[2,192,896]{2,1,0:T(8,128)(2,1)S(1)}, u32[]{:S(2)}, u32[]{:S(2)}) collective-permute-start(bf16[2,192,896]{2,1,0:T(8,128)(2,1)S(1)} %shard_map.88.refs_2_), channel_id=1, source_target_pairs={{0,16},{8,24},{16,0},{24,8},{1,17},{9,25},{17,1},{25,9},{2,18},{10... | collective-permute-start | bytes 2064392 | tf_op jit(solution)/shard_map/ppermute | solution.py:441
  62.8 2.2 %shard_map.90 = (bf16[8,2,32,768]{3,2,1,0:T(8,128)(2,1)}, f32[2,256]{1,0:T(2,128)S(1)}) custom-call(bf16[2,768,2048]{2,1,0:T(8,128)(2,1)S(1)} %copy-done, bf16[2,32,1280]{2,1,0:T(8,128)(2,1)S(1)} %get-tuple-element.40.refs_3_.refs_1_, bf16[2,64,1280]{2,1,0:T(8,128)(2,1)S(1)} %get-tuple-element.41.refs_5_.refs_2_, ...), custom_call_target="tpu_custom_call" | custom-call | flops 1 | bytes 1 | tf_op jit(solution)/shard_map/pallas_call | solution.py:43
  66.5 2.1 %collective-permute-done.17 = f32[2,256]{1,0:T(2,128)S(1)} collective-permute-done((f32[2,256]{1,0:T(2,128)S(1)}, f32[2,256]{1,0:T(2,128)S(1)}, u32[]{:S(2)}, u32[]{:S(2)}) %collective-permute-start.17) | collective-permute-done | bytes 2080 | tf_op jit(solution)/shard_map/ppermute | solution.py:482
  68.6 2.3 %collective-permute-start.18 = (f32[2,2,256]{2,1,0:T(2,128)S(1)}, f32[2,2,256]{2,1,0:T(2,128)S(1)}, u32[]{:S(2)}, u32[]{:S(2)}) collective-permute-start(f32[2,2,256]{2,1,0:T(2,128)S(1)} %pad_maximum_fusion.refs_2_), channel_id=1, source_target_pairs={{2,0},{3,1},{4,2},{5,3},{6,4},{7,5},{0,6},{1,7},{10,8},{11,9},{12,... | collective-permute-start | bytes 12296 | tf_op jit(solution)/shard_map/ppermute | solution.py:484
  73.4 5.4 %collective-permute-done.21.refs_2_ = bf16[2,192,896]{2,1,0:T(8,128)(2,1)S(1)} collective-permute-done((bf16[2,192,896]{2,1,0:T(8,128)(2,1)S(1)}, bf16[2,192,896]{2,1,0:T(8,128)(2,1)S(1)}, u32[]{:S(2)}, u32[]{:S(2)}) %collective-permute-start.21) | collective-permute-done | bytes 688160 | tf_op jit(solution)/shard_map/ppermute | solution.py:441
  78.8 1.6 %shard_map.92 = (f32[192,2,2048]{2,1,0:T(2,128)}, f32[8,128]{1,0:T(8,128)S(1)}) custom-call(bf16[2,2,192,896]{3,2,1,0:T(8,128)(2,1)S(1)} %get-tuple-element.55.refs_7_.refs_0_, bf16[2,2,192,896]{3,2,1,0:T(8,128)(2,1)S(1)} %collective-permute-done.16.refs_1_, ...), custom_call_target="tpu_custom_call", output_to_operand_aliasing={{0}: (3, {})} | custom-call | flops 1 | bytes 1 | tf_op jit(solution)/shard_map/pallas_call | solution.py:43
  81.4 2.9 %collective-permute-done.22.refs_2_ = bf16[2,192,384]{2,1,0:T(8,128)(2,1)S(1)} collective-permute-done((bf16[2,192,384]{2,1,0:T(8,128)(2,1)S(1)}, bf16[2,192,384]{2,1,0:T(8,128)(2,1)S(1)}, u32[]{:S(2)}, u32[]{:S(2)}) %collective-permute-start.22) | collective-permute-done | bytes 294944 | tf_op jit(solution)/shard_map/ppermute | solution.py:441
  84.3 1.7 %shard_map.94 = (f32[192,2,2048]{2,1,0:T(2,128)}, f32[8,128]{1,0:T(8,128)}) custom-call(bf16[2,2,192,384]{3,2,1,0:T(8,128)(2,1)S(1)} %get-tuple-element.56.refs_2_.refs_0_, bf16[2,2,192,384]{3,2,1,0:T(8,128)(2,1)S(1)} %collective-permute-done.15.refs_1_, bf16[2,192,384]{2,1,0:T(8,128)(2,1)S(1)} %collective-permute-done.22.refs_2_, ...), custom_call_target="tpu_custom_call", output_to_operand_aliasing={{0}: (3, {})} | custom-call | flops 1 | bytes 1 | tf_op jit(solution)/shard_map/pallas_call | solution.py:43
  (56 shorter events, 18.2 us)
Async XLA Ops:
  2.7 11.6 %collective-permute-start = (bf16[144,768]{1,0:T(8,128)(2,1)}, bf16[144,768]{1,0:T(8,128)(2,1)S(1)}, u32[]{:S(2)}, u32[]{:S(2)}) collective-permute-start(bf16[144,768]{1,0:T(8,128)(2,1)} %get-tuple-element.37.refs_0_), channel_id=1, source_target_pairs={{0,2},{1,3},{2,4},{3,5},{4,6},{5,7},{6,0},{7,1},{8,10},{9,11},{10,... | collective-permute-start | bytes 663560 | tf_op jit(solution)/shard_map/ppermute | solution.py:327
  5.8 14.6 %collective-permute-start.1 = (bf16[144,768]{1,0:T(8,128)(2,1)}, bf16[144,768]{1,0:T(8,128)(2,1)S(1)}, u32[]{:S(2)}, u32[]{:S(2)}) collective-permute-start(bf16[144,768]{1,0:T(8,128)(2,1)} %get-tuple-element.37.refs_0_), channel_id=1, source_target_pairs={{0,6},{1,7},{2,0},{3,1},{4,2},{5,3},{6,4},{7,5},{8,14},{9,15},{10,... | collective-permute-start | bytes 663560 | tf_op jit(solution)/shard_map/ppermute | solution.py:327
  14.3 11.1 %collective-permute-start.2 = (bf16[144,768]{1,0:T(8,128)(2,1)S(1)}, bf16[144,768]{1,0:T(8,128)(2,1)S(1)}, u32[]{:S(2)}, u32[]{:S(2)}) collective-permute-start(bf16[144,768]{1,0:T(8,128)(2,1)S(1)} %collective-permute-done.refs_1_), channel_id=1, source_target_pairs={{0,2},{1,3},{2,4},{3,5},{4,6},{5,7},{6,0},{7,1},{8,10},{9,11},{10,... | collective-permute-start | bytes 663560 | tf_op jit(solution)/shard_map/ppermute | solution.py:327
  14.3 18.0 %collective-permute-start.3 = (bf16[128,1280]{1,0:T(8,128)(2,1)}, bf16[128,1280]{1,0:T(8,128)(2,1)S(1)}, u32[]{:S(2)}, u32[]{:S(2)}) collective-permute-start(bf16[128,1280]{1,0:T(8,128)(2,1)} %get-tuple-element.36.refs_0_), channel_id=1, source_target_pairs={{0,2},{1,3},{2,4},{3,5},{4,6},{5,7},{6,0},{7,1},{8,10},{9,11},{10,... | collective-permute-start | bytes 983048 | tf_op jit(solution)/shard_map/ppermute | solution.py:327
  18.4 18.0 %collective-permute-start.4 = (bf16[128,1280]{1,0:T(8,128)(2,1)}, bf16[128,1280]{1,0:T(8,128)(2,1)S(1)}, u32[]{:S(2)}, u32[]{:S(2)}) collective-permute-start(bf16[128,1280]{1,0:T(8,128)(2,1)} %get-tuple-element.36.refs_0_), channel_id=1, source_target_pairs={{0,6},{1,7},{2,0},{3,1},{4,2},{5,3},{6,4},{7,5},{8,14},{9,15},{10,... | collective-permute-start | bytes 983048 | tf_op jit(solution)/shard_map/ppermute | solution.py:327
  21.4 15.4 %collective-permute-start.6 = (bf16[2,96,768]{2,1,0:T(8,128)(2,1)S(1)}, bf16[2,96,768]{2,1,0:T(8,128)(2,1)S(1)}, u32[]{:S(2)}, u32[]{:S(2)}) collective-permute-start(bf16[2,96,768]{2,1,0:T(8,128)(2,1)S(1)} %get-tuple-element.44), channel_id=1, source_target_pairs={{0,1},{1,0},{2,3},{3,2},{4,5},{5,4},{6,7},{7,6},{8,9},{9,8},{10,11... | collective-permute-start | bytes 884744 | tf_op jit(solution)/shard_map/ppermute | solution.py:338
  25.9 10.9 %collective-permute-start.8 = (bf16[2,32,1280]{2,1,0:T(8,128)(2,1)S(1)}, bf16[2,32,1280]{2,1,0:T(8,128)(2,1)S(1)}, u32[]{:S(2)}, u32[]{:S(2)}) collective-permute-start(bf16[2,32,1280]{2,1,0:T(8,128)(2,1)S(1)} %get-tuple-element.46), channel_id=1, source_target_pairs={{0,1},{1,0},{2,3},{3,2},{4,5},{5,4},{6,7},{7,6},{8,9},{9,8},{10,11... | collective-permute-start | bytes 491528 | tf_op jit(solution)/shard_map/ppermute | solution.py:338
  27.4 9.3 %collective-permute-start.7 = (bf16[2,32,768]{2,1,0:T(8,128)(2,1)S(1)}, bf16[2,32,768]{2,1,0:T(8,128)(2,1)S(1)}, u32[]{:S(2)}, u32[]{:S(2)}) collective-permute-start(bf16[2,32,768]{2,1,0:T(8,128)(2,1)S(1)} %get-tuple-element.45), channel_id=1, source_target_pairs={{0,1},{1,0},{2,3},{3,2},{4,5},{5,4},{6,7},{7,6},{8,9},{9,8},{10,11... | collective-permute-start | bytes 294920 | tf_op jit(solution)/shard_map/ppermute | solution.py:338
  36.4 14.9 %copy-start = (bf16[2,768,2048]{2,1,0:T(8,128)(2,1)S(1)}, bf16[2,768,2048]{2,1,0:T(8,128)(2,1)}, u32[]{:S(2)}) copy-start(bf16[2,768,2048]{2,1,0:T(8,128)(2,1)} %refs_0_.3) | copy-start | bytes 18874372
  37.6 2.9 %collective-permute-start.9 = (bf16[2,2,192,768]{3,2,1,0:T(8,128)(2,1)S(1)}, bf16[2,2,192,768]{3,2,1,0:T(8,128)(2,1)S(1)}, u32[]{:S(2)}, u32[]{:S(2)}) collective-permute-start(bf16[2,2,192,768]{3,2,1,0:T(8,128)(2,1)S(1)} %get-tuple-element.48), channel_id=1, source_target_pairs={{0,8},{8,0},{16,24},{24,16},{1,9},{9,1},{17,25},{25,17},{2,10},{10... | collective-permute-start | bytes 3538952 | tf_op jit(solution)/shard_map/ppermute | solution.py:430
  37.7 11.9 %collective-permute-start.5 = (bf16[128,1280]{1,0:T(8,128)(2,1)S(1)}, bf16[128,1280]{1,0:T(8,128)(2,1)S(1)}, u32[]{:S(2)}, u32[]{:S(2)}) collective-permute-start(bf16[128,1280]{1,0:T(8,128)(2,1)S(1)} %collective-permute-done.3.refs_0_), channel_id=1, source_target_pairs={{0,2},{1,3},{2,4},{3,5},{4,6},{5,7},{6,0},{7,1},{8,10},{9,11},{10,... | collective-permute-start | bytes 983048 | tf_op jit(solution)/shard_map/ppermute | solution.py:327
  38.8 13.3 %collective-permute-start.10 = (bf16[2,64,1280]{2,1,0:T(8,128)(2,1)S(1)}, bf16[2,64,1280]{2,1,0:T(8,128)(2,1)S(1)}, u32[]{:S(2)}, u32[]{:S(2)}) collective-permute-start(bf16[2,64,1280]{2,1,0:T(8,128)(2,1)S(1)} %get-tuple-element.51), channel_id=1, source_target_pairs={{0,1},{1,0},{2,3},{3,2},{4,5},{5,4},{6,7},{7,6},{8,9},{9,8},{10,11... | collective-permute-start | bytes 983048 | tf_op jit(solution)/shard_map/ppermute | solution.py:338
  40.6 15.0 %collective-permute-start.12 = (bf16[2,64,768]{2,1,0:T(8,128)(2,1)S(1)}, bf16[2,64,768]{2,1,0:T(8,128)(2,1)S(1)}, u32[]{:S(2)}, u32[]{:S(2)}) collective-permute-start(bf16[2,64,768]{2,1,0:T(8,128)(2,1)S(1)} %get-tuple-element.49.refs_2_), channel_id=1, source_target_pairs={{0,16},{8,24},{16,0},{24,8},{1,17},{9,25},{17,1},{25,9},{2,18},{10... | collective-permute-start | bytes 589832 | tf_op jit(solution)/shard_map/ppermute | solution.py:441
  42.2 13.4 %collective-permute-start.13 = (bf16[2,64,768]{2,1,0:T(8,128)(2,1)S(1)}, bf16[2,64,768]{2,1,0:T(8,128)(2,1)S(1)}, u32[]{:S(2)}, u32[]{:S(2)}) collective-permute-start(bf16[2,64,768]{2,1,0:T(8,128)(2,1)S(1)} %get-tuple-element.53), channel_id=1, source_target_pairs={{0,16},{8,24},{16,0},{24,8},{1,17},{9,25},{17,1},{25,9},{2,18},{10... | collective-permute-start | bytes 589832 | tf_op jit(solution)/shard_map/ppermute | solution.py:441
  42.7 13.3 %collective-permute-start.14 = (bf16[2,64,768]{2,1,0:T(8,128)(2,1)S(1)}, bf16[2,64,768]{2,1,0:T(8,128)(2,1)S(1)}, u32[]{:S(2)}, u32[]{:S(2)}) collective-permute-start(bf16[2,64,768]{2,1,0:T(8,128)(2,1)S(1)} %get-tuple-element.54), channel_id=1, source_target_pairs={{0,16},{8,24},{16,0},{24,8},{1,17},{9,25},{17,1},{25,9},{2,18},{10... | collective-permute-start | bytes 589832 | tf_op jit(solution)/shard_map/ppermute | solution.py:441
  49.8 5.8 %collective-permute-start.11 = (bf16[2,32,1280]{2,1,0:T(8,128)(2,1)S(1)}, bf16[2,32,1280]{2,1,0:T(8,128)(2,1)S(1)}, u32[]{:S(2)}, u32[]{:S(2)}) collective-permute-start(bf16[2,32,1280]{2,1,0:T(8,128)(2,1)S(1)} %get-tuple-element.52), channel_id=1, source_target_pairs={{0,1},{1,0},{2,3},{3,2},{4,5},{5,4},{6,7},{7,6},{8,9},{9,8},{10,11... | collective-permute-start | bytes 491528 | tf_op jit(solution)/shard_map/ppermute | solution.py:338
  57.1 3.2 %collective-permute-start.16 = (bf16[2,2,192,896]{3,2,1,0:T(8,128)(2,1)S(1)}, bf16[2,2,192,896]{3,2,1,0:T(8,128)(2,1)S(1)}, u32[]{:S(2)}, u32[]{:S(2)}) collective-permute-start(bf16[2,2,192,896]{3,2,1,0:T(8,128)(2,1)S(1)} %get-tuple-element.58), channel_id=1, source_target_pairs={{0,8},{8,0},{16,24},{24,16},{1,9},{9,1},{17,25},{25,17},{2,10},{10... | collective-permute-start | bytes 4128776 | tf_op jit(solution)/shard_map/ppermute | solution.py:430
  57.7 4.3 %collective-permute-start.15 = (bf16[2,2,192,384]{3,2,1,0:T(8,128)(2,1)S(1)}, bf16[2,2,192,384]{3,2,1,0:T(8,128)(2,1)S(1)}, u32[]{:S(2)}, u32[]{:S(2)}) collective-permute-start(bf16[2,2,192,384]{3,2,1,0:T(8,128)(2,1)S(1)} %get-tuple-element.57), channel_id=1, source_target_pairs={{0,8},{8,0},{16,24},{24,16},{1,9},{9,1},{17,25},{25,17},{2,10},{10... | collective-permute-start | bytes 1769480 | tf_op jit(solution)/shard_map/ppermute | solution.py:430
  60.4 18.3 %collective-permute-start.21 = (bf16[2,192,896]{2,1,0:T(8,128)(2,1)S(1)}, bf16[2,192,896]{2,1,0:T(8,128)(2,1)S(1)}, u32[]{:S(2)}, u32[]{:S(2)}) collective-permute-start(bf16[2,192,896]{2,1,0:T(8,128)(2,1)S(1)} %shard_map.88.refs_2_), channel_id=1, source_target_pairs={{0,16},{8,24},{16,0},{24,8},{1,17},{9,25},{17,1},{25,9},{2,18},{10... | collective-permute-start | bytes 2064392 | tf_op jit(solution)/shard_map/ppermute | solution.py:441
  62.1 22.2 %collective-permute-start.22 = (bf16[2,192,384]{2,1,0:T(8,128)(2,1)S(1)}, bf16[2,192,384]{2,1,0:T(8,128)(2,1)S(1)}, u32[]{:S(2)}, u32[]{:S(2)}) collective-permute-start(bf16[2,192,384]{2,1,0:T(8,128)(2,1)S(1)} %shard_map.89.refs_9_), channel_id=1, source_target_pairs={{0,16},{8,24},{16,0},{24,8},{1,17},{9,25},{17,1},{25,9},{2,18},{10... | collective-permute-start | bytes 884744 | tf_op jit(solution)/shard_map/ppermute | solution.py:441
  65.0 3.6 %collective-permute-start.17 = (f32[2,256]{1,0:T(2,128)S(1)}, f32[2,256]{1,0:T(2,128)S(1)}, u32[]{:S(2)}, u32[]{:S(2)}) collective-permute-start(f32[2,256]{1,0:T(2,128)S(1)} %get-tuple-element.61.refs_5_), channel_id=1, source_target_pairs={{0,1},{1,0},{2,3},{3,2},{4,5},{5,4},{6,7},{7,6},{8,9},{9,8},{10,11... | collective-permute-start | bytes 6152 | tf_op jit(solution)/shard_map/ppermute | solution.py:482
  68.6 11.8 %collective-permute-start.18 = (f32[2,2,256]{2,1,0:T(2,128)S(1)}, f32[2,2,256]{2,1,0:T(2,128)S(1)}, u32[]{:S(2)}, u32[]{:S(2)}) collective-permute-start(f32[2,2,256]{2,1,0:T(2,128)S(1)} %pad_maximum_fusion.refs_2_), channel_id=1, source_target_pairs={{2,0},{3,1},{4,2},{5,3},{6,4},{7,5},{0,6},{1,7},{10,8},{11,9},{12,... | collective-permute-start | bytes 12296 | tf_op jit(solution)/shard_map/ppermute | solution.py:484
  70.9 9.5 %collective-permute-start.19 = (f32[2,2,256]{2,1,0:T(2,128)S(1)}, f32[2,2,256]{2,1,0:T(2,128)S(1)}, u32[]{:S(2)}, u32[]{:S(2)}) collective-permute-start(f32[2,2,256]{2,1,0:T(2,128)S(1)} %pad_maximum_fusion.refs_2_), channel_id=1, source_target_pairs={{4,0},{5,1},{6,2},{7,3},{0,4},{1,5},{2,6},{3,7},{12,8},{13,9},{14,... | collective-permute-start | bytes 12296 | tf_op jit(solution)/shard_map/ppermute | solution.py:484
  71.2 9.2 %collective-permute-start.20 = (f32[2,2,256]{2,1,0:T(2,128)S(1)}, f32[2,2,256]{2,1,0:T(2,128)S(1)}, u32[]{:S(2)}, u32[]{:S(2)}) collective-permute-start(f32[2,2,256]{2,1,0:T(2,128)S(1)} %pad_maximum_fusion.refs_2_), channel_id=1, source_target_pairs={{6,0},{7,1},{0,2},{1,3},{2,4},{3,5},{4,6},{5,7},{14,8},{15,9},{8,1... | collective-permute-start | bytes 12296 | tf_op jit(solution)/shard_map/ppermute | solution.py:484
  (6 other events, 13.1 us)

commit v20 on v17

--- a/solution.py
+++ b/solution.py
@@ -295,7 +295,8 @@
 
 
 def cuts_of(share, first):
-    return [share // 3] * 3 if first else [share]
+    half = 16 * (share // 32)
+    return [half, share - half] if first else [share]
 
 
 sds = jax.ShapeDtypeStruct

time: 85.5 us -> 85.5 us (level)
  starting transfers between devices: 29.5 us -> 28 us
  waiting for transfers between devices: 39.2 us -> 40.7 us
    ppermute x6, waiting for transfers between devices: 23.3 us -> 24.8 us  [along(): return lax.ppermute(block, 'expert', pairs)]
    ppermute x5 -> x4, starting transfers between devices: 6.19 us -> 4.66 us  [paired(): others.append(lax.ppermute(pair, 'dp', shift))]
    ppermute x5 -> x4, waiting for transfers between devices: 8.48 us -> 8.48 us  [paired(): others.append(lax.ppermute(pair, 'dp', shift))]
  transfers between devices with their start and end apart: 23 -> 22, of which waited for: 12 -> 12; matrix products, arithmetic and copies ran while one was open for 0% -> 0% of each run, Pallas kernels for 11% -> 11%
where the time goes in v20:
time: 85.5 us; the launch traced here: 85.3 us
  waiting for transfers between devices  40.7 us (48%)
  starting transfers between devices  28 us (33%)
  Pallas kernels  14.7 us (17%)
  local copies, waits for them, and re-layouts  1.06 us (1%)
  between operations  0.89 us (1%)
    ppermute x6, waiting for transfers between devices, along(): return lax.ppermute(block, 'expert', pairs)  24.8 us
    pallas_call x20, Pallas kernels, __call__(): pl.pallas_call(body, out_shape=outs, in_specs=in_specs, compiler_params=p...  14.7 us
    ppermute x6, starting transfers between devices, along(): return lax.ppermute(block, 'expert', pairs)  11.1 us
    ppermute x4, waiting for transfers between devices, paired(): others.append(lax.ppermute(pair, 'dp', shift))  8.48 us
    ppermute x5, starting transfers between devices, pick(): lax.ppermute(other, 'expert', [(i, i ^ 1) for i in range(LINE * SIDES)])  6.7 us
    ppermute x4, starting transfers between devices, paired(): others.append(lax.ppermute(pair, 'dp', shift))  4.66 us
    ppermute x5, waiting for transfers between devices, pick(): lax.ppermute(other, 'expert', [(i, i ^ 1) for i in range(LINE * SIDES)])  3.45 us
    ppermute x3, starting transfers between devices, body(): lax.ppermute(both, 'expert', [(moved(i, d, 0), i) for i in range(groups)])  3.36 us
  transfers between devices with their start and end apart: 22, of which 12 were waited for; matrix products, arithmetic and copies ran while one was open for 0% of the time, Pallas kernels for 11%

profile of v20, /device:TPU:0, one launch (start us, length us, event | category | flops | bytes accessed | tf_op | source)
XLA Modules:
  0.0 85.3 jit_solution(4854119563244446454)
XLA Ops:
  0.6 1.9 %shard_map.76 = (s32[2,128]{1,0:T(2,128)}, bf16[144,768]{1,0:T(8,128)(2,1)}) custom-call(s32[2,128]{1,0:T(2,128)} %bitcast.13, f32[2,128]{1,0:T(2,128)} %bitcast.10, bf16[128,2048]{1,0:T(8,128)(2,1)} %refs_0_.3), custom_call_target="tpu_custom_call" | custom-call | flops 1 | bytes 1 | tf_op jit(solution)/shard_map/pallas_call | solution.py:43
  2.5 3.1 %collective-permute-start = (bf16[144,768]{1,0:T(8,128)(2,1)}, bf16[144,768]{1,0:T(8,128)(2,1)S(1)}, u32[]{:S(2)}, u32[]{:S(2)}) collective-permute-start(bf16[144,768]{1,0:T(8,128)(2,1)} %get-tuple-element.34.refs_0_), channel_id=1, source_target_pairs={{0,2},{1,3},{2,4},{3,5},{4,6},{5,7},{6,0},{7,1},{8,10},{9,11},{10,... | collective-permute-start | bytes 663560 | tf_op jit(solution)/shard_map/ppermute | solution.py:345
  5.6 2.1 %collective-permute-start.1 = (bf16[144,768]{1,0:T(8,128)(2,1)}, bf16[144,768]{1,0:T(8,128)(2,1)S(1)}, u32[]{:S(2)}, u32[]{:S(2)}) collective-permute-start(bf16[144,768]{1,0:T(8,128)(2,1)} %get-tuple-element.34.refs_0_), channel_id=1, source_target_pairs={{0,6},{1,7},{2,0},{3,1},{4,2},{5,3},{6,4},{7,5},{8,14},{9,15},{10,... | collective-permute-start | bytes 663560 | tf_op jit(solution)/shard_map/ppermute | solution.py:345
  7.7 6.4 %collective-permute-done.refs_1_ = bf16[144,768]{1,0:T(8,128)(2,1)S(1)} collective-permute-done((bf16[144,768]{1,0:T(8,128)(2,1)}, bf16[144,768]{1,0:T(8,128)(2,1)S(1)}, u32[]{:S(2)}, u32[]{:S(2)}) %collective-permute-start) | collective-permute-done | bytes 221216 | tf_op jit(solution)/shard_map/ppermute | solution.py:345
  15.3 4.1 %collective-permute-start.3 = (bf16[128,1280]{1,0:T(8,128)(2,1)S(1)}, bf16[128,1280]{1,0:T(8,128)(2,1)S(1)}, u32[]{:S(2)}, u32[]{:S(2)}) collective-permute-start(bf16[128,1280]{1,0:T(8,128)(2,1)S(1)} %shard_map.77.refs_1_.refs_0_), channel_id=1, source_target_pairs={{0,2},{1,3},{2,4},{3,5},{4,6},{5,7},{6,0},{7,1},{8,10},{9,11},{10,... | collective-permute-start | bytes 983048 | tf_op jit(solution)/shard_map/ppermute | solution.py:345
  20.6 1.6 %collective-permute-start.6 = (bf16[2,96,768]{2,1,0:T(8,128)(2,1)S(1)}, bf16[2,96,768]{2,1,0:T(8,128)(2,1)S(1)}, u32[]{:S(2)}, u32[]{:S(2)}) collective-permute-start(bf16[2,96,768]{2,1,0:T(8,128)(2,1)S(1)} %get-tuple-element.41), channel_id=1, source_target_pairs={{0,1},{1,0},{2,3},{3,2},{4,5},{5,4},{6,7},{7,6},{8,9},{9,8},{10,11... | collective-permute-start | bytes 884744 | tf_op jit(solution)/shard_map/ppermute | solution.py:356
  22.2 3.1 %collective-permute-done.2.refs_0_ = bf16[144,768]{1,0:T(8,128)(2,1)S(1)} collective-permute-done((bf16[144,768]{1,0:T(8,128)(2,1)S(1)}, bf16[144,768]{1,0:T(8,128)(2,1)S(1)}, u32[]{:S(2)}, u32[]{:S(2)}) %collective-permute-start.2) | collective-permute-done | bytes 221216 | tf_op jit(solution)/shard_map/ppermute | solution.py:345
  25.7 1.6 %collective-permute-start.8 = (bf16[2,32,1280]{2,1,0:T(8,128)(2,1)S(1)}, bf16[2,32,1280]{2,1,0:T(8,128)(2,1)S(1)}, u32[]{:S(2)}, u32[]{:S(2)}) collective-permute-start(bf16[2,32,1280]{2,1,0:T(8,128)(2,1)S(1)} %get-tuple-element.43), channel_id=1, source_target_pairs={{0,1},{1,0},{2,3},{3,2},{4,5},{5,4},{6,7},{7,6},{8,9},{9,8},{10,11... | collective-permute-start | bytes 491528 | tf_op jit(solution)/shard_map/ppermute | solution.py:356
  27.8 4.4 %collective-permute-done.3.refs_0_ = bf16[128,1280]{1,0:T(8,128)(2,1)S(1)} collective-permute-done((bf16[128,1280]{1,0:T(8,128)(2,1)S(1)}, bf16[128,1280]{1,0:T(8,128)(2,1)S(1)}, u32[]{:S(2)}, u32[]{:S(2)}) %collective-permute-start.3) | collective-permute-done | bytes 327712 | tf_op jit(solution)/shard_map/ppermute | solution.py:345
  32.2 4.1 %collective-permute-done.4.refs_1_ = bf16[128,1280]{1,0:T(8,128)(2,1)S(1)} collective-permute-done((bf16[128,1280]{1,0:T(8,128)(2,1)S(1)}, bf16[128,1280]{1,0:T(8,128)(2,1)S(1)}, u32[]{:S(2)}, u32[]{:S(2)}) %collective-permute-start.4) | collective-permute-done | bytes 327712 | tf_op jit(solution)/shard_map/ppermute | solution.py:345
  38.6 1.5 %collective-permute-start.10 = (bf16[2,64,1280]{2,1,0:T(8,128)(2,1)S(1)}, bf16[2,64,1280]{2,1,0:T(8,128)(2,1)S(1)}, u32[]{:S(2)}, u32[]{:S(2)}) collective-permute-start(bf16[2,64,1280]{2,1,0:T(8,128)(2,1)S(1)} %get-tuple-element.48), channel_id=1, source_target_pairs={{0,1},{1,0},{2,3},{3,2},{4,5},{5,4},{6,7},{7,6},{8,9},{9,8},{10,11... | collective-permute-start | bytes 983048 | tf_op jit(solution)/shard_map/ppermute | solution.py:356
  40.5 1.6 %collective-permute-start.12 = (bf16[2,96,768]{2,1,0:T(8,128)(2,1)S(1)}, bf16[2,96,768]{2,1,0:T(8,128)(2,1)S(1)}, u32[]{:S(2)}, u32[]{:S(2)}) collective-permute-start(bf16[2,96,768]{2,1,0:T(8,128)(2,1)S(1)} %get-tuple-element.46.refs_2_), channel_id=1, source_target_pairs={{0,16},{8,24},{16,0},{24,8},{1,17},{9,25},{17,1},{25,9},{2,18},{10... | collective-permute-start | bytes 884744 | tf_op jit(solution)/shard_map/ppermute | solution.py:459
  42.5 6.8 %collective-permute-done.5.refs_0_ = bf16[128,1280]{1,0:T(8,128)(2,1)S(1)} collective-permute-done((bf16[128,1280]{1,0:T(8,128)(2,1)S(1)}, bf16[128,1280]{1,0:T(8,128)(2,1)S(1)}, u32[]{:S(2)}, u32[]{:S(2)}) %collective-permute-start.5) | collective-permute-done | bytes 327712 | tf_op jit(solution)/shard_map/ppermute | solution.py:345
  49.6 1.6 %collective-permute-start.11 = (bf16[2,32,1280]{2,1,0:T(8,128)(2,1)S(1)}, bf16[2,32,1280]{2,1,0:T(8,128)(2,1)S(1)}, u32[]{:S(2)}, u32[]{:S(2)}) collective-permute-start(bf16[2,32,1280]{2,1,0:T(8,128)(2,1)S(1)} %get-tuple-element.49), channel_id=1, source_target_pairs={{0,1},{1,0},{2,3},{3,2},{4,5},{5,4},{6,7},{7,6},{8,9},{9,8},{10,11... | collective-permute-start | bytes 491528 | tf_op jit(solution)/shard_map/ppermute | solution.py:356
  52.0 3.4 %collective-permute-done.11.refs_6_ = bf16[2,32,1280]{2,1,0:T(8,128)(2,1)S(1)} collective-permute-done((bf16[2,32,1280]{2,1,0:T(8,128)(2,1)S(1)}, bf16[2,32,1280]{2,1,0:T(8,128)(2,1)S(1)}, u32[]{:S(2)}, u32[]{:S(2)}) %collective-permute-start.11) | collective-permute-done | bytes 163872 | tf_op jit(solution)/shard_map/ppermute | solution.py:356
  57.9 1.7 %collective-permute-done.15.refs_1_ = bf16[2,2,192,768]{3,2,1,0:T(8,128)(2,1)S(1)} collective-permute-done((bf16[2,2,192,768]{3,2,1,0:T(8,128)(2,1)S(1)}, bf16[2,2,192,768]{3,2,1,0:T(8,128)(2,1)S(1)}, u32[]{:S(2)}, u32[]{:S(2)}) %collective-permute-start.15) | collective-permute-done | bytes 1179680 | tf_op jit(solution)/shard_map/ppermute | solution.py:448
  59.7 1.6 %collective-permute-start.20 = (bf16[2,192,768]{2,1,0:T(8,128)(2,1)S(1)}, bf16[2,192,768]{2,1,0:T(8,128)(2,1)S(1)}, u32[]{:S(2)}, u32[]{:S(2)}) collective-permute-start(bf16[2,192,768]{2,1,0:T(8,128)(2,1)S(1)} %shard_map.89.refs_2_), channel_id=1, source_target_pairs={{0,16},{8,24},{16,0},{24,8},{1,17},{9,25},{17,1},{25,9},{2,18},{10... | collective-permute-start | bytes 1769480 | tf_op jit(solution)/shard_map/ppermute | solution.py:459
  62.4 2.2 %shard_map.91 = (bf16[8,2,32,768]{3,2,1,0:T(8,128)(2,1)}, f32[2,256]{1,0:T(2,128)S(1)}) custom-call(bf16[2,768,2048]{2,1,0:T(8,128)(2,1)S(1)} %copy-done, bf16[2,32,1280]{2,1,0:T(8,128)(2,1)S(1)} %get-tuple-element.37.refs_3_.refs_1_, bf16[2,64,1280]{2,1,0:T(8,128)(2,1)S(1)} %get-tuple-element.38.refs_5_.refs_2_, ...), custom_call_target="tpu_custom_call" | custom-call | flops 1 | bytes 1 | tf_op jit(solution)/shard_map/pallas_call | solution.py:43
  64.6 1.5 %collective-permute-start.16 = (f32[2,256]{1,0:T(2,128)S(1)}, f32[2,256]{1,0:T(2,128)S(1)}, u32[]{:S(2)}, u32[]{:S(2)}) collective-permute-start(f32[2,256]{1,0:T(2,128)S(1)} %get-tuple-element.57.refs_4_), channel_id=1, source_target_pairs={{0,1},{1,0},{2,3},{3,2},{4,5},{5,4},{6,7},{7,6},{8,9},{9,8},{10,11... | collective-permute-start | bytes 6152 | tf_op jit(solution)/shard_map/ppermute | solution.py:500
  66.1 2.1 %collective-permute-done.16 = f32[2,256]{1,0:T(2,128)S(1)} collective-permute-done((f32[2,256]{1,0:T(2,128)S(1)}, f32[2,256]{1,0:T(2,128)S(1)}, u32[]{:S(2)}, u32[]{:S(2)}) %collective-permute-start.16) | collective-permute-done | bytes 2080 | tf_op jit(solution)/shard_map/ppermute | solution.py:500
  68.2 2.3 %collective-permute-start.17 = (f32[2,2,256]{2,1,0:T(2,128)S(1)}, f32[2,2,256]{2,1,0:T(2,128)S(1)}, u32[]{:S(2)}, u32[]{:S(2)}) collective-permute-start(f32[2,2,256]{2,1,0:T(2,128)S(1)} %pad_maximum_fusion.refs_2_), channel_id=1, source_target_pairs={{2,0},{3,1},{4,2},{5,3},{6,4},{7,5},{0,6},{1,7},{10,8},{11,9},{12,... | collective-permute-start | bytes 12296 | tf_op jit(solution)/shard_map/ppermute | solution.py:502
  73.0 2.9 %collective-permute-done.20.refs_2_ = bf16[2,192,768]{2,1,0:T(8,128)(2,1)S(1)} collective-permute-done((bf16[2,192,768]{2,1,0:T(8,128)(2,1)S(1)}, bf16[2,192,768]{2,1,0:T(8,128)(2,1)S(1)}, u32[]{:S(2)}, u32[]{:S(2)}) %collective-permute-start.20) | collective-permute-done | bytes 589856 | tf_op jit(solution)/shard_map/ppermute | solution.py:459
  78.5 5.1 %collective-permute-done.21.refs_2_ = bf16[2,192,512]{2,1,0:T(8,128)(2,1)S(1)} collective-permute-done((bf16[2,192,512]{2,1,0:T(8,128)(2,1)S(1)}, bf16[2,192,512]{2,1,0:T(8,128)(2,1)S(1)}, u32[]{:S(2)}, u32[]{:S(2)}) %collective-permute-start.21) | collective-permute-done | bytes 393248 | tf_op jit(solution)/shard_map/ppermute | solution.py:459
  83.6 1.7 %shard_map.95 = (f32[192,2,2048]{2,1,0:T(2,128)}, f32[8,128]{1,0:T(8,128)}) custom-call(bf16[2,2,192,512]{3,2,1,0:T(8,128)(2,1)S(1)} %get-tuple-element.52.refs_2_.refs_0_, bf16[2,2,192,512]{3,2,1,0:T(8,128)(2,1)S(1)} %collective-permute-done.14.refs_1_, bf16[2,192,512]{2,1,0:T(8,128)(2,1)S(1)} %collective-permute-done.21.refs_2_, ...), custom_call_target="tpu_custom_call", output_to_operand_aliasing={{0}: (3, {})} | custom-call | flops 1 | bytes 1 | tf_op jit(solution)/shard_map/pallas_call | solution.py:43
  (53 shorter events, 16.1 us)
Async XLA Ops:
  0.6 19.4 %copy-start.1 = (bf16[1,8,2,32,768]{4,3,2,1,0:T(8,128)(2,1)S(1)}, bf16[1,8,2,32,768]{4,3,2,1,0:T(8,128)(2,1)}, u32[]{:S(2)}) copy-start(bf16[1,8,2,32,768]{4,3,2,1,0:T(8,128)(2,1)} %param.8) | copy-start | bytes 2359300
  2.5 11.6 %collective-permute-start = (bf16[144,768]{1,0:T(8,128)(2,1)}, bf16[144,768]{1,0:T(8,128)(2,1)S(1)}, u32[]{:S(2)}, u32[]{:S(2)}) collective-permute-start(bf16[144,768]{1,0:T(8,128)(2,1)} %get-tuple-element.34.refs_0_), channel_id=1, source_target_pairs={{0,2},{1,3},{2,4},{3,5},{4,6},{5,7},{6,0},{7,1},{8,10},{9,11},{10,... | collective-permute-start | bytes 663560 | tf_op jit(solution)/shard_map/ppermute | solution.py:345
  5.6 14.7 %collective-permute-start.1 = (bf16[144,768]{1,0:T(8,128)(2,1)}, bf16[144,768]{1,0:T(8,128)(2,1)S(1)}, u32[]{:S(2)}, u32[]{:S(2)}) collective-permute-start(bf16[144,768]{1,0:T(8,128)(2,1)} %get-tuple-element.34.refs_0_), channel_id=1, source_target_pairs={{0,6},{1,7},{2,0},{3,1},{4,2},{5,3},{6,4},{7,5},{8,14},{9,15},{10,... | collective-permute-start | bytes 663560 | tf_op jit(solution)/shard_map/ppermute | solution.py:345
  14.1 11.1 %collective-permute-start.2 = (bf16[144,768]{1,0:T(8,128)(2,1)S(1)}, bf16[144,768]{1,0:T(8,128)(2,1)S(1)}, u32[]{:S(2)}, u32[]{:S(2)}) collective-permute-start(bf16[144,768]{1,0:T(8,128)(2,1)S(1)} %collective-permute-done.refs_1_), channel_id=1, source_target_pairs={{0,2},{1,3},{2,4},{3,5},{4,6},{5,7},{6,0},{7,1},{8,10},{9,11},{10,... | collective-permute-start | bytes 663560 | tf_op jit(solution)/shard_map/ppermute | solution.py:345
  15.3 16.9 %collective-permute-start.3 = (bf16[128,1280]{1,0:T(8,128)(2,1)S(1)}, bf16[128,1280]{1,0:T(8,128)(2,1)S(1)}, u32[]{:S(2)}, u32[]{:S(2)}) collective-permute-start(bf16[128,1280]{1,0:T(8,128)(2,1)S(1)} %shard_map.77.refs_1_.refs_0_), channel_id=1, source_target_pairs={{0,2},{1,3},{2,4},{3,5},{4,6},{5,7},{6,0},{7,1},{8,10},{9,11},{10,... | collective-permute-start | bytes 983048 | tf_op jit(solution)/shard_map/ppermute | solution.py:345
  19.4 16.9 %collective-permute-start.4 = (bf16[128,1280]{1,0:T(8,128)(2,1)S(1)}, bf16[128,1280]{1,0:T(8,128)(2,1)S(1)}, u32[]{:S(2)}, u32[]{:S(2)}) collective-permute-start(bf16[128,1280]{1,0:T(8,128)(2,1)S(1)} %shard_map.77.refs_1_.refs_0_), channel_id=1, source_target_pairs={{0,6},{1,7},{2,0},{3,1},{4,2},{5,3},{6,4},{7,5},{8,14},{9,15},{10,... | collective-permute-start | bytes 983048 | tf_op jit(solution)/shard_map/ppermute | solution.py:345
  20.6 16.0 %collective-permute-start.6 = (bf16[2,96,768]{2,1,0:T(8,128)(2,1)S(1)}, bf16[2,96,768]{2,1,0:T(8,128)(2,1)S(1)}, u32[]{:S(2)}, u32[]{:S(2)}) collective-permute-start(bf16[2,96,768]{2,1,0:T(8,128)(2,1)S(1)} %get-tuple-element.41), channel_id=1, source_target_pairs={{0,1},{1,0},{2,3},{3,2},{4,5},{5,4},{6,7},{7,6},{8,9},{9,8},{10,11... | collective-permute-start | bytes 884744 | tf_op jit(solution)/shard_map/ppermute | solution.py:356
  25.7 10.9 %collective-permute-start.8 = (bf16[2,32,1280]{2,1,0:T(8,128)(2,1)S(1)}, bf16[2,32,1280]{2,1,0:T(8,128)(2,1)S(1)}, u32[]{:S(2)}, u32[]{:S(2)}) collective-permute-start(bf16[2,32,1280]{2,1,0:T(8,128)(2,1)S(1)} %get-tuple-element.43), channel_id=1, source_target_pairs={{0,1},{1,0},{2,3},{3,2},{4,5},{5,4},{6,7},{7,6},{8,9},{9,8},{10,11... | collective-permute-start | bytes 491528 | tf_op jit(solution)/shard_map/ppermute | solution.py:356
  27.2 9.3 %collective-permute-start.7 = (bf16[2,32,768]{2,1,0:T(8,128)(2,1)S(1)}, bf16[2,32,768]{2,1,0:T(8,128)(2,1)S(1)}, u32[]{:S(2)}, u32[]{:S(2)}) collective-permute-start(bf16[2,32,768]{2,1,0:T(8,128)(2,1)S(1)} %get-tuple-element.42), channel_id=1, source_target_pairs={{0,1},{1,0},{2,3},{3,2},{4,5},{5,4},{6,7},{7,6},{8,9},{9,8},{10,11... | collective-permute-start | bytes 294920 | tf_op jit(solution)/shard_map/ppermute | solution.py:356
  36.2 14.9 %copy-start = (bf16[2,768,2048]{2,1,0:T(8,128)(2,1)S(1)}, bf16[2,768,2048]{2,1,0:T(8,128)(2,1)}, u32[]{:S(2)}) copy-start(bf16[2,768,2048]{2,1,0:T(8,128)(2,1)} %refs_0_.5) | copy-start | bytes 18874372
  37.4 2.9 %collective-permute-start.9 = (bf16[2,2,192,768]{3,2,1,0:T(8,128)(2,1)S(1)}, bf16[2,2,192,768]{3,2,1,0:T(8,128)(2,1)S(1)}, u32[]{:S(2)}, u32[]{:S(2)}) collective-permute-start(bf16[2,2,192,768]{3,2,1,0:T(8,128)(2,1)S(1)} %get-tuple-element.45), channel_id=1, source_target_pairs={{0,8},{8,0},{16,24},{24,16},{1,9},{9,1},{17,25},{25,17},{2,10},{10... | collective-permute-start | bytes 3538952 | tf_op jit(solution)/shard_map/ppermute | solution.py:448
  37.5 11.9 %collective-permute-start.5 = (bf16[128,1280]{1,0:T(8,128)(2,1)S(1)}, bf16[128,1280]{1,0:T(8,128)(2,1)S(1)}, u32[]{:S(2)}, u32[]{:S(2)}) collective-permute-start(bf16[128,1280]{1,0:T(8,128)(2,1)S(1)} %collective-permute-done.3.refs_0_), channel_id=1, source_target_pairs={{0,2},{1,3},{2,4},{3,5},{4,6},{5,7},{6,0},{7,1},{8,10},{9,11},{10,... | collective-permute-start | bytes 983048 | tf_op jit(solution)/shard_map/ppermute | solution.py:345
  38.6 13.3 %collective-permute-start.10 = (bf16[2,64,1280]{2,1,0:T(8,128)(2,1)S(1)}, bf16[2,64,1280]{2,1,0:T(8,128)(2,1)S(1)}, u32[]{:S(2)}, u32[]{:S(2)}) collective-permute-start(bf16[2,64,1280]{2,1,0:T(8,128)(2,1)S(1)} %get-tuple-element.48), channel_id=1, source_target_pairs={{0,1},{1,0},{2,3},{3,2},{4,5},{5,4},{6,7},{7,6},{8,9},{9,8},{10,11... | collective-permute-start | bytes 983048 | tf_op jit(solution)/shard_map/ppermute | solution.py:356
  40.5 15.0 %collective-permute-start.12 = (bf16[2,96,768]{2,1,0:T(8,128)(2,1)S(1)}, bf16[2,96,768]{2,1,0:T(8,128)(2,1)S(1)}, u32[]{:S(2)}, u32[]{:S(2)}) collective-permute-start(bf16[2,96,768]{2,1,0:T(8,128)(2,1)S(1)} %get-tuple-element.46.refs_2_), channel_id=1, source_target_pairs={{0,16},{8,24},{16,0},{24,8},{1,17},{9,25},{17,1},{25,9},{2,18},{10... | collective-permute-start | bytes 884744 | tf_op jit(solution)/shard_map/ppermute | solution.py:459
  42.1 13.8 %collective-permute-start.13 = (bf16[2,96,768]{2,1,0:T(8,128)(2,1)S(1)}, bf16[2,96,768]{2,1,0:T(8,128)(2,1)S(1)}, u32[]{:S(2)}, u32[]{:S(2)}) collective-permute-start(bf16[2,96,768]{2,1,0:T(8,128)(2,1)S(1)} %get-tuple-element.50), channel_id=1, source_target_pairs={{0,16},{8,24},{16,0},{24,8},{1,17},{9,25},{17,1},{25,9},{2,18},{10... | collective-permute-start | bytes 884744 | tf_op jit(solution)/shard_map/ppermute | solution.py:459
  49.6 5.8 %collective-permute-start.11 = (bf16[2,32,1280]{2,1,0:T(8,128)(2,1)S(1)}, bf16[2,32,1280]{2,1,0:T(8,128)(2,1)S(1)}, u32[]{:S(2)}, u32[]{:S(2)}) collective-permute-start(bf16[2,32,1280]{2,1,0:T(8,128)(2,1)S(1)} %get-tuple-element.49), channel_id=1, source_target_pairs={{0,1},{1,0},{2,3},{3,2},{4,5},{5,4},{6,7},{7,6},{8,9},{9,8},{10,11... | collective-permute-start | bytes 491528 | tf_op jit(solution)/shard_map/ppermute | solution.py:356
  56.7 2.9 %collective-permute-start.15 = (bf16[2,2,192,768]{3,2,1,0:T(8,128)(2,1)S(1)}, bf16[2,2,192,768]{3,2,1,0:T(8,128)(2,1)S(1)}, u32[]{:S(2)}, u32[]{:S(2)}) collective-permute-start(bf16[2,2,192,768]{3,2,1,0:T(8,128)(2,1)S(1)} %get-tuple-element.54), channel_id=1, source_target_pairs={{0,8},{8,0},{16,24},{24,16},{1,9},{9,1},{17,25},{25,17},{2,10},{10... | collective-permute-start | bytes 3538952 | tf_op jit(solution)/shard_map/ppermute | solution.py:448
  57.3 4.0 %collective-permute-start.14 = (bf16[2,2,192,512]{3,2,1,0:T(8,128)(2,1)S(1)}, bf16[2,2,192,512]{3,2,1,0:T(8,128)(2,1)S(1)}, u32[]{:S(2)}, u32[]{:S(2)}) collective-permute-start(bf16[2,2,192,512]{3,2,1,0:T(8,128)(2,1)S(1)} %get-tuple-element.53), channel_id=1, source_target_pairs={{0,8},{8,0},{16,24},{24,16},{1,9},{9,1},{17,25},{25,17},{2,10},{10... | collective-permute-start | bytes 2359304 | tf_op jit(solution)/shard_map/ppermute | solution.py:448
  59.7 16.2 %collective-permute-start.20 = (bf16[2,192,768]{2,1,0:T(8,128)(2,1)S(1)}, bf16[2,192,768]{2,1,0:T(8,128)(2,1)S(1)}, u32[]{:S(2)}, u32[]{:S(2)}) collective-permute-start(bf16[2,192,768]{2,1,0:T(8,128)(2,1)S(1)} %shard_map.89.refs_2_), channel_id=1, source_target_pairs={{0,16},{8,24},{16,0},{24,8},{1,17},{9,25},{17,1},{25,9},{2,18},{10... | collective-permute-start | bytes 1769480 | tf_op jit(solution)/shard_map/ppermute | solution.py:459
  61.4 22.2 %collective-permute-start.21 = (bf16[2,192,512]{2,1,0:T(8,128)(2,1)S(1)}, bf16[2,192,512]{2,1,0:T(8,128)(2,1)S(1)}, u32[]{:S(2)}, u32[]{:S(2)}) collective-permute-start(bf16[2,192,512]{2,1,0:T(8,128)(2,1)S(1)} %shard_map.90.refs_9_), channel_id=1, source_target_pairs={{0,16},{8,24},{16,0},{24,8},{1,17},{9,25},{17,1},{25,9},{2,18},{10... | collective-permute-start | bytes 1179656 | tf_op jit(solution)/shard_map/ppermute | solution.py:459
  64.6 3.6 %collective-permute-start.16 = (f32[2,256]{1,0:T(2,128)S(1)}, f32[2,256]{1,0:T(2,128)S(1)}, u32[]{:S(2)}, u32[]{:S(2)}) collective-permute-start(f32[2,256]{1,0:T(2,128)S(1)} %get-tuple-element.57.refs_4_), channel_id=1, source_target_pairs={{0,1},{1,0},{2,3},{3,2},{4,5},{5,4},{6,7},{7,6},{8,9},{9,8},{10,11... | collective-permute-start | bytes 6152 | tf_op jit(solution)/shard_map/ppermute | solution.py:500
  68.2 9.2 %collective-permute-start.17 = (f32[2,2,256]{2,1,0:T(2,128)S(1)}, f32[2,2,256]{2,1,0:T(2,128)S(1)}, u32[]{:S(2)}, u32[]{:S(2)}) collective-permute-start(f32[2,2,256]{2,1,0:T(2,128)S(1)} %pad_maximum_fusion.refs_2_), channel_id=1, source_target_pairs={{2,0},{3,1},{4,2},{5,3},{6,4},{7,5},{0,6},{1,7},{10,8},{11,9},{12,... | collective-permute-start | bytes 12296 | tf_op jit(solution)/shard_map/ppermute | solution.py:502
  70.5 6.9 %collective-permute-start.18 = (f32[2,2,256]{2,1,0:T(2,128)S(1)}, f32[2,2,256]{2,1,0:T(2,128)S(1)}, u32[]{:S(2)}, u32[]{:S(2)}) collective-permute-start(f32[2,2,256]{2,1,0:T(2,128)S(1)} %pad_maximum_fusion.refs_2_), channel_id=1, source_target_pairs={{4,0},{5,1},{6,2},{7,3},{0,4},{1,5},{2,6},{3,7},{12,8},{13,9},{14,... | collective-permute-start | bytes 12296 | tf_op jit(solution)/shard_map/ppermute | solution.py:502
  70.8 6.7 %collective-permute-start.19 = (f32[2,2,256]{2,1,0:T(2,128)S(1)}, f32[2,2,256]{2,1,0:T(2,128)S(1)}, u32[]{:S(2)}, u32[]{:S(2)}) collective-permute-start(f32[2,2,256]{2,1,0:T(2,128)S(1)} %pad_maximum_fusion.refs_2_), channel_id=1, source_target_pairs={{6,0},{7,1},{0,2},{1,3},{2,4},{3,5},{4,6},{5,7},{14,8},{15,9},{8,1... | collective-permute-start | bytes 12296 | tf_op jit(solution)/shard_map/ppermute | solution.py:502
  (4 other events, 9.1 us)

commit v21 on v20

--- a/solution.py
+++ b/solution.py
@@ -291,7 +291,7 @@
 
 def chunks_of(features):
     unit = features // 16
-    return [[6 * unit], [6 * unit, 4 * unit]]
+    return [[6 * unit], [5 * unit, 5 * unit]]
 
 
 def cuts_of(share, first):

time: 85.5 us -> 85.4 us (level)
  waiting for transfers between devices: 40.7 us -> 38 us
  local copies, waits for them, and re-layouts: 1.06 us -> 3.13 us
    unnamed x12 -> x14, local copies, waits for them, and re-layouts: 1.06 us -> 3.13 us
    ppermute x6, waiting for transfers between devices: 24.8 us -> 22.8 us  [along(): return lax.ppermute(block, 'expert', pairs)]
    ppermute x4, waiting for transfers between devices: 8.48 us -> 7.03 us  [paired(): others.append(lax.ppermute(pair, 'dp', shift))]
    ppermute x3, waiting for transfers between devices: 0.01 us -> 1.26 us  [body(): lax.ppermute(both, 'expert', [(moved(i, d, 0), i) for i in range(groups)])]
  transfers between devices with their start and end apart: 22 -> 22, of which waited for: 12 -> 14; matrix products, arithmetic and copies ran while one was open for 0% -> 0% of each run, Pallas kernels for 11% -> 11%
where the time goes in v21:
time: 85.4 us; the launch traced here: 85.2 us
  waiting for transfers between devices  38 us (44%)
  starting transfers between devices  28.3 us (33%)
  Pallas kernels  15 us (18%)
  local copies, waits for them, and re-layouts  3.13 us (4%)
  between operations  0.86 us (1%)
    ppermute x6, waiting for transfers between devices, along(): return lax.ppermute(block, 'expert', pairs)  22.8 us
    pallas_call x20, Pallas kernels, __call__(): pl.pallas_call(body, out_shape=outs, in_specs=in_specs, compiler_params=p...  15 us
    ppermute x6, starting transfers between devices, along(): return lax.ppermute(block, 'expert', pairs)  11.1 us
    ppermute x4, waiting for transfers between devices, paired(): others.append(lax.ppermute(pair, 'dp', shift))  7.03 us
    ppermute x5, starting transfers between devices, pick(): lax.ppermute(other, 'expert', [(i, i ^ 1) for i in range(LINE * SIDES)])  6.7 us
    ppermute x4, starting transfers between devices, paired(): others.append(lax.ppermute(pair, 'dp', shift))  4.93 us
    ppermute x5, waiting for transfers between devices, pick(): lax.ppermute(other, 'expert', [(i, i ^ 1) for i in range(LINE * SIDES)])  3.45 us
    ppermute x3, starting transfers between devices, body(): lax.ppermute(both, 'expert', [(moved(i, d, 0), i) for i in range(groups)])  3.36 us
  transfers between devices with their start and end apart: 22, of which 14 were waited for; matrix products, arithmetic and copies ran while one was open for 0% of the time, Pallas kernels for 11%

profile of v21, /device:TPU:0, one launch (start us, length us, event | category | flops | bytes accessed | tf_op | source)
XLA Modules:
  0.0 85.2 jit_solution(13479818278166479183)
XLA Ops:
  0.6 1.8 %shard_map.76 = (s32[2,128]{1,0:T(2,128)}, bf16[144,768]{1,0:T(8,128)(2,1)}) custom-call(s32[2,128]{1,0:T(2,128)} %bitcast.13, f32[2,128]{1,0:T(2,128)} %bitcast.10, bf16[128,2048]{1,0:T(8,128)(2,1)} %refs_0_.3), custom_call_target="tpu_custom_call" | custom-call | flops 1 | bytes 1 | tf_op jit(solution)/shard_map/pallas_call | solution.py:43
  2.5 3.1 %collective-permute-start = (bf16[144,768]{1,0:T(8,128)(2,1)}, bf16[144,768]{1,0:T(8,128)(2,1)S(1)}, u32[]{:S(2)}, u32[]{:S(2)}) collective-permute-start(bf16[144,768]{1,0:T(8,128)(2,1)} %get-tuple-element.34.refs_0_), channel_id=1, source_target_pairs={{0,2},{1,3},{2,4},{3,5},{4,6},{5,7},{6,0},{7,1},{8,10},{9,11},{10,... | collective-permute-start | bytes 663560 | tf_op jit(solution)/shard_map/ppermute | solution.py:345
  5.5 2.1 %collective-permute-start.1 = (bf16[144,768]{1,0:T(8,128)(2,1)}, bf16[144,768]{1,0:T(8,128)(2,1)S(1)}, u32[]{:S(2)}, u32[]{:S(2)}) collective-permute-start(bf16[144,768]{1,0:T(8,128)(2,1)} %get-tuple-element.34.refs_0_), channel_id=1, source_target_pairs={{0,6},{1,7},{2,0},{3,1},{4,2},{5,3},{6,4},{7,5},{8,14},{9,15},{10,... | collective-permute-start | bytes 663560 | tf_op jit(solution)/shard_map/ppermute | solution.py:345
  7.6 6.4 %collective-permute-done.refs_1_ = bf16[144,768]{1,0:T(8,128)(2,1)S(1)} collective-permute-done((bf16[144,768]{1,0:T(8,128)(2,1)}, bf16[144,768]{1,0:T(8,128)(2,1)S(1)}, u32[]{:S(2)}, u32[]{:S(2)}) %collective-permute-start) | collective-permute-done | bytes 221216 | tf_op jit(solution)/shard_map/ppermute | solution.py:345
  15.2 4.1 %collective-permute-start.3 = (bf16[128,1280]{1,0:T(8,128)(2,1)S(1)}, bf16[128,1280]{1,0:T(8,128)(2,1)S(1)}, u32[]{:S(2)}, u32[]{:S(2)}) collective-permute-start(bf16[128,1280]{1,0:T(8,128)(2,1)S(1)} %shard_map.77.refs_1_.refs_0_), channel_id=1, source_target_pairs={{0,2},{1,3},{2,4},{3,5},{4,6},{5,7},{6,0},{7,1},{8,10},{9,11},{10,... | collective-permute-start | bytes 983048 | tf_op jit(solution)/shard_map/ppermute | solution.py:345
  22.6 1.6 %collective-permute-start.6 = (bf16[2,96,768]{2,1,0:T(8,128)(2,1)S(1)}, bf16[2,96,768]{2,1,0:T(8,128)(2,1)S(1)}, u32[]{:S(2)}, u32[]{:S(2)}) collective-permute-start(bf16[2,96,768]{2,1,0:T(8,128)(2,1)S(1)} %get-tuple-element.41), channel_id=1, source_target_pairs={{0,1},{1,0},{2,3},{3,2},{4,5},{5,4},{6,7},{7,6},{8,9},{9,8},{10,11... | collective-permute-start | bytes 884744 | tf_op jit(solution)/shard_map/ppermute | solution.py:356
  25.6 1.6 %collective-permute-start.8 = (bf16[2,32,1280]{2,1,0:T(8,128)(2,1)S(1)}, bf16[2,32,1280]{2,1,0:T(8,128)(2,1)S(1)}, u32[]{:S(2)}, u32[]{:S(2)}) collective-permute-start(bf16[2,32,1280]{2,1,0:T(8,128)(2,1)S(1)} %get-tuple-element.43), channel_id=1, source_target_pairs={{0,1},{1,0},{2,3},{3,2},{4,5},{5,4},{6,7},{7,6},{8,9},{9,8},{10,11... | collective-permute-start | bytes 491528 | tf_op jit(solution)/shard_map/ppermute | solution.py:356
  27.7 4.4 %collective-permute-done.3.refs_0_ = bf16[128,1280]{1,0:T(8,128)(2,1)S(1)} collective-permute-done((bf16[128,1280]{1,0:T(8,128)(2,1)S(1)}, bf16[128,1280]{1,0:T(8,128)(2,1)S(1)}, u32[]{:S(2)}, u32[]{:S(2)}) %collective-permute-start.3) | collective-permute-done | bytes 327712 | tf_op jit(solution)/shard_map/ppermute | solution.py:345
  32.1 4.1 %collective-permute-done.4.refs_1_ = bf16[128,1280]{1,0:T(8,128)(2,1)S(1)} collective-permute-done((bf16[128,1280]{1,0:T(8,128)(2,1)S(1)}, bf16[128,1280]{1,0:T(8,128)(2,1)S(1)}, u32[]{:S(2)}, u32[]{:S(2)}) %collective-permute-start.4) | collective-permute-done | bytes 327712 | tf_op jit(solution)/shard_map/ppermute | solution.py:345
  38.6 1.5 %collective-permute-start.10 = (bf16[2,64,1280]{2,1,0:T(8,128)(2,1)S(1)}, bf16[2,64,1280]{2,1,0:T(8,128)(2,1)S(1)}, u32[]{:S(2)}, u32[]{:S(2)}) collective-permute-start(bf16[2,64,1280]{2,1,0:T(8,128)(2,1)S(1)} %get-tuple-element.48), channel_id=1, source_target_pairs={{0,1},{1,0},{2,3},{3,2},{4,5},{5,4},{6,7},{7,6},{8,9},{9,8},{10,11... | collective-permute-start | bytes 983048 | tf_op jit(solution)/shard_map/ppermute | solution.py:356
  40.4 1.6 %collective-permute-start.12 = (bf16[2,96,768]{2,1,0:T(8,128)(2,1)S(1)}, bf16[2,96,768]{2,1,0:T(8,128)(2,1)S(1)}, u32[]{:S(2)}, u32[]{:S(2)}) collective-permute-start(bf16[2,96,768]{2,1,0:T(8,128)(2,1)S(1)} %get-tuple-element.46.refs_2_), channel_id=1, source_target_pairs={{0,16},{8,24},{16,0},{24,8},{1,17},{9,25},{17,1},{25,9},{2,18},{10... | collective-permute-start | bytes 884744 | tf_op jit(solution)/shard_map/ppermute | solution.py:459
  42.5 6.8 %collective-permute-done.5.refs_0_ = bf16[128,1280]{1,0:T(8,128)(2,1)S(1)} collective-permute-done((bf16[128,1280]{1,0:T(8,128)(2,1)S(1)}, bf16[128,1280]{1,0:T(8,128)(2,1)S(1)}, u32[]{:S(2)}, u32[]{:S(2)}) %collective-permute-start.5) | collective-permute-done | bytes 327712 | tf_op jit(solution)/shard_map/ppermute | solution.py:345
  49.5 1.6 %collective-permute-start.11 = (bf16[2,32,1280]{2,1,0:T(8,128)(2,1)S(1)}, bf16[2,32,1280]{2,1,0:T(8,128)(2,1)S(1)}, u32[]{:S(2)}, u32[]{:S(2)}) collective-permute-start(bf16[2,32,1280]{2,1,0:T(8,128)(2,1)S(1)} %get-tuple-element.49), channel_id=1, source_target_pairs={{0,1},{1,0},{2,3},{3,2},{4,5},{5,4},{6,7},{7,6},{8,9},{9,8},{10,11... | collective-permute-start | bytes 491528 | tf_op jit(solution)/shard_map/ppermute | solution.py:356
  51.9 3.4 %collective-permute-done.11.refs_6_ = bf16[2,32,1280]{2,1,0:T(8,128)(2,1)S(1)} collective-permute-done((bf16[2,32,1280]{2,1,0:T(8,128)(2,1)S(1)}, bf16[2,32,1280]{2,1,0:T(8,128)(2,1)S(1)}, u32[]{:S(2)}, u32[]{:S(2)}) %collective-permute-start.11) | collective-permute-done | bytes 163872 | tf_op jit(solution)/shard_map/ppermute | solution.py:356
  59.4 1.6 %collective-permute-start.20 = (bf16[2,192,640]{2,1,0:T(8,128)(2,1)S(1)}, bf16[2,192,640]{2,1,0:T(8,128)(2,1)S(1)}, u32[]{:S(2)}, u32[]{:S(2)}) collective-permute-start(bf16[2,192,640]{2,1,0:T(8,128)(2,1)S(1)} %shard_map.89.refs_2_), channel_id=1, source_target_pairs={{0,16},{8,24},{16,0},{24,8},{1,17},{9,25},{17,1},{25,9},{2,18},{10... | collective-permute-start | bytes 1474568 | tf_op jit(solution)/shard_map/ppermute | solution.py:459
  61.1 1.3 %collective-permute-start.21 = (bf16[2,192,640]{2,1,0:T(8,128)(2,1)S(1)}, bf16[2,192,640]{2,1,0:T(8,128)(2,1)S(1)}, u32[]{:S(2)}, u32[]{:S(2)}) collective-permute-start(bf16[2,192,640]{2,1,0:T(8,128)(2,1)S(1)} %shard_map.90.refs_9_), channel_id=1, source_target_pairs={{0,16},{8,24},{16,0},{24,8},{1,17},{9,25},{17,1},{25,9},{2,18},{10... | collective-permute-start | bytes 1474568 | tf_op jit(solution)/shard_map/ppermute | solution.py:459
  62.3 2.2 %shard_map.91 = (bf16[8,2,32,768]{3,2,1,0:T(8,128)(2,1)}, f32[2,256]{1,0:T(2,128)S(1)}) custom-call(bf16[2,768,2048]{2,1,0:T(8,128)(2,1)S(1)} %copy-done, bf16[2,32,1280]{2,1,0:T(8,128)(2,1)S(1)} %get-tuple-element.37.refs_3_.refs_1_, bf16[2,64,1280]{2,1,0:T(8,128)(2,1)S(1)} %get-tuple-element.38.refs_5_.refs_2_, ...), custom_call_target="tpu_custom_call" | custom-call | flops 1 | bytes 1 | tf_op jit(solution)/shard_map/pallas_call | solution.py:43
  64.6 1.5 %collective-permute-start.16 = (f32[2,256]{1,0:T(2,128)S(1)}, f32[2,256]{1,0:T(2,128)S(1)}, u32[]{:S(2)}, u32[]{:S(2)}) collective-permute-start(f32[2,256]{1,0:T(2,128)S(1)} %get-tuple-element.57.refs_4_), channel_id=1, source_target_pairs={{0,1},{1,0},{2,3},{3,2},{4,5},{5,4},{6,7},{7,6},{8,9},{9,8},{10,11... | collective-permute-start | bytes 6152 | tf_op jit(solution)/shard_map/ppermute | solution.py:500
  66.1 2.1 %collective-permute-done.16 = f32[2,256]{1,0:T(2,128)S(1)} collective-permute-done((f32[2,256]{1,0:T(2,128)S(1)}, f32[2,256]{1,0:T(2,128)S(1)}, u32[]{:S(2)}, u32[]{:S(2)}) %collective-permute-start.16) | collective-permute-done | bytes 2080 | tf_op jit(solution)/shard_map/ppermute | solution.py:500
  68.2 2.3 %collective-permute-start.17 = (f32[2,2,256]{2,1,0:T(2,128)S(1)}, f32[2,2,256]{2,1,0:T(2,128)S(1)}, u32[]{:S(2)}, u32[]{:S(2)}) collective-permute-start(f32[2,2,256]{2,1,0:T(2,128)S(1)} %pad_maximum_fusion.refs_2_), channel_id=1, source_target_pairs={{2,0},{3,1},{4,2},{5,3},{6,4},{7,5},{0,6},{1,7},{10,8},{11,9},{12,... | collective-permute-start | bytes 12296 | tf_op jit(solution)/shard_map/ppermute | solution.py:502
  71.5 1.5 %shard_map.92 = (f32[192,2,2048]{2,1,0:T(2,128)}, f32[8,128]{1,0:T(8,128)S(1)}) custom-call(bf16[2,2,192,768]{3,2,1,0:T(8,128)(2,1)S(1)} %get-tuple-element.44.refs_0_.refs_2_, bf16[2,2,192,768]{3,2,1,0:T(8,128)(2,1)S(1)} %collective-permute-done.9.refs_1_, bf16[2,96,768]{2,1,0:T(8,128)(2,1)S(1)} %collective-permute-done.12.refs_8_.refs_2_, ...), custom_call_target="tpu_custom_call" | custom-call | flops 1 | bytes 1 | tf_op jit(solution)/shard_map/pallas_call | solution.py:43
  73.5 1.4 %shard_map.93 = (f32[192,2,2048]{2,1,0:T(2,128)}, f32[8,128]{1,0:T(8,128)S(1)}) custom-call(bf16[2,2,192,640]{3,2,1,0:T(8,128)(2,1)S(1)} %get-tuple-element.51.refs_7_.refs_0_, bf16[2,2,192,640]{3,2,1,0:T(8,128)(2,1)S(1)} %collective-permute-done.15.refs_1_, ...), custom_call_target="tpu_custom_call", output_to_operand_aliasing={{0}: (3, {})} | custom-call | flops 1 | bytes 1 | tf_op jit(solution)/shard_map/pallas_call | solution.py:43
  77.2 6.1 %collective-permute-done.21.refs_2_ = bf16[2,192,640]{2,1,0:T(8,128)(2,1)S(1)} collective-permute-done((bf16[2,192,640]{2,1,0:T(8,128)(2,1)S(1)}, bf16[2,192,640]{2,1,0:T(8,128)(2,1)S(1)}, u32[]{:S(2)}, u32[]{:S(2)}) %collective-permute-start.21) | collective-permute-done | bytes 491552 | tf_op jit(solution)/shard_map/ppermute | solution.py:459
  83.2 1.9 %shard_map.95 = (f32[192,2,2048]{2,1,0:T(2,128)}, f32[8,128]{1,0:T(8,128)}) custom-call(bf16[2,2,192,640]{3,2,1,0:T(8,128)(2,1)S(1)} %get-tuple-element.52.refs_2_.refs_0_, bf16[2,2,192,640]{3,2,1,0:T(8,128)(2,1)S(1)} %collective-permute-done.14.refs_1_, bf16[2,192,640]{2,1,0:T(8,128)(2,1)S(1)} %collective-permute-done.21.refs_2_, ...), custom_call_target="tpu_custom_call", output_to_operand_aliasing={{0}: (3, {})} | custom-call | flops 1 | bytes 1 | tf_op jit(solution)/shard_map/pallas_call | solution.py:43
  (55 shorter events, 18.5 us)
Async XLA Ops:
  2.5 11.6 %collective-permute-start = (bf16[144,768]{1,0:T(8,128)(2,1)}, bf16[144,768]{1,0:T(8,128)(2,1)S(1)}, u32[]{:S(2)}, u32[]{:S(2)}) collective-permute-start(bf16[144,768]{1,0:T(8,128)(2,1)} %get-tuple-element.34.refs_0_), channel_id=1, source_target_pairs={{0,2},{1,3},{2,4},{3,5},{4,6},{5,7},{6,0},{7,1},{8,10},{9,11},{10,... | collective-permute-start | bytes 663560 | tf_op jit(solution)/shard_map/ppermute | solution.py:345
  5.5 15.8 %collective-permute-start.1 = (bf16[144,768]{1,0:T(8,128)(2,1)}, bf16[144,768]{1,0:T(8,128)(2,1)S(1)}, u32[]{:S(2)}, u32[]{:S(2)}) collective-permute-start(bf16[144,768]{1,0:T(8,128)(2,1)} %get-tuple-element.34.refs_0_), channel_id=1, source_target_pairs={{0,6},{1,7},{2,0},{3,1},{4,2},{5,3},{6,4},{7,5},{8,14},{9,15},{10,... | collective-permute-start | bytes 663560 | tf_op jit(solution)/shard_map/ppermute | solution.py:345
  14.1 11.1 %collective-permute-start.2 = (bf16[144,768]{1,0:T(8,128)(2,1)S(1)}, bf16[144,768]{1,0:T(8,128)(2,1)S(1)}, u32[]{:S(2)}, u32[]{:S(2)}) collective-permute-start(bf16[144,768]{1,0:T(8,128)(2,1)S(1)} %collective-permute-done.refs_1_), channel_id=1, source_target_pairs={{0,2},{1,3},{2,4},{3,5},{4,6},{5,7},{6,0},{7,1},{8,10},{9,11},{10,... | collective-permute-start | bytes 663560 | tf_op jit(solution)/shard_map/ppermute | solution.py:345
  15.2 16.9 %collective-permute-start.3 = (bf16[128,1280]{1,0:T(8,128)(2,1)S(1)}, bf16[128,1280]{1,0:T(8,128)(2,1)S(1)}, u32[]{:S(2)}, u32[]{:S(2)}) collective-permute-start(bf16[128,1280]{1,0:T(8,128)(2,1)S(1)} %shard_map.77.refs_1_.refs_0_), channel_id=1, source_target_pairs={{0,2},{1,3},{2,4},{3,5},{4,6},{5,7},{6,0},{7,1},{8,10},{9,11},{10,... | collective-permute-start | bytes 983048 | tf_op jit(solution)/shard_map/ppermute | solution.py:345
  19.3 16.9 %collective-permute-start.4 = (bf16[128,1280]{1,0:T(8,128)(2,1)S(1)}, bf16[128,1280]{1,0:T(8,128)(2,1)S(1)}, u32[]{:S(2)}, u32[]{:S(2)}) collective-permute-start(bf16[128,1280]{1,0:T(8,128)(2,1)S(1)} %shard_map.77.refs_1_.refs_0_), channel_id=1, source_target_pairs={{0,6},{1,7},{2,0},{3,1},{4,2},{5,3},{6,4},{7,5},{8,14},{9,15},{10,... | collective-permute-start | bytes 983048 | tf_op jit(solution)/shard_map/ppermute | solution.py:345
  22.6 13.9 %collective-permute-start.6 = (bf16[2,96,768]{2,1,0:T(8,128)(2,1)S(1)}, bf16[2,96,768]{2,1,0:T(8,128)(2,1)S(1)}, u32[]{:S(2)}, u32[]{:S(2)}) collective-permute-start(bf16[2,96,768]{2,1,0:T(8,128)(2,1)S(1)} %get-tuple-element.41), channel_id=1, source_target_pairs={{0,1},{1,0},{2,3},{3,2},{4,5},{5,4},{6,7},{7,6},{8,9},{9,8},{10,11... | collective-permute-start | bytes 884744 | tf_op jit(solution)/shard_map/ppermute | solution.py:356
  25.6 10.9 %collective-permute-start.8 = (bf16[2,32,1280]{2,1,0:T(8,128)(2,1)S(1)}, bf16[2,32,1280]{2,1,0:T(8,128)(2,1)S(1)}, u32[]{:S(2)}, u32[]{:S(2)}) collective-permute-start(bf16[2,32,1280]{2,1,0:T(8,128)(2,1)S(1)} %get-tuple-element.43), channel_id=1, source_target_pairs={{0,1},{1,0},{2,3},{3,2},{4,5},{5,4},{6,7},{7,6},{8,9},{9,8},{10,11... | collective-permute-start | bytes 491528 | tf_op jit(solution)/shard_map/ppermute | solution.py:356
  27.2 9.3 %collective-permute-start.7 = (bf16[2,32,768]{2,1,0:T(8,128)(2,1)S(1)}, bf16[2,32,768]{2,1,0:T(8,128)(2,1)S(1)}, u32[]{:S(2)}, u32[]{:S(2)}) collective-permute-start(bf16[2,32,768]{2,1,0:T(8,128)(2,1)S(1)} %get-tuple-element.42), channel_id=1, source_target_pairs={{0,1},{1,0},{2,3},{3,2},{4,5},{5,4},{6,7},{7,6},{8,9},{9,8},{10,11... | collective-permute-start | bytes 294920 | tf_op jit(solution)/shard_map/ppermute | solution.py:356
  36.2 14.9 %copy-start = (bf16[2,768,2048]{2,1,0:T(8,128)(2,1)S(1)}, bf16[2,768,2048]{2,1,0:T(8,128)(2,1)}, u32[]{:S(2)}) copy-start(bf16[2,768,2048]{2,1,0:T(8,128)(2,1)} %refs_0_.5) | copy-start | bytes 18874372
  37.3 2.9 %collective-permute-start.9 = (bf16[2,2,192,768]{3,2,1,0:T(8,128)(2,1)S(1)}, bf16[2,2,192,768]{3,2,1,0:T(8,128)(2,1)S(1)}, u32[]{:S(2)}, u32[]{:S(2)}) collective-permute-start(bf16[2,2,192,768]{3,2,1,0:T(8,128)(2,1)S(1)} %get-tuple-element.45), channel_id=1, source_target_pairs={{0,8},{8,0},{16,24},{24,16},{1,9},{9,1},{17,25},{25,17},{2,10},{10... | collective-permute-start | bytes 3538952 | tf_op jit(solution)/shard_map/ppermute | solution.py:448
  37.4 11.9 %collective-permute-start.5 = (bf16[128,1280]{1,0:T(8,128)(2,1)S(1)}, bf16[128,1280]{1,0:T(8,128)(2,1)S(1)}, u32[]{:S(2)}, u32[]{:S(2)}) collective-permute-start(bf16[128,1280]{1,0:T(8,128)(2,1)S(1)} %collective-permute-done.3.refs_0_), channel_id=1, source_target_pairs={{0,2},{1,3},{2,4},{3,5},{4,6},{5,7},{6,0},{7,1},{8,10},{9,11},{10,... | collective-permute-start | bytes 983048 | tf_op jit(solution)/shard_map/ppermute | solution.py:345
  38.6 13.3 %collective-permute-start.10 = (bf16[2,64,1280]{2,1,0:T(8,128)(2,1)S(1)}, bf16[2,64,1280]{2,1,0:T(8,128)(2,1)S(1)}, u32[]{:S(2)}, u32[]{:S(2)}) collective-permute-start(bf16[2,64,1280]{2,1,0:T(8,128)(2,1)S(1)} %get-tuple-element.48), channel_id=1, source_target_pairs={{0,1},{1,0},{2,3},{3,2},{4,5},{5,4},{6,7},{7,6},{8,9},{9,8},{10,11... | collective-permute-start | bytes 983048 | tf_op jit(solution)/shard_map/ppermute | solution.py:356
  40.4 15.0 %collective-permute-start.12 = (bf16[2,96,768]{2,1,0:T(8,128)(2,1)S(1)}, bf16[2,96,768]{2,1,0:T(8,128)(2,1)S(1)}, u32[]{:S(2)}, u32[]{:S(2)}) collective-permute-start(bf16[2,96,768]{2,1,0:T(8,128)(2,1)S(1)} %get-tuple-element.46.refs_2_), channel_id=1, source_target_pairs={{0,16},{8,24},{16,0},{24,8},{1,17},{9,25},{17,1},{25,9},{2,18},{10... | collective-permute-start | bytes 884744 | tf_op jit(solution)/shard_map/ppermute | solution.py:459
  42.0 13.8 %collective-permute-start.13 = (bf16[2,96,768]{2,1,0:T(8,128)(2,1)S(1)}, bf16[2,96,768]{2,1,0:T(8,128)(2,1)S(1)}, u32[]{:S(2)}, u32[]{:S(2)}) collective-permute-start(bf16[2,96,768]{2,1,0:T(8,128)(2,1)S(1)} %get-tuple-element.50), channel_id=1, source_target_pairs={{0,16},{8,24},{16,0},{24,8},{1,17},{9,25},{17,1},{25,9},{2,18},{10... | collective-permute-start | bytes 884744 | tf_op jit(solution)/shard_map/ppermute | solution.py:459
  49.5 5.8 %collective-permute-start.11 = (bf16[2,32,1280]{2,1,0:T(8,128)(2,1)S(1)}, bf16[2,32,1280]{2,1,0:T(8,128)(2,1)S(1)}, u32[]{:S(2)}, u32[]{:S(2)}) collective-permute-start(bf16[2,32,1280]{2,1,0:T(8,128)(2,1)S(1)} %get-tuple-element.49), channel_id=1, source_target_pairs={{0,1},{1,0},{2,3},{3,2},{4,5},{5,4},{6,7},{7,6},{8,9},{9,8},{10,11... | collective-permute-start | bytes 491528 | tf_op jit(solution)/shard_map/ppermute | solution.py:356
  56.6 2.6 %collective-permute-start.15 = (bf16[2,2,192,640]{3,2,1,0:T(8,128)(2,1)S(1)}, bf16[2,2,192,640]{3,2,1,0:T(8,128)(2,1)S(1)}, u32[]{:S(2)}, u32[]{:S(2)}) collective-permute-start(bf16[2,2,192,640]{3,2,1,0:T(8,128)(2,1)S(1)} %get-tuple-element.54), channel_id=1, source_target_pairs={{0,8},{8,0},{16,24},{24,16},{1,9},{9,1},{17,25},{25,17},{2,10},{10... | collective-permute-start | bytes 2949128 | tf_op jit(solution)/shard_map/ppermute | solution.py:448
  57.5 3.5 %collective-permute-start.14 = (bf16[2,2,192,640]{3,2,1,0:T(8,128)(2,1)S(1)}, bf16[2,2,192,640]{3,2,1,0:T(8,128)(2,1)S(1)}, u32[]{:S(2)}, u32[]{:S(2)}) collective-permute-start(bf16[2,2,192,640]{3,2,1,0:T(8,128)(2,1)S(1)} %get-tuple-element.53), channel_id=1, source_target_pairs={{0,8},{8,0},{16,24},{24,16},{1,9},{9,1},{17,25},{25,17},{2,10},{10... | collective-permute-start | bytes 2949128 | tf_op jit(solution)/shard_map/ppermute | solution.py:448
  59.4 14.1 %collective-permute-start.20 = (bf16[2,192,640]{2,1,0:T(8,128)(2,1)S(1)}, bf16[2,192,640]{2,1,0:T(8,128)(2,1)S(1)}, u32[]{:S(2)}, u32[]{:S(2)}) collective-permute-start(bf16[2,192,640]{2,1,0:T(8,128)(2,1)S(1)} %shard_map.89.refs_2_), channel_id=1, source_target_pairs={{0,16},{8,24},{16,0},{24,8},{1,17},{9,25},{17,1},{25,9},{2,18},{10... | collective-permute-start | bytes 1474568 | tf_op jit(solution)/shard_map/ppermute | solution.py:459
  61.1 22.2 %collective-permute-start.21 = (bf16[2,192,640]{2,1,0:T(8,128)(2,1)S(1)}, bf16[2,192,640]{2,1,0:T(8,128)(2,1)S(1)}, u32[]{:S(2)}, u32[]{:S(2)}) collective-permute-start(bf16[2,192,640]{2,1,0:T(8,128)(2,1)S(1)} %shard_map.90.refs_9_), channel_id=1, source_target_pairs={{0,16},{8,24},{16,0},{24,8},{1,17},{9,25},{17,1},{25,9},{2,18},{10... | collective-permute-start | bytes 1474568 | tf_op jit(solution)/shard_map/ppermute | solution.py:459
  64.6 3.6 %collective-permute-start.16 = (f32[2,256]{1,0:T(2,128)S(1)}, f32[2,256]{1,0:T(2,128)S(1)}, u32[]{:S(2)}, u32[]{:S(2)}) collective-permute-start(f32[2,256]{1,0:T(2,128)S(1)} %get-tuple-element.57.refs_4_), channel_id=1, source_target_pairs={{0,1},{1,0},{2,3},{3,2},{4,5},{5,4},{6,7},{7,6},{8,9},{9,8},{10,11... | collective-permute-start | bytes 6152 | tf_op jit(solution)/shard_map/ppermute | solution.py:500
  68.2 6.7 %collective-permute-start.17 = (f32[2,2,256]{2,1,0:T(2,128)S(1)}, f32[2,2,256]{2,1,0:T(2,128)S(1)}, u32[]{:S(2)}, u32[]{:S(2)}) collective-permute-start(f32[2,2,256]{2,1,0:T(2,128)S(1)} %pad_maximum_fusion.refs_2_), channel_id=1, source_target_pairs={{2,0},{3,1},{4,2},{5,3},{6,4},{7,5},{0,6},{1,7},{10,8},{11,9},{12,... | collective-permute-start | bytes 12296 | tf_op jit(solution)/shard_map/ppermute | solution.py:502
  70.5 4.5 %collective-permute-start.18 = (f32[2,2,256]{2,1,0:T(2,128)S(1)}, f32[2,2,256]{2,1,0:T(2,128)S(1)}, u32[]{:S(2)}, u32[]{:S(2)}) collective-permute-start(f32[2,2,256]{2,1,0:T(2,128)S(1)} %pad_maximum_fusion.refs_2_), channel_id=1, source_target_pairs={{4,0},{5,1},{6,2},{7,3},{0,4},{1,5},{2,6},{3,7},{12,8},{13,9},{14,... | collective-permute-start | bytes 12296 | tf_op jit(solution)/shard_map/ppermute | solution.py:502
  70.7 5.4 %collective-permute-start.19 = (f32[2,2,256]{2,1,0:T(2,128)S(1)}, f32[2,2,256]{2,1,0:T(2,128)S(1)}, u32[]{:S(2)}, u32[]{:S(2)}) collective-permute-start(f32[2,2,256]{2,1,0:T(2,128)S(1)} %pad_maximum_fusion.refs_2_), channel_id=1, source_target_pairs={{6,0},{7,1},{0,2},{1,3},{2,4},{3,5},{4,6},{5,7},{14,8},{15,9},{8,1... | collective-permute-start | bytes 12296 | tf_op jit(solution)/shard_map/ppermute | solution.py:502
  73.0 3.2 %copy-start.5 = (f32[128,2]{0,1:T(2,128)S(1)}, f32[128,2]{0,1:T(2,128)}, u32[]{:S(2)}) copy-start(f32[128,2]{0,1:T(2,128)} %param.7) | copy-start | bytes 3076
  (5 other events, 9.4 us)
